TPU v7x, 32 devices: a whole 2x2x4 slice. The times are simulated.
32 devices in a mesh: dp: 16 (over z, y, x), tensor: 2 (over core).
Axes of the slice: x: 2, y: 2, z: 4, core: 2. Of those that a mesh axis runs over, the one named last changes fastest.
Arguments:
- tokens: bfloat16 [4096, 1024], P(('dp', 'tensor')), may hold values from -6 to 6
- lengths: int32 [16, 4], P('dp'), may hold values from 0 to 160, as said below
- attn_gain: float32 [1024], replicated, may hold values from 0.1 to 1.9
- query_gain: float32 [64], replicated, may hold values from 0.1 to 1.9
- key_gain: float32 [64], replicated, may hold values from 0.1 to 1.9
- ffn_gain: float32 [1024], replicated, may hold values from 0.1 to 1.9
- w_query: bfloat16 [1024, 1024], P('dp', 'tensor'), may hold values from -0.1875 to 0.1875
- w_key: bfloat16 [1024, 512], P('dp', 'tensor'), may hold values from -0.1875 to 0.1875
- w_value: bfloat16 [1024, 512], P('dp', 'tensor'), may hold values from -0.1875 to 0.1875
- w_out: bfloat16 [1024, 1024], P('dp', 'tensor'), may hold values from -0.75 to 0.75
- w_gate: bfloat16 [1024, 4608], P('dp', 'tensor'), may hold values from -0.1875 to 0.1875
- w_up: bfloat16 [1024, 4608], P('dp', 'tensor'), may hold values from -0.1875 to 0.1875
- w_down: bfloat16 [1024, 4608], P('dp', 'tensor'), may hold values from -0.09375 to 0.09375
- cotangent: bfloat16 [4096, 1024], P(('dp', 'tensor')), may hold values from -8 to 8
Outputs:
- block_out: bfloat16 [4096, 1024], P(('dp', 'tensor'))
- grad_tokens: float32 [4096, 1024], P(('dp', 'tensor'))
- grad_attn_gain: float32 [1024], replicated
- grad_query_gain: float32 [64], replicated
- grad_key_gain: float32 [64], replicated
- grad_ffn_gain: float32 [1024], replicated
- grad_w_query: float32 [1024, 1024], P('dp', 'tensor')
- grad_w_key: float32 [1024, 512], P('dp', 'tensor')
- grad_w_value: float32 [1024, 512], P('dp', 'tensor')
- grad_w_out: float32 [1024, 1024], P('dp', 'tensor')
- grad_w_gate: float32 [1024, 4608], P('dp', 'tensor')
- grad_w_up: float32 [1024, 4608], P('dp', 'tensor')
- grad_w_down: float32 [1024, 4608], P('dp', 'tensor')
Inputs may be any that keep to these rules, and one draw needn't show every extreme that they name: `lengths`: row g belongs to dp index g. Its entries sum to between 192 and 256, both reached in every draw; exactly one entry of each row is longer than 128, and 160 is reached in every draw.
All inputs are finite; a program needn't handle non-finite values.
Results may differ from a plain program's by a relative error of at most 0.015.
Values may be sent and summed in bfloat16 or wider, within the bound.
No kernel may reach another device: no remote copies, remote signals or barrier semaphores. Data moves between devices by JAX's collectives and lax.ppermute only.
A program may use at most 128 MiB of HBM per device.

v0:
```python
import jax
import jax.numpy as jnp
from jax import lax
from jax.sharding import PartitionSpec as P

HEAD_DIM = 64


epsilon = 1e-05
rope_base = 1000000.0
masked_score = -1e30


def inverse_rms(values):
    return lax.rsqrt(jnp.mean(values * values, axis=-1, keepdims=True) + epsilon)


def norm_back(grad_unit, unit, factor):
    return factor * (grad_unit - unit * jnp.mean(grad_unit * unit, axis=-1, keepdims=True))


def matmul(first_op, second_op):
    return jnp.dot(first_op, second_op, preferred_element_type=jnp.float32)


def matmul_nt(first_op, second_op):
    return lax.dot_general(
        first_op, second_op, (((1,), (1,)), ((), ())), preferred_element_type=jnp.float32
    )


def matmul_tn(first_op, second_op):
    return lax.dot_general(
        first_op, second_op, (((0,), (0,)), ((), ())), preferred_element_type=jnp.float32
    )


def seq_layout(seq_lengths, total_rows):
    ends = jnp.cumsum(seq_lengths, dtype=jnp.int32)
    starts = ends - seq_lengths
    row_ids = jnp.arange(total_rows, dtype=jnp.int32)
    segment = jnp.sum(
        (row_ids[:, None] >= ends[None, :]).astype(jnp.int32), axis=1, dtype=jnp.int32
    )
    slot_ids = jnp.arange(seq_lengths.shape[0], dtype=jnp.int32)
    picked = (segment[:, None] == slot_ids[None, :]).astype(jnp.int32)
    begin = (
        jnp.sum(picked * starts[None, :], axis=1, dtype=jnp.int32)
        + (segment == seq_lengths.shape[0]).astype(jnp.int32) * ends[-1]
    )
    allowed = (segment[:, None] == segment[None, :]) & (row_ids[:, None] >= row_ids[None, :])
    return (row_ids - begin, row_ids < ends[-1], allowed)


def rope_tables(position, head_size):
    half_dim = head_size // 2
    freqs = rope_base ** (-jnp.arange(half_dim, dtype=jnp.float32) * 2.0 / head_size)
    angles = position.astype(jnp.float32)[:, None] * freqs[None, :]
    return (jnp.cos(angles)[:, None, :], jnp.sin(angles)[:, None, :])


def rotate(values, cosine, sine):
    half_dim = values.shape[-1] // 2
    first_half = values[..., :half_dim]
    second_half = values[..., half_dim:]
    return jnp.concatenate(
        [first_half * cosine - second_half * sine, second_half * cosine + first_half * sine],
        axis=-1,
    )


def rotate_back(grads, cosine, sine):
    half_dim = grads.shape[-1] // 2
    first_half = grads[..., :half_dim]
    second_half = grads[..., half_dim:]
    return jnp.concatenate(
        [first_half * cosine + second_half * sine, second_half * cosine - first_half * sine],
        axis=-1,
    )


def body(
    tokens,
    lengths,
    attn_gain,
    query_gain,
    key_gain,
    ffn_gain,
    w_query,
    w_key,
    w_value,
    w_out,
    w_gate,
    w_up,
    w_down,
    cotangent,
):
    shards = (w_query, w_key, w_value, w_out, w_gate, w_up, w_down)
    full_query, full_key, full_value, full_out, full_gate, full_up, full_down = (
        lax.all_gather(shards[0], "dp", axis=0, tiled=True),
        lax.all_gather(shards[1], "dp", axis=0, tiled=True),
        lax.all_gather(shards[2], "dp", axis=0, tiled=True),
        lax.all_gather(shards[3], "dp", axis=0, tiled=True),
        lax.all_gather(shards[4], "dp", axis=0, tiled=True),
        lax.all_gather(shards[5], "dp", axis=0, tiled=True),
        lax.all_gather(shards[6], "dp", axis=0, tiled=True),
    )
    tensor_index = lax.axis_index("tensor")
    local_rows = tokens.shape[0]
    total_rows = local_rows * lax.axis_size("tensor")
    local_heads = full_query.shape[1] // HEAD_DIM
    local_kv = full_key.shape[1] // HEAD_DIM
    share = local_heads // local_kv
    score_scale = HEAD_DIM ** (-0.5)
    position, live, allowed = seq_layout(lengths[0], total_rows)
    live_local = lax.dynamic_slice_in_dim(live, tensor_index * local_rows, local_rows)
    cosine, sine = rope_tables(position, HEAD_DIM)
    inputs = tokens.astype(jnp.float32)
    factor_a = inverse_rms(inputs)
    unit_a = inputs * factor_a
    normed = lax.all_gather((unit_a * attn_gain).astype(jnp.bfloat16), "tensor", axis=0, tiled=True)
    query_pre = matmul(normed, full_query).reshape(total_rows, local_heads, HEAD_DIM)
    key_pre = matmul(normed, full_key).reshape(total_rows, local_kv, HEAD_DIM)
    value_low = (
        matmul(normed, full_value).astype(jnp.bfloat16).reshape(total_rows, local_kv, HEAD_DIM)
    )
    factor_q = inverse_rms(query_pre)
    unit_q = query_pre * factor_q
    factor_k = inverse_rms(key_pre)
    unit_k = key_pre * factor_k
    query_low = rotate(unit_q * query_gain, cosine, sine).astype(jnp.bfloat16)
    key_low = rotate(unit_k * key_gain, cosine, sine).astype(jnp.bfloat16)
    grouped = query_low.reshape(total_rows, local_kv, share, HEAD_DIM)
    scores = (
        jnp.einsum("qgjd,kgd->gjqk", grouped, key_low, preferred_element_type=jnp.float32)
        * score_scale
    )
    scores = jnp.where(allowed, scores, masked_score)
    top = jnp.max(scores, axis=-1, keepdims=True)
    expd = jnp.exp(scores - top)
    totals = jnp.sum(expd, axis=-1, keepdims=True)
    log_total = top + jnp.log(totals)
    probs_low = (expd / totals).astype(jnp.bfloat16)
    mixed = jnp.einsum("gjqk,kgd->qgjd", probs_low, value_low, preferred_element_type=jnp.float32)
    mixed_low = mixed.reshape(total_rows, local_heads * HEAD_DIM).astype(jnp.bfloat16)
    attn_branch = lax.psum_scatter(
        matmul_nt(mixed_low, full_out), "tensor", scatter_dimension=0, tiled=True
    )
    hidden = inputs + attn_branch
    factor_b = inverse_rms(hidden)
    unit_b = hidden * factor_b
    normed2 = lax.all_gather((unit_b * ffn_gain).astype(jnp.bfloat16), "tensor", axis=0, tiled=True)
    gate = matmul(normed2, full_gate)
    up_proj = matmul(normed2, full_up)
    sigma = jax.nn.sigmoid(gate)
    silu_gate = gate * sigma
    act_low = (silu_gate * up_proj).astype(jnp.bfloat16)
    ffn_branch = lax.psum_scatter(
        matmul_nt(act_low, full_down).astype(jnp.bfloat16),
        "tensor",
        scatter_dimension=0,
        tiled=True,
    ).astype(jnp.float32)
    block_out = (hidden + ffn_branch).astype(jnp.bfloat16)
    full_query, full_key, full_value, full_out, full_gate, full_up, full_down = (
        lax.all_gather(shards[0], "dp", axis=0, tiled=True),
        lax.all_gather(shards[1], "dp", axis=0, tiled=True),
        lax.all_gather(shards[2], "dp", axis=0, tiled=True),
        lax.all_gather(shards[3], "dp", axis=0, tiled=True),
        lax.all_gather(shards[4], "dp", axis=0, tiled=True),
        lax.all_gather(shards[5], "dp", axis=0, tiled=True),
        lax.all_gather(shards[6], "dp", axis=0, tiled=True),
    )
    grad_out = jnp.where(live_local[:, None], cotangent, jnp.zeros_like(cotangent))
    grad_rows = lax.all_gather(grad_out, "tensor", axis=0, tiled=True)
    d_act = matmul(grad_rows, full_down)
    grad_down = matmul_tn(grad_rows, act_low)
    d_gate = (d_act * up_proj * sigma * (1.0 + gate * (1.0 - sigma))).astype(jnp.bfloat16)
    d_up = (d_act * silu_gate).astype(jnp.bfloat16)
    grad_gate = matmul_tn(normed2, d_gate)
    grad_up = matmul_tn(normed2, d_up)
    d_normed2 = lax.psum_scatter(
        (matmul_nt(d_gate, full_gate) + matmul_nt(d_up, full_up)).astype(jnp.bfloat16),
        "tensor",
        scatter_dimension=0,
        tiled=True,
    ).astype(jnp.float32)
    gain_ffn = jnp.sum(d_normed2 * unit_b, axis=0)
    d_hidden = grad_out.astype(jnp.float32) + norm_back(d_normed2 * ffn_gain, unit_b, factor_b)
    hidden_rows = lax.all_gather(d_hidden.astype(jnp.bfloat16), "tensor", axis=0, tiled=True)
    grad_out_proj = matmul_tn(hidden_rows, mixed_low)
    d_mixed = (
        matmul(hidden_rows, full_out)
        .astype(jnp.bfloat16)
        .reshape(total_rows, local_kv, share, HEAD_DIM)
    )
    again_scores = (
        jnp.einsum("qgjd,kgd->gjqk", grouped, key_low, preferred_element_type=jnp.float32)
        * score_scale
    )
    probs = jnp.exp(jnp.where(allowed, again_scores, masked_score) - log_total)
    again_low = probs.astype(jnp.bfloat16)
    d_value = jnp.einsum("gjqk,qgjd->kgd", again_low, d_mixed, preferred_element_type=jnp.float32)
    d_value_low = d_value.astype(jnp.bfloat16).reshape(total_rows, local_kv * HEAD_DIM)
    d_probs = jnp.einsum("qgjd,kgd->gjqk", d_mixed, value_low, preferred_element_type=jnp.float32)
    centre = jnp.sum(probs * d_probs, axis=-1, keepdims=True)
    d_scores = (probs * (d_probs - centre)).astype(jnp.bfloat16)
    d_query_rot = jnp.einsum(
        "gjqk,kgd->qgjd", d_scores, key_low, preferred_element_type=jnp.float32
    )
    d_query_rot = d_query_rot.reshape(total_rows, local_heads, HEAD_DIM) * score_scale
    d_key_rot = (
        jnp.einsum("gjqk,qgjd->kgd", d_scores, grouped, preferred_element_type=jnp.float32)
        * score_scale
    )
    turned_q = rotate_back(d_query_rot, cosine, sine)
    turned_k = rotate_back(d_key_rot, cosine, sine)
    gain_query = jnp.sum(turned_q * unit_q, axis=(0, 1))
    gain_key = jnp.sum(turned_k * unit_k, axis=(0, 1))
    d_query = (
        norm_back(turned_q * query_gain, unit_q, factor_q)
        .astype(jnp.bfloat16)
        .reshape(total_rows, local_heads * HEAD_DIM)
    )
    d_key = (
        norm_back(turned_k * key_gain, unit_k, factor_k)
        .astype(jnp.bfloat16)
        .reshape(total_rows, local_kv * HEAD_DIM)
    )
    grad_query = matmul_tn(normed, d_query)
    grad_key = matmul_tn(normed, d_key)
    grad_value = matmul_tn(normed, d_value_low)
    d_normed_part = (
        matmul_nt(d_query, full_query)
        + matmul_nt(d_key, full_key)
        + matmul_nt(d_value_low, full_value)
    )
    d_normed = lax.psum_scatter(
        d_normed_part.astype(jnp.bfloat16), "tensor", scatter_dimension=0, tiled=True
    ).astype(jnp.float32)
    gain_attn = jnp.sum(d_normed * unit_a, axis=0)
    grad_tokens = d_hidden + norm_back(d_normed * attn_gain, unit_a, factor_a)
    sum_attn, sum_query, sum_key, sum_ffn = lax.psum(
        (gain_attn, gain_query, gain_key, gain_ffn), ("dp", "tensor")
    )
    owned = (
        lax.psum_scatter(grad_query, "dp", scatter_dimension=0, tiled=True),
        lax.psum_scatter(grad_key, "dp", scatter_dimension=0, tiled=True),
        lax.psum_scatter(grad_value, "dp", scatter_dimension=0, tiled=True),
        lax.psum_scatter(grad_out_proj, "dp", scatter_dimension=0, tiled=True),
        lax.psum_scatter(grad_gate, "dp", scatter_dimension=0, tiled=True),
        lax.psum_scatter(grad_up, "dp", scatter_dimension=0, tiled=True),
        lax.psum_scatter(grad_down, "dp", scatter_dimension=0, tiled=True),
    )
    return (
        block_out,
        grad_tokens,
        sum_attn,
        sum_query,
        sum_key,
        sum_ffn,
        owned[0],
        owned[1],
        owned[2],
        owned[3],
        owned[4],
        owned[5],
        owned[6],
    )


def solution(mesh):
    placed = (
        P(("dp", "tensor"), None),
        P("dp", None),
        P(),
        P(),
        P(),
        P(),
        P("dp", "tensor"),
        P("dp", "tensor"),
        P("dp", "tensor"),
        P("dp", "tensor"),
        P("dp", "tensor"),
        P("dp", "tensor"),
        P("dp", "tensor"),
        P(("dp", "tensor"), None),
    )
    return jax.shard_map(
        body,
        mesh=mesh,
        in_specs=placed,
        out_specs=(
            P(("dp", "tensor"), None),
            P(("dp", "tensor"), None),
            P(),
            P(),
            P(),
            P(),
            P("dp", "tensor"),
            P("dp", "tensor"),
            P("dp", "tensor"),
            P("dp", "tensor"),
            P("dp", "tensor"),
            P("dp", "tensor"),
            P("dp", "tensor"),
        ),
        check_vma=False,
    )
```

profile of v0, /device:TPU:0, one launch (start us, length us, event | category | flops | bytes accessed | tf_op | source)
XLA Modules:
  0.0 1302.3 jit_solution(5634068565129644279)
XLA Ops:
  7.2 0.7 all-gather.6.cloned.1.call-update
  8.0 0.7 all-gather.8.cloned.1.call-update
  8.7 0.8 reduce-window.4
  10.8 1.1 fusion.29
  12.4 1.1 fusion.26
  13.5 2.3 all_gather.40
  15.9 0.7 fusion.33
  16.7 46.6 %all_gather.42 = bf16[1024,256]{1,0:T(8,128)(2,1)S(1)} all-gather(bf16[64,256]{1,0:T(8,128)(2,1)} %param.21), channel_id=1, replica_groups=mesh['dp'=16,'tensor'=2] {'dp'}, dimensions={0}, use_global_device_ids=true | all-gather | bytes 557056 | tf_op jit(solution)/shard_map/all_gather | solution.py:101
  64.1 39.3 %all_gather.41 = bf16[1024,256]{1,0:T(8,128)(2,1)S(1)} all-gather(bf16[64,256]{1,0:T(8,128)(2,1)S(1)} %copy-done.51), channel_id=1, replica_groups=mesh['dp'=16,'tensor'=2] {'dp'}, dimensions={0}, use_global_device_ids=true | all-gather | bytes 557056 | tf_op jit(solution)/shard_map/all_gather | solution.py:102
  104.8 0.7 subtract_convert_fusion.1
  105.5 1.7 fusion.43
  109.9 17.4 %all-gather.8.cloned.1.call-done = bf16[1024,512]{1,0:T(8,128)(2,1)} async-done(((bf16[64,512]{1,0:T(8,128)(2,1)}), bf16[1024,512]{1,0:T(8,128)(2,1)}) %all-gather.8.cloned.1.call-update) | async-done | bytes 1048592 | tf_op jit(solution)/shard_map/all_gather | solution.py:103
  127.3 2.8 fusion.44
  132.7 2.3 all_gather.49
  135.0 2.6 reduce-scatter.12.cloned.1.call-done
  137.6 1.2 multiply_reduce_fusion.2
  139.0 2.3 all_gather.45
  141.3 81.0 %all-gather.10.cloned.1.call-done = bf16[1024,2304]{1,0:T(8,128)(2,1)} async-done(((bf16[64,2304]{1,0:T(8,128)(2,1)}), bf16[1024,2304]{1,0:T(8,128)(2,1)}) %all-gather.10.cloned.1.call-update) | async-done | bytes 4718608 | tf_op jit(solution)/shard_map/all_gather | solution.py:104
  222.3 5.3 fusion.45
  227.6 76.9 %all-gather.12.cloned.1.call-done = bf16[1024,2304]{1,0:T(8,128)(2,1)} async-done(((bf16[64,2304]{1,0:T(8,128)(2,1)}), bf16[1024,2304]{1,0:T(8,128)(2,1)}) %all-gather.12.cloned.1.call-update) | async-done | bytes 4718608 | tf_op jit(solution)/shard_map/all_gather | solution.py:105
  304.4 5.3 fusion.46
  309.8 76.8 %all-gather.14.cloned.1.call-done = bf16[1024,2304]{1,0:T(8,128)(2,1)} async-done(((bf16[64,2304]{1,0:T(8,128)(2,1)}), bf16[1024,2304]{1,0:T(8,128)(2,1)}) %all-gather.14.cloned.1.call-update) | async-done | bytes 4718608 | tf_op jit(solution)/shard_map/all_gather | solution.py:106
  386.6 6.8 multiply_convert_fusion
  393.4 4.6 fusion.47
  398.1 2.2 fusion.6
  400.4 0.7 mul.488
  401.8 0.7 mul.507
  402.4 0.8 mul.446
  403.3 2.0 copy.57
  405.3 0.7 log_add_fusion
  406.0 1.1 reduce-scatter.16.cloned.1.call-done
  407.1 1.9 fusion.25
  409.0 1.2 fusion.41
  410.2 2.4 all_gather.50
  412.6 0.8 copy-done.6
  413.4 1.2 convolution_convert_fusion.1
  414.6 1.8 copy.52
  416.4 1.5 fusion.1
  419.1 1.1 fusion.9
  421.5 1.0 copy.54
  422.6 1.0 copy.56
  423.6 0.9 multiply_add_fusion.1
  424.9 1.4 multiply_reduce_fusion
  427.3 1.1 fusion.7
  428.6 4.9 convolution_convert_fusion
  433.6 1.4 fusion.50
  435.0 1.3 fusion.51
  436.5 1.8 fusion.49
  438.4 2.9 fusion.52
  441.4 5.1 fusion.53
  446.5 1.3 copy-done.24
  447.8 5.1 fusion.54
  453.0 1.0 copy-done.20
  454.3 5.1 fusion.55
  460.1 1.2 fusion.28
  461.3 41.0 %all-reduce = (f32[1024]{0:T(1024)}, f32[64]{0:T(128)}, f32[64]{0:T(128)}, f32[1024]{0:T(1024)}) all-reduce(f32[1024]{0:T(1024)S(1)} %get-tuple-element.15, f32[64]{0:T(128)S(1)} %reduce_sum.173, f32[64]{0:T(128)S(1)} %reduce_sum.176, f32[1024]{0:T(1024)S(1)} %copy-done.52), channel_id=1, replica_groups=mesh['dp'=16,'tensor'=2] {'dp','tensor'}, use_global_device_ids=true, to_apply=%region_19.20 | all-reduce | flops 2176 | bytes 17408 | tf_op jit(solution)/shard_map/psum | solution.py:243
  502.4 2.2 fusion.21
  504.6 26.3 %reduce-scatter.22.cloned.1.call-done = f32[64,256]{1,0:T(8,128)} async-done(((f32[1024,256]{1,0:T(8,128)}), f32[64,256]{1,0:T(8,128)}) %reduce-scatter.22.cloned.1.call-update) | async-done | bytes 65552 | tf_op jit(solution)/shard_map/reduce_scatter | solution.py:248
  530.9 77.1 %reduce-scatter.24.cloned.1.call-done = f32[64,256]{1,0:T(8,128)} async-done(((f32[1024,256]{1,0:T(8,128)}), f32[64,256]{1,0:T(8,128)}) %reduce-scatter.24.cloned.1.call-update) | async-done | bytes 65552 | tf_op jit(solution)/shard_map/reduce_scatter | solution.py:249
  608.0 79.7 %reduce-scatter.20.cloned.1.call-done = f32[64,512]{1,0:T(8,128)} async-done(((f32[1024,512]{1,0:T(8,128)}), f32[64,512]{1,0:T(8,128)}) %reduce-scatter.20.cloned.1.call-update) | async-done | bytes 131088 | tf_op jit(solution)/shard_map/reduce_scatter | solution.py:247
  687.7 80.6 %reduce-scatter.26.cloned.1.call-done = f32[64,512]{1,0:T(8,128)} async-done(((f32[1024,512]{1,0:T(8,128)}), f32[64,512]{1,0:T(8,128)}) %reduce-scatter.26.cloned.1.call-update) | async-done | bytes 131088 | tf_op jit(solution)/shard_map/reduce_scatter | solution.py:250
  768.2 174.3 %reduce-scatter.28.cloned.1.call-done = f32[64,2304]{1,0:T(8,128)} async-done(((f32[1024,2304]{1,0:T(8,128)}), f32[64,2304]{1,0:T(8,128)}) %reduce-scatter.28.cloned.1.call-update) | async-done | bytes 589840 | tf_op jit(solution)/shard_map/reduce_scatter | solution.py:251
  942.5 177.3 %reduce-scatter.30.cloned.1.call-done = f32[64,2304]{1,0:T(8,128)} async-done(((f32[1024,2304]{1,0:T(8,128)}), f32[64,2304]{1,0:T(8,128)}) %reduce-scatter.30.cloned.1.call-update) | async-done | bytes 589840 | tf_op jit(solution)/shard_map/reduce_scatter | solution.py:252
  1119.8 176.0 %reduce-scatter.32.cloned.1.call-done = f32[64,2304]{1,0:T(8,128)} async-done(((f32[1024,2304]{1,0:T(8,128)}), f32[64,2304]{1,0:T(8,128)}) %reduce-scatter.32.cloned.1.call-update) | async-done | bytes 589840 | tf_op jit(solution)/shard_map/reduce_scatter | solution.py:253
  (213 shorter events, 15.5 us)
Async XLA Ops:
  7.2 56.9 %copy-start.51 = (bf16[64,256]{1,0:T(8,128)(2,1)S(1)}, bf16[64,256]{1,0:T(8,128)(2,1)}, u32[]{:S(2)}) copy-start(bf16[64,256]{1,0:T(8,128)(2,1)} %param.22) | copy-start | bytes 98308
  7.2 98.3 %all-gather.6.cloned.1.call-start = ((), (), s32[]{:S(2)}) async-start(), calls=%async_computation.11 | async-start | bytes 1114112 | tf_op jit(solution)/shard_map/all_gather | solution.py:100
  7.9 119.4 %all-gather.8.cloned.1.call-start = ((), (), s32[]{:S(2)}) async-start(), calls=%async_computation.12 | async-start | bytes 1114112 | tf_op jit(solution)/shard_map/all_gather | solution.py:103
  8.7 128.9 %reduce-scatter.12.cloned.1.call-start = ((), (), s32[]{:S(2)}) async-start(), calls=%async_computation.13 | async-start | bytes 1572864 | tf_op jit(solution)/shard_map/reduce_scatter | solution.py:146
  13.5 91.2 %copy-start.63 = (f32[64]{0:T(128)S(1)}, f32[64]{0:T(128)}, u32[]{:S(2)}) copy-start(f32[64]{0:T(128)} %param.18) | copy-start | bytes 772
  63.6 43.5 %copy-start.14 = (f32[256,256]{0,1:T(8,128)}, f32[256,256]{0,1:T(8,128)S(1)}, u32[]{:S(2)}) copy-start(f32[256,256]{0,1:T(8,128)S(1)} %get-tuple-element.47) | copy-start | bytes 786436
  64.1 41.4 %copy-start.46 = (f32[256,4]{0,1:T(4,128)}, f32[256,4]{0,1:T(4,128)S(1)}, u32[]{:S(2)}) copy-start(f32[256,4]{0,1:T(4,128)S(1)} %add_rsqrt_fusion.1) | copy-start | bytes 12292
  103.4 2.0 copy-start.4
  104.6 3.0 copy-start.31
  104.7 3.0 copy-start.33
  104.8 2.7 copy-start.58
  107.7 1.6 copy-start.35
  107.7 1.6 copy-start.37
  109.9 17.4 %copy-start.30 = (bf16[4,64,2,256]{3,1,2,0:T(8,128)(2,1)}, bf16[4,64,2,256]{3,1,2,0:T(8,128)(2,1)S(1)}, u32[]{:S(2)}) copy-start(bf16[4,64,2,256]{3,1,2,0:T(8,128)(2,1)S(1)} %convolution_convert_fusion.2) | copy-start | bytes 786436
  127.3 5.3 copy-start.17
  130.1 7.5 copy-start.2
  130.1 8.8 copy-start.43
  130.1 92.2 %all-gather.10.cloned.1.call-start = ((), (), s32[]{:S(2)}) async-start(), calls=%async_computation.14 | async-start | bytes 5013504 | tf_op jit(solution)/shard_map/all_gather | solution.py:104
  130.7 173.8 %all-gather.12.cloned.1.call-start = ((), (), s32[]{:S(2)}) async-start(), calls=%async_computation.15 | async-start | bytes 5013504 | tf_op jit(solution)/shard_map/all_gather | solution.py:105
  131.3 255.3 %all-gather.14.cloned.1.call-start = ((), (), s32[]{:S(2)}) async-start(), calls=%async_computation.16 | async-start | bytes 5013504 | tf_op jit(solution)/shard_map/all_gather | solution.py:106
  131.8 275.2 %reduce-scatter.16.cloned.1.call-start = ((), (), s32[]{:S(2)}) async-start(), calls=%async_computation.18 | async-start | bytes 786432 | tf_op jit(solution)/shard_map/reduce_scatter | solution.py:182
  132.6 6.2 copy-start.56
  138.8 88.8 %copy-start.54 = (f32[128]{0:T(128)}, f32[128]{0:T(128)S(1)}, u32[]{:S(2)}) copy-start(f32[128]{0:T(128)S(1)} %add_rsqrt_fusion.2) | copy-start | bytes 1540
  393.4 4.7 copy-start.25
  393.4 4.7 copy-start.23
  393.4 4.7 copy-start.68
  398.1 2.3 copy-start.59
  400.4 59.4 %reduce-scatter.18.cloned.1.call-start = ((), (), s32[]{:S(2)}) async-start(), calls=%async_computation.19 | async-start | bytes 786432 | tf_op jit(solution)/shard_map/reduce_scatter | solution.py:238
  407.1 6.3 copy-start.12
  409.0 3.6 copy-start.66
  418.7 1.5 copy-start.16
  419.1 1.6 copy-start.32
  419.1 1.6 copy-start.34
  421.3 2.3 copy-start.29
  421.3 3.2 copy-start.15
  421.3 3.2 copy-start.47
  421.5 3.0 copy-start.64
  421.5 3.2 copy-start.65
  421.5 3.3 copy-start.11
  421.5 3.3 copy-start.53
  423.6 2.7 copy-start.13
  424.9 1.9 copy-start.27
  424.9 1.9 copy-start.9
  428.5 73.8 %reduce-scatter.14.cloned.1.call-start = ((), (), s32[]{:S(2)}) async-start(), calls=%async_computation.17 | async-start | bytes 786432 | tf_op jit(solution)/shard_map/reduce_scatter | solution.py:158
  428.6 5.0 copy-start.28
  433.5 97.3 %reduce-scatter.22.cloned.1.call-start = ((), (), s32[]{:S(2)}) async-start(), calls=%async_computation.21 | async-start | bytes 1114112 | tf_op jit(solution)/shard_map/reduce_scatter | solution.py:248
  435.0 173.0 %reduce-scatter.24.cloned.1.call-start = ((), (), s32[]{:S(2)}) async-start(), calls=%async_computation.22 | async-start | bytes 1114112 | tf_op jit(solution)/shard_map/reduce_scatter | solution.py:249
  436.4 2.0 copy-start.7
  436.4 251.3 %reduce-scatter.20.cloned.1.call-start = ((), (), s32[]{:S(2)}) async-start(), calls=%async_computation.20 | async-start | bytes 2228224 | tf_op jit(solution)/shard_map/reduce_scatter | solution.py:247
  438.3 3.0 copy-start.3
  438.3 3.0 copy-start.26
  438.3 329.9 %reduce-scatter.26.cloned.1.call-start = ((), (), s32[]{:S(2)}) async-start(), calls=%async_computation.23 | async-start | bytes 2228224 | tf_op jit(solution)/shard_map/reduce_scatter | solution.py:250
  441.3 501.2 %reduce-scatter.28.cloned.1.call-start = ((), (), s32[]{:S(2)}) async-start(), calls=%async_computation.24 | async-start | bytes 10027008 | tf_op jit(solution)/shard_map/reduce_scatter | solution.py:251
  446.5 1.4 copy-start.24
  446.5 673.3 %reduce-scatter.30.cloned.1.call-start = ((), (), s32[]{:S(2)}) async-start(), calls=%async_computation.25 | async-start | bytes 10027008 | tf_op jit(solution)/shard_map/reduce_scatter | solution.py:252
  452.9 1.4 copy-start.22
  452.9 842.9 %reduce-scatter.32.cloned.1.call-start = ((), (), s32[]{:S(2)}) async-start(), calls=%async_computation.26 | async-start | bytes 10027008 | tf_op jit(solution)/shard_map/reduce_scatter | solution.py:253
  459.4 1.9 copy-start.52
  459.4 42.9 %copy-start.18 = (bf16[128,1024]{1,0:T(8,128)(2,1)S(1)}, bf16[128,1024]{1,0:T(8,128)(2,1)}, u32[]{:S(2)}) copy-start(bf16[128,1024]{1,0:T(8,128)(2,1)} %param.27) | copy-start | bytes 786436
  459.4 42.9 %copy-start.19 = (bf16[128,1024]{1,0:T(8,128)(2,1)S(1)}, bf16[128,1024]{1,0:T(8,128)(2,1)}, u32[]{:S(2)}) copy-start(bf16[128,1024]{1,0:T(8,128)(2,1)} %reduce-scatter.16.cloned.1.call-done) | copy-start | bytes 786436
  459.4 42.9 %copy-start.44 = (f32[1024]{0:T(1024)S(1)}, f32[1024]{0:T(1024)}, u32[]{:S(2)}) copy-start(f32[1024]{0:T(1024)} %param.19) | copy-start | bytes 12292
  459.4 42.9 %copy-start.55 = (f32[128]{0:T(128)S(1)}, f32[128]{0:T(128)}, u32[]{:S(2)}) copy-start(f32[128]{0:T(128)} %copy-done.54) | copy-start | bytes 1540
  459.5 42.9 %copy-start.57 = (pred[128]{0:T(512)(128)(4,1)S(1)}, pred[128]{0:T(512)(128)(4,1)}, u32[]{:S(2)}) copy-start(pred[128]{0:T(512)(128)(4,1)} %copy-done.56) | copy-start | bytes 388
  459.5 42.9 %copy-start.67 = (f32[128]{0:T(128)S(1)}, f32[128]{0:T(128)}, u32[]{:S(2)}) copy-start(f32[128]{0:T(128)} %copy-done.66) | copy-start | bytes 1540
  (21 other events, 19.0 us)
Sparse Core Ops, SparseCore 0:
  10.8 59.4 all-gather.5
  73.0 54.2 all-gather.7
  130.2 7.3 reduce-scatter.11
  140.6 81.5 all-gather.9
  225.3 79.0 all-gather.11
  307.5 79.0 all-gather.13
  400.5 6.5 reduce-scatter.15
  428.6 9.1 reduce-scatter.17
  440.1 9.1 reduce-scatter.13
  452.0 78.8 reduce-scatter.21
  533.8 74.1 reduce-scatter.23
  610.7 76.9 reduce-scatter.19
  690.5 77.6 reduce-scatter.25
  774.3 168.1 reduce-scatter.27
  949.6 170.1 reduce-scatter.29
  1125.9 169.8 reduce-scatter.31
where the time goes:
time: 1300 us
  waiting for transfers between devices  1050 us (81%)
  blocking collectives  136 us (10%)
  matrix products  64.6 us (5%)
  other arithmetic  19.4 us (1%)
  local copies, waits for them, and re-layouts  16.6 us (1%)
  between operations  14.8 us (1%)
    reduce_scatter x1, waiting for transfers between devices, body(): lax.psum_scatter(grad_up, 'dp', scatter_dimension=0, tiled=True)  177 us
    reduce_scatter x1, waiting for transfers between devices, body(): lax.psum_scatter(grad_down, 'dp', scatter_dimension=0, tiled=True)  176 us
    reduce_scatter x1, waiting for transfers between devices, body(): lax.psum_scatter(grad_gate, 'dp', scatter_dimension=0, tiled=True)  174 us
    all_gather x1, waiting for transfers between devices, body(): lax.all_gather(shards[4], 'dp', axis=0, tiled=True)  81 us
    reduce_scatter x1, waiting for transfers between devices, body(): lax.psum_scatter(grad_out_proj, 'dp', scatter_dimension=0, tiled=True)  80.6 us
    reduce_scatter x1, waiting for transfers between devices, body(): lax.psum_scatter(grad_query, 'dp', scatter_dimension=0, tiled=True)  79.7 us
    reduce_scatter x1, waiting for transfers between devices, body(): lax.psum_scatter(grad_value, 'dp', scatter_dimension=0, tiled=True)  77.1 us
    all_gather x1, waiting for transfers between devices, body(): lax.all_gather(shards[5], 'dp', axis=0, tiled=True)  76.9 us
  transfers between devices with their start and end apart: 16, of which 13 were waited for; matrix products, arithmetic and copies ran while one was open for 5% of the time, Pallas kernels for 0%

commit v1 on v0

v1 whole, which is shorter than its diff:
```python
import jax
import jax.numpy as jnp
from jax import lax
from jax.sharding import PartitionSpec as P

HEAD_DIM = 64


epsilon = 1e-05
rope_base = 1000000.0
masked_score = -1e30


def inverse_rms(values):
    return lax.rsqrt(jnp.mean(values * values, axis=-1, keepdims=True) + epsilon)


def norm_back(grad_unit, unit, factor):
    return factor * (grad_unit - unit * jnp.mean(grad_unit * unit, axis=-1, keepdims=True))


def matmul(first_op, second_op):
    return jnp.dot(first_op, second_op, preferred_element_type=jnp.float32)


def matmul_nt(first_op, second_op):
    return lax.dot_general(
        first_op, second_op, (((1,), (1,)), ((), ())), preferred_element_type=jnp.float32
    )


def matmul_tn(first_op, second_op):
    return lax.dot_general(
        first_op, second_op, (((0,), (0,)), ((), ())), preferred_element_type=jnp.float32
    )


def seq_layout(seq_lengths, total_rows):
    ends = jnp.cumsum(seq_lengths, dtype=jnp.int32)
    starts = ends - seq_lengths
    row_ids = jnp.arange(total_rows, dtype=jnp.int32)
    segment = jnp.sum(
        (row_ids[:, None] >= ends[None, :]).astype(jnp.int32), axis=1, dtype=jnp.int32
    )
    slot_ids = jnp.arange(seq_lengths.shape[0], dtype=jnp.int32)
    picked = (segment[:, None] == slot_ids[None, :]).astype(jnp.int32)
    begin = (
        jnp.sum(picked * starts[None, :], axis=1, dtype=jnp.int32)
        + (segment == seq_lengths.shape[0]).astype(jnp.int32) * ends[-1]
    )
    allowed = (segment[:, None] == segment[None, :]) & (row_ids[:, None] >= row_ids[None, :])
    return (row_ids - begin, row_ids < ends[-1], allowed)


def rope_tables(position, head_size):
    half_dim = head_size // 2
    freqs = rope_base ** (-jnp.arange(half_dim, dtype=jnp.float32) * 2.0 / head_size)
    angles = position.astype(jnp.float32)[:, None] * freqs[None, :]
    return (jnp.cos(angles)[:, None, :], jnp.sin(angles)[:, None, :])


def rotate(values, cosine, sine):
    half_dim = values.shape[-1] // 2
    first_half = values[..., :half_dim]
    second_half = values[..., half_dim:]
    return jnp.concatenate(
        [first_half * cosine - second_half * sine, second_half * cosine + first_half * sine],
        axis=-1,
    )


def rotate_back(grads, cosine, sine):
    half_dim = grads.shape[-1] // 2
    first_half = grads[..., :half_dim]
    second_half = grads[..., half_dim:]
    return jnp.concatenate(
        [first_half * cosine + second_half * sine, second_half * cosine - first_half * sine],
        axis=-1,
    )


PLANE = 4


def send_plane(values, mask):
    count = lax.axis_size("dp")
    return lax.ppermute(values, "dp", [(i, i ^ mask) for i in range(count)])


def send_deep(values, step):
    count = lax.axis_size("dp")
    return lax.ppermute(values, "dp", [(i, (i + PLANE * step) % count) for i in range(count)])


def swap_cores(values):
    return lax.ppermute(values, "tensor", [(0, 1), (1, 0)])


def gather_weight(pieces):
    dp = lax.axis_index("dp")
    place, depth = dp % PLANE, dp // PLANE
    layers = lax.axis_size("dp") // PLANE
    _, rows, columns = pieces.shape
    plane = jnp.zeros((PLANE, rows, columns), pieces.dtype)
    for mask in range(PLANE):
        part = lax.dynamic_index_in_dim(pieces, place ^ mask, 0, keepdims=True)
        if mask:
            part = send_plane(part, mask)
        plane = lax.dynamic_update_slice(plane, part, (place ^ mask, 0, 0))
    plane = plane.reshape(1, PLANE * rows, columns)
    whole = jnp.zeros((layers, PLANE * rows, columns), pieces.dtype)
    for step in range(layers):
        part = send_deep(plane, step) if step else plane
        whole = lax.dynamic_update_slice(whole, part, ((depth - step) % layers, 0, 0))
    return whole.reshape(layers * PLANE * rows, columns)


def scatter_weight(partial):
    dp = lax.axis_index("dp")
    place, depth = dp % PLANE, dp // PLANE
    layers = lax.axis_size("dp") // PLANE
    all_rows, columns = partial.shape
    rows = all_rows // layers // PLANE
    partial = partial.reshape(layers, PLANE * rows, columns)
    low = partial.astype(jnp.bfloat16)
    total = lax.dynamic_index_in_dim(partial, depth, 0, keepdims=False)
    for step in range(1, layers):
        part = lax.dynamic_index_in_dim(low, (depth + step) % layers, 0, keepdims=False)
        total = total + send_deep(part, step).astype(jnp.float32)
    total = total.reshape(PLANE, rows, columns)
    low = total.astype(jnp.bfloat16)
    result = jnp.zeros((PLANE, rows, columns), jnp.float32)
    for mask in range(PLANE):
        if mask:
            part = lax.dynamic_index_in_dim(low, place ^ mask, 0, keepdims=True)
            part = send_plane(part, mask).astype(jnp.float32)
        else:
            part = lax.dynamic_index_in_dim(total, place, 0, keepdims=True)
        result = lax.dynamic_update_slice(result, part, (place ^ mask, 0, 0))
    return result.transpose(1, 0, 2)


def gather_rows(local):
    parts = [local] + [send_plane(local, mask) for mask in range(1, PLANE)]
    half = jnp.stack(parts)
    return lax.all_gather(half, "tensor", axis=0, tiled=False)


def scatter_rows(partial, rows):
    core = lax.axis_index("tensor")
    partial = partial.reshape(2, PLANE, rows, partial.shape[-1])
    other = lax.dynamic_index_in_dim(partial, 1 - core, 0, keepdims=False).astype(jnp.bfloat16)
    mine = lax.dynamic_index_in_dim(partial, core, 0, keepdims=False)
    chip = mine + swap_cores(other).astype(jnp.float32)
    low = chip.astype(jnp.bfloat16)
    total = chip[0]
    for mask in range(1, PLANE):
        total = total + send_plane(low[mask], mask).astype(jnp.float32)
    return total


def sum_all(values):
    dp = lax.axis_index("dp")
    layers = lax.axis_size("dp") // PLANE
    depth = dp // PLANE
    values = values + swap_cores(values)
    first = values + send_plane(values, 1)
    both = first + send_plane(first, 2)
    every = jnp.zeros((layers,) + both.shape, both.dtype)
    for step in range(layers):
        part = send_deep(both, step) if step else both
        every = lax.dynamic_update_slice(every, part[None], ((depth - step) % layers,) + (0,) * both.ndim)
    return jnp.sum(every, axis=0)


def by_group(values):
    values = values.reshape(2, PLANE, -1, values.shape[-1])
    return values.transpose(1, 0, 2, 3).reshape(PLANE, -1, values.shape[-1])


def by_row(values):
    values = values.reshape(PLANE, 2, -1, values.shape[-1])
    return values.transpose(1, 0, 2, 3).reshape(-1, values.shape[-1])


def split_places(weight):
    rows, columns = weight.shape
    return weight.reshape(rows, PLANE, columns // PLANE).transpose(1, 0, 2)


def body(
    tokens,
    lengths,
    attn_gain,
    query_gain,
    key_gain,
    ffn_gain,
    w_query,
    w_key,
    w_value,
    w_out,
    w_gate,
    w_up,
    w_down,
    cotangent,
):
    tensor_index = lax.axis_index("tensor")
    local_rows = tokens.shape[0]
    total_rows = local_rows * lax.axis_size("tensor")
    q_cols = w_query.shape[1] // PLANE
    kv_cols = w_key.shape[1] // PLANE
    ff_cols = w_gate.shape[1] // PLANE
    local_kv = kv_cols // HEAD_DIM
    share = q_cols // kv_cols
    score_scale = HEAD_DIM ** (-0.5)

    inputs = tokens.astype(jnp.float32)
    factor_a = inverse_rms(inputs)
    unit_a = inputs * factor_a
    normed = gather_rows((unit_a * attn_gain).astype(jnp.bfloat16)).reshape(-1, tokens.shape[1])
    attn_weight = gather_weight(
        jnp.concatenate([split_places(w) for w in (w_query, w_key, w_value, w_out)], axis=2)
    )
    full_qkv = attn_weight[:, : q_cols + 2 * kv_cols]
    full_out = attn_weight[:, q_cols + 2 * kv_cols :]

    all_lengths = jnp.concatenate([lengths] + [send_plane(lengths, m) for m in range(1, PLANE)])
    position, live, allowed = jax.vmap(lambda one: seq_layout(one, total_rows))(all_lengths)
    live_local = lax.dynamic_slice_in_dim(live[0], tensor_index * local_rows, local_rows)
    cosine, sine = jax.vmap(lambda one: rope_tables(one, HEAD_DIM))(position)
    grad_out = jnp.where(live_local[:, None], cotangent, jnp.zeros_like(cotangent))
    grad_rows = gather_rows(grad_out).reshape(-1, tokens.shape[1])
    gate_up = gather_weight(
        jnp.concatenate([split_places(w) for w in (w_gate, w_up)], axis=2)
    )
    full_down = gather_weight(split_places(w_down))

    pre = by_group(matmul(normed, full_qkv))
    query_pre = pre[..., :q_cols].reshape(PLANE, total_rows, local_kv * share, HEAD_DIM)
    key_pre = pre[..., q_cols : q_cols + kv_cols].reshape(PLANE, total_rows, local_kv, HEAD_DIM)
    value_low = (
        pre[..., q_cols + kv_cols :]
        .astype(jnp.bfloat16)
        .reshape(PLANE, total_rows, local_kv, HEAD_DIM)
    )
    factor_q = inverse_rms(query_pre)
    unit_q = query_pre * factor_q
    factor_k = inverse_rms(key_pre)
    unit_k = key_pre * factor_k
    query_low = rotate(unit_q * query_gain, cosine, sine).astype(jnp.bfloat16)
    key_low = rotate(unit_k * key_gain, cosine, sine).astype(jnp.bfloat16)
    grouped = query_low.reshape(PLANE, total_rows, local_kv, share, HEAD_DIM)
    scores = (
        jnp.einsum("bqgjd,bkgd->bgjqk", grouped, key_low, preferred_element_type=jnp.float32)
        * score_scale
    )
    scores = jnp.where(allowed[:, None, None], scores, masked_score)
    top = jnp.max(scores, axis=-1, keepdims=True)
    expd = jnp.exp(scores - top)
    totals = jnp.sum(expd, axis=-1, keepdims=True)
    probs = expd / totals
    probs_low = probs.astype(jnp.bfloat16)
    mixed = jnp.einsum(
        "bgjqk,bkgd->bqgjd", probs_low, value_low, preferred_element_type=jnp.float32
    )
    mixed_low = by_row(mixed.astype(jnp.bfloat16).reshape(PLANE, total_rows, q_cols))
    hidden = inputs + scatter_rows(matmul_nt(mixed_low, full_out), local_rows)
    factor_b = inverse_rms(hidden)
    unit_b = hidden * factor_b
    normed2 = gather_rows((unit_b * ffn_gain).astype(jnp.bfloat16)).reshape(-1, tokens.shape[1])

    both = matmul(normed2, gate_up)
    gate, up_proj = both[:, :ff_cols], both[:, ff_cols:]
    sigma = jax.nn.sigmoid(gate)
    silu_gate = gate * sigma
    act_low = (silu_gate * up_proj).astype(jnp.bfloat16)
    ffn_branch = scatter_rows(matmul_nt(act_low, full_down), local_rows)
    block_out = (hidden + ffn_branch).astype(jnp.bfloat16)

    d_act = matmul(grad_rows, full_down)
    own_down = scatter_weight(matmul_tn(grad_rows, act_low))
    d_gate = (d_act * up_proj * sigma * (1.0 + gate * (1.0 - sigma))).astype(jnp.bfloat16)
    d_up = (d_act * silu_gate).astype(jnp.bfloat16)
    d_both = jnp.concatenate([d_gate, d_up], axis=1)
    d_normed2 = scatter_rows(matmul_nt(d_both, gate_up), local_rows)
    own_both = scatter_weight(matmul_tn(normed2, d_both))
    gain_ffn = jnp.sum(d_normed2 * unit_b, axis=0)
    d_hidden = grad_out.astype(jnp.float32) + norm_back(d_normed2 * ffn_gain, unit_b, factor_b)
    hidden_rows = gather_rows(d_hidden.astype(jnp.bfloat16)).reshape(-1, tokens.shape[1])
    grad_out_proj = matmul_tn(hidden_rows, mixed_low)
    d_mixed = by_group(matmul(hidden_rows, full_out).astype(jnp.bfloat16)).reshape(
        PLANE, total_rows, local_kv, share, HEAD_DIM
    )
    d_value = jnp.einsum(
        "bgjqk,bqgjd->bkgd", probs_low, d_mixed, preferred_element_type=jnp.float32
    )
    d_value_low = d_value.astype(jnp.bfloat16).reshape(PLANE, total_rows, kv_cols)
    d_probs = jnp.einsum("bqgjd,bkgd->bgjqk", d_mixed, value_low, preferred_element_type=jnp.float32)
    centre = jnp.sum(probs * d_probs, axis=-1, keepdims=True)
    d_scores = (probs * (d_probs - centre)).astype(jnp.bfloat16)
    d_query_rot = jnp.einsum(
        "bgjqk,bkgd->bqgjd", d_scores, key_low, preferred_element_type=jnp.float32
    )
    d_query_rot = (
        d_query_rot.reshape(PLANE, total_rows, local_kv * share, HEAD_DIM) * score_scale
    )
    d_key_rot = (
        jnp.einsum("bgjqk,bqgjd->bkgd", d_scores, grouped, preferred_element_type=jnp.float32)
        * score_scale
    )
    turned_q = rotate_back(d_query_rot, cosine, sine)
    turned_k = rotate_back(d_key_rot, cosine, sine)
    gain_query = jnp.sum(turned_q * unit_q, axis=(0, 1, 2))
    gain_key = jnp.sum(turned_k * unit_k, axis=(0, 1, 2))
    d_query = (
        norm_back(turned_q * query_gain, unit_q, factor_q)
        .astype(jnp.bfloat16)
        .reshape(PLANE, total_rows, q_cols)
    )
    d_key = (
        norm_back(turned_k * key_gain, unit_k, factor_k)
        .astype(jnp.bfloat16)
        .reshape(PLANE, total_rows, kv_cols)
    )
    d_qkv = by_row(jnp.concatenate([d_query, d_key, d_value_low], axis=2))
    d_normed = scatter_rows(matmul_nt(d_qkv, full_qkv), local_rows)
    own_attn = scatter_weight(
        jnp.concatenate([matmul_tn(normed, d_qkv), grad_out_proj], axis=1)
    )
    gain_attn = jnp.sum(d_normed * unit_a, axis=0)
    grad_tokens = d_hidden + norm_back(d_normed * attn_gain, unit_a, factor_a)
    gains = sum_all(jnp.concatenate([gain_attn, gain_ffn, gain_query, gain_key]))
    width = tokens.shape[1]

    def joined(part):
        return part.reshape(part.shape[0], -1)

    marks = (q_cols, q_cols + kv_cols, q_cols + 2 * kv_cols)
    return (
        block_out,
        grad_tokens,
        gains[:width],
        gains[2 * width : 2 * width + HEAD_DIM],
        gains[2 * width + HEAD_DIM :],
        gains[width : 2 * width],
        joined(own_attn[..., : marks[0]]),
        joined(own_attn[..., marks[0] : marks[1]]),
        joined(own_attn[..., marks[1] : marks[2]]),
        joined(own_attn[..., marks[2] :]),
        joined(own_both[..., :ff_cols]),
        joined(own_both[..., ff_cols:]),
        joined(own_down),
    )


def solution(mesh):
    placed = (
        P(("dp", "tensor"), None),
        P("dp", None),
        P(),
        P(),
        P(),
        P(),
        P("dp", "tensor"),
        P("dp", "tensor"),
        P("dp", "tensor"),
        P("dp", "tensor"),
        P("dp", "tensor"),
        P("dp", "tensor"),
        P("dp", "tensor"),
        P(("dp", "tensor"), None),
    )
    return jax.shard_map(
        body,
        mesh=mesh,
        in_specs=placed,
        out_specs=(
            P(("dp", "tensor"), None),
            P(("dp", "tensor"), None),
            P(),
            P(),
            P(),
            P(),
            P("dp", "tensor"),
            P("dp", "tensor"),
            P("dp", "tensor"),
            P("dp", "tensor"),
            P("dp", "tensor"),
            P("dp", "tensor"),
            P("dp", "tensor"),
        ),
        check_vma=False,
    )
```

time: 1300 us -> 477 us (0.37)
  waiting for transfers between devices: 1050 us -> 108 us
  blocking collectives: 136 us -> 0 us
  starting transfers between devices: 0.65 us -> 129 us
  local copies, waits for them, and re-layouts: 16.6 us -> 136 us
  matrix products: 64.6 us -> 35.7 us
  other arithmetic: 19.4 us -> 43.2 us
    reduce_scatter x11 -> x0, waiting for transfers between devices: 795 us -> none  [the longest x1 177 us: body(): lax.psum_scatter(grad_up, 'dp', scatter_dimension=0, tiled=True)]
    all_gather x5 -> x4, waiting for transfers between devices: 252 us -> 0.03 us  [gather_rows(): return lax.all_gather(half, 'tensor', axis=0, tiled=False)]
    ppermute x0 -> x73, starting transfers between devices: none -> 128 us  [the longest x21 69.5 us: send_deep(): lax.ppermute(values, 'dp', [(i, (i + PLANE * step) % count) for i in rang...]
    ppermute x0 -> x73, waiting for transfers between devices: none -> 108 us  [the longest x47 61 us: send_plane(): return lax.ppermute(values, 'dp', [(i, i ^ mask) for i in range(count)])]
    all_gather x6 -> x0, blocking collectives: 95.2 us -> none  [the longest x1 46.6 us: body(): lax.all_gather(shards[1], 'dp', axis=0, tiled=True)]
    dynamic_update_slice x0 -> x38, local copies, waits for them, and re-layouts: none -> 61.3 us  [the longest x12 38.1 us: gather_weight(): lax.dynamic_update_slice(whole, part, ((depth - step) % layers, 0, 0))]
    psum x1 -> x0, blocking collectives: 41 us -> none  [body(): lax.psum((gain_attn, gain_query, gain_key, gain_ffn), ('dp', 'tensor'))]
    reshape x0 -> x19, local copies, waits for them, and re-layouts: none -> 26.5 us  [the longest x6 7.05 us: joined(): return part.reshape(part.shape[0], -1)]
  transfers between devices with their start and end apart: 16 -> 77, of which waited for: 13 -> 33; matrix products, arithmetic and copies ran while one was open for 5% -> 32% of each run, Pallas kernels for 0% -> 0%
where the time goes in v1:
time: 477 us; the launch traced here: 468 us
  local copies, waits for them, and re-layouts  136 us (29%)
  starting transfers between devices  129 us (27%)
  waiting for transfers between devices  108 us (23%)
  other arithmetic  43.2 us (9%)
  matrix products  35.7 us (7%)
  between operations  15.9 us (3%)
    ppermute x21, starting transfers between devices, send_deep(): lax.ppermute(values, 'dp', [(i, (i + PLANE * step) % count) for i in rang...  69.5 us
    ppermute x47, waiting for transfers between devices, send_plane(): return lax.ppermute(values, 'dp', [(i, i ^ mask) for i in range(count)])  61 us
    ppermute x47, starting transfers between devices, send_plane(): return lax.ppermute(values, 'dp', [(i, i ^ mask) for i in range(count)])  58.6 us
    ppermute x21, waiting for transfers between devices, send_deep(): lax.ppermute(values, 'dp', [(i, (i + PLANE * step) % count) for i in rang...  46.8 us
    dynamic_update_slice x12, local copies, waits for them, and re-layouts, gather_weight(): lax.dynamic_update_slice(whole, part, ((depth - step) % layers, 0, 0))  38.1 us
    unnamed x152, local copies, waits for them, and re-layouts  14.2 us
    dot_general x4, matrix products, matmul(): return jnp.dot(first_op, second_op, preferred_element_type=jnp.float32)  13.5 us
    dynamic_update_slice x13, local copies, waits for them, and re-layouts, gather_weight(): plane = lax.dynamic_update_slice(plane, part, (place ^ mask, 0, 0))  12.7 us
  transfers between devices with their start and end apart: 77, of which 33 were waited for; matrix products, arithmetic and copies ran while one was open for 32% of the time, Pallas kernels for 0%

profile of v1, /device:TPU:0, one launch (start us, length us, event | category | flops | bytes accessed | tf_op | source)
XLA Modules:
  0.0 467.7 jit_solution(12543254457503569443)
XLA Ops:
  9.4 3.0 collective-permute-start
  22.7 3.2 collective-permute-done.10
  25.9 2.0 collective-permute-start.3
  34.1 2.7 collective-permute-done.5
  38.9 2.7 collective-permute-start.7
  44.4 5.6 %collective-permute-done.7 = bf16[1,256,384]{2,1,0:T(8,128)(2,1)S(1)} collective-permute-done((bf16[1,256,384]{2,1,0:T(8,128)(2,1)S(1)}, bf16[1,256,384]{2,1,0:T(8,128)(2,1)S(1)}, u32[]{:S(2)}, u32[]{:S(2)}) %collective-permute-start.7) | collective-permute-done | bytes 196640 | tf_op jit(solution)/shard_map/ppermute | solution.py:92
  50.1 2.6 convolution_bitcast_fusion.1
  75.3 2.9 collective-permute-done.36
  78.2 2.2 collective-permute-done.37
  80.4 2.3 pad_maximum_fusion.4
  83.0 2.3 fusion.108
  85.7 2.3 collective-permute-start.14
  88.9 3.4 fusion.59
  92.4 2.3 collective-permute-done.13
  94.7 4.0 collective-permute-done.14
  112.7 2.6 collective-permute-done.18
  115.3 2.2 pad_maximum_fusion.3
  124.3 3.4 collective-permute-done.20
  131.3 3.1 collective-permute-start.22
  138.8 3.8 collective-permute-start.30
  145.3 7.5 %dynamic_update_slice.140 = bf16[4,256,576]{1,0,2:T(4,128)(2,1)S(1)} dynamic-update-slice(bf16[4,256,576]{1,0,2:T(4,128)(2,1)S(1)} %broadcast_in_dim.58, bf16[1,256,576]{1,0,2:T(2,128)(2,1)S(1)} %copy.196, s32[]{:T(128)S(6)} %select_n.234, s32[]{:T(128)} %constant.286.clone.1, s32[]{:T(128)} %constant.286.clone.1) | dynamic-update-slice | bytes 589828 | tf_op jit(solution)/shard_map/dynamic_update_slice | solution.py:114
  152.8 4.3 collective-permute-done.28
  162.6 7.5 %dynamic_update_slice.141 = bf16[4,256,576]{1,0,2:T(4,128)(2,1)S(1)} dynamic-update-slice(bf16[4,256,576]{1,0,2:T(4,128)(2,1)S(1)} %dynamic_update_slice.140, bf16[1,256,576]{1,0,2:T(2,128)(2,1)S(1)} %copy.197, s32[]{:T(128)S(6)} %select_n.236, s32[]{:T(128)} %constant.286.clone.1, s32[]{:T(128)} %constant.286.clone.1) | dynamic-update-slice | bytes 589828 | tf_op jit(solution)/shard_map/dynamic_update_slice | solution.py:114
  170.1 19.0 %collective-permute-done.29 = bf16[1,256,576]{2,1,0:T(8,128)(2,1)} collective-permute-done((bf16[1,256,576]{2,1,0:T(8,128)(2,1)}, bf16[1,256,576]{2,1,0:T(8,128)(2,1)}, u32[]{:S(2)}, u32[]{:S(2)}) %collective-permute-start.29) | collective-permute-done | bytes 294944 | tf_op jit(solution)/shard_map/ppermute | solution.py:92
  190.9 7.5 %dynamic_update_slice.142 = bf16[4,256,576]{1,0,2:T(4,128)(2,1)S(1)} dynamic-update-slice(bf16[4,256,576]{1,0,2:T(4,128)(2,1)S(1)} %dynamic_update_slice.141, bf16[1,256,576]{1,0,2:T(2,128)(2,1)S(1)} %copy.198, s32[]{:T(128)S(6)} %select_n.238, s32[]{:T(128)} %constant.286.clone.1, s32[]{:T(128)} %constant.286.clone.1) | dynamic-update-slice | bytes 589828 | tf_op jit(solution)/shard_map/dynamic_update_slice | solution.py:114
  200.1 7.5 %dynamic_update_slice.143 = bf16[4,256,576]{1,0,2:T(4,128)(2,1)S(1)} dynamic-update-slice(bf16[4,256,576]{1,0,2:T(4,128)(2,1)S(1)} %dynamic_update_slice.142, bf16[1,256,576]{1,0,2:T(2,128)(2,1)S(1)} %copy.199, s32[]{:T(128)S(6)} %select_n.240, s32[]{:T(128)} %constant.286.clone.1, s32[]{:T(128)} %constant.286.clone.1) | dynamic-update-slice | bytes 589828 | tf_op jit(solution)/shard_map/dynamic_update_slice | solution.py:114
  217.5 4.0 copy.223
  221.5 3.9 copy.220
  225.4 5.3 %fusion.117 = f32[1024,1152]{1,0:T(8,128)S(1)} fusion(bf16[1024,1024]{1,0:T(8,128)(2,1)} %bitcast.396, bf16[1024,1152]{1,0:T(8,128)(2,1)} %bitcast.47), kind=kOutput, calls=%fused_computation.281 | convolution fusion | flops 2415919104 | bytes 9175040 | tf_op jit(solution)/shard_map/dot_general | solution.py:23
  230.8 2.4 multiply_convert_fusion.1
  234.8 19.2 %collective-permute-start.67 = (bf16[256,576]{0,1:T(8,128)(2,1)S(1)}, bf16[256,576]{0,1:T(8,128)(2,1)S(1)}, u32[]{:S(2)}, u32[]{:S(2)}) collective-permute-start(bf16[256,576]{0,1:T(8,128)(2,1)S(1)} %get-tuple-element.39), channel_id=1, source_target_pairs={{0,8},{2,10},{4,12},{6,14},{8,16},{10,18},{12,20},{14,22},{16,24},... | collective-permute-start | bytes 884744 | tf_op jit(solution)/shard_map/ppermute | solution.py:92
  254.0 3.9 collective-permute-start.68
  258.7 4.6 fusion.118
  270.3 4.5 fusion.115
  276.7 2.2 collective-permute-start.41
  280.2 4.5 collective-permute-done.39
  286.7 2.1 collective-permute-done.41
  292.6 9.3 %collective-permute-done.69 = bf16[256,576]{0,1:T(8,128)(2,1)S(1)} collective-permute-done((bf16[256,576]{0,1:T(8,128)(2,1)S(1)}, bf16[256,576]{0,1:T(8,128)(2,1)S(1)}, u32[]{:S(2)}, u32[]{:S(2)}) %collective-permute-start.69) | collective-permute-done | bytes 294944 | tf_op jit(solution)/shard_map/ppermute | solution.py:92
  308.3 7.9 %collective-permute-start.63 = (bf16[256,1152]{1,0:T(8,128)(2,1)}, bf16[256,1152]{1,0:T(8,128)(2,1)}, u32[]{:S(2)}, u32[]{:S(2)}) collective-permute-start(bf16[256,1152]{1,0:T(8,128)(2,1)} %get-tuple-element.35), channel_id=1, source_target_pairs={{0,24},{2,26},{4,28},{6,30},{8,0},{10,2},{12,4},{14,6},{16,8},{18,... | collective-permute-start | bytes 1769480 | tf_op jit(solution)/shard_map/ppermute | solution.py:92
  316.2 3.5 collective-permute-start.44
  320.3 3.7 dynamic_update_slice.159
  325.5 2.2 pad_maximum_fusion.5
  327.8 3.1 collective-permute-done.62
  330.9 2.1 fusion.12
  334.5 2.2 collective-permute-start.66
  336.8 2.3 collective-permute-done.64
  342.1 2.3 dynamic_update_slice.155
  345.6 2.3 reshape.450
  349.1 4.1 fusion.107
  353.3 3.1 convolution_convert_fusion
  372.8 2.7 fusion.56
  377.3 2.0 reshape.443
  382.9 11.0 %collective-permute-start.55 = (bf16[256,384]{1,0:T(8,128)(2,1)}, bf16[256,384]{1,0:T(8,128)(2,1)}, u32[]{:S(2)}, u32[]{:S(2)}) collective-permute-start(bf16[256,384]{1,0:T(8,128)(2,1)} %get-tuple-element.56), channel_id=1, source_target_pairs={{0,8},{2,10},{4,12},{6,14},{8,16},{10,18},{12,20},{14,22},{16,24},... | collective-permute-start | bytes 589832 | tf_op jit(solution)/shard_map/ppermute | solution.py:92
  393.9 2.8 collective-permute-start.56
  396.6 2.7 fusion.23
  402.8 4.2 collective-permute-done.56
  412.4 3.8 fusion.104
  422.3 2.4 dynamic_update_slice.151
  426.5 2.2 collective-permute-start.34
  428.8 10.7 %collective-permute-done.47 = bf16[128,1024]{1,0:T(8,128)(2,1)} collective-permute-done((bf16[128,1024]{1,0:T(8,128)(2,1)S(1)}, bf16[128,1024]{1,0:T(8,128)(2,1)}, u32[]{:S(2)}, u32[]{:S(2)}) %collective-permute-start.47) | collective-permute-done | bytes 262176 | tf_op jit(solution)/shard_map/ppermute | solution.py:87
  447.0 2.8 collective-permute-done.51
  449.8 4.6 collective-permute-start.52
  454.3 2.4 collective-permute-start.54
  456.8 2.3 fusion.37
  (461 shorter events, 178.4 us)
Async XLA Ops:
  7.2 42.9 %all-gather.9.cloned.1.call-start = ((), (), s32[]{:S(2)}) async-start(), calls=%async_computation | async-start | bytes 3145728 | tf_op jit(solution)/shard_map/all_gather | solution.py:146
  9.4 21.7 %collective-permute-start = (bf16[128,1024]{1,0:T(8,128)(2,1)S(1)}, bf16[128,1024]{1,0:T(8,128)(2,1)S(1)}, u32[]{:S(2)}, u32[]{:S(2)}) collective-permute-start(bf16[128,1024]{1,0:T(8,128)(2,1)S(1)} %fusion.33), channel_id=1, source_target_pairs={{0,2},{2,0},{4,6},{6,4},{8,10},{10,8},{12,14},{14,12},{16,18},{18,... | collective-permute-start | bytes 786440 | tf_op jit(solution)/shard_map/ppermute | solution.py:87
  12.4 18.8 %collective-permute-start.1 = (bf16[128,1024]{1,0:T(8,128)(2,1)S(1)}, bf16[128,1024]{1,0:T(8,128)(2,1)S(1)}, u32[]{:S(2)}, u32[]{:S(2)}) collective-permute-start(bf16[128,1024]{1,0:T(8,128)(2,1)S(1)} %fusion.33), channel_id=1, source_target_pairs={{0,4},{2,6},{4,0},{6,2},{8,12},{10,14},{12,8},{14,10},{16,20},{18,... | collective-permute-start | bytes 786440 | tf_op jit(solution)/shard_map/ppermute | solution.py:87
  14.0 17.3 %collective-permute-start.2 = (bf16[128,1024]{1,0:T(8,128)(2,1)S(1)}, bf16[128,1024]{1,0:T(8,128)(2,1)S(1)}, u32[]{:S(2)}, u32[]{:S(2)}) collective-permute-start(bf16[128,1024]{1,0:T(8,128)(2,1)S(1)} %fusion.33), channel_id=1, source_target_pairs={{0,6},{2,4},{4,2},{6,0},{8,14},{10,12},{12,10},{14,8},{16,22},{18,... | collective-permute-start | bytes 786440 | tf_op jit(solution)/shard_map/ppermute | solution.py:87
  14.0 11.9 %collective-permute-start.10 = (s32[1,4]{1,0:T(1,128)}, s32[1,4]{1,0:T(1,128)S(1)}, u32[]{:S(2)}, u32[]{:S(2)}) collective-permute-start(s32[1,4]{1,0:T(1,128)} %param.15), channel_id=1, source_target_pairs={{0,4},{2,6},{4,0},{6,2},{8,12},{10,14},{12,8},{14,10},{16,20},{18,... | collective-permute-start | bytes 56 | tf_op jit(solution)/shard_map/ppermute | solution.py:87
  15.9 10.0 %collective-permute-start.11 = (s32[1,4]{1,0:T(1,128)}, s32[1,4]{1,0:T(1,128)S(1)}, u32[]{:S(2)}, u32[]{:S(2)}) collective-permute-start(s32[1,4]{1,0:T(1,128)} %param.15), channel_id=1, source_target_pairs={{0,6},{2,4},{4,2},{6,0},{8,14},{10,12},{12,10},{14,8},{16,22},{18,... | collective-permute-start | bytes 56 | tf_op jit(solution)/shard_map/ppermute | solution.py:87
  25.9 8.0 %collective-permute-start.3 = (bf16[1,64,384]{2,0,1:T(2,128)(2,1)S(1)}, bf16[1,64,384]{2,0,1:T(2,128)(2,1)S(1)}, u32[]{:S(2)}, u32[]{:S(2)}) collective-permute-start(bf16[1,64,384]{2,0,1:T(2,128)(2,1)S(1)} %get-tuple-element.94), channel_id=1, source_target_pairs={{0,2},{2,0},{4,6},{6,4},{8,10},{10,8},{12,14},{14,12},{16,18},{18,... | collective-permute-start | bytes 147464 | tf_op jit(solution)/shard_map/ppermute | solution.py:87
  32.4 185.1 %all-gather.13.cloned.1.call-start = ((), (), s32[]{:S(2)}) async-start(), calls=%async_computation.2 | async-start | bytes 3145728 | tf_op jit(solution)/shard_map/all_gather | solution.py:146
  36.8 7.6 %collective-permute-start.6 = (bf16[1,256,384]{2,1,0:T(8,128)(2,1)S(1)}, bf16[1,256,384]{2,1,0:T(8,128)(2,1)S(1)}, u32[]{:S(2)}, u32[]{:S(2)}) collective-permute-start(bf16[1,256,384]{2,1,0:T(8,128)(2,1)S(1)} %bitcast.412), channel_id=1, source_target_pairs={{0,8},{2,10},{4,12},{6,14},{8,16},{10,18},{12,20},{14,22},{16,24},... | collective-permute-start | bytes 589832 | tf_op jit(solution)/shard_map/ppermute | solution.py:92
  38.9 11.0 %collective-permute-start.7 = (bf16[1,256,384]{2,1,0:T(8,128)(2,1)S(1)}, bf16[1,256,384]{2,1,0:T(8,128)(2,1)S(1)}, u32[]{:S(2)}, u32[]{:S(2)}) collective-permute-start(bf16[1,256,384]{2,1,0:T(8,128)(2,1)S(1)} %bitcast.413), channel_id=1, source_target_pairs={{0,16},{2,18},{4,20},{6,22},{8,24},{10,26},{12,28},{14,30},{16,0},... | collective-permute-start | bytes 589832 | tf_op jit(solution)/shard_map/ppermute | solution.py:92
  41.6 8.4 %collective-permute-start.8 = (bf16[1,256,384]{2,1,0:T(8,128)(2,1)S(1)}, bf16[1,256,384]{2,1,0:T(8,128)(2,1)S(1)}, u32[]{:S(2)}, u32[]{:S(2)}) collective-permute-start(bf16[1,256,384]{2,1,0:T(8,128)(2,1)S(1)} %bitcast.414), channel_id=1, source_target_pairs={{0,24},{2,26},{4,28},{6,30},{8,0},{10,2},{12,4},{14,6},{16,8},{18,... | collective-permute-start | bytes 589832 | tf_op jit(solution)/shard_map/ppermute | solution.py:92
  63.6 19.4 %collective-permute-start.12 = (bf16[4,128,1024]{2,1,0:T(8,128)(2,1)}, bf16[4,128,1024]{2,1,0:T(8,128)(2,1)}, u32[]{:S(2)}, u32[]{:S(2)}) collective-permute-start(bf16[4,128,1024]{2,1,0:T(8,128)(2,1)} %fusion.20), channel_id=1, source_target_pairs={{0,1},{1,0},{2,3},{3,2},{4,5},{5,4},{6,7},{7,6},{8,9},{9,8},{10,11... | collective-permute-start | bytes 3145736 | tf_op jit(solution)/shard_map/ppermute | solution.py:96
  64.2 9.3 %collective-permute-start.35 = (bf16[128,1024]{1,0:T(8,128)(2,1)S(1)}, bf16[128,1024]{1,0:T(8,128)(2,1)}, u32[]{:S(2)}, u32[]{:S(2)}) collective-permute-start(bf16[128,1024]{1,0:T(8,128)(2,1)S(1)} %broadcast_select_fusion), channel_id=1, source_target_pairs={{0,2},{2,0},{4,6},{6,4},{8,10},{10,8},{12,14},{14,12},{16,18},{18,... | collective-permute-start | bytes 786440 | tf_op jit(solution)/shard_map/ppermute | solution.py:87
  65.2 13.0 %collective-permute-start.36 = (bf16[128,1024]{1,0:T(8,128)(2,1)S(1)}, bf16[128,1024]{1,0:T(8,128)(2,1)}, u32[]{:S(2)}, u32[]{:S(2)}) collective-permute-start(bf16[128,1024]{1,0:T(8,128)(2,1)S(1)} %broadcast_select_fusion), channel_id=1, source_target_pairs={{0,4},{2,6},{4,0},{6,2},{8,12},{10,14},{12,8},{14,10},{16,20},{18,... | collective-permute-start | bytes 786440 | tf_op jit(solution)/shard_map/ppermute | solution.py:87
  66.3 14.2 %collective-permute-start.37 = (bf16[128,1024]{1,0:T(8,128)(2,1)S(1)}, bf16[128,1024]{1,0:T(8,128)(2,1)}, u32[]{:S(2)}, u32[]{:S(2)}) collective-permute-start(bf16[128,1024]{1,0:T(8,128)(2,1)S(1)} %broadcast_select_fusion), channel_id=1, source_target_pairs={{0,6},{2,4},{4,2},{6,0},{8,14},{10,12},{12,10},{14,8},{16,22},{18,... | collective-permute-start | bytes 786440 | tf_op jit(solution)/shard_map/ppermute | solution.py:87
  69.0 48.5 %collective-permute-start.25 = (bf16[1,64,576]{2,1,0:T(8,128)(2,1)}, bf16[1,64,576]{2,1,0:T(8,128)(2,1)}, u32[]{:S(2)}, u32[]{:S(2)}) collective-permute-start(bf16[1,64,576]{2,1,0:T(8,128)(2,1)} %bitcast.371), channel_id=1, source_target_pairs={{0,2},{2,0},{4,6},{6,4},{8,10},{10,8},{12,14},{14,12},{16,18},{18,... | collective-permute-start | bytes 221192 | tf_op jit(solution)/shard_map/ppermute | solution.py:87
  73.4 47.4 %collective-permute-start.26 = (bf16[1,64,576]{2,1,0:T(8,128)(2,1)}, bf16[1,64,576]{2,1,0:T(8,128)(2,1)}, u32[]{:S(2)}, u32[]{:S(2)}) collective-permute-start(bf16[1,64,576]{2,1,0:T(8,128)(2,1)} %bitcast.370), channel_id=1, source_target_pairs={{0,4},{2,6},{4,0},{6,2},{8,12},{10,14},{12,8},{14,10},{16,20},{18,... | collective-permute-start | bytes 221192 | tf_op jit(solution)/shard_map/ppermute | solution.py:87
  82.7 138.8 %all-gather.11.cloned.1.call-start = ((), (), s32[]{:S(2)}) async-start(), calls=%async_computation.1 | async-start | bytes 3145728 | tf_op jit(solution)/shard_map/all_gather | solution.py:146
  85.4 9.3 %collective-permute-start.13 = (bf16[128,1024]{1,0:T(8,128)(2,1)S(1)}, bf16[128,1024]{1,0:T(8,128)(2,1)S(1)}, u32[]{:S(2)}, u32[]{:S(2)}) collective-permute-start(bf16[128,1024]{1,0:T(8,128)(2,1)S(1)} %get-tuple-element.53), channel_id=1, source_target_pairs={{0,2},{2,0},{4,6},{6,4},{8,10},{10,8},{12,14},{14,12},{16,18},{18,... | collective-permute-start | bytes 786440 | tf_op jit(solution)/shard_map/ppermute | solution.py:87
  85.7 13.0 %collective-permute-start.14 = (bf16[128,1024]{1,0:T(8,128)(2,1)S(1)}, bf16[128,1024]{1,0:T(8,128)(2,1)S(1)}, u32[]{:S(2)}, u32[]{:S(2)}) collective-permute-start(bf16[128,1024]{1,0:T(8,128)(2,1)S(1)} %get-tuple-element.55), channel_id=1, source_target_pairs={{0,4},{2,6},{4,0},{6,2},{8,12},{10,14},{12,8},{14,10},{16,20},{18,... | collective-permute-start | bytes 786440 | tf_op jit(solution)/shard_map/ppermute | solution.py:87
  88.0 10.7 %collective-permute-start.15 = (bf16[128,1024]{1,0:T(8,128)(2,1)S(1)}, bf16[128,1024]{1,0:T(8,128)(2,1)S(1)}, u32[]{:S(2)}, u32[]{:S(2)}) collective-permute-start(bf16[128,1024]{1,0:T(8,128)(2,1)S(1)} %get-tuple-element.54), channel_id=1, source_target_pairs={{0,6},{2,4},{4,2},{6,0},{8,14},{10,12},{12,10},{14,8},{16,22},{18,... | collective-permute-start | bytes 786440 | tf_op jit(solution)/shard_map/ppermute | solution.py:87
  99.2 8.9 %collective-permute-start.16 = (bf16[128,1024]{1,0:T(8,128)(2,1)S(1)}, bf16[128,1024]{1,0:T(8,128)(2,1)}, u32[]{:S(2)}, u32[]{:S(2)}) collective-permute-start(bf16[128,1024]{1,0:T(8,128)(2,1)S(1)} %multiply_convert_fusion.4), channel_id=1, source_target_pairs={{0,2},{2,0},{4,6},{6,4},{8,10},{10,8},{12,14},{14,12},{16,18},{18,... | collective-permute-start | bytes 786440 | tf_op jit(solution)/shard_map/ppermute | solution.py:87
  100.9 11.0 %collective-permute-start.17 = (bf16[128,1024]{1,0:T(8,128)(2,1)S(1)}, bf16[128,1024]{1,0:T(8,128)(2,1)}, u32[]{:S(2)}, u32[]{:S(2)}) collective-permute-start(bf16[128,1024]{1,0:T(8,128)(2,1)S(1)} %multiply_convert_fusion.4), channel_id=1, source_target_pairs={{0,4},{2,6},{4,0},{6,2},{8,12},{10,14},{12,8},{14,10},{16,20},{18,... | collective-permute-start | bytes 786440 | tf_op jit(solution)/shard_map/ppermute | solution.py:87
  101.2 14.1 %collective-permute-start.18 = (bf16[128,1024]{1,0:T(8,128)(2,1)S(1)}, bf16[128,1024]{1,0:T(8,128)(2,1)}, u32[]{:S(2)}, u32[]{:S(2)}) collective-permute-start(bf16[128,1024]{1,0:T(8,128)(2,1)S(1)} %multiply_convert_fusion.4), channel_id=1, source_target_pairs={{0,6},{2,4},{4,2},{6,0},{8,14},{10,12},{12,10},{14,8},{16,22},{18,... | collective-permute-start | bytes 786440 | tf_op jit(solution)/shard_map/ppermute | solution.py:87
  108.0 26.3 %collective-permute-start.27 = (bf16[1,64,576]{2,1,0:T(8,128)(2,1)}, bf16[1,64,576]{2,1,0:T(8,128)(2,1)}, u32[]{:S(2)}, u32[]{:S(2)}) collective-permute-start(bf16[1,64,576]{2,1,0:T(8,128)(2,1)} %bitcast.369), channel_id=1, source_target_pairs={{0,6},{2,4},{4,2},{6,0},{8,14},{10,12},{12,10},{14,8},{16,22},{18,... | collective-permute-start | bytes 221192 | tf_op jit(solution)/shard_map/ppermute | solution.py:87
  112.0 10.4 %collective-permute-start.19 = (bf16[1,64,1152]{2,0,1:T(2,128)(2,1)}, bf16[1,64,1152]{2,0,1:T(2,128)(2,1)S(1)}, u32[]{:S(2)}, u32[]{:S(2)}) collective-permute-start(bf16[1,64,1152]{2,0,1:T(2,128)(2,1)} %get-tuple-element.65), channel_id=1, source_target_pairs={{0,2},{2,0},{4,6},{6,4},{8,10},{10,8},{12,14},{14,12},{16,18},{18,... | collective-permute-start | bytes 442376 | tf_op jit(solution)/shard_map/ppermute | solution.py:87
  115.3 12.5 %collective-permute-start.20 = (bf16[1,64,1152]{2,0,1:T(2,128)(2,1)}, bf16[1,64,1152]{2,0,1:T(2,128)(2,1)S(1)}, u32[]{:S(2)}, u32[]{:S(2)}) collective-permute-start(bf16[1,64,1152]{2,0,1:T(2,128)(2,1)} %get-tuple-element.66), channel_id=1, source_target_pairs={{0,4},{2,6},{4,0},{6,2},{8,12},{10,14},{12,8},{14,10},{16,20},{18,... | collective-permute-start | bytes 442376 | tf_op jit(solution)/shard_map/ppermute | solution.py:87
  117.5 235.7 %all-gather.15.cloned.1.call-start = ((), (), s32[]{:S(2)}) async-start(), calls=%async_computation.3 | async-start | bytes 3145728 | tf_op jit(solution)/shard_map/all_gather | solution.py:146
  117.6 13.0 %collective-permute-start.21 = (bf16[1,64,1152]{2,0,1:T(2,128)(2,1)S(1)}, bf16[1,64,1152]{2,0,1:T(2,128)(2,1)S(1)}, u32[]{:S(2)}, u32[]{:S(2)}) collective-permute-start(bf16[1,64,1152]{2,0,1:T(2,128)(2,1)S(1)} %get-tuple-element.63), channel_id=1, source_target_pairs={{0,6},{2,4},{4,2},{6,0},{8,14},{10,12},{12,10},{14,8},{16,22},{18,... | collective-permute-start | bytes 442376 | tf_op jit(solution)/shard_map/ppermute | solution.py:87
  131.3 79.3 %collective-permute-start.22 = (bf16[1,256,1152]{2,1,0:T(8,128)(2,1)}, bf16[1,256,1152]{2,1,0:T(8,128)(2,1)}, u32[]{:S(2)}, u32[]{:S(2)}) collective-permute-start(bf16[1,256,1152]{2,1,0:T(8,128)(2,1)} %bitcast.46), channel_id=1, source_target_pairs={{0,8},{2,10},{4,12},{6,14},{8,16},{10,18},{12,20},{14,22},{16,24},... | collective-permute-start | bytes 1769480 | tf_op jit(solution)/shard_map/ppermute | solution.py:92
  135.9 21.2 %collective-permute-start.28 = (bf16[1,256,576]{2,1,0:T(8,128)(2,1)}, bf16[1,256,576]{2,1,0:T(8,128)(2,1)}, u32[]{:S(2)}, u32[]{:S(2)}) collective-permute-start(bf16[1,256,576]{2,1,0:T(8,128)(2,1)} %bitcast.49), channel_id=1, source_target_pairs={{0,8},{2,10},{4,12},{6,14},{8,16},{10,18},{12,20},{14,22},{16,24},... | collective-permute-start | bytes 884744 | tf_op jit(solution)/shard_map/ppermute | solution.py:92
  135.9 76.7 %collective-permute-start.23 = (bf16[1,256,1152]{2,1,0:T(8,128)(2,1)}, bf16[1,256,1152]{2,1,0:T(8,128)(2,1)}, u32[]{:S(2)}, u32[]{:S(2)}) collective-permute-start(bf16[1,256,1152]{2,1,0:T(8,128)(2,1)} %bitcast.46), channel_id=1, source_target_pairs={{0,16},{2,18},{4,20},{6,22},{8,24},{10,26},{12,28},{14,30},{16,0},... | collective-permute-start | bytes 1769480 | tf_op jit(solution)/shard_map/ppermute | solution.py:92
  137.5 51.6 %collective-permute-start.29 = (bf16[1,256,576]{2,1,0:T(8,128)(2,1)}, bf16[1,256,576]{2,1,0:T(8,128)(2,1)}, u32[]{:S(2)}, u32[]{:S(2)}) collective-permute-start(bf16[1,256,576]{2,1,0:T(8,128)(2,1)} %bitcast.49), channel_id=1, source_target_pairs={{0,16},{2,18},{4,20},{6,22},{8,24},{10,26},{12,28},{14,30},{16,0},... | collective-permute-start | bytes 884744 | tf_op jit(solution)/shard_map/ppermute | solution.py:92
  138.8 59.6 %collective-permute-start.30 = (bf16[1,256,576]{2,1,0:T(8,128)(2,1)}, bf16[1,256,576]{2,1,0:T(8,128)(2,1)}, u32[]{:S(2)}, u32[]{:S(2)}) collective-permute-start(bf16[1,256,576]{2,1,0:T(8,128)(2,1)} %bitcast.49), channel_id=1, source_target_pairs={{0,24},{2,26},{4,28},{6,30},{8,0},{10,2},{12,4},{14,6},{16,8},{18,... | collective-permute-start | bytes 884744 | tf_op jit(solution)/shard_map/ppermute | solution.py:92
  157.1 57.4 %collective-permute-start.24 = (bf16[1,256,1152]{2,1,0:T(8,128)(2,1)}, bf16[1,256,1152]{2,1,0:T(8,128)(2,1)}, u32[]{:S(2)}, u32[]{:S(2)}) collective-permute-start(bf16[1,256,1152]{2,1,0:T(8,128)(2,1)} %bitcast.46), channel_id=1, source_target_pairs={{0,24},{2,26},{4,28},{6,30},{8,0},{10,2},{12,4},{14,6},{16,8},{18,... | collective-permute-start | bytes 1769480 | tf_op jit(solution)/shard_map/ppermute | solution.py:92
  234.8 57.8 %collective-permute-start.67 = (bf16[256,576]{0,1:T(8,128)(2,1)S(1)}, bf16[256,576]{0,1:T(8,128)(2,1)S(1)}, u32[]{:S(2)}, u32[]{:S(2)}) collective-permute-start(bf16[256,576]{0,1:T(8,128)(2,1)S(1)} %get-tuple-element.39), channel_id=1, source_target_pairs={{0,8},{2,10},{4,12},{6,14},{8,16},{10,18},{12,20},{14,22},{16,24},... | collective-permute-start | bytes 884744 | tf_op jit(solution)/shard_map/ppermute | solution.py:92
  254.0 38.5 %collective-permute-start.68 = (bf16[256,576]{0,1:T(8,128)(2,1)S(1)}, bf16[256,576]{0,1:T(8,128)(2,1)S(1)}, u32[]{:S(2)}, u32[]{:S(2)}) collective-permute-start(bf16[256,576]{0,1:T(8,128)(2,1)S(1)} %get-tuple-element.41), channel_id=1, source_target_pairs={{0,16},{2,18},{4,20},{6,22},{8,24},{10,26},{12,28},{14,30},{16,0},... | collective-permute-start | bytes 884744 | tf_op jit(solution)/shard_map/ppermute | solution.py:92
  263.5 11.3 %collective-permute-start.38 = (bf16[4,128,1024]{2,1,0:T(8,128)(2,1)S(1)}, bf16[4,128,1024]{2,1,0:T(8,128)(2,1)S(1)}, u32[]{:S(2)}, u32[]{:S(2)}) collective-permute-start(bf16[4,128,1024]{2,1,0:T(8,128)(2,1)S(1)} %fusion.22), channel_id=1, source_target_pairs={{0,1},{1,0},{2,3},{3,2},{4,5},{5,4},{6,7},{7,6},{8,9},{9,8},{10,11... | collective-permute-start | bytes 3145736 | tf_op jit(solution)/shard_map/ppermute | solution.py:96
  275.4 9.3 %collective-permute-start.39 = (bf16[128,1024]{1,0:T(8,128)(2,1)S(1)}, bf16[128,1024]{1,0:T(8,128)(2,1)S(1)}, u32[]{:S(2)}, u32[]{:S(2)}) collective-permute-start(bf16[128,1024]{1,0:T(8,128)(2,1)S(1)} %get-tuple-element.47), channel_id=1, source_target_pairs={{0,2},{2,0},{4,6},{6,4},{8,10},{10,8},{12,14},{14,12},{16,18},{18,... | collective-permute-start | bytes 786440 | tf_op jit(solution)/shard_map/ppermute | solution.py:87
  275.8 9.8 %collective-permute-start.40 = (bf16[128,1024]{1,0:T(8,128)(2,1)S(1)}, bf16[128,1024]{1,0:T(8,128)(2,1)S(1)}, u32[]{:S(2)}, u32[]{:S(2)}) collective-permute-start(bf16[128,1024]{1,0:T(8,128)(2,1)S(1)} %get-tuple-element.49), channel_id=1, source_target_pairs={{0,4},{2,6},{4,0},{6,2},{8,12},{10,14},{12,8},{14,10},{16,20},{18,... | collective-permute-start | bytes 786440 | tf_op jit(solution)/shard_map/ppermute | solution.py:87
  276.7 12.2 %collective-permute-start.41 = (bf16[128,1024]{1,0:T(8,128)(2,1)S(1)}, bf16[128,1024]{1,0:T(8,128)(2,1)S(1)}, u32[]{:S(2)}, u32[]{:S(2)}) collective-permute-start(bf16[128,1024]{1,0:T(8,128)(2,1)S(1)} %get-tuple-element.48), channel_id=1, source_target_pairs={{0,6},{2,4},{4,2},{6,0},{8,14},{10,12},{12,10},{14,8},{16,22},{18,... | collective-permute-start | bytes 786440 | tf_op jit(solution)/shard_map/ppermute | solution.py:87
  284.7 17.1 %collective-permute-start.69 = (bf16[256,576]{0,1:T(8,128)(2,1)S(1)}, bf16[256,576]{0,1:T(8,128)(2,1)S(1)}, u32[]{:S(2)}, u32[]{:S(2)}) collective-permute-start(bf16[256,576]{0,1:T(8,128)(2,1)S(1)} %get-tuple-element.40), channel_id=1, source_target_pairs={{0,24},{2,26},{4,28},{6,30},{8,0},{10,2},{12,4},{14,6},{16,8},{18,... | collective-permute-start | bytes 884744 | tf_op jit(solution)/shard_map/ppermute | solution.py:92
  285.6 42.1 %collective-permute-start.61 = (bf16[256,1152]{1,0:T(8,128)(2,1)}, bf16[256,1152]{1,0:T(8,128)(2,1)}, u32[]{:S(2)}, u32[]{:S(2)}) collective-permute-start(bf16[256,1152]{1,0:T(8,128)(2,1)} %get-tuple-element.34), channel_id=1, source_target_pairs={{0,8},{2,10},{4,12},{6,14},{8,16},{10,18},{12,20},{14,22},{16,24},... | collective-permute-start | bytes 1769480 | tf_op jit(solution)/shard_map/ppermute | solution.py:92
  290.8 25.4 %collective-permute-start.42 = (bf16[128,1024]{1,0:T(8,128)(2,1)S(1)}, bf16[128,1024]{1,0:T(8,128)(2,1)}, u32[]{:S(2)}, u32[]{:S(2)}) collective-permute-start(bf16[128,1024]{1,0:T(8,128)(2,1)S(1)} %fusion.100), channel_id=1, source_target_pairs={{0,2},{2,0},{4,6},{6,4},{8,10},{10,8},{12,14},{14,12},{16,18},{18,... | collective-permute-start | bytes 786440 | tf_op jit(solution)/shard_map/ppermute | solution.py:87
  304.1 12.1 %collective-permute-start.72 = (bf16[1,64,576]{2,1,0:T(8,128)(2,1)S(1)}, bf16[1,64,576]{2,1,0:T(8,128)(2,1)S(1)}, u32[]{:S(2)}, u32[]{:S(2)}) collective-permute-start(bf16[1,64,576]{2,1,0:T(8,128)(2,1)S(1)} %get-tuple-element.78), channel_id=1, source_target_pairs={{0,6},{2,4},{4,2},{6,0},{8,14},{10,12},{12,10},{14,8},{16,22},{18,... | collective-permute-start | bytes 221192 | tf_op jit(solution)/shard_map/ppermute | solution.py:87
  307.2 23.7 %collective-permute-start.62 = (bf16[256,1152]{1,0:T(8,128)(2,1)}, bf16[256,1152]{1,0:T(8,128)(2,1)S(1)}, u32[]{:S(2)}, u32[]{:S(2)}) collective-permute-start(bf16[256,1152]{1,0:T(8,128)(2,1)} %get-tuple-element.36), channel_id=1, source_target_pairs={{0,16},{2,18},{4,20},{6,22},{8,24},{10,26},{12,28},{14,30},{16,0},... | collective-permute-start | bytes 1769480 | tf_op jit(solution)/shard_map/ppermute | solution.py:92
  308.3 22.6 %collective-permute-start.63 = (bf16[256,1152]{1,0:T(8,128)(2,1)}, bf16[256,1152]{1,0:T(8,128)(2,1)}, u32[]{:S(2)}, u32[]{:S(2)}) collective-permute-start(bf16[256,1152]{1,0:T(8,128)(2,1)} %get-tuple-element.35), channel_id=1, source_target_pairs={{0,24},{2,26},{4,28},{6,30},{8,0},{10,2},{12,4},{14,6},{16,8},{18,... | collective-permute-start | bytes 1769480 | tf_op jit(solution)/shard_map/ppermute | solution.py:92
  316.2 9.3 %collective-permute-start.43 = (bf16[128,1024]{1,0:T(8,128)(2,1)S(1)}, bf16[128,1024]{1,0:T(8,128)(2,1)}, u32[]{:S(2)}, u32[]{:S(2)}) collective-permute-start(bf16[128,1024]{1,0:T(8,128)(2,1)S(1)} %fusion.100), channel_id=1, source_target_pairs={{0,4},{2,6},{4,0},{6,2},{8,12},{10,14},{12,8},{14,10},{16,20},{18,... | collective-permute-start | bytes 786440 | tf_op jit(solution)/shard_map/ppermute | solution.py:87
  316.2 9.3 %collective-permute-start.44 = (bf16[128,1024]{1,0:T(8,128)(2,1)S(1)}, bf16[128,1024]{1,0:T(8,128)(2,1)}, u32[]{:S(2)}, u32[]{:S(2)}) collective-permute-start(bf16[128,1024]{1,0:T(8,128)(2,1)S(1)} %fusion.100), channel_id=1, source_target_pairs={{0,6},{2,4},{4,2},{6,0},{8,14},{10,12},{12,10},{14,8},{16,22},{18,... | collective-permute-start | bytes 786440 | tf_op jit(solution)/shard_map/ppermute | solution.py:87
  325.5 23.7 %collective-permute-start.31 = (bf16[4,128,1024]{2,1,0:T(8,128)(2,1)}, bf16[4,128,1024]{2,1,0:T(8,128)(2,1)}, u32[]{:S(2)}, u32[]{:S(2)}) collective-permute-start(bf16[4,128,1024]{2,1,0:T(8,128)(2,1)} %fusion.21), channel_id=1, source_target_pairs={{0,1},{1,0},{2,3},{3,2},{4,5},{5,4},{6,7},{7,6},{8,9},{9,8},{10,11... | collective-permute-start | bytes 3145736 | tf_op jit(solution)/shard_map/ppermute | solution.py:96
  333.2 7.8 %collective-permute-start.65 = (bf16[1,64,1152]{2,1,0:T(8,128)(2,1)S(1)}, bf16[1,64,1152]{2,1,0:T(8,128)(2,1)S(1)}, u32[]{:S(2)}, u32[]{:S(2)}) collective-permute-start(bf16[1,64,1152]{2,1,0:T(8,128)(2,1)S(1)} %get-tuple-element.68), channel_id=1, source_target_pairs={{0,4},{2,6},{4,0},{6,2},{8,12},{10,14},{12,8},{14,10},{16,20},{18,... | collective-permute-start | bytes 442376 | tf_op jit(solution)/shard_map/ppermute | solution.py:87
  382.9 19.9 %collective-permute-start.55 = (bf16[256,384]{1,0:T(8,128)(2,1)}, bf16[256,384]{1,0:T(8,128)(2,1)}, u32[]{:S(2)}, u32[]{:S(2)}) collective-permute-start(bf16[256,384]{1,0:T(8,128)(2,1)} %get-tuple-element.56), channel_id=1, source_target_pairs={{0,8},{2,10},{4,12},{6,14},{8,16},{10,18},{12,20},{14,22},{16,24},... | collective-permute-start | bytes 589832 | tf_op jit(solution)/shard_map/ppermute | solution.py:92
  393.9 13.1 %collective-permute-start.56 = (bf16[256,384]{1,0:T(8,128)(2,1)S(1)}, bf16[256,384]{1,0:T(8,128)(2,1)}, u32[]{:S(2)}, u32[]{:S(2)}) collective-permute-start(bf16[256,384]{1,0:T(8,128)(2,1)S(1)} %get-tuple-element.57), channel_id=1, source_target_pairs={{0,16},{2,18},{4,20},{6,22},{8,24},{10,26},{12,28},{14,30},{16,0},... | collective-permute-start | bytes 589832 | tf_op jit(solution)/shard_map/ppermute | solution.py:92
  396.6 10.4 %collective-permute-start.57 = (bf16[256,384]{1,0:T(8,128)(2,1)S(1)}, bf16[256,384]{1,0:T(8,128)(2,1)}, u32[]{:S(2)}, u32[]{:S(2)}) collective-permute-start(bf16[256,384]{1,0:T(8,128)(2,1)S(1)} %get-tuple-element.58), channel_id=1, source_target_pairs={{0,24},{2,26},{4,28},{6,30},{8,0},{10,2},{12,4},{14,6},{16,8},{18,... | collective-permute-start | bytes 589832 | tf_op jit(solution)/shard_map/ppermute | solution.py:92
  399.3 13.1 %collective-permute-start.45 = (bf16[4,128,1024]{2,1,0:T(8,128)(2,1)}, bf16[4,128,1024]{2,1,0:T(8,128)(2,1)}, u32[]{:S(2)}, u32[]{:S(2)}) collective-permute-start(bf16[4,128,1024]{2,1,0:T(8,128)(2,1)} %fusion.23), channel_id=1, source_target_pairs={{0,1},{1,0},{2,3},{3,2},{4,5},{5,4},{6,7},{7,6},{8,9},{9,8},{10,11... | collective-permute-start | bytes 3145736 | tf_op jit(solution)/shard_map/ppermute | solution.py:96
  400.2 54.1 %collective-permute-start.32 = (bf16[128,1024]{1,0:T(8,128)(2,1)}, bf16[128,1024]{1,0:T(8,128)(2,1)S(1)}, u32[]{:S(2)}, u32[]{:S(2)}) collective-permute-start(bf16[128,1024]{1,0:T(8,128)(2,1)} %get-tuple-element.50), channel_id=1, source_target_pairs={{0,2},{2,0},{4,6},{6,4},{8,10},{10,8},{12,14},{14,12},{16,18},{18,... | collective-permute-start | bytes 786440 | tf_op jit(solution)/shard_map/ppermute | solution.py:87
  410.0 9.8 %collective-permute-start.59 = (bf16[1,64,384]{2,1,0:T(8,128)(2,1)S(1)}, bf16[1,64,384]{2,1,0:T(8,128)(2,1)S(1)}, u32[]{:S(2)}, u32[]{:S(2)}) collective-permute-start(bf16[1,64,384]{2,1,0:T(8,128)(2,1)S(1)} %get-tuple-element.90), channel_id=1, source_target_pairs={{0,4},{2,6},{4,0},{6,2},{8,12},{10,14},{12,8},{14,10},{16,20},{18,... | collective-permute-start | bytes 147464 | tf_op jit(solution)/shard_map/ppermute | solution.py:87
  411.2 9.5 %collective-permute-start.60 = (bf16[1,64,384]{2,1,0:T(8,128)(2,1)S(1)}, bf16[1,64,384]{2,1,0:T(8,128)(2,1)S(1)}, u32[]{:S(2)}, u32[]{:S(2)}) collective-permute-start(bf16[1,64,384]{2,1,0:T(8,128)(2,1)S(1)} %get-tuple-element.89), channel_id=1, source_target_pairs={{0,6},{2,4},{4,2},{6,0},{8,14},{10,12},{12,10},{14,8},{16,22},{18,... | collective-permute-start | bytes 147464 | tf_op jit(solution)/shard_map/ppermute | solution.py:87
  417.0 9.6 %collective-permute-start.46 = (bf16[128,1024]{1,0:T(8,128)(2,1)}, bf16[128,1024]{1,0:T(8,128)(2,1)}, u32[]{:S(2)}, u32[]{:S(2)}) collective-permute-start(bf16[128,1024]{1,0:T(8,128)(2,1)} %get-tuple-element.44), channel_id=1, source_target_pairs={{0,2},{2,0},{4,6},{6,4},{8,10},{10,8},{12,14},{14,12},{16,18},{18,... | collective-permute-start | bytes 786440 | tf_op jit(solution)/shard_map/ppermute | solution.py:87
  418.9 20.6 %collective-permute-start.47 = (bf16[128,1024]{1,0:T(8,128)(2,1)S(1)}, bf16[128,1024]{1,0:T(8,128)(2,1)}, u32[]{:S(2)}, u32[]{:S(2)}) collective-permute-start(bf16[128,1024]{1,0:T(8,128)(2,1)S(1)} %get-tuple-element.46), channel_id=1, source_target_pairs={{0,4},{2,6},{4,0},{6,2},{8,12},{10,14},{12,8},{14,10},{16,20},{18,... | collective-permute-start | bytes 786440 | tf_op jit(solution)/shard_map/ppermute | solution.py:87
  419.8 19.7 %collective-permute-start.48 = (bf16[128,1024]{1,0:T(8,128)(2,1)S(1)}, bf16[128,1024]{1,0:T(8,128)(2,1)}, u32[]{:S(2)}, u32[]{:S(2)}) collective-permute-start(bf16[128,1024]{1,0:T(8,128)(2,1)S(1)} %get-tuple-element.45), channel_id=1, source_target_pairs={{0,6},{2,4},{4,2},{6,0},{8,14},{10,12},{12,10},{14,8},{16,22},{18,... | collective-permute-start | bytes 786440 | tf_op jit(solution)/shard_map/ppermute | solution.py:87
  420.8 36.0 %collective-permute-start.33 = (bf16[128,1024]{1,0:T(8,128)(2,1)}, bf16[128,1024]{1,0:T(8,128)(2,1)S(1)}, u32[]{:S(2)}, u32[]{:S(2)}) collective-permute-start(bf16[128,1024]{1,0:T(8,128)(2,1)} %get-tuple-element.52), channel_id=1, source_target_pairs={{0,4},{2,6},{4,0},{6,2},{8,12},{10,14},{12,8},{14,10},{16,20},{18,... | collective-permute-start | bytes 786440 | tf_op jit(solution)/shard_map/ppermute | solution.py:87
  426.5 30.2 %collective-permute-start.34 = (bf16[128,1024]{1,0:T(8,128)(2,1)}, bf16[128,1024]{1,0:T(8,128)(2,1)}, u32[]{:S(2)}, u32[]{:S(2)}) collective-permute-start(bf16[128,1024]{1,0:T(8,128)(2,1)} %get-tuple-element.51), channel_id=1, source_target_pairs={{0,6},{2,4},{4,2},{6,0},{8,14},{10,12},{12,10},{14,8},{16,22},{18,... | collective-permute-start | bytes 786440 | tf_op jit(solution)/shard_map/ppermute | solution.py:87
  449.8 9.5 %collective-permute-start.52 = (f32[2176]{0:T(1024)S(1)}, f32[2176]{0:T(1024)S(1)}, u32[]{:S(2)}, u32[]{:S(2)}) collective-permute-start(f32[2176]{0:T(1024)S(1)} %add.406), channel_id=1, source_target_pairs={{0,8},{2,10},{4,12},{6,14},{8,16},{10,18},{12,20},{14,22},{16,24},... | collective-permute-start | bytes 26120 | tf_op jit(solution)/shard_map/ppermute | solution.py:92
  (86 other events, 1015.8 us)
Sparse Core Ops, SparseCore 0:
  32.5 12.3 all-gather.8
  82.8 11.8 all-gather.12
  117.7 11.9 all-gather.10
  327.9 8.5 all-gather.14

commit v2 on v1

v2 whole, which is shorter than its diff:
```python
import jax
import jax.numpy as jnp
from jax import lax
from jax.experimental import pallas as pl
from jax.experimental.pallas import tpu as pltpu
from jax.sharding import PartitionSpec as P

HEAD_DIM = 64


epsilon = 1e-05
rope_base = 1000000.0
masked_score = -1e30


def inverse_rms(values):
    return lax.rsqrt(jnp.mean(values * values, axis=-1, keepdims=True) + epsilon)


def norm_back(grad_unit, unit, factor):
    return factor * (grad_unit - unit * jnp.mean(grad_unit * unit, axis=-1, keepdims=True))


def matmul(first_op, second_op):
    return jnp.dot(first_op, second_op, preferred_element_type=jnp.float32)


def matmul_nt(first_op, second_op):
    return lax.dot_general(
        first_op, second_op, (((1,), (1,)), ((), ())), preferred_element_type=jnp.float32
    )


def matmul_tn(first_op, second_op):
    return lax.dot_general(
        first_op, second_op, (((0,), (0,)), ((), ())), preferred_element_type=jnp.float32
    )


def seq_layout(seq_lengths, total_rows):
    ends = jnp.cumsum(seq_lengths, dtype=jnp.int32)
    starts = ends - seq_lengths
    row_ids = jnp.arange(total_rows, dtype=jnp.int32)
    segment = jnp.sum(
        (row_ids[:, None] >= ends[None, :]).astype(jnp.int32), axis=1, dtype=jnp.int32
    )
    slot_ids = jnp.arange(seq_lengths.shape[0], dtype=jnp.int32)
    picked = (segment[:, None] == slot_ids[None, :]).astype(jnp.int32)
    begin = (
        jnp.sum(picked * starts[None, :], axis=1, dtype=jnp.int32)
        + (segment == seq_lengths.shape[0]).astype(jnp.int32) * ends[-1]
    )
    allowed = (segment[:, None] == segment[None, :]) & (row_ids[:, None] >= row_ids[None, :])
    return (row_ids - begin, row_ids < ends[-1], allowed)


def rope_tables(position, head_size):
    half_dim = head_size // 2
    freqs = rope_base ** (-jnp.arange(half_dim, dtype=jnp.float32) * 2.0 / head_size)
    angles = position.astype(jnp.float32)[:, None] * freqs[None, :]
    return (jnp.cos(angles)[:, None, :], jnp.sin(angles)[:, None, :])


def rotate(values, cosine, sine):
    half_dim = values.shape[-1] // 2
    first_half = values[..., :half_dim]
    second_half = values[..., half_dim:]
    return jnp.concatenate(
        [first_half * cosine - second_half * sine, second_half * cosine + first_half * sine],
        axis=-1,
    )


def rotate_back(grads, cosine, sine):
    half_dim = grads.shape[-1] // 2
    first_half = grads[..., :half_dim]
    second_half = grads[..., half_dim:]
    return jnp.concatenate(
        [first_half * cosine + second_half * sine, second_half * cosine - first_half * sine],
        axis=-1,
    )

PLANE = 4
LANES = 128
HALF = 64
VMEM_BYTES = 60 * 1024 * 1024
float32 = jnp.float32
bfloat16 = jnp.bfloat16


def send_plane(values, mask):
    count = lax.axis_size("dp")
    return lax.ppermute(values, "dp", [(i, i ^ mask) for i in range(count)])


def send_deep(values, step):
    count = lax.axis_size("dp")
    return lax.ppermute(values, "dp", [(i, (i + PLANE * step) % count) for i in range(count)])


def swap_cores(values):
    return lax.ppermute(values, "tensor", [(0, 1), (1, 0)])


def call(kernel, outs, *operands, scalars=0, scratch=(), flops=0, **more):
    specs = [pl.BlockSpec(memory_space=pltpu.SMEM)] * scalars
    specs += [pl.BlockSpec(memory_space=pltpu.VMEM)] * (len(operands) - scalars)
    shapes = [jax.ShapeDtypeStruct(shape, kind) for shape, kind in outs]
    moved = sum(x.size * x.dtype.itemsize for x in operands) + sum(
        s.size * s.dtype.itemsize for s in shapes
    )
    return pl.pallas_call(
        kernel,
        out_shape=shapes,
        in_specs=specs,
        out_specs=[pl.BlockSpec(memory_space=pltpu.VMEM)] * len(shapes),
        scratch_shapes=list(scratch),
        compiler_params=pltpu.CompilerParams(vmem_limit_bytes=VMEM_BYTES),
        cost_estimate=pl.CostEstimate(flops=flops, bytes_accessed=moved, transcendentals=0),
        **more,
    )(*operands)


def lane_ids(shape):
    return lax.broadcasted_iota(jnp.int32, shape, len(shape) - 1)


def half_tile(ref, first_tile, place, upper):
    start = pl.multiple_of((first_tile + place // 2) * LANES, LANES)
    tile = ref[:, pl.ds(start, LANES)].astype(float32)
    turned = pltpu.roll(tile, HALF, 1)
    odd = place % 2 == 1
    if upper:
        return jnp.where(odd, tile, turned)
    return jnp.where(odd, turned, tile)


def padded(values, rows):
    if values.shape[0] == rows:
        return values
    blank = jnp.zeros((rows - values.shape[0], values.shape[1]), values.dtype)
    return jnp.concatenate([values, blank], axis=0)


def attn_rows(rows):
    return (2, rows // 2) if rows % 32 == 0 else (1, max(rows, 16))


def pack_kernel(where_ref, lengths_ref, tok, cot, w_q, w_k, w_v, w_o, w_g, w_u, w_d, *outs):
    rows = w_q.shape[0]
    local = tok.shape[0]
    parts, high = attn_rows(rows)
    tall = max(rows, 16)
    big = w_g.shape[1] // LANES // PLANE * LANES
    last = w_g.shape[1] // LANES // PLANE * PLANE
    place = where_ref[0]
    lane = lane_ids((rows, LANES))
    for mask in range(PLANE):
        other = place ^ mask
        first, second = outs[mask], outs[PLANE + mask]
        at = pl.multiple_of(other * LANES, LANES)
        tile = jnp.where(
            lane < HALF, half_tile(w_k, 0, other, False), half_tile(w_v, 0, other, True)
        )
        piece = jnp.concatenate(
            [w_q[:, pl.ds(at, LANES)].astype(float32), tile, w_o[:, pl.ds(at, LANES)].astype(float32)],
            axis=1,
        )
        first[:local, :] = tok[...]
        pieces = [piece[: rows // 2], piece[rows // 2 :]] if parts == 2 else [padded(piece, high)]
        width = piece.shape[1]
        for part, values in enumerate(pieces):
            first[local:, part * width : (part + 1) * width] = values.astype(bfloat16)
        free = first.shape[1] - parts * width
        ids = lane_ids((high, free))
        marks = jnp.zeros((high, free), float32)
        for slot in range(lengths_ref.shape[1]):
            marks = jnp.where(ids == free - LANES + slot, lengths_ref[0, slot].astype(float32), marks)
        first[local:, parts * width :] = marks.astype(bfloat16)

        at = pl.multiple_of(other * big, LANES)
        second[:local, :] = cot[...]
        small = jnp.where(
            lane < HALF, half_tile(w_g, last, other, False), half_tile(w_u, last, other, True)
        )
        small_down = jnp.where(lane < HALF, half_tile(w_d, last, other, False), 0.0)
        upper = jnp.concatenate(
            [w_g[:, pl.ds(at, big)].astype(float32), w_u[:, pl.ds(at, big)].astype(float32)], axis=1
        )
        lower = jnp.concatenate(
            [w_d[:, pl.ds(at, big)].astype(float32), small, small_down], axis=1
        )
        second[local : local + tall, :] = padded(upper, tall).astype(bfloat16)
        second[local + tall :, : lower.shape[1]] = padded(lower, tall).astype(bfloat16)
        second[local + tall :, lower.shape[1] :] = jnp.zeros(
            (tall, second.shape[1] - lower.shape[1]), bfloat16
        )


def unpack_first_kernel(where_ref, own, one, two, three, tok_out, weight_out, lens_out, held):
    local = tok_out.shape[0] // PLANE
    rows = weight_out.shape[0] // PLANE
    width = weight_out.shape[1]
    parts, high = attn_rows(rows)
    place = where_ref[0]
    for mask, message in enumerate((own, one, two, three)):
        tok_out[mask * local : (mask + 1) * local, :] = message[:local, :]
        at = pl.multiple_of((place ^ mask) * rows, rows)
        values = [
            message[local:, part * width : (part + 1) * width].astype(float32)
            for part in range(parts)
        ]
        piece = jnp.concatenate(values, axis=0) if parts == 2 else values[0][:rows]
        held[pl.ds(at, rows), :] = piece
        ends = message[local : local + 16, message.shape[1] - LANES :].astype(float32)
        lens_out[mask * 8 : (mask + 1) * 8, :] = ends[:8]
    weight_out[...] = held[...].astype(bfloat16)


def unpack_second_kernel(where_ref, own, one, two, three, cot_out, weight_out, held):
    local = cot_out.shape[0] // PLANE
    rows = weight_out.shape[0] // PLANE
    tall = max(rows, 16)
    place = where_ref[0]
    for mask, message in enumerate((own, one, two, three)):
        cot_out[mask * local : (mask + 1) * local, :] = message[:local, :]
        at = pl.multiple_of((place ^ mask) * rows, rows)
        width = message.shape[1]
        held[pl.ds(at, rows), :width] = message[local : local + tall, :].astype(float32)[:rows]
        rest = held.shape[1] - width
        held[pl.ds(at, rows), width:] = message[local + tall :, :rest].astype(float32)[:rows]
    weight_out[...] = held[...].astype(bfloat16)


def stack_kernel(where_ref, *refs):
    *pieces, out = refs
    rows = pieces[0].shape[0]
    depth = where_ref[1]
    for step, piece in enumerate(pieces):
        at = lax.rem(depth - step + len(pieces), len(pieces)) * rows
        out[pl.ds(pl.multiple_of(at, rows), rows), :] = piece[...]


def ffn_kernel(layers, where_ref, ends_ref, x_o, x_m, g_o, g_m, *refs):
    pieces, refs = refs[:layers], refs[layers:]
    out_send, out_keep, dn_send, dn_keep, own_grad = refs[:5]
    grad_pieces = refs[5 : 4 + layers]
    weight, total = refs[4 + layers :]
    step = pl.program_id(0)
    depth, core = where_ref[1], where_ref[2]
    rows = pieces[0].shape[0]
    width = x_o.shape[1]
    both = width
    big = both // 2
    local = x_o.shape[0] // 2

    def row_of(index):
        at = lax.rem(depth + index + layers, layers) * rows
        return pl.ds(pl.multiple_of(at, rows), rows)

    @pl.when(step == 0)
    def _():
        for index, piece in enumerate(pieces):
            weight[row_of(-index), :] = piece[...]
        total[...] = jnp.zeros_like(total)

    def live_rows(values, group, at_core):
        ids = lax.broadcasted_iota(jnp.int32, values.shape, 0) + at_core * local
        return jnp.where(ids < ends_ref[group, ends_ref.shape[1] - 1], values, jnp.zeros_like(values))

    x = jnp.concatenate([x_o[...], x_m[...]], axis=0)
    grads = jnp.concatenate(
        [live_rows(g_o[k * local : (k + 1) * local, :], 2 * step + k, 1 - core) for k in range(2)]
        + [live_rows(g_m[k * local : (k + 1) * local, :], 2 * step + k, core) for k in range(2)],
        axis=0,
    )
    half = 2 * local
    w_both = weight[:, :both]
    w_down = weight[:, both : both + big]
    w_small = weight[:, both + big : both + big + LANES]
    w_small_down = weight[:, both + big + LANES :]
    lane = lane_ids((x.shape[0], LANES))

    def parts_of(gate, up, d_act):
        sigma = 1.0 / (1.0 + jnp.exp(-gate))
        silu = gate * sigma
        act = silu * up
        d_gate = d_act * up * sigma * (1.0 + gate * (1.0 - sigma))
        return act, d_gate, d_act * silu

    pre = matmul(x, w_both)
    act, d_gate, d_up = parts_of(pre[:, :big], pre[:, big:], matmul(grads, w_down))
    pre = matmul(x, w_small)
    act_s, d_gate_s, d_up_s = parts_of(
        pre, pltpu.roll(pre, HALF, 1), matmul(grads, w_small_down)
    )
    act_s = jnp.where(lane < HALF, act_s, 0.0).astype(bfloat16)
    d_small = jnp.where(lane < HALF, d_gate_s, pltpu.roll(d_up_s, HALF, 1)).astype(bfloat16)
    act = act.astype(bfloat16)
    d_both = jnp.concatenate([d_gate, d_up], axis=1).astype(bfloat16)

    partial = matmul_nt(act, w_down) + matmul_nt(act_s, w_small_down)
    out_send[...] = partial[:half].astype(bfloat16)
    out_keep[...] = partial[half:]
    partial = matmul_nt(d_both, w_both) + matmul_nt(d_small, w_small)
    dn_send[...] = partial[:half].astype(bfloat16)
    dn_keep[...] = partial[half:]
    total[:, :both] += matmul_tn(x, d_both)
    total[:, both : both + big] += matmul_tn(grads, act)
    total[:, both + big : both + big + LANES] += matmul_tn(x, d_small)
    total[:, both + big + LANES :] += matmul_tn(grads, act_s)

    @pl.when(step == pl.num_programs(0) - 1)
    def _():
        own_grad[...] = total[row_of(0), :]
        for index, piece in enumerate(grad_pieces):
            piece[...] = total[row_of(index + 1), :].astype(bfloat16)


def ffn(where, ends, x_mine, x_other, g_mine, g_other, pieces):
    layers = len(pieces)
    rows, width = x_mine.shape
    high, columns = pieces[0].shape
    block = rows // 2
    row_spec = pl.BlockSpec((block, width), lambda i: (i, 0))

    def whole(shape):
        return pl.BlockSpec(shape, lambda i: (0, 0), pipeline_mode=pl.Buffered(1))

    scalar = pl.BlockSpec(memory_space=pltpu.SMEM)
    flops = 2 * 2 * rows * width * columns // 3 * 9 // 2
    return pl.pallas_call(
        lambda *refs: ffn_kernel(layers, *refs),
        grid=(2,),
        in_specs=[scalar, scalar] + [row_spec] * 4 + [whole((high, columns))] * layers,
        out_specs=[row_spec] * 4 + [whole((high, columns))] * layers,
        out_shape=[
            jax.ShapeDtypeStruct((rows, width), bfloat16),
            jax.ShapeDtypeStruct((rows, width), float32),
            jax.ShapeDtypeStruct((rows, width), bfloat16),
            jax.ShapeDtypeStruct((rows, width), float32),
            jax.ShapeDtypeStruct((high, columns), float32),
        ]
        + [jax.ShapeDtypeStruct((high, columns), bfloat16)] * (layers - 1),
        scratch_shapes=[
            pltpu.VMEM((layers * high, columns), bfloat16),
            pltpu.VMEM((layers * high, columns), float32),
        ],
        compiler_params=pltpu.CompilerParams(vmem_limit_bytes=VMEM_BYTES),
        cost_estimate=pl.CostEstimate(
            flops=flops, bytes_accessed=40 * 1024 * 1024, transcendentals=0
        ),
    )(where, ends, x_other, x_mine, g_other, g_mine, *pieces)


def chip_sum_kernel(keep, received, *outs):
    rows = outs[0].shape[0]
    for mask, out in enumerate(outs):
        span = slice(mask * rows, (mask + 1) * rows)
        out[...] = (keep[span, :] + received[span, :].astype(float32)).astype(out.dtype)


def chip_sum(keep, received):
    shape = (keep.shape[0] // PLANE, keep.shape[1])
    own, *rest = call(
        chip_sum_kernel, [(shape, float32)] + [(shape, bfloat16)] * (PLANE - 1), keep, received
    )
    return [own] + [send_plane(part, mask + 1) for mask, part in enumerate(rest)]


def add_up(parts):
    return sum(part.astype(float32) for part in parts)


def plane_sum_kernel(where_ref, own, *refs):
    received, outs, held = refs[: -PLANE - 1], refs[-PLANE - 1 : -1], refs[-1]
    value = own[...]
    for part in received:
        value = value + part[...].astype(float32)
    held[...] = value
    place = where_ref[0]
    rows = outs[0].shape[0]
    for mask, out in enumerate(outs):
        at = pl.multiple_of((place ^ mask) * rows, rows)
        out[...] = held[pl.ds(at, rows), :].astype(out.dtype)


def plane_sum(where, own, grad_pieces):
    received = [send_deep(piece, step + 1) for step, piece in enumerate(grad_pieces)]
    shape = (own.shape[0] // PLANE, own.shape[1])
    mine, *rest = call(
        plane_sum_kernel,
        [(shape, float32)] + [(shape, bfloat16)] * (PLANE - 1),
        where,
        own,
        *received,
        scalars=1,
        scratch=[pltpu.VMEM(own.shape, float32)],
    )
    return [mine] + [send_plane(part, mask + 1) for mask, part in enumerate(rest)]


def pick_place(refs, place, target, columns):
    value = jnp.zeros((refs[0].shape[0], columns.stop - columns.start), float32)
    for mask, ref in enumerate(refs):
        value = jnp.where(place ^ mask == target, ref[:, columns].astype(float32), value)
    return value


def place_ffn_kernel(where_ref, own, one, two, three, out_g, out_u, out_d):
    place = where_ref[0]
    refs = (own, one, two, three)
    big = out_g.shape[1] // LANES // PLANE * LANES
    last = PLANE * big
    for mask, ref in enumerate(refs):
        at = pl.ds(pl.multiple_of((place ^ mask) * big, LANES), big)
        for number, out in enumerate((out_g, out_u, out_d)):
            out[:, at] = ref[:, number * big : (number + 1) * big].astype(float32)
    for pair in range(PLANE // 2):
        low = pick_place(refs, place, 2 * pair, slice(3 * big, 3 * big + 2 * LANES))
        high = pick_place(refs, place, 2 * pair + 1, slice(3 * big, 3 * big + 2 * LANES))
        lane = lane_ids((low.shape[0], LANES))
        span = slice(last + pair * LANES, last + (pair + 1) * LANES)
        gu_low, gu_high = low[:, :LANES], high[:, :LANES]
        out_g[:, span] = jnp.where(lane < HALF, gu_low, pltpu.roll(gu_high, HALF, 1))
        out_u[:, span] = jnp.where(lane < HALF, pltpu.roll(gu_low, HALF, 1), gu_high)
        out_d[:, span] = jnp.where(lane < HALF, low[:, LANES:], pltpu.roll(high[:, LANES:], HALF, 1))


def place_attn_kernel(where_ref, own, one, two, three, out_q, out_k, out_v, out_o):
    place = where_ref[0]
    refs = (own, one, two, three)
    for mask, ref in enumerate(refs):
        at = pl.ds(pl.multiple_of((place ^ mask) * LANES, LANES), LANES)
        out_q[:, at] = ref[:, :LANES].astype(float32)
        out_o[:, at] = ref[:, 2 * LANES :].astype(float32)
    for pair in range(PLANE // 2):
        low = pick_place(refs, place, 2 * pair, slice(LANES, 2 * LANES))
        high = pick_place(refs, place, 2 * pair + 1, slice(LANES, 2 * LANES))
        lane = lane_ids(low.shape)
        span = slice(pair * LANES, (pair + 1) * LANES)
        out_k[:, span] = jnp.where(lane < HALF, low, pltpu.roll(high, HALF, 1))
        out_v[:, span] = jnp.where(lane < HALF, pltpu.roll(low, HALF, 1), high)


def split_grad_kernel(where_ref, grad, own, *pieces):
    layers = len(pieces) + 1
    rows = own.shape[0]
    depth = where_ref[1]
    for step, out in enumerate((own,) + pieces):
        at = lax.rem(depth + step, layers) * rows
        out[...] = grad[pl.ds(pl.multiple_of(at, rows), rows), :].astype(out.dtype)


def gather_rows(local):
    mine = jnp.concatenate([local] + [send_plane(local, mask) for mask in range(1, PLANE)])
    return mine, swap_cores(mine)


def sum_all(values):
    dp = lax.axis_index("dp")
    layers = lax.axis_size("dp") // PLANE
    depth = dp // PLANE
    values = values + swap_cores(values)
    first = values + send_plane(values, 1)
    both = first + send_plane(first, 2)
    every = jnp.zeros((layers,) + both.shape, both.dtype)
    for step in range(layers):
        part = send_deep(both, step) if step else both
        every = lax.dynamic_update_slice(
            every, part[None], ((depth - step) % layers,) + (0,) * both.ndim
        )
    return jnp.sum(every, axis=0)


def body(
    tokens,
    lengths,
    attn_gain,
    query_gain,
    key_gain,
    ffn_gain,
    w_query,
    w_key,
    w_value,
    w_out,
    w_gate,
    w_up,
    w_down,
    cotangent,
):
    dp = lax.axis_index("dp")
    core = lax.axis_index("tensor")
    layers = lax.axis_size("dp") // PLANE
    where = jnp.stack([dp % PLANE, dp // PLANE, core]).astype(jnp.int32)
    local_rows, model = tokens.shape
    total_rows = local_rows * lax.axis_size("tensor")
    rows = w_query.shape[0]
    q_cols = w_query.shape[1] // PLANE
    kv_cols = w_key.shape[1] // PLANE
    local_kv = kv_cols // HEAD_DIM
    share = q_cols // kv_cols
    score_scale = HEAD_DIM ** (-0.5)
    attn_cols = 2 * q_cols + 2 * kv_cols
    ff_cols = 3 * (w_gate.shape[1] // LANES // PLANE * LANES) + 2 * LANES

    parts, high = attn_rows(rows)
    tall = max(rows, 16)
    messages = call(
        pack_kernel,
        [((local_rows + high, model), bfloat16)] * PLANE
        + [((local_rows + 2 * tall, model), bfloat16)] * PLANE,
        where,
        lengths,
        tokens,
        cotangent,
        w_query,
        w_key,
        w_value,
        w_out,
        w_gate,
        w_up,
        w_down,
        scalars=2,
    )
    first = [messages[0]] + [send_plane(messages[m], m) for m in range(1, PLANE)]
    second = [messages[PLANE]] + [send_plane(messages[PLANE + m], m) for m in range(1, PLANE)]
    tok_mine, attn_piece, lens = call(
        unpack_first_kernel,
        [
            ((PLANE * local_rows, model), bfloat16),
            ((PLANE * rows, attn_cols), bfloat16),
            ((PLANE * 8, LANES), float32),
        ],
        where,
        *first,
        scalars=1,
        scratch=[pltpu.VMEM((PLANE * rows, attn_cols), float32)],
    )
    attn_pieces = [attn_piece] + [send_deep(attn_piece, step) for step in range(1, layers)]
    tok_other = swap_cores(tok_mine)
    cot_mine, ff_piece = call(
        unpack_second_kernel,
        [((PLANE * local_rows, model), bfloat16), ((PLANE * rows, ff_cols), bfloat16)],
        where,
        *second,
        scalars=1,
        scratch=[pltpu.VMEM((PLANE * rows, ff_cols), float32)],
    )
    ff_pieces = [ff_piece] + [send_deep(ff_piece, step) for step in range(1, layers)]
    cot_other = swap_cores(cot_mine)
    (attn_weight,) = call(
        stack_kernel, [((model, attn_cols), bfloat16)], where, *attn_pieces, scalars=1
    )
    full_qkv = attn_weight[:, : q_cols + 2 * kv_cols]
    full_out = attn_weight[:, q_cols + 2 * kv_cols :]

    slots = lengths.shape[1]
    all_lengths = lens.reshape(PLANE, 8, LANES)[:, 0, :slots].astype(jnp.int32)
    ends = jnp.cumsum(all_lengths, axis=1, dtype=jnp.int32)
    row_ids = jnp.arange(total_rows, dtype=jnp.int32)
    begin = jnp.max(
        jnp.where(row_ids[None, :, None] >= ends[:, None, :], ends[:, None, :], 0), axis=2
    )
    position = row_ids[None, :] - begin
    allowed = (row_ids[None, None, :] >= begin[:, :, None]) & (
        row_ids[None, None, :] <= row_ids[None, :, None]
    )
    cosine, sine = jax.vmap(lambda one: rope_tables(one, HEAD_DIM))(position)

    def by_group(mine, other):
        mine = mine.reshape(PLANE, local_rows, -1)
        other = other.reshape(PLANE, local_rows, -1)
        low = jnp.where(core == 0, mine, other)
        upper = jnp.where(core == 0, other, mine)
        return jnp.concatenate([low, upper], axis=1)

    def by_core(values):
        low, upper = values[:, :local_rows], values[:, local_rows:]
        mine = jnp.where(core == 0, low, upper).reshape(PLANE * local_rows, -1)
        other = jnp.where(core == 0, upper, low).reshape(PLANE * local_rows, -1)
        return mine, other

    inputs = tokens.astype(jnp.float32)
    factor_a = inverse_rms(inputs)
    unit_a = inputs * factor_a
    group_tokens = by_group(tok_mine, tok_other).astype(jnp.float32)
    normed = (group_tokens * inverse_rms(group_tokens) * attn_gain).astype(jnp.bfloat16)
    normed = normed.reshape(-1, model)
    pre = matmul(normed, full_qkv).reshape(PLANE, total_rows, -1)
    query_pre = pre[..., :q_cols].reshape(PLANE, total_rows, local_kv * share, HEAD_DIM)
    key_pre = pre[..., q_cols : q_cols + kv_cols].reshape(PLANE, total_rows, local_kv, HEAD_DIM)
    value_low = (
        pre[..., q_cols + kv_cols :]
        .astype(jnp.bfloat16)
        .reshape(PLANE, total_rows, local_kv, HEAD_DIM)
    )
    factor_q = inverse_rms(query_pre)
    unit_q = query_pre * factor_q
    factor_k = inverse_rms(key_pre)
    unit_k = key_pre * factor_k
    query_low = rotate(unit_q * query_gain, cosine, sine).astype(jnp.bfloat16)
    key_low = rotate(unit_k * key_gain, cosine, sine).astype(jnp.bfloat16)
    grouped = query_low.reshape(PLANE, total_rows, local_kv, share, HEAD_DIM)
    scores = (
        jnp.einsum("bqgjd,bkgd->bgjqk", grouped, key_low, preferred_element_type=jnp.float32)
        * score_scale
    )
    scores = jnp.where(allowed[:, None, None], scores, masked_score)
    top = jnp.max(scores, axis=-1, keepdims=True)
    expd = jnp.exp(scores - top)
    totals = jnp.sum(expd, axis=-1, keepdims=True)
    probs = expd / totals
    probs_low = probs.astype(jnp.bfloat16)
    mixed = jnp.einsum(
        "bgjqk,bkgd->bqgjd", probs_low, value_low, preferred_element_type=jnp.float32
    )
    mixed_low = mixed.astype(jnp.bfloat16).reshape(PLANE, total_rows, q_cols)
    mixed_mine, mixed_other = by_core(mixed_low)
    received = swap_cores(matmul_nt(mixed_other, full_out).astype(jnp.bfloat16))
    hidden = inputs + add_up(chip_sum(matmul_nt(mixed_mine, full_out), received))
    factor_b = inverse_rms(hidden)
    unit_b = hidden * factor_b
    x_mine, x_other = gather_rows((unit_b * ffn_gain).astype(jnp.bfloat16))

    out_send, out_keep, dn_send, dn_keep, own_ff, *ff_grads = ffn(
        where, ends, x_mine, x_other, cot_mine, cot_other, ff_pieces
    )
    d_normed2 = add_up(chip_sum(dn_keep, swap_cores(dn_send)))
    grad_out = jnp.where(
        (jnp.arange(local_rows) + core * local_rows < ends[0, slots - 1])[:, None],
        cotangent,
        jnp.zeros_like(cotangent),
    )
    gain_ffn = jnp.sum(d_normed2 * unit_b, axis=0)
    d_hidden = grad_out.astype(jnp.float32) + norm_back(d_normed2 * ffn_gain, unit_b, factor_b)
    h_mine, h_other = gather_rows(d_hidden.astype(jnp.bfloat16))
    ff_parts = plane_sum(where, own_ff, ff_grads)
    block_out = (hidden + add_up(chip_sum(out_keep, swap_cores(out_send)))).astype(jnp.bfloat16)

    hidden_rows = by_group(h_mine, h_other).reshape(-1, model)
    grad_out_proj = matmul_tn(hidden_rows, mixed_low.reshape(-1, q_cols))
    d_mixed = matmul(hidden_rows, full_out).astype(jnp.bfloat16).reshape(
        PLANE, total_rows, local_kv, share, HEAD_DIM
    )
    d_value = jnp.einsum(
        "bgjqk,bqgjd->bkgd", probs_low, d_mixed, preferred_element_type=jnp.float32
    )
    d_value_low = d_value.astype(jnp.bfloat16).reshape(PLANE, total_rows, kv_cols)
    d_probs = jnp.einsum(
        "bqgjd,bkgd->bgjqk", d_mixed, value_low, preferred_element_type=jnp.float32
    )
    centre = jnp.sum(probs * d_probs, axis=-1, keepdims=True)
    d_scores = (probs * (d_probs - centre)).astype(jnp.bfloat16)
    d_query_rot = jnp.einsum(
        "bgjqk,bkgd->bqgjd", d_scores, key_low, preferred_element_type=jnp.float32
    )
    d_query_rot = (
        d_query_rot.reshape(PLANE, total_rows, local_kv * share, HEAD_DIM) * score_scale
    )
    d_key_rot = (
        jnp.einsum("bgjqk,bqgjd->bkgd", d_scores, grouped, preferred_element_type=jnp.float32)
        * score_scale
    )
    turned_q = rotate_back(d_query_rot, cosine, sine)
    turned_k = rotate_back(d_key_rot, cosine, sine)
    gain_query = jnp.sum(turned_q * unit_q, axis=(0, 1, 2))
    gain_key = jnp.sum(turned_k * unit_k, axis=(0, 1, 2))
    d_query = (
        norm_back(turned_q * query_gain, unit_q, factor_q)
        .astype(jnp.bfloat16)
        .reshape(PLANE, total_rows, q_cols)
    )
    d_key = (
        norm_back(turned_k * key_gain, unit_k, factor_k)
        .astype(jnp.bfloat16)
        .reshape(PLANE, total_rows, kv_cols)
    )
    d_qkv = jnp.concatenate([d_query, d_key, d_value_low], axis=2)
    attn_grad = jnp.concatenate(
        [matmul_tn(normed, d_qkv.reshape(-1, d_qkv.shape[-1])), grad_out_proj], axis=1
    )
    d_mine, d_other = by_core(d_qkv)
    received = swap_cores(matmul_nt(d_other, full_qkv).astype(jnp.bfloat16))
    d_normed = add_up(chip_sum(matmul_nt(d_mine, full_qkv), received))
    own_attn, *attn_grads = call(
        split_grad_kernel,
        [((PLANE * rows, attn_cols), float32)]
        + [((PLANE * rows, attn_cols), bfloat16)] * (layers - 1),
        where,
        attn_grad,
        scalars=1,
    )
    attn_parts = plane_sum(where, own_attn, attn_grads)
    gain_attn = jnp.sum(d_normed * unit_a, axis=0)
    grad_tokens = d_hidden + norm_back(d_normed * attn_gain, unit_a, factor_a)
    gains = sum_all(jnp.concatenate([gain_attn, gain_ffn, gain_query, gain_key]))
    grad_gate, grad_up, grad_down = call(
        place_ffn_kernel, [(w_gate.shape, float32)] * 3, where, *ff_parts, scalars=1
    )
    grad_query, grad_key, grad_value, grad_out_w = call(
        place_attn_kernel,
        [(w.shape, float32) for w in (w_query, w_key, w_value, w_out)],
        where,
        *attn_parts,
        scalars=1,
    )
    return (
        block_out,
        grad_tokens,
        gains[:model],
        gains[2 * model : 2 * model + HEAD_DIM],
        gains[2 * model + HEAD_DIM :],
        gains[model : 2 * model],
        grad_query,
        grad_key,
        grad_value,
        grad_out_w,
        grad_gate,
        grad_up,
        grad_down,
    )


def solution(mesh):
    placed = (
        P(("dp", "tensor"), None),
        P("dp", None),
        P(),
        P(),
        P(),
        P(),
        P("dp", "tensor"),
        P("dp", "tensor"),
        P("dp", "tensor"),
        P("dp", "tensor"),
        P("dp", "tensor"),
        P("dp", "tensor"),
        P("dp", "tensor"),
        P(("dp", "tensor"), None),
    )
    return jax.shard_map(
        body,
        mesh=mesh,
        in_specs=placed,
        out_specs=(
            P(("dp", "tensor"), None),
            P(("dp", "tensor"), None),
            P(),
            P(),
            P(),
            P(),
            P("dp", "tensor"),
            P("dp", "tensor"),
            P("dp", "tensor"),
            P("dp", "tensor"),
            P("dp", "tensor"),
            P("dp", "tensor"),
            P("dp", "tensor"),
        ),
        check_vma=False,
    )
```

time: 477 us -> 422 us (0.88); the launches traced: 468 us -> 421 us
  local copies, waits for them, and re-layouts: 136 us -> 24.4 us
  waiting for transfers between devices: 108 us -> 201 us
  Pallas kernels: 0 us -> 56.9 us
  starting transfers between devices: 129 us -> 99.5 us
  other arithmetic: 43.2 us -> 18.1 us
  matrix products: 35.7 us -> 19 us
  between operations: 15.9 us -> 1.59 us
    ppermute x21 -> x15, waiting for transfers between devices: 46.8 us -> 123 us  [send_deep(): lax.ppermute(values, 'dp', [(i, (i + PLANE * step) % count) for i in rang...]
    dynamic_update_slice x34 -> x0, local copies, waits for them, and re-layouts: 60.8 us -> none  [the longest x12 38.1 us: gather_weight(): lax.dynamic_update_slice(whole, part, ((depth - step) % layers, 0, 0))]
    pallas_call x0 -> x14, Pallas kernels: none -> 56.9 us  [the longest x13 35.9 us: call(): pl.pallas_call(kernel, out_shape=shapes, in_specs=specs, out_specs=[pl.Bl...]
    reshape x19 -> x0, local copies, waits for them, and re-layouts: 26.5 us -> none  [the longest x6 7.05 us: joined(): return part.reshape(part.shape[0], -1)]
    ppermute x47 -> x32, starting transfers between devices: 58.6 us -> 37.1 us  [send_plane(): return lax.ppermute(values, 'dp', [(i, i ^ mask) for i in range(count)])]
    ppermute x47 -> x32, waiting for transfers between devices: 61 us -> 73 us  [send_plane(): return lax.ppermute(values, 'dp', [(i, i ^ mask) for i in range(count)])]
    convert_element_type x10 -> x3, other arithmetic: 12.3 us -> 1.22 us  [the longest x1 1.1 us: body(): h_mine, h_other = gather_rows(d_hidden.astype(jnp.bfloat16))]
    dot_general x4 -> x2, matrix products: 13.5 us -> 3.33 us  [matmul(): return jnp.dot(first_op, second_op, preferred_element_type=jnp.float32)]
  transfers between devices with their start and end apart: 77 -> 56, of which waited for: 33 -> 29; matrix products, arithmetic and copies ran while one was open for 32% -> 6% of each run, Pallas kernels for 0% -> 6%
where the time goes in v2:
time: 422 us; the launch traced here: 421 us
  waiting for transfers between devices  201 us (48%)
  starting transfers between devices  99.5 us (24%)
  Pallas kernels  56.9 us (13%)
  local copies, waits for them, and re-layouts  24.4 us (6%)
  matrix products  19 us (5%)
  other arithmetic  18.1 us (4%)
    ppermute x15, waiting for transfers between devices, send_deep(): lax.ppermute(values, 'dp', [(i, (i + PLANE * step) % count) for i in rang...  123 us
    ppermute x32, waiting for transfers between devices, send_plane(): return lax.ppermute(values, 'dp', [(i, i ^ mask) for i in range(count)])  73 us
    ppermute x15, starting transfers between devices, send_deep(): lax.ppermute(values, 'dp', [(i, (i + PLANE * step) % count) for i in rang...  61.6 us
    ppermute x32, starting transfers between devices, send_plane(): return lax.ppermute(values, 'dp', [(i, i ^ mask) for i in range(count)])  37.1 us
    pallas_call x13, Pallas kernels, call(): pl.pallas_call(kernel, out_shape=shapes, in_specs=specs, out_specs=[pl.Bl...  35.9 us
    pallas_call x1, Pallas kernels, ffn(): pl.pallas_call(lambda *refs: ffn_kernel(layers, *refs), grid=(2,), in_spe...  21 us
    unnamed x163, local copies, waits for them, and re-layouts  12.5 us
  transfers between devices with their start and end apart: 56, of which 29 were waited for; matrix products, arithmetic and copies ran while one was open for 6% of the time, Pallas kernels for 6%

profile of v2, /device:TPU:0, one launch (start us, length us, event | category | flops | bytes accessed | tf_op | source)
XLA Modules:
  0.0 421.0 jit_solution(2595314779669652858)
XLA Ops:
  1.3 3.3 shard_map.237
  4.6 2.9 collective-permute-start
  7.5 1.5 collective-permute-start.1
  9.1 7.2 %collective-permute-done.one = bf16[160,1024]{1,0:T(8,128)(2,1)S(1)} collective-permute-done((bf16[160,1024]{1,0:T(8,128)(2,1)}, bf16[160,1024]{1,0:T(8,128)(2,1)S(1)}, u32[]{:S(2)}, u32[]{:S(2)}) %collective-permute-start) | collective-permute-done | bytes 327712 | tf_op jit(solution)/shard_map/ppermute | solution.py:93
  16.3 7.7 %collective-permute-done.1.two = bf16[160,1024]{1,0:T(8,128)(2,1)S(1)} collective-permute-done((bf16[160,1024]{1,0:T(8,128)(2,1)}, bf16[160,1024]{1,0:T(8,128)(2,1)S(1)}, u32[]{:S(2)}, u32[]{:S(2)}) %collective-permute-start.1) | collective-permute-done | bytes 327712 | tf_op jit(solution)/shard_map/ppermute | solution.py:93
  24.8 2.4 shard_map.238
  27.2 1.6 collective-permute-start.4
  28.8 2.6 collective-permute-start.5
  35.0 2.1 collective-permute-done.4.refs_1_
  37.1 8.1 %collective-permute-done.5.refs_2_ = bf16[256,384]{1,0:T(8,128)(2,1)S(1)} collective-permute-done((bf16[256,384]{1,0:T(8,128)(2,1)}, bf16[256,384]{1,0:T(8,128)(2,1)S(1)}, u32[]{:S(2)}, u32[]{:S(2)}) %collective-permute-start.5) | collective-permute-done | bytes 196640 | tf_op jit(solution)/shard_map/ppermute | solution.py:98
  46.5 2.3 shard_map.239
  55.9 1.8 fusion.45.keep
  59.5 2.9 shard_map.240
  62.5 1.5 collective-permute-start.10
  68.0 4.8 %collective-permute-done.10 = bf16[128,1024]{1,0:T(8,128)(2,1)S(1)} collective-permute-done((bf16[128,1024]{1,0:T(8,128)(2,1)}, bf16[128,1024]{1,0:T(8,128)(2,1)S(1)}, u32[]{:S(2)}, u32[]{:S(2)}) %collective-permute-start.10) | collective-permute-done | bytes 262176 | tf_op jit(solution)/shard_map/ppermute | solution.py:93
  74.3 4.2 collective-permute-done.8
  78.5 1.8 multiply_reduce_fusion.3
  82.1 7.6 %collective-permute-done.15.one = bf16[256,1024]{1,0:T(8,128)(2,1)S(1)} collective-permute-done((bf16[256,1024]{1,0:T(8,128)(2,1)}, bf16[256,1024]{1,0:T(8,128)(2,1)S(1)}, u32[]{:S(2)}, u32[]{:S(2)}) %collective-permute-start.15) | collective-permute-done | bytes 524320 | tf_op jit(solution)/shard_map/ppermute | solution.py:93
  90.8 10.1 %collective-permute-done.17.three = bf16[256,1024]{1,0:T(8,128)(2,1)S(1)} collective-permute-done((bf16[256,1024]{1,0:T(8,128)(2,1)}, bf16[256,1024]{1,0:T(8,128)(2,1)S(1)}, u32[]{:S(2)}, u32[]{:S(2)}) %collective-permute-start.17) | collective-permute-done | bytes 524320 | tf_op jit(solution)/shard_map/ppermute | solution.py:93
  101.7 3.0 shard_map.241
  104.7 1.9 collective-permute-done.11
  106.6 4.9 %collective-permute-done.13 = bf16[128,1024]{1,0:T(8,128)(2,1)} collective-permute-done((bf16[128,1024]{1,0:T(8,128)(2,1)S(1)}, bf16[128,1024]{1,0:T(8,128)(2,1)}, u32[]{:S(2)}, u32[]{:S(2)}) %collective-permute-start.13) | collective-permute-done | bytes 262176 | tf_op jit(solution)/shard_map/ppermute | solution.py:93
  112.7 4.1 collective-permute-start.19
  116.8 2.3 collective-permute-start.20
  119.2 20.6 %collective-permute-done.19.refs_7_ = bf16[256,1792]{1,0:T(8,128)(2,1)S(1)} collective-permute-done((bf16[256,1792]{1,0:T(8,128)(2,1)S(1)}, bf16[256,1792]{1,0:T(8,128)(2,1)S(1)}, u32[]{:S(2)}, u32[]{:S(2)}) %collective-permute-start.19) | collective-permute-done | bytes 917536 | tf_op jit(solution)/shard_map/ppermute | solution.py:98
  139.8 39.0 %collective-permute-done.20.refs_8_ = bf16[256,1792]{1,0:T(8,128)(2,1)S(1)} collective-permute-done((bf16[256,1792]{1,0:T(8,128)(2,1)S(1)}, bf16[256,1792]{1,0:T(8,128)(2,1)S(1)}, u32[]{:S(2)}, u32[]{:S(2)}) %collective-permute-start.20) | collective-permute-done | bytes 917536 | tf_op jit(solution)/shard_map/ppermute | solution.py:98
  180.1 21.0 %shard_map.242 = (bf16[512,1024]{1,0:T(8,128)(2,1)}, f32[512,1024]{1,0:T(8,128)}, bf16[512,1024]{1,0:T(8,128)(2,1)}, f32[512,1024]{1,0:T(8,128)}, f32[256,1792]{...) custom-call(s32[3]{0:T(128)} %pad_add_fusion.where_ref.refs_0_, ...), custom_call_target="tpu_custom_call" | custom-call | flops 5637144576 | bytes 41943040 | tf_op jit(solution)/shard_map/pallas_call | solution.py:332
  201.7 3.2 collective-permute-done.26.received
  204.9 2.9 shard_map.244
  214.3 3.0 shard_map.243
  220.8 3.2 collective-permute-done.29
  223.9 2.2 multiply_reduce_fusion
  226.1 2.4 collective-permute-done.23
  228.5 4.2 %collective-permute-done.24 = bf16[128,1024]{1,0:T(8,128)(2,1)S(1)} collective-permute-done((bf16[128,1024]{1,0:T(8,128)(2,1)}, bf16[128,1024]{1,0:T(8,128)(2,1)S(1)}, u32[]{:S(2)}, u32[]{:S(2)}) %collective-permute-start.24) | collective-permute-done | bytes 262176 | tf_op jit(solution)/shard_map/ppermute | solution.py:93
  232.7 1.6 collective-permute-done.25
  236.1 1.5 collective-permute-start.31
  238.9 5.8 %collective-permute-done.30 = bf16[128,1024]{1,0:T(8,128)(2,1)S(1)} collective-permute-done((bf16[128,1024]{1,0:T(8,128)(2,1)S(1)}, bf16[128,1024]{1,0:T(8,128)(2,1)S(1)}, u32[]{:S(2)}, u32[]{:S(2)}) %collective-permute-start.30) | collective-permute-done | bytes 262176 | tf_op jit(solution)/shard_map/ppermute | solution.py:93
  244.6 5.1 %collective-permute-done.31 = bf16[128,1024]{1,0:T(8,128)(2,1)S(1)} collective-permute-done((bf16[128,1024]{1,0:T(8,128)(2,1)S(1)}, bf16[128,1024]{1,0:T(8,128)(2,1)S(1)}, u32[]{:S(2)}, u32[]{:S(2)}) %collective-permute-start.31) | collective-permute-done | bytes 262176 | tf_op jit(solution)/shard_map/ppermute | solution.py:93
  254.4 2.4 convolution_convert_fusion.2
  256.8 2.0 reshape.328
  258.8 1.9 copy.59
  260.7 2.4 fusion.3
  269.1 2.5 convolution_convert_fusion.1
  272.0 19.9 %collective-permute-start.50 = (bf16[256,1792]{1,0:T(8,128)(2,1)}, bf16[256,1792]{1,0:T(8,128)(2,1)}, u32[]{:S(2)}, u32[]{:S(2)}) collective-permute-start(bf16[256,1792]{1,0:T(8,128)(2,1)} %get-tuple-element.115), channel_id=1, source_target_pairs={{0,8},{2,10},{4,12},{6,14},{8,16},{10,18},{12,20},{14,22},{16,24},... | collective-permute-start | bytes 2752520 | tf_op jit(solution)/shard_map/ppermute | solution.py:98
  292.8 1.5 collective-permute-start.52
  294.4 1.6 fusion.81
  295.9 1.9 copy.64
  297.9 2.8 fusion.40.keep
  300.7 2.0 fusion.12
  302.7 3.1 shard_map.245
  307.8 6.1 %collective-permute-done.50.refs_0_ = bf16[256,1792]{1,0:T(8,128)(2,1)} collective-permute-done((bf16[256,1792]{1,0:T(8,128)(2,1)}, bf16[256,1792]{1,0:T(8,128)(2,1)}, u32[]{:S(2)}, u32[]{:S(2)}) %collective-permute-start.50) | collective-permute-done | bytes 917536 | tf_op jit(solution)/shard_map/ppermute | solution.py:98
  316.6 2.5 shard_map.246
  319.1 33.8 %collective-permute-done.51.refs_1_ = bf16[256,1792]{1,0:T(8,128)(2,1)} collective-permute-done((bf16[256,1792]{1,0:T(8,128)(2,1)}, bf16[256,1792]{1,0:T(8,128)(2,1)}, u32[]{:S(2)}, u32[]{:S(2)}) %collective-permute-start.51) | collective-permute-done | bytes 917536 | tf_op jit(solution)/shard_map/ppermute | solution.py:98
  352.9 18.7 %collective-permute-start.44 = (bf16[256,384]{1,0:T(8,128)(2,1)}, bf16[256,384]{1,0:T(8,128)(2,1)S(1)}, u32[]{:S(2)}, u32[]{:S(2)}) collective-permute-start(bf16[256,384]{1,0:T(8,128)(2,1)} %get-tuple-element.103), channel_id=1, source_target_pairs={{0,8},{2,10},{4,12},{6,14},{8,16},{10,18},{12,20},{14,22},{16,24},... | collective-permute-start | bytes 589832 | tf_op jit(solution)/shard_map/ppermute | solution.py:98
  371.7 4.1 shard_map.249
  376.7 2.8 collective-permute-done.44.refs_0_
  384.7 8.3 %collective-permute-done.45.refs_1_ = bf16[256,384]{1,0:T(8,128)(2,1)} collective-permute-done((bf16[256,384]{1,0:T(8,128)(2,1)}, bf16[256,384]{1,0:T(8,128)(2,1)}, u32[]{:S(2)}, u32[]{:S(2)}) %collective-permute-start.45) | collective-permute-done | bytes 196640 | tf_op jit(solution)/shard_map/ppermute | solution.py:98
  393.2 2.0 shard_map.247
  400.5 2.6 shard_map.250
  403.8 1.7 shard_map.248
  406.7 2.6 collective-permute-done.40
  409.3 3.9 collective-permute-start.41
  413.2 2.6 collective-permute-start.42
  418.0 1.6 collective-permute-done.43
  (316 shorter events, 73.7 us)
Async XLA Ops:
  4.6 11.7 %collective-permute-start = (bf16[160,1024]{1,0:T(8,128)(2,1)}, bf16[160,1024]{1,0:T(8,128)(2,1)S(1)}, u32[]{:S(2)}, u32[]{:S(2)}) collective-permute-start(bf16[160,1024]{1,0:T(8,128)(2,1)} %get-tuple-element.70), channel_id=1, source_target_pairs={{0,2},{2,0},{4,6},{6,4},{8,10},{10,8},{12,14},{14,12},{16,18},{18,... | collective-permute-start | bytes 983048 | tf_op jit(solution)/shard_map/ppermute | solution.py:93
  7.5 16.4 %collective-permute-start.1 = (bf16[160,1024]{1,0:T(8,128)(2,1)}, bf16[160,1024]{1,0:T(8,128)(2,1)S(1)}, u32[]{:S(2)}, u32[]{:S(2)}) collective-permute-start(bf16[160,1024]{1,0:T(8,128)(2,1)} %get-tuple-element.71), channel_id=1, source_target_pairs={{0,4},{2,6},{4,0},{6,2},{8,12},{10,14},{12,8},{14,10},{16,20},{18,... | collective-permute-start | bytes 983048 | tf_op jit(solution)/shard_map/ppermute | solution.py:93
  9.0 14.9 %collective-permute-start.2 = (bf16[160,1024]{1,0:T(8,128)(2,1)}, bf16[160,1024]{1,0:T(8,128)(2,1)S(1)}, u32[]{:S(2)}, u32[]{:S(2)}) collective-permute-start(bf16[160,1024]{1,0:T(8,128)(2,1)} %get-tuple-element.72), channel_id=1, source_target_pairs={{0,6},{2,4},{4,2},{6,0},{8,14},{10,12},{12,10},{14,8},{16,22},{18,... | collective-permute-start | bytes 983048 | tf_op jit(solution)/shard_map/ppermute | solution.py:93
  27.2 21.6 %copy-start.14 = (bf16[512,1024]{1,0:T(8,128)(2,1)S(1)}, bf16[512,1024]{1,0:T(8,128)(2,1)}, u32[]{:S(2)}) copy-start(bf16[512,1024]{1,0:T(8,128)(2,1)} %get-tuple-element.73) | copy-start | bytes 3145732
  27.2 21.6 %collective-permute-start.3 = (bf16[512,1024]{1,0:T(8,128)(2,1)}, bf16[512,1024]{1,0:T(8,128)(2,1)S(1)}, u32[]{:S(2)}, u32[]{:S(2)}) collective-permute-start(bf16[512,1024]{1,0:T(8,128)(2,1)} %get-tuple-element.73), channel_id=1, source_target_pairs={{0,1},{1,0},{2,3},{3,2},{4,5},{5,4},{6,7},{7,6},{8,9},{9,8},{10,11... | collective-permute-start | bytes 3145736 | tf_op jit(solution)/shard_map/ppermute | solution.py:102
  27.2 24.7 %copy-start.62 = (f32[32]{0:T(128)}, f32[32]{0:T(128)S(1)}, u32[]{:S(2)}) copy-start(f32[32]{0:T(128)S(1)} %multiply_power_fusion) | copy-start | bytes 388
  27.2 9.9 %collective-permute-start.4 = (bf16[256,384]{1,0:T(8,128)(2,1)}, bf16[256,384]{1,0:T(8,128)(2,1)S(1)}, u32[]{:S(2)}, u32[]{:S(2)}) collective-permute-start(bf16[256,384]{1,0:T(8,128)(2,1)} %get-tuple-element.74.refs_0_), channel_id=1, source_target_pairs={{0,8},{2,10},{4,12},{6,14},{8,16},{10,18},{12,20},{14,22},{16,24},... | collective-permute-start | bytes 589832 | tf_op jit(solution)/shard_map/ppermute | solution.py:98
  28.8 16.3 %collective-permute-start.5 = (bf16[256,384]{1,0:T(8,128)(2,1)}, bf16[256,384]{1,0:T(8,128)(2,1)S(1)}, u32[]{:S(2)}, u32[]{:S(2)}) collective-permute-start(bf16[256,384]{1,0:T(8,128)(2,1)} %get-tuple-element.74.refs_0_), channel_id=1, source_target_pairs={{0,16},{2,18},{4,20},{6,22},{8,24},{10,26},{12,28},{14,30},{16,0},... | collective-permute-start | bytes 589832 | tf_op jit(solution)/shard_map/ppermute | solution.py:98
  31.4 13.7 %collective-permute-start.6 = (bf16[256,384]{1,0:T(8,128)(2,1)}, bf16[256,384]{1,0:T(8,128)(2,1)S(1)}, u32[]{:S(2)}, u32[]{:S(2)}) collective-permute-start(bf16[256,384]{1,0:T(8,128)(2,1)} %get-tuple-element.74.refs_0_), channel_id=1, source_target_pairs={{0,24},{2,26},{4,28},{6,30},{8,0},{10,2},{12,4},{14,6},{16,8},{18,... | collective-permute-start | bytes 589832 | tf_op jit(solution)/shard_map/ppermute | solution.py:98
  55.8 2.7 collective-permute-start.7
  57.7 22.6 %copy-start.52 = (f32[1024]{0:T(1024)S(1)}, f32[1024]{0:T(1024)}, u32[]{:S(2)}) copy-start(f32[1024]{0:T(1024)} %param.19) | copy-start | bytes 12292
  62.5 10.3 %collective-permute-start.10 = (bf16[128,1024]{1,0:T(8,128)(2,1)}, bf16[128,1024]{1,0:T(8,128)(2,1)S(1)}, u32[]{:S(2)}, u32[]{:S(2)}) collective-permute-start(bf16[128,1024]{1,0:T(8,128)(2,1)} %get-tuple-element.79), channel_id=1, source_target_pairs={{0,6},{2,4},{4,2},{6,0},{8,14},{10,12},{12,10},{14,8},{16,22},{18,... | collective-permute-start | bytes 786440 | tf_op jit(solution)/shard_map/ppermute | solution.py:93
  64.0 14.5 %collective-permute-start.8 = (bf16[128,1024]{1,0:T(8,128)(2,1)}, bf16[128,1024]{1,0:T(8,128)(2,1)S(1)}, u32[]{:S(2)}, u32[]{:S(2)}) collective-permute-start(bf16[128,1024]{1,0:T(8,128)(2,1)} %get-tuple-element.77), channel_id=1, source_target_pairs={{0,2},{2,0},{4,6},{6,4},{8,10},{10,8},{12,14},{14,12},{16,18},{18,... | collective-permute-start | bytes 786440 | tf_op jit(solution)/shard_map/ppermute | solution.py:93
  65.5 13.0 %collective-permute-start.9 = (bf16[128,1024]{1,0:T(8,128)(2,1)}, bf16[128,1024]{1,0:T(8,128)(2,1)S(1)}, u32[]{:S(2)}, u32[]{:S(2)}) collective-permute-start(bf16[128,1024]{1,0:T(8,128)(2,1)} %get-tuple-element.78), channel_id=1, source_target_pairs={{0,4},{2,6},{4,0},{6,2},{8,12},{10,14},{12,8},{14,10},{16,20},{18,... | collective-permute-start | bytes 786440 | tf_op jit(solution)/shard_map/ppermute | solution.py:93
  66.0 23.7 %collective-permute-start.15 = (bf16[256,1024]{1,0:T(8,128)(2,1)}, bf16[256,1024]{1,0:T(8,128)(2,1)S(1)}, u32[]{:S(2)}, u32[]{:S(2)}) collective-permute-start(bf16[256,1024]{1,0:T(8,128)(2,1)} %get-tuple-element.81), channel_id=1, source_target_pairs={{0,2},{2,0},{4,6},{6,4},{8,10},{10,8},{12,14},{14,12},{16,18},{18,... | collective-permute-start | bytes 1572872 | tf_op jit(solution)/shard_map/ppermute | solution.py:93
  67.1 23.7 %collective-permute-start.16 = (bf16[256,1024]{1,0:T(8,128)(2,1)}, bf16[256,1024]{1,0:T(8,128)(2,1)S(1)}, u32[]{:S(2)}, u32[]{:S(2)}) collective-permute-start(bf16[256,1024]{1,0:T(8,128)(2,1)} %get-tuple-element.82), channel_id=1, source_target_pairs={{0,4},{2,6},{4,0},{6,2},{8,12},{10,14},{12,8},{14,10},{16,20},{18,... | collective-permute-start | bytes 1572872 | tf_op jit(solution)/shard_map/ppermute | solution.py:93
  72.8 28.1 %collective-permute-start.17 = (bf16[256,1024]{1,0:T(8,128)(2,1)}, bf16[256,1024]{1,0:T(8,128)(2,1)S(1)}, u32[]{:S(2)}, u32[]{:S(2)}) collective-permute-start(bf16[256,1024]{1,0:T(8,128)(2,1)} %get-tuple-element.83), channel_id=1, source_target_pairs={{0,6},{2,4},{4,2},{6,0},{8,14},{10,12},{12,10},{14,8},{16,22},{18,... | collective-permute-start | bytes 1572872 | tf_op jit(solution)/shard_map/ppermute | solution.py:93
  80.3 32.3 %copy-start.66 = (f32[128]{0:T(128)}, f32[128]{0:T(128)S(1)}, u32[]{:S(2)}) copy-start(f32[128]{0:T(128)S(1)} %add_rsqrt_fusion.4) | copy-start | bytes 1540
  80.4 26.2 %collective-permute-start.11 = (bf16[128,1024]{1,0:T(8,128)(2,1)S(1)}, bf16[128,1024]{1,0:T(8,128)(2,1)S(1)}, u32[]{:S(2)}, u32[]{:S(2)}) collective-permute-start(bf16[128,1024]{1,0:T(8,128)(2,1)S(1)} %multiply_convert_fusion), channel_id=1, source_target_pairs={{0,2},{2,0},{4,6},{6,4},{8,10},{10,8},{12,14},{14,12},{16,18},{18,... | collective-permute-start | bytes 786440 | tf_op jit(solution)/shard_map/ppermute | solution.py:93
  81.0 25.6 %collective-permute-start.12 = (bf16[128,1024]{1,0:T(8,128)(2,1)S(1)}, bf16[128,1024]{1,0:T(8,128)(2,1)}, u32[]{:S(2)}, u32[]{:S(2)}) collective-permute-start(bf16[128,1024]{1,0:T(8,128)(2,1)S(1)} %multiply_convert_fusion), channel_id=1, source_target_pairs={{0,4},{2,6},{4,0},{6,2},{8,12},{10,14},{12,8},{14,10},{16,20},{18,... | collective-permute-start | bytes 786440 | tf_op jit(solution)/shard_map/ppermute | solution.py:93
  89.7 21.8 %collective-permute-start.13 = (bf16[128,1024]{1,0:T(8,128)(2,1)S(1)}, bf16[128,1024]{1,0:T(8,128)(2,1)}, u32[]{:S(2)}, u32[]{:S(2)}) collective-permute-start(bf16[128,1024]{1,0:T(8,128)(2,1)S(1)} %multiply_convert_fusion), channel_id=1, source_target_pairs={{0,6},{2,4},{4,2},{6,0},{8,14},{10,12},{12,10},{14,8},{16,22},{18,... | collective-permute-start | bytes 786440 | tf_op jit(solution)/shard_map/ppermute | solution.py:93
  104.7 74.1 %collective-permute-start.18 = (bf16[512,1024]{1,0:T(8,128)(2,1)}, bf16[512,1024]{1,0:T(8,128)(2,1)}, u32[]{:S(2)}, u32[]{:S(2)}) collective-permute-start(bf16[512,1024]{1,0:T(8,128)(2,1)} %get-tuple-element.84.refs_5_), channel_id=1, source_target_pairs={{0,1},{1,0},{2,3},{3,2},{4,5},{5,4},{6,7},{7,6},{8,9},{9,8},{10,11... | collective-permute-start | bytes 3145736 | tf_op jit(solution)/shard_map/ppermute | solution.py:102
  112.6 67.5 %copy-start.18 = (bf16[512,1024]{1,0:T(8,128)(2,1)}, bf16[512,1024]{1,0:T(8,128)(2,1)S(1)}, u32[]{:S(2)}) copy-start(bf16[512,1024]{1,0:T(8,128)(2,1)S(1)} %pad_maximum_fusion.3.refs_3_) | copy-start | bytes 3145732
  112.6 67.5 %collective-permute-start.14 = (bf16[512,1024]{1,0:T(8,128)(2,1)S(1)}, bf16[512,1024]{1,0:T(8,128)(2,1)}, u32[]{:S(2)}, u32[]{:S(2)}) collective-permute-start(bf16[512,1024]{1,0:T(8,128)(2,1)S(1)} %pad_maximum_fusion.3.refs_3_), channel_id=1, source_target_pairs={{0,1},{1,0},{2,3},{3,2},{4,5},{5,4},{6,7},{7,6},{8,9},{9,8},{10,11... | collective-permute-start | bytes 3145736 | tf_op jit(solution)/shard_map/ppermute | solution.py:102
  112.7 27.1 %collective-permute-start.19 = (bf16[256,1792]{1,0:T(8,128)(2,1)S(1)}, bf16[256,1792]{1,0:T(8,128)(2,1)S(1)}, u32[]{:S(2)}, u32[]{:S(2)}) collective-permute-start(bf16[256,1792]{1,0:T(8,128)(2,1)S(1)} %copy-done.76), channel_id=1, source_target_pairs={{0,8},{2,10},{4,12},{6,14},{8,16},{10,18},{12,20},{14,22},{16,24},... | collective-permute-start | bytes 2752520 | tf_op jit(solution)/shard_map/ppermute | solution.py:98
  116.8 62.1 %collective-permute-start.20 = (bf16[256,1792]{1,0:T(8,128)(2,1)S(1)}, bf16[256,1792]{1,0:T(8,128)(2,1)S(1)}, u32[]{:S(2)}, u32[]{:S(2)}) collective-permute-start(bf16[256,1792]{1,0:T(8,128)(2,1)S(1)} %copy-done.76), channel_id=1, source_target_pairs={{0,16},{2,18},{4,20},{6,22},{8,24},{10,26},{12,28},{14,30},{16,0},... | collective-permute-start | bytes 2752520 | tf_op jit(solution)/shard_map/ppermute | solution.py:98
  119.0 59.8 %collective-permute-start.21 = (bf16[256,1792]{1,0:T(8,128)(2,1)S(1)}, bf16[256,1792]{1,0:T(8,128)(2,1)S(1)}, u32[]{:S(2)}, u32[]{:S(2)}) collective-permute-start(bf16[256,1792]{1,0:T(8,128)(2,1)S(1)} %copy-done.76), channel_id=1, source_target_pairs={{0,24},{2,26},{4,28},{6,30},{8,0},{10,2},{12,4},{14,6},{16,8},{18,... | collective-permute-start | bytes 2752520 | tf_op jit(solution)/shard_map/ppermute | solution.py:98
  139.8 39.1 %copy-start.77 = (bf16[256,1792]{1,0:T(8,128)(2,1)}, bf16[256,1792]{1,0:T(8,128)(2,1)S(1)}, u32[]{:S(2)}) copy-start(bf16[256,1792]{1,0:T(8,128)(2,1)S(1)} %collective-permute-done.19.refs_7_) | copy-start | bytes 2752516
  201.1 3.8 collective-permute-start.26
  201.2 12.0 %collective-permute-start.22 = (bf16[512,1024]{1,0:T(8,128)(2,1)}, bf16[512,1024]{1,0:T(8,128)(2,1)S(1)}, u32[]{:S(2)}, u32[]{:S(2)}) collective-permute-start(bf16[512,1024]{1,0:T(8,128)(2,1)} %get-tuple-element.87), channel_id=1, source_target_pairs={{0,1},{1,0},{2,3},{3,2},{4,5},{5,4},{6,7},{7,6},{8,9},{9,8},{10,11... | collective-permute-start | bytes 3145736 | tf_op jit(solution)/shard_map/ppermute | solution.py:102
  207.8 11.5 %collective-permute-start.27 = (bf16[128,1024]{1,0:T(8,128)(2,1)}, bf16[128,1024]{1,0:T(8,128)(2,1)}, u32[]{:S(2)}, u32[]{:S(2)}) collective-permute-start(bf16[128,1024]{1,0:T(8,128)(2,1)} %get-tuple-element.95), channel_id=1, source_target_pairs={{0,2},{2,0},{4,6},{6,4},{8,10},{10,8},{12,14},{14,12},{16,18},{18,... | collective-permute-start | bytes 786440 | tf_op jit(solution)/shard_map/ppermute | solution.py:93
  209.0 11.8 %collective-permute-start.28 = (bf16[128,1024]{1,0:T(8,128)(2,1)}, bf16[128,1024]{1,0:T(8,128)(2,1)}, u32[]{:S(2)}, u32[]{:S(2)}) collective-permute-start(bf16[128,1024]{1,0:T(8,128)(2,1)} %get-tuple-element.96), channel_id=1, source_target_pairs={{0,4},{2,6},{4,0},{6,2},{8,12},{10,14},{12,8},{14,10},{16,20},{18,... | collective-permute-start | bytes 786440 | tf_op jit(solution)/shard_map/ppermute | solution.py:93
  209.9 14.0 %collective-permute-start.29 = (bf16[128,1024]{1,0:T(8,128)(2,1)}, bf16[128,1024]{1,0:T(8,128)(2,1)}, u32[]{:S(2)}, u32[]{:S(2)}) collective-permute-start(bf16[128,1024]{1,0:T(8,128)(2,1)} %get-tuple-element.97), channel_id=1, source_target_pairs={{0,6},{2,4},{4,2},{6,0},{8,14},{10,12},{12,10},{14,8},{16,22},{18,... | collective-permute-start | bytes 786440 | tf_op jit(solution)/shard_map/ppermute | solution.py:93
  217.3 11.2 %collective-permute-start.23 = (bf16[128,1024]{1,0:T(8,128)(2,1)}, bf16[128,1024]{1,0:T(8,128)(2,1)S(1)}, u32[]{:S(2)}, u32[]{:S(2)}) collective-permute-start(bf16[128,1024]{1,0:T(8,128)(2,1)} %get-tuple-element.89), channel_id=1, source_target_pairs={{0,2},{2,0},{4,6},{6,4},{8,10},{10,8},{12,14},{14,12},{16,18},{18,... | collective-permute-start | bytes 786440 | tf_op jit(solution)/shard_map/ppermute | solution.py:93
  218.4 14.3 %collective-permute-start.24 = (bf16[128,1024]{1,0:T(8,128)(2,1)}, bf16[128,1024]{1,0:T(8,128)(2,1)S(1)}, u32[]{:S(2)}, u32[]{:S(2)}) collective-permute-start(bf16[128,1024]{1,0:T(8,128)(2,1)} %get-tuple-element.90), channel_id=1, source_target_pairs={{0,4},{2,6},{4,0},{6,2},{8,12},{10,14},{12,8},{14,10},{16,20},{18,... | collective-permute-start | bytes 786440 | tf_op jit(solution)/shard_map/ppermute | solution.py:93
  219.3 14.9 %collective-permute-start.25 = (bf16[128,1024]{1,0:T(8,128)(2,1)}, bf16[128,1024]{1,0:T(8,128)(2,1)S(1)}, u32[]{:S(2)}, u32[]{:S(2)}) collective-permute-start(bf16[128,1024]{1,0:T(8,128)(2,1)} %get-tuple-element.91), channel_id=1, source_target_pairs={{0,6},{2,4},{4,2},{6,0},{8,14},{10,12},{12,10},{14,8},{16,22},{18,... | collective-permute-start | bytes 786440 | tf_op jit(solution)/shard_map/ppermute | solution.py:93
  235.4 9.2 %collective-permute-start.30 = (bf16[128,1024]{1,0:T(8,128)(2,1)S(1)}, bf16[128,1024]{1,0:T(8,128)(2,1)S(1)}, u32[]{:S(2)}, u32[]{:S(2)}) collective-permute-start(bf16[128,1024]{1,0:T(8,128)(2,1)S(1)} %get-tuple-element.132), channel_id=1, source_target_pairs={{0,2},{2,0},{4,6},{6,4},{8,10},{10,8},{12,14},{14,12},{16,18},{18,... | collective-permute-start | bytes 786440 | tf_op jit(solution)/shard_map/ppermute | solution.py:93
  236.1 13.6 %collective-permute-start.31 = (bf16[128,1024]{1,0:T(8,128)(2,1)S(1)}, bf16[128,1024]{1,0:T(8,128)(2,1)S(1)}, u32[]{:S(2)}, u32[]{:S(2)}) collective-permute-start(bf16[128,1024]{1,0:T(8,128)(2,1)S(1)} %get-tuple-element.132), channel_id=1, source_target_pairs={{0,4},{2,6},{4,0},{6,2},{8,12},{10,14},{12,8},{14,10},{16,20},{18,... | collective-permute-start | bytes 786440 | tf_op jit(solution)/shard_map/ppermute | solution.py:93
  237.7 12.1 %collective-permute-start.32 = (bf16[128,1024]{1,0:T(8,128)(2,1)S(1)}, bf16[128,1024]{1,0:T(8,128)(2,1)S(1)}, u32[]{:S(2)}, u32[]{:S(2)}) collective-permute-start(bf16[128,1024]{1,0:T(8,128)(2,1)S(1)} %get-tuple-element.132), channel_id=1, source_target_pairs={{0,6},{2,4},{4,2},{6,0},{8,14},{10,12},{12,10},{14,8},{16,22},{18,... | collective-permute-start | bytes 786440 | tf_op jit(solution)/shard_map/ppermute | solution.py:93
  250.8 2.9 collective-permute-start.33
  271.6 31.1 %collective-permute-start.34 = (bf16[512,1024]{1,0:T(8,128)(2,1)}, bf16[512,1024]{1,0:T(8,128)(2,1)}, u32[]{:S(2)}, u32[]{:S(2)}) collective-permute-start(bf16[512,1024]{1,0:T(8,128)(2,1)} %convolution_convert_fusion.1), channel_id=1, source_target_pairs={{0,1},{1,0},{2,3},{3,2},{4,5},{5,4},{6,7},{7,6},{8,9},{9,8},{10,11... | collective-permute-start | bytes 3145736 | tf_op jit(solution)/shard_map/ppermute | solution.py:102
  272.0 41.9 %collective-permute-start.50 = (bf16[256,1792]{1,0:T(8,128)(2,1)}, bf16[256,1792]{1,0:T(8,128)(2,1)}, u32[]{:S(2)}, u32[]{:S(2)}) collective-permute-start(bf16[256,1792]{1,0:T(8,128)(2,1)} %get-tuple-element.115), channel_id=1, source_target_pairs={{0,8},{2,10},{4,12},{6,14},{8,16},{10,18},{12,20},{14,22},{16,24},... | collective-permute-start | bytes 2752520 | tf_op jit(solution)/shard_map/ppermute | solution.py:98
  291.9 61.0 %collective-permute-start.51 = (bf16[256,1792]{1,0:T(8,128)(2,1)}, bf16[256,1792]{1,0:T(8,128)(2,1)}, u32[]{:S(2)}, u32[]{:S(2)}) collective-permute-start(bf16[256,1792]{1,0:T(8,128)(2,1)} %get-tuple-element.116), channel_id=1, source_target_pairs={{0,16},{2,18},{4,20},{6,22},{8,24},{10,26},{12,28},{14,30},{16,0},... | collective-permute-start | bytes 2752520 | tf_op jit(solution)/shard_map/ppermute | solution.py:98
  292.8 78.8 %collective-permute-start.52 = (bf16[256,1792]{1,0:T(8,128)(2,1)}, bf16[256,1792]{1,0:T(8,128)(2,1)}, u32[]{:S(2)}, u32[]{:S(2)}) collective-permute-start(bf16[256,1792]{1,0:T(8,128)(2,1)} %get-tuple-element.117), channel_id=1, source_target_pairs={{0,24},{2,26},{4,28},{6,30},{8,0},{10,2},{12,4},{14,6},{16,8},{18,... | collective-permute-start | bytes 2752520 | tf_op jit(solution)/shard_map/ppermute | solution.py:98
  305.8 75.5 %collective-permute-start.35 = (bf16[128,1024]{1,0:T(8,128)(2,1)}, bf16[128,1024]{1,0:T(8,128)(2,1)S(1)}, u32[]{:S(2)}, u32[]{:S(2)}) collective-permute-start(bf16[128,1024]{1,0:T(8,128)(2,1)} %get-tuple-element.99), channel_id=1, source_target_pairs={{0,2},{2,0},{4,6},{6,4},{8,10},{10,8},{12,14},{14,12},{16,18},{18,... | collective-permute-start | bytes 786440 | tf_op jit(solution)/shard_map/ppermute | solution.py:93
  306.6 75.9 %collective-permute-start.36 = (bf16[128,1024]{1,0:T(8,128)(2,1)}, bf16[128,1024]{1,0:T(8,128)(2,1)S(1)}, u32[]{:S(2)}, u32[]{:S(2)}) collective-permute-start(bf16[128,1024]{1,0:T(8,128)(2,1)} %get-tuple-element.100), channel_id=1, source_target_pairs={{0,4},{2,6},{4,0},{6,2},{8,12},{10,14},{12,8},{14,10},{16,20},{18,... | collective-permute-start | bytes 786440 | tf_op jit(solution)/shard_map/ppermute | solution.py:93
  313.9 57.7 %copy-start.75 = (f32[128]{0:T(128)S(1)}, f32[128]{0:T(128)}, u32[]{:S(2)}) copy-start(f32[128]{0:T(128)} %get-tuple-element.156) | copy-start | bytes 1540
  313.9 69.6 %collective-permute-start.37 = (bf16[128,1024]{1,0:T(8,128)(2,1)}, bf16[128,1024]{1,0:T(8,128)(2,1)S(1)}, u32[]{:S(2)}, u32[]{:S(2)}) collective-permute-start(bf16[128,1024]{1,0:T(8,128)(2,1)} %get-tuple-element.101), channel_id=1, source_target_pairs={{0,6},{2,4},{4,2},{6,0},{8,14},{10,12},{12,10},{14,8},{16,22},{18,... | collective-permute-start | bytes 786440 | tf_op jit(solution)/shard_map/ppermute | solution.py:93
  352.9 26.6 %collective-permute-start.44 = (bf16[256,384]{1,0:T(8,128)(2,1)}, bf16[256,384]{1,0:T(8,128)(2,1)S(1)}, u32[]{:S(2)}, u32[]{:S(2)}) collective-permute-start(bf16[256,384]{1,0:T(8,128)(2,1)} %get-tuple-element.103), channel_id=1, source_target_pairs={{0,8},{2,10},{4,12},{6,14},{8,16},{10,18},{12,20},{14,22},{16,24},... | collective-permute-start | bytes 589832 | tf_op jit(solution)/shard_map/ppermute | solution.py:98
  375.8 20.5 %collective-permute-start.53 = (bf16[64,1792]{1,0:T(8,128)(2,1)}, bf16[64,1792]{1,0:T(8,128)(2,1)S(1)}, u32[]{:S(2)}, u32[]{:S(2)}) collective-permute-start(bf16[64,1792]{1,0:T(8,128)(2,1)} %get-tuple-element.119), channel_id=1, source_target_pairs={{0,2},{2,0},{4,6},{6,4},{8,10},{10,8},{12,14},{14,12},{16,18},{18,... | collective-permute-start | bytes 688136 | tf_op jit(solution)/shard_map/ppermute | solution.py:93
  380.2 18.5 %collective-permute-start.54 = (bf16[64,1792]{1,0:T(8,128)(2,1)}, bf16[64,1792]{1,0:T(8,128)(2,1)S(1)}, u32[]{:S(2)}, u32[]{:S(2)}) collective-permute-start(bf16[64,1792]{1,0:T(8,128)(2,1)} %get-tuple-element.120), channel_id=1, source_target_pairs={{0,4},{2,6},{4,0},{6,2},{8,12},{10,14},{12,8},{14,10},{16,20},{18,... | collective-permute-start | bytes 688136 | tf_op jit(solution)/shard_map/ppermute | solution.py:93
  381.3 18.5 %collective-permute-start.55 = (bf16[64,1792]{1,0:T(8,128)(2,1)}, bf16[64,1792]{1,0:T(8,128)(2,1)S(1)}, u32[]{:S(2)}, u32[]{:S(2)}) collective-permute-start(bf16[64,1792]{1,0:T(8,128)(2,1)} %get-tuple-element.121), channel_id=1, source_target_pairs={{0,6},{2,4},{4,2},{6,0},{8,14},{10,12},{12,10},{14,8},{16,22},{18,... | collective-permute-start | bytes 688136 | tf_op jit(solution)/shard_map/ppermute | solution.py:93
  382.5 10.5 %collective-permute-start.45 = (bf16[256,384]{1,0:T(8,128)(2,1)}, bf16[256,384]{1,0:T(8,128)(2,1)}, u32[]{:S(2)}, u32[]{:S(2)}) collective-permute-start(bf16[256,384]{1,0:T(8,128)(2,1)} %get-tuple-element.104), channel_id=1, source_target_pairs={{0,16},{2,18},{4,20},{6,22},{8,24},{10,26},{12,28},{14,30},{16,0},... | collective-permute-start | bytes 589832 | tf_op jit(solution)/shard_map/ppermute | solution.py:98
  383.5 9.7 %collective-permute-start.46 = (bf16[256,384]{1,0:T(8,128)(2,1)}, bf16[256,384]{1,0:T(8,128)(2,1)}, u32[]{:S(2)}, u32[]{:S(2)}) collective-permute-start(bf16[256,384]{1,0:T(8,128)(2,1)} %get-tuple-element.105), channel_id=1, source_target_pairs={{0,24},{2,26},{4,28},{6,30},{8,0},{10,2},{12,4},{14,6},{16,8},{18,... | collective-permute-start | bytes 589832 | tf_op jit(solution)/shard_map/ppermute | solution.py:98
  384.3 31.6 %copy-start.10 = (f32[128,1024]{1,0:T(8,128)S(1)}, f32[128,1024]{1,0:T(8,128)}, u32[]{:S(2)}) copy-start(f32[128,1024]{1,0:T(8,128)} %get-tuple-element.133) | copy-start | bytes 1572868
  393.0 4.3 %collective-permute-start.38 = (f32[2176]{0:T(1024)S(1)}, f32[2176]{0:T(1024)S(1)}, u32[]{:S(2)}, u32[]{:S(2)}) collective-permute-start(f32[2176]{0:T(1024)S(1)} %concatenate.68), channel_id=1, source_target_pairs={{0,1},{1,0},{2,3},{3,2},{4,5},{5,4},{6,7},{7,6},{8,9},{9,8},{10,11... | collective-permute-start | bytes 26120 | tf_op jit(solution)/shard_map/ppermute | solution.py:102
  395.2 8.0 %collective-permute-start.47 = (bf16[64,384]{1,0:T(8,128)(2,1)}, bf16[64,384]{1,0:T(8,128)(2,1)S(1)}, u32[]{:S(2)}, u32[]{:S(2)}) collective-permute-start(bf16[64,384]{1,0:T(8,128)(2,1)} %get-tuple-element.107), channel_id=1, source_target_pairs={{0,2},{2,0},{4,6},{6,4},{8,10},{10,8},{12,14},{14,12},{16,18},{18,... | collective-permute-start | bytes 147464 | tf_op jit(solution)/shard_map/ppermute | solution.py:93
  396.3 6.9 %collective-permute-start.48 = (bf16[64,384]{1,0:T(8,128)(2,1)}, bf16[64,384]{1,0:T(8,128)(2,1)S(1)}, u32[]{:S(2)}, u32[]{:S(2)}) collective-permute-start(bf16[64,384]{1,0:T(8,128)(2,1)} %get-tuple-element.108), channel_id=1, source_target_pairs={{0,4},{2,6},{4,0},{6,2},{8,12},{10,14},{12,8},{14,10},{16,20},{18,... | collective-permute-start | bytes 147464 | tf_op jit(solution)/shard_map/ppermute | solution.py:93
  397.4 5.8 %collective-permute-start.49 = (bf16[64,384]{1,0:T(8,128)(2,1)}, bf16[64,384]{1,0:T(8,128)(2,1)S(1)}, u32[]{:S(2)}, u32[]{:S(2)}) collective-permute-start(bf16[64,384]{1,0:T(8,128)(2,1)} %get-tuple-element.109), channel_id=1, source_target_pairs={{0,6},{2,4},{4,2},{6,0},{8,14},{10,12},{12,10},{14,8},{16,22},{18,... | collective-permute-start | bytes 147464 | tf_op jit(solution)/shard_map/ppermute | solution.py:93
  398.7 6.8 %collective-permute-start.39 = (f32[2176]{0:T(1024)S(1)}, f32[2176]{0:T(1024)S(1)}, u32[]{:S(2)}, u32[]{:S(2)}) collective-permute-start(f32[2176]{0:T(1024)S(1)} %add.188), channel_id=1, source_target_pairs={{0,2},{2,0},{4,6},{6,4},{8,10},{10,8},{12,14},{14,12},{16,18},{18,... | collective-permute-start | bytes 26120 | tf_op jit(solution)/shard_map/ppermute | solution.py:93
  405.6 3.8 collective-permute-start.40
  409.3 7.8 %collective-permute-start.41 = (f32[2176]{0:T(1024)S(1)}, f32[2176]{0:T(1024)S(1)}, u32[]{:S(2)}, u32[]{:S(2)}) collective-permute-start(f32[2176]{0:T(1024)S(1)} %add.190), channel_id=1, source_target_pairs={{0,8},{2,10},{4,12},{6,14},{8,16},{10,18},{12,20},{14,22},{16,24},... | collective-permute-start | bytes 26120 | tf_op jit(solution)/shard_map/ppermute | solution.py:98
  413.2 4.6 %collective-permute-start.42 = (f32[2176]{0:T(1024)S(1)}, f32[2176]{0:T(1024)S(1)}, u32[]{:S(2)}, u32[]{:S(2)}) collective-permute-start(f32[2176]{0:T(1024)S(1)} %add.190), channel_id=1, source_target_pairs={{0,16},{2,18},{4,20},{6,22},{8,24},{10,26},{12,28},{14,30},{16,0},... | collective-permute-start | bytes 26120 | tf_op jit(solution)/shard_map/ppermute | solution.py:98
  415.9 3.7 collective-permute-start.43
  (72 other events, 324.9 us)

commit v3 on v2

v3 whole, which is shorter than its diff:
```python
import jax
import jax.numpy as jnp
from jax import lax
from jax.experimental import pallas as pl
from jax.experimental.pallas import tpu as pltpu
from jax.sharding import PartitionSpec as P

HEAD_DIM = 64


epsilon = 1e-05
rope_base = 1000000.0
masked_score = -1e30


def inverse_rms(values):
    return lax.rsqrt(jnp.mean(values * values, axis=-1, keepdims=True) + epsilon)


def norm_back(grad_unit, unit, factor):
    return factor * (grad_unit - unit * jnp.mean(grad_unit * unit, axis=-1, keepdims=True))


def matmul(first_op, second_op):
    return jnp.dot(first_op, second_op, preferred_element_type=jnp.float32)


def matmul_nt(first_op, second_op):
    return lax.dot_general(
        first_op, second_op, (((1,), (1,)), ((), ())), preferred_element_type=jnp.float32
    )


def matmul_tn(first_op, second_op):
    return lax.dot_general(
        first_op, second_op, (((0,), (0,)), ((), ())), preferred_element_type=jnp.float32
    )


def seq_layout(seq_lengths, total_rows):
    ends = jnp.cumsum(seq_lengths, dtype=jnp.int32)
    starts = ends - seq_lengths
    row_ids = jnp.arange(total_rows, dtype=jnp.int32)
    segment = jnp.sum(
        (row_ids[:, None] >= ends[None, :]).astype(jnp.int32), axis=1, dtype=jnp.int32
    )
    slot_ids = jnp.arange(seq_lengths.shape[0], dtype=jnp.int32)
    picked = (segment[:, None] == slot_ids[None, :]).astype(jnp.int32)
    begin = (
        jnp.sum(picked * starts[None, :], axis=1, dtype=jnp.int32)
        + (segment == seq_lengths.shape[0]).astype(jnp.int32) * ends[-1]
    )
    allowed = (segment[:, None] == segment[None, :]) & (row_ids[:, None] >= row_ids[None, :])
    return (row_ids - begin, row_ids < ends[-1], allowed)


def rope_tables(position, head_size):
    half_dim = head_size // 2
    freqs = rope_base ** (-jnp.arange(half_dim, dtype=jnp.float32) * 2.0 / head_size)
    angles = position.astype(jnp.float32)[:, None] * freqs[None, :]
    return (jnp.cos(angles)[:, None, :], jnp.sin(angles)[:, None, :])


def rotate(values, cosine, sine):
    half_dim = values.shape[-1] // 2
    first_half = values[..., :half_dim]
    second_half = values[..., half_dim:]
    return jnp.concatenate(
        [first_half * cosine - second_half * sine, second_half * cosine + first_half * sine],
        axis=-1,
    )


def rotate_back(grads, cosine, sine):
    half_dim = grads.shape[-1] // 2
    first_half = grads[..., :half_dim]
    second_half = grads[..., half_dim:]
    return jnp.concatenate(
        [first_half * cosine + second_half * sine, second_half * cosine - first_half * sine],
        axis=-1,
    )

PLANE = 4
LANES = 128
HALF = 64
VMEM_BYTES = 60 * 1024 * 1024
COST = pl.CostEstimate(flops=1024, bytes_accessed=1024, transcendentals=0)
GAIN_ROWS = 8
float32 = jnp.float32
bfloat16 = jnp.bfloat16


def send_plane(values, mask):
    count = lax.axis_size("dp")
    return lax.ppermute(values, "dp", [(i, i ^ mask) for i in range(count)])


def send_deep(values, step):
    count = lax.axis_size("dp")
    return lax.ppermute(values, "dp", [(i, (i + PLANE * step) % count) for i in range(count)])


def swap_cores(values):
    return lax.ppermute(values, "tensor", [(0, 1), (1, 0)])


def call(kernel, outs, *operands, scalars=0, scratch=()):
    specs = [pl.BlockSpec(memory_space=pltpu.SMEM)] * scalars
    specs += [pl.BlockSpec(memory_space=pltpu.VMEM)] * (len(operands) - scalars)
    return pl.pallas_call(
        kernel,
        out_shape=[jax.ShapeDtypeStruct(shape, kind) for shape, kind in outs],
        in_specs=specs,
        out_specs=[pl.BlockSpec(memory_space=pltpu.VMEM)] * len(outs),
        scratch_shapes=list(scratch),
        compiler_params=pltpu.CompilerParams(vmem_limit_bytes=VMEM_BYTES),
        cost_estimate=COST,
    )(*operands)


def lane_ids(shape):
    return lax.broadcasted_iota(jnp.int32, shape, len(shape) - 1)


def half_tile(ref, first_tile, place, upper):
    start = pl.multiple_of((first_tile + place // 2) * LANES, LANES)
    tile = ref[:, pl.ds(start, LANES)].astype(float32)
    turned = pltpu.roll(tile, HALF, 1)
    odd = place % 2 == 1
    if upper:
        return jnp.where(odd, tile, turned)
    return jnp.where(odd, turned, tile)


def padded(values, rows):
    if values.shape[0] == rows:
        return values
    blank = jnp.zeros((rows - values.shape[0], values.shape[1]), values.dtype)
    return jnp.concatenate([values, blank], axis=0)


def attn_rows(rows):
    return (2, rows // 2) if rows % 32 == 0 else (1, max(rows, 16))


def pack_kernel(where_ref, lengths_ref, w_q, w_k, w_v, w_o, w_g, w_u, w_d, *outs):
    rows = w_q.shape[0]
    parts, high = attn_rows(rows)
    tall = max(rows, 16)
    big = w_g.shape[1] // LANES // PLANE * LANES
    last = w_g.shape[1] // LANES // PLANE * PLANE
    place = where_ref[0]
    lane = lane_ids((rows, LANES))
    for mask, out in enumerate(outs):
        other = place ^ mask
        at = pl.multiple_of(other * LANES, LANES)
        tile = jnp.where(
            lane < HALF, half_tile(w_k, 0, other, False), half_tile(w_v, 0, other, True)
        )
        piece = jnp.concatenate(
            [w_q[:, pl.ds(at, LANES)].astype(float32), tile, w_o[:, pl.ds(at, LANES)].astype(float32)],
            axis=1,
        )
        pieces = [piece[: rows // 2], piece[rows // 2 :]] if parts == 2 else [padded(piece, high)]
        width = piece.shape[1]
        for part, values in enumerate(pieces):
            out[:high, part * width : (part + 1) * width] = values.astype(bfloat16)
        free = out.shape[1] - parts * width
        ids = lane_ids((high, free))
        marks = jnp.zeros((high, free), float32)
        for slot in range(lengths_ref.shape[1]):
            marks = jnp.where(ids == free - LANES + slot, lengths_ref[0, slot].astype(float32), marks)
        out[:high, parts * width :] = marks.astype(bfloat16)

        at = pl.multiple_of(other * big, LANES)
        small = jnp.where(
            lane < HALF, half_tile(w_g, last, other, False), half_tile(w_u, last, other, True)
        )
        small_down = jnp.where(lane < HALF, half_tile(w_d, last, other, False), 0.0)
        upper = jnp.concatenate(
            [w_g[:, pl.ds(at, big)].astype(float32), w_u[:, pl.ds(at, big)].astype(float32)], axis=1
        )
        lower = jnp.concatenate(
            [w_d[:, pl.ds(at, big)].astype(float32), small, small_down], axis=1
        )
        out[high : high + tall, :] = padded(upper, tall).astype(bfloat16)
        out[high + tall :, : lower.shape[1]] = padded(lower, tall).astype(bfloat16)
        out[high + tall :, lower.shape[1] :] = jnp.zeros(
            (tall, out.shape[1] - lower.shape[1]), bfloat16
        )


def unpack_kernel(where_ref, own, one, two, three, attn_out, ffn_out, lens_out, held_attn, held_ffn):
    rows = attn_out.shape[0] // PLANE
    width = attn_out.shape[1]
    parts, high = attn_rows(rows)
    tall = max(rows, 16)
    place = where_ref[0]
    for mask, message in enumerate((own, one, two, three)):
        at = pl.ds(pl.multiple_of((place ^ mask) * rows, rows), rows)
        values = [
            message[:high, part * width : (part + 1) * width].astype(float32)
            for part in range(parts)
        ]
        held_attn[at, :] = jnp.concatenate(values, axis=0) if parts == 2 else values[0][:rows]
        lens = message[:16, message.shape[1] - LANES :].astype(float32)
        lens_out[mask * 8 : (mask + 1) * 8, :] = lens[:8]
        full = message.shape[1]
        held_ffn[at, :full] = message[high : high + tall, :].astype(float32)[:rows]
        rest = held_ffn.shape[1] - full
        held_ffn[at, full:] = message[high + tall :, :rest].astype(float32)[:rows]
    attn_out[...] = held_attn[...].astype(bfloat16)
    ffn_out[...] = held_ffn[...].astype(bfloat16)


def split_rows_kernel(own, one, two, three, tok_out, cot_out):
    local = own.shape[0] // 2
    for mask, message in enumerate((own, one, two, three)):
        span = slice(mask * local, (mask + 1) * local)
        tok_out[span, :] = message[:local, :]
        cot_out[span, :] = message[local:, :]


def head_mean(values):
    low = lane_ids(values.shape) < HALF
    first = jnp.sum(jnp.where(low, values, 0.0), axis=1, keepdims=True)
    second = jnp.sum(jnp.where(low, 0.0, values), axis=1, keepdims=True)
    return jnp.where(low, first, second) * (1.0 / HALF)


def turn_halves(values):
    first = lane_ids(values.shape) % HALF < HALF // 2
    return jnp.where(
        first, pltpu.roll(values, LANES - HALF // 2, 1), pltpu.roll(values, HALF // 2, 1)
    )


def at_head(values, head):
    low = lane_ids(values.shape) < HALF
    if head == 0:
        return jnp.where(low, values, 0.0).astype(bfloat16)
    return jnp.where(low, 0.0, pltpu.roll(values, HALF, 1)).astype(bfloat16)


def group_probs(query, key, begin, row_ids, col_ids):
    scores = matmul_nt(query, key) * HEAD_DIM ** (-0.5)
    scores = jnp.where((col_ids >= begin) & (col_ids <= row_ids), scores, masked_score)
    expd = jnp.exp(scores - jnp.max(scores, axis=1, keepdims=True))
    return expd / jnp.sum(expd, axis=1, keepdims=True)


def group_mask(ends_ref, group, rows):
    row_ids = lax.broadcasted_iota(jnp.int32, (rows, rows), 0)
    col_ids = lax.broadcasted_iota(jnp.int32, (rows, rows), 1)
    begin = jnp.zeros((rows, rows), jnp.int32)
    for slot in range(ends_ref.shape[1]):
        end = ends_ref[group, slot]
        begin = jnp.maximum(begin, jnp.where(row_ids >= end, end, 0))
    return begin, row_ids, col_ids


def group_rows(core, mine, other):
    first = jnp.where(core == 0, mine, other)
    second = jnp.where(core == 0, other, mine)
    return jnp.concatenate([first, second], axis=0)


def deep_rows(depth, step, layers, rows):
    at = lax.rem(depth + step + layers, layers) * rows
    return pl.ds(pl.multiple_of(at, rows), rows)


def attn_kernel(layers, where_ref, ends_ref, tok_m, tok_o, a_gain, q_gain, k_gain, cos, sin, *refs):
    pieces, refs = refs[:layers], refs[layers:]
    send, keep, pre_out, low_out, mixed_out, weight, held = refs
    group = pl.program_id(0)
    depth, core = where_ref[1], where_ref[2]
    local = tok_m.shape[0]

    @pl.when(group == 0)
    def _():
        for step, piece in enumerate(pieces):
            weight[deep_rows(depth, -step, layers, piece.shape[0]), :] = piece[...]

    x = group_rows(core, tok_m[...].astype(float32), tok_o[...].astype(float32))
    normed = (x * inverse_rms(x) * a_gain[...]).astype(bfloat16)
    pre = matmul(normed, weight[:, : 2 * LANES])
    pre_out[...] = pre
    cosine, sine = cos[...], sin[...]
    tiles = []
    for number, gain in enumerate((q_gain[...], k_gain[...])):
        tile = pre[:, number * LANES : (number + 1) * LANES]
        scaled = tile * lax.rsqrt(head_mean(tile * tile) + epsilon) * gain
        tiles.append(scaled * cosine + turn_halves(scaled) * sine)
    lane = lane_ids(tiles[0].shape)
    query = tiles[0].astype(bfloat16)
    key_value = jnp.where(lane < HALF, tiles[1], pre[:, LANES:])
    low_out[:, :LANES] = query
    low_out[:, LANES:] = key_value.astype(bfloat16)
    begin, row_ids, col_ids = group_mask(ends_ref, group, x.shape[0])
    turned = pltpu.roll(key_value, HALF, 1)
    mixed = jnp.zeros(tiles[0].shape, float32)
    for head in range(2):
        probs = group_probs(query, at_head(key_value, head), begin, row_ids, col_ids)
        mixed += matmul(probs.astype(bfloat16), at_head(turned, head))
    mixed = mixed.astype(bfloat16)
    mixed_out[...] = mixed
    held[...] = matmul_nt(mixed, weight[:, 2 * LANES :])
    mine = pl.multiple_of(core * local, local)
    other = pl.multiple_of((1 - core) * local, local)
    send[...] = held[pl.ds(other, local), :].astype(bfloat16)
    keep[...] = held[pl.ds(mine, local), :]


def attn_back_kernel(
    layers, where_ref, ends_ref, tok_m, tok_o, a_gain, q_gain, k_gain, cos, sin, dh_m, dh_o,
    pre_ref, low_ref, mixed_ref, weight, gain_ffn, *refs,
):
    send, keep, own, gains_out = refs[:4]
    pieces = refs[4 : 3 + layers]
    held, total, sum_a, sum_qk = refs[3 + layers :]
    group = pl.program_id(0)
    depth, core = where_ref[1], where_ref[2]
    local = tok_m.shape[0]

    @pl.when(group == 0)
    def _():
        total[...] = jnp.zeros_like(total)
        sum_a[...] = jnp.zeros_like(sum_a)
        sum_qk[...] = jnp.zeros_like(sum_qk)

    x = group_rows(core, tok_m[...].astype(float32), tok_o[...].astype(float32))
    unit_a = x * inverse_rms(x)
    normed = (unit_a * a_gain[...]).astype(bfloat16)
    d_hidden = group_rows(core, dh_m[...], dh_o[...])
    mixed = mixed_ref[...]
    total[:, 2 * LANES :] += matmul_tn(d_hidden, mixed)
    d_mixed = matmul(d_hidden, weight[:, 2 * LANES :]).astype(bfloat16)
    query = low_ref[:, :LANES]
    key_value = low_ref[:, LANES:].astype(float32)
    turned = pltpu.roll(key_value, HALF, 1)
    begin, row_ids, col_ids = group_mask(ends_ref, group, x.shape[0])
    scale = HEAD_DIM ** (-0.5)
    shape = mixed.shape
    d_query = jnp.zeros(shape, float32)
    d_keys, d_values = [], []
    for head in range(2):
        key = at_head(key_value, head)
        probs = group_probs(query, key, begin, row_ids, col_ids)
        d_values.append(matmul_tn(probs.astype(bfloat16), d_mixed))
        d_probs = matmul_nt(d_mixed, at_head(turned, head))
        centre = jnp.sum(probs * d_probs, axis=1, keepdims=True)
        d_scores = (probs * (d_probs - centre)).astype(bfloat16)
        d_query += matmul(d_scores, key)
        d_keys.append(matmul_tn(d_scores, query))
    d_key = d_keys[0] + pltpu.roll(d_keys[1], HALF, 1)
    d_value = pltpu.roll(d_values[0], HALF, 1) + d_values[1]
    lane = lane_ids(shape)
    cosine, sine = cos[...], sin[...]
    tiles = []
    for number, (grad, gain) in enumerate(((d_query, q_gain[...]), (d_key, k_gain[...]))):
        grad = grad * scale
        back = grad * cosine - turn_halves(grad) * sine
        tile = pre_ref[:, number * LANES : (number + 1) * LANES]
        factor = lax.rsqrt(head_mean(tile * tile) + epsilon)
        unit = tile * factor
        sum_qk[number : number + 1, :] += jnp.sum(back * unit, axis=0, keepdims=True)
        back = back * gain
        tiles.append(factor * (back - unit * head_mean(back * unit)))
    tiles[1] = jnp.where(lane < HALF, tiles[1], d_value)
    d_qkv = jnp.concatenate(tiles, axis=1).astype(bfloat16)
    total[:, : 2 * LANES] += matmul_tn(normed, d_qkv)
    held[...] = matmul_nt(d_qkv, weight[:, : 2 * LANES])
    sum_a[...] += jnp.sum(held[...] * unit_a, axis=0, keepdims=True)
    mine = pl.multiple_of(core * local, local)
    other = pl.multiple_of((1 - core) * local, local)
    send[...] = held[pl.ds(other, local), :].astype(bfloat16)
    keep[...] = held[pl.ds(mine, local), :]

    @pl.when(group == pl.num_programs(0) - 1)
    def _():
        for row in range(GAIN_ROWS):
            gains_out[row : row + 1, :LANES] = sum_a[:, row * LANES : (row + 1) * LANES]
            gains_out[row : row + 1, LANES : 2 * LANES] = gain_ffn[:, row * LANES : (row + 1) * LANES]
        q_sum = sum_qk[0:1, :] + pltpu.roll(sum_qk[0:1, :], HALF, 1)
        k_sum = pltpu.roll(sum_qk[1:2, :], HALF, 1)
        qk_sum = jnp.where(lane_ids(q_sum.shape) < HALF, q_sum, k_sum)
        ids = lax.broadcasted_iota(jnp.int32, (GAIN_ROWS, LANES), 0)
        gains_out[:, 2 * LANES :] = jnp.where(ids == 0, qk_sum, 0.0)
        gains = gains_out[...]
        top = gains.astype(bfloat16)
        rest = (gains - top.astype(float32)).astype(bfloat16)
        tail = jnp.concatenate([top.astype(float32), rest.astype(float32)], axis=0).astype(bfloat16)
        rows = own.shape[0]
        own[...] = total[deep_rows(depth, 0, layers, rows), :]
        for index, piece in enumerate(pieces):
            piece[:rows, :] = total[deep_rows(depth, index + 1, layers, rows), :].astype(bfloat16)
            piece[rows:, :] = tail


def attn_specs(rows, width, group_height):
    scalar = pl.BlockSpec(memory_space=pltpu.SMEM)
    block = pl.BlockSpec((rows, width), lambda i: (i, 0))
    gain = pl.BlockSpec((1, width), lambda i: (0, 0))
    small = pl.BlockSpec((1, LANES), lambda i: (0, 0))
    table = pl.BlockSpec((group_height, LANES), lambda i: (i, 0))
    wide = pl.BlockSpec((group_height, 2 * LANES), lambda i: (i, 0))
    return scalar, block, gain, small, table, wide


def whole_spec(shape):
    return pl.BlockSpec(shape, lambda i: (0, 0), pipeline_mode=pl.Buffered(1))


def attn(where, ends, tok_mine, tok_other, gains, tables, pieces):
    layers = len(pieces)
    rows, width = tok_mine.shape
    local = rows // PLANE
    scalar, block, gain, small, table, wide = attn_specs(local, width, 2 * local)
    high, columns = pieces[0].shape
    weight = (layers * high, columns)
    return pl.pallas_call(
        lambda *refs: attn_kernel(layers, *refs),
        grid=(PLANE,),
        in_specs=[scalar, scalar, block, block, gain, small, small, table, table]
        + [whole_spec((high, columns))] * layers,
        out_specs=[block, block, wide, wide, table, whole_spec(weight)],
        out_shape=[
            jax.ShapeDtypeStruct((rows, width), bfloat16),
            jax.ShapeDtypeStruct((rows, width), float32),
            jax.ShapeDtypeStruct((2 * rows, 2 * LANES), float32),
            jax.ShapeDtypeStruct((2 * rows, 2 * LANES), bfloat16),
            jax.ShapeDtypeStruct((2 * rows, LANES), bfloat16),
            jax.ShapeDtypeStruct(weight, bfloat16),
        ],
        scratch_shapes=[pltpu.VMEM((2 * local, width), float32)],
        compiler_params=pltpu.CompilerParams(vmem_limit_bytes=VMEM_BYTES),
        cost_estimate=COST,
    )(where, ends, tok_mine, tok_other, *gains, *tables, *pieces)


def attn_back(where, ends, layers, tok_mine, tok_other, gains, tables, dh, saved, weight, gain_ffn):
    rows, width = tok_mine.shape
    local = rows // PLANE
    scalar, block, gain, small, table, wide = attn_specs(local, width, 2 * local)
    high, columns = weight.shape[0] // layers, weight.shape[1]
    tail = 2 * GAIN_ROWS
    return pl.pallas_call(
        lambda *refs: attn_back_kernel(layers, *refs),
        grid=(PLANE,),
        in_specs=[scalar, scalar, block, block, gain, small, small, table, table, block, block]
        + [wide, wide, table, whole_spec(weight.shape), gain],
        out_specs=[block, block, whole_spec((high, columns)), whole_spec((GAIN_ROWS, columns))]
        + [whole_spec((high + tail, columns))] * (layers - 1),
        out_shape=[
            jax.ShapeDtypeStruct((rows, width), bfloat16),
            jax.ShapeDtypeStruct((rows, width), float32),
            jax.ShapeDtypeStruct((high, columns), float32),
            jax.ShapeDtypeStruct((GAIN_ROWS, columns), float32),
        ]
        + [jax.ShapeDtypeStruct((high + tail, columns), bfloat16)] * (layers - 1),
        scratch_shapes=[
            pltpu.VMEM((2 * local, width), float32),
            pltpu.VMEM(weight.shape, float32),
            pltpu.VMEM((1, width), float32),
            pltpu.VMEM((8, LANES), float32),
        ],
        compiler_params=pltpu.CompilerParams(vmem_limit_bytes=VMEM_BYTES),
        cost_estimate=COST,
    )(where, ends, tok_mine, tok_other, *gains, *tables, *dh, *saved, weight, gain_ffn)


def ffn_kernel(layers, where_ref, ends_ref, x_o, x_m, g_o, g_m, *refs):
    pieces, refs = refs[:layers], refs[layers:]
    out_send, out_keep, dn_send, dn_keep, own_grad = refs[:5]
    grad_pieces = refs[5 : 4 + layers]
    weight, total = refs[4 + layers :]
    step = pl.program_id(0)
    depth, core = where_ref[1], where_ref[2]
    rows = pieces[0].shape[0]
    width = x_o.shape[1]
    both = width
    big = both // 2
    local = x_o.shape[0] // 2

    def row_of(index):
        at = lax.rem(depth + index + layers, layers) * rows
        return pl.ds(pl.multiple_of(at, rows), rows)

    @pl.when(step == 0)
    def _():
        for index, piece in enumerate(pieces):
            weight[row_of(-index), :] = piece[...]
        total[...] = jnp.zeros_like(total)

    def live_rows(values, group, at_core):
        ids = lax.broadcasted_iota(jnp.int32, values.shape, 0) + at_core * local
        return jnp.where(ids < ends_ref[group, ends_ref.shape[1] - 1], values, jnp.zeros_like(values))

    x = jnp.concatenate([x_o[...], x_m[...]], axis=0)
    grads = jnp.concatenate(
        [live_rows(g_o[k * local : (k + 1) * local, :], 2 * step + k, 1 - core) for k in range(2)]
        + [live_rows(g_m[k * local : (k + 1) * local, :], 2 * step + k, core) for k in range(2)],
        axis=0,
    )
    half = 2 * local
    w_both = weight[:, :both]
    w_down = weight[:, both : both + big]
    w_small = weight[:, both + big : both + big + LANES]
    w_small_down = weight[:, both + big + LANES :]
    lane = lane_ids((x.shape[0], LANES))

    def parts_of(gate, up, d_act):
        sigma = 1.0 / (1.0 + jnp.exp(-gate))
        silu = gate * sigma
        act = silu * up
        d_gate = d_act * up * sigma * (1.0 + gate * (1.0 - sigma))
        return act, d_gate, d_act * silu

    pre = matmul(x, w_both)
    act, d_gate, d_up = parts_of(pre[:, :big], pre[:, big:], matmul(grads, w_down))
    pre = matmul(x, w_small)
    act_s, d_gate_s, d_up_s = parts_of(
        pre, pltpu.roll(pre, HALF, 1), matmul(grads, w_small_down)
    )
    act_s = jnp.where(lane < HALF, act_s, 0.0).astype(bfloat16)
    d_small = jnp.where(lane < HALF, d_gate_s, pltpu.roll(d_up_s, HALF, 1)).astype(bfloat16)
    act = act.astype(bfloat16)
    d_both = jnp.concatenate([d_gate, d_up], axis=1).astype(bfloat16)

    partial = matmul_nt(act, w_down) + matmul_nt(act_s, w_small_down)
    out_send[...] = partial[:half].astype(bfloat16)
    out_keep[...] = partial[half:]
    partial = matmul_nt(d_both, w_both) + matmul_nt(d_small, w_small)
    dn_send[...] = partial[:half].astype(bfloat16)
    dn_keep[...] = partial[half:]
    total[:, :both] += matmul_tn(x, d_both)
    total[:, both : both + big] += matmul_tn(grads, act)
    total[:, both + big : both + big + LANES] += matmul_tn(x, d_small)
    total[:, both + big + LANES :] += matmul_tn(grads, act_s)

    @pl.when(step == pl.num_programs(0) - 1)
    def _():
        own_grad[...] = total[row_of(0), :]
        for index, piece in enumerate(grad_pieces):
            piece[...] = total[row_of(index + 1), :].astype(bfloat16)


def ffn(where, ends, x_mine, x_other, g_mine, g_other, pieces):
    layers = len(pieces)
    rows, width = x_mine.shape
    high, columns = pieces[0].shape
    block = rows // 2
    row_spec = pl.BlockSpec((block, width), lambda i: (i, 0))

    scalar = pl.BlockSpec(memory_space=pltpu.SMEM)
    return pl.pallas_call(
        lambda *refs: ffn_kernel(layers, *refs),
        grid=(2,),
        in_specs=[scalar, scalar] + [row_spec] * 4 + [whole_spec((high, columns))] * layers,
        out_specs=[row_spec] * 4 + [whole_spec((high, columns))] * layers,
        out_shape=[
            jax.ShapeDtypeStruct((rows, width), bfloat16),
            jax.ShapeDtypeStruct((rows, width), float32),
            jax.ShapeDtypeStruct((rows, width), bfloat16),
            jax.ShapeDtypeStruct((rows, width), float32),
            jax.ShapeDtypeStruct((high, columns), float32),
        ]
        + [jax.ShapeDtypeStruct((high, columns), bfloat16)] * (layers - 1),
        scratch_shapes=[
            pltpu.VMEM((layers * high, columns), bfloat16),
            pltpu.VMEM((layers * high, columns), float32),
        ],
        compiler_params=pltpu.CompilerParams(vmem_limit_bytes=VMEM_BYTES),
        cost_estimate=COST,
    )(where, ends, x_other, x_mine, g_other, g_mine, *pieces)


def chip_sum_kernel(keep, received, *outs):
    rows = outs[0].shape[0]
    for mask, out in enumerate(outs):
        span = slice(mask * rows, (mask + 1) * rows)
        out[...] = (keep[span, :] + received[span, :].astype(float32)).astype(out.dtype)


def chip_sum(keep, received):
    shape = (keep.shape[0] // PLANE, keep.shape[1])
    own, *rest = call(
        chip_sum_kernel, [(shape, float32)] + [(shape, bfloat16)] * (PLANE - 1), keep, received
    )
    return [own] + [send_plane(part, mask + 1) for mask, part in enumerate(rest)]


def add_up(parts):
    return sum(part.astype(float32) for part in parts)


def plane_sum_kernel(where_ref, own, *refs):
    received, outs, held = refs[: -PLANE - 1], refs[-PLANE - 1 : -1], refs[-1]
    value = own[...]
    high = own.shape[0]
    for part in received:
        value = value + part[:high, :].astype(float32)
    held[...] = value
    place = where_ref[0]
    rows = high // PLANE
    for mask, out in enumerate(outs):
        at = pl.multiple_of((place ^ mask) * rows, rows)
        out[...] = held[pl.ds(at, rows), :].astype(out.dtype)


def joined_gains(tail):
    return tail[:GAIN_ROWS] + tail[GAIN_ROWS:]


def split_gains(gains):
    top = gains.astype(bfloat16).astype(float32)
    rest = (gains - top).astype(bfloat16).astype(float32)
    return jnp.concatenate([top, rest], axis=0)


def plane_sum_attn_kernel(where_ref, own, gains, *refs):
    received, outs = refs[: -PLANE - 2], refs[-PLANE - 2 : -2]
    held, held_gains = refs[-2:]
    layers = len(received) + 1
    value = own[...]
    high = own.shape[0]
    depth = where_ref[1]
    held_gains[deep_rows(depth, 0, layers, GAIN_ROWS), :] = joined_gains(split_gains(gains[...]))
    for step, part in enumerate(received):
        value = value + part[:high, :].astype(float32)
        held_gains[deep_rows(depth, -1 - step, layers, GAIN_ROWS), :] = joined_gains(
            part[high:, :].astype(float32)
        )
    held[...] = value
    sums = held_gains[:GAIN_ROWS, :]
    for layer in range(1, layers):
        sums = sums + held_gains[layer * GAIN_ROWS : (layer + 1) * GAIN_ROWS, :]
    tail = split_gains(sums)
    place = where_ref[0]
    rows = high // PLANE
    for mask, out in enumerate(outs):
        at = pl.multiple_of((place ^ mask) * rows, rows)
        part = held[pl.ds(at, rows), :]
        if mask:
            tall = out.shape[0] - tail.shape[0]
            out[:tall, :] = padded(part, tall).astype(bfloat16)
            out[tall:, :] = tail.astype(bfloat16)
        else:
            out[:rows, :] = part
            out[rows:, :] = tail


def plane_sum(where, own, grad_pieces, gains=None):
    received = [send_deep(piece, step + 1) for step, piece in enumerate(grad_pieces)]
    rows, columns = own.shape[0] // PLANE, own.shape[1]
    scratch = [pltpu.VMEM(own.shape, float32)]
    if gains is None:
        shapes = [((rows, columns), float32)] + [((rows, columns), bfloat16)] * (PLANE - 1)
        outs = call(plane_sum_kernel, shapes, where, own, *received, scalars=1, scratch=scratch)
    else:
        tail = 2 * GAIN_ROWS
        shapes = [((rows + tail, columns), float32)]
        shapes += [((max(rows, 16) + tail, columns), bfloat16)] * (PLANE - 1)
        scratch.append(pltpu.VMEM(((len(received) + 1) * GAIN_ROWS, columns), float32))
        outs = call(
            plane_sum_attn_kernel, shapes, where, own, gains, *received, scalars=1, scratch=scratch
        )
    return [outs[0]] + [send_plane(part, mask + 1) for mask, part in enumerate(outs[1:])]


def pick_place(refs, place, target, columns, rows):
    value = jnp.zeros((rows, columns.stop - columns.start), float32)
    for mask, ref in enumerate(refs):
        value = jnp.where(place ^ mask == target, ref[:, columns].astype(float32)[:rows], value)
    return value


def place_ffn_kernel(where_ref, own, one, two, three, out_g, out_u, out_d):
    place = where_ref[0]
    refs = (own, one, two, three)
    big = out_g.shape[1] // LANES // PLANE * LANES
    last = PLANE * big
    for mask, ref in enumerate(refs):
        at = pl.ds(pl.multiple_of((place ^ mask) * big, LANES), big)
        for number, out in enumerate((out_g, out_u, out_d)):
            out[:, at] = ref[:, number * big : (number + 1) * big].astype(float32)
    for pair in range(PLANE // 2):
        low = pick_place(refs, place, 2 * pair, slice(3 * big, 3 * big + 2 * LANES), out_g.shape[0])
        high = pick_place(refs, place, 2 * pair + 1, slice(3 * big, 3 * big + 2 * LANES), out_g.shape[0])
        lane = lane_ids((low.shape[0], LANES))
        span = slice(last + pair * LANES, last + (pair + 1) * LANES)
        gu_low, gu_high = low[:, :LANES], high[:, :LANES]
        out_g[:, span] = jnp.where(lane < HALF, gu_low, pltpu.roll(gu_high, HALF, 1))
        out_u[:, span] = jnp.where(lane < HALF, pltpu.roll(gu_low, HALF, 1), gu_high)
        out_d[:, span] = jnp.where(lane < HALF, low[:, LANES:], pltpu.roll(high[:, LANES:], HALF, 1))


def place_attn_kernel(where_ref, own, one, two, three, out_q, out_k, out_v, out_o, out_gains):
    place = where_ref[0]
    refs = (own, one, two, three)
    rows = out_q.shape[0]
    for mask, ref in enumerate(refs):
        at = pl.ds(pl.multiple_of((place ^ mask) * LANES, LANES), LANES)
        out_q[:, at] = ref[:, :LANES].astype(float32)[:rows]
        out_o[:, at] = ref[:, 2 * LANES :].astype(float32)[:rows]
    for pair in range(PLANE // 2):
        low = pick_place(refs, place, 2 * pair, slice(LANES, 2 * LANES), rows)
        high = pick_place(refs, place, 2 * pair + 1, slice(LANES, 2 * LANES), rows)
        lane = lane_ids(low.shape)
        span = slice(pair * LANES, (pair + 1) * LANES)
        out_k[:, span] = jnp.where(lane < HALF, low, pltpu.roll(high, HALF, 1))
        out_v[:, span] = jnp.where(lane < HALF, pltpu.roll(low, HALF, 1), high)
    tails = [joined_gains(ref[ref.shape[0] - 2 * GAIN_ROWS :, :].astype(float32)) for ref in refs]
    out_gains[...] = (tails[0] + tails[1]) + (tails[2] + tails[3])


def gather_rows(local):
    mine = jnp.concatenate([local] + [send_plane(local, mask) for mask in range(1, PLANE)])
    return mine, swap_cores(mine)


def body(
    tokens,
    lengths,
    attn_gain,
    query_gain,
    key_gain,
    ffn_gain,
    w_query,
    w_key,
    w_value,
    w_out,
    w_gate,
    w_up,
    w_down,
    cotangent,
):
    dp = lax.axis_index("dp")
    core = lax.axis_index("tensor")
    layers = lax.axis_size("dp") // PLANE
    where = jnp.stack([dp % PLANE, dp // PLANE, core]).astype(jnp.int32)
    local_rows, model = tokens.shape
    total_rows = local_rows * lax.axis_size("tensor")
    rows = w_query.shape[0]
    q_cols = w_query.shape[1] // PLANE
    kv_cols = w_key.shape[1] // PLANE
    local_kv = kv_cols // HEAD_DIM
    share = q_cols // kv_cols
    attn_cols = 2 * q_cols + 2 * kv_cols
    ff_cols = 3 * (w_gate.shape[1] // LANES // PLANE * LANES) + 2 * LANES

    parts, high = attn_rows(rows)
    tall = max(rows, 16)
    messages = call(
        pack_kernel,
        [((high + 2 * tall, model), bfloat16)] * PLANE,
        where,
        lengths,
        w_query,
        w_key,
        w_value,
        w_out,
        w_gate,
        w_up,
        w_down,
        scalars=2,
    )
    messages = [messages[0]] + [send_plane(messages[m], m) for m in range(1, PLANE)]
    attn_piece, ff_piece, lens = call(
        unpack_kernel,
        [
            ((PLANE * rows, attn_cols), bfloat16),
            ((PLANE * rows, ff_cols), bfloat16),
            ((PLANE * 8, LANES), float32),
        ],
        where,
        *messages,
        scalars=1,
        scratch=[
            pltpu.VMEM((PLANE * rows, attn_cols), float32),
            pltpu.VMEM((PLANE * rows, ff_cols), float32),
        ],
    )
    attn_pieces = [attn_piece] + [send_deep(attn_piece, step) for step in range(1, layers)]
    ff_pieces = [ff_piece] + [send_deep(ff_piece, step) for step in range(1, layers)]
    local = jnp.concatenate([tokens, cotangent])
    tok_mine, cot_mine = call(
        split_rows_kernel,
        [((PLANE * local_rows, model), bfloat16)] * 2,
        local,
        *[send_plane(local, m) for m in range(1, PLANE)],
    )
    tok_other = swap_cores(tok_mine)
    cot_other = swap_cores(cot_mine)

    slots = lengths.shape[1]
    all_lengths = lens.reshape(PLANE, 8, LANES)[:, 0, :slots].astype(jnp.int32)
    ends = jnp.cumsum(all_lengths, axis=1, dtype=jnp.int32)
    row_ids = jnp.arange(total_rows, dtype=jnp.int32)
    begin = jnp.max(
        jnp.where(row_ids[None, :, None] >= ends[:, None, :], ends[:, None, :], 0), axis=2
    )
    position = (row_ids[None, :] - begin).reshape(-1).astype(jnp.float32)
    spread = jnp.arange(LANES, dtype=jnp.int32) % (HEAD_DIM // 2)
    freqs = rope_base ** (-spread.astype(jnp.float32) * 2.0 / HEAD_DIM)
    angles = position[:, None] * freqs[None, :]
    sign = jnp.where(jnp.arange(LANES) % HEAD_DIM < HEAD_DIM // 2, -1.0, 1.0).astype(jnp.float32)
    tables = (jnp.cos(angles), jnp.sin(angles) * sign)
    gains = (
        attn_gain[None, :],
        jnp.concatenate([query_gain, query_gain])[None, :],
        jnp.concatenate([key_gain, key_gain])[None, :],
    )

    inputs = tokens.astype(jnp.float32)
    factor_a = inverse_rms(inputs)
    unit_a = inputs * factor_a
    send, keep, *saved, attn_weight = attn(
        where, ends, tok_mine, tok_other, gains, tables, attn_pieces
    )
    hidden = inputs + add_up(chip_sum(keep, swap_cores(send)))
    factor_b = inverse_rms(hidden)
    unit_b = hidden * factor_b
    x_mine, x_other = gather_rows((unit_b * ffn_gain).astype(jnp.bfloat16))

    out_send, out_keep, dn_send, dn_keep, own_ff, *ff_grads = ffn(
        where, ends, x_mine, x_other, cot_mine, cot_other, ff_pieces
    )
    d_normed2 = add_up(chip_sum(dn_keep, swap_cores(dn_send)))
    grad_out = jnp.where(
        (jnp.arange(local_rows) + core * local_rows < ends[0, slots - 1])[:, None],
        cotangent,
        jnp.zeros_like(cotangent),
    )
    gain_ffn = jnp.sum(d_normed2 * unit_b, axis=0)
    d_hidden = grad_out.astype(jnp.float32) + norm_back(d_normed2 * ffn_gain, unit_b, factor_b)
    h_mine, h_other = gather_rows(d_hidden.astype(jnp.bfloat16))
    ff_parts = plane_sum(where, own_ff, ff_grads)
    block_out = (hidden + add_up(chip_sum(out_keep, swap_cores(out_send)))).astype(jnp.bfloat16)

    send, keep, own_attn, part_gains, *attn_grads = attn_back(
        where, ends, layers, tok_mine, tok_other, gains, tables, (h_mine, h_other), saved,
        attn_weight, gain_ffn[None, :],
    )
    attn_parts = plane_sum(where, own_attn, attn_grads, part_gains)
    d_normed = add_up(chip_sum(keep, swap_cores(send)))
    grad_tokens = d_hidden + norm_back(d_normed * attn_gain, unit_a, factor_a)
    grad_gate, grad_up, grad_down = call(
        place_ffn_kernel, [(w_gate.shape, float32)] * 3, where, *ff_parts, scalars=1
    )
    grad_query, grad_key, grad_value, grad_out_w, sums = call(
        place_attn_kernel,
        [(w.shape, float32) for w in (w_query, w_key, w_value, w_out)]
        + [((GAIN_ROWS, attn_cols), float32)],
        where,
        *attn_parts,
        scalars=1,
    )
    sums = sums + swap_cores(sums)
    return (
        block_out,
        grad_tokens,
        sums[:, :LANES].reshape(-1),
        sums[0, 2 * LANES : 2 * LANES + HEAD_DIM],
        sums[0, 2 * LANES + HEAD_DIM :],
        sums[:, LANES : 2 * LANES].reshape(-1),
        grad_query,
        grad_key,
        grad_value,
        grad_out_w,
        grad_gate,
        grad_up,
        grad_down,
    )


def solution(mesh):
    placed = (
        P(("dp", "tensor"), None),
        P("dp", None),
        P(),
        P(),
        P(),
        P(),
        P("dp", "tensor"),
        P("dp", "tensor"),
        P("dp", "tensor"),
        P("dp", "tensor"),
        P("dp", "tensor"),
        P("dp", "tensor"),
        P("dp", "tensor"),
        P(("dp", "tensor"), None),
    )
    return jax.shard_map(
        body,
        mesh=mesh,
        in_specs=placed,
        out_specs=(
            P(("dp", "tensor"), None),
            P(("dp", "tensor"), None),
            P(),
            P(),
            P(),
            P(),
            P("dp", "tensor"),
            P("dp", "tensor"),
            P("dp", "tensor"),
            P("dp", "tensor"),
            P("dp", "tensor"),
            P("dp", "tensor"),
            P("dp", "tensor"),
        ),
        check_vma=False,
    )
```

time: 422 us -> 420 us (level)
  waiting for transfers between devices: 201 us -> 239 us
  starting transfers between devices: 99.5 us -> 71.9 us
  Pallas kernels: 56.9 us -> 77.6 us
  matrix products: 19 us -> 0 us
  local copies, waits for them, and re-layouts: 24.4 us -> 16.9 us
  other arithmetic: 18.1 us -> 12.8 us
    ppermute x15 -> x12, waiting for transfers between devices: 123 us -> 153 us  [send_deep(): lax.ppermute(values, 'dp', [(i, (i + PLANE * step) % count) for i in rang...]
    ppermute x15 -> x12, starting transfers between devices: 61.6 us -> 32.2 us  [send_deep(): lax.ppermute(values, 'dp', [(i, (i + PLANE * step) % count) for i in rang...]
    pallas_call x13, Pallas kernels: 35.9 us -> 56.6 us  [the longest x11 30.3 us: call(): pl.pallas_call(kernel, out_shape=[jax.ShapeDtypeStruct(shape, kind) for s...]
    dot_general x14 -> x0, matrix products: 19 us -> none  [the longest x4 7.53 us: matmul_nt(): lax.dot_general(first_op, second_op, (((1,), (1,)), ((), ())), preferred_...]
    ppermute x32 -> x30, waiting for transfers between devices: 73 us -> 81.5 us  [send_plane(): return lax.ppermute(values, 'dp', [(i, i ^ mask) for i in range(count)])]
    ppermute x32 -> x30, starting transfers between devices: 37.1 us -> 38.9 us  [send_plane(): return lax.ppermute(values, 'dp', [(i, i ^ mask) for i in range(count)])]
    unnamed x163 -> x88, local copies, waits for them, and re-layouts: 12.5 us -> 12.8 us
  transfers between devices with their start and end apart: 56 -> 51, of which waited for: 29 -> 28; matrix products, arithmetic and copies ran while one was open for 6% -> 2% of each run, Pallas kernels for 6% -> 10%
where the time goes in v3:
time: 420 us
  waiting for transfers between devices  239 us (57%)
  Pallas kernels  77.6 us (18%)
  starting transfers between devices  71.9 us (17%)
  local copies, waits for them, and re-layouts  16.9 us (4%)
  other arithmetic  12.8 us (3%)
    ppermute x12, waiting for transfers between devices, send_deep(): lax.ppermute(values, 'dp', [(i, (i + PLANE * step) % count) for i in rang...  153 us
    ppermute x30, waiting for transfers between devices, send_plane(): return lax.ppermute(values, 'dp', [(i, i ^ mask) for i in range(count)])  81.5 us
    ppermute x30, starting transfers between devices, send_plane(): return lax.ppermute(values, 'dp', [(i, i ^ mask) for i in range(count)])  38.9 us
    ppermute x12, starting transfers between devices, send_deep(): lax.ppermute(values, 'dp', [(i, (i + PLANE * step) % count) for i in rang...  32.2 us
    pallas_call x11, Pallas kernels, call(): pl.pallas_call(kernel, out_shape=[jax.ShapeDtypeStruct(shape, kind) for s...  30.3 us
    pallas_call x1, Pallas kernels, ffn(): pl.pallas_call(lambda *refs: ffn_kernel(layers, *refs), grid=(2,), in_spe...  21 us
    pallas_call x1, Pallas kernels, attn_back(): pl.pallas_call(lambda *refs: attn_back_kernel(layers, *refs), grid=(PLANE...  16 us
    unnamed x88, local copies, waits for them, and re-layouts  12.8 us
  transfers between devices with their start and end apart: 51, of which 28 were waited for; matrix products, arithmetic and copies ran while one was open for 2% of the time, Pallas kernels for 10%

profile of v3, /device:TPU:0, one launch (start us, length us, event | category | flops | bytes accessed | tf_op | source)
XLA Modules:
  0.0 419.7 jit_solution(2031212621706868368)
XLA Ops:
  2.6 4.0 collective-permute-start.5
  7.9 2.5 shard_map.237
  10.4 1.9 collective-permute-start
  12.3 1.5 collective-permute-start.1
  13.8 5.6 %collective-permute-done.5.three = bf16[256,1024]{1,0:T(8,128)(2,1)S(1)} collective-permute-done((bf16[256,1024]{1,0:T(8,128)(2,1)S(1)}, bf16[256,1024]{1,0:T(8,128)(2,1)S(1)}, u32[]{:S(2)}, u32[]{:S(2)}) %collective-permute-start.5) | collective-permute-done | bytes 524320 | tf_op jit(solution)/shard_map/ppermute | solution.py:95
  19.4 2.9 collective-permute-start.2
  22.3 7.5 %collective-permute-done.4.two = bf16[256,1024]{1,0:T(8,128)(2,1)S(1)} collective-permute-done((bf16[256,1024]{1,0:T(8,128)(2,1)S(1)}, bf16[256,1024]{1,0:T(8,128)(2,1)S(1)}, u32[]{:S(2)}, u32[]{:S(2)}) %collective-permute-start.4) | collective-permute-done | bytes 524320 | tf_op jit(solution)/shard_map/ppermute | solution.py:95
  32.0 3.0 shard_map.239
  35.6 2.6 collective-permute-done.one
  38.2 5.6 %collective-permute-done.2.three = bf16[160,1024]{1,0:T(8,128)(2,1)S(1)} collective-permute-done((bf16[160,1024]{1,0:T(8,128)(2,1)}, bf16[160,1024]{1,0:T(8,128)(2,1)S(1)}, u32[]{:S(2)}, u32[]{:S(2)}) %collective-permute-start.2) | collective-permute-done | bytes 327712 | tf_op jit(solution)/shard_map/ppermute | solution.py:95
  44.6 2.5 shard_map.238
  47.0 3.8 collective-permute-start.9
  52.9 3.1 fusion.6
  56.6 10.3 %collective-permute-done.8.refs_11_ = bf16[256,384]{1,0:T(8,128)(2,1)S(1)} collective-permute-done((bf16[256,384]{1,0:T(8,128)(2,1)}, bf16[256,384]{1,0:T(8,128)(2,1)S(1)}, u32[]{:S(2)}, u32[]{:S(2)}) %collective-permute-start.8) | collective-permute-done | bytes 196640 | tf_op jit(solution)/shard_map/ppermute | solution.py:100
  68.1 10.2 %shard_map.240 = (bf16[512,1024]{1,0:T(8,128)(2,1)}, f32[512,1024]{1,0:T(8,128)}, f32[1024,256]{1,0:T(8,128)}, bf16[1024,256]{1,0:T(8,128)(2,1)}, bf16[1024,128]{1,0:T(8,128)(2,1)}, /*index=5*/bf16[1024,384]{1,0:T(8,128)(2,1)}) custom-call(s32[3]{0:T(128)} %pad_add_fusion.where_ref.refs_0_, s32[4,4]{1,0:T(4,128)} %copy-done.38, ...), custom_call_target="tpu_custom_call" | custom-call | flops 1024 | bytes 1024 | tf_op jit(solution)/shard_map/pallas_call | solution.py:422
  78.4 2.9 collective-permute-done.10.received
  82.2 3.0 shard_map.241
  85.2 1.5 collective-permute-start.11
  86.7 1.6 collective-permute-start.12
  88.7 5.9 %collective-permute-done.11 = bf16[128,1024]{1,0:T(8,128)(2,1)S(1)} collective-permute-done((bf16[128,1024]{1,0:T(8,128)(2,1)}, bf16[128,1024]{1,0:T(8,128)(2,1)S(1)}, u32[]{:S(2)}, u32[]{:S(2)}) %collective-permute-start.11) | collective-permute-done | bytes 262176 | tf_op jit(solution)/shard_map/ppermute | solution.py:95
  94.5 6.0 %collective-permute-done.12 = bf16[128,1024]{1,0:T(8,128)(2,1)S(1)} collective-permute-done((bf16[128,1024]{1,0:T(8,128)(2,1)}, bf16[128,1024]{1,0:T(8,128)(2,1)S(1)}, u32[]{:S(2)}, u32[]{:S(2)}) %collective-permute-start.12) | collective-permute-done | bytes 262176 | tf_op jit(solution)/shard_map/ppermute | solution.py:95
  102.1 1.6 collective-permute-start.16
  105.7 6.7 %collective-permute-done.16 = bf16[128,1024]{1,0:T(8,128)(2,1)S(1)} collective-permute-done((bf16[128,1024]{1,0:T(8,128)(2,1)S(1)}, bf16[128,1024]{1,0:T(8,128)(2,1)S(1)}, u32[]{:S(2)}, u32[]{:S(2)}) %collective-permute-start.16) | collective-permute-done | bytes 262176 | tf_op jit(solution)/shard_map/ppermute | solution.py:95
  112.4 3.6 collective-permute-done.15
  116.6 2.5 collective-permute-start.20
  119.1 1.9 collective-permute-start.19
  121.0 17.9 %collective-permute-done.21.refs_9_ = bf16[256,1792]{1,0:T(8,128)(2,1)S(1)} collective-permute-done((bf16[256,1792]{1,0:T(8,128)(2,1)S(1)}, bf16[256,1792]{1,0:T(8,128)(2,1)S(1)}, u32[]{:S(2)}, u32[]{:S(2)}) %collective-permute-start.21) | collective-permute-done | bytes 917536 | tf_op jit(solution)/shard_map/ppermute | solution.py:100
  139.0 60.0 %collective-permute-done.20.refs_8_ = bf16[256,1792]{1,0:T(8,128)(2,1)S(1)} collective-permute-done((bf16[256,1792]{1,0:T(8,128)(2,1)S(1)}, bf16[256,1792]{1,0:T(8,128)(2,1)S(1)}, u32[]{:S(2)}, u32[]{:S(2)}) %collective-permute-start.20) | collective-permute-done | bytes 917536 | tf_op jit(solution)/shard_map/ppermute | solution.py:100
  201.2 21.0 %shard_map.242 = (bf16[512,1024]{1,0:T(8,128)(2,1)}, f32[512,1024]{1,0:T(8,128)}, bf16[512,1024]{1,0:T(8,128)(2,1)}, f32[512,1024]{1,0:T(8,128)}, f32[256,1792]{...) custom-call(s32[3]{0:T(128)} %pad_add_fusion.where_ref.refs_0_, ...), custom_call_target="tpu_custom_call" | custom-call | flops 1024 | bytes 1024 | tf_op jit(solution)/shard_map/pallas_call | solution.py:557
  222.7 2.4 collective-permute-done.26.received
  226.1 3.0 shard_map.244
  229.0 1.5 collective-permute-start.27
  231.1 1.4 collective-permute-start.29
  235.4 3.0 shard_map.243
  238.5 1.5 collective-permute-start.23
  240.5 1.4 collective-permute-start.25
  242.0 2.2 collective-permute-done.28
  245.8 3.9 collective-permute-done.23
  249.7 5.9 %collective-permute-done.24 = bf16[128,1024]{1,0:T(8,128)(2,1)S(1)} collective-permute-done((bf16[128,1024]{1,0:T(8,128)(2,1)}, bf16[128,1024]{1,0:T(8,128)(2,1)S(1)}, u32[]{:S(2)}, u32[]{:S(2)}) %collective-permute-start.24) | collective-permute-done | bytes 262176 | tf_op jit(solution)/shard_map/ppermute | solution.py:95
  256.6 1.4 collective-permute-start.32
  258.6 1.5 collective-permute-start.30
  260.1 6.6 %collective-permute-done.32 = bf16[128,1024]{1,0:T(8,128)(2,1)S(1)} collective-permute-done((bf16[128,1024]{1,0:T(8,128)(2,1)S(1)}, bf16[128,1024]{1,0:T(8,128)(2,1)S(1)}, u32[]{:S(2)}, u32[]{:S(2)}) %collective-permute-start.32) | collective-permute-done | bytes 262176 | tf_op jit(solution)/shard_map/ppermute | solution.py:95
  266.7 4.6 %collective-permute-done.31 = bf16[128,1024]{1,0:T(8,128)(2,1)S(1)} collective-permute-done((bf16[128,1024]{1,0:T(8,128)(2,1)S(1)}, bf16[128,1024]{1,0:T(8,128)(2,1)S(1)}, u32[]{:S(2)}, u32[]{:S(2)}) %collective-permute-start.31) | collective-permute-done | bytes 262176 | tf_op jit(solution)/shard_map/ppermute | solution.py:95
  271.6 3.7 collective-permute-start.47
  276.3 16.0 %shard_map.245 = (bf16[512,1024]{1,0:T(8,128)(2,1)}, f32[512,1024]{1,0:T(8,128)}, f32[256,384]{1,0:T(8,128)}, f32[8,384]{1,0:T(8,128)}, bf16[272,384]{1,0:T(8,12...) custom-call(s32[3]{0:T(128)} %pad_add_fusion.where_ref.refs_0_, s32[4,4]{1,0:T(4,128)} %copy-done.38, ...), custom_call_target="tpu_custom_call" | custom-call | flops 1024 | bytes 1024 | tf_op jit(solution)/shard_map/pallas_call | solution.py:448
  293.0 47.2 %collective-permute-done.38.refs_0_ = bf16[272,384]{1,0:T(8,128)(2,1)S(1)} collective-permute-done((bf16[272,384]{1,0:T(8,128)(2,1)}, bf16[272,384]{1,0:T(8,128)(2,1)S(1)}, u32[]{:S(2)}, u32[]{:S(2)}) %collective-permute-start.38) | collective-permute-done | bytes 208928 | tf_op jit(solution)/shard_map/ppermute | solution.py:100
  340.2 17.7 %collective-permute-start.39 = (bf16[272,384]{1,0:T(8,128)(2,1)}, bf16[272,384]{1,0:T(8,128)(2,1)S(1)}, u32[]{:S(2)}, u32[]{:S(2)}) collective-permute-start(bf16[272,384]{1,0:T(8,128)(2,1)} %get-tuple-element.115), channel_id=1, source_target_pairs={{0,16},{2,18},{4,20},{6,22},{8,24},{10,26},{12,28},{14,30},{16,0},... | collective-permute-start | bytes 626696 | tf_op jit(solution)/shard_map/ppermute | solution.py:100
  357.9 9.9 %collective-permute-done.39.refs_1_ = bf16[272,384]{1,0:T(8,128)(2,1)S(1)} collective-permute-done((bf16[272,384]{1,0:T(8,128)(2,1)}, bf16[272,384]{1,0:T(8,128)(2,1)S(1)}, u32[]{:S(2)}, u32[]{:S(2)}) %collective-permute-start.39) | collective-permute-done | bytes 208928 | tf_op jit(solution)/shard_map/ppermute | solution.py:100
  368.1 6.9 %collective-permute-done.40.refs_2_ = bf16[272,384]{1,0:T(8,128)(2,1)S(1)} collective-permute-done((bf16[272,384]{1,0:T(8,128)(2,1)}, bf16[272,384]{1,0:T(8,128)(2,1)S(1)}, u32[]{:S(2)}, u32[]{:S(2)}) %collective-permute-start.40) | collective-permute-done | bytes 208928 | tf_op jit(solution)/shard_map/ppermute | solution.py:100
  375.7 2.1 shard_map.247
  378.4 1.4 collective-permute-start.42
  379.8 1.4 collective-permute-start.43
  381.2 3.9 shard_map.249
  385.8 1.4 collective-permute-start.49
  387.3 1.4 collective-permute-start.50
  389.3 1.7 shard_map.248
  391.1 2.6 collective-permute-done.48.one
  393.6 2.8 collective-permute-done.49.two
  397.2 2.6 shard_map.250
  401.5 3.0 shard_map.246
  406.5 1.5 collective-permute-start.37
  409.1 3.3 collective-permute-done.35
  412.4 3.9 collective-permute-done.36
  417.6 2.1 fusion.5
  (167 shorter events, 39.0 us)
Async XLA Ops:
  0.6 34.3 %copy-start.41 = (f32[64]{0:T(128)S(1)}, f32[64]{0:T(128)}, u32[]{:S(2)}) copy-start(f32[64]{0:T(128)} %param.18) | copy-start | bytes 772
  0.7 34.3 %copy-start.40 = (f32[64]{0:T(128)S(1)}, f32[64]{0:T(128)}, u32[]{:S(2)}) copy-start(f32[64]{0:T(128)} %param.17) | copy-start | bytes 772
  2.6 28.6 %copy-start.4 = (bf16[256,1024]{1,0:T(8,128)(2,1)}, bf16[256,1024]{1,0:T(8,128)(2,1)S(1)}, u32[]{:S(2)}) copy-start(bf16[256,1024]{1,0:T(8,128)(2,1)S(1)} %constant_dynamic-update-slice_fusion.own) | copy-start | bytes 1572868
  2.6 16.8 %collective-permute-start.5 = (bf16[256,1024]{1,0:T(8,128)(2,1)S(1)}, bf16[256,1024]{1,0:T(8,128)(2,1)S(1)}, u32[]{:S(2)}, u32[]{:S(2)}) collective-permute-start(bf16[256,1024]{1,0:T(8,128)(2,1)S(1)} %constant_dynamic-update-slice_fusion.own), channel_id=1, source_target_pairs={{0,6},{2,4},{4,2},{6,0},{8,14},{10,12},{12,10},{14,8},{16,22},{18,... | collective-permute-start | bytes 1572872 | tf_op jit(solution)/shard_map/ppermute | solution.py:95
  6.6 23.3 %collective-permute-start.4 = (bf16[256,1024]{1,0:T(8,128)(2,1)S(1)}, bf16[256,1024]{1,0:T(8,128)(2,1)S(1)}, u32[]{:S(2)}, u32[]{:S(2)}) collective-permute-start(bf16[256,1024]{1,0:T(8,128)(2,1)S(1)} %constant_dynamic-update-slice_fusion.own), channel_id=1, source_target_pairs={{0,4},{2,6},{4,0},{6,2},{8,12},{10,14},{12,8},{14,10},{16,20},{18,... | collective-permute-start | bytes 1572872 | tf_op jit(solution)/shard_map/ppermute | solution.py:95
  7.1 24.1 %collective-permute-start.3 = (bf16[256,1024]{1,0:T(8,128)(2,1)S(1)}, bf16[256,1024]{1,0:T(8,128)(2,1)S(1)}, u32[]{:S(2)}, u32[]{:S(2)}) collective-permute-start(bf16[256,1024]{1,0:T(8,128)(2,1)S(1)} %constant_dynamic-update-slice_fusion.own), channel_id=1, source_target_pairs={{0,2},{2,0},{4,6},{6,4},{8,10},{10,8},{12,14},{14,12},{16,18},{18,... | collective-permute-start | bytes 1572872 | tf_op jit(solution)/shard_map/ppermute | solution.py:95
  10.4 27.8 %collective-permute-start = (bf16[160,1024]{1,0:T(8,128)(2,1)}, bf16[160,1024]{1,0:T(8,128)(2,1)S(1)}, u32[]{:S(2)}, u32[]{:S(2)}) collective-permute-start(bf16[160,1024]{1,0:T(8,128)(2,1)} %get-tuple-element.76), channel_id=1, source_target_pairs={{0,2},{2,0},{4,6},{6,4},{8,10},{10,8},{12,14},{14,12},{16,18},{18,... | collective-permute-start | bytes 983048 | tf_op jit(solution)/shard_map/ppermute | solution.py:95
  12.3 25.9 %collective-permute-start.1 = (bf16[160,1024]{1,0:T(8,128)(2,1)}, bf16[160,1024]{1,0:T(8,128)(2,1)S(1)}, u32[]{:S(2)}, u32[]{:S(2)}) collective-permute-start(bf16[160,1024]{1,0:T(8,128)(2,1)} %get-tuple-element.77), channel_id=1, source_target_pairs={{0,4},{2,6},{4,0},{6,2},{8,12},{10,14},{12,8},{14,10},{16,20},{18,... | collective-permute-start | bytes 983048 | tf_op jit(solution)/shard_map/ppermute | solution.py:95
  19.4 24.4 %collective-permute-start.2 = (bf16[160,1024]{1,0:T(8,128)(2,1)}, bf16[160,1024]{1,0:T(8,128)(2,1)S(1)}, u32[]{:S(2)}, u32[]{:S(2)}) collective-permute-start(bf16[160,1024]{1,0:T(8,128)(2,1)} %get-tuple-element.78), channel_id=1, source_target_pairs={{0,6},{2,4},{4,2},{6,0},{8,14},{10,12},{12,10},{14,8},{16,22},{18,... | collective-permute-start | bytes 983048 | tf_op jit(solution)/shard_map/ppermute | solution.py:95
  35.0 31.9 %collective-permute-start.6 = (bf16[512,1024]{1,0:T(8,128)(2,1)}, bf16[512,1024]{1,0:T(8,128)(2,1)S(1)}, u32[]{:S(2)}, u32[]{:S(2)}) collective-permute-start(bf16[512,1024]{1,0:T(8,128)(2,1)} %get-tuple-element.80.refs_2_), channel_id=1, source_target_pairs={{0,1},{1,0},{2,3},{3,2},{4,5},{5,4},{6,7},{7,6},{8,9},{9,8},{10,11... | collective-permute-start | bytes 3145736 | tf_op jit(solution)/shard_map/ppermute | solution.py:104
  47.0 9.5 %collective-permute-start.9 = (bf16[256,384]{1,0:T(8,128)(2,1)}, bf16[256,384]{1,0:T(8,128)(2,1)S(1)}, u32[]{:S(2)}, u32[]{:S(2)}) collective-permute-start(bf16[256,384]{1,0:T(8,128)(2,1)} %get-tuple-element.81.refs_9_), channel_id=1, source_target_pairs={{0,24},{2,26},{4,28},{6,30},{8,0},{10,2},{12,4},{14,6},{16,8},{18,... | collective-permute-start | bytes 589832 | tf_op jit(solution)/shard_map/ppermute | solution.py:100
  50.8 16.0 %collective-permute-start.8 = (bf16[256,384]{1,0:T(8,128)(2,1)}, bf16[256,384]{1,0:T(8,128)(2,1)S(1)}, u32[]{:S(2)}, u32[]{:S(2)}) collective-permute-start(bf16[256,384]{1,0:T(8,128)(2,1)} %get-tuple-element.81.refs_9_), channel_id=1, source_target_pairs={{0,16},{2,18},{4,20},{6,22},{8,24},{10,26},{12,28},{14,30},{16,0},... | collective-permute-start | bytes 589832 | tf_op jit(solution)/shard_map/ppermute | solution.py:100
  50.8 16.0 %collective-permute-start.7 = (bf16[256,384]{1,0:T(8,128)(2,1)}, bf16[256,384]{1,0:T(8,128)(2,1)S(1)}, u32[]{:S(2)}, u32[]{:S(2)}) collective-permute-start(bf16[256,384]{1,0:T(8,128)(2,1)} %get-tuple-element.81.refs_9_), channel_id=1, source_target_pairs={{0,8},{2,10},{4,12},{6,14},{8,16},{10,18},{12,20},{14,22},{16,24},... | collective-permute-start | bytes 589832 | tf_op jit(solution)/shard_map/ppermute | solution.py:100
  78.3 22.3 %copy-start.3 = (bf16[128,1024]{1,0:T(8,128)(2,1)S(1)}, bf16[128,1024]{1,0:T(8,128)(2,1)}, u32[]{:S(2)}) copy-start(bf16[128,1024]{1,0:T(8,128)(2,1)} %param.14) | copy-start | bytes 786436
  78.3 2.9 collective-permute-start.10
  82.2 19.8 %copy-start.39 = (f32[1024]{0:T(1024)S(1)}, f32[1024]{0:T(1024)}, u32[]{:S(2)}) copy-start(f32[1024]{0:T(1024)} %param.19) | copy-start | bytes 12292
  85.2 20.5 %copy-start.6 = (bf16[512,1024]{1,0:T(8,128)(2,1)S(1)}, bf16[512,1024]{1,0:T(8,128)(2,1)}, u32[]{:S(2)}) copy-start(bf16[512,1024]{1,0:T(8,128)(2,1)} %get-tuple-element.88.refs_5_) | copy-start | bytes 3145732
  85.2 9.4 %collective-permute-start.11 = (bf16[128,1024]{1,0:T(8,128)(2,1)}, bf16[128,1024]{1,0:T(8,128)(2,1)S(1)}, u32[]{:S(2)}, u32[]{:S(2)}) collective-permute-start(bf16[128,1024]{1,0:T(8,128)(2,1)} %get-tuple-element.85), channel_id=1, source_target_pairs={{0,2},{2,0},{4,6},{6,4},{8,10},{10,8},{12,14},{14,12},{16,18},{18,... | collective-permute-start | bytes 786440 | tf_op jit(solution)/shard_map/ppermute | solution.py:95
  86.7 13.9 %collective-permute-start.12 = (bf16[128,1024]{1,0:T(8,128)(2,1)}, bf16[128,1024]{1,0:T(8,128)(2,1)S(1)}, u32[]{:S(2)}, u32[]{:S(2)}) collective-permute-start(bf16[128,1024]{1,0:T(8,128)(2,1)} %get-tuple-element.86), channel_id=1, source_target_pairs={{0,4},{2,6},{4,0},{6,2},{8,12},{10,14},{12,8},{14,10},{16,20},{18,... | collective-permute-start | bytes 786440 | tf_op jit(solution)/shard_map/ppermute | solution.py:95
  88.2 12.3 %collective-permute-start.13 = (bf16[128,1024]{1,0:T(8,128)(2,1)}, bf16[128,1024]{1,0:T(8,128)(2,1)S(1)}, u32[]{:S(2)}, u32[]{:S(2)}) collective-permute-start(bf16[128,1024]{1,0:T(8,128)(2,1)} %get-tuple-element.87), channel_id=1, source_target_pairs={{0,6},{2,4},{4,2},{6,0},{8,14},{10,12},{12,10},{14,8},{16,22},{18,... | collective-permute-start | bytes 786440 | tf_op jit(solution)/shard_map/ppermute | solution.py:95
  102.1 10.2 %collective-permute-start.16 = (bf16[128,1024]{1,0:T(8,128)(2,1)S(1)}, bf16[128,1024]{1,0:T(8,128)(2,1)S(1)}, u32[]{:S(2)}, u32[]{:S(2)}) collective-permute-start(bf16[128,1024]{1,0:T(8,128)(2,1)S(1)} %multiply_convert_fusion), channel_id=1, source_target_pairs={{0,6},{2,4},{4,2},{6,0},{8,14},{10,12},{12,10},{14,8},{16,22},{18,... | collective-permute-start | bytes 786440 | tf_op jit(solution)/shard_map/ppermute | solution.py:95
  103.7 12.3 %collective-permute-start.15 = (bf16[128,1024]{1,0:T(8,128)(2,1)S(1)}, bf16[128,1024]{1,0:T(8,128)(2,1)S(1)}, u32[]{:S(2)}, u32[]{:S(2)}) collective-permute-start(bf16[128,1024]{1,0:T(8,128)(2,1)S(1)} %multiply_convert_fusion), channel_id=1, source_target_pairs={{0,4},{2,6},{4,0},{6,2},{8,12},{10,14},{12,8},{14,10},{16,20},{18,... | collective-permute-start | bytes 786440 | tf_op jit(solution)/shard_map/ppermute | solution.py:95
  104.9 11.1 %collective-permute-start.14 = (bf16[128,1024]{1,0:T(8,128)(2,1)S(1)}, bf16[128,1024]{1,0:T(8,128)(2,1)S(1)}, u32[]{:S(2)}, u32[]{:S(2)}) collective-permute-start(bf16[128,1024]{1,0:T(8,128)(2,1)S(1)} %multiply_convert_fusion), channel_id=1, source_target_pairs={{0,2},{2,0},{4,6},{6,4},{8,10},{10,8},{12,14},{14,12},{16,18},{18,... | collective-permute-start | bytes 786440 | tf_op jit(solution)/shard_map/ppermute | solution.py:95
  105.7 93.3 %collective-permute-start.18 = (bf16[512,1024]{1,0:T(8,128)(2,1)S(1)}, bf16[512,1024]{1,0:T(8,128)(2,1)S(1)}, u32[]{:S(2)}, u32[]{:S(2)}) collective-permute-start(bf16[512,1024]{1,0:T(8,128)(2,1)S(1)} %copy-done.6), channel_id=1, source_target_pairs={{0,1},{1,0},{2,3},{3,2},{4,5},{5,4},{6,7},{7,6},{8,9},{9,8},{10,11... | collective-permute-start | bytes 3145736 | tf_op jit(solution)/shard_map/ppermute | solution.py:104
  116.1 85.1 %copy-start.1 = (bf16[512,1024]{1,0:T(8,128)(2,1)}, bf16[512,1024]{1,0:T(8,128)(2,1)S(1)}, u32[]{:S(2)}) copy-start(bf16[512,1024]{1,0:T(8,128)(2,1)S(1)} %pad_maximum_fusion.refs_3_) | copy-start | bytes 3145732
  116.1 85.0 %collective-permute-start.17 = (bf16[512,1024]{1,0:T(8,128)(2,1)S(1)}, bf16[512,1024]{1,0:T(8,128)(2,1)}, u32[]{:S(2)}, u32[]{:S(2)}) collective-permute-start(bf16[512,1024]{1,0:T(8,128)(2,1)S(1)} %pad_maximum_fusion.refs_3_), channel_id=1, source_target_pairs={{0,1},{1,0},{2,3},{3,2},{4,5},{5,4},{6,7},{7,6},{8,9},{9,8},{10,11... | collective-permute-start | bytes 3145736 | tf_op jit(solution)/shard_map/ppermute | solution.py:104
  116.2 22.7 %collective-permute-start.21 = (bf16[256,1792]{1,0:T(8,128)(2,1)S(1)}, bf16[256,1792]{1,0:T(8,128)(2,1)S(1)}, u32[]{:S(2)}, u32[]{:S(2)}) collective-permute-start(bf16[256,1792]{1,0:T(8,128)(2,1)S(1)} %copy-done.13), channel_id=1, source_target_pairs={{0,24},{2,26},{4,28},{6,30},{8,0},{10,2},{12,4},{14,6},{16,8},{18,... | collective-permute-start | bytes 2752520 | tf_op jit(solution)/shard_map/ppermute | solution.py:100
  116.6 82.3 %collective-permute-start.20 = (bf16[256,1792]{1,0:T(8,128)(2,1)S(1)}, bf16[256,1792]{1,0:T(8,128)(2,1)S(1)}, u32[]{:S(2)}, u32[]{:S(2)}) collective-permute-start(bf16[256,1792]{1,0:T(8,128)(2,1)S(1)} %copy-done.13), channel_id=1, source_target_pairs={{0,16},{2,18},{4,20},{6,22},{8,24},{10,26},{12,28},{14,30},{16,0},... | collective-permute-start | bytes 2752520 | tf_op jit(solution)/shard_map/ppermute | solution.py:100
  119.1 79.8 %collective-permute-start.19 = (bf16[256,1792]{1,0:T(8,128)(2,1)S(1)}, bf16[256,1792]{1,0:T(8,128)(2,1)S(1)}, u32[]{:S(2)}, u32[]{:S(2)}) collective-permute-start(bf16[256,1792]{1,0:T(8,128)(2,1)S(1)} %copy-done.13), channel_id=1, source_target_pairs={{0,8},{2,10},{4,12},{6,14},{8,16},{10,18},{12,20},{14,22},{16,24},... | collective-permute-start | bytes 2752520 | tf_op jit(solution)/shard_map/ppermute | solution.py:100
  139.0 60.0 %copy-start.14 = (bf16[256,1792]{1,0:T(8,128)(2,1)}, bf16[256,1792]{1,0:T(8,128)(2,1)S(1)}, u32[]{:S(2)}) copy-start(bf16[256,1792]{1,0:T(8,128)(2,1)S(1)} %collective-permute-done.21.refs_9_) | copy-start | bytes 2752516
  222.2 2.9 collective-permute-start.26
  222.2 12.2 %collective-permute-start.22 = (bf16[512,1024]{1,0:T(8,128)(2,1)}, bf16[512,1024]{1,0:T(8,128)(2,1)S(1)}, u32[]{:S(2)}, u32[]{:S(2)}) collective-permute-start(bf16[512,1024]{1,0:T(8,128)(2,1)} %get-tuple-element.91), channel_id=1, source_target_pairs={{0,1},{1,0},{2,3},{3,2},{4,5},{5,4},{6,7},{7,6},{8,9},{9,8},{10,11... | collective-permute-start | bytes 3145736 | tf_op jit(solution)/shard_map/ppermute | solution.py:104
  229.0 11.5 %collective-permute-start.27 = (bf16[128,1024]{1,0:T(8,128)(2,1)}, bf16[128,1024]{1,0:T(8,128)(2,1)S(1)}, u32[]{:S(2)}, u32[]{:S(2)}) collective-permute-start(bf16[128,1024]{1,0:T(8,128)(2,1)} %get-tuple-element.99), channel_id=1, source_target_pairs={{0,2},{2,0},{4,6},{6,4},{8,10},{10,8},{12,14},{14,12},{16,18},{18,... | collective-permute-start | bytes 786440 | tf_op jit(solution)/shard_map/ppermute | solution.py:95
  230.5 13.7 %collective-permute-start.28 = (bf16[128,1024]{1,0:T(8,128)(2,1)}, bf16[128,1024]{1,0:T(8,128)(2,1)S(1)}, u32[]{:S(2)}, u32[]{:S(2)}) collective-permute-start(bf16[128,1024]{1,0:T(8,128)(2,1)} %get-tuple-element.100), channel_id=1, source_target_pairs={{0,4},{2,6},{4,0},{6,2},{8,12},{10,14},{12,8},{14,10},{16,20},{18,... | collective-permute-start | bytes 786440 | tf_op jit(solution)/shard_map/ppermute | solution.py:95
  231.1 13.8 %collective-permute-start.29 = (bf16[128,1024]{1,0:T(8,128)(2,1)}, bf16[128,1024]{1,0:T(8,128)(2,1)S(1)}, u32[]{:S(2)}, u32[]{:S(2)}) collective-permute-start(bf16[128,1024]{1,0:T(8,128)(2,1)} %get-tuple-element.101), channel_id=1, source_target_pairs={{0,6},{2,4},{4,2},{6,0},{8,14},{10,12},{12,10},{14,8},{16,22},{18,... | collective-permute-start | bytes 786440 | tf_op jit(solution)/shard_map/ppermute | solution.py:95
  235.4 20.2 %copy-start.5 = (bf16[128,1024]{1,0:T(8,128)(2,1)S(1)}, bf16[128,1024]{1,0:T(8,128)(2,1)}, u32[]{:S(2)}) copy-start(bf16[128,1024]{1,0:T(8,128)(2,1)} %param.27) | copy-start | bytes 786436
  238.5 17.2 %copy-start.17 = (f32[128,1024]{1,0:T(8,128)S(1)}, f32[128,1024]{1,0:T(8,128)}, u32[]{:S(2)}) copy-start(f32[128,1024]{1,0:T(8,128)} %get-tuple-element.92) | copy-start | bytes 1572868
  238.5 11.2 %collective-permute-start.23 = (bf16[128,1024]{1,0:T(8,128)(2,1)}, bf16[128,1024]{1,0:T(8,128)(2,1)S(1)}, u32[]{:S(2)}, u32[]{:S(2)}) collective-permute-start(bf16[128,1024]{1,0:T(8,128)(2,1)} %get-tuple-element.93), channel_id=1, source_target_pairs={{0,2},{2,0},{4,6},{6,4},{8,10},{10,8},{12,14},{14,12},{16,18},{18,... | collective-permute-start | bytes 786440 | tf_op jit(solution)/shard_map/ppermute | solution.py:95
  239.9 15.7 %collective-permute-start.24 = (bf16[128,1024]{1,0:T(8,128)(2,1)}, bf16[128,1024]{1,0:T(8,128)(2,1)S(1)}, u32[]{:S(2)}, u32[]{:S(2)}) collective-permute-start(bf16[128,1024]{1,0:T(8,128)(2,1)} %get-tuple-element.94), channel_id=1, source_target_pairs={{0,4},{2,6},{4,0},{6,2},{8,12},{10,14},{12,8},{14,10},{16,20},{18,... | collective-permute-start | bytes 786440 | tf_op jit(solution)/shard_map/ppermute | solution.py:95
  240.5 15.1 %collective-permute-start.25 = (bf16[128,1024]{1,0:T(8,128)(2,1)}, bf16[128,1024]{1,0:T(8,128)(2,1)S(1)}, u32[]{:S(2)}, u32[]{:S(2)}) collective-permute-start(bf16[128,1024]{1,0:T(8,128)(2,1)} %get-tuple-element.95), channel_id=1, source_target_pairs={{0,6},{2,4},{4,2},{6,0},{8,14},{10,12},{12,10},{14,8},{16,22},{18,... | collective-permute-start | bytes 786440 | tf_op jit(solution)/shard_map/ppermute | solution.py:95
  255.6 16.0 %copy-start.42 = (bf16[256,1792]{1,0:T(8,128)(2,1)S(1)}, bf16[256,1792]{1,0:T(8,128)(2,1)}, u32[]{:S(2)}) copy-start(bf16[256,1792]{1,0:T(8,128)(2,1)} %get-tuple-element.129) | copy-start | bytes 2752516
  256.6 10.1 %collective-permute-start.32 = (bf16[128,1024]{1,0:T(8,128)(2,1)S(1)}, bf16[128,1024]{1,0:T(8,128)(2,1)S(1)}, u32[]{:S(2)}, u32[]{:S(2)}) collective-permute-start(bf16[128,1024]{1,0:T(8,128)(2,1)S(1)} %get-tuple-element.139), channel_id=1, source_target_pairs={{0,6},{2,4},{4,2},{6,0},{8,14},{10,12},{12,10},{14,8},{16,22},{18,... | collective-permute-start | bytes 786440 | tf_op jit(solution)/shard_map/ppermute | solution.py:95
  258.0 13.3 %collective-permute-start.31 = (bf16[128,1024]{1,0:T(8,128)(2,1)S(1)}, bf16[128,1024]{1,0:T(8,128)(2,1)S(1)}, u32[]{:S(2)}, u32[]{:S(2)}) collective-permute-start(bf16[128,1024]{1,0:T(8,128)(2,1)S(1)} %get-tuple-element.139), channel_id=1, source_target_pairs={{0,4},{2,6},{4,0},{6,2},{8,12},{10,14},{12,8},{14,10},{16,20},{18,... | collective-permute-start | bytes 786440 | tf_op jit(solution)/shard_map/ppermute | solution.py:95
  258.6 12.7 %collective-permute-start.30 = (bf16[128,1024]{1,0:T(8,128)(2,1)S(1)}, bf16[128,1024]{1,0:T(8,128)(2,1)S(1)}, u32[]{:S(2)}, u32[]{:S(2)}) collective-permute-start(bf16[128,1024]{1,0:T(8,128)(2,1)S(1)} %get-tuple-element.139), channel_id=1, source_target_pairs={{0,2},{2,0},{4,6},{6,4},{8,10},{10,8},{12,14},{14,12},{16,18},{18,... | collective-permute-start | bytes 786440 | tf_op jit(solution)/shard_map/ppermute | solution.py:95
  271.4 4.0 collective-permute-start.33
  271.4 106.9 %collective-permute-start.45 = (bf16[256,1792]{1,0:T(8,128)(2,1)}, bf16[256,1792]{1,0:T(8,128)(2,1)}, u32[]{:S(2)}, u32[]{:S(2)}) collective-permute-start(bf16[256,1792]{1,0:T(8,128)(2,1)} %get-tuple-element.127), channel_id=1, source_target_pairs={{0,8},{2,10},{4,12},{6,14},{8,16},{10,18},{12,20},{14,22},{16,24},... | collective-permute-start | bytes 2752520 | tf_op jit(solution)/shard_map/ppermute | solution.py:100
  271.5 108.3 %collective-permute-start.46 = (bf16[256,1792]{1,0:T(8,128)(2,1)}, bf16[256,1792]{1,0:T(8,128)(2,1)}, u32[]{:S(2)}, u32[]{:S(2)}) collective-permute-start(bf16[256,1792]{1,0:T(8,128)(2,1)} %get-tuple-element.128), channel_id=1, source_target_pairs={{0,16},{2,18},{4,20},{6,22},{8,24},{10,26},{12,28},{14,30},{16,0},... | collective-permute-start | bytes 2752520 | tf_op jit(solution)/shard_map/ppermute | solution.py:100
  271.6 109.6 %collective-permute-start.47 = (bf16[256,1792]{1,0:T(8,128)(2,1)S(1)}, bf16[256,1792]{1,0:T(8,128)(2,1)}, u32[]{:S(2)}, u32[]{:S(2)}) collective-permute-start(bf16[256,1792]{1,0:T(8,128)(2,1)S(1)} %copy-done.42), channel_id=1, source_target_pairs={{0,24},{2,26},{4,28},{6,30},{8,0},{10,2},{12,4},{14,6},{16,8},{18,... | collective-permute-start | bytes 2752520 | tf_op jit(solution)/shard_map/ppermute | solution.py:100
  292.3 108.2 %collective-permute-start.34 = (bf16[512,1024]{1,0:T(8,128)(2,1)}, bf16[512,1024]{1,0:T(8,128)(2,1)S(1)}, u32[]{:S(2)}, u32[]{:S(2)}) collective-permute-start(bf16[512,1024]{1,0:T(8,128)(2,1)} %get-tuple-element.107), channel_id=1, source_target_pairs={{0,1},{1,0},{2,3},{3,2},{4,5},{5,4},{6,7},{7,6},{8,9},{9,8},{10,11... | collective-permute-start | bytes 3145736 | tf_op jit(solution)/shard_map/ppermute | solution.py:104
  292.4 47.8 %collective-permute-start.38 = (bf16[272,384]{1,0:T(8,128)(2,1)}, bf16[272,384]{1,0:T(8,128)(2,1)S(1)}, u32[]{:S(2)}, u32[]{:S(2)}) collective-permute-start(bf16[272,384]{1,0:T(8,128)(2,1)} %get-tuple-element.114), channel_id=1, source_target_pairs={{0,8},{2,10},{4,12},{6,14},{8,16},{10,18},{12,20},{14,22},{16,24},... | collective-permute-start | bytes 626696 | tf_op jit(solution)/shard_map/ppermute | solution.py:100
  340.2 34.8 %copy-start.28 = (bf16[272,384]{1,0:T(8,128)(2,1)}, bf16[272,384]{1,0:T(8,128)(2,1)S(1)}, u32[]{:S(2)}) copy-start(bf16[272,384]{1,0:T(8,128)(2,1)S(1)} %collective-permute-done.38.refs_0_) | copy-start | bytes 626692
  340.2 27.6 %collective-permute-start.39 = (bf16[272,384]{1,0:T(8,128)(2,1)}, bf16[272,384]{1,0:T(8,128)(2,1)S(1)}, u32[]{:S(2)}, u32[]{:S(2)}) collective-permute-start(bf16[272,384]{1,0:T(8,128)(2,1)} %get-tuple-element.115), channel_id=1, source_target_pairs={{0,16},{2,18},{4,20},{6,22},{8,24},{10,26},{12,28},{14,30},{16,0},... | collective-permute-start | bytes 626696 | tf_op jit(solution)/shard_map/ppermute | solution.py:100
  367.8 7.2 %collective-permute-start.40 = (bf16[272,384]{1,0:T(8,128)(2,1)}, bf16[272,384]{1,0:T(8,128)(2,1)S(1)}, u32[]{:S(2)}, u32[]{:S(2)}) collective-permute-start(bf16[272,384]{1,0:T(8,128)(2,1)} %get-tuple-element.116), channel_id=1, source_target_pairs={{0,24},{2,26},{4,28},{6,30},{8,0},{10,2},{12,4},{14,6},{16,8},{18,... | collective-permute-start | bytes 626696 | tf_op jit(solution)/shard_map/ppermute | solution.py:100
  377.7 8.1 %collective-permute-start.41 = (bf16[80,384]{1,0:T(8,128)(2,1)}, bf16[80,384]{1,0:T(8,128)(2,1)S(1)}, u32[]{:S(2)}, u32[]{:S(2)}) collective-permute-start(bf16[80,384]{1,0:T(8,128)(2,1)} %get-tuple-element.118), channel_id=1, source_target_pairs={{0,2},{2,0},{4,6},{6,4},{8,10},{10,8},{12,14},{14,12},{16,18},{18,... | collective-permute-start | bytes 184328 | tf_op jit(solution)/shard_map/ppermute | solution.py:95
  378.4 8.9 %collective-permute-start.42 = (bf16[80,384]{1,0:T(8,128)(2,1)}, bf16[80,384]{1,0:T(8,128)(2,1)S(1)}, u32[]{:S(2)}, u32[]{:S(2)}) collective-permute-start(bf16[80,384]{1,0:T(8,128)(2,1)} %get-tuple-element.119), channel_id=1, source_target_pairs={{0,4},{2,6},{4,0},{6,2},{8,12},{10,14},{12,8},{14,10},{16,20},{18,... | collective-permute-start | bytes 184328 | tf_op jit(solution)/shard_map/ppermute | solution.py:95
  379.8 8.9 %collective-permute-start.43 = (bf16[80,384]{1,0:T(8,128)(2,1)}, bf16[80,384]{1,0:T(8,128)(2,1)S(1)}, u32[]{:S(2)}, u32[]{:S(2)}) collective-permute-start(bf16[80,384]{1,0:T(8,128)(2,1)} %get-tuple-element.120), channel_id=1, source_target_pairs={{0,6},{2,4},{4,2},{6,0},{8,14},{10,12},{12,10},{14,8},{16,22},{18,... | collective-permute-start | bytes 184328 | tf_op jit(solution)/shard_map/ppermute | solution.py:95
  385.2 8.4 %collective-permute-start.48 = (bf16[64,1792]{1,0:T(8,128)(2,1)}, bf16[64,1792]{1,0:T(8,128)(2,1)S(1)}, u32[]{:S(2)}, u32[]{:S(2)}) collective-permute-start(bf16[64,1792]{1,0:T(8,128)(2,1)} %get-tuple-element.131), channel_id=1, source_target_pairs={{0,2},{2,0},{4,6},{6,4},{8,10},{10,8},{12,14},{14,12},{16,18},{18,... | collective-permute-start | bytes 688136 | tf_op jit(solution)/shard_map/ppermute | solution.py:95
  385.8 10.6 %collective-permute-start.49 = (bf16[64,1792]{1,0:T(8,128)(2,1)}, bf16[64,1792]{1,0:T(8,128)(2,1)S(1)}, u32[]{:S(2)}, u32[]{:S(2)}) collective-permute-start(bf16[64,1792]{1,0:T(8,128)(2,1)} %get-tuple-element.132), channel_id=1, source_target_pairs={{0,4},{2,6},{4,0},{6,2},{8,12},{10,14},{12,8},{14,10},{16,20},{18,... | collective-permute-start | bytes 688136 | tf_op jit(solution)/shard_map/ppermute | solution.py:95
  387.3 9.2 %collective-permute-start.50 = (bf16[64,1792]{1,0:T(8,128)(2,1)}, bf16[64,1792]{1,0:T(8,128)(2,1)S(1)}, u32[]{:S(2)}, u32[]{:S(2)}) collective-permute-start(bf16[64,1792]{1,0:T(8,128)(2,1)} %get-tuple-element.133), channel_id=1, source_target_pairs={{0,6},{2,4},{4,2},{6,0},{8,14},{10,12},{12,10},{14,8},{16,22},{18,... | collective-permute-start | bytes 688136 | tf_op jit(solution)/shard_map/ppermute | solution.py:95
  391.1 8.8 %collective-permute-start.44 = (f32[8,384]{1,0:T(8,128)}, f32[8,384]{1,0:T(8,128)S(1)}, u32[]{:S(2)}, u32[]{:S(2)}) collective-permute-start(f32[8,384]{1,0:T(8,128)} %get-tuple-element.121), channel_id=1, source_target_pairs={{0,1},{1,0},{2,3},{3,2},{4,5},{5,4},{6,7},{7,6},{8,9},{9,8},{10,11... | collective-permute-start | bytes 36872 | tf_op jit(solution)/shard_map/ppermute | solution.py:104
  397.2 19.1 %copy-start.34 = (f32[1024]{0:T(1024)S(1)}, f32[1024]{0:T(1024)}, u32[]{:S(2)}) copy-start(f32[1024]{0:T(1024)} %param.16) | copy-start | bytes 12292
  404.5 7.9 %collective-permute-start.35 = (bf16[128,1024]{1,0:T(8,128)(2,1)}, bf16[128,1024]{1,0:T(8,128)(2,1)S(1)}, u32[]{:S(2)}, u32[]{:S(2)}) collective-permute-start(bf16[128,1024]{1,0:T(8,128)(2,1)} %get-tuple-element.109), channel_id=1, source_target_pairs={{0,2},{2,0},{4,6},{6,4},{8,10},{10,8},{12,14},{14,12},{16,18},{18,... | collective-permute-start | bytes 786440 | tf_op jit(solution)/shard_map/ppermute | solution.py:95
  405.9 10.4 %collective-permute-start.36 = (bf16[128,1024]{1,0:T(8,128)(2,1)}, bf16[128,1024]{1,0:T(8,128)(2,1)S(1)}, u32[]{:S(2)}, u32[]{:S(2)}) collective-permute-start(bf16[128,1024]{1,0:T(8,128)(2,1)} %get-tuple-element.110), channel_id=1, source_target_pairs={{0,4},{2,6},{4,0},{6,2},{8,12},{10,14},{12,8},{14,10},{16,20},{18,... | collective-permute-start | bytes 786440 | tf_op jit(solution)/shard_map/ppermute | solution.py:95
  406.5 9.8 %collective-permute-start.37 = (bf16[128,1024]{1,0:T(8,128)(2,1)}, bf16[128,1024]{1,0:T(8,128)(2,1)S(1)}, u32[]{:S(2)}, u32[]{:S(2)}) collective-permute-start(bf16[128,1024]{1,0:T(8,128)(2,1)} %get-tuple-element.111), channel_id=1, source_target_pairs={{0,6},{2,4},{4,2},{6,0},{8,14},{10,12},{12,10},{14,8},{16,22},{18,... | collective-permute-start | bytes 786440 | tf_op jit(solution)/shard_map/ppermute | solution.py:95
  (30 other events, 113.7 us)

commit v4 on v3

--- a/solution.py
+++ b/solution.py
@@ -470,27 +470,16 @@
     )(where, ends, tok_mine, tok_other, *gains, *tables, *dh, *saved, weight, gain_ffn)
 
 
-def ffn_kernel(layers, where_ref, ends_ref, x_o, x_m, g_o, g_m, *refs):
-    pieces, refs = refs[:layers], refs[layers:]
-    out_send, out_keep, dn_send, dn_keep, own_grad = refs[:5]
-    grad_pieces = refs[5 : 4 + layers]
-    weight, total = refs[4 + layers :]
+def ffn_kernel(where_ref, ends_ref, x_o, x_m, g_o, g_m, weight, *refs):
+    out_send, out_keep, dn_send, dn_keep, grad_out, total = refs
     step = pl.program_id(0)
-    depth, core = where_ref[1], where_ref[2]
-    rows = pieces[0].shape[0]
-    width = x_o.shape[1]
-    both = width
+    core = where_ref[2]
+    both = x_o.shape[1]
     big = both // 2
     local = x_o.shape[0] // 2
 
-    def row_of(index):
-        at = lax.rem(depth + index + layers, layers) * rows
-        return pl.ds(pl.multiple_of(at, rows), rows)
-
     @pl.when(step == 0)
     def _():
-        for index, piece in enumerate(pieces):
-            weight[row_of(-index), :] = piece[...]
         total[...] = jnp.zeros_like(total)
 
     def live_rows(values, group, at_core):
@@ -541,39 +530,29 @@
 
     @pl.when(step == pl.num_programs(0) - 1)
     def _():
-        own_grad[...] = total[row_of(0), :]
-        for index, piece in enumerate(grad_pieces):
-            piece[...] = total[row_of(index + 1), :].astype(bfloat16)
-
-
-def ffn(where, ends, x_mine, x_other, g_mine, g_other, pieces):
-    layers = len(pieces)
+        grad_out[...] = total[...].astype(bfloat16)
+
+
+def ffn(where, ends, x_mine, x_other, g_mine, g_other, weight):
     rows, width = x_mine.shape
-    high, columns = pieces[0].shape
-    block = rows // 2
-    row_spec = pl.BlockSpec((block, width), lambda i: (i, 0))
-
+    row_spec = pl.BlockSpec((rows // 2, width), lambda i: (i, 0))
     scalar = pl.BlockSpec(memory_space=pltpu.SMEM)
     return pl.pallas_call(
-        lambda *refs: ffn_kernel(layers, *refs),
+        ffn_kernel,
         grid=(2,),
-        in_specs=[scalar, scalar] + [row_spec] * 4 + [whole_spec((high, columns))] * layers,
-        out_specs=[row_spec] * 4 + [whole_spec((high, columns))] * layers,
+        in_specs=[scalar, scalar] + [row_spec] * 4 + [whole_spec(weight.shape)],
+        out_specs=[row_spec] * 4 + [whole_spec(weight.shape)],
         out_shape=[
             jax.ShapeDtypeStruct((rows, width), bfloat16),
             jax.ShapeDtypeStruct((rows, width), float32),
             jax.ShapeDtypeStruct((rows, width), bfloat16),
             jax.ShapeDtypeStruct((rows, width), float32),
-            jax.ShapeDtypeStruct((high, columns), float32),
-        ]
-        + [jax.ShapeDtypeStruct((high, columns), bfloat16)] * (layers - 1),
-        scratch_shapes=[
-            pltpu.VMEM((layers * high, columns), bfloat16),
-            pltpu.VMEM((layers * high, columns), float32),
+            jax.ShapeDtypeStruct(weight.shape, bfloat16),
         ],
+        scratch_shapes=[pltpu.VMEM(weight.shape, float32)],
         compiler_params=pltpu.CompilerParams(vmem_limit_bytes=VMEM_BYTES),
         cost_estimate=COST,
-    )(where, ends, x_other, x_mine, g_other, g_mine, *pieces)
+    )(where, ends, x_other, x_mine, g_other, g_mine, weight)
 
 
 def chip_sum_kernel(keep, received, *outs):
@@ -597,7 +576,7 @@
 
 def plane_sum_kernel(where_ref, own, *refs):
     received, outs, held = refs[: -PLANE - 1], refs[-PLANE - 1 : -1], refs[-1]
-    value = own[...]
+    value = own[...].astype(float32)
     high = own.shape[0]
     for part in received:
         value = value + part[:high, :].astype(float32)
@@ -783,7 +762,10 @@
         ],
     )
     attn_pieces = [attn_piece] + [send_deep(attn_piece, step) for step in range(1, layers)]
-    ff_pieces = [ff_piece] + [send_deep(ff_piece, step) for step in range(1, layers)]
+    columns = [list(range(k, layers * PLANE, PLANE)) for k in range(PLANE)]
+    ff_weight = lax.all_gather(
+        ff_piece, "dp", axis=0, tiled=True, axis_index_groups=columns
+    )
     local = jnp.concatenate([tokens, cotangent])
     tok_mine, cot_mine = call(
         split_rows_kernel,
@@ -824,8 +806,8 @@
     unit_b = hidden * factor_b
     x_mine, x_other = gather_rows((unit_b * ffn_gain).astype(jnp.bfloat16))
 
-    out_send, out_keep, dn_send, dn_keep, own_ff, *ff_grads = ffn(
-        where, ends, x_mine, x_other, cot_mine, cot_other, ff_pieces
+    out_send, out_keep, dn_send, dn_keep, ff_grad = ffn(
+        where, ends, x_mine, x_other, cot_mine, cot_other, ff_weight
     )
     d_normed2 = add_up(chip_sum(dn_keep, swap_cores(dn_send)))
     grad_out = jnp.where(
@@ -836,7 +818,10 @@
     gain_ffn = jnp.sum(d_normed2 * unit_b, axis=0)
     d_hidden = grad_out.astype(jnp.float32) + norm_back(d_normed2 * ffn_gain, unit_b, factor_b)
     h_mine, h_other = gather_rows(d_hidden.astype(jnp.bfloat16))
-    ff_parts = plane_sum(where, own_ff, ff_grads)
+    own_ff = lax.psum_scatter(
+        ff_grad, "dp", scatter_dimension=0, tiled=True, axis_index_groups=columns
+    )
+    ff_parts = plane_sum(where, own_ff, [])
     block_out = (hidden + add_up(chip_sum(out_keep, swap_cores(out_send)))).astype(jnp.bfloat16)
 
     send, keep, own_attn, part_gains, *attn_grads = attn_back(

time: 420 us -> 327 us (0.78)
  waiting for transfers between devices: 239 us -> 163 us
  starting transfers between devices: 71.9 us -> 46.3 us
  between operations: 1 us -> 14.4 us
    ppermute x12 -> x6, waiting for transfers between devices: 153 us -> 48.2 us  [send_deep(): lax.ppermute(values, 'dp', [(i, (i + PLANE * step) % count) for i in rang...]
    ppermute x12 -> x6, starting transfers between devices: 32.2 us -> 8.89 us  [send_deep(): lax.ppermute(values, 'dp', [(i, (i + PLANE * step) % count) for i in rang...]
    ppermute x30, waiting for transfers between devices: 81.5 us -> 104 us  [send_plane(): return lax.ppermute(values, 'dp', [(i, i ^ mask) for i in range(count)])]
    ppermute x9, waiting for transfers between devices: 5.24 us -> 10.7 us  [swap_cores(): return lax.ppermute(values, 'tensor', [(0, 1), (1, 0)])]
    unnamed x88 -> x82, local copies, waits for them, and re-layouts: 12.8 us -> 11.6 us
  transfers between devices with their start and end apart: 51 -> 47, of which waited for: 28 -> 30; matrix products, arithmetic and copies ran while one was open for 2% -> 4% of each run, Pallas kernels for 10% -> 14%
where the time goes in v4:
time: 327 us; the launch traced here: 325 us
  waiting for transfers between devices  163 us (50%)
  Pallas kernels  75.4 us (23%)
  starting transfers between devices  46.3 us (14%)
  local copies, waits for them, and re-layouts  14.8 us (5%)
  between operations  14.4 us (4%)
  other arithmetic  11.7 us (4%)
    ppermute x30, waiting for transfers between devices, send_plane(): return lax.ppermute(values, 'dp', [(i, i ^ mask) for i in range(count)])  104 us
    ppermute x6, waiting for transfers between devices, send_deep(): lax.ppermute(values, 'dp', [(i, (i + PLANE * step) % count) for i in rang...  48.2 us
    ppermute x30, starting transfers between devices, send_plane(): return lax.ppermute(values, 'dp', [(i, i ^ mask) for i in range(count)])  36 us
    pallas_call x11, Pallas kernels, call(): pl.pallas_call(kernel, out_shape=[jax.ShapeDtypeStruct(shape, kind) for s...  28.6 us
    pallas_call x1, Pallas kernels, ffn(): pl.pallas_call(ffn_kernel, grid=(2,), in_specs=[scalar, scalar] + [row_sp...  20.5 us
    pallas_call x1, Pallas kernels, attn_back(): pl.pallas_call(lambda *refs: attn_back_kernel(layers, *refs), grid=(PLANE...  16.1 us
    unnamed x82, local copies, waits for them, and re-layouts  11.6 us
    ppermute x9, waiting for transfers between devices, swap_cores(): return lax.ppermute(values, 'tensor', [(0, 1), (1, 0)])  10.7 us
  transfers between devices with their start and end apart: 47, of which 30 were waited for; matrix products, arithmetic and copies ran while one was open for 4% of the time, Pallas kernels for 14%

profile of v4, /device:TPU:0, one launch (start us, length us, event | category | flops | bytes accessed | tf_op | source)
XLA Modules:
  0.0 325.2 jit_solution(9963102780823280425)
XLA Ops:
  7.9 2.5 shard_map.237
  10.4 2.9 collective-permute-start
  13.3 1.5 collective-permute-start.1
  14.9 7.2 %collective-permute-done.one = bf16[160,1024]{1,0:T(8,128)(2,1)S(1)} collective-permute-done((bf16[160,1024]{1,0:T(8,128)(2,1)}, bf16[160,1024]{1,0:T(8,128)(2,1)S(1)}, u32[]{:S(2)}, u32[]{:S(2)}) %collective-permute-start) | collective-permute-done | bytes 327712 | tf_op jit(solution)/shard_map/ppermute | solution.py:95
  22.1 7.7 %collective-permute-done.1.two = bf16[160,1024]{1,0:T(8,128)(2,1)S(1)} collective-permute-done((bf16[160,1024]{1,0:T(8,128)(2,1)}, bf16[160,1024]{1,0:T(8,128)(2,1)S(1)}, u32[]{:S(2)}, u32[]{:S(2)}) %collective-permute-start.1) | collective-permute-done | bytes 327712 | tf_op jit(solution)/shard_map/ppermute | solution.py:95
  30.6 2.5 shard_map.238
  33.2 1.6 collective-permute-start.5
  36.8 12.3 %collective-permute-done.5.three = bf16[256,1024]{1,0:T(8,128)(2,1)S(1)} collective-permute-done((bf16[256,1024]{1,0:T(8,128)(2,1)S(1)}, bf16[256,1024]{1,0:T(8,128)(2,1)S(1)}, u32[]{:S(2)}, u32[]{:S(2)}) %collective-permute-start.5) | collective-permute-done | bytes 524320 | tf_op jit(solution)/shard_map/ppermute | solution.py:95
  49.0 8.9 %collective-permute-done.4.two = bf16[256,1024]{1,0:T(8,128)(2,1)S(1)} collective-permute-done((bf16[256,1024]{1,0:T(8,128)(2,1)S(1)}, bf16[256,1024]{1,0:T(8,128)(2,1)S(1)}, u32[]{:S(2)}, u32[]{:S(2)}) %collective-permute-start.4) | collective-permute-done | bytes 524320 | tf_op jit(solution)/shard_map/ppermute | solution.py:95
  59.5 2.9 shard_map.239
  63.2 3.6 %collective-permute-start.9 = (bf16[256,384]{1,0:T(8,128)(2,1)S(1)}, bf16[256,384]{1,0:T(8,128)(2,1)S(1)}, u32[]{:S(2)}, u32[]{:S(2)}) collective-permute-start(bf16[256,384]{1,0:T(8,128)(2,1)S(1)} %copy-done.28), channel_id=1, source_target_pairs={{0,24},{2,26},{4,28},{6,30},{8,0},{10,2},{12,4},{14,6},{16,8},{18,... | collective-permute-start | bytes 589832 | tf_op jit(solution)/shard_map/ppermute | solution.py:100
  68.8 3.1 fusion.6
  71.9 6.4 %collective-permute-done.9.refs_12_ = bf16[256,384]{1,0:T(8,128)(2,1)S(1)} collective-permute-done((bf16[256,384]{1,0:T(8,128)(2,1)S(1)}, bf16[256,384]{1,0:T(8,128)(2,1)S(1)}, u32[]{:S(2)}, u32[]{:S(2)}) %collective-permute-start.9) | collective-permute-done | bytes 196640 | tf_op jit(solution)/shard_map/ppermute | solution.py:100
  78.3 27.9 %collective-permute-done.8.refs_11_ = bf16[256,384]{1,0:T(8,128)(2,1)S(1)} collective-permute-done((bf16[256,384]{1,0:T(8,128)(2,1)S(1)}, bf16[256,384]{1,0:T(8,128)(2,1)S(1)}, u32[]{:S(2)}, u32[]{:S(2)}) %collective-permute-start.8) | collective-permute-done | bytes 196640 | tf_op jit(solution)/shard_map/ppermute | solution.py:100
  107.4 10.2 %shard_map.240 = (bf16[512,1024]{1,0:T(8,128)(2,1)}, f32[512,1024]{1,0:T(8,128)}, f32[1024,256]{1,0:T(8,128)}, bf16[1024,256]{1,0:T(8,128)(2,1)}, bf16[1024,128]{1,0:T(8,128)(2,1)}, /*index=5*/bf16[1024,384]{1,0:T(8,128)(2,1)}) custom-call(s32[3]{0:T(128)} %pad_add_fusion.where_ref.refs_0_, s32[4,4]{1,0:T(4,128)} %copy-done.36, ...), custom_call_target="tpu_custom_call" | custom-call | flops 1024 | bytes 1024 | tf_op jit(solution)/shard_map/pallas_call | solution.py:422
  117.9 2.6 collective-permute-done.10.received
  121.5 3.0 shard_map.241
  124.5 1.5 collective-permute-start.11
  125.9 1.4 collective-permute-start.12
  128.0 5.9 %collective-permute-done.11 = bf16[128,1024]{1,0:T(8,128)(2,1)S(1)} collective-permute-done((bf16[128,1024]{1,0:T(8,128)(2,1)}, bf16[128,1024]{1,0:T(8,128)(2,1)S(1)}, u32[]{:S(2)}, u32[]{:S(2)}) %collective-permute-start.11) | collective-permute-done | bytes 262176 | tf_op jit(solution)/shard_map/ppermute | solution.py:95
  133.8 6.1 %collective-permute-done.12 = bf16[128,1024]{1,0:T(8,128)(2,1)S(1)} collective-permute-done((bf16[128,1024]{1,0:T(8,128)(2,1)}, bf16[128,1024]{1,0:T(8,128)(2,1)S(1)}, u32[]{:S(2)}, u32[]{:S(2)}) %collective-permute-start.12) | collective-permute-done | bytes 262176 | tf_op jit(solution)/shard_map/ppermute | solution.py:95
  139.9 1.3 multiply_reduce_fusion.2
  141.4 1.4 collective-permute-start.16
  145.0 6.7 %collective-permute-done.16 = bf16[128,1024]{1,0:T(8,128)(2,1)S(1)} collective-permute-done((bf16[128,1024]{1,0:T(8,128)(2,1)S(1)}, bf16[128,1024]{1,0:T(8,128)(2,1)S(1)}, u32[]{:S(2)}, u32[]{:S(2)}) %collective-permute-start.16) | collective-permute-done | bytes 262176 | tf_op jit(solution)/shard_map/ppermute | solution.py:95
  151.6 3.5 %collective-permute-done.15 = bf16[128,1024]{1,0:T(8,128)(2,1)S(1)} collective-permute-done((bf16[128,1024]{1,0:T(8,128)(2,1)S(1)}, bf16[128,1024]{1,0:T(8,128)(2,1)S(1)}, u32[]{:S(2)}, u32[]{:S(2)}) %collective-permute-start.15) | collective-permute-done | bytes 262176 | tf_op jit(solution)/shard_map/ppermute | solution.py:95
  156.3 1.7 collective-permute-done.17.x_o
  158.1 20.5 %shard_map.242 = (bf16[512,1024]{1,0:T(8,128)(2,1)}, f32[512,1024]{1,0:T(8,128)}, bf16[512,1024]{1,0:T(8,128)(2,1)}, f32[512,1024]{1,0:T(8,128)}, bf16[1024,1792]{1,0:T(8,128)(2,1)}) custom-call(s32[3]{0:T(128)} %pad_add_fusion.where_ref.refs_0_, s32[4,4]{1,0:T(4,128)} %copy-done.36, bf16[512,1024]{1,0:T(8,128)(2,1)} %collective-permute-done.17.x_o, ...), custom_call_target="tpu_custom_call" | custom-call | flops 1024 | bytes 1024 | tf_op jit(solution)/shard_map/pallas_call | solution.py:540
  179.1 2.4 collective-permute-done.23.received
  182.4 3.1 shard_map.244
  185.5 1.5 collective-permute-start.24
  187.0 1.3 collective-permute-start.25
  189.0 1.3 slice.19
  192.0 2.9 shard_map.243
  194.9 1.5 collective-permute-start.20
  196.4 1.3 collective-permute-start.21
  198.4 2.7 collective-permute-done.25
  202.1 4.1 %collective-permute-done.20 = bf16[128,1024]{1,0:T(8,128)(2,1)S(1)} collective-permute-done((bf16[128,1024]{1,0:T(8,128)(2,1)}, bf16[128,1024]{1,0:T(8,128)(2,1)S(1)}, u32[]{:S(2)}, u32[]{:S(2)}) %collective-permute-start.20) | collective-permute-done | bytes 262176 | tf_op jit(solution)/shard_map/ppermute | solution.py:95
  206.2 6.0 %collective-permute-done.21 = bf16[128,1024]{1,0:T(8,128)(2,1)S(1)} collective-permute-done((bf16[128,1024]{1,0:T(8,128)(2,1)}, bf16[128,1024]{1,0:T(8,128)(2,1)S(1)}, u32[]{:S(2)}, u32[]{:S(2)}) %collective-permute-start.21) | collective-permute-done | bytes 262176 | tf_op jit(solution)/shard_map/ppermute | solution.py:95
  213.1 1.3 collective-permute-start.29
  216.6 6.6 %collective-permute-done.29 = bf16[128,1024]{1,0:T(8,128)(2,1)S(1)} collective-permute-done((bf16[128,1024]{1,0:T(8,128)(2,1)S(1)}, bf16[128,1024]{1,0:T(8,128)(2,1)S(1)}, u32[]{:S(2)}, u32[]{:S(2)}) %collective-permute-start.29) | collective-permute-done | bytes 262176 | tf_op jit(solution)/shard_map/ppermute | solution.py:95
  223.2 4.0 %collective-permute-done.28 = bf16[128,1024]{1,0:T(8,128)(2,1)S(1)} collective-permute-done((bf16[128,1024]{1,0:T(8,128)(2,1)S(1)}, bf16[128,1024]{1,0:T(8,128)(2,1)S(1)}, u32[]{:S(2)}, u32[]{:S(2)}) %collective-permute-start.28) | collective-permute-done | bytes 262176 | tf_op jit(solution)/shard_map/ppermute | solution.py:95
  227.4 2.6 collective-permute-done.30.refs_10_
  231.0 16.1 %shard_map.245 = (bf16[512,1024]{1,0:T(8,128)(2,1)}, f32[512,1024]{1,0:T(8,128)}, f32[256,384]{1,0:T(8,128)}, f32[8,384]{1,0:T(8,128)}, bf16[272,384]{1,0:T(8,12...) custom-call(s32[3]{0:T(128)} %pad_add_fusion.where_ref.refs_0_, s32[4,4]{1,0:T(4,128)} %copy-done.36, ...), custom_call_target="tpu_custom_call" | custom-call | flops 1024 | bytes 1024 | tf_op jit(solution)/shard_map/pallas_call | solution.py:448
  247.3 1.3 collective-permute-start.36
  248.6 2.9 collective-permute-start.37
  251.5 5.9 %collective-permute-done.35.refs_0_ = bf16[272,384]{1,0:T(8,128)(2,1)S(1)} collective-permute-done((bf16[272,384]{1,0:T(8,128)(2,1)}, bf16[272,384]{1,0:T(8,128)(2,1)S(1)}, u32[]{:S(2)}, u32[]{:S(2)}) %collective-permute-start.35) | collective-permute-done | bytes 208928 | tf_op jit(solution)/shard_map/ppermute | solution.py:100
  257.4 8.0 %collective-permute-done.36.refs_1_ = bf16[272,384]{1,0:T(8,128)(2,1)S(1)} collective-permute-done((bf16[272,384]{1,0:T(8,128)(2,1)}, bf16[272,384]{1,0:T(8,128)(2,1)S(1)}, u32[]{:S(2)}, u32[]{:S(2)}) %collective-permute-start.36) | collective-permute-done | bytes 208928 | tf_op jit(solution)/shard_map/ppermute | solution.py:100
  266.1 2.1 shard_map.247
  270.0 1.7 collective-permute-start.40
  271.7 1.5 collective-permute-done.38.one
  273.6 1.6 collective-permute-done.40.three
  275.9 1.7 shard_map.248
  277.7 1.4 collective-permute-done.41
  280.7 2.9 shard_map.246
  283.7 1.6 collective-permute-start.32
  288.3 4.7 %collective-permute-done.32 = bf16[128,1024]{1,0:T(8,128)(2,1)S(1)} collective-permute-done((bf16[128,1024]{1,0:T(8,128)(2,1)}, bf16[128,1024]{1,0:T(8,128)(2,1)S(1)}, u32[]{:S(2)}, u32[]{:S(2)}) %collective-permute-start.32) | collective-permute-done | bytes 262176 | tf_op jit(solution)/shard_map/ppermute | solution.py:95
  293.0 6.1 %collective-permute-done.33 = bf16[128,1024]{1,0:T(8,128)(2,1)S(1)} collective-permute-done((bf16[128,1024]{1,0:T(8,128)(2,1)}, bf16[128,1024]{1,0:T(8,128)(2,1)S(1)}, u32[]{:S(2)}, u32[]{:S(2)}) %collective-permute-start.33) | collective-permute-done | bytes 262176 | tf_op jit(solution)/shard_map/ppermute | solution.py:95
  299.2 1.3 fusion.2
  300.5 2.3 shard_map.249
  303.3 1.3 collective-permute-start.43
  304.6 1.8 collective-permute-start.44
  307.4 4.2 %collective-permute-done.42.one = bf16[64,1792]{1,0:T(8,128)(2,1)S(1)} collective-permute-done((bf16[64,1792]{1,0:T(8,128)(2,1)}, bf16[64,1792]{1,0:T(8,128)(2,1)S(1)}, u32[]{:S(2)}, u32[]{:S(2)}) %collective-permute-start.42) | collective-permute-done | bytes 229408 | tf_op jit(solution)/shard_map/ppermute | solution.py:95
  311.6 3.4 %collective-permute-done.43.two = bf16[64,1792]{1,0:T(8,128)(2,1)S(1)} collective-permute-done((bf16[64,1792]{1,0:T(8,128)(2,1)}, bf16[64,1792]{1,0:T(8,128)(2,1)S(1)}, u32[]{:S(2)}, u32[]{:S(2)}) %collective-permute-start.43) | collective-permute-done | bytes 229408 | tf_op jit(solution)/shard_map/ppermute | solution.py:95
  315.8 2.6 shard_map.250
  (155 shorter events, 35.2 us)
Async XLA Ops:
  7.2 26.0 %copy-start.3 = (bf16[128,1024]{1,0:T(8,128)(2,1)S(1)}, bf16[128,1024]{1,0:T(8,128)(2,1)}, u32[]{:S(2)}) copy-start(bf16[128,1024]{1,0:T(8,128)(2,1)} %param.14) | copy-start | bytes 786436
  7.2 26.0 %copy-start.6 = (bf16[128,1024]{1,0:T(8,128)(2,1)S(1)}, bf16[128,1024]{1,0:T(8,128)(2,1)}, u32[]{:S(2)}) copy-start(bf16[128,1024]{1,0:T(8,128)(2,1)} %param.27) | copy-start | bytes 786436
  7.2 150.9 %all-gather.2.cloned.1.call-start = ((), (), s32[]{:S(2)}) async-start(), calls=%async_computation.1 | async-start | bytes 4587520 | tf_op jit(solution)/shard_map/all_gather | solution.py:766
  10.4 11.7 %collective-permute-start = (bf16[160,1024]{1,0:T(8,128)(2,1)}, bf16[160,1024]{1,0:T(8,128)(2,1)S(1)}, u32[]{:S(2)}, u32[]{:S(2)}) collective-permute-start(bf16[160,1024]{1,0:T(8,128)(2,1)} %get-tuple-element.73), channel_id=1, source_target_pairs={{0,2},{2,0},{4,6},{6,4},{8,10},{10,8},{12,14},{14,12},{16,18},{18,... | collective-permute-start | bytes 983048 | tf_op jit(solution)/shard_map/ppermute | solution.py:95
  13.3 16.4 %collective-permute-start.1 = (bf16[160,1024]{1,0:T(8,128)(2,1)}, bf16[160,1024]{1,0:T(8,128)(2,1)S(1)}, u32[]{:S(2)}, u32[]{:S(2)}) collective-permute-start(bf16[160,1024]{1,0:T(8,128)(2,1)} %get-tuple-element.74), channel_id=1, source_target_pairs={{0,4},{2,6},{4,0},{6,2},{8,12},{10,14},{12,8},{14,10},{16,20},{18,... | collective-permute-start | bytes 983048 | tf_op jit(solution)/shard_map/ppermute | solution.py:95
  14.8 14.9 %collective-permute-start.2 = (bf16[160,1024]{1,0:T(8,128)(2,1)}, bf16[160,1024]{1,0:T(8,128)(2,1)S(1)}, u32[]{:S(2)}, u32[]{:S(2)}) collective-permute-start(bf16[160,1024]{1,0:T(8,128)(2,1)} %get-tuple-element.75), channel_id=1, source_target_pairs={{0,6},{2,4},{4,2},{6,0},{8,14},{10,12},{12,10},{14,8},{16,22},{18,... | collective-permute-start | bytes 983048 | tf_op jit(solution)/shard_map/ppermute | solution.py:95
  22.1 7.7 %copy-start.19 = (bf16[160,1024]{1,0:T(8,128)(2,1)}, bf16[160,1024]{1,0:T(8,128)(2,1)S(1)}, u32[]{:S(2)}) copy-start(bf16[160,1024]{1,0:T(8,128)(2,1)S(1)} %collective-permute-done.one) | copy-start | bytes 983044
  33.0 29.5 %copy-start.38 = (f32[64]{0:T(128)S(1)}, f32[64]{0:T(128)}, u32[]{:S(2)}) copy-start(f32[64]{0:T(128)} %param.17) | copy-start | bytes 772
  33.0 29.5 %copy-start.39 = (f32[64]{0:T(128)S(1)}, f32[64]{0:T(128)}, u32[]{:S(2)}) copy-start(f32[64]{0:T(128)} %param.18) | copy-start | bytes 772
  33.0 30.1 %copy-start.28 = (bf16[256,384]{1,0:T(8,128)(2,1)S(1)}, bf16[256,384]{1,0:T(8,128)(2,1)}, u32[]{:S(2)}) copy-start(bf16[256,384]{1,0:T(8,128)(2,1)} %get-tuple-element.78.refs_9_) | copy-start | bytes 589828
  33.1 267.4 %reduce-scatter.2.cloned.1.call-start = ((), (), s32[]{:S(2)}) async-start(), calls=%async_computation.2 | async-start | bytes 4587520 | tf_op jit(solution)/shard_map/reduce_scatter | solution.py:821
  33.2 24.7 %copy-start.5 = (bf16[256,1024]{1,0:T(8,128)(2,1)}, bf16[256,1024]{1,0:T(8,128)(2,1)S(1)}, u32[]{:S(2)}) copy-start(bf16[256,1024]{1,0:T(8,128)(2,1)S(1)} %constant_dynamic-update-slice_fusion.own) | copy-start | bytes 1572868
  33.2 15.8 %collective-permute-start.5 = (bf16[256,1024]{1,0:T(8,128)(2,1)S(1)}, bf16[256,1024]{1,0:T(8,128)(2,1)S(1)}, u32[]{:S(2)}, u32[]{:S(2)}) collective-permute-start(bf16[256,1024]{1,0:T(8,128)(2,1)S(1)} %constant_dynamic-update-slice_fusion.own), channel_id=1, source_target_pairs={{0,6},{2,4},{4,2},{6,0},{8,14},{10,12},{12,10},{14,8},{16,22},{18,... | collective-permute-start | bytes 1572872 | tf_op jit(solution)/shard_map/ppermute | solution.py:95
  34.8 23.1 %collective-permute-start.4 = (bf16[256,1024]{1,0:T(8,128)(2,1)S(1)}, bf16[256,1024]{1,0:T(8,128)(2,1)S(1)}, u32[]{:S(2)}, u32[]{:S(2)}) collective-permute-start(bf16[256,1024]{1,0:T(8,128)(2,1)S(1)} %constant_dynamic-update-slice_fusion.own), channel_id=1, source_target_pairs={{0,4},{2,6},{4,0},{6,2},{8,12},{10,14},{12,8},{14,10},{16,20},{18,... | collective-permute-start | bytes 1572872 | tf_op jit(solution)/shard_map/ppermute | solution.py:95
  35.9 22.0 %collective-permute-start.3 = (bf16[256,1024]{1,0:T(8,128)(2,1)S(1)}, bf16[256,1024]{1,0:T(8,128)(2,1)S(1)}, u32[]{:S(2)}, u32[]{:S(2)}) collective-permute-start(bf16[256,1024]{1,0:T(8,128)(2,1)S(1)} %constant_dynamic-update-slice_fusion.own), channel_id=1, source_target_pairs={{0,2},{2,0},{4,6},{6,4},{8,10},{10,8},{12,14},{14,12},{16,18},{18,... | collective-permute-start | bytes 1572872 | tf_op jit(solution)/shard_map/ppermute | solution.py:95
  49.0 8.9 %copy-start.16 = (bf16[256,1024]{1,0:T(8,128)(2,1)}, bf16[256,1024]{1,0:T(8,128)(2,1)S(1)}, u32[]{:S(2)}) copy-start(bf16[256,1024]{1,0:T(8,128)(2,1)S(1)} %collective-permute-done.5.three) | copy-start | bytes 1572868
  62.4 43.8 %collective-permute-start.6 = (bf16[512,1024]{1,0:T(8,128)(2,1)}, bf16[512,1024]{1,0:T(8,128)(2,1)S(1)}, u32[]{:S(2)}, u32[]{:S(2)}) collective-permute-start(bf16[512,1024]{1,0:T(8,128)(2,1)} %get-tuple-element.77.refs_2_), channel_id=1, source_target_pairs={{0,1},{1,0},{2,3},{3,2},{4,5},{5,4},{6,7},{7,6},{8,9},{9,8},{10,11... | collective-permute-start | bytes 3145736 | tf_op jit(solution)/shard_map/ppermute | solution.py:104
  63.2 15.1 %collective-permute-start.9 = (bf16[256,384]{1,0:T(8,128)(2,1)S(1)}, bf16[256,384]{1,0:T(8,128)(2,1)S(1)}, u32[]{:S(2)}, u32[]{:S(2)}) collective-permute-start(bf16[256,384]{1,0:T(8,128)(2,1)S(1)} %copy-done.28), channel_id=1, source_target_pairs={{0,24},{2,26},{4,28},{6,30},{8,0},{10,2},{12,4},{14,6},{16,8},{18,... | collective-permute-start | bytes 589832 | tf_op jit(solution)/shard_map/ppermute | solution.py:100
  66.8 39.5 %collective-permute-start.8 = (bf16[256,384]{1,0:T(8,128)(2,1)S(1)}, bf16[256,384]{1,0:T(8,128)(2,1)S(1)}, u32[]{:S(2)}, u32[]{:S(2)}) collective-permute-start(bf16[256,384]{1,0:T(8,128)(2,1)S(1)} %copy-done.28), channel_id=1, source_target_pairs={{0,16},{2,18},{4,20},{6,22},{8,24},{10,26},{12,28},{14,30},{16,0},... | collective-permute-start | bytes 589832 | tf_op jit(solution)/shard_map/ppermute | solution.py:100
  66.8 39.5 %collective-permute-start.7 = (bf16[256,384]{1,0:T(8,128)(2,1)S(1)}, bf16[256,384]{1,0:T(8,128)(2,1)S(1)}, u32[]{:S(2)}, u32[]{:S(2)}) collective-permute-start(bf16[256,384]{1,0:T(8,128)(2,1)S(1)} %copy-done.28), channel_id=1, source_target_pairs={{0,8},{2,10},{4,12},{6,14},{8,16},{10,18},{12,20},{14,22},{16,24},... | collective-permute-start | bytes 589832 | tf_op jit(solution)/shard_map/ppermute | solution.py:100
  68.7 37.6 %copy-start.36 = (s32[4,4]{1,0:T(4,128)}, s32[4,4]{1,0:T(4,128)S(1)}, u32[]{:S(2)}) copy-start(s32[4,4]{1,0:T(4,128)S(1)} %reduce_window_sum.11.refs_1_.ends_ref) | copy-start | bytes 196
  78.3 28.0 %copy-start.29 = (bf16[256,384]{1,0:T(8,128)(2,1)}, bf16[256,384]{1,0:T(8,128)(2,1)S(1)}, u32[]{:S(2)}) copy-start(bf16[256,384]{1,0:T(8,128)(2,1)S(1)} %collective-permute-done.9.refs_12_) | copy-start | bytes 589828
  117.6 2.9 collective-permute-start.10
  121.5 19.8 %copy-start.37 = (f32[1024]{0:T(1024)S(1)}, f32[1024]{0:T(1024)}, u32[]{:S(2)}) copy-start(f32[1024]{0:T(1024)} %param.19) | copy-start | bytes 12292
  124.5 20.5 %copy-start.7 = (bf16[512,1024]{1,0:T(8,128)(2,1)S(1)}, bf16[512,1024]{1,0:T(8,128)(2,1)}, u32[]{:S(2)}) copy-start(bf16[512,1024]{1,0:T(8,128)(2,1)} %get-tuple-element.85.g_m) | copy-start | bytes 3145732
  124.5 9.4 %collective-permute-start.11 = (bf16[128,1024]{1,0:T(8,128)(2,1)}, bf16[128,1024]{1,0:T(8,128)(2,1)S(1)}, u32[]{:S(2)}, u32[]{:S(2)}) collective-permute-start(bf16[128,1024]{1,0:T(8,128)(2,1)} %get-tuple-element.82), channel_id=1, source_target_pairs={{0,2},{2,0},{4,6},{6,4},{8,10},{10,8},{12,14},{14,12},{16,18},{18,... | collective-permute-start | bytes 786440 | tf_op jit(solution)/shard_map/ppermute | solution.py:95
  125.9 14.0 %collective-permute-start.12 = (bf16[128,1024]{1,0:T(8,128)(2,1)}, bf16[128,1024]{1,0:T(8,128)(2,1)S(1)}, u32[]{:S(2)}, u32[]{:S(2)}) collective-permute-start(bf16[128,1024]{1,0:T(8,128)(2,1)} %get-tuple-element.83), channel_id=1, source_target_pairs={{0,4},{2,6},{4,0},{6,2},{8,12},{10,14},{12,8},{14,10},{16,20},{18,... | collective-permute-start | bytes 786440 | tf_op jit(solution)/shard_map/ppermute | solution.py:95
  127.4 12.6 %collective-permute-start.13 = (bf16[128,1024]{1,0:T(8,128)(2,1)}, bf16[128,1024]{1,0:T(8,128)(2,1)S(1)}, u32[]{:S(2)}, u32[]{:S(2)}) collective-permute-start(bf16[128,1024]{1,0:T(8,128)(2,1)} %get-tuple-element.84), channel_id=1, source_target_pairs={{0,6},{2,4},{4,2},{6,0},{8,14},{10,12},{12,10},{14,8},{16,22},{18,... | collective-permute-start | bytes 786440 | tf_op jit(solution)/shard_map/ppermute | solution.py:95
  141.4 10.3 %collective-permute-start.16 = (bf16[128,1024]{1,0:T(8,128)(2,1)S(1)}, bf16[128,1024]{1,0:T(8,128)(2,1)S(1)}, u32[]{:S(2)}, u32[]{:S(2)}) collective-permute-start(bf16[128,1024]{1,0:T(8,128)(2,1)S(1)} %multiply_convert_fusion), channel_id=1, source_target_pairs={{0,6},{2,4},{4,2},{6,0},{8,14},{10,12},{12,10},{14,8},{16,22},{18,... | collective-permute-start | bytes 786440 | tf_op jit(solution)/shard_map/ppermute | solution.py:95
  142.8 12.3 %collective-permute-start.15 = (bf16[128,1024]{1,0:T(8,128)(2,1)S(1)}, bf16[128,1024]{1,0:T(8,128)(2,1)S(1)}, u32[]{:S(2)}, u32[]{:S(2)}) collective-permute-start(bf16[128,1024]{1,0:T(8,128)(2,1)S(1)} %multiply_convert_fusion), channel_id=1, source_target_pairs={{0,4},{2,6},{4,0},{6,2},{8,12},{10,14},{12,8},{14,10},{16,20},{18,... | collective-permute-start | bytes 786440 | tf_op jit(solution)/shard_map/ppermute | solution.py:95
  144.0 11.2 %collective-permute-start.14 = (bf16[128,1024]{1,0:T(8,128)(2,1)S(1)}, bf16[128,1024]{1,0:T(8,128)(2,1)S(1)}, u32[]{:S(2)}, u32[]{:S(2)}) collective-permute-start(bf16[128,1024]{1,0:T(8,128)(2,1)S(1)} %multiply_convert_fusion), channel_id=1, source_target_pairs={{0,2},{2,0},{4,6},{6,4},{8,10},{10,8},{12,14},{14,12},{16,18},{18,... | collective-permute-start | bytes 786440 | tf_op jit(solution)/shard_map/ppermute | solution.py:95
  145.0 10.3 %collective-permute-start.18 = (bf16[512,1024]{1,0:T(8,128)(2,1)S(1)}, bf16[512,1024]{1,0:T(8,128)(2,1)S(1)}, u32[]{:S(2)}, u32[]{:S(2)}) collective-permute-start(bf16[512,1024]{1,0:T(8,128)(2,1)S(1)} %copy-done.7), channel_id=1, source_target_pairs={{0,1},{1,0},{2,3},{3,2},{4,5},{5,4},{6,7},{7,6},{8,9},{9,8},{10,11... | collective-permute-start | bytes 3145736 | tf_op jit(solution)/shard_map/ppermute | solution.py:104
  155.2 2.9 collective-permute-start.17
  178.5 2.9 collective-permute-start.23
  178.7 12.2 %collective-permute-start.19 = (bf16[512,1024]{1,0:T(8,128)(2,1)}, bf16[512,1024]{1,0:T(8,128)(2,1)S(1)}, u32[]{:S(2)}, u32[]{:S(2)}) collective-permute-start(bf16[512,1024]{1,0:T(8,128)(2,1)} %get-tuple-element.88), channel_id=1, source_target_pairs={{0,1},{1,0},{2,3},{3,2},{4,5},{5,4},{6,7},{7,6},{8,9},{9,8},{10,11... | collective-permute-start | bytes 3145736 | tf_op jit(solution)/shard_map/ppermute | solution.py:104
  185.5 15.8 %copy-start.15 = (f32[128,1024]{1,0:T(8,128)S(1)}, f32[128,1024]{1,0:T(8,128)}, u32[]{:S(2)}) copy-start(f32[128,1024]{1,0:T(8,128)} %get-tuple-element.95) | copy-start | bytes 1572868
  185.5 12.1 %collective-permute-start.24 = (bf16[128,1024]{1,0:T(8,128)(2,1)}, bf16[128,1024]{1,0:T(8,128)(2,1)S(1)}, u32[]{:S(2)}, u32[]{:S(2)}) collective-permute-start(bf16[128,1024]{1,0:T(8,128)(2,1)} %get-tuple-element.96), channel_id=1, source_target_pairs={{0,2},{2,0},{4,6},{6,4},{8,10},{10,8},{12,14},{14,12},{16,18},{18,... | collective-permute-start | bytes 786440 | tf_op jit(solution)/shard_map/ppermute | solution.py:95
  187.0 14.1 %collective-permute-start.25 = (bf16[128,1024]{1,0:T(8,128)(2,1)}, bf16[128,1024]{1,0:T(8,128)(2,1)S(1)}, u32[]{:S(2)}, u32[]{:S(2)}) collective-permute-start(bf16[128,1024]{1,0:T(8,128)(2,1)} %get-tuple-element.97), channel_id=1, source_target_pairs={{0,4},{2,6},{4,0},{6,2},{8,12},{10,14},{12,8},{14,10},{16,20},{18,... | collective-permute-start | bytes 786440 | tf_op jit(solution)/shard_map/ppermute | solution.py:95
  188.3 13.0 %collective-permute-start.26 = (bf16[128,1024]{1,0:T(8,128)(2,1)}, bf16[128,1024]{1,0:T(8,128)(2,1)S(1)}, u32[]{:S(2)}, u32[]{:S(2)}) collective-permute-start(bf16[128,1024]{1,0:T(8,128)(2,1)} %get-tuple-element.98), channel_id=1, source_target_pairs={{0,6},{2,4},{4,2},{6,0},{8,14},{10,12},{12,10},{14,8},{16,22},{18,... | collective-permute-start | bytes 786440 | tf_op jit(solution)/shard_map/ppermute | solution.py:95
  194.9 17.3 %copy-start.14 = (f32[128,1024]{1,0:T(8,128)S(1)}, f32[128,1024]{1,0:T(8,128)}, u32[]{:S(2)}) copy-start(f32[128,1024]{1,0:T(8,128)} %get-tuple-element.89) | copy-start | bytes 1572868
  194.9 11.3 %collective-permute-start.20 = (bf16[128,1024]{1,0:T(8,128)(2,1)}, bf16[128,1024]{1,0:T(8,128)(2,1)S(1)}, u32[]{:S(2)}, u32[]{:S(2)}) collective-permute-start(bf16[128,1024]{1,0:T(8,128)(2,1)} %get-tuple-element.90), channel_id=1, source_target_pairs={{0,2},{2,0},{4,6},{6,4},{8,10},{10,8},{12,14},{14,12},{16,18},{18,... | collective-permute-start | bytes 786440 | tf_op jit(solution)/shard_map/ppermute | solution.py:95
  196.4 15.8 %collective-permute-start.21 = (bf16[128,1024]{1,0:T(8,128)(2,1)}, bf16[128,1024]{1,0:T(8,128)(2,1)S(1)}, u32[]{:S(2)}, u32[]{:S(2)}) collective-permute-start(bf16[128,1024]{1,0:T(8,128)(2,1)} %get-tuple-element.91), channel_id=1, source_target_pairs={{0,4},{2,6},{4,0},{6,2},{8,12},{10,14},{12,8},{14,10},{16,20},{18,... | collective-permute-start | bytes 786440 | tf_op jit(solution)/shard_map/ppermute | solution.py:95
  197.7 14.5 %collective-permute-start.22 = (bf16[128,1024]{1,0:T(8,128)(2,1)}, bf16[128,1024]{1,0:T(8,128)(2,1)S(1)}, u32[]{:S(2)}, u32[]{:S(2)}) collective-permute-start(bf16[128,1024]{1,0:T(8,128)(2,1)} %get-tuple-element.92), channel_id=1, source_target_pairs={{0,6},{2,4},{4,2},{6,0},{8,14},{10,12},{12,10},{14,8},{16,22},{18,... | collective-permute-start | bytes 786440 | tf_op jit(solution)/shard_map/ppermute | solution.py:95
  213.1 10.1 %collective-permute-start.29 = (bf16[128,1024]{1,0:T(8,128)(2,1)S(1)}, bf16[128,1024]{1,0:T(8,128)(2,1)S(1)}, u32[]{:S(2)}, u32[]{:S(2)}) collective-permute-start(bf16[128,1024]{1,0:T(8,128)(2,1)S(1)} %get-tuple-element.133), channel_id=1, source_target_pairs={{0,6},{2,4},{4,2},{6,0},{8,14},{10,12},{12,10},{14,8},{16,22},{18,... | collective-permute-start | bytes 786440 | tf_op jit(solution)/shard_map/ppermute | solution.py:95
  214.4 12.8 %collective-permute-start.28 = (bf16[128,1024]{1,0:T(8,128)(2,1)S(1)}, bf16[128,1024]{1,0:T(8,128)(2,1)S(1)}, u32[]{:S(2)}, u32[]{:S(2)}) collective-permute-start(bf16[128,1024]{1,0:T(8,128)(2,1)S(1)} %get-tuple-element.133), channel_id=1, source_target_pairs={{0,4},{2,6},{4,0},{6,2},{8,12},{10,14},{12,8},{14,10},{16,20},{18,... | collective-permute-start | bytes 786440 | tf_op jit(solution)/shard_map/ppermute | solution.py:95
  215.6 11.6 %collective-permute-start.27 = (bf16[128,1024]{1,0:T(8,128)(2,1)S(1)}, bf16[128,1024]{1,0:T(8,128)(2,1)S(1)}, u32[]{:S(2)}, u32[]{:S(2)}) collective-permute-start(bf16[128,1024]{1,0:T(8,128)(2,1)S(1)} %get-tuple-element.133), channel_id=1, source_target_pairs={{0,2},{2,0},{4,6},{6,4},{8,10},{10,8},{12,14},{14,12},{16,18},{18,... | collective-permute-start | bytes 786440 | tf_op jit(solution)/shard_map/ppermute | solution.py:95
  227.3 2.7 collective-permute-start.30
  247.0 32.7 %collective-permute-start.31 = (bf16[512,1024]{1,0:T(8,128)(2,1)}, bf16[512,1024]{1,0:T(8,128)(2,1)S(1)}, u32[]{:S(2)}, u32[]{:S(2)}) collective-permute-start(bf16[512,1024]{1,0:T(8,128)(2,1)} %get-tuple-element.104), channel_id=1, source_target_pairs={{0,1},{1,0},{2,3},{3,2},{4,5},{5,4},{6,7},{7,6},{8,9},{9,8},{10,11... | collective-permute-start | bytes 3145736 | tf_op jit(solution)/shard_map/ppermute | solution.py:104
  247.3 10.2 %collective-permute-start.35 = (bf16[272,384]{1,0:T(8,128)(2,1)}, bf16[272,384]{1,0:T(8,128)(2,1)S(1)}, u32[]{:S(2)}, u32[]{:S(2)}) collective-permute-start(bf16[272,384]{1,0:T(8,128)(2,1)} %get-tuple-element.111), channel_id=1, source_target_pairs={{0,8},{2,10},{4,12},{6,14},{8,16},{10,18},{12,20},{14,22},{16,24},... | collective-permute-start | bytes 626696 | tf_op jit(solution)/shard_map/ppermute | solution.py:100
  247.3 18.1 %collective-permute-start.36 = (bf16[272,384]{1,0:T(8,128)(2,1)}, bf16[272,384]{1,0:T(8,128)(2,1)S(1)}, u32[]{:S(2)}, u32[]{:S(2)}) collective-permute-start(bf16[272,384]{1,0:T(8,128)(2,1)} %get-tuple-element.112), channel_id=1, source_target_pairs={{0,16},{2,18},{4,20},{6,22},{8,24},{10,26},{12,28},{14,30},{16,0},... | collective-permute-start | bytes 626696 | tf_op jit(solution)/shard_map/ppermute | solution.py:100
  248.6 16.8 %collective-permute-start.37 = (bf16[272,384]{1,0:T(8,128)(2,1)}, bf16[272,384]{1,0:T(8,128)(2,1)S(1)}, u32[]{:S(2)}, u32[]{:S(2)}) collective-permute-start(bf16[272,384]{1,0:T(8,128)(2,1)} %get-tuple-element.113), channel_id=1, source_target_pairs={{0,24},{2,26},{4,28},{6,30},{8,0},{10,2},{12,4},{14,6},{16,8},{18,... | collective-permute-start | bytes 626696 | tf_op jit(solution)/shard_map/ppermute | solution.py:100
  257.4 8.0 %copy-start.25 = (bf16[272,384]{1,0:T(8,128)(2,1)}, bf16[272,384]{1,0:T(8,128)(2,1)S(1)}, u32[]{:S(2)}) copy-start(bf16[272,384]{1,0:T(8,128)(2,1)S(1)} %collective-permute-done.35.refs_0_) | copy-start | bytes 626692
  266.1 33.1 %copy-start.32 = (f32[1024]{0:T(1024)S(1)}, f32[1024]{0:T(1024)}, u32[]{:S(2)}) copy-start(f32[1024]{0:T(1024)} %param.16) | copy-start | bytes 12292
  268.2 5.0 %collective-permute-start.38 = (bf16[80,384]{1,0:T(8,128)(2,1)}, bf16[80,384]{1,0:T(8,128)(2,1)S(1)}, u32[]{:S(2)}, u32[]{:S(2)}) collective-permute-start(bf16[80,384]{1,0:T(8,128)(2,1)} %get-tuple-element.115), channel_id=1, source_target_pairs={{0,2},{2,0},{4,6},{6,4},{8,10},{10,8},{12,14},{14,12},{16,18},{18,... | collective-permute-start | bytes 184328 | tf_op jit(solution)/shard_map/ppermute | solution.py:95
  269.2 4.4 %collective-permute-start.39 = (bf16[80,384]{1,0:T(8,128)(2,1)}, bf16[80,384]{1,0:T(8,128)(2,1)S(1)}, u32[]{:S(2)}, u32[]{:S(2)}) collective-permute-start(bf16[80,384]{1,0:T(8,128)(2,1)} %get-tuple-element.116), channel_id=1, source_target_pairs={{0,4},{2,6},{4,0},{6,2},{8,12},{10,14},{12,8},{14,10},{16,20},{18,... | collective-permute-start | bytes 184328 | tf_op jit(solution)/shard_map/ppermute | solution.py:95
  270.0 5.3 %collective-permute-start.40 = (bf16[80,384]{1,0:T(8,128)(2,1)}, bf16[80,384]{1,0:T(8,128)(2,1)S(1)}, u32[]{:S(2)}, u32[]{:S(2)}) collective-permute-start(bf16[80,384]{1,0:T(8,128)(2,1)} %get-tuple-element.117), channel_id=1, source_target_pairs={{0,6},{2,4},{4,2},{6,0},{8,14},{10,12},{12,10},{14,8},{16,22},{18,... | collective-permute-start | bytes 184328 | tf_op jit(solution)/shard_map/ppermute | solution.py:95
  277.6 1.4 collective-permute-start.41
  283.7 22.7 %copy-start.4 = (f32[128,1024]{1,0:T(8,128)S(1)}, f32[128,1024]{1,0:T(8,128)}, u32[]{:S(2)}) copy-start(f32[128,1024]{1,0:T(8,128)} %get-tuple-element.105) | copy-start | bytes 1572868
  283.7 9.4 %collective-permute-start.32 = (bf16[128,1024]{1,0:T(8,128)(2,1)}, bf16[128,1024]{1,0:T(8,128)(2,1)S(1)}, u32[]{:S(2)}, u32[]{:S(2)}) collective-permute-start(bf16[128,1024]{1,0:T(8,128)(2,1)} %get-tuple-element.106), channel_id=1, source_target_pairs={{0,2},{2,0},{4,6},{6,4},{8,10},{10,8},{12,14},{14,12},{16,18},{18,... | collective-permute-start | bytes 786440 | tf_op jit(solution)/shard_map/ppermute | solution.py:95
  285.2 13.9 %collective-permute-start.33 = (bf16[128,1024]{1,0:T(8,128)(2,1)}, bf16[128,1024]{1,0:T(8,128)(2,1)S(1)}, u32[]{:S(2)}, u32[]{:S(2)}) collective-permute-start(bf16[128,1024]{1,0:T(8,128)(2,1)} %get-tuple-element.107), channel_id=1, source_target_pairs={{0,4},{2,6},{4,0},{6,2},{8,12},{10,14},{12,8},{14,10},{16,20},{18,... | collective-permute-start | bytes 786440 | tf_op jit(solution)/shard_map/ppermute | solution.py:95
  286.0 13.2 %collective-permute-start.34 = (bf16[128,1024]{1,0:T(8,128)(2,1)}, bf16[128,1024]{1,0:T(8,128)(2,1)S(1)}, u32[]{:S(2)}, u32[]{:S(2)}) collective-permute-start(bf16[128,1024]{1,0:T(8,128)(2,1)} %get-tuple-element.108), channel_id=1, source_target_pairs={{0,6},{2,4},{4,2},{6,0},{8,14},{10,12},{12,10},{14,8},{16,22},{18,... | collective-permute-start | bytes 786440 | tf_op jit(solution)/shard_map/ppermute | solution.py:95
  302.8 8.8 %collective-permute-start.42 = (bf16[64,1792]{1,0:T(8,128)(2,1)}, bf16[64,1792]{1,0:T(8,128)(2,1)S(1)}, u32[]{:S(2)}, u32[]{:S(2)}) collective-permute-start(bf16[64,1792]{1,0:T(8,128)(2,1)} %get-tuple-element.125), channel_id=1, source_target_pairs={{0,2},{2,0},{4,6},{6,4},{8,10},{10,8},{12,14},{14,12},{16,18},{18,... | collective-permute-start | bytes 688136 | tf_op jit(solution)/shard_map/ppermute | solution.py:95
  303.3 11.7 %collective-permute-start.43 = (bf16[64,1792]{1,0:T(8,128)(2,1)}, bf16[64,1792]{1,0:T(8,128)(2,1)S(1)}, u32[]{:S(2)}, u32[]{:S(2)}) collective-permute-start(bf16[64,1792]{1,0:T(8,128)(2,1)} %get-tuple-element.126), channel_id=1, source_target_pairs={{0,4},{2,6},{4,0},{6,2},{8,12},{10,14},{12,8},{14,10},{16,20},{18,... | collective-permute-start | bytes 688136 | tf_op jit(solution)/shard_map/ppermute | solution.py:95
  304.6 10.4 %collective-permute-start.44 = (bf16[64,1792]{1,0:T(8,128)(2,1)}, bf16[64,1792]{1,0:T(8,128)(2,1)S(1)}, u32[]{:S(2)}, u32[]{:S(2)}) collective-permute-start(bf16[64,1792]{1,0:T(8,128)(2,1)} %get-tuple-element.127), channel_id=1, source_target_pairs={{0,6},{2,4},{4,2},{6,0},{8,14},{10,12},{12,10},{14,8},{16,22},{18,... | collective-permute-start | bytes 688136 | tf_op jit(solution)/shard_map/ppermute | solution.py:95
  (23 other events, 27.8 us)
Sparse Core Ops, SparseCore 0:
  33.2 89.0 all-gather.1
  178.7 66.0 reduce-scatter.1

commit v5 on v4

--- a/solution.py
+++ b/solution.py
@@ -116,6 +116,10 @@
         compiler_params=pltpu.CompilerParams(vmem_limit_bytes=VMEM_BYTES),
         cost_estimate=COST,
     )(*operands)
+
+
+def ordered(first, second):
+    return lax.optimization_barrier((first, second))
 
 
 def lane_ids(shape):
@@ -563,29 +567,53 @@
 
 
 def chip_sum(keep, received):
-    shape = (keep.shape[0] // PLANE, keep.shape[1])
-    own, *rest = call(
-        chip_sum_kernel, [(shape, float32)] + [(shape, bfloat16)] * (PLANE - 1), keep, received
-    )
-    return [own] + [send_plane(part, mask + 1) for mask, part in enumerate(rest)]
+    rows, width = keep.shape
+    shape = (rows // PLANE, width)
+    block = 2 * LANES
+
+    def columns(height):
+        return pl.BlockSpec((height, block), lambda i: (0, i))
+
+    return pl.pallas_call(
+        chip_sum_kernel,
+        grid=(width // block,),
+        in_specs=[columns(rows)] * 2,
+        out_specs=[columns(shape[0])] * PLANE,
+        out_shape=[jax.ShapeDtypeStruct(shape, float32)]
+        + [jax.ShapeDtypeStruct(shape, bfloat16)] * (PLANE - 1),
+        compiler_params=pltpu.CompilerParams(vmem_limit_bytes=VMEM_BYTES),
+        cost_estimate=COST,
+    )(keep, received)
+
+
+def plane_total(parts):
+    return add_up([parts[0]] + [send_plane(part, mask + 1) for mask, part in enumerate(parts[1:])])
 
 
 def add_up(parts):
     return sum(part.astype(float32) for part in parts)
 
 
-def plane_sum_kernel(where_ref, own, *refs):
-    received, outs, held = refs[: -PLANE - 1], refs[-PLANE - 1 : -1], refs[-1]
-    value = own[...].astype(float32)
-    high = own.shape[0]
-    for part in received:
-        value = value + part[:high, :].astype(float32)
-    held[...] = value
+def plane_split_kernel(where_ref, own, *refs):
+    outs, held = refs[:-1], refs[-1]
+    held[...] = own[...].astype(float32)
     place = where_ref[0]
-    rows = high // PLANE
+    rows = own.shape[0] // PLANE
     for mask, out in enumerate(outs):
         at = pl.multiple_of((place ^ mask) * rows, rows)
         out[...] = held[pl.ds(at, rows), :].astype(out.dtype)
+
+
+def plane_split(where, own):
+    shape = (own.shape[0] // PLANE, own.shape[1])
+    return call(
+        plane_split_kernel,
+        [(shape, bfloat16)] * PLANE,
+        where,
+        own,
+        scalars=1,
+        scratch=[pltpu.VMEM(own.shape, float32)],
+    )
 
 
 def joined_gains(tail):
@@ -630,22 +658,19 @@
             out[rows:, :] = tail
 
 
-def plane_sum(where, own, grad_pieces, gains=None):
+def plane_split_attn(where, own, grad_pieces, gains):
     received = [send_deep(piece, step + 1) for step, piece in enumerate(grad_pieces)]
     rows, columns = own.shape[0] // PLANE, own.shape[1]
-    scratch = [pltpu.VMEM(own.shape, float32)]
-    if gains is None:
-        shapes = [((rows, columns), float32)] + [((rows, columns), bfloat16)] * (PLANE - 1)
-        outs = call(plane_sum_kernel, shapes, where, own, *received, scalars=1, scratch=scratch)
-    else:
-        tail = 2 * GAIN_ROWS
-        shapes = [((rows + tail, columns), float32)]
-        shapes += [((max(rows, 16) + tail, columns), bfloat16)] * (PLANE - 1)
-        scratch.append(pltpu.VMEM(((len(received) + 1) * GAIN_ROWS, columns), float32))
-        outs = call(
-            plane_sum_attn_kernel, shapes, where, own, gains, *received, scalars=1, scratch=scratch
-        )
-    return [outs[0]] + [send_plane(part, mask + 1) for mask, part in enumerate(outs[1:])]
+    tail = 2 * GAIN_ROWS
+    shapes = [((rows + tail, columns), float32)]
+    shapes += [((max(rows, 16) + tail, columns), bfloat16)] * (PLANE - 1)
+    scratch = [
+        pltpu.VMEM(own.shape, float32),
+        pltpu.VMEM(((len(received) + 1) * GAIN_ROWS, columns), float32),
+    ]
+    return call(
+        plane_sum_attn_kernel, shapes, where, own, gains, *received, scalars=1, scratch=scratch
+    )
 
 
 def pick_place(refs, place, target, columns, rows):
@@ -746,6 +771,8 @@
         scalars=2,
     )
     messages = [messages[0]] + [send_plane(messages[m], m) for m in range(1, PLANE)]
+    messages, local = ordered(messages, jnp.concatenate([tokens, cotangent]))
+    rows_messages = [local] + [send_plane(local, m) for m in range(1, PLANE)]
     attn_piece, ff_piece, lens = call(
         unpack_kernel,
         [
@@ -762,16 +789,13 @@
         ],
     )
     attn_pieces = [attn_piece] + [send_deep(attn_piece, step) for step in range(1, layers)]
+    attn_pieces, (ff_piece, rows_messages) = ordered(attn_pieces, (ff_piece, rows_messages))
     columns = [list(range(k, layers * PLANE, PLANE)) for k in range(PLANE)]
     ff_weight = lax.all_gather(
         ff_piece, "dp", axis=0, tiled=True, axis_index_groups=columns
     )
-    local = jnp.concatenate([tokens, cotangent])
     tok_mine, cot_mine = call(
-        split_rows_kernel,
-        [((PLANE * local_rows, model), bfloat16)] * 2,
-        local,
-        *[send_plane(local, m) for m in range(1, PLANE)],
+        split_rows_kernel, [((PLANE * local_rows, model), bfloat16)] * 2, *rows_messages
     )
     tok_other = swap_cores(tok_mine)
     cot_other = swap_cores(cot_mine)
@@ -801,7 +825,7 @@
     send, keep, *saved, attn_weight = attn(
         where, ends, tok_mine, tok_other, gains, tables, attn_pieces
     )
-    hidden = inputs + add_up(chip_sum(keep, swap_cores(send)))
+    hidden = inputs + plane_total(chip_sum(keep, swap_cores(send)))
     factor_b = inverse_rms(hidden)
     unit_b = hidden * factor_b
     x_mine, x_other = gather_rows((unit_b * ffn_gain).astype(jnp.bfloat16))
@@ -809,7 +833,9 @@
     out_send, out_keep, dn_send, dn_keep, ff_grad = ffn(
         where, ends, x_mine, x_other, cot_mine, cot_other, ff_weight
     )
-    d_normed2 = add_up(chip_sum(dn_keep, swap_cores(dn_send)))
+    dn_parts = chip_sum(dn_keep, swap_cores(dn_send))
+    dn_parts, out_keep = ordered(dn_parts, out_keep)
+    d_normed2 = plane_total(dn_parts)
     grad_out = jnp.where(
         (jnp.arange(local_rows) + core * local_rows < ends[0, slots - 1])[:, None],
         cotangent,
@@ -821,16 +847,27 @@
     own_ff = lax.psum_scatter(
         ff_grad, "dp", scatter_dimension=0, tiled=True, axis_index_groups=columns
     )
-    ff_parts = plane_sum(where, own_ff, [])
-    block_out = (hidden + add_up(chip_sum(out_keep, swap_cores(out_send)))).astype(jnp.bfloat16)
+    out_parts = chip_sum(out_keep, swap_cores(out_send))
+    (h_mine, h_other), out_parts = ordered((h_mine, h_other), out_parts)
+    ffn_branch = plane_total(out_parts)
+    block_out = (hidden + ffn_branch).astype(jnp.bfloat16)
 
     send, keep, own_attn, part_gains, *attn_grads = attn_back(
         where, ends, layers, tok_mine, tok_other, gains, tables, (h_mine, h_other), saved,
         attn_weight, gain_ffn[None, :],
     )
-    attn_parts = plane_sum(where, own_attn, attn_grads, part_gains)
-    d_normed = add_up(chip_sum(keep, swap_cores(send)))
+    ff_parts = plane_split(where, own_ff)
+    ff_parts, keep = ordered(ff_parts, keep)
+    dn_parts = chip_sum(keep, swap_cores(send))
+    (dn_parts, block_out), own_attn = ordered((dn_parts, block_out), own_attn)
+    attn_parts = plane_split_attn(where, own_attn, attn_grads, part_gains)
+    d_normed = plane_total(dn_parts)
+    ff_parts = [ff_parts[0]] + [send_plane(part, mask + 1) for mask, part in enumerate(ff_parts[1:])]
+    attn_parts = [attn_parts[0]] + [
+        send_plane(part, mask + 1) for mask, part in enumerate(attn_parts[1:])
+    ]
     grad_tokens = d_hidden + norm_back(d_normed * attn_gain, unit_a, factor_a)
+    (ff_parts, d_normed), attn_parts = ordered((ff_parts, d_normed), attn_parts)
     grad_gate, grad_up, grad_down = call(
         place_ffn_kernel, [(w_gate.shape, float32)] * 3, where, *ff_parts, scalars=1
     )

time: 327 us -> 281 us (0.86)
  waiting for transfers between devices: 163 us -> 110 us
  Pallas kernels: 75.4 us -> 79.4 us
  local copies, waits for them, and re-layouts: 14.8 us -> 10.9 us
  starting transfers between devices: 46.3 us -> 49.6 us
    ppermute x6, waiting for transfers between devices: 48.2 us -> 18.1 us  [send_deep(): lax.ppermute(values, 'dp', [(i, (i + PLANE * step) % count) for i in rang...]
    ppermute x30, waiting for transfers between devices: 104 us -> 74.3 us  [send_plane(): return lax.ppermute(values, 'dp', [(i, i ^ mask) for i in range(count)])]
    pallas_call x0 -> x4, Pallas kernels: none -> 15.8 us  [chip_sum(): pl.pallas_call(chip_sum_kernel, grid=(width // block,), in_specs=[columns...]
    pallas_call x11 -> x7, Pallas kernels: 28.6 us -> 16.7 us  [call(): pl.pallas_call(kernel, out_shape=[jax.ShapeDtypeStruct(shape, kind) for s...]
    all_gather x1, waiting for transfers between devices: 0.01 us -> 10.3 us  [body(): lax.all_gather(ff_piece, 'dp', axis=0, tiled=True, axis_index_groups=colu...]
    unnamed x82 -> x89, local copies, waits for them, and re-layouts: 11.6 us -> 7.74 us
    ppermute x9, waiting for transfers between devices: 10.7 us -> 6.94 us  [swap_cores(): return lax.ppermute(values, 'tensor', [(0, 1), (1, 0)])]
  transfers between devices with their start and end apart: 47 -> 47, of which waited for: 30 -> 21; matrix products, arithmetic and copies ran while one was open for 4% -> 5% of each run, Pallas kernels for 14% -> 20%
where the time goes in v5:
time: 281 us; the launch traced here: 278 us
  waiting for transfers between devices  110 us (39%)
  Pallas kernels  79.4 us (28%)
  starting transfers between devices  49.6 us (18%)
  between operations  14.5 us (5%)
  other arithmetic  13.4 us (5%)
  local copies, waits for them, and re-layouts  10.9 us (4%)
    ppermute x30, waiting for transfers between devices, send_plane(): return lax.ppermute(values, 'dp', [(i, i ^ mask) for i in range(count)])  74.3 us
    ppermute x30, starting transfers between devices, send_plane(): return lax.ppermute(values, 'dp', [(i, i ^ mask) for i in range(count)])  36.1 us
    pallas_call x1, Pallas kernels, ffn(): pl.pallas_call(ffn_kernel, grid=(2,), in_specs=[scalar, scalar] + [row_sp...  20.5 us
    ppermute x6, waiting for transfers between devices, send_deep(): lax.ppermute(values, 'dp', [(i, (i + PLANE * step) % count) for i in rang...  18.1 us
    pallas_call x7, Pallas kernels, call(): pl.pallas_call(kernel, out_shape=[jax.ShapeDtypeStruct(shape, kind) for s...  16.7 us
    pallas_call x1, Pallas kernels, attn_back(): pl.pallas_call(lambda *refs: attn_back_kernel(layers, *refs), grid=(PLANE...  16.2 us
    pallas_call x4, Pallas kernels, chip_sum(): pl.pallas_call(chip_sum_kernel, grid=(width // block,), in_specs=[columns...  15.8 us
    ppermute x6, starting transfers between devices, send_deep(): lax.ppermute(values, 'dp', [(i, (i + PLANE * step) % count) for i in rang...  12.1 us
  transfers between devices with their start and end apart: 47, of which 21 were waited for; matrix products, arithmetic and copies ran while one was open for 5% of the time, Pallas kernels for 20%

profile of v5, /device:TPU:0, one launch (start us, length us, event | category | flops | bytes accessed | tf_op | source)
XLA Modules:
  0.0 277.5 jit_solution(6743227849676000607)
XLA Ops:
  7.9 2.4 shard_map.237
  10.4 2.9 %collective-permute-start = (bf16[160,1024]{1,0:T(8,128)(2,1)}, bf16[160,1024]{1,0:T(8,128)(2,1)S(1)}, u32[]{:S(2)}, u32[]{:S(2)}) collective-permute-start(bf16[160,1024]{1,0:T(8,128)(2,1)} %get-tuple-element.117), channel_id=1, source_target_pairs={{0,2},{2,0},{4,6},{6,4},{8,10},{10,8},{12,14},{14,12},{16,18},{18,... | collective-permute-start | bytes 983048 | tf_op jit(solution)/shard_map/ppermute | solution.py:95
  13.3 1.5 collective-permute-start.1
  15.9 6.1 %collective-permute-done.one = bf16[160,1024]{1,0:T(8,128)(2,1)S(1)} collective-permute-done((bf16[160,1024]{1,0:T(8,128)(2,1)}, bf16[160,1024]{1,0:T(8,128)(2,1)S(1)}, u32[]{:S(2)}, u32[]{:S(2)}) %collective-permute-start) | collective-permute-done | bytes 327712 | tf_op jit(solution)/shard_map/ppermute | solution.py:95
  22.0 7.7 %collective-permute-done.1.two = bf16[160,1024]{1,0:T(8,128)(2,1)S(1)} collective-permute-done((bf16[160,1024]{1,0:T(8,128)(2,1)}, bf16[160,1024]{1,0:T(8,128)(2,1)S(1)}, u32[]{:S(2)}, u32[]{:S(2)}) %collective-permute-start.1) | collective-permute-done | bytes 327712 | tf_op jit(solution)/shard_map/ppermute | solution.py:95
  29.7 1.6 collective-permute-start.8
  31.3 1.1 collective-permute-start.7
  33.3 2.5 shard_map.238
  35.8 3.6 %collective-permute-start.5 = (bf16[256,384]{1,0:T(8,128)(2,1)}, bf16[256,384]{1,0:T(8,128)(2,1)S(1)}, u32[]{:S(2)}, u32[]{:S(2)}) collective-permute-start(bf16[256,384]{1,0:T(8,128)(2,1)} %get-tuple-element.133.refs_9_), channel_id=1, source_target_pairs={{0,24},{2,26},{4,28},{6,30},{8,0},{10,2},{12,4},{14,6},{16,8},{18,... | collective-permute-start | bytes 589832 | tf_op jit(solution)/shard_map/ppermute | solution.py:100
  39.4 5.7 %collective-permute-done.5.refs_12_ = bf16[256,384]{1,0:T(8,128)(2,1)S(1)} collective-permute-done((bf16[256,384]{1,0:T(8,128)(2,1)}, bf16[256,384]{1,0:T(8,128)(2,1)S(1)}, u32[]{:S(2)}, u32[]{:S(2)}) %collective-permute-start.5) | collective-permute-done | bytes 196640 | tf_op jit(solution)/shard_map/ppermute | solution.py:100
  45.0 6.6 %collective-permute-start.3 = (bf16[256,384]{1,0:T(8,128)(2,1)}, bf16[256,384]{1,0:T(8,128)(2,1)S(1)}, u32[]{:S(2)}, u32[]{:S(2)}) collective-permute-start(bf16[256,384]{1,0:T(8,128)(2,1)} %get-tuple-element.133.refs_9_), channel_id=1, source_target_pairs={{0,8},{2,10},{4,12},{6,14},{8,16},{10,18},{12,20},{14,22},{16,24},... | collective-permute-start | bytes 589832 | tf_op jit(solution)/shard_map/ppermute | solution.py:100
  51.6 3.6 %collective-permute-done.4.refs_11_ = bf16[256,384]{1,0:T(8,128)(2,1)S(1)} collective-permute-done((bf16[256,384]{1,0:T(8,128)(2,1)}, bf16[256,384]{1,0:T(8,128)(2,1)S(1)}, u32[]{:S(2)}, u32[]{:S(2)}) %collective-permute-start.4) | collective-permute-done | bytes 196640 | tf_op jit(solution)/shard_map/ppermute | solution.py:100
  56.5 3.0 %shard_map.239 = (bf16[512,1024]{1,0:T(8,128)(2,1)}, bf16[512,1024]{1,0:T(8,128)(2,1)}) custom-call(bf16[256,1024]{1,0:T(8,128)(2,1)} %copy-done.4, bf16[256,1024]{1,0:T(8,128)(2,1)} %copy-done.15, bf16[256,1024]{1,0:T(8,128)(2,1)} %copy-done.14, bf16[256,1024]{1,0:T(8,128)(2,1)} %copy-done.13), custom_call_target="tpu_custom_call" | custom-call | flops 1024 | bytes 1024 | tf_op jit(solution)/shard_map/pallas_call | solution.py:110
  61.1 3.1 %fusion.6 = (f32[1024,128]{1,0:T(8,128)}, f32[1024,128]{1,0:T(8,128)}) fusion(f32[128]{0:T(128)S(1)} %get-tuple-element.235, f32[128]{0:T(128)S(1)} %get-tuple-element.236, f32[1024]{0:T(1024)S(1)} %bitcast.28), kind=kLoop, calls=%fused_computation.13 | loop fusion | flops 262144 | bytes 1053696 | tf_op jit(solution)/shard_map/mul | solution.py:815
  65.1 10.2 %shard_map.240 = (bf16[512,1024]{1,0:T(8,128)(2,1)}, f32[512,1024]{1,0:T(8,128)}, f32[1024,256]{1,0:T(8,128)}, bf16[1024,256]{1,0:T(8,128)(2,1)}, bf16[1024,128]{1,0:T(8,128)(2,1)}, /*index=5*/bf16[1024,384]{1,0:T(8,128)(2,1)}) custom-call(s32[3]{0:T(128)} %pad_add_fusion.where_ref.refs_0_, s32[4,4]{1,0:T(4,128)} %copy-done.32, ...), custom_call_target="tpu_custom_call" | custom-call | flops 1024 | bytes 1024 | tf_op jit(solution)/shard_map/pallas_call | solution.py:426
  76.0 2.5 collective-permute-done.10.received
  79.4 3.8 %shard_map.241 = (f32[128,1024]{1,0:T(8,128)}, bf16[128,1024]{1,0:T(8,128)(2,1)}, bf16[128,1024]{1,0:T(8,128)(2,1)}, bf16[128,1024]{1,0:T(8,128)(2,1)}) custom-call(f32[512,1024]{1,0:T(8,128)} %get-tuple-element.137.keep, bf16[512,1024]{1,0:T(8,128)(2,1)} %copy-done.9), custom_call_target="tpu_custom_call" | custom-call | flops 1024 | bytes 1024 | tf_op jit(solution)/shard_map/pallas_call | solution.py:577
  83.2 1.2 collective-permute-start.11
  85.4 1.4 collective-permute-start.13
  86.8 5.8 %collective-permute-done.11 = bf16[128,1024]{1,0:T(8,128)(2,1)S(1)} collective-permute-done((bf16[128,1024]{1,0:T(8,128)(2,1)}, bf16[128,1024]{1,0:T(8,128)(2,1)S(1)}, u32[]{:S(2)}, u32[]{:S(2)}) %collective-permute-start.11) | collective-permute-done | bytes 262176 | tf_op jit(solution)/shard_map/ppermute | solution.py:95
  92.6 5.9 %collective-permute-done.12 = bf16[128,1024]{1,0:T(8,128)(2,1)S(1)} collective-permute-done((bf16[128,1024]{1,0:T(8,128)(2,1)}, bf16[128,1024]{1,0:T(8,128)(2,1)S(1)}, u32[]{:S(2)}, u32[]{:S(2)}) %collective-permute-start.12) | collective-permute-done | bytes 262176 | tf_op jit(solution)/shard_map/ppermute | solution.py:95
  98.6 1.3 multiply_reduce_fusion.2
  100.1 1.2 collective-permute-start.16
  101.3 1.2 collective-permute-start.15
  102.4 1.2 collective-permute-start.14
  103.6 6.7 %collective-permute-done.16 = bf16[128,1024]{1,0:T(8,128)(2,1)S(1)} collective-permute-done((bf16[128,1024]{1,0:T(8,128)(2,1)S(1)}, bf16[128,1024]{1,0:T(8,128)(2,1)S(1)}, u32[]{:S(2)}, u32[]{:S(2)}) %collective-permute-start.16) | collective-permute-done | bytes 262176 | tf_op jit(solution)/shard_map/ppermute | solution.py:95
  110.3 3.4 %collective-permute-done.15 = bf16[128,1024]{1,0:T(8,128)(2,1)S(1)} collective-permute-done((bf16[128,1024]{1,0:T(8,128)(2,1)S(1)}, bf16[128,1024]{1,0:T(8,128)(2,1)S(1)}, u32[]{:S(2)}, u32[]{:S(2)}) %collective-permute-start.15) | collective-permute-done | bytes 262176 | tf_op jit(solution)/shard_map/ppermute | solution.py:95
  114.0 1.1 copy-done.8
  115.1 1.6 collective-permute-done.17.x_o
  116.7 10.3 %all-gather.2.cloned.1.call-done.weight = bf16[1024,1792]{1,0:T(8,128)(2,1)} async-done(((bf16[256,1792]{1,0:T(8,128)(2,1)}), bf16[1024,1792]{1,0:T(8,128)(2,1)}) %all-gather.2.cloned.1.call-update) | async-done | bytes 3670032 | tf_op jit(solution)/shard_map/all_gather | solution.py:794
  127.0 20.5 %shard_map.242 = (bf16[512,1024]{1,0:T(8,128)(2,1)}, f32[512,1024]{1,0:T(8,128)}, bf16[512,1024]{1,0:T(8,128)(2,1)}, f32[512,1024]{1,0:T(8,128)}, bf16[1024,1792]{1,0:T(8,128)(2,1)}) custom-call(s32[3]{0:T(128)} %pad_add_fusion.where_ref.refs_0_, s32[4,4]{1,0:T(4,128)} %copy-done.32, bf16[512,1024]{1,0:T(8,128)(2,1)} %collective-permute-done.17.x_o, ...), custom_call_target="tpu_custom_call" | custom-call | flops 1024 | bytes 1024 | tf_op jit(solution)/shard_map/pallas_call | solution.py:544
  147.6 2.9 %collective-permute-done.19.received = bf16[512,1024]{1,0:T(8,128)(2,1)S(1)} collective-permute-done((bf16[512,1024]{1,0:T(8,128)(2,1)}, bf16[512,1024]{1,0:T(8,128)(2,1)S(1)}, u32[]{:S(2)}, u32[]{:S(2)}) %collective-permute-start.19) | collective-permute-done | bytes 1048608 | tf_op jit(solution)/shard_map/ppermute | solution.py:104
  151.4 4.1 %shard_map.244 = (f32[128,1024]{1,0:T(8,128)}, bf16[128,1024]{1,0:T(8,128)(2,1)}, bf16[128,1024]{1,0:T(8,128)(2,1)}, bf16[128,1024]{1,0:T(8,128)(2,1)}) custom-call(f32[512,1024]{1,0:T(8,128)} %get-tuple-element.150.keep, bf16[512,1024]{1,0:T(8,128)(2,1)} %copy-done.10), custom_call_target="tpu_custom_call" | custom-call | flops 1024 | bytes 1024 | tf_op jit(solution)/shard_map/pallas_call | solution.py:577
  155.6 1.4 collective-permute-start.20
  156.9 1.5 collective-permute-start.21
  159.0 1.3 slice.19
  161.0 4.0 %collective-permute-done.20 = bf16[128,1024]{1,0:T(8,128)(2,1)S(1)} collective-permute-done((bf16[128,1024]{1,0:T(8,128)(2,1)}, bf16[128,1024]{1,0:T(8,128)(2,1)S(1)}, u32[]{:S(2)}, u32[]{:S(2)}) %collective-permute-start.20) | collective-permute-done | bytes 262176 | tf_op jit(solution)/shard_map/ppermute | solution.py:95
  164.9 5.9 %collective-permute-done.21 = bf16[128,1024]{1,0:T(8,128)(2,1)S(1)} collective-permute-done((bf16[128,1024]{1,0:T(8,128)(2,1)}, bf16[128,1024]{1,0:T(8,128)(2,1)S(1)}, u32[]{:S(2)}, u32[]{:S(2)}) %collective-permute-start.21) | collective-permute-done | bytes 262176 | tf_op jit(solution)/shard_map/ppermute | solution.py:95
  170.8 2.0 multiply_reduce_fusion
  173.0 1.6 collective-permute-start.25
  174.6 1.2 collective-permute-start.24
  176.6 6.7 %collective-permute-done.25 = bf16[128,1024]{1,0:T(8,128)(2,1)S(1)} collective-permute-done((bf16[128,1024]{1,0:T(8,128)(2,1)S(1)}, bf16[128,1024]{1,0:T(8,128)(2,1)S(1)}, u32[]{:S(2)}, u32[]{:S(2)}) %collective-permute-start.25) | collective-permute-done | bytes 262176 | tf_op jit(solution)/shard_map/ppermute | solution.py:95
  183.2 3.6 %collective-permute-done.24 = bf16[128,1024]{1,0:T(8,128)(2,1)S(1)} collective-permute-done((bf16[128,1024]{1,0:T(8,128)(2,1)S(1)}, bf16[128,1024]{1,0:T(8,128)(2,1)S(1)}, u32[]{:S(2)}, u32[]{:S(2)}) %collective-permute-start.24) | collective-permute-done | bytes 262176 | tf_op jit(solution)/shard_map/ppermute | solution.py:95
  187.1 4.0 %shard_map.245 = (f32[128,1024]{1,0:T(8,128)}, bf16[128,1024]{1,0:T(8,128)(2,1)}, bf16[128,1024]{1,0:T(8,128)(2,1)}, bf16[128,1024]{1,0:T(8,128)(2,1)}) custom-call(f32[512,1024]{1,0:T(8,128)} %get-tuple-element.161.keep, bf16[512,1024]{1,0:T(8,128)(2,1)} %collective-permute-done.27.received), custom_call_target="tpu_custom_call" | custom-call | flops 1024 | bytes 1024 | tf_op jit(solution)/shard_map/pallas_call | solution.py:577
  192.2 16.2 %shard_map.246 = (bf16[512,1024]{1,0:T(8,128)(2,1)}, f32[512,1024]{1,0:T(8,128)}, f32[256,384]{1,0:T(8,128)}, f32[8,384]{1,0:T(8,128)}, bf16[272,384]{1,0:T(8,12...) custom-call(s32[3]{0:T(128)} %pad_add_fusion.where_ref.refs_0_, s32[4,4]{1,0:T(4,128)} %copy-done.32, ...), custom_call_target="tpu_custom_call" | custom-call | flops 1024 | bytes 1024 | tf_op jit(solution)/shard_map/pallas_call | solution.py:452
  209.6 1.2 collective-permute-start.30
  210.8 1.4 collective-permute-start.31
  212.2 5.8 %collective-permute-done.29 = bf16[128,1024]{1,0:T(8,128)(2,1)S(1)} collective-permute-done((bf16[128,1024]{1,0:T(8,128)(2,1)}, bf16[128,1024]{1,0:T(8,128)(2,1)S(1)}, u32[]{:S(2)}, u32[]{:S(2)}) %collective-permute-start.29) | collective-permute-done | bytes 262176 | tf_op jit(solution)/shard_map/ppermute | solution.py:95
  218.0 5.6 %collective-permute-done.30 = bf16[128,1024]{1,0:T(8,128)(2,1)S(1)} collective-permute-done((bf16[128,1024]{1,0:T(8,128)(2,1)}, bf16[128,1024]{1,0:T(8,128)(2,1)S(1)}, u32[]{:S(2)}, u32[]{:S(2)}) %collective-permute-start.30) | collective-permute-done | bytes 262176 | tf_op jit(solution)/shard_map/ppermute | solution.py:95
  224.6 2.3 shard_map.243
  227.9 3.8 %shard_map.247 = (f32[128,1024]{1,0:T(8,128)}, bf16[128,1024]{1,0:T(8,128)(2,1)}, bf16[128,1024]{1,0:T(8,128)(2,1)}, bf16[128,1024]{1,0:T(8,128)(2,1)}) custom-call(f32[512,1024]{1,0:T(8,128)} %get-tuple-element.174.keep, bf16[512,1024]{1,0:T(8,128)(2,1)} %copy-done.6), custom_call_target="tpu_custom_call" | custom-call | flops 1024 | bytes 1024 | tf_op jit(solution)/shard_map/pallas_call | solution.py:577
  231.7 1.1 collective-permute-start.32
  233.5 1.8 collective-permute-start.34
  237.2 8.8 %collective-permute-done.39.refs_1_ = bf16[272,384]{1,0:T(8,128)(2,1)S(1)} collective-permute-done((bf16[272,384]{1,0:T(8,128)(2,1)S(1)}, bf16[272,384]{1,0:T(8,128)(2,1)S(1)}, u32[]{:S(2)}, u32[]{:S(2)}) %collective-permute-start.39) | collective-permute-done | bytes 208928 | tf_op jit(solution)/shard_map/ppermute | solution.py:100
  246.8 1.2 collective-permute-start.36
  248.0 2.1 shard_map.248
  250.1 1.6 collective-permute-start.37
  252.5 1.2 collective-permute-start.42
  253.7 1.3 fusion.2
  255.0 3.3 %collective-permute-done.41.one = bf16[80,384]{1,0:T(8,128)(2,1)S(1)} collective-permute-done((bf16[80,384]{1,0:T(8,128)(2,1)}, bf16[80,384]{1,0:T(8,128)(2,1)S(1)}, u32[]{:S(2)}, u32[]{:S(2)}) %collective-permute-start.41) | collective-permute-done | bytes 61472 | tf_op jit(solution)/shard_map/ppermute | solution.py:95
  258.3 1.4 collective-permute-start.43
  259.7 3.7 %collective-permute-done.43.three = bf16[80,384]{1,0:T(8,128)(2,1)S(1)} collective-permute-done((bf16[80,384]{1,0:T(8,128)(2,1)S(1)}, bf16[80,384]{1,0:T(8,128)(2,1)S(1)}, u32[]{:S(2)}, u32[]{:S(2)}) %collective-permute-start.43) | collective-permute-done | bytes 61472 | tf_op jit(solution)/shard_map/ppermute | solution.py:95
  264.0 1.7 shard_map.249
  266.8 2.6 shard_map.250
  (163 shorter events, 24.0 us)
Async XLA Ops:
  7.2 119.8 %all-gather.2.cloned.1.call-start = ((), (), s32[]{:S(2)}) async-start(), calls=%async_computation.1 | async-start | bytes 4587520 | tf_op jit(solution)/shard_map/all_gather | solution.py:794
  10.4 11.7 %collective-permute-start = (bf16[160,1024]{1,0:T(8,128)(2,1)}, bf16[160,1024]{1,0:T(8,128)(2,1)S(1)}, u32[]{:S(2)}, u32[]{:S(2)}) collective-permute-start(bf16[160,1024]{1,0:T(8,128)(2,1)} %get-tuple-element.117), channel_id=1, source_target_pairs={{0,2},{2,0},{4,6},{6,4},{8,10},{10,8},{12,14},{14,12},{16,18},{18,... | collective-permute-start | bytes 983048 | tf_op jit(solution)/shard_map/ppermute | solution.py:95
  13.3 16.4 %collective-permute-start.1 = (bf16[160,1024]{1,0:T(8,128)(2,1)}, bf16[160,1024]{1,0:T(8,128)(2,1)S(1)}, u32[]{:S(2)}, u32[]{:S(2)}) collective-permute-start(bf16[160,1024]{1,0:T(8,128)(2,1)} %get-tuple-element.118), channel_id=1, source_target_pairs={{0,4},{2,6},{4,0},{6,2},{8,12},{10,14},{12,8},{14,10},{16,20},{18,... | collective-permute-start | bytes 983048 | tf_op jit(solution)/shard_map/ppermute | solution.py:95
  14.8 14.9 %collective-permute-start.2 = (bf16[160,1024]{1,0:T(8,128)(2,1)}, bf16[160,1024]{1,0:T(8,128)(2,1)S(1)}, u32[]{:S(2)}, u32[]{:S(2)}) collective-permute-start(bf16[160,1024]{1,0:T(8,128)(2,1)} %get-tuple-element.119), channel_id=1, source_target_pairs={{0,6},{2,4},{4,2},{6,0},{8,14},{10,12},{12,10},{14,8},{16,22},{18,... | collective-permute-start | bytes 983048 | tf_op jit(solution)/shard_map/ppermute | solution.py:95
  15.9 39.6 %copy-start.4 = (bf16[256,1024]{1,0:T(8,128)(2,1)}, bf16[256,1024]{1,0:T(8,128)(2,1)S(1)}, u32[]{:S(2)}) copy-start(bf16[256,1024]{1,0:T(8,128)(2,1)S(1)} %pad_maximum_fusion.2.own) | copy-start | bytes 1572868
  29.7 29.8 %copy-start.35 = (f32[64]{0:T(128)S(1)}, f32[64]{0:T(128)}, u32[]{:S(2)}) copy-start(f32[64]{0:T(128)} %param.17) | copy-start | bytes 772
  29.7 29.8 %copy-start.36 = (f32[64]{0:T(128)S(1)}, f32[64]{0:T(128)}, u32[]{:S(2)}) copy-start(f32[64]{0:T(128)} %param.18) | copy-start | bytes 772
  29.7 25.6 %collective-permute-start.8 = (bf16[256,1024]{1,0:T(8,128)(2,1)S(1)}, bf16[256,1024]{1,0:T(8,128)(2,1)S(1)}, u32[]{:S(2)}, u32[]{:S(2)}) collective-permute-start(bf16[256,1024]{1,0:T(8,128)(2,1)S(1)} %pad_maximum_fusion.2.own), channel_id=1, source_target_pairs={{0,6},{2,4},{4,2},{6,0},{8,14},{10,12},{12,10},{14,8},{16,22},{18,... | collective-permute-start | bytes 1572872 | tf_op jit(solution)/shard_map/ppermute | solution.py:95
  31.3 24.0 %collective-permute-start.7 = (bf16[256,1024]{1,0:T(8,128)(2,1)S(1)}, bf16[256,1024]{1,0:T(8,128)(2,1)S(1)}, u32[]{:S(2)}, u32[]{:S(2)}) collective-permute-start(bf16[256,1024]{1,0:T(8,128)(2,1)S(1)} %pad_maximum_fusion.2.own), channel_id=1, source_target_pairs={{0,4},{2,6},{4,0},{6,2},{8,12},{10,14},{12,8},{14,10},{16,20},{18,... | collective-permute-start | bytes 1572872 | tf_op jit(solution)/shard_map/ppermute | solution.py:95
  32.4 22.9 %collective-permute-start.6 = (bf16[256,1024]{1,0:T(8,128)(2,1)S(1)}, bf16[256,1024]{1,0:T(8,128)(2,1)S(1)}, u32[]{:S(2)}, u32[]{:S(2)}) collective-permute-start(bf16[256,1024]{1,0:T(8,128)(2,1)S(1)} %pad_maximum_fusion.2.own), channel_id=1, source_target_pairs={{0,2},{2,0},{4,6},{6,4},{8,10},{10,8},{12,14},{14,12},{16,18},{18,... | collective-permute-start | bytes 1572872 | tf_op jit(solution)/shard_map/ppermute | solution.py:95
  35.8 9.3 %collective-permute-start.5 = (bf16[256,384]{1,0:T(8,128)(2,1)}, bf16[256,384]{1,0:T(8,128)(2,1)S(1)}, u32[]{:S(2)}, u32[]{:S(2)}) collective-permute-start(bf16[256,384]{1,0:T(8,128)(2,1)} %get-tuple-element.133.refs_9_), channel_id=1, source_target_pairs={{0,24},{2,26},{4,28},{6,30},{8,0},{10,2},{12,4},{14,6},{16,8},{18,... | collective-permute-start | bytes 589832 | tf_op jit(solution)/shard_map/ppermute | solution.py:100
  39.4 15.9 %collective-permute-start.4 = (bf16[256,384]{1,0:T(8,128)(2,1)}, bf16[256,384]{1,0:T(8,128)(2,1)S(1)}, u32[]{:S(2)}, u32[]{:S(2)}) collective-permute-start(bf16[256,384]{1,0:T(8,128)(2,1)} %get-tuple-element.133.refs_9_), channel_id=1, source_target_pairs={{0,16},{2,18},{4,20},{6,22},{8,24},{10,26},{12,28},{14,30},{16,0},... | collective-permute-start | bytes 589832 | tf_op jit(solution)/shard_map/ppermute | solution.py:100
  45.0 19.1 %copy-start.25 = (bf16[256,384]{1,0:T(8,128)(2,1)}, bf16[256,384]{1,0:T(8,128)(2,1)S(1)}, u32[]{:S(2)}) copy-start(bf16[256,384]{1,0:T(8,128)(2,1)S(1)} %collective-permute-done.5.refs_12_) | copy-start | bytes 589828
  45.0 10.2 %collective-permute-start.3 = (bf16[256,384]{1,0:T(8,128)(2,1)}, bf16[256,384]{1,0:T(8,128)(2,1)S(1)}, u32[]{:S(2)}, u32[]{:S(2)}) collective-permute-start(bf16[256,384]{1,0:T(8,128)(2,1)} %get-tuple-element.133.refs_9_), channel_id=1, source_target_pairs={{0,8},{2,10},{4,12},{6,14},{8,16},{10,18},{12,20},{14,22},{16,24},... | collective-permute-start | bytes 589832 | tf_op jit(solution)/shard_map/ppermute | solution.py:100
  55.4 169.2 %reduce-scatter.2.cloned.1.call-start = ((), (), s32[]{:S(2)}) async-start(), calls=%async_computation.2 | async-start | bytes 4587520 | tf_op jit(solution)/shard_map/reduce_scatter | solution.py:847
  59.4 4.7 %collective-permute-start.9 = (bf16[512,1024]{1,0:T(8,128)(2,1)}, bf16[512,1024]{1,0:T(8,128)(2,1)S(1)}, u32[]{:S(2)}, u32[]{:S(2)}) collective-permute-start(bf16[512,1024]{1,0:T(8,128)(2,1)} %get-tuple-element.132.refs_2_), channel_id=1, source_target_pairs={{0,1},{1,0},{2,3},{3,2},{4,5},{5,4},{6,7},{7,6},{8,9},{9,8},{10,11... | collective-permute-start | bytes 3145736 | tf_op jit(solution)/shard_map/ppermute | solution.py:104
  75.4 23.2 %copy-start.3 = (bf16[128,1024]{1,0:T(8,128)(2,1)S(1)}, bf16[128,1024]{1,0:T(8,128)(2,1)}, u32[]{:S(2)}) copy-start(bf16[128,1024]{1,0:T(8,128)(2,1)} %param.14) | copy-start | bytes 786436
  75.4 3.1 %collective-permute-start.10 = (bf16[512,1024]{1,0:T(8,128)(2,1)}, bf16[512,1024]{1,0:T(8,128)(2,1)S(1)}, u32[]{:S(2)}, u32[]{:S(2)}) collective-permute-start(bf16[512,1024]{1,0:T(8,128)(2,1)} %get-tuple-element.138), channel_id=1, source_target_pairs={{0,1},{1,0},{2,3},{3,2},{4,5},{5,4},{6,7},{7,6},{8,9},{9,8},{10,11... | collective-permute-start | bytes 3145736 | tf_op jit(solution)/shard_map/ppermute | solution.py:104
  79.4 20.5 %copy-start.33 = (f32[1024]{0:T(1024)S(1)}, f32[1024]{0:T(1024)}, u32[]{:S(2)}) copy-start(f32[1024]{0:T(1024)} %param.19) | copy-start | bytes 12292
  83.2 20.4 %copy-start.5 = (bf16[512,1024]{1,0:T(8,128)(2,1)S(1)}, bf16[512,1024]{1,0:T(8,128)(2,1)}, u32[]{:S(2)}) copy-start(bf16[512,1024]{1,0:T(8,128)(2,1)} %get-tuple-element.143.g_m) | copy-start | bytes 3145732
  83.2 9.4 %collective-permute-start.11 = (bf16[128,1024]{1,0:T(8,128)(2,1)}, bf16[128,1024]{1,0:T(8,128)(2,1)S(1)}, u32[]{:S(2)}, u32[]{:S(2)}) collective-permute-start(bf16[128,1024]{1,0:T(8,128)(2,1)} %get-tuple-element.140), channel_id=1, source_target_pairs={{0,2},{2,0},{4,6},{6,4},{8,10},{10,8},{12,14},{14,12},{16,18},{18,... | collective-permute-start | bytes 786440 | tf_op jit(solution)/shard_map/ppermute | solution.py:95
  84.5 14.1 %collective-permute-start.12 = (bf16[128,1024]{1,0:T(8,128)(2,1)}, bf16[128,1024]{1,0:T(8,128)(2,1)S(1)}, u32[]{:S(2)}, u32[]{:S(2)}) collective-permute-start(bf16[128,1024]{1,0:T(8,128)(2,1)} %get-tuple-element.141), channel_id=1, source_target_pairs={{0,4},{2,6},{4,0},{6,2},{8,12},{10,14},{12,8},{14,10},{16,20},{18,... | collective-permute-start | bytes 786440 | tf_op jit(solution)/shard_map/ppermute | solution.py:95
  85.4 13.2 %collective-permute-start.13 = (bf16[128,1024]{1,0:T(8,128)(2,1)}, bf16[128,1024]{1,0:T(8,128)(2,1)S(1)}, u32[]{:S(2)}, u32[]{:S(2)}) collective-permute-start(bf16[128,1024]{1,0:T(8,128)(2,1)} %get-tuple-element.142), channel_id=1, source_target_pairs={{0,6},{2,4},{4,2},{6,0},{8,14},{10,12},{12,10},{14,8},{16,22},{18,... | collective-permute-start | bytes 786440 | tf_op jit(solution)/shard_map/ppermute | solution.py:95
  100.1 10.3 %collective-permute-start.16 = (bf16[128,1024]{1,0:T(8,128)(2,1)S(1)}, bf16[128,1024]{1,0:T(8,128)(2,1)S(1)}, u32[]{:S(2)}, u32[]{:S(2)}) collective-permute-start(bf16[128,1024]{1,0:T(8,128)(2,1)S(1)} %multiply_convert_fusion), channel_id=1, source_target_pairs={{0,6},{2,4},{4,2},{6,0},{8,14},{10,12},{12,10},{14,8},{16,22},{18,... | collective-permute-start | bytes 786440 | tf_op jit(solution)/shard_map/ppermute | solution.py:95
  101.3 12.4 %collective-permute-start.15 = (bf16[128,1024]{1,0:T(8,128)(2,1)S(1)}, bf16[128,1024]{1,0:T(8,128)(2,1)S(1)}, u32[]{:S(2)}, u32[]{:S(2)}) collective-permute-start(bf16[128,1024]{1,0:T(8,128)(2,1)S(1)} %multiply_convert_fusion), channel_id=1, source_target_pairs={{0,4},{2,6},{4,0},{6,2},{8,12},{10,14},{12,8},{14,10},{16,20},{18,... | collective-permute-start | bytes 786440 | tf_op jit(solution)/shard_map/ppermute | solution.py:95
  102.4 11.3 %collective-permute-start.14 = (bf16[128,1024]{1,0:T(8,128)(2,1)S(1)}, bf16[128,1024]{1,0:T(8,128)(2,1)S(1)}, u32[]{:S(2)}, u32[]{:S(2)}) collective-permute-start(bf16[128,1024]{1,0:T(8,128)(2,1)S(1)} %multiply_convert_fusion), channel_id=1, source_target_pairs={{0,2},{2,0},{4,6},{6,4},{8,10},{10,8},{12,14},{14,12},{16,18},{18,... | collective-permute-start | bytes 786440 | tf_op jit(solution)/shard_map/ppermute | solution.py:95
  103.6 10.4 %collective-permute-start.18 = (bf16[512,1024]{1,0:T(8,128)(2,1)S(1)}, bf16[512,1024]{1,0:T(8,128)(2,1)S(1)}, u32[]{:S(2)}, u32[]{:S(2)}) collective-permute-start(bf16[512,1024]{1,0:T(8,128)(2,1)S(1)} %copy-done.5), channel_id=1, source_target_pairs={{0,1},{1,0},{2,3},{3,2},{4,5},{5,4},{6,7},{7,6},{8,9},{9,8},{10,11... | collective-permute-start | bytes 3145736 | tf_op jit(solution)/shard_map/ppermute | solution.py:104
  113.8 13.2 %copy-start.2 = (bf16[512,1024]{1,0:T(8,128)(2,1)}, bf16[512,1024]{1,0:T(8,128)(2,1)S(1)}, u32[]{:S(2)}) copy-start(bf16[512,1024]{1,0:T(8,128)(2,1)S(1)} %pad_maximum_fusion.x_m) | copy-start | bytes 3145732
  113.8 2.9 %collective-permute-start.17 = (bf16[512,1024]{1,0:T(8,128)(2,1)S(1)}, bf16[512,1024]{1,0:T(8,128)(2,1)}, u32[]{:S(2)}, u32[]{:S(2)}) collective-permute-start(bf16[512,1024]{1,0:T(8,128)(2,1)S(1)} %pad_maximum_fusion.x_m), channel_id=1, source_target_pairs={{0,1},{1,0},{2,3},{3,2},{4,5},{5,4},{6,7},{7,6},{8,9},{9,8},{10,11... | collective-permute-start | bytes 3145736 | tf_op jit(solution)/shard_map/ppermute | solution.py:104
  147.5 2.9 %collective-permute-start.19 = (bf16[512,1024]{1,0:T(8,128)(2,1)}, bf16[512,1024]{1,0:T(8,128)(2,1)S(1)}, u32[]{:S(2)}, u32[]{:S(2)}) collective-permute-start(bf16[512,1024]{1,0:T(8,128)(2,1)} %get-tuple-element.151), channel_id=1, source_target_pairs={{0,1},{1,0},{2,3},{3,2},{4,5},{5,4},{6,7},{7,6},{8,9},{9,8},{10,11... | collective-permute-start | bytes 3145736 | tf_op jit(solution)/shard_map/ppermute | solution.py:104
  151.4 21.3 %copy-start.11 = (bf16[128,1024]{1,0:T(8,128)(2,1)S(1)}, bf16[128,1024]{1,0:T(8,128)(2,1)}, u32[]{:S(2)}) copy-start(bf16[128,1024]{1,0:T(8,128)(2,1)} %param.27) | copy-start | bytes 786436
  155.6 9.4 %collective-permute-start.20 = (bf16[128,1024]{1,0:T(8,128)(2,1)}, bf16[128,1024]{1,0:T(8,128)(2,1)S(1)}, u32[]{:S(2)}, u32[]{:S(2)}) collective-permute-start(bf16[128,1024]{1,0:T(8,128)(2,1)} %get-tuple-element.158), channel_id=1, source_target_pairs={{0,2},{2,0},{4,6},{6,4},{8,10},{10,8},{12,14},{14,12},{16,18},{18,... | collective-permute-start | bytes 786440 | tf_op jit(solution)/shard_map/ppermute | solution.py:95
  156.9 13.9 %collective-permute-start.21 = (bf16[128,1024]{1,0:T(8,128)(2,1)}, bf16[128,1024]{1,0:T(8,128)(2,1)S(1)}, u32[]{:S(2)}, u32[]{:S(2)}) collective-permute-start(bf16[128,1024]{1,0:T(8,128)(2,1)} %get-tuple-element.159), channel_id=1, source_target_pairs={{0,4},{2,6},{4,0},{6,2},{8,12},{10,14},{12,8},{14,10},{16,20},{18,... | collective-permute-start | bytes 786440 | tf_op jit(solution)/shard_map/ppermute | solution.py:95
  158.4 12.4 %collective-permute-start.22 = (bf16[128,1024]{1,0:T(8,128)(2,1)}, bf16[128,1024]{1,0:T(8,128)(2,1)S(1)}, u32[]{:S(2)}, u32[]{:S(2)}) collective-permute-start(bf16[128,1024]{1,0:T(8,128)(2,1)} %get-tuple-element.160), channel_id=1, source_target_pairs={{0,6},{2,4},{4,2},{6,0},{8,14},{10,12},{12,10},{14,8},{16,22},{18,... | collective-permute-start | bytes 786440 | tf_op jit(solution)/shard_map/ppermute | solution.py:95
  161.0 15.6 %copy-start.37 = (bf16[512,1024]{1,0:T(8,128)(2,1)S(1)}, bf16[512,1024]{1,0:T(8,128)(2,1)}, u32[]{:S(2)}) copy-start(bf16[512,1024]{1,0:T(8,128)(2,1)} %get-tuple-element.162) | copy-start | bytes 3145732
  173.0 10.2 %collective-permute-start.25 = (bf16[128,1024]{1,0:T(8,128)(2,1)S(1)}, bf16[128,1024]{1,0:T(8,128)(2,1)S(1)}, u32[]{:S(2)}, u32[]{:S(2)}) collective-permute-start(bf16[128,1024]{1,0:T(8,128)(2,1)S(1)} %get-tuple-element.223), channel_id=1, source_target_pairs={{0,6},{2,4},{4,2},{6,0},{8,14},{10,12},{12,10},{14,8},{16,22},{18,... | collective-permute-start | bytes 786440 | tf_op jit(solution)/shard_map/ppermute | solution.py:95
  174.6 12.3 %collective-permute-start.24 = (bf16[128,1024]{1,0:T(8,128)(2,1)S(1)}, bf16[128,1024]{1,0:T(8,128)(2,1)S(1)}, u32[]{:S(2)}, u32[]{:S(2)}) collective-permute-start(bf16[128,1024]{1,0:T(8,128)(2,1)S(1)} %get-tuple-element.223), channel_id=1, source_target_pairs={{0,4},{2,6},{4,0},{6,2},{8,12},{10,14},{12,8},{14,10},{16,20},{18,... | collective-permute-start | bytes 786440 | tf_op jit(solution)/shard_map/ppermute | solution.py:95
  175.7 11.1 %collective-permute-start.23 = (bf16[128,1024]{1,0:T(8,128)(2,1)S(1)}, bf16[128,1024]{1,0:T(8,128)(2,1)S(1)}, u32[]{:S(2)}, u32[]{:S(2)}) collective-permute-start(bf16[128,1024]{1,0:T(8,128)(2,1)S(1)} %get-tuple-element.223), channel_id=1, source_target_pairs={{0,2},{2,0},{4,6},{6,4},{8,10},{10,8},{12,14},{14,12},{16,18},{18,... | collective-permute-start | bytes 786440 | tf_op jit(solution)/shard_map/ppermute | solution.py:95
  176.6 10.6 %collective-permute-start.27 = (bf16[512,1024]{1,0:T(8,128)(2,1)S(1)}, bf16[512,1024]{1,0:T(8,128)(2,1)}, u32[]{:S(2)}, u32[]{:S(2)}) collective-permute-start(bf16[512,1024]{1,0:T(8,128)(2,1)S(1)} %copy-done.37), channel_id=1, source_target_pairs={{0,1},{1,0},{2,3},{3,2},{4,5},{5,4},{6,7},{7,6},{8,9},{9,8},{10,11... | collective-permute-start | bytes 3145736 | tf_op jit(solution)/shard_map/ppermute | solution.py:104
  186.9 4.2 %collective-permute-start.26 = (bf16[512,1024]{1,0:T(8,128)(2,1)S(1)}, bf16[512,1024]{1,0:T(8,128)(2,1)S(1)}, u32[]{:S(2)}, u32[]{:S(2)}) collective-permute-start(bf16[512,1024]{1,0:T(8,128)(2,1)S(1)} %pad_maximum_fusion.1.refs_9_), channel_id=1, source_target_pairs={{0,1},{1,0},{2,3},{3,2},{4,5},{5,4},{6,7},{7,6},{8,9},{9,8},{10,11... | collective-permute-start | bytes 3145736 | tf_op jit(solution)/shard_map/ppermute | solution.py:104
  192.2 31.5 %copy-start.12 = (f32[128,1024]{1,0:T(8,128)S(1)}, f32[128,1024]{1,0:T(8,128)}, u32[]{:S(2)}) copy-start(f32[128,1024]{1,0:T(8,128)} %get-tuple-element.180) | copy-start | bytes 1572868
  208.4 18.5 %collective-permute-start.28 = (bf16[512,1024]{1,0:T(8,128)(2,1)}, bf16[512,1024]{1,0:T(8,128)(2,1)S(1)}, u32[]{:S(2)}, u32[]{:S(2)}) collective-permute-start(bf16[512,1024]{1,0:T(8,128)(2,1)} %get-tuple-element.175), channel_id=1, source_target_pairs={{0,1},{1,0},{2,3},{3,2},{4,5},{5,4},{6,7},{7,6},{8,9},{9,8},{10,11... | collective-permute-start | bytes 3145736 | tf_op jit(solution)/shard_map/ppermute | solution.py:104
  208.7 9.3 %collective-permute-start.29 = (bf16[128,1024]{1,0:T(8,128)(2,1)}, bf16[128,1024]{1,0:T(8,128)(2,1)S(1)}, u32[]{:S(2)}, u32[]{:S(2)}) collective-permute-start(bf16[128,1024]{1,0:T(8,128)(2,1)} %get-tuple-element.181), channel_id=1, source_target_pairs={{0,2},{2,0},{4,6},{6,4},{8,10},{10,8},{12,14},{14,12},{16,18},{18,... | collective-permute-start | bytes 786440 | tf_op jit(solution)/shard_map/ppermute | solution.py:95
  209.6 14.0 %collective-permute-start.30 = (bf16[128,1024]{1,0:T(8,128)(2,1)}, bf16[128,1024]{1,0:T(8,128)(2,1)S(1)}, u32[]{:S(2)}, u32[]{:S(2)}) collective-permute-start(bf16[128,1024]{1,0:T(8,128)(2,1)} %get-tuple-element.182), channel_id=1, source_target_pairs={{0,4},{2,6},{4,0},{6,2},{8,12},{10,14},{12,8},{14,10},{16,20},{18,... | collective-permute-start | bytes 786440 | tf_op jit(solution)/shard_map/ppermute | solution.py:95
  210.8 12.9 %collective-permute-start.31 = (bf16[128,1024]{1,0:T(8,128)(2,1)}, bf16[128,1024]{1,0:T(8,128)(2,1)S(1)}, u32[]{:S(2)}, u32[]{:S(2)}) collective-permute-start(bf16[128,1024]{1,0:T(8,128)(2,1)} %get-tuple-element.183), channel_id=1, source_target_pairs={{0,6},{2,4},{4,2},{6,0},{8,14},{10,12},{12,10},{14,8},{16,22},{18,... | collective-permute-start | bytes 786440 | tf_op jit(solution)/shard_map/ppermute | solution.py:95
  212.2 24.2 %collective-permute-start.38 = (bf16[272,384]{1,0:T(8,128)(2,1)}, bf16[272,384]{1,0:T(8,128)(2,1)S(1)}, u32[]{:S(2)}, u32[]{:S(2)}) collective-permute-start(bf16[272,384]{1,0:T(8,128)(2,1)} %get-tuple-element.196), channel_id=1, source_target_pairs={{0,8},{2,10},{4,12},{6,14},{8,16},{10,18},{12,20},{14,22},{16,24},... | collective-permute-start | bytes 626696 | tf_op jit(solution)/shard_map/ppermute | solution.py:100
  224.6 11.8 %copy-start.41 = (bf16[272,384]{1,0:T(8,128)(2,1)S(1)}, bf16[272,384]{1,0:T(8,128)(2,1)}, u32[]{:S(2)}) copy-start(bf16[272,384]{1,0:T(8,128)(2,1)} %get-tuple-element.198) | copy-start | bytes 626692
  226.9 19.1 %copy-start.40 = (bf16[64,1792]{1,0:T(8,128)(2,1)S(1)}, bf16[64,1792]{1,0:T(8,128)(2,1)}, u32[]{:S(2)}) copy-start(bf16[64,1792]{1,0:T(8,128)(2,1)} %get-tuple-element.191) | copy-start | bytes 688132
  226.9 19.9 %copy-start.39 = (bf16[64,1792]{1,0:T(8,128)(2,1)S(1)}, bf16[64,1792]{1,0:T(8,128)(2,1)}, u32[]{:S(2)}) copy-start(bf16[64,1792]{1,0:T(8,128)(2,1)} %get-tuple-element.192) | copy-start | bytes 688132
  226.9 23.2 %copy-start.38 = (bf16[64,1792]{1,0:T(8,128)(2,1)S(1)}, bf16[64,1792]{1,0:T(8,128)(2,1)}, u32[]{:S(2)}) copy-start(bf16[64,1792]{1,0:T(8,128)(2,1)} %get-tuple-element.193) | copy-start | bytes 688132
  226.9 26.8 %copy-start.28 = (f32[1024]{0:T(1024)S(1)}, f32[1024]{0:T(1024)}, u32[]{:S(2)}) copy-start(f32[1024]{0:T(1024)} %param.16) | copy-start | bytes 12292
  231.7 18.4 %collective-permute-start.32 = (bf16[128,1024]{1,0:T(8,128)(2,1)}, bf16[128,1024]{1,0:T(8,128)(2,1)S(1)}, u32[]{:S(2)}, u32[]{:S(2)}) collective-permute-start(bf16[128,1024]{1,0:T(8,128)(2,1)} %get-tuple-element.187), channel_id=1, source_target_pairs={{0,2},{2,0},{4,6},{6,4},{8,10},{10,8},{12,14},{14,12},{16,18},{18,... | collective-permute-start | bytes 786440 | tf_op jit(solution)/shard_map/ppermute | solution.py:95
  232.9 18.9 %collective-permute-start.33 = (bf16[128,1024]{1,0:T(8,128)(2,1)}, bf16[128,1024]{1,0:T(8,128)(2,1)S(1)}, u32[]{:S(2)}, u32[]{:S(2)}) collective-permute-start(bf16[128,1024]{1,0:T(8,128)(2,1)} %get-tuple-element.188), channel_id=1, source_target_pairs={{0,4},{2,6},{4,0},{6,2},{8,12},{10,14},{12,8},{14,10},{16,20},{18,... | collective-permute-start | bytes 786440 | tf_op jit(solution)/shard_map/ppermute | solution.py:95
  233.5 19.0 %collective-permute-start.34 = (bf16[128,1024]{1,0:T(8,128)(2,1)}, bf16[128,1024]{1,0:T(8,128)(2,1)S(1)}, u32[]{:S(2)}, u32[]{:S(2)}) collective-permute-start(bf16[128,1024]{1,0:T(8,128)(2,1)} %get-tuple-element.189), channel_id=1, source_target_pairs={{0,6},{2,4},{4,2},{6,0},{8,14},{10,12},{12,10},{14,8},{16,22},{18,... | collective-permute-start | bytes 786440 | tf_op jit(solution)/shard_map/ppermute | solution.py:95
  235.2 10.8 %collective-permute-start.39 = (bf16[272,384]{1,0:T(8,128)(2,1)S(1)}, bf16[272,384]{1,0:T(8,128)(2,1)S(1)}, u32[]{:S(2)}, u32[]{:S(2)}) collective-permute-start(bf16[272,384]{1,0:T(8,128)(2,1)S(1)} %copy-done.42), channel_id=1, source_target_pairs={{0,16},{2,18},{4,20},{6,22},{8,24},{10,26},{12,28},{14,30},{16,0},... | collective-permute-start | bytes 626696 | tf_op jit(solution)/shard_map/ppermute | solution.py:100
  236.3 11.7 %copy-start.22 = (bf16[272,384]{1,0:T(8,128)(2,1)}, bf16[272,384]{1,0:T(8,128)(2,1)S(1)}, u32[]{:S(2)}) copy-start(bf16[272,384]{1,0:T(8,128)(2,1)S(1)} %collective-permute-done.38.refs_0_) | copy-start | bytes 626692
  236.3 10.5 %collective-permute-start.40 = (bf16[272,384]{1,0:T(8,128)(2,1)S(1)}, bf16[272,384]{1,0:T(8,128)(2,1)S(1)}, u32[]{:S(2)}, u32[]{:S(2)}) collective-permute-start(bf16[272,384]{1,0:T(8,128)(2,1)S(1)} %copy-done.41), channel_id=1, source_target_pairs={{0,24},{2,26},{4,28},{6,30},{8,0},{10,2},{12,4},{14,6},{16,8},{18,... | collective-permute-start | bytes 626696 | tf_op jit(solution)/shard_map/ppermute | solution.py:100
  246.0 17.4 %collective-permute-start.35 = (bf16[64,1792]{1,0:T(8,128)(2,1)S(1)}, bf16[64,1792]{1,0:T(8,128)(2,1)S(1)}, u32[]{:S(2)}, u32[]{:S(2)}) collective-permute-start(bf16[64,1792]{1,0:T(8,128)(2,1)S(1)} %copy-done.40), channel_id=1, source_target_pairs={{0,2},{2,0},{4,6},{6,4},{8,10},{10,8},{12,14},{14,12},{16,18},{18,... | collective-permute-start | bytes 688136 | tf_op jit(solution)/shard_map/ppermute | solution.py:95
  246.8 16.6 %collective-permute-start.36 = (bf16[64,1792]{1,0:T(8,128)(2,1)S(1)}, bf16[64,1792]{1,0:T(8,128)(2,1)S(1)}, u32[]{:S(2)}, u32[]{:S(2)}) collective-permute-start(bf16[64,1792]{1,0:T(8,128)(2,1)S(1)} %copy-done.39), channel_id=1, source_target_pairs={{0,4},{2,6},{4,0},{6,2},{8,12},{10,14},{12,8},{14,10},{16,20},{18,... | collective-permute-start | bytes 688136 | tf_op jit(solution)/shard_map/ppermute | solution.py:95
  250.1 13.3 %collective-permute-start.37 = (bf16[64,1792]{1,0:T(8,128)(2,1)S(1)}, bf16[64,1792]{1,0:T(8,128)(2,1)S(1)}, u32[]{:S(2)}, u32[]{:S(2)}) collective-permute-start(bf16[64,1792]{1,0:T(8,128)(2,1)S(1)} %copy-done.38), channel_id=1, source_target_pairs={{0,6},{2,4},{4,2},{6,0},{8,14},{10,12},{12,10},{14,8},{16,22},{18,... | collective-permute-start | bytes 688136 | tf_op jit(solution)/shard_map/ppermute | solution.py:95
  251.7 6.6 %collective-permute-start.41 = (bf16[80,384]{1,0:T(8,128)(2,1)}, bf16[80,384]{1,0:T(8,128)(2,1)S(1)}, u32[]{:S(2)}, u32[]{:S(2)}) collective-permute-start(bf16[80,384]{1,0:T(8,128)(2,1)} %get-tuple-element.200), channel_id=1, source_target_pairs={{0,2},{2,0},{4,6},{6,4},{8,10},{10,8},{12,14},{14,12},{16,18},{18,... | collective-permute-start | bytes 184328 | tf_op jit(solution)/shard_map/ppermute | solution.py:95
  252.5 7.2 %collective-permute-start.42 = (bf16[80,384]{1,0:T(8,128)(2,1)}, bf16[80,384]{1,0:T(8,128)(2,1)S(1)}, u32[]{:S(2)}, u32[]{:S(2)}) collective-permute-start(bf16[80,384]{1,0:T(8,128)(2,1)} %get-tuple-element.201), channel_id=1, source_target_pairs={{0,4},{2,6},{4,0},{6,2},{8,12},{10,14},{12,8},{14,10},{16,20},{18,... | collective-permute-start | bytes 184328 | tf_op jit(solution)/shard_map/ppermute | solution.py:95
  258.3 5.1 %collective-permute-start.43 = (bf16[80,384]{1,0:T(8,128)(2,1)S(1)}, bf16[80,384]{1,0:T(8,128)(2,1)S(1)}, u32[]{:S(2)}, u32[]{:S(2)}) collective-permute-start(bf16[80,384]{1,0:T(8,128)(2,1)S(1)} %copy-done.43), channel_id=1, source_target_pairs={{0,6},{2,4},{4,2},{6,0},{8,14},{10,12},{12,10},{14,8},{16,22},{18,... | collective-permute-start | bytes 184328 | tf_op jit(solution)/shard_map/ppermute | solution.py:95
  265.8 3.7 %collective-permute-start.44 = (f32[8,384]{1,0:T(8,128)}, f32[8,384]{1,0:T(8,128)S(1)}, u32[]{:S(2)}, u32[]{:S(2)}) collective-permute-start(f32[8,384]{1,0:T(8,128)} %get-tuple-element.207), channel_id=1, source_target_pairs={{0,1},{1,0},{2,3},{3,2},{4,5},{5,4},{6,7},{7,6},{8,9},{9,8},{10,11... | collective-permute-start | bytes 36872 | tf_op jit(solution)/shard_map/ppermute | solution.py:104
  (27 other events, 98.2 us)
Sparse Core Ops, SparseCore 0:
  55.5 71.4 all-gather.1
  147.6 67.0 reduce-scatter.1

commit v6 on v5

--- a/solution.py
+++ b/solution.py
@@ -85,6 +85,10 @@
 HALF = 64
 VMEM_BYTES = 60 * 1024 * 1024
 COST = pl.CostEstimate(flops=1024, bytes_accessed=1024, transcendentals=0)
+
+
+def cost(megabytes):
+    return pl.CostEstimate(flops=1024, bytes_accessed=megabytes * 1000000, transcendentals=0)
 GAIN_ROWS = 8
 float32 = jnp.float32
 bfloat16 = jnp.bfloat16
@@ -118,8 +122,8 @@
     )(*operands)
 
 
-def ordered(first, second):
-    return lax.optimization_barrier((first, second))
+def after(first, second):
+    return lax.optimization_barrier((first, second))[1]
 
 
 def lane_ids(shape):
@@ -155,8 +159,9 @@
     last = w_g.shape[1] // LANES // PLANE * PLANE
     place = where_ref[0]
     lane = lane_ids((rows, LANES))
-    for mask, out in enumerate(outs):
+    for mask in range(PLANE):
         other = place ^ mask
+        out, second = outs[mask], outs[PLANE + mask]
         at = pl.multiple_of(other * LANES, LANES)
         tile = jnp.where(
             lane < HALF, half_tile(w_k, 0, other, False), half_tile(w_v, 0, other, True)
@@ -168,13 +173,13 @@
         pieces = [piece[: rows // 2], piece[rows // 2 :]] if parts == 2 else [padded(piece, high)]
         width = piece.shape[1]
         for part, values in enumerate(pieces):
-            out[:high, part * width : (part + 1) * width] = values.astype(bfloat16)
+            out[:, part * width : (part + 1) * width] = values.astype(bfloat16)
         free = out.shape[1] - parts * width
         ids = lane_ids((high, free))
         marks = jnp.zeros((high, free), float32)
         for slot in range(lengths_ref.shape[1]):
             marks = jnp.where(ids == free - LANES + slot, lengths_ref[0, slot].astype(float32), marks)
-        out[:high, parts * width :] = marks.astype(bfloat16)
+        out[:, parts * width :] = marks.astype(bfloat16)
 
         at = pl.multiple_of(other * big, LANES)
         small = jnp.where(
@@ -187,42 +192,39 @@
         lower = jnp.concatenate(
             [w_d[:, pl.ds(at, big)].astype(float32), small, small_down], axis=1
         )
-        out[high : high + tall, :] = padded(upper, tall).astype(bfloat16)
-        out[high + tall :, : lower.shape[1]] = padded(lower, tall).astype(bfloat16)
-        out[high + tall :, lower.shape[1] :] = jnp.zeros(
-            (tall, out.shape[1] - lower.shape[1]), bfloat16
+        second[:tall, :] = padded(upper, tall).astype(bfloat16)
+        second[tall:, : lower.shape[1]] = padded(lower, tall).astype(bfloat16)
+        second[tall:, lower.shape[1] :] = jnp.zeros(
+            (tall, second.shape[1] - lower.shape[1]), bfloat16
         )
 
 
-def unpack_kernel(where_ref, own, one, two, three, attn_out, ffn_out, lens_out, held_attn, held_ffn):
+def unpack_attn_kernel(where_ref, own, one, two, three, attn_out, lens_out, held):
     rows = attn_out.shape[0] // PLANE
     width = attn_out.shape[1]
-    parts, high = attn_rows(rows)
+    parts, _ = attn_rows(rows)
+    place = where_ref[0]
+    for mask, message in enumerate((own, one, two, three)):
+        at = pl.ds(pl.multiple_of((place ^ mask) * rows, rows), rows)
+        values = [
+            message[:, part * width : (part + 1) * width].astype(float32) for part in range(parts)
+        ]
+        held[at, :] = jnp.concatenate(values, axis=0) if parts == 2 else values[0][:rows]
+        lens = message[:16, message.shape[1] - LANES :].astype(float32)
+        lens_out[mask * 8 : (mask + 1) * 8, :] = lens[:8]
+    attn_out[...] = held[...].astype(bfloat16)
+
+
+def unpack_ffn_kernel(where_ref, own, one, two, three, ffn_out, held):
+    rows = ffn_out.shape[0] // PLANE
     tall = max(rows, 16)
     place = where_ref[0]
     for mask, message in enumerate((own, one, two, three)):
         at = pl.ds(pl.multiple_of((place ^ mask) * rows, rows), rows)
-        values = [
-            message[:high, part * width : (part + 1) * width].astype(float32)
-            for part in range(parts)
-        ]
-        held_attn[at, :] = jnp.concatenate(values, axis=0) if parts == 2 else values[0][:rows]
-        lens = message[:16, message.shape[1] - LANES :].astype(float32)
-        lens_out[mask * 8 : (mask + 1) * 8, :] = lens[:8]
         full = message.shape[1]
-        held_ffn[at, :full] = message[high : high + tall, :].astype(float32)[:rows]
-        rest = held_ffn.shape[1] - full
-        held_ffn[at, full:] = message[high + tall :, :rest].astype(float32)[:rows]
-    attn_out[...] = held_attn[...].astype(bfloat16)
-    ffn_out[...] = held_ffn[...].astype(bfloat16)
-
-
-def split_rows_kernel(own, one, two, three, tok_out, cot_out):
-    local = own.shape[0] // 2
-    for mask, message in enumerate((own, one, two, three)):
-        span = slice(mask * local, (mask + 1) * local)
-        tok_out[span, :] = message[:local, :]
-        cot_out[span, :] = message[local:, :]
+        held[at, :full] = message[:tall, :].astype(float32)[:rows]
+        held[at, full:] = message[tall:, : held.shape[1] - full].astype(float32)[:rows]
+    ffn_out[...] = held[...].astype(bfloat16)
 
 
 def head_mean(values):
@@ -274,17 +276,11 @@
     return pl.ds(pl.multiple_of(at, rows), rows)
 
 
-def attn_kernel(layers, where_ref, ends_ref, tok_m, tok_o, a_gain, q_gain, k_gain, cos, sin, *refs):
-    pieces, refs = refs[:layers], refs[layers:]
-    send, keep, pre_out, low_out, mixed_out, weight, held = refs
+def attn_kernel(where_ref, ends_ref, tok_m, tok_o, a_gain, q_gain, k_gain, cos, sin, weight, *refs):
+    send, keep, pre_out, low_out, mixed_out, held = refs
     group = pl.program_id(0)
-    depth, core = where_ref[1], where_ref[2]
+    core = where_ref[2]
     local = tok_m.shape[0]
-
-    @pl.when(group == 0)
-    def _():
-        for step, piece in enumerate(pieces):
-            weight[deep_rows(depth, -step, layers, piece.shape[0]), :] = piece[...]
 
     x = group_rows(core, tok_m[...].astype(float32), tok_o[...].astype(float32))
     normed = (x * inverse_rms(x) * a_gain[...]).astype(bfloat16)
@@ -317,14 +313,12 @@
 
 
 def attn_back_kernel(
-    layers, where_ref, ends_ref, tok_m, tok_o, a_gain, q_gain, k_gain, cos, sin, dh_m, dh_o,
+    where_ref, ends_ref, tok_m, tok_o, a_gain, q_gain, k_gain, cos, sin, dh_m, dh_o,
     pre_ref, low_ref, mixed_ref, weight, gain_ffn, *refs,
 ):
-    send, keep, own, gains_out = refs[:4]
-    pieces = refs[4 : 3 + layers]
-    held, total, sum_a, sum_qk = refs[3 + layers :]
+    send, keep, grad_out, gains_out, held, total, sum_a, sum_qk = refs
     group = pl.program_id(0)
-    depth, core = where_ref[1], where_ref[2]
+    core = where_ref[2]
     local = tok_m.shape[0]
 
     @pl.when(group == 0)
@@ -391,15 +385,7 @@
         qk_sum = jnp.where(lane_ids(q_sum.shape) < HALF, q_sum, k_sum)
         ids = lax.broadcasted_iota(jnp.int32, (GAIN_ROWS, LANES), 0)
         gains_out[:, 2 * LANES :] = jnp.where(ids == 0, qk_sum, 0.0)
-        gains = gains_out[...]
-        top = gains.astype(bfloat16)
-        rest = (gains - top.astype(float32)).astype(bfloat16)
-        tail = jnp.concatenate([top.astype(float32), rest.astype(float32)], axis=0).astype(bfloat16)
-        rows = own.shape[0]
-        own[...] = total[deep_rows(depth, 0, layers, rows), :]
-        for index, piece in enumerate(pieces):
-            piece[:rows, :] = total[deep_rows(depth, index + 1, layers, rows), :].astype(bfloat16)
-            piece[rows:, :] = tail
+        grad_out[...] = total[...].astype(bfloat16)
 
 
 def attn_specs(rows, width, group_height):
@@ -416,53 +402,46 @@
     return pl.BlockSpec(shape, lambda i: (0, 0), pipeline_mode=pl.Buffered(1))
 
 
-def attn(where, ends, tok_mine, tok_other, gains, tables, pieces):
-    layers = len(pieces)
+def attn(where, ends, tok_mine, tok_other, gains, tables, weight):
     rows, width = tok_mine.shape
     local = rows // PLANE
     scalar, block, gain, small, table, wide = attn_specs(local, width, 2 * local)
-    high, columns = pieces[0].shape
-    weight = (layers * high, columns)
     return pl.pallas_call(
-        lambda *refs: attn_kernel(layers, *refs),
+        attn_kernel,
         grid=(PLANE,),
         in_specs=[scalar, scalar, block, block, gain, small, small, table, table]
-        + [whole_spec((high, columns))] * layers,
-        out_specs=[block, block, wide, wide, table, whole_spec(weight)],
+        + [whole_spec(weight.shape)],
+        out_specs=[block, block, wide, wide, table],
         out_shape=[
             jax.ShapeDtypeStruct((rows, width), bfloat16),
             jax.ShapeDtypeStruct((rows, width), float32),
             jax.ShapeDtypeStruct((2 * rows, 2 * LANES), float32),
             jax.ShapeDtypeStruct((2 * rows, 2 * LANES), bfloat16),
             jax.ShapeDtypeStruct((2 * rows, LANES), bfloat16),
-            jax.ShapeDtypeStruct(weight, bfloat16),
         ],
         scratch_shapes=[pltpu.VMEM((2 * local, width), float32)],
         compiler_params=pltpu.CompilerParams(vmem_limit_bytes=VMEM_BYTES),
-        cost_estimate=COST,
-    )(where, ends, tok_mine, tok_other, *gains, *tables, *pieces)
-
-
-def attn_back(where, ends, layers, tok_mine, tok_other, gains, tables, dh, saved, weight, gain_ffn):
+        cost_estimate=cost(36),
+    )(where, ends, tok_mine, tok_other, *gains, *tables, weight)
+
+
+def attn_back(where, ends, tok_mine, tok_other, gains, tables, dh, saved, weight, gain_ffn):
     rows, width = tok_mine.shape
     local = rows // PLANE
     scalar, block, gain, small, table, wide = attn_specs(local, width, 2 * local)
-    high, columns = weight.shape[0] // layers, weight.shape[1]
-    tail = 2 * GAIN_ROWS
+    columns = weight.shape[1]
     return pl.pallas_call(
-        lambda *refs: attn_back_kernel(layers, *refs),
+        attn_back_kernel,
         grid=(PLANE,),
         in_specs=[scalar, scalar, block, block, gain, small, small, table, table, block, block]
         + [wide, wide, table, whole_spec(weight.shape), gain],
-        out_specs=[block, block, whole_spec((high, columns)), whole_spec((GAIN_ROWS, columns))]
-        + [whole_spec((high + tail, columns))] * (layers - 1),
+        out_specs=[block, block, whole_spec(weight.shape), whole_spec((GAIN_ROWS, columns))],
         out_shape=[
             jax.ShapeDtypeStruct((rows, width), bfloat16),
             jax.ShapeDtypeStruct((rows, width), float32),
-            jax.ShapeDtypeStruct((high, columns), float32),
+            jax.ShapeDtypeStruct(weight.shape, bfloat16),
             jax.ShapeDtypeStruct((GAIN_ROWS, columns), float32),
-        ]
-        + [jax.ShapeDtypeStruct((high + tail, columns), bfloat16)] * (layers - 1),
+        ],
         scratch_shapes=[
             pltpu.VMEM((2 * local, width), float32),
             pltpu.VMEM(weight.shape, float32),
@@ -470,7 +449,7 @@
             pltpu.VMEM((8, LANES), float32),
         ],
         compiler_params=pltpu.CompilerParams(vmem_limit_bytes=VMEM_BYTES),
-        cost_estimate=COST,
+        cost_estimate=cost(58),
     )(where, ends, tok_mine, tok_other, *gains, *tables, *dh, *saved, weight, gain_ffn)
 
 
@@ -555,7 +534,7 @@
         ],
         scratch_shapes=[pltpu.VMEM(weight.shape, float32)],
         compiler_params=pltpu.CompilerParams(vmem_limit_bytes=VMEM_BYTES),
-        cost_estimate=COST,
+        cost_estimate=cost(74),
     )(where, ends, x_other, x_mine, g_other, g_mine, weight)
 
 
@@ -567,23 +546,9 @@
 
 
 def chip_sum(keep, received):
-    rows, width = keep.shape
-    shape = (rows // PLANE, width)
-    block = 2 * LANES
-
-    def columns(height):
-        return pl.BlockSpec((height, block), lambda i: (0, i))
-
-    return pl.pallas_call(
-        chip_sum_kernel,
-        grid=(width // block,),
-        in_specs=[columns(rows)] * 2,
-        out_specs=[columns(shape[0])] * PLANE,
-        out_shape=[jax.ShapeDtypeStruct(shape, float32)]
-        + [jax.ShapeDtypeStruct(shape, bfloat16)] * (PLANE - 1),
-        compiler_params=pltpu.CompilerParams(vmem_limit_bytes=VMEM_BYTES),
-        cost_estimate=COST,
-    )(keep, received)
+    shape = (keep.shape[0] // PLANE, keep.shape[1])
+    outs = [(shape, float32)] + [(shape, bfloat16)] * (PLANE - 1)
+    return call(chip_sum_kernel, outs, keep, received)
 
 
 def plane_total(parts):
@@ -594,25 +559,44 @@
     return sum(part.astype(float32) for part in parts)
 
 
-def plane_split_kernel(where_ref, own, *refs):
-    outs, held = refs[:-1], refs[-1]
-    held[...] = own[...].astype(float32)
+def tail_kernel(where_ref, keep, received, own_ff, own, ff_out, *refs):
+    messages, held = refs[:-1], refs[-1]
+    held[...] = own_ff[...].astype(float32)
     place = where_ref[0]
-    rows = own.shape[0] // PLANE
-    for mask, out in enumerate(outs):
-        at = pl.multiple_of((place ^ mask) * rows, rows)
-        out[...] = held[pl.ds(at, rows), :].astype(out.dtype)
-
-
-def plane_split(where, own):
-    shape = (own.shape[0] // PLANE, own.shape[1])
+    local = own.shape[0]
+    rows = ff_out.shape[0]
+    tall = (messages[0].shape[0] - local) // 2
+    width = own.shape[1]
+    for mask in range(PLANE):
+        span = slice(mask * local, (mask + 1) * local)
+        value = keep[span, :] + received[span, :].astype(float32)
+        grads = held[pl.ds(pl.multiple_of((place ^ mask) * rows, rows), rows), :]
+        if mask == 0:
+            own[...] = value
+            ff_out[...] = grads
+            continue
+        out = messages[mask - 1]
+        out[:local, :] = value.astype(bfloat16)
+        out[local : local + tall, :] = padded(grads[:, :width], tall).astype(bfloat16)
+        rest = grads.shape[1] - width
+        out[local + tall :, :rest] = padded(grads[:, width:], tall).astype(bfloat16)
+        out[local + tall :, rest:] = jnp.zeros((tall, width - rest), bfloat16)
+
+
+def tail_messages(where, keep, received, own_ff):
+    local, width = keep.shape[0] // PLANE, keep.shape[1]
+    rows, columns = own_ff.shape[0] // PLANE, own_ff.shape[1]
+    message = (local + 2 * max(rows, 16), width)
     return call(
-        plane_split_kernel,
-        [(shape, bfloat16)] * PLANE,
+        tail_kernel,
+        [((local, width), float32), ((rows, columns), float32)]
+        + [(message, bfloat16)] * (PLANE - 1),
         where,
-        own,
+        keep,
+        received,
+        own_ff,
         scalars=1,
-        scratch=[pltpu.VMEM(own.shape, float32)],
+        scratch=[pltpu.VMEM(own_ff.shape, float32)],
     )
 
 
@@ -626,29 +610,22 @@
     return jnp.concatenate([top, rest], axis=0)
 
 
-def plane_sum_attn_kernel(where_ref, own, gains, *refs):
+def split_attn_kernel(where_ref, own, gains, *refs):
     received, outs = refs[: -PLANE - 2], refs[-PLANE - 2 : -2]
     held, held_gains = refs[-2:]
     layers = len(received) + 1
-    value = own[...]
-    high = own.shape[0]
     depth = where_ref[1]
-    held_gains[deep_rows(depth, 0, layers, GAIN_ROWS), :] = joined_gains(split_gains(gains[...]))
-    for step, part in enumerate(received):
-        value = value + part[:high, :].astype(float32)
-        held_gains[deep_rows(depth, -1 - step, layers, GAIN_ROWS), :] = joined_gains(
-            part[high:, :].astype(float32)
-        )
-    held[...] = value
+    for step, part in enumerate((gains,) + received):
+        held_gains[deep_rows(depth, -step, layers, GAIN_ROWS), :] = part[...]
+    held[...] = own[...].astype(float32)
     sums = held_gains[:GAIN_ROWS, :]
     for layer in range(1, layers):
         sums = sums + held_gains[layer * GAIN_ROWS : (layer + 1) * GAIN_ROWS, :]
     tail = split_gains(sums)
     place = where_ref[0]
-    rows = high // PLANE
+    rows = own.shape[0] // PLANE
     for mask, out in enumerate(outs):
-        at = pl.multiple_of((place ^ mask) * rows, rows)
-        part = held[pl.ds(at, rows), :]
+        part = held[pl.ds(pl.multiple_of((place ^ mask) * rows, rows), rows), :]
         if mask:
             tall = out.shape[0] - tail.shape[0]
             out[:tall, :] = padded(part, tall).astype(bfloat16)
@@ -658,8 +635,7 @@
             out[rows:, :] = tail
 
 
-def plane_split_attn(where, own, grad_pieces, gains):
-    received = [send_deep(piece, step + 1) for step, piece in enumerate(grad_pieces)]
+def split_attn(where, own, gains, received):
     rows, columns = own.shape[0] // PLANE, own.shape[1]
     tail = 2 * GAIN_ROWS
     shapes = [((rows + tail, columns), float32)]
@@ -668,9 +644,7 @@
         pltpu.VMEM(own.shape, float32),
         pltpu.VMEM(((len(received) + 1) * GAIN_ROWS, columns), float32),
     ]
-    return call(
-        plane_sum_attn_kernel, shapes, where, own, gains, *received, scalars=1, scratch=scratch
-    )
+    return call(split_attn_kernel, shapes, where, own, gains, *received, scalars=1, scratch=scratch)
 
 
 def pick_place(refs, place, target, columns, rows):
@@ -680,19 +654,29 @@
     return value
 
 
-def place_ffn_kernel(where_ref, own, one, two, three, out_g, out_u, out_d):
+def place_ffn_kernel(where_ref, own, one, two, three, out_g, out_u, out_d, held):
     place = where_ref[0]
-    refs = (own, one, two, three)
+    rows = out_g.shape[0]
     big = out_g.shape[1] // LANES // PLANE * LANES
     last = PLANE * big
-    for mask, ref in enumerate(refs):
+    width = one.shape[1]
+    tall = max(rows, 16)
+    start = one.shape[0] - 2 * tall
+    for mask, ref in enumerate((own, one, two, three)):
+        if mask:
+            top = ref[start : start + tall, :].astype(float32)[:rows]
+            rest = ref[start + tall :, : held.shape[2] - width].astype(float32)[:rows]
+            held[mask, :, :width] = top
+            held[mask, :, width:] = rest
+        else:
+            held[mask] = ref[...]
         at = pl.ds(pl.multiple_of((place ^ mask) * big, LANES), big)
         for number, out in enumerate((out_g, out_u, out_d)):
-            out[:, at] = ref[:, number * big : (number + 1) * big].astype(float32)
+            out[:, at] = held[mask, :, number * big : (number + 1) * big]
     for pair in range(PLANE // 2):
-        low = pick_place(refs, place, 2 * pair, slice(3 * big, 3 * big + 2 * LANES), out_g.shape[0])
-        high = pick_place(refs, place, 2 * pair + 1, slice(3 * big, 3 * big + 2 * LANES), out_g.shape[0])
-        lane = lane_ids((low.shape[0], LANES))
+        low = held[place ^ (2 * pair), :, 3 * big :]
+        high = held[place ^ (2 * pair + 1), :, 3 * big :]
+        lane = lane_ids((rows, LANES))
         span = slice(last + pair * LANES, last + (pair + 1) * LANES)
         gu_low, gu_high = low[:, :LANES], high[:, :LANES]
         out_g[:, span] = jnp.where(lane < HALF, gu_low, pltpu.roll(gu_high, HALF, 1))
@@ -719,9 +703,17 @@
     out_gains[...] = (tails[0] + tails[1]) + (tails[2] + tails[3])
 
 
+def plane_parts(local):
+    return [local] + [send_plane(local, mask) for mask in range(1, PLANE)]
+
+
+def both_cores(parts):
+    mine = jnp.concatenate(parts)
+    return mine, swap_cores(mine)
+
+
 def gather_rows(local):
-    mine = jnp.concatenate([local] + [send_plane(local, mask) for mask in range(1, PLANE)])
-    return mine, swap_cores(mine)
+    return both_cores(plane_parts(local))
 
 
 def body(
@@ -756,9 +748,9 @@
 
     parts, high = attn_rows(rows)
     tall = max(rows, 16)
-    messages = call(
+    first = call(
         pack_kernel,
-        [((high + 2 * tall, model), bfloat16)] * PLANE,
+        [((high, model), bfloat16)] * PLANE + [((2 * tall, model), bfloat16)] * PLANE,
         where,
         lengths,
         w_query,
@@ -770,35 +762,38 @@
         w_down,
         scalars=2,
     )
-    messages = [messages[0]] + [send_plane(messages[m], m) for m in range(1, PLANE)]
-    messages, local = ordered(messages, jnp.concatenate([tokens, cotangent]))
-    rows_messages = [local] + [send_plane(local, m) for m in range(1, PLANE)]
-    attn_piece, ff_piece, lens = call(
-        unpack_kernel,
-        [
-            ((PLANE * rows, attn_cols), bfloat16),
-            ((PLANE * rows, ff_cols), bfloat16),
-            ((PLANE * 8, LANES), float32),
-        ],
+    first, second = first[:PLANE], first[PLANE:]
+    attn_piece, lens = call(
+        unpack_attn_kernel,
+        [((PLANE * rows, attn_cols), bfloat16), ((PLANE * 8, LANES), float32)],
         where,
-        *messages,
+        first[0],
+        *[send_plane(first[m], m) for m in range(1, PLANE)],
         scalars=1,
-        scratch=[
-            pltpu.VMEM((PLANE * rows, attn_cols), float32),
-            pltpu.VMEM((PLANE * rows, ff_cols), float32),
-        ],
-    )
-    attn_pieces = [attn_piece] + [send_deep(attn_piece, step) for step in range(1, layers)]
-    attn_pieces, (ff_piece, rows_messages) = ordered(attn_pieces, (ff_piece, rows_messages))
+        scratch=[pltpu.VMEM((PLANE * rows, attn_cols), float32)],
+    )
     columns = [list(range(k, layers * PLANE, PLANE)) for k in range(PLANE)]
-    ff_weight = lax.all_gather(
-        ff_piece, "dp", axis=0, tiled=True, axis_index_groups=columns
-    )
-    tok_mine, cot_mine = call(
-        split_rows_kernel, [((PLANE * local_rows, model), bfloat16)] * 2, *rows_messages
-    )
-    tok_other = swap_cores(tok_mine)
-    cot_other = swap_cores(cot_mine)
+    attn_weight = lax.all_gather(
+        attn_piece, "dp", axis=0, tiled=True, axis_index_groups=columns
+    )
+    tok_parts = plane_parts(tokens)
+    tok_parts = after(attn_piece, tok_parts)
+    second = after(tok_parts, second)
+    tok_mine, tok_other = both_cores(tok_parts)
+    second = [second[0]] + [send_plane(second[m], m) for m in range(1, PLANE)]
+    cotangent_sent = after(second, cotangent)
+    (ff_piece,) = call(
+        unpack_ffn_kernel,
+        [((PLANE * rows, ff_cols), bfloat16)],
+        where,
+        *second,
+        scalars=1,
+        scratch=[pltpu.VMEM((PLANE * rows, ff_cols), float32)],
+    )
+    ff_weight = lax.all_gather(ff_piece, "dp", axis=0, tiled=True, axis_index_groups=columns)
+    cot_parts = plane_parts(cotangent_sent)
+    cot_mine, cot_other = both_cores(cot_parts)
+    attn_weight = after(ff_piece, attn_weight)
 
     slots = lengths.shape[1]
     all_lengths = lens.reshape(PLANE, 8, LANES)[:, 0, :slots].astype(jnp.int32)
@@ -822,9 +817,8 @@
     inputs = tokens.astype(jnp.float32)
     factor_a = inverse_rms(inputs)
     unit_a = inputs * factor_a
-    send, keep, *saved, attn_weight = attn(
-        where, ends, tok_mine, tok_other, gains, tables, attn_pieces
-    )
+    send, keep, *saved = attn(where, ends, tok_mine, tok_other, gains, tables, attn_weight)
+    send = after(cot_parts, send)
     hidden = inputs + plane_total(chip_sum(keep, swap_cores(send)))
     factor_b = inverse_rms(hidden)
     unit_b = hidden * factor_b
@@ -834,7 +828,7 @@
         where, ends, x_mine, x_other, cot_mine, cot_other, ff_weight
     )
     dn_parts = chip_sum(dn_keep, swap_cores(dn_send))
-    dn_parts, out_keep = ordered(dn_parts, out_keep)
+    out_keep = after(dn_parts, out_keep)
     d_normed2 = plane_total(dn_parts)
     grad_out = jnp.where(
         (jnp.arange(local_rows) + core * local_rows < ends[0, slots - 1])[:, None],
@@ -848,28 +842,36 @@
         ff_grad, "dp", scatter_dimension=0, tiled=True, axis_index_groups=columns
     )
     out_parts = chip_sum(out_keep, swap_cores(out_send))
-    (h_mine, h_other), out_parts = ordered((h_mine, h_other), out_parts)
+    out_parts = after((h_mine, h_other), out_parts)
     ffn_branch = plane_total(out_parts)
     block_out = (hidden + ffn_branch).astype(jnp.bfloat16)
 
-    send, keep, own_attn, part_gains, *attn_grads = attn_back(
-        where, ends, layers, tok_mine, tok_other, gains, tables, (h_mine, h_other), saved,
-        attn_weight, gain_ffn[None, :],
-    )
-    ff_parts = plane_split(where, own_ff)
-    ff_parts, keep = ordered(ff_parts, keep)
-    dn_parts = chip_sum(keep, swap_cores(send))
-    (dn_parts, block_out), own_attn = ordered((dn_parts, block_out), own_attn)
-    attn_parts = plane_split_attn(where, own_attn, attn_grads, part_gains)
-    d_normed = plane_total(dn_parts)
-    ff_parts = [ff_parts[0]] + [send_plane(part, mask + 1) for mask, part in enumerate(ff_parts[1:])]
+    send, keep, attn_grad, part_gains = attn_back(
+        where, ends, tok_mine, tok_other, gains, tables, (h_mine, h_other), saved, attn_weight,
+        gain_ffn[None, :],
+    )
+    send, keep, attn_grad, part_gains = after(block_out, (send, keep, attn_grad, part_gains))
+    own_attn = lax.psum_scatter(
+        attn_grad, "dp", scatter_dimension=0, tiled=True, axis_index_groups=columns
+    )
+    far_gains = [send_deep(part_gains, step) for step in range(1, layers)]
+    own_dn, own_ff, *messages = tail_messages(where, keep, swap_cores(send), own_ff)
+    messages = [send_plane(part, mask + 1) for mask, part in enumerate(messages)]
+    own_attn = after(messages, own_attn)
+    attn_parts = split_attn(where, own_attn, part_gains, far_gains)
     attn_parts = [attn_parts[0]] + [
         send_plane(part, mask + 1) for mask, part in enumerate(attn_parts[1:])
     ]
+    d_normed = own_dn + add_up([part[:local_rows] for part in messages])
     grad_tokens = d_hidden + norm_back(d_normed * attn_gain, unit_a, factor_a)
-    (ff_parts, d_normed), attn_parts = ordered((ff_parts, d_normed), attn_parts)
     grad_gate, grad_up, grad_down = call(
-        place_ffn_kernel, [(w_gate.shape, float32)] * 3, where, *ff_parts, scalars=1
+        place_ffn_kernel,
+        [(w_gate.shape, float32)] * 3,
+        where,
+        own_ff,
+        *messages,
+        scalars=1,
+        scratch=[pltpu.VMEM((PLANE, rows, ff_cols), float32)],
     )
     grad_query, grad_key, grad_value, grad_out_w, sums = call(
         place_attn_kernel,

time: 281 us -> 285 us (1.014)
  blocking collectives: 0 us -> 29.1 us
  waiting for transfers between devices: 110 us -> 96.2 us
  Pallas kernels: 79.4 us -> 72.4 us
  starting transfers between devices: 49.6 us -> 46.1 us
    all_gather x0 -> x1, blocking collectives: none -> 29.1 us  [body(): lax.all_gather(attn_piece, 'dp', axis=0, tiled=True, axis_index_groups=co...]
    ppermute x6 -> x3, waiting for transfers between devices: 18.1 us -> 0.01 us  [send_deep(): lax.ppermute(values, 'dp', [(i, (i + PLANE * step) % count) for i in rang...]
    pallas_call x6 -> x2, Pallas kernels: 42.3 us -> 26.1 us  [the longest x1 16 us: attn_back(): pl.pallas_call(attn_back_kernel, grid=(PLANE,), in_specs=[scalar, scalar,...]
    all_gather x1, waiting for transfers between devices: 10.3 us -> 0.01 us  [body(): lax.all_gather(ff_piece, 'dp', axis=0, tiled=True, axis_index_groups=colu...]
    pallas_call x7 -> x10, Pallas kernels: 16.7 us -> 25.8 us  [call(): pl.pallas_call(kernel, out_shape=[jax.ShapeDtypeStruct(shape, kind) for s...]
    ppermute x6 -> x3, starting transfers between devices: 12.1 us -> 4.14 us  [send_deep(): lax.ppermute(values, 'dp', [(i, (i + PLANE * step) % count) for i in rang...]
    reduce_scatter x0 -> x1, waiting for transfers between devices: none -> 6.36 us  [body(): lax.psum_scatter(attn_grad, 'dp', scatter_dimension=0, tiled=True, axis_i...]
    ppermute x30 -> x33, starting transfers between devices: 36.1 us -> 41.1 us  [send_plane(): return lax.ppermute(values, 'dp', [(i, i ^ mask) for i in range(count)])]
  transfers between devices with their start and end apart: 47 -> 48, of which waited for: 21 -> 24; matrix products, arithmetic and copies ran while one was open for 5% -> 5% of each run, Pallas kernels for 20% -> 16%
where the time goes in v6:
time: 285 us; the launch traced here: 284 us
  waiting for transfers between devices  96.2 us (34%)
  Pallas kernels  72.4 us (25%)
  starting transfers between devices  46.1 us (16%)
  blocking collectives  29.1 us (10%)
  between operations  14.2 us (5%)
  local copies, waits for them, and re-layouts  13.7 us (5%)
  other arithmetic  12.3 us (4%)
    ppermute x33, waiting for transfers between devices, send_plane(): return lax.ppermute(values, 'dp', [(i, i ^ mask) for i in range(count)])  76.3 us
    ppermute x33, starting transfers between devices, send_plane(): return lax.ppermute(values, 'dp', [(i, i ^ mask) for i in range(count)])  41.1 us
    all_gather x1, blocking collectives, body(): lax.all_gather(attn_piece, 'dp', axis=0, tiled=True, axis_index_groups=co...  29.1 us
    pallas_call x10, Pallas kernels, call(): pl.pallas_call(kernel, out_shape=[jax.ShapeDtypeStruct(shape, kind) for s...  25.8 us
    pallas_call x1, Pallas kernels, ffn(): pl.pallas_call(ffn_kernel, grid=(2,), in_specs=[scalar, scalar] + [row_sp...  20.5 us
    pallas_call x1, Pallas kernels, attn_back(): pl.pallas_call(attn_back_kernel, grid=(PLANE,), in_specs=[scalar, scalar,...  16 us
    unnamed x91, local copies, waits for them, and re-layouts  10.5 us
    pallas_call x1, Pallas kernels, attn(): pl.pallas_call(attn_kernel, grid=(PLANE,), in_specs=[scalar, scalar, bloc...  10.1 us
  transfers between devices with their start and end apart: 48, of which 24 were waited for; matrix products, arithmetic and copies ran while one was open for 5% of the time, Pallas kernels for 16%

profile of v6, /device:TPU:0, one launch (start us, length us, event | category | flops | bytes accessed | tf_op | source)
XLA Modules:
  0.0 283.9 jit_solution(14424775938985644023)
XLA Ops:
  7.2 3.0 %collective-permute-start.4 = (bf16[128,1024]{1,0:T(8,128)(2,1)}, bf16[128,1024]{1,0:T(8,128)(2,1)S(1)}, u32[]{:S(2)}, u32[]{:S(2)}) collective-permute-start(bf16[128,1024]{1,0:T(8,128)(2,1)} %param.14), channel_id=1, source_target_pairs={{0,4},{2,6},{4,0},{6,2},{8,12},{10,14},{12,8},{14,10},{16,20},{18,... | collective-permute-start | bytes 786440 | tf_op jit(solution)/shard_map/ppermute | solution.py:99
  10.3 1.5 collective-permute-start.3
  12.4 2.5 shard_map.237
  14.9 1.9 collective-permute-start
  16.9 1.5 collective-permute-start.1
  18.4 6.9 %collective-permute-done.one = bf16[32,1024]{1,0:T(8,128)(2,1)S(1)} collective-permute-done((bf16[32,1024]{1,0:T(8,128)(2,1)}, bf16[32,1024]{1,0:T(8,128)(2,1)S(1)}, u32[]{:S(2)}, u32[]{:S(2)}) %collective-permute-start) | collective-permute-done | bytes 65568 | tf_op jit(solution)/shard_map/ppermute | solution.py:99
  25.3 1.4 collective-permute-start.2
  26.7 3.9 %collective-permute-done.2.three = bf16[32,1024]{1,0:T(8,128)(2,1)S(1)} collective-permute-done((bf16[32,1024]{1,0:T(8,128)(2,1)}, bf16[32,1024]{1,0:T(8,128)(2,1)S(1)}, u32[]{:S(2)}, u32[]{:S(2)}) %collective-permute-start.2) | collective-permute-done | bytes 65568 | tf_op jit(solution)/shard_map/ppermute | solution.py:99
  31.3 1.7 shard_map.238
  33.0 1.6 collective-permute-start.7
  35.1 1.5 collective-permute-start.9
  36.6 5.2 %collective-permute-done.7.one = bf16[128,1024]{1,0:T(8,128)(2,1)S(1)} collective-permute-done((bf16[128,1024]{1,0:T(8,128)(2,1)}, bf16[128,1024]{1,0:T(8,128)(2,1)S(1)}, u32[]{:S(2)}, u32[]{:S(2)}) %collective-permute-start.7) | collective-permute-done | bytes 262176 | tf_op jit(solution)/shard_map/ppermute | solution.py:99
  41.8 4.0 %collective-permute-done.8.two = bf16[128,1024]{1,0:T(8,128)(2,1)S(1)} collective-permute-done((bf16[128,1024]{1,0:T(8,128)(2,1)}, bf16[128,1024]{1,0:T(8,128)(2,1)S(1)}, u32[]{:S(2)}, u32[]{:S(2)}) %collective-permute-start.8) | collective-permute-done | bytes 262176 | tf_op jit(solution)/shard_map/ppermute | solution.py:99
  47.2 2.4 shard_map.239
  51.5 29.1 %all_gather.6.weight = bf16[1024,384]{1,0:T(8,128)(2,1)} all-gather(bf16[256,384]{1,0:T(8,128)(2,1)S(1)} %copy-done.23), channel_id=1, replica_groups={{0,8,16,24},{2,10,18,26},{4,12,20,28},{6,14,22,30},{1,9,17,25},{3,11,19..., dimensions={0}, use_global_device_ids=true | all-gather | bytes 983040 | tf_op jit(solution)/shard_map/all_gather | solution.py:776
  81.3 2.8 collective-permute-start.10
  84.1 3.1 %fusion.6 = (f32[1024,128]{1,0:T(8,128)}, f32[1024,128]{1,0:T(8,128)}) fusion(f32[128]{0:T(128)S(1)} %get-tuple-element.175, f32[128]{0:T(128)S(1)} %get-tuple-element.176, f32[1024]{0:T(1024)S(1)} %bitcast.28), kind=kLoop, calls=%fused_computation.13 | loop fusion | flops 262144 | bytes 1053696 | tf_op jit(solution)/shard_map/mul | solution.py:810
  88.1 10.1 %shard_map.240 = (bf16[512,1024]{1,0:T(8,128)(2,1)}, f32[512,1024]{1,0:T(8,128)}, f32[1024,256]{1,0:T(8,128)}, bf16[1024,256]{1,0:T(8,128)(2,1)}, bf16[1024,128]{1,0:T(8,128)(2,1)}) custom-call(s32[3]{0:T(128)} %pad_add_fusion.where_ref, s32[4,4]{1,0:T(4,128)} %copy-done.31, bf16[512,1024]{1,0:T(8,128)(2,1)} %copy-done, bf16[512,1024]{1,0:T(8,128)(2,1)} %copy-done.1, ...), custom_call_target="tpu_custom_call" | custom-call | flops 1024 | bytes 36000000 | tf_op jit(solution)/shard_map/pallas_call | solution.py:409
  99.7 2.9 %collective-permute-done.13.received = bf16[512,1024]{1,0:T(8,128)(2,1)S(1)} collective-permute-done((bf16[512,1024]{1,0:T(8,128)(2,1)}, bf16[512,1024]{1,0:T(8,128)(2,1)S(1)}, u32[]{:S(2)}, u32[]{:S(2)}) %collective-permute-start.13) | collective-permute-done | bytes 1048608 | tf_op jit(solution)/shard_map/ppermute | solution.py:108
  103.5 2.9 %shard_map.241 = (f32[128,1024]{1,0:T(8,128)}, bf16[128,1024]{1,0:T(8,128)(2,1)}, bf16[128,1024]{1,0:T(8,128)(2,1)}, bf16[128,1024]{1,0:T(8,128)(2,1)}) custom-call(f32[512,1024]{1,0:T(8,128)} %get-tuple-element.106.keep, bf16[512,1024]{1,0:T(8,128)(2,1)} %copy-done.11), custom_call_target="tpu_custom_call" | custom-call | flops 1024 | bytes 1024 | tf_op jit(solution)/shard_map/pallas_call | solution.py:114
  107.1 2.9 %collective-permute-start.16 = (bf16[128,1024]{1,0:T(8,128)(2,1)}, bf16[128,1024]{1,0:T(8,128)(2,1)S(1)}, u32[]{:S(2)}, u32[]{:S(2)}) collective-permute-start(bf16[128,1024]{1,0:T(8,128)(2,1)} %get-tuple-element.113), channel_id=1, source_target_pairs={{0,6},{2,4},{4,2},{6,0},{8,14},{10,12},{12,10},{14,8},{16,22},{18,... | collective-permute-start | bytes 786440 | tf_op jit(solution)/shard_map/ppermute | solution.py:99
  110.1 5.8 %collective-permute-done.14 = bf16[128,1024]{1,0:T(8,128)(2,1)S(1)} collective-permute-done((bf16[128,1024]{1,0:T(8,128)(2,1)}, bf16[128,1024]{1,0:T(8,128)(2,1)S(1)}, u32[]{:S(2)}, u32[]{:S(2)}) %collective-permute-start.14) | collective-permute-done | bytes 262176 | tf_op jit(solution)/shard_map/ppermute | solution.py:99
  115.9 4.9 %collective-permute-done.15 = bf16[128,1024]{1,0:T(8,128)(2,1)S(1)} collective-permute-done((bf16[128,1024]{1,0:T(8,128)(2,1)}, bf16[128,1024]{1,0:T(8,128)(2,1)S(1)}, u32[]{:S(2)}, u32[]{:S(2)}) %collective-permute-start.15) | collective-permute-done | bytes 262176 | tf_op jit(solution)/shard_map/ppermute | solution.py:99
  120.8 1.3 multiply_reduce_fusion.2
  122.3 1.5 collective-permute-start.19
  123.7 1.7 collective-permute-start.18
  126.0 6.5 %collective-permute-done.19 = bf16[128,1024]{1,0:T(8,128)(2,1)S(1)} collective-permute-done((bf16[128,1024]{1,0:T(8,128)(2,1)S(1)}, bf16[128,1024]{1,0:T(8,128)(2,1)S(1)}, u32[]{:S(2)}, u32[]{:S(2)}) %collective-permute-start.19) | collective-permute-done | bytes 262176 | tf_op jit(solution)/shard_map/ppermute | solution.py:99
  132.5 3.4 %collective-permute-done.18 = bf16[128,1024]{1,0:T(8,128)(2,1)S(1)} collective-permute-done((bf16[128,1024]{1,0:T(8,128)(2,1)S(1)}, bf16[128,1024]{1,0:T(8,128)(2,1)S(1)}, u32[]{:S(2)}, u32[]{:S(2)}) %collective-permute-start.18) | collective-permute-done | bytes 262176 | tf_op jit(solution)/shard_map/ppermute | solution.py:99
  136.6 1.1 copy-done.10
  137.7 1.7 collective-permute-done.20.x_o
  139.4 20.5 %shard_map.242 = (bf16[512,1024]{1,0:T(8,128)(2,1)}, f32[512,1024]{1,0:T(8,128)}, bf16[512,1024]{1,0:T(8,128)(2,1)}, f32[512,1024]{1,0:T(8,128)}, bf16[1024,1792]{1,0:T(8,128)(2,1)}) custom-call(s32[3]{0:T(128)} %pad_add_fusion.where_ref, s32[4,4]{1,0:T(4,128)} %copy-done.31, bf16[512,1024]{1,0:T(8,128)(2,1)} %collective-permute-done.20.x_o, ...), custom_call_target="tpu_custom_call" | custom-call | flops 1024 | bytes 74000000 | tf_op jit(solution)/shard_map/pallas_call | solution.py:523
  161.2 2.5 collective-permute-done.22.received
  164.8 3.0 %shard_map.243 = (f32[128,1024]{1,0:T(8,128)}, bf16[128,1024]{1,0:T(8,128)(2,1)}, bf16[128,1024]{1,0:T(8,128)(2,1)}, bf16[128,1024]{1,0:T(8,128)(2,1)}) custom-call(f32[512,1024]{1,0:T(8,128)} %get-tuple-element.114.keep, bf16[512,1024]{1,0:T(8,128)(2,1)} %copy-done.12), custom_call_target="tpu_custom_call" | custom-call | flops 1024 | bytes 1024 | tf_op jit(solution)/shard_map/pallas_call | solution.py:114
  167.7 1.4 collective-permute-start.23
  169.7 1.5 collective-permute-start.25
  171.2 1.3 slice.28
  173.1 4.0 %collective-permute-done.23 = bf16[128,1024]{1,0:T(8,128)(2,1)S(1)} collective-permute-done((bf16[128,1024]{1,0:T(8,128)(2,1)}, bf16[128,1024]{1,0:T(8,128)(2,1)S(1)}, u32[]{:S(2)}, u32[]{:S(2)}) %collective-permute-start.23) | collective-permute-done | bytes 262176 | tf_op jit(solution)/shard_map/ppermute | solution.py:99
  177.1 5.9 %collective-permute-done.24 = bf16[128,1024]{1,0:T(8,128)(2,1)S(1)} collective-permute-done((bf16[128,1024]{1,0:T(8,128)(2,1)}, bf16[128,1024]{1,0:T(8,128)(2,1)S(1)}, u32[]{:S(2)}, u32[]{:S(2)}) %collective-permute-start.24) | collective-permute-done | bytes 262176 | tf_op jit(solution)/shard_map/ppermute | solution.py:99
  183.0 2.0 multiply_reduce_fusion
  185.2 1.6 collective-permute-start.28
  187.4 1.4 collective-permute-start.26
  188.8 6.7 %collective-permute-done.28 = bf16[128,1024]{1,0:T(8,128)(2,1)S(1)} collective-permute-done((bf16[128,1024]{1,0:T(8,128)(2,1)S(1)}, bf16[128,1024]{1,0:T(8,128)(2,1)S(1)}, u32[]{:S(2)}, u32[]{:S(2)}) %collective-permute-start.28) | collective-permute-done | bytes 262176 | tf_op jit(solution)/shard_map/ppermute | solution.py:99
  195.5 3.8 %collective-permute-done.27 = bf16[128,1024]{1,0:T(8,128)(2,1)S(1)} collective-permute-done((bf16[128,1024]{1,0:T(8,128)(2,1)S(1)}, bf16[128,1024]{1,0:T(8,128)(2,1)S(1)}, u32[]{:S(2)}, u32[]{:S(2)}) %collective-permute-start.27) | collective-permute-done | bytes 262176 | tf_op jit(solution)/shard_map/ppermute | solution.py:99
  199.5 3.2 %shard_map.244 = (f32[128,1024]{1,0:T(8,128)}, bf16[128,1024]{1,0:T(8,128)(2,1)}, bf16[128,1024]{1,0:T(8,128)(2,1)}, bf16[128,1024]{1,0:T(8,128)(2,1)}) custom-call(f32[512,1024]{1,0:T(8,128)} %get-tuple-element.121.keep, bf16[512,1024]{1,0:T(8,128)(2,1)} %collective-permute-done.30.received), custom_call_target="tpu_custom_call" | custom-call | flops 1024 | bytes 1024 | tf_op jit(solution)/shard_map/pallas_call | solution.py:114
  203.2 1.4 collective-permute-start.32
  204.6 1.6 collective-permute-start.33
  206.2 16.0 %shard_map.245 = (bf16[512,1024]{1,0:T(8,128)(2,1)}, f32[512,1024]{1,0:T(8,128)}, bf16[1024,384]{1,0:T(8,128)(2,1)}, f32[8,384]{1,0:T(8,128)}) custom-call(s32[3]{0:T(128)} %pad_add_fusion.where_ref, s32[4,4]{1,0:T(4,128)} %copy-done.31, bf16[512,1024]{1,0:T(8,128)(2,1)} %copy-done, bf16[512,1024]{1,0:T(8,128)(2,1)} %copy-done.1, f32[1,1024]{1,0:T(1,128)} %bitcast.26, ...), custom_call_target="tpu_custom_call" | custom-call | flops 1024 | bytes 58000000 | tf_op jit(solution)/shard_map/pallas_call | solution.py:433
  223.2 2.8 collective-permute-done.34.received
  226.0 3.5 %reduce-scatter.3.cloned.1.call-done.own_ff = bf16[256,1792]{1,0:T(8,128)(2,1)} async-done(((bf16[1024,1792]{1,0:T(8,128)(2,1)}), bf16[256,1792]{1,0:T(8,128)(2,1)}) %reduce-scatter.3.cloned.1.call-update) | async-done | bytes 917520 | tf_op jit(solution)/shard_map/reduce_scatter | solution.py:841
  229.5 3.8 %shard_map.246 = (f32[128,1024]{1,0:T(8,128)}, f32[64,1792]{1,0:T(8,128)}, bf16[256,1024]{1,0:T(8,128)(2,1)}, bf16[256,1024]{1,0:T(8,128)(2,1)}, bf16[256,1024]{1,0:T(8,128)(2,1)}) custom-call(s32[3]{0:T(128)} %pad_add_fusion.where_ref, f32[512,1024]{1,0:T(8,128)} %get-tuple-element.138.keep, bf16[512,1024]{1,0:T(8,128)(2,1)} %copy-done.14, ...), custom_call_target="tpu_custom_call" | custom-call | flops 1024 | bytes 1024 | tf_op jit(solution)/shard_map/pallas_call | solution.py:114
  233.3 1.5 collective-permute-start.35
  234.7 1.5 collective-permute-start.36
  236.8 2.5 collective-permute-start.40
  239.6 8.7 %collective-permute-done.35.one = bf16[256,1024]{1,0:T(8,128)(2,1)S(1)} collective-permute-done((bf16[256,1024]{1,0:T(8,128)(2,1)}, bf16[256,1024]{1,0:T(8,128)(2,1)S(1)}, u32[]{:S(2)}, u32[]{:S(2)}) %collective-permute-start.35) | collective-permute-done | bytes 524320 | tf_op jit(solution)/shard_map/ppermute | solution.py:99
  248.3 1.3 collective-permute-start.38
  249.6 6.4 %reduce-scatter.5.cloned.1.call-done.own = bf16[256,384]{1,0:T(8,128)(2,1)} async-done(((bf16[1024,384]{1,0:T(8,128)(2,1)}), bf16[256,384]{1,0:T(8,128)(2,1)}) %reduce-scatter.5.cloned.1.call-update) | async-done | bytes 196624 | tf_op jit(solution)/shard_map/reduce_scatter | solution.py:854
  256.0 3.4 %collective-permute-done.36.two = bf16[256,1024]{1,0:T(8,128)(2,1)S(1)} collective-permute-done((bf16[256,1024]{1,0:T(8,128)(2,1)}, bf16[256,1024]{1,0:T(8,128)(2,1)S(1)}, u32[]{:S(2)}, u32[]{:S(2)}) %collective-permute-start.36) | collective-permute-done | bytes 524320 | tf_op jit(solution)/shard_map/ppermute | solution.py:99
  260.7 1.7 shard_map.247
  262.4 1.2 collective-permute-start.41
  264.5 1.5 collective-permute-start.43
  265.9 1.3 fusion.2
  268.0 1.8 collective-permute-done.43.three
  270.4 1.7 shard_map.248
  273.2 2.9 %shard_map.249 = (f32[64,2304]{1,0:T(8,128)}, f32[64,2304]{1,0:T(8,128)}, f32[64,2304]{1,0:T(8,128)}) custom-call(s32[3]{0:T(128)} %pad_add_fusion.where_ref, f32[64,1792]{1,0:T(8,128)} %get-tuple-element.157.own, bf16[256,1024]{1,0:T(8,128)(2,1)} %copy-done.5, bf16[256,1024]{1,0:T(8,128)(2,1)} %copy-done.6, bf16[256,1024]{1,0:T(8,128)(2,1)} %copy-done.7), custom_call_target="tpu_custom_call" | custom-call | flops 1024 | bytes 1024 | tf_op jit(solution)/shard_map/pallas_call | solution.py:114
  (169 shorter events, 23.9 us)
Async XLA Ops:
  7.2 132.2 %all-gather.2.cloned.1.call-start = ((), (), s32[]{:S(2)}) async-start(), calls=%async_computation.2 | async-start | bytes 4587520 | tf_op jit(solution)/shard_map/all_gather | solution.py:793
  7.2 25.8 %collective-permute-start.4 = (bf16[128,1024]{1,0:T(8,128)(2,1)}, bf16[128,1024]{1,0:T(8,128)(2,1)S(1)}, u32[]{:S(2)}, u32[]{:S(2)}) collective-permute-start(bf16[128,1024]{1,0:T(8,128)(2,1)} %param.14), channel_id=1, source_target_pairs={{0,4},{2,6},{4,0},{6,2},{8,12},{10,14},{12,8},{14,10},{16,20},{18,... | collective-permute-start | bytes 786440 | tf_op jit(solution)/shard_map/ppermute | solution.py:99
  10.3 22.7 %collective-permute-start.3 = (bf16[128,1024]{1,0:T(8,128)(2,1)}, bf16[128,1024]{1,0:T(8,128)(2,1)S(1)}, u32[]{:S(2)}, u32[]{:S(2)}) collective-permute-start(bf16[128,1024]{1,0:T(8,128)(2,1)} %param.14), channel_id=1, source_target_pairs={{0,2},{2,0},{4,6},{6,4},{8,10},{10,8},{12,14},{14,12},{16,18},{18,... | collective-permute-start | bytes 786440 | tf_op jit(solution)/shard_map/ppermute | solution.py:99
  11.7 21.2 %collective-permute-start.5 = (bf16[128,1024]{1,0:T(8,128)(2,1)}, bf16[128,1024]{1,0:T(8,128)(2,1)S(1)}, u32[]{:S(2)}, u32[]{:S(2)}) collective-permute-start(bf16[128,1024]{1,0:T(8,128)(2,1)} %param.14), channel_id=1, source_target_pairs={{0,6},{2,4},{4,2},{6,0},{8,14},{10,12},{12,10},{14,8},{16,22},{18,... | collective-permute-start | bytes 786440 | tf_op jit(solution)/shard_map/ppermute | solution.py:99
  12.4 37.2 %copy-start.38 = (f32[64]{0:T(128)S(1)}, f32[64]{0:T(128)}, u32[]{:S(2)}) copy-start(f32[64]{0:T(128)} %param.17) | copy-start | bytes 772
  12.4 37.3 %copy-start.39 = (f32[64]{0:T(128)S(1)}, f32[64]{0:T(128)}, u32[]{:S(2)}) copy-start(f32[64]{0:T(128)} %param.18) | copy-start | bytes 772
  12.4 38.6 %copy-start.4 = (bf16[128,1024]{1,0:T(8,128)(2,1)S(1)}, bf16[128,1024]{1,0:T(8,128)(2,1)}, u32[]{:S(2)}) copy-start(bf16[128,1024]{1,0:T(8,128)(2,1)} %param.14) | copy-start | bytes 786436
  14.9 10.4 %collective-permute-start = (bf16[32,1024]{1,0:T(8,128)(2,1)}, bf16[32,1024]{1,0:T(8,128)(2,1)S(1)}, u32[]{:S(2)}, u32[]{:S(2)}) collective-permute-start(bf16[32,1024]{1,0:T(8,128)(2,1)} %get-tuple-element.88), channel_id=1, source_target_pairs={{0,2},{2,0},{4,6},{6,4},{8,10},{10,8},{12,14},{14,12},{16,18},{18,... | collective-permute-start | bytes 196616 | tf_op jit(solution)/shard_map/ppermute | solution.py:99
  16.9 9.9 %collective-permute-start.1 = (bf16[32,1024]{1,0:T(8,128)(2,1)}, bf16[32,1024]{1,0:T(8,128)(2,1)S(1)}, u32[]{:S(2)}, u32[]{:S(2)}) collective-permute-start(bf16[32,1024]{1,0:T(8,128)(2,1)} %get-tuple-element.89), channel_id=1, source_target_pairs={{0,4},{2,6},{4,0},{6,2},{8,12},{10,14},{12,8},{14,10},{16,20},{18,... | collective-permute-start | bytes 196616 | tf_op jit(solution)/shard_map/ppermute | solution.py:99
  25.3 5.4 %collective-permute-start.2 = (bf16[32,1024]{1,0:T(8,128)(2,1)}, bf16[32,1024]{1,0:T(8,128)(2,1)S(1)}, u32[]{:S(2)}, u32[]{:S(2)}) collective-permute-start(bf16[32,1024]{1,0:T(8,128)(2,1)} %get-tuple-element.90), channel_id=1, source_target_pairs={{0,6},{2,4},{4,2},{6,0},{8,14},{10,12},{12,10},{14,8},{16,22},{18,... | collective-permute-start | bytes 196616 | tf_op jit(solution)/shard_map/ppermute | solution.py:99
  33.0 18.5 %copy-start.23 = (bf16[256,384]{1,0:T(8,128)(2,1)S(1)}, bf16[256,384]{1,0:T(8,128)(2,1)}, u32[]{:S(2)}) copy-start(bf16[256,384]{1,0:T(8,128)(2,1)} %get-tuple-element.92) | copy-start | bytes 589828
  33.0 8.8 %collective-permute-start.7 = (bf16[128,1024]{1,0:T(8,128)(2,1)}, bf16[128,1024]{1,0:T(8,128)(2,1)S(1)}, u32[]{:S(2)}, u32[]{:S(2)}) collective-permute-start(bf16[128,1024]{1,0:T(8,128)(2,1)} %get-tuple-element.102), channel_id=1, source_target_pairs={{0,2},{2,0},{4,6},{6,4},{8,10},{10,8},{12,14},{14,12},{16,18},{18,... | collective-permute-start | bytes 786440 | tf_op jit(solution)/shard_map/ppermute | solution.py:99
  34.6 11.3 %collective-permute-start.8 = (bf16[128,1024]{1,0:T(8,128)(2,1)}, bf16[128,1024]{1,0:T(8,128)(2,1)S(1)}, u32[]{:S(2)}, u32[]{:S(2)}) collective-permute-start(bf16[128,1024]{1,0:T(8,128)(2,1)} %get-tuple-element.103), channel_id=1, source_target_pairs={{0,4},{2,6},{4,0},{6,2},{8,12},{10,14},{12,8},{14,10},{16,20},{18,... | collective-permute-start | bytes 786440 | tf_op jit(solution)/shard_map/ppermute | solution.py:99
  35.1 10.8 %collective-permute-start.9 = (bf16[128,1024]{1,0:T(8,128)(2,1)}, bf16[128,1024]{1,0:T(8,128)(2,1)S(1)}, u32[]{:S(2)}, u32[]{:S(2)}) collective-permute-start(bf16[128,1024]{1,0:T(8,128)(2,1)} %get-tuple-element.104), channel_id=1, source_target_pairs={{0,6},{2,4},{4,2},{6,0},{8,14},{10,12},{12,10},{14,8},{16,22},{18,... | collective-permute-start | bytes 786440 | tf_op jit(solution)/shard_map/ppermute | solution.py:99
  49.6 31.0 %copy-start.13 = (bf16[128,1024]{1,0:T(8,128)(2,1)S(1)}, bf16[128,1024]{1,0:T(8,128)(2,1)}, u32[]{:S(2)}) copy-start(bf16[128,1024]{1,0:T(8,128)(2,1)} %param.27) | copy-start | bytes 786436
  49.6 179.9 %reduce-scatter.3.cloned.1.call-start = ((), (), s32[]{:S(2)}) async-start(), calls=%async_computation.3 | async-start | bytes 4587520 | tf_op jit(solution)/shard_map/reduce_scatter | solution.py:841
  51.1 36.0 %copy-start = (bf16[512,1024]{1,0:T(8,128)(2,1)}, bf16[512,1024]{1,0:T(8,128)(2,1)S(1)}, u32[]{:S(2)}) copy-start(bf16[512,1024]{1,0:T(8,128)(2,1)S(1)} %constant_dynamic-update-slice_fusion.tok_m) | copy-start | bytes 3145732
  51.1 36.0 %collective-permute-start.6 = (bf16[512,1024]{1,0:T(8,128)(2,1)S(1)}, bf16[512,1024]{1,0:T(8,128)(2,1)S(1)}, u32[]{:S(2)}, u32[]{:S(2)}) collective-permute-start(bf16[512,1024]{1,0:T(8,128)(2,1)S(1)} %constant_dynamic-update-slice_fusion.tok_m), channel_id=1, source_target_pairs={{0,1},{1,0},{2,3},{3,2},{4,5},{5,4},{6,7},{7,6},{8,9},{9,8},{10,11... | collective-permute-start | bytes 3145736 | tf_op jit(solution)/shard_map/ppermute | solution.py:108
  51.4 35.8 %copy-start.31 = (s32[4,4]{1,0:T(4,128)}, s32[4,4]{1,0:T(4,128)S(1)}, u32[]{:S(2)}) copy-start(s32[4,4]{1,0:T(4,128)S(1)} %reduce_window_sum.11.ends_ref) | copy-start | bytes 196
  80.6 17.7 %collective-permute-start.12 = (bf16[128,1024]{1,0:T(8,128)(2,1)S(1)}, bf16[128,1024]{1,0:T(8,128)(2,1)S(1)}, u32[]{:S(2)}, u32[]{:S(2)}) collective-permute-start(bf16[128,1024]{1,0:T(8,128)(2,1)S(1)} %copy-done.13), channel_id=1, source_target_pairs={{0,6},{2,4},{4,2},{6,0},{8,14},{10,12},{12,10},{14,8},{16,22},{18,... | collective-permute-start | bytes 786440 | tf_op jit(solution)/shard_map/ppermute | solution.py:99
  80.6 17.7 %collective-permute-start.11 = (bf16[128,1024]{1,0:T(8,128)(2,1)S(1)}, bf16[128,1024]{1,0:T(8,128)(2,1)S(1)}, u32[]{:S(2)}, u32[]{:S(2)}) collective-permute-start(bf16[128,1024]{1,0:T(8,128)(2,1)S(1)} %copy-done.13), channel_id=1, source_target_pairs={{0,4},{2,6},{4,0},{6,2},{8,12},{10,14},{12,8},{14,10},{16,20},{18,... | collective-permute-start | bytes 786440 | tf_op jit(solution)/shard_map/ppermute | solution.py:99
  81.3 17.0 %collective-permute-start.10 = (bf16[128,1024]{1,0:T(8,128)(2,1)S(1)}, bf16[128,1024]{1,0:T(8,128)(2,1)S(1)}, u32[]{:S(2)}, u32[]{:S(2)}) collective-permute-start(bf16[128,1024]{1,0:T(8,128)(2,1)S(1)} %copy-done.13), channel_id=1, source_target_pairs={{0,2},{2,0},{4,6},{6,4},{8,10},{10,8},{12,14},{14,12},{16,18},{18,... | collective-permute-start | bytes 786440 | tf_op jit(solution)/shard_map/ppermute | solution.py:99
  99.7 2.9 %collective-permute-start.13 = (bf16[512,1024]{1,0:T(8,128)(2,1)}, bf16[512,1024]{1,0:T(8,128)(2,1)S(1)}, u32[]{:S(2)}, u32[]{:S(2)}) collective-permute-start(bf16[512,1024]{1,0:T(8,128)(2,1)} %get-tuple-element.109), channel_id=1, source_target_pairs={{0,1},{1,0},{2,3},{3,2},{4,5},{5,4},{6,7},{7,6},{8,9},{9,8},{10,11... | collective-permute-start | bytes 3145736 | tf_op jit(solution)/shard_map/ppermute | solution.py:108
  106.5 15.7 %copy-start.32 = (f32[1024]{0:T(1024)S(1)}, f32[1024]{0:T(1024)}, u32[]{:S(2)}) copy-start(f32[1024]{0:T(1024)} %param.19) | copy-start | bytes 12292
  106.5 19.3 %copy-start.22 = (bf16[128,1024]{1,0:T(8,128)(2,1)S(1)}, bf16[128,1024]{1,0:T(8,128)(2,1)}, u32[]{:S(2)}) copy-start(bf16[128,1024]{1,0:T(8,128)(2,1)} %copy-done.21) | copy-start | bytes 786436
  106.5 19.4 %copy-start.20 = (bf16[128,1024]{1,0:T(8,128)(2,1)S(1)}, bf16[128,1024]{1,0:T(8,128)(2,1)}, u32[]{:S(2)}) copy-start(bf16[128,1024]{1,0:T(8,128)(2,1)} %copy-done.19) | copy-start | bytes 786436
  106.5 9.4 %collective-permute-start.14 = (bf16[128,1024]{1,0:T(8,128)(2,1)}, bf16[128,1024]{1,0:T(8,128)(2,1)S(1)}, u32[]{:S(2)}, u32[]{:S(2)}) collective-permute-start(bf16[128,1024]{1,0:T(8,128)(2,1)} %get-tuple-element.111), channel_id=1, source_target_pairs={{0,2},{2,0},{4,6},{6,4},{8,10},{10,8},{12,14},{14,12},{16,18},{18,... | collective-permute-start | bytes 786440 | tf_op jit(solution)/shard_map/ppermute | solution.py:99
  106.6 14.2 %collective-permute-start.15 = (bf16[128,1024]{1,0:T(8,128)(2,1)}, bf16[128,1024]{1,0:T(8,128)(2,1)S(1)}, u32[]{:S(2)}, u32[]{:S(2)}) collective-permute-start(bf16[128,1024]{1,0:T(8,128)(2,1)} %get-tuple-element.112), channel_id=1, source_target_pairs={{0,4},{2,6},{4,0},{6,2},{8,12},{10,14},{12,8},{14,10},{16,20},{18,... | collective-permute-start | bytes 786440 | tf_op jit(solution)/shard_map/ppermute | solution.py:99
  107.1 13.7 %collective-permute-start.16 = (bf16[128,1024]{1,0:T(8,128)(2,1)}, bf16[128,1024]{1,0:T(8,128)(2,1)S(1)}, u32[]{:S(2)}, u32[]{:S(2)}) collective-permute-start(bf16[128,1024]{1,0:T(8,128)(2,1)} %get-tuple-element.113), channel_id=1, source_target_pairs={{0,6},{2,4},{4,2},{6,0},{8,14},{10,12},{12,10},{14,8},{16,22},{18,... | collective-permute-start | bytes 786440 | tf_op jit(solution)/shard_map/ppermute | solution.py:99
  122.3 10.3 %collective-permute-start.19 = (bf16[128,1024]{1,0:T(8,128)(2,1)S(1)}, bf16[128,1024]{1,0:T(8,128)(2,1)S(1)}, u32[]{:S(2)}, u32[]{:S(2)}) collective-permute-start(bf16[128,1024]{1,0:T(8,128)(2,1)S(1)} %multiply_convert_fusion), channel_id=1, source_target_pairs={{0,6},{2,4},{4,2},{6,0},{8,14},{10,12},{12,10},{14,8},{16,22},{18,... | collective-permute-start | bytes 786440 | tf_op jit(solution)/shard_map/ppermute | solution.py:99
  123.7 12.2 %collective-permute-start.18 = (bf16[128,1024]{1,0:T(8,128)(2,1)S(1)}, bf16[128,1024]{1,0:T(8,128)(2,1)S(1)}, u32[]{:S(2)}, u32[]{:S(2)}) collective-permute-start(bf16[128,1024]{1,0:T(8,128)(2,1)S(1)} %multiply_convert_fusion), channel_id=1, source_target_pairs={{0,4},{2,6},{4,0},{6,2},{8,12},{10,14},{12,8},{14,10},{16,20},{18,... | collective-permute-start | bytes 786440 | tf_op jit(solution)/shard_map/ppermute | solution.py:99
  125.5 11.0 %collective-permute-start.17 = (bf16[128,1024]{1,0:T(8,128)(2,1)S(1)}, bf16[128,1024]{1,0:T(8,128)(2,1)S(1)}, u32[]{:S(2)}, u32[]{:S(2)}) collective-permute-start(bf16[128,1024]{1,0:T(8,128)(2,1)S(1)} %multiply_convert_fusion), channel_id=1, source_target_pairs={{0,2},{2,0},{4,6},{6,4},{8,10},{10,8},{12,14},{14,12},{16,18},{18,... | collective-permute-start | bytes 786440 | tf_op jit(solution)/shard_map/ppermute | solution.py:99
  125.9 10.7 %collective-permute-start.21 = (bf16[512,1024]{1,0:T(8,128)(2,1)S(1)}, bf16[512,1024]{1,0:T(8,128)(2,1)S(1)}, u32[]{:S(2)}, u32[]{:S(2)}) collective-permute-start(bf16[512,1024]{1,0:T(8,128)(2,1)S(1)} %constant_dynamic-update-slice_fusion.4.g_m), channel_id=1, source_target_pairs={{0,1},{1,0},{2,3},{3,2},{4,5},{5,4},{6,7},{7,6},{8,9},{9,8},{10,11... | collective-permute-start | bytes 3145736 | tf_op jit(solution)/shard_map/ppermute | solution.py:108
  136.5 2.9 %collective-permute-start.20 = (bf16[512,1024]{1,0:T(8,128)(2,1)S(1)}, bf16[512,1024]{1,0:T(8,128)(2,1)}, u32[]{:S(2)}, u32[]{:S(2)}) collective-permute-start(bf16[512,1024]{1,0:T(8,128)(2,1)S(1)} %pad_maximum_fusion.x_m), channel_id=1, source_target_pairs={{0,1},{1,0},{2,3},{3,2},{4,5},{5,4},{6,7},{7,6},{8,9},{9,8},{10,11... | collective-permute-start | bytes 3145736 | tf_op jit(solution)/shard_map/ppermute | solution.py:108
  159.9 96.1 %reduce-scatter.5.cloned.1.call-start = ((), (), s32[]{:S(2)}) async-start(), calls=%async_computation.4 | async-start | bytes 983040 | tf_op jit(solution)/shard_map/reduce_scatter | solution.py:854
  161.1 2.7 collective-permute-start.22
  167.7 9.4 %collective-permute-start.23 = (bf16[128,1024]{1,0:T(8,128)(2,1)}, bf16[128,1024]{1,0:T(8,128)(2,1)S(1)}, u32[]{:S(2)}, u32[]{:S(2)}) collective-permute-start(bf16[128,1024]{1,0:T(8,128)(2,1)} %get-tuple-element.117), channel_id=1, source_target_pairs={{0,2},{2,0},{4,6},{6,4},{8,10},{10,8},{12,14},{14,12},{16,18},{18,... | collective-permute-start | bytes 786440 | tf_op jit(solution)/shard_map/ppermute | solution.py:99
  169.1 13.9 %collective-permute-start.24 = (bf16[128,1024]{1,0:T(8,128)(2,1)}, bf16[128,1024]{1,0:T(8,128)(2,1)S(1)}, u32[]{:S(2)}, u32[]{:S(2)}) collective-permute-start(bf16[128,1024]{1,0:T(8,128)(2,1)} %get-tuple-element.118), channel_id=1, source_target_pairs={{0,4},{2,6},{4,0},{6,2},{8,12},{10,14},{12,8},{14,10},{16,20},{18,... | collective-permute-start | bytes 786440 | tf_op jit(solution)/shard_map/ppermute | solution.py:99
  169.7 13.3 %collective-permute-start.25 = (bf16[128,1024]{1,0:T(8,128)(2,1)}, bf16[128,1024]{1,0:T(8,128)(2,1)S(1)}, u32[]{:S(2)}, u32[]{:S(2)}) collective-permute-start(bf16[128,1024]{1,0:T(8,128)(2,1)} %get-tuple-element.119), channel_id=1, source_target_pairs={{0,6},{2,4},{4,2},{6,0},{8,14},{10,12},{12,10},{14,8},{16,22},{18,... | collective-permute-start | bytes 786440 | tf_op jit(solution)/shard_map/ppermute | solution.py:99
  185.2 10.2 %collective-permute-start.28 = (bf16[128,1024]{1,0:T(8,128)(2,1)S(1)}, bf16[128,1024]{1,0:T(8,128)(2,1)S(1)}, u32[]{:S(2)}, u32[]{:S(2)}) collective-permute-start(bf16[128,1024]{1,0:T(8,128)(2,1)S(1)} %get-tuple-element.163), channel_id=1, source_target_pairs={{0,6},{2,4},{4,2},{6,0},{8,14},{10,12},{12,10},{14,8},{16,22},{18,... | collective-permute-start | bytes 786440 | tf_op jit(solution)/shard_map/ppermute | solution.py:99
  186.8 12.4 %collective-permute-start.27 = (bf16[128,1024]{1,0:T(8,128)(2,1)S(1)}, bf16[128,1024]{1,0:T(8,128)(2,1)S(1)}, u32[]{:S(2)}, u32[]{:S(2)}) collective-permute-start(bf16[128,1024]{1,0:T(8,128)(2,1)S(1)} %get-tuple-element.163), channel_id=1, source_target_pairs={{0,4},{2,6},{4,0},{6,2},{8,12},{10,14},{12,8},{14,10},{16,20},{18,... | collective-permute-start | bytes 786440 | tf_op jit(solution)/shard_map/ppermute | solution.py:99
  187.4 11.8 %collective-permute-start.26 = (bf16[128,1024]{1,0:T(8,128)(2,1)S(1)}, bf16[128,1024]{1,0:T(8,128)(2,1)S(1)}, u32[]{:S(2)}, u32[]{:S(2)}) collective-permute-start(bf16[128,1024]{1,0:T(8,128)(2,1)S(1)} %get-tuple-element.163), channel_id=1, source_target_pairs={{0,2},{2,0},{4,6},{6,4},{8,10},{10,8},{12,14},{14,12},{16,18},{18,... | collective-permute-start | bytes 786440 | tf_op jit(solution)/shard_map/ppermute | solution.py:99
  188.8 10.7 %collective-permute-start.30 = (bf16[512,1024]{1,0:T(8,128)(2,1)S(1)}, bf16[512,1024]{1,0:T(8,128)(2,1)}, u32[]{:S(2)}, u32[]{:S(2)}) collective-permute-start(bf16[512,1024]{1,0:T(8,128)(2,1)S(1)} %copy-done.40), channel_id=1, source_target_pairs={{0,1},{1,0},{2,3},{3,2},{4,5},{5,4},{6,7},{7,6},{8,9},{9,8},{10,11... | collective-permute-start | bytes 3145736 | tf_op jit(solution)/shard_map/ppermute | solution.py:108
  199.3 3.4 %collective-permute-start.29 = (bf16[512,1024]{1,0:T(8,128)(2,1)S(1)}, bf16[512,1024]{1,0:T(8,128)(2,1)}, u32[]{:S(2)}, u32[]{:S(2)}) collective-permute-start(bf16[512,1024]{1,0:T(8,128)(2,1)S(1)} %pad_maximum_fusion.1.dh_m), channel_id=1, source_target_pairs={{0,1},{1,0},{2,3},{3,2},{4,5},{5,4},{6,7},{7,6},{8,9},{9,8},{10,11... | collective-permute-start | bytes 3145736 | tf_op jit(solution)/shard_map/ppermute | solution.py:108
  202.7 19.5 %collective-permute-start.31 = (bf16[128,1024]{1,0:T(8,128)(2,1)}, bf16[128,1024]{1,0:T(8,128)(2,1)S(1)}, u32[]{:S(2)}, u32[]{:S(2)}) collective-permute-start(bf16[128,1024]{1,0:T(8,128)(2,1)} %get-tuple-element.128), channel_id=1, source_target_pairs={{0,2},{2,0},{4,6},{6,4},{8,10},{10,8},{12,14},{14,12},{16,18},{18,... | collective-permute-start | bytes 786440 | tf_op jit(solution)/shard_map/ppermute | solution.py:99
  203.2 19.1 %collective-permute-start.32 = (bf16[128,1024]{1,0:T(8,128)(2,1)}, bf16[128,1024]{1,0:T(8,128)(2,1)S(1)}, u32[]{:S(2)}, u32[]{:S(2)}) collective-permute-start(bf16[128,1024]{1,0:T(8,128)(2,1)} %get-tuple-element.129), channel_id=1, source_target_pairs={{0,4},{2,6},{4,0},{6,2},{8,12},{10,14},{12,8},{14,10},{16,20},{18,... | collective-permute-start | bytes 786440 | tf_op jit(solution)/shard_map/ppermute | solution.py:99
  204.6 17.7 %collective-permute-start.33 = (bf16[128,1024]{1,0:T(8,128)(2,1)}, bf16[128,1024]{1,0:T(8,128)(2,1)S(1)}, u32[]{:S(2)}, u32[]{:S(2)}) collective-permute-start(bf16[128,1024]{1,0:T(8,128)(2,1)} %get-tuple-element.130), channel_id=1, source_target_pairs={{0,6},{2,4},{4,2},{6,0},{8,14},{10,12},{12,10},{14,8},{16,22},{18,... | collective-permute-start | bytes 786440 | tf_op jit(solution)/shard_map/ppermute | solution.py:99
  206.2 16.1 %copy-start.15 = (f32[128,1024]{1,0:T(8,128)S(1)}, f32[128,1024]{1,0:T(8,128)}, u32[]{:S(2)}) copy-start(f32[128,1024]{1,0:T(8,128)} %get-tuple-element.127) | copy-start | bytes 1572868
  223.1 2.9 %collective-permute-start.34 = (bf16[512,1024]{1,0:T(8,128)(2,1)}, bf16[512,1024]{1,0:T(8,128)(2,1)S(1)}, u32[]{:S(2)}, u32[]{:S(2)}) collective-permute-start(bf16[512,1024]{1,0:T(8,128)(2,1)} %get-tuple-element.139), channel_id=1, source_target_pairs={{0,1},{1,0},{2,3},{3,2},{4,5},{5,4},{6,7},{7,6},{8,9},{9,8},{10,11... | collective-permute-start | bytes 3145736 | tf_op jit(solution)/shard_map/ppermute | solution.py:108
  223.2 42.7 %copy-start.24 = (f32[1024]{0:T(1024)S(1)}, f32[1024]{0:T(1024)}, u32[]{:S(2)}) copy-start(f32[1024]{0:T(1024)} %param.16) | copy-start | bytes 12292
  233.3 38.9 %copy-start.8 = (f32[128,1024]{1,0:T(8,128)S(1)}, f32[128,1024]{1,0:T(8,128)}, u32[]{:S(2)}) copy-start(f32[128,1024]{1,0:T(8,128)} %get-tuple-element.141) | copy-start | bytes 1572868
  233.3 15.0 %collective-permute-start.35 = (bf16[256,1024]{1,0:T(8,128)(2,1)}, bf16[256,1024]{1,0:T(8,128)(2,1)S(1)}, u32[]{:S(2)}, u32[]{:S(2)}) collective-permute-start(bf16[256,1024]{1,0:T(8,128)(2,1)} %get-tuple-element.142), channel_id=1, source_target_pairs={{0,2},{2,0},{4,6},{6,4},{8,10},{10,8},{12,14},{14,12},{16,18},{18,... | collective-permute-start | bytes 1572872 | tf_op jit(solution)/shard_map/ppermute | solution.py:99
  234.7 24.7 %collective-permute-start.36 = (bf16[256,1024]{1,0:T(8,128)(2,1)}, bf16[256,1024]{1,0:T(8,128)(2,1)S(1)}, u32[]{:S(2)}, u32[]{:S(2)}) collective-permute-start(bf16[256,1024]{1,0:T(8,128)(2,1)} %get-tuple-element.143), channel_id=1, source_target_pairs={{0,4},{2,6},{4,0},{6,2},{8,12},{10,14},{12,8},{14,10},{16,20},{18,... | collective-permute-start | bytes 1572872 | tf_op jit(solution)/shard_map/ppermute | solution.py:99
  236.2 23.2 %collective-permute-start.37 = (bf16[256,1024]{1,0:T(8,128)(2,1)}, bf16[256,1024]{1,0:T(8,128)(2,1)S(1)}, u32[]{:S(2)}, u32[]{:S(2)}) collective-permute-start(bf16[256,1024]{1,0:T(8,128)(2,1)} %get-tuple-element.144), channel_id=1, source_target_pairs={{0,6},{2,4},{4,2},{6,0},{8,14},{10,12},{12,10},{14,8},{16,22},{18,... | collective-permute-start | bytes 1572872 | tf_op jit(solution)/shard_map/ppermute | solution.py:99
  236.8 22.7 %collective-permute-start.40 = (f32[8,384]{1,0:T(8,128)S(1)}, f32[8,384]{1,0:T(8,128)S(1)}, u32[]{:S(2)}, u32[]{:S(2)}) collective-permute-start(f32[8,384]{1,0:T(8,128)S(1)} %copy-done.34), channel_id=1, source_target_pairs={{0,24},{2,26},{4,28},{6,30},{8,0},{10,2},{12,4},{14,6},{16,8},{18,... | collective-permute-start | bytes 36872 | tf_op jit(solution)/shard_map/ppermute | solution.py:104
  239.2 20.2 %collective-permute-start.39 = (f32[8,384]{1,0:T(8,128)S(1)}, f32[8,384]{1,0:T(8,128)S(1)}, u32[]{:S(2)}, u32[]{:S(2)}) collective-permute-start(f32[8,384]{1,0:T(8,128)S(1)} %copy-done.34), channel_id=1, source_target_pairs={{0,16},{2,18},{4,20},{6,22},{8,24},{10,26},{12,28},{14,30},{16,0},... | collective-permute-start | bytes 36872 | tf_op jit(solution)/shard_map/ppermute | solution.py:104
  248.3 24.9 %copy-start.5 = (bf16[256,1024]{1,0:T(8,128)(2,1)}, bf16[256,1024]{1,0:T(8,128)(2,1)S(1)}, u32[]{:S(2)}) copy-start(bf16[256,1024]{1,0:T(8,128)(2,1)S(1)} %collective-permute-done.35.one) | copy-start | bytes 1572868
  248.3 11.2 %collective-permute-start.38 = (f32[8,384]{1,0:T(8,128)S(1)}, f32[8,384]{1,0:T(8,128)S(1)}, u32[]{:S(2)}, u32[]{:S(2)}) collective-permute-start(f32[8,384]{1,0:T(8,128)S(1)} %copy-done.34), channel_id=1, source_target_pairs={{0,8},{2,10},{4,12},{6,14},{8,16},{10,18},{12,20},{14,22},{16,24},... | collective-permute-start | bytes 36872 | tf_op jit(solution)/shard_map/ppermute | solution.py:104
  259.4 13.8 %copy-start.6 = (bf16[256,1024]{1,0:T(8,128)(2,1)}, bf16[256,1024]{1,0:T(8,128)(2,1)S(1)}, u32[]{:S(2)}) copy-start(bf16[256,1024]{1,0:T(8,128)(2,1)S(1)} %collective-permute-done.36.two) | copy-start | bytes 1572868
  259.4 13.8 %copy-start.7 = (bf16[256,1024]{1,0:T(8,128)(2,1)}, bf16[256,1024]{1,0:T(8,128)(2,1)S(1)}, u32[]{:S(2)}) copy-start(bf16[256,1024]{1,0:T(8,128)(2,1)S(1)} %collective-permute-done.37.three) | copy-start | bytes 1572868
  262.4 5.0 %collective-permute-start.41 = (bf16[80,384]{1,0:T(8,128)(2,1)}, bf16[80,384]{1,0:T(8,128)(2,1)S(1)}, u32[]{:S(2)}, u32[]{:S(2)}) collective-permute-start(bf16[80,384]{1,0:T(8,128)(2,1)} %get-tuple-element.149), channel_id=1, source_target_pairs={{0,2},{2,0},{4,6},{6,4},{8,10},{10,8},{12,14},{14,12},{16,18},{18,... | collective-permute-start | bytes 184328 | tf_op jit(solution)/shard_map/ppermute | solution.py:99
  263.6 4.4 %collective-permute-start.42 = (bf16[80,384]{1,0:T(8,128)(2,1)}, bf16[80,384]{1,0:T(8,128)(2,1)S(1)}, u32[]{:S(2)}, u32[]{:S(2)}) collective-permute-start(bf16[80,384]{1,0:T(8,128)(2,1)} %get-tuple-element.150), channel_id=1, source_target_pairs={{0,4},{2,6},{4,0},{6,2},{8,12},{10,14},{12,8},{14,10},{16,20},{18,... | collective-permute-start | bytes 184328 | tf_op jit(solution)/shard_map/ppermute | solution.py:99
  264.5 5.3 %collective-permute-start.43 = (bf16[80,384]{1,0:T(8,128)(2,1)}, bf16[80,384]{1,0:T(8,128)(2,1)S(1)}, u32[]{:S(2)}, u32[]{:S(2)}) collective-permute-start(bf16[80,384]{1,0:T(8,128)(2,1)} %get-tuple-element.151), channel_id=1, source_target_pairs={{0,6},{2,4},{4,2},{6,0},{8,14},{10,12},{12,10},{14,8},{16,22},{18,... | collective-permute-start | bytes 184328 | tf_op jit(solution)/shard_map/ppermute | solution.py:99
  272.2 4.0 %collective-permute-start.44 = (f32[8,384]{1,0:T(8,128)}, f32[8,384]{1,0:T(8,128)S(1)}, u32[]{:S(2)}, u32[]{:S(2)}) collective-permute-start(f32[8,384]{1,0:T(8,128)} %get-tuple-element.152), channel_id=1, source_target_pairs={{0,1},{1,0},{2,3},{3,2},{4,5},{5,4},{6,7},{7,6},{8,9},{9,8},{10,11... | collective-permute-start | bytes 36872 | tf_op jit(solution)/shard_map/ppermute | solution.py:108
  (26 other events, 78.9 us)
Sparse Core Ops, SparseCore 0:
  49.7 79.8 all-gather.1
  160.0 69.4 reduce-scatter.2
  231.8 24.1 reduce-scatter.4

commit v7 on v6

--- a/solution.py
+++ b/solution.py
@@ -151,17 +151,13 @@
     return (2, rows // 2) if rows % 32 == 0 else (1, max(rows, 16))
 
 
-def pack_kernel(where_ref, lengths_ref, w_q, w_k, w_v, w_o, w_g, w_u, w_d, *outs):
+def pack_attn_kernel(where_ref, lengths_ref, w_q, w_k, w_v, w_o, *outs):
     rows = w_q.shape[0]
     parts, high = attn_rows(rows)
-    tall = max(rows, 16)
-    big = w_g.shape[1] // LANES // PLANE * LANES
-    last = w_g.shape[1] // LANES // PLANE * PLANE
     place = where_ref[0]
     lane = lane_ids((rows, LANES))
-    for mask in range(PLANE):
+    for mask, out in enumerate(outs):
         other = place ^ mask
-        out, second = outs[mask], outs[PLANE + mask]
         at = pl.multiple_of(other * LANES, LANES)
         tile = jnp.where(
             lane < HALF, half_tile(w_k, 0, other, False), half_tile(w_v, 0, other, True)
@@ -181,22 +177,30 @@
             marks = jnp.where(ids == free - LANES + slot, lengths_ref[0, slot].astype(float32), marks)
         out[:, parts * width :] = marks.astype(bfloat16)
 
-        at = pl.multiple_of(other * big, LANES)
-        small = jnp.where(
-            lane < HALF, half_tile(w_g, last, other, False), half_tile(w_u, last, other, True)
-        )
-        small_down = jnp.where(lane < HALF, half_tile(w_d, last, other, False), 0.0)
-        upper = jnp.concatenate(
-            [w_g[:, pl.ds(at, big)].astype(float32), w_u[:, pl.ds(at, big)].astype(float32)], axis=1
-        )
-        lower = jnp.concatenate(
-            [w_d[:, pl.ds(at, big)].astype(float32), small, small_down], axis=1
-        )
-        second[:tall, :] = padded(upper, tall).astype(bfloat16)
-        second[tall:, : lower.shape[1]] = padded(lower, tall).astype(bfloat16)
-        second[tall:, lower.shape[1] :] = jnp.zeros(
-            (tall, second.shape[1] - lower.shape[1]), bfloat16
-        )
+
+def pack_ffn_kernel(where_ref, w_g, w_u, w_d, *outs):
+    rows = w_g.shape[0]
+    big = w_g.shape[1] // LANES // PLANE * LANES
+    half = big // 2
+    last = w_g.shape[1] // LANES // PLANE * PLANE
+    place = where_ref[0]
+    lane = lane_ids((rows, LANES))
+    for mask, out in enumerate(outs):
+        other = place ^ mask
+        parts = []
+        for number in range(2):
+            at = pl.ds(pl.multiple_of(other * big + number * half, LANES), half)
+            parts += [w[:, at].astype(float32) for w in (w_g, w_u, w_d)]
+            if number == 0:
+                parts.append(
+                    jnp.where(
+                        lane < HALF,
+                        half_tile(w_g, last, other, False),
+                        half_tile(w_u, last, other, True),
+                    )
+                )
+                parts.append(jnp.where(lane < HALF, half_tile(w_d, last, other, False), 0.0))
+        out[...] = padded(jnp.concatenate(parts, axis=1), out.shape[0]).astype(bfloat16)
 
 
 def unpack_attn_kernel(where_ref, own, one, two, three, attn_out, lens_out, held):
@@ -215,16 +219,15 @@
     attn_out[...] = held[...].astype(bfloat16)
 
 
-def unpack_ffn_kernel(where_ref, own, one, two, three, ffn_out, held):
-    rows = ffn_out.shape[0] // PLANE
-    tall = max(rows, 16)
+def unpack_ffn_kernel(where_ref, own, one, two, three, first_out, second_out, held):
+    rows = first_out.shape[0] // PLANE
     place = where_ref[0]
     for mask, message in enumerate((own, one, two, three)):
         at = pl.ds(pl.multiple_of((place ^ mask) * rows, rows), rows)
-        full = message.shape[1]
-        held[at, :full] = message[:tall, :].astype(float32)[:rows]
-        held[at, full:] = message[tall:, : held.shape[1] - full].astype(float32)[:rows]
-    ffn_out[...] = held[...].astype(bfloat16)
+        held[at, :] = message[...].astype(float32)[:rows]
+    width = first_out.shape[1]
+    first_out[...] = held[:, :width].astype(bfloat16)
+    second_out[...] = held[:, width:].astype(bfloat16)
 
 
 def head_mean(values):
@@ -276,11 +279,17 @@
     return pl.ds(pl.multiple_of(at, rows), rows)
 
 
-def attn_kernel(where_ref, ends_ref, tok_m, tok_o, a_gain, q_gain, k_gain, cos, sin, weight, *refs):
-    send, keep, pre_out, low_out, mixed_out, held = refs
+def attn_kernel(layers, where_ref, ends_ref, tok_m, tok_o, a_gain, q_gain, k_gain, cos, sin, *refs):
+    pieces, refs = refs[:layers], refs[layers:]
+    send, keep, pre_out, low_out, mixed_out, weight, held = refs
     group = pl.program_id(0)
-    core = where_ref[2]
+    depth, core = where_ref[1], where_ref[2]
     local = tok_m.shape[0]
+
+    @pl.when(group == 0)
+    def _():
+        for step, piece in enumerate(pieces):
+            weight[deep_rows(depth, -step, layers, piece.shape[0]), :] = piece[...]
 
     x = group_rows(core, tok_m[...].astype(float32), tok_o[...].astype(float32))
     normed = (x * inverse_rms(x) * a_gain[...]).astype(bfloat16)
@@ -313,12 +322,14 @@
 
 
 def attn_back_kernel(
-    where_ref, ends_ref, tok_m, tok_o, a_gain, q_gain, k_gain, cos, sin, dh_m, dh_o,
+    layers, where_ref, ends_ref, tok_m, tok_o, a_gain, q_gain, k_gain, cos, sin, dh_m, dh_o,
     pre_ref, low_ref, mixed_ref, weight, gain_ffn, *refs,
 ):
-    send, keep, grad_out, gains_out, held, total, sum_a, sum_qk = refs
+    send, keep, own, gains_out = refs[:4]
+    pieces = refs[4 : 3 + layers]
+    held, total, sum_a, sum_qk = refs[3 + layers :]
     group = pl.program_id(0)
-    core = where_ref[2]
+    depth, core = where_ref[1], where_ref[2]
     local = tok_m.shape[0]
 
     @pl.when(group == 0)
@@ -385,7 +396,15 @@
         qk_sum = jnp.where(lane_ids(q_sum.shape) < HALF, q_sum, k_sum)
         ids = lax.broadcasted_iota(jnp.int32, (GAIN_ROWS, LANES), 0)
         gains_out[:, 2 * LANES :] = jnp.where(ids == 0, qk_sum, 0.0)
-        grad_out[...] = total[...].astype(bfloat16)
+        gains = gains_out[...]
+        top = gains.astype(bfloat16)
+        rest = (gains - top.astype(float32)).astype(bfloat16)
+        tail = jnp.concatenate([top.astype(float32), rest.astype(float32)], axis=0).astype(bfloat16)
+        rows = own.shape[0]
+        own[...] = total[deep_rows(depth, 0, layers, rows), :]
+        for index, piece in enumerate(pieces):
+            piece[:rows, :] = total[deep_rows(depth, index + 1, layers, rows), :].astype(bfloat16)
+            piece[rows:, :] = tail
 
 
 def attn_specs(rows, width, group_height):
@@ -402,46 +421,53 @@
     return pl.BlockSpec(shape, lambda i: (0, 0), pipeline_mode=pl.Buffered(1))
 
 
-def attn(where, ends, tok_mine, tok_other, gains, tables, weight):
+def attn(where, ends, tok_mine, tok_other, gains, tables, pieces):
+    layers = len(pieces)
     rows, width = tok_mine.shape
     local = rows // PLANE
     scalar, block, gain, small, table, wide = attn_specs(local, width, 2 * local)
+    high, columns = pieces[0].shape
+    weight = (layers * high, columns)
     return pl.pallas_call(
-        attn_kernel,
+        lambda *refs: attn_kernel(layers, *refs),
         grid=(PLANE,),
         in_specs=[scalar, scalar, block, block, gain, small, small, table, table]
-        + [whole_spec(weight.shape)],
-        out_specs=[block, block, wide, wide, table],
+        + [whole_spec((high, columns))] * layers,
+        out_specs=[block, block, wide, wide, table, whole_spec(weight)],
         out_shape=[
             jax.ShapeDtypeStruct((rows, width), bfloat16),
             jax.ShapeDtypeStruct((rows, width), float32),
             jax.ShapeDtypeStruct((2 * rows, 2 * LANES), float32),
             jax.ShapeDtypeStruct((2 * rows, 2 * LANES), bfloat16),
             jax.ShapeDtypeStruct((2 * rows, LANES), bfloat16),
+            jax.ShapeDtypeStruct(weight, bfloat16),
         ],
         scratch_shapes=[pltpu.VMEM((2 * local, width), float32)],
         compiler_params=pltpu.CompilerParams(vmem_limit_bytes=VMEM_BYTES),
         cost_estimate=cost(36),
-    )(where, ends, tok_mine, tok_other, *gains, *tables, weight)
-
-
-def attn_back(where, ends, tok_mine, tok_other, gains, tables, dh, saved, weight, gain_ffn):
+    )(where, ends, tok_mine, tok_other, *gains, *tables, *pieces)
+
+
+def attn_back(where, ends, layers, tok_mine, tok_other, gains, tables, dh, saved, weight, gain_ffn):
     rows, width = tok_mine.shape
     local = rows // PLANE
     scalar, block, gain, small, table, wide = attn_specs(local, width, 2 * local)
-    columns = weight.shape[1]
+    high, columns = weight.shape[0] // layers, weight.shape[1]
+    tail = 2 * GAIN_ROWS
     return pl.pallas_call(
-        attn_back_kernel,
+        lambda *refs: attn_back_kernel(layers, *refs),
         grid=(PLANE,),
         in_specs=[scalar, scalar, block, block, gain, small, small, table, table, block, block]
         + [wide, wide, table, whole_spec(weight.shape), gain],
-        out_specs=[block, block, whole_spec(weight.shape), whole_spec((GAIN_ROWS, columns))],
+        out_specs=[block, block, whole_spec((high, columns)), whole_spec((GAIN_ROWS, columns))]
+        + [whole_spec((high + tail, columns))] * (layers - 1),
         out_shape=[
             jax.ShapeDtypeStruct((rows, width), bfloat16),
             jax.ShapeDtypeStruct((rows, width), float32),
-            jax.ShapeDtypeStruct(weight.shape, bfloat16),
+            jax.ShapeDtypeStruct((high, columns), float32),
             jax.ShapeDtypeStruct((GAIN_ROWS, columns), float32),
-        ],
+        ]
+        + [jax.ShapeDtypeStruct((high + tail, columns), bfloat16)] * (layers - 1),
         scratch_shapes=[
             pltpu.VMEM((2 * local, width), float32),
             pltpu.VMEM(weight.shape, float32),
@@ -449,82 +475,145 @@
             pltpu.VMEM((8, LANES), float32),
         ],
         compiler_params=pltpu.CompilerParams(vmem_limit_bytes=VMEM_BYTES),
-        cost_estimate=cost(58),
+        cost_estimate=cost(24),
     )(where, ends, tok_mine, tok_other, *gains, *tables, *dh, *saved, weight, gain_ffn)
 
 
-def ffn_kernel(where_ref, ends_ref, x_o, x_m, g_o, g_m, weight, *refs):
-    out_send, out_keep, dn_send, dn_keep, grad_out, total = refs
-    step = pl.program_id(0)
-    core = where_ref[2]
-    both = x_o.shape[1]
-    big = both // 2
-    local = x_o.shape[0] // 2
-
-    @pl.when(step == 0)
+def live_rows(ends_ref, values, step, core):
+    local = values.shape[0] // 2
+    parts = []
+    for k in range(2):
+        part = values[k * local : (k + 1) * local, :]
+        ids = lax.broadcasted_iota(jnp.int32, part.shape, 0) + core * local
+        end = ends_ref[2 * step + k, ends_ref.shape[1] - 1]
+        parts.append(jnp.where(ids < end, part, jnp.zeros_like(part)))
+    return parts
+
+
+def swiglu(gate, up, d_act):
+    sigma = 1.0 / (1.0 + jnp.exp(-gate))
+    silu = gate * sigma
+    d_gate = d_act * up * sigma * (1.0 + gate * (1.0 - sigma))
+    return silu * up, d_gate, d_act * silu
+
+
+def ffn_rows(where_ref, ends_ref, x_o, x_m, g_o, g_m):
+    step, core = pl.program_id(0), where_ref[2]
+    x = jnp.concatenate([x_o[...], x_m[...]], axis=0)
+    grads = live_rows(ends_ref, g_o[...], step, 1 - core) + live_rows(ends_ref, g_m[...], step, core)
+    return x, jnp.concatenate(grads, axis=0)
+
+
+def half_layer(x, grads, weight, total):
+    half = x.shape[1] // 4
+    pre = matmul(x, weight[:, : 2 * half])
+    act, d_gate, d_up = swiglu(
+        pre[:, :half], pre[:, half:], matmul(grads, weight[:, 2 * half : 3 * half])
+    )
+    act = act.astype(bfloat16)
+    d_both = jnp.concatenate([d_gate, d_up], axis=1).astype(bfloat16)
+    total[:, : 2 * half] += matmul_tn(x, d_both)
+    total[:, 2 * half : 3 * half] += matmul_tn(grads, act)
+    return act, d_both
+
+
+def ffn_first_kernel(
+    where_ref, ends_ref, x_o, x_m, g_o, g_m, weight, act_out, d_out, grad_out, total
+):
+    @pl.when(pl.program_id(0) == 0)
     def _():
         total[...] = jnp.zeros_like(total)
 
-    def live_rows(values, group, at_core):
-        ids = lax.broadcasted_iota(jnp.int32, values.shape, 0) + at_core * local
-        return jnp.where(ids < ends_ref[group, ends_ref.shape[1] - 1], values, jnp.zeros_like(values))
-
-    x = jnp.concatenate([x_o[...], x_m[...]], axis=0)
-    grads = jnp.concatenate(
-        [live_rows(g_o[k * local : (k + 1) * local, :], 2 * step + k, 1 - core) for k in range(2)]
-        + [live_rows(g_m[k * local : (k + 1) * local, :], 2 * step + k, core) for k in range(2)],
-        axis=0,
-    )
-    half = 2 * local
-    w_both = weight[:, :both]
-    w_down = weight[:, both : both + big]
-    w_small = weight[:, both + big : both + big + LANES]
-    w_small_down = weight[:, both + big + LANES :]
-    lane = lane_ids((x.shape[0], LANES))
-
-    def parts_of(gate, up, d_act):
-        sigma = 1.0 / (1.0 + jnp.exp(-gate))
-        silu = gate * sigma
-        act = silu * up
-        d_gate = d_act * up * sigma * (1.0 + gate * (1.0 - sigma))
-        return act, d_gate, d_act * silu
-
-    pre = matmul(x, w_both)
-    act, d_gate, d_up = parts_of(pre[:, :big], pre[:, big:], matmul(grads, w_down))
-    pre = matmul(x, w_small)
-    act_s, d_gate_s, d_up_s = parts_of(
-        pre, pltpu.roll(pre, HALF, 1), matmul(grads, w_small_down)
-    )
-    act_s = jnp.where(lane < HALF, act_s, 0.0).astype(bfloat16)
-    d_small = jnp.where(lane < HALF, d_gate_s, pltpu.roll(d_up_s, HALF, 1)).astype(bfloat16)
-    act = act.astype(bfloat16)
-    d_both = jnp.concatenate([d_gate, d_up], axis=1).astype(bfloat16)
-
-    partial = matmul_nt(act, w_down) + matmul_nt(act_s, w_small_down)
-    out_send[...] = partial[:half].astype(bfloat16)
-    out_keep[...] = partial[half:]
-    partial = matmul_nt(d_both, w_both) + matmul_nt(d_small, w_small)
-    dn_send[...] = partial[:half].astype(bfloat16)
-    dn_keep[...] = partial[half:]
-    total[:, :both] += matmul_tn(x, d_both)
-    total[:, both : both + big] += matmul_tn(grads, act)
-    total[:, both + big : both + big + LANES] += matmul_tn(x, d_small)
-    total[:, both + big + LANES :] += matmul_tn(grads, act_s)
-
-    @pl.when(step == pl.num_programs(0) - 1)
+    x, grads = ffn_rows(where_ref, ends_ref, x_o, x_m, g_o, g_m)
+    half = x.shape[1] // 4
+    act, d_both = half_layer(x, grads, weight, total)
+    act_out[:, :half] = act
+    d_out[:, : 2 * half] = d_both
+    pre = matmul(x, weight[:, 3 * half : 3 * half + LANES])
+    d_act = matmul(grads, weight[:, 3 * half + LANES :])
+    act, d_gate, d_up = swiglu(pre, pltpu.roll(pre, HALF, 1), d_act)
+    lane = lane_ids(pre.shape)
+    act = jnp.where(lane < HALF, act, 0.0).astype(bfloat16)
+    d_both = jnp.where(lane < HALF, d_gate, pltpu.roll(d_up, HALF, 1)).astype(bfloat16)
+    total[:, 3 * half : 3 * half + LANES] += matmul_tn(x, d_both)
+    total[:, 3 * half + LANES :] += matmul_tn(grads, act)
+    act_out[:, half:] = act
+    d_out[:, 2 * half :] = d_both
+
+    @pl.when(pl.program_id(0) == pl.num_programs(0) - 1)
     def _():
         grad_out[...] = total[...].astype(bfloat16)
 
 
-def ffn(where, ends, x_mine, x_other, g_mine, g_other, weight):
+def ffn_second_kernel(
+    where_ref, ends_ref, x_o, x_m, g_o, g_m, weight, first_weight, first_act, first_d,
+    out_send, out_keep, dn_send, dn_keep, grad_out, total,
+):
+    @pl.when(pl.program_id(0) == 0)
+    def _():
+        total[...] = jnp.zeros_like(total)
+
+    x, grads = ffn_rows(where_ref, ends_ref, x_o, x_m, g_o, g_m)
+    half = x.shape[1] // 4
+    act, d_both = half_layer(x, grads, weight, total)
+    height = x.shape[0] // 2
+    partial = (
+        matmul_nt(d_both, weight[:, : 2 * half])
+        + matmul_nt(first_d[:, : 2 * half], first_weight[:, : 2 * half])
+        + matmul_nt(first_d[:, 2 * half :], first_weight[:, 3 * half : 3 * half + LANES])
+    )
+    dn_send[...] = partial[:height].astype(bfloat16)
+    dn_keep[...] = partial[height:]
+    partial = (
+        matmul_nt(act, weight[:, 2 * half :])
+        + matmul_nt(first_act[:, :half], first_weight[:, 2 * half : 3 * half])
+        + matmul_nt(first_act[:, half:], first_weight[:, 3 * half + LANES :])
+    )
+    out_send[...] = partial[:height].astype(bfloat16)
+    out_keep[...] = partial[height:]
+
+    @pl.when(pl.program_id(0) == pl.num_programs(0) - 1)
+    def _():
+        grad_out[...] = total[...].astype(bfloat16)
+
+
+def ffn_specs(rows, width):
+    scalar = pl.BlockSpec(memory_space=pltpu.SMEM)
+    block = pl.BlockSpec((rows // 2, width), lambda i: (i, 0))
+    act = pl.BlockSpec((rows, width // 4 + LANES), lambda i: (i, 0))
+    d_both = pl.BlockSpec((rows, width // 2 + LANES), lambda i: (i, 0))
+    return scalar, block, act, d_both
+
+
+def ffn_first(where, ends, x_mine, x_other, g_mine, g_other, weight):
     rows, width = x_mine.shape
-    row_spec = pl.BlockSpec((rows // 2, width), lambda i: (i, 0))
-    scalar = pl.BlockSpec(memory_space=pltpu.SMEM)
+    scalar, block, act, d_both = ffn_specs(rows, width)
     return pl.pallas_call(
-        ffn_kernel,
+        ffn_first_kernel,
         grid=(2,),
-        in_specs=[scalar, scalar] + [row_spec] * 4 + [whole_spec(weight.shape)],
-        out_specs=[row_spec] * 4 + [whole_spec(weight.shape)],
+        in_specs=[scalar, scalar] + [block] * 4 + [whole_spec(weight.shape)],
+        out_specs=[act, d_both, whole_spec(weight.shape)],
+        out_shape=[
+            jax.ShapeDtypeStruct((2 * rows, width // 4 + LANES), bfloat16),
+            jax.ShapeDtypeStruct((2 * rows, width // 2 + LANES), bfloat16),
+            jax.ShapeDtypeStruct(weight.shape, bfloat16),
+        ],
+        scratch_shapes=[pltpu.VMEM(weight.shape, float32)],
+        compiler_params=pltpu.CompilerParams(vmem_limit_bytes=VMEM_BYTES),
+        cost_estimate=cost(25),
+    )(where, ends, x_other, x_mine, g_other, g_mine, weight)
+
+
+def ffn_second(where, ends, x_mine, x_other, g_mine, g_other, weight, first_weight, saved):
+    rows, width = x_mine.shape
+    scalar, block, act, d_both = ffn_specs(rows, width)
+    return pl.pallas_call(
+        ffn_second_kernel,
+        grid=(2,),
+        in_specs=[scalar, scalar]
+        + [block] * 4
+        + [whole_spec(weight.shape), whole_spec(first_weight.shape), act, d_both],
+        out_specs=[block] * 4 + [whole_spec(weight.shape)],
         out_shape=[
             jax.ShapeDtypeStruct((rows, width), bfloat16),
             jax.ShapeDtypeStruct((rows, width), float32),
@@ -534,8 +623,8 @@
         ],
         scratch_shapes=[pltpu.VMEM(weight.shape, float32)],
         compiler_params=pltpu.CompilerParams(vmem_limit_bytes=VMEM_BYTES),
-        cost_estimate=cost(74),
-    )(where, ends, x_other, x_mine, g_other, g_mine, weight)
+        cost_estimate=cost(50),
+    )(where, ends, x_other, x_mine, g_other, g_mine, weight, first_weight, *saved)
 
 
 def chip_sum_kernel(keep, received, *outs):
@@ -564,9 +653,7 @@
     held[...] = own_ff[...].astype(float32)
     place = where_ref[0]
     local = own.shape[0]
-    rows = ff_out.shape[0]
-    tall = (messages[0].shape[0] - local) // 2
-    width = own.shape[1]
+    rows, columns = ff_out.shape
     for mask in range(PLANE):
         span = slice(mask * local, (mask + 1) * local)
         value = keep[span, :] + received[span, :].astype(float32)
@@ -576,18 +663,18 @@
             ff_out[...] = grads
             continue
         out = messages[mask - 1]
+        tall = out.shape[0] - local
         out[:local, :] = value.astype(bfloat16)
-        out[local : local + tall, :] = padded(grads[:, :width], tall).astype(bfloat16)
-        rest = grads.shape[1] - width
-        out[local + tall :, :rest] = padded(grads[:, width:], tall).astype(bfloat16)
-        out[local + tall :, rest:] = jnp.zeros((tall, width - rest), bfloat16)
+        out[local:, :columns] = padded(grads, tall).astype(bfloat16)
+        if columns < out.shape[1]:
+            out[local:, columns:] = jnp.zeros((tall, out.shape[1] - columns), bfloat16)
 
 
 def tail_messages(where, keep, received, own_ff):
     local, width = keep.shape[0] // PLANE, keep.shape[1]
     rows, columns = own_ff.shape[0] // PLANE, own_ff.shape[1]
-    message = (local + 2 * max(rows, 16), width)
-    return call(
+    message = (local + max(rows, 16), width)
+    own, ff_out, *messages = call(
         tail_kernel,
         [((local, width), float32), ((rows, columns), float32)]
         + [(message, bfloat16)] * (PLANE - 1),
@@ -598,6 +685,7 @@
         scalars=1,
         scratch=[pltpu.VMEM(own_ff.shape, float32)],
     )
+    return own, ff_out, messages
 
 
 def joined_gains(tail):
@@ -610,22 +698,29 @@
     return jnp.concatenate([top, rest], axis=0)
 
 
-def split_attn_kernel(where_ref, own, gains, *refs):
+def plane_sum_attn_kernel(where_ref, own, gains, *refs):
     received, outs = refs[: -PLANE - 2], refs[-PLANE - 2 : -2]
     held, held_gains = refs[-2:]
     layers = len(received) + 1
+    value = own[...]
+    high = own.shape[0]
     depth = where_ref[1]
-    for step, part in enumerate((gains,) + received):
-        held_gains[deep_rows(depth, -step, layers, GAIN_ROWS), :] = part[...]
-    held[...] = own[...].astype(float32)
+    held_gains[deep_rows(depth, 0, layers, GAIN_ROWS), :] = joined_gains(split_gains(gains[...]))
+    for step, part in enumerate(received):
+        value = value + part[:high, :].astype(float32)
+        held_gains[deep_rows(depth, -1 - step, layers, GAIN_ROWS), :] = joined_gains(
+            part[high:, :].astype(float32)
+        )
+    held[...] = value
     sums = held_gains[:GAIN_ROWS, :]
     for layer in range(1, layers):
         sums = sums + held_gains[layer * GAIN_ROWS : (layer + 1) * GAIN_ROWS, :]
     tail = split_gains(sums)
     place = where_ref[0]
-    rows = own.shape[0] // PLANE
+    rows = high // PLANE
     for mask, out in enumerate(outs):
-        part = held[pl.ds(pl.multiple_of((place ^ mask) * rows, rows), rows), :]
+        at = pl.multiple_of((place ^ mask) * rows, rows)
+        part = held[pl.ds(at, rows), :]
         if mask:
             tall = out.shape[0] - tail.shape[0]
             out[:tall, :] = padded(part, tall).astype(bfloat16)
@@ -635,7 +730,7 @@
             out[rows:, :] = tail
 
 
-def split_attn(where, own, gains, received):
+def plane_split_attn(where, own, received, gains):
     rows, columns = own.shape[0] // PLANE, own.shape[1]
     tail = 2 * GAIN_ROWS
     shapes = [((rows + tail, columns), float32)]
@@ -644,7 +739,9 @@
         pltpu.VMEM(own.shape, float32),
         pltpu.VMEM(((len(received) + 1) * GAIN_ROWS, columns), float32),
     ]
-    return call(split_attn_kernel, shapes, where, own, gains, *received, scalars=1, scratch=scratch)
+    return call(
+        plane_sum_attn_kernel, shapes, where, own, gains, *received, scalars=1, scratch=scratch
+    )
 
 
 def pick_place(refs, place, target, columns, rows):
@@ -654,28 +751,25 @@
     return value
 
 
-def place_ffn_kernel(where_ref, own, one, two, three, out_g, out_u, out_d, held):
+def place_ffn_kernel(where_ref, *refs):
+    firsts, seconds, (out_g, out_u, out_d, held) = refs[:PLANE], refs[PLANE : 2 * PLANE], refs[2 * PLANE :]
     place = where_ref[0]
     rows = out_g.shape[0]
     big = out_g.shape[1] // LANES // PLANE * LANES
+    half = big // 2
     last = PLANE * big
-    width = one.shape[1]
     tall = max(rows, 16)
-    start = one.shape[0] - 2 * tall
-    for mask, ref in enumerate((own, one, two, three)):
-        if mask:
-            top = ref[start : start + tall, :].astype(float32)[:rows]
-            rest = ref[start + tall :, : held.shape[2] - width].astype(float32)[:rows]
-            held[mask, :, :width] = top
-            held[mask, :, width:] = rest
-        else:
-            held[mask] = ref[...]
-        at = pl.ds(pl.multiple_of((place ^ mask) * big, LANES), big)
-        for number, out in enumerate((out_g, out_u, out_d)):
-            out[:, at] = held[mask, :, number * big : (number + 1) * big]
+    for mask in range(PLANE):
+        start = firsts[mask].shape[0] - tall if mask else 0
+        parts = [ref[start:, :].astype(float32)[:rows] for ref in (firsts[mask], seconds[mask])]
+        for part, values in enumerate(parts):
+            at = pl.ds(pl.multiple_of((place ^ mask) * big + part * half, LANES), half)
+            for number, out in enumerate((out_g, out_u, out_d)):
+                out[:, at] = values[:, number * half : (number + 1) * half]
+        held[mask] = parts[0][:, 3 * half :]
     for pair in range(PLANE // 2):
-        low = held[place ^ (2 * pair), :, 3 * big :]
-        high = held[place ^ (2 * pair + 1), :, 3 * big :]
+        low = held[place ^ (2 * pair)]
+        high = held[place ^ (2 * pair + 1)]
         lane = lane_ids((rows, LANES))
         span = slice(last + pair * LANES, last + (pair + 1) * LANES)
         gu_low, gu_high = low[:, :LANES], high[:, :LANES]
@@ -749,51 +843,60 @@
     parts, high = attn_rows(rows)
     tall = max(rows, 16)
     first = call(
-        pack_kernel,
-        [((high, model), bfloat16)] * PLANE + [((2 * tall, model), bfloat16)] * PLANE,
+        pack_attn_kernel,
+        [((high, model), bfloat16)] * PLANE,
         where,
         lengths,
         w_query,
         w_key,
         w_value,
         w_out,
+        scalars=2,
+    )
+    second = call(
+        pack_ffn_kernel,
+        [((tall, ff_cols), bfloat16)] * PLANE,
+        where,
         w_gate,
         w_up,
         w_down,
-        scalars=2,
-    )
-    first, second = first[:PLANE], first[PLANE:]
+        scalars=1,
+    )
+    first = [first[0]] + [send_plane(first[m], m) for m in range(1, PLANE)]
     attn_piece, lens = call(
         unpack_attn_kernel,
         [((PLANE * rows, attn_cols), bfloat16), ((PLANE * 8, LANES), float32)],
         where,
-        first[0],
-        *[send_plane(first[m], m) for m in range(1, PLANE)],
+        *first,
         scalars=1,
         scratch=[pltpu.VMEM((PLANE * rows, attn_cols), float32)],
     )
-    columns = [list(range(k, layers * PLANE, PLANE)) for k in range(PLANE)]
-    attn_weight = lax.all_gather(
-        attn_piece, "dp", axis=0, tiled=True, axis_index_groups=columns
-    )
-    tok_parts = plane_parts(tokens)
-    tok_parts = after(attn_piece, tok_parts)
-    second = after(tok_parts, second)
-    tok_mine, tok_other = both_cores(tok_parts)
+    attn_pieces = [attn_piece] + [send_deep(attn_piece, step) for step in range(1, layers)]
+    second = after(first, second)
     second = [second[0]] + [send_plane(second[m], m) for m in range(1, PLANE)]
-    cotangent_sent = after(second, cotangent)
-    (ff_piece,) = call(
+    second = after(attn_pieces, second)
+    ff_first_cols = ff_cols - 3 * model // 4
+    ff_pieces = call(
         unpack_ffn_kernel,
-        [((PLANE * rows, ff_cols), bfloat16)],
+        [
+            ((PLANE * rows, ff_first_cols), bfloat16),
+            ((PLANE * rows, ff_cols - ff_first_cols), bfloat16),
+        ],
         where,
         *second,
         scalars=1,
         scratch=[pltpu.VMEM((PLANE * rows, ff_cols), float32)],
     )
-    ff_weight = lax.all_gather(ff_piece, "dp", axis=0, tiled=True, axis_index_groups=columns)
-    cot_parts = plane_parts(cotangent_sent)
+    columns = [list(range(k, layers * PLANE, PLANE)) for k in range(PLANE)]
+    ff_weights = [
+        lax.all_gather(piece, "dp", axis=0, tiled=True, axis_index_groups=columns)
+        for piece in ff_pieces
+    ]
+    attn_pieces = after(ff_pieces, attn_pieces)
+    tok_parts = plane_parts(tokens)
+    cot_parts = plane_parts(after(second, cotangent))
+    tok_mine, tok_other = both_cores(tok_parts)
     cot_mine, cot_other = both_cores(cot_parts)
-    attn_weight = after(ff_piece, attn_weight)
 
     slots = lengths.shape[1]
     all_lengths = lens.reshape(PLANE, 8, LANES)[:, 0, :slots].astype(jnp.int32)
@@ -817,15 +920,25 @@
     inputs = tokens.astype(jnp.float32)
     factor_a = inverse_rms(inputs)
     unit_a = inputs * factor_a
-    send, keep, *saved = attn(where, ends, tok_mine, tok_other, gains, tables, attn_weight)
+    send, keep, *saved, attn_weight = attn(
+        where, ends, tok_mine, tok_other, gains, tables, attn_pieces
+    )
     send = after(cot_parts, send)
     hidden = inputs + plane_total(chip_sum(keep, swap_cores(send)))
     factor_b = inverse_rms(hidden)
     unit_b = hidden * factor_b
     x_mine, x_other = gather_rows((unit_b * ffn_gain).astype(jnp.bfloat16))
 
-    out_send, out_keep, dn_send, dn_keep, ff_grad = ffn(
-        where, ends, x_mine, x_other, cot_mine, cot_other, ff_weight
+    x_and_grads = (x_mine, x_other, cot_mine, cot_other)
+    *ff_saved, ff_grad = ffn_first(where, ends, *x_and_grads, ff_weights[0])
+    own_first = lax.psum_scatter(
+        ff_grad, "dp", scatter_dimension=0, tiled=True, axis_index_groups=columns
+    )
+    out_send, out_keep, dn_send, dn_keep, ff_grad = ffn_second(
+        where, ends, *x_and_grads, ff_weights[1], ff_weights[0], ff_saved
+    )
+    own_second = lax.psum_scatter(
+        ff_grad, "dp", scatter_dimension=0, tiled=True, axis_index_groups=columns
     )
     dn_parts = chip_sum(dn_keep, swap_cores(dn_send))
     out_keep = after(dn_parts, out_keep)
@@ -837,41 +950,41 @@
     )
     gain_ffn = jnp.sum(d_normed2 * unit_b, axis=0)
     d_hidden = grad_out.astype(jnp.float32) + norm_back(d_normed2 * ffn_gain, unit_b, factor_b)
-    h_mine, h_other = gather_rows(d_hidden.astype(jnp.bfloat16))
-    own_ff = lax.psum_scatter(
-        ff_grad, "dp", scatter_dimension=0, tiled=True, axis_index_groups=columns
-    )
-    out_parts = chip_sum(out_keep, swap_cores(out_send))
-    out_parts = after((h_mine, h_other), out_parts)
-    ffn_branch = plane_total(out_parts)
-    block_out = (hidden + ffn_branch).astype(jnp.bfloat16)
-
-    send, keep, attn_grad, part_gains = attn_back(
-        where, ends, tok_mine, tok_other, gains, tables, (h_mine, h_other), saved, attn_weight,
-        gain_ffn[None, :],
-    )
-    send, keep, attn_grad, part_gains = after(block_out, (send, keep, attn_grad, part_gains))
-    own_attn = lax.psum_scatter(
-        attn_grad, "dp", scatter_dimension=0, tiled=True, axis_index_groups=columns
-    )
-    far_gains = [send_deep(part_gains, step) for step in range(1, layers)]
-    own_dn, own_ff, *messages = tail_messages(where, keep, swap_cores(send), own_ff)
-    messages = [send_plane(part, mask + 1) for mask, part in enumerate(messages)]
-    own_attn = after(messages, own_attn)
-    attn_parts = split_attn(where, own_attn, part_gains, far_gains)
+    h_mine, h_other = gather_rows(after(own_first, d_hidden.astype(jnp.bfloat16)))
+    own_out, ff_first, messages = tail_messages(where, out_keep, swap_cores(out_send), own_first)
+    messages = after((h_mine, h_other), messages)
+    first_messages = [send_plane(part, mask + 1) for mask, part in enumerate(messages)]
+    block_out = hidden + (own_out + add_up([part[:local_rows] for part in first_messages]))
+    block_out = block_out.astype(jnp.bfloat16)
+
+    send, keep, own_attn, part_gains, *attn_grads = after(
+        (block_out, own_second),
+        attn_back(
+            where, ends, layers, tok_mine, tok_other, gains, tables, (h_mine, h_other), saved,
+            attn_weight, gain_ffn[None, :],
+        ),
+    )
+    attn_grads = [send_deep(piece, step + 1) for step, piece in enumerate(attn_grads)]
+    keep = after((attn_grads[0], attn_grads[-1]), keep)
+    own_dn, ff_second, messages = tail_messages(where, keep, swap_cores(send), own_second)
+    second_messages = [send_plane(part, mask + 1) for mask, part in enumerate(messages)]
+    own_attn = after(second_messages[:2], own_attn)
+    attn_parts = plane_split_attn(where, own_attn, attn_grads, part_gains)
     attn_parts = [attn_parts[0]] + [
         send_plane(part, mask + 1) for mask, part in enumerate(attn_parts[1:])
     ]
-    d_normed = own_dn + add_up([part[:local_rows] for part in messages])
+    d_normed = own_dn + add_up([part[:local_rows] for part in second_messages])
     grad_tokens = d_hidden + norm_back(d_normed * attn_gain, unit_a, factor_a)
     grad_gate, grad_up, grad_down = call(
         place_ffn_kernel,
         [(w_gate.shape, float32)] * 3,
         where,
-        own_ff,
-        *messages,
+        ff_first,
+        *first_messages,
+        ff_second,
+        *second_messages,
         scalars=1,
-        scratch=[pltpu.VMEM((PLANE, rows, ff_cols), float32)],
+        scratch=[pltpu.VMEM((PLANE, rows, 2 * LANES), float32)],
     )
     grad_query, grad_key, grad_value, grad_out_w, sums = call(
         place_attn_kernel,

time: 285 us -> 281 us (0.986)
  blocking collectives: 29.1 us -> 0 us
  waiting for transfers between devices: 96.2 us -> 106 us
  Pallas kernels: 72.4 us -> 81.5 us
  starting transfers between devices: 46.1 us -> 51.1 us
    all_gather x1 -> x0, blocking collectives: 29.1 us -> none  [body(): lax.all_gather(attn_piece, 'dp', axis=0, tiled=True, axis_index_groups=co...]
    ppermute x3 -> x6, waiting for transfers between devices: 0.01 us -> 18.9 us  [send_deep(): lax.ppermute(values, 'dp', [(i, (i + PLANE * step) % count) for i in rang...]
    pallas_call x3 -> x4, Pallas kernels: 46.6 us -> 53.7 us  [the longest x1 16.1 us: attn_back(): pl.pallas_call(lambda *refs: attn_back_kernel(layers, *refs), grid=(PLANE...]
    reduce_scatter x1 -> x0, waiting for transfers between devices: 6.36 us -> none  [body(): lax.psum_scatter(attn_grad, 'dp', scatter_dimension=0, tiled=True, axis_i...]
    ppermute x3 -> x6, starting transfers between devices: 4.14 us -> 10.4 us  [send_deep(): lax.ppermute(values, 'dp', [(i, (i + PLANE * step) % count) for i in rang...]
    pallas_call x10 -> x11, Pallas kernels: 25.8 us -> 27.8 us  [call(): pl.pallas_call(kernel, out_shape=[jax.ShapeDtypeStruct(shape, kind) for s...]
    unnamed x91 -> x92, local copies, waits for them, and re-layouts: 10.5 us -> 9.05 us
  transfers between devices with their start and end apart: 48 -> 52, of which waited for: 24 -> 25; matrix products, arithmetic and copies ran while one was open for 5% -> 5% of each run, Pallas kernels for 16% -> 25%
where the time goes in v7:
time: 281 us; the launch traced here: 279 us
  waiting for transfers between devices  106 us (38%)
  Pallas kernels  81.5 us (29%)
  starting transfers between devices  51.1 us (18%)
  between operations  14.4 us (5%)
  other arithmetic  13.5 us (5%)
  local copies, waits for them, and re-layouts  12.3 us (4%)
    ppermute x33, waiting for transfers between devices, send_plane(): return lax.ppermute(values, 'dp', [(i, i ^ mask) for i in range(count)])  75.1 us
    ppermute x33, starting transfers between devices, send_plane(): return lax.ppermute(values, 'dp', [(i, i ^ mask) for i in range(count)])  39.6 us
    pallas_call x11, Pallas kernels, call(): pl.pallas_call(kernel, out_shape=[jax.ShapeDtypeStruct(shape, kind) for s...  27.8 us
    ppermute x6, waiting for transfers between devices, send_deep(): lax.ppermute(values, 'dp', [(i, (i + PLANE * step) % count) for i in rang...  18.9 us
    pallas_call x1, Pallas kernels, attn_back(): pl.pallas_call(lambda *refs: attn_back_kernel(layers, *refs), grid=(PLANE...  16.1 us
    pallas_call x1, Pallas kernels, ffn_second(): pl.pallas_call(ffn_second_kernel, grid=(2,), in_specs=[scalar, scalar] +...  15.3 us
    pallas_call x1, Pallas kernels, ffn_first(): pl.pallas_call(ffn_first_kernel, grid=(2,), in_specs=[scalar, scalar] + [...  12.1 us
    ppermute x6, starting transfers between devices, send_deep(): lax.ppermute(values, 'dp', [(i, (i + PLANE * step) % count) for i in rang...  10.4 us
  transfers between devices with their start and end apart: 52, of which 25 were waited for; matrix products, arithmetic and copies ran while one was open for 5% of the time, Pallas kernels for 25%

profile of v7, /device:TPU:0, one launch (start us, length us, event | category | flops | bytes accessed | tf_op | source)
XLA Modules:
  0.0 279.0 jit_solution(2258557886060443772)
XLA Ops:
  7.8 1.7 shard_map.237
  9.6 2.9 %collective-permute-start = (bf16[32,1024]{1,0:T(8,128)(2,1)}, bf16[32,1024]{1,0:T(8,128)(2,1)S(1)}, u32[]{:S(2)}, u32[]{:S(2)}) collective-permute-start(bf16[32,1024]{1,0:T(8,128)(2,1)} %get-tuple-element.105), channel_id=1, source_target_pairs={{0,2},{2,0},{4,6},{6,4},{8,10},{10,8},{12,14},{14,12},{16,18},{18,... | collective-permute-start | bytes 196616 | tf_op jit(solution)/shard_map/ppermute | solution.py:99
  12.5 1.5 collective-permute-start.1
  15.2 1.8 collective-permute-done.1.two
  17.0 2.4 collective-permute-done.2.three
  20.0 1.7 shard_map.238
  21.7 3.7 %collective-permute-start.9 = (bf16[256,384]{1,0:T(8,128)(2,1)}, bf16[256,384]{1,0:T(8,128)(2,1)S(1)}, u32[]{:S(2)}, u32[]{:S(2)}) collective-permute-start(bf16[256,384]{1,0:T(8,128)(2,1)} %get-tuple-element.124.refs_9_), channel_id=1, source_target_pairs={{0,24},{2,26},{4,28},{6,30},{8,0},{10,2},{12,4},{14,6},{16,8},{18,... | collective-permute-start | bytes 589832 | tf_op jit(solution)/shard_map/ppermute | solution.py:104
  25.4 2.2 shard_map.239
  28.6 2.4 collective-permute-start.12
  32.0 10.3 %collective-permute-done.8.refs_11_ = bf16[256,384]{1,0:T(8,128)(2,1)S(1)} collective-permute-done((bf16[256,384]{1,0:T(8,128)(2,1)}, bf16[256,384]{1,0:T(8,128)(2,1)S(1)}, u32[]{:S(2)}, u32[]{:S(2)}) %collective-permute-start.8) | collective-permute-done | bytes 196640 | tf_op jit(solution)/shard_map/ppermute | solution.py:104
  44.4 2.4 shard_map.240
  48.5 2.0 collective-permute-start.5
  50.5 5.7 %collective-permute-done.3 = bf16[128,1024]{1,0:T(8,128)(2,1)S(1)} collective-permute-done((bf16[128,1024]{1,0:T(8,128)(2,1)S(1)}, bf16[128,1024]{1,0:T(8,128)(2,1)S(1)}, u32[]{:S(2)}, u32[]{:S(2)}) %collective-permute-start.3) | collective-permute-done | bytes 262176 | tf_op jit(solution)/shard_map/ppermute | solution.py:99
  56.2 4.2 %collective-permute-done.4 = bf16[128,1024]{1,0:T(8,128)(2,1)S(1)} collective-permute-done((bf16[128,1024]{1,0:T(8,128)(2,1)S(1)}, bf16[128,1024]{1,0:T(8,128)(2,1)S(1)}, u32[]{:S(2)}, u32[]{:S(2)}) %collective-permute-start.4) | collective-permute-done | bytes 262176 | tf_op jit(solution)/shard_map/ppermute | solution.py:99
  62.3 1.2 collective-permute-start.15
  63.5 1.5 collective-permute-start.14
  65.9 3.1 %fusion.6 = (f32[1024,128]{1,0:T(8,128)}, f32[1024,128]{1,0:T(8,128)}) fusion(f32[128]{0:T(128)S(1)} %get-tuple-element.209, f32[128]{0:T(128)S(1)} %get-tuple-element.210, f32[1024]{0:T(1024)S(1)} %bitcast.28), kind=kLoop, calls=%fused_computation.12 | loop fusion | flops 262144 | bytes 1053696 | tf_op jit(solution)/shard_map/mul | solution.py:913
  70.0 10.2 %shard_map.241 = (bf16[512,1024]{1,0:T(8,128)(2,1)}, f32[512,1024]{1,0:T(8,128)}, f32[1024,256]{1,0:T(8,128)}, bf16[1024,256]{1,0:T(8,128)(2,1)}, bf16[1024,128]{1,0:T(8,128)(2,1)}, /*index=5*/bf16[1024,384]{1,0:T(8,128)(2,1)}) custom-call(s32[3]{0:T(128)} %pad_add_fusion.where_ref.refs_0_, s32[4,4]{1,0:T(4,128)} %copy-done.26, bf16[512,1024]{1,0:T(8,128)(2,1)} %copy-done.1, ...), custom_call_target="tpu_custom_call" | custom-call | flops 1024 | bytes 36000000 | tf_op jit(solution)/shard_map/pallas_call | solution.py:431
  80.3 2.9 %collective-permute-done.16.received = bf16[512,1024]{1,0:T(8,128)(2,1)S(1)} collective-permute-done((bf16[512,1024]{1,0:T(8,128)(2,1)}, bf16[512,1024]{1,0:T(8,128)(2,1)S(1)}, u32[]{:S(2)}, u32[]{:S(2)}) %collective-permute-start.16) | collective-permute-done | bytes 1048608 | tf_op jit(solution)/shard_map/ppermute | solution.py:108
  84.2 2.9 %shard_map.242 = (f32[128,1024]{1,0:T(8,128)}, bf16[128,1024]{1,0:T(8,128)(2,1)}, bf16[128,1024]{1,0:T(8,128)(2,1)}, bf16[128,1024]{1,0:T(8,128)(2,1)}) custom-call(f32[512,1024]{1,0:T(8,128)} %get-tuple-element.128.keep, bf16[512,1024]{1,0:T(8,128)(2,1)} %copy-done.13), custom_call_target="tpu_custom_call" | custom-call | flops 1024 | bytes 1024 | tf_op jit(solution)/shard_map/pallas_call | solution.py:114
  87.1 1.2 collective-permute-start.17
  88.8 1.8 collective-permute-start.19
  90.7 5.8 %collective-permute-done.17 = bf16[128,1024]{1,0:T(8,128)(2,1)S(1)} collective-permute-done((bf16[128,1024]{1,0:T(8,128)(2,1)}, bf16[128,1024]{1,0:T(8,128)(2,1)S(1)}, u32[]{:S(2)}, u32[]{:S(2)}) %collective-permute-start.17) | collective-permute-done | bytes 262176 | tf_op jit(solution)/shard_map/ppermute | solution.py:99
  96.5 5.7 %collective-permute-done.18 = bf16[128,1024]{1,0:T(8,128)(2,1)S(1)} collective-permute-done((bf16[128,1024]{1,0:T(8,128)(2,1)}, bf16[128,1024]{1,0:T(8,128)(2,1)S(1)}, u32[]{:S(2)}, u32[]{:S(2)}) %collective-permute-start.18) | collective-permute-done | bytes 262176 | tf_op jit(solution)/shard_map/ppermute | solution.py:99
  102.2 1.4 multiply_reduce_fusion.2
  103.8 1.3 collective-permute-start.22
  106.1 1.2 collective-permute-start.20
  107.5 6.5 %collective-permute-done.22 = bf16[128,1024]{1,0:T(8,128)(2,1)S(1)} collective-permute-done((bf16[128,1024]{1,0:T(8,128)(2,1)S(1)}, bf16[128,1024]{1,0:T(8,128)(2,1)S(1)}, u32[]{:S(2)}, u32[]{:S(2)}) %collective-permute-start.22) | collective-permute-done | bytes 262176 | tf_op jit(solution)/shard_map/ppermute | solution.py:99
  114.0 3.4 %collective-permute-done.21 = bf16[128,1024]{1,0:T(8,128)(2,1)S(1)} collective-permute-done((bf16[128,1024]{1,0:T(8,128)(2,1)S(1)}, bf16[128,1024]{1,0:T(8,128)(2,1)S(1)}, u32[]{:S(2)}, u32[]{:S(2)}) %collective-permute-start.21) | collective-permute-done | bytes 262176 | tf_op jit(solution)/shard_map/ppermute | solution.py:99
  117.7 2.7 collective-permute-done.23.x_o
  120.4 12.1 %shard_map.243 = (bf16[1024,384]{1,0:T(8,128)(2,1)}, bf16[1024,640]{1,0:T(8,128)(2,1)}, bf16[1024,1024]{1,0:T(8,128)(2,1)}) custom-call(s32[3]{0:T(128)} %pad_add_fusion.where_ref.refs_0_, s32[4,4]{1,0:T(4,128)} %copy-done.26, bf16[512,1024]{1,0:T(8,128)(2,1)} %collective-permute-done.23.x_o, bf16[512,1024]{1,0:T(8,128)(2,1)} %copy-done, ...), custom_call_target="tpu_custom_call" | custom-call | flops 1024 | bytes 25000000 | tf_op jit(solution)/shard_map/pallas_call | solution.py:591
  132.7 15.3 %shard_map.244 = (bf16[512,1024]{1,0:T(8,128)(2,1)}, f32[512,1024]{1,0:T(8,128)}, bf16[512,1024]{1,0:T(8,128)(2,1)}, f32[512,1024]{1,0:T(8,128)}, bf16[1024,768]{1,0:T(8,128)(2,1)}) custom-call(s32[3]{0:T(128)} %pad_add_fusion.where_ref.refs_0_, s32[4,4]{1,0:T(4,128)} %copy-done.26, bf16[512,1024]{1,0:T(8,128)(2,1)} %collective-permute-done.23.x_o, ...), custom_call_target="tpu_custom_call" | custom-call | flops 1024 | bytes 50000000 | tf_op jit(solution)/shard_map/pallas_call | solution.py:610
  148.2 2.7 collective-permute-done.25.received
  152.0 3.0 %shard_map.245 = (f32[128,1024]{1,0:T(8,128)}, bf16[128,1024]{1,0:T(8,128)(2,1)}, bf16[128,1024]{1,0:T(8,128)(2,1)}, bf16[128,1024]{1,0:T(8,128)(2,1)}) custom-call(f32[512,1024]{1,0:T(8,128)} %get-tuple-element.138.keep, bf16[512,1024]{1,0:T(8,128)(2,1)} %copy-done.14), custom_call_target="tpu_custom_call" | custom-call | flops 1024 | bytes 1024 | tf_op jit(solution)/shard_map/pallas_call | solution.py:114
  155.8 1.4 collective-permute-start.28
  157.2 1.2 collective-permute-start.29
  158.4 1.3 slice.37
  160.4 3.9 %collective-permute-done.27 = bf16[128,1024]{1,0:T(8,128)(2,1)S(1)} collective-permute-done((bf16[128,1024]{1,0:T(8,128)(2,1)}, bf16[128,1024]{1,0:T(8,128)(2,1)S(1)}, u32[]{:S(2)}, u32[]{:S(2)}) %collective-permute-start.27) | collective-permute-done | bytes 262176 | tf_op jit(solution)/shard_map/ppermute | solution.py:99
  164.3 4.5 %collective-permute-done.28 = bf16[128,1024]{1,0:T(8,128)(2,1)S(1)} collective-permute-done((bf16[128,1024]{1,0:T(8,128)(2,1)}, bf16[128,1024]{1,0:T(8,128)(2,1)S(1)}, u32[]{:S(2)}, u32[]{:S(2)}) %collective-permute-start.28) | collective-permute-done | bytes 262176 | tf_op jit(solution)/shard_map/ppermute | solution.py:99
  169.7 1.9 multiply_reduce_fusion
  171.9 4.0 %reduce-scatter.3.cloned.1.call-done.own_ff = bf16[256,1024]{1,0:T(8,128)(2,1)} async-done(((bf16[1024,1024]{1,0:T(8,128)(2,1)}), bf16[256,1024]{1,0:T(8,128)(2,1)}) %reduce-scatter.3.cloned.1.call-update) | async-done | bytes 524304 | tf_op jit(solution)/shard_map/reduce_scatter | solution.py:934
  175.9 1.5 collective-permute-start.30
  177.3 1.5 collective-permute-start.31
  179.4 5.7 %collective-permute-done.30 = bf16[128,1024]{1,0:T(8,128)(2,1)S(1)} collective-permute-done((bf16[128,1024]{1,0:T(8,128)(2,1)S(1)}, bf16[128,1024]{1,0:T(8,128)(2,1)S(1)}, u32[]{:S(2)}, u32[]{:S(2)}) %collective-permute-start.30) | collective-permute-done | bytes 262176 | tf_op jit(solution)/shard_map/ppermute | solution.py:99
  185.1 5.5 %collective-permute-done.31 = bf16[128,1024]{1,0:T(8,128)(2,1)S(1)} collective-permute-done((bf16[128,1024]{1,0:T(8,128)(2,1)S(1)}, bf16[128,1024]{1,0:T(8,128)(2,1)S(1)}, u32[]{:S(2)}, u32[]{:S(2)}) %collective-permute-start.31) | collective-permute-done | bytes 262176 | tf_op jit(solution)/shard_map/ppermute | solution.py:99
  190.7 3.7 %shard_map.246 = (f32[128,1024]{1,0:T(8,128)}, f32[64,1024]{1,0:T(8,128)}, bf16[192,1024]{1,0:T(8,128)(2,1)}, bf16[192,1024]{1,0:T(8,128)(2,1)}, bf16[192,1024]{1,0:T(8,128)(2,1)}) custom-call(s32[3]{0:T(128)} %pad_add_fusion.where_ref.refs_0_, f32[512,1024]{1,0:T(8,128)} %get-tuple-element.145.keep, bf16[512,1024]{1,0:T(8,128)(2,1)} %collective-permute-done.26.received, ...), custom_call_target="tpu_custom_call" | custom-call | flops 1024 | bytes 1024 | tf_op jit(solution)/shard_map/pallas_call | solution.py:114
  196.3 1.6 collective-permute-start.36
  197.9 16.1 %shard_map.247 = (bf16[512,1024]{1,0:T(8,128)(2,1)}, f32[512,1024]{1,0:T(8,128)}, f32[256,384]{1,0:T(8,128)}, f32[8,384]{1,0:T(8,128)}, bf16[272,384]{1,0:T(8,12...) custom-call(s32[3]{0:T(128)} %pad_add_fusion.where_ref.refs_0_, s32[4,4]{1,0:T(4,128)} %copy-done.26, ...), custom_call_target="tpu_custom_call" | custom-call | flops 1024 | bytes 24000000 | tf_op jit(solution)/shard_map/pallas_call | solution.py:457
  215.9 1.9 add_convert_fusion
  217.9 3.8 %collective-permute-start.38 = (bf16[272,384]{1,0:T(8,128)(2,1)S(1)}, bf16[272,384]{1,0:T(8,128)(2,1)S(1)}, u32[]{:S(2)}, u32[]{:S(2)}) collective-permute-start(bf16[272,384]{1,0:T(8,128)(2,1)S(1)} %copy-done.39), channel_id=1, source_target_pairs={{0,24},{2,26},{4,28},{6,30},{8,0},{10,2},{12,4},{14,6},{16,8},{18,... | collective-permute-start | bytes 626696 | tf_op jit(solution)/shard_map/ppermute | solution.py:104
  221.7 6.0 %collective-permute-done.37.refs_0_ = bf16[272,384]{1,0:T(8,128)(2,1)S(1)} collective-permute-done((bf16[272,384]{1,0:T(8,128)(2,1)S(1)}, bf16[272,384]{1,0:T(8,128)(2,1)S(1)}, u32[]{:S(2)}, u32[]{:S(2)}) %collective-permute-start.37) | collective-permute-done | bytes 208928 | tf_op jit(solution)/shard_map/ppermute | solution.py:104
  227.7 2.7 collective-permute-done.38.refs_2_
  231.4 3.3 %shard_map.248 = (f32[128,1024]{1,0:T(8,128)}, f32[64,768]{1,0:T(8,128)}, bf16[192,1024]{1,0:T(8,128)(2,1)}, bf16[192,1024]{1,0:T(8,128)(2,1)}, bf16[192,1024]{1,0:T(8,128)(2,1)}) custom-call(s32[3]{0:T(128)} %pad_add_fusion.where_ref.refs_0_, f32[512,1024]{1,0:T(8,128)} %get-tuple-element.171.keep, bf16[512,1024]{1,0:T(8,128)(2,1)} %copy-done.16, ...), custom_call_target="tpu_custom_call" | custom-call | flops 1024 | bytes 1024 | tf_op jit(solution)/shard_map/pallas_call | solution.py:114
  235.6 1.5 collective-permute-start.41
  238.3 1.9 collective-permute-start.43
  240.2 6.8 %collective-permute-done.40.refs_5_ = bf16[192,1024]{1,0:T(8,128)(2,1)S(1)} collective-permute-done((bf16[192,1024]{1,0:T(8,128)(2,1)}, bf16[192,1024]{1,0:T(8,128)(2,1)S(1)}, u32[]{:S(2)}, u32[]{:S(2)}) %collective-permute-start.40) | collective-permute-done | bytes 393248 | tf_op jit(solution)/shard_map/ppermute | solution.py:99
  247.0 7.5 %collective-permute-done.41.refs_6_ = bf16[192,1024]{1,0:T(8,128)(2,1)S(1)} collective-permute-done((bf16[192,1024]{1,0:T(8,128)(2,1)}, bf16[192,1024]{1,0:T(8,128)(2,1)S(1)}, u32[]{:S(2)}, u32[]{:S(2)}) %collective-permute-start.41) | collective-permute-done | bytes 393248 | tf_op jit(solution)/shard_map/ppermute | solution.py:99
  255.3 2.1 shard_map.249
  257.4 2.0 collective-permute-start.45
  259.4 1.5 collective-permute-start.46
  260.9 1.5 fusion.2
  262.4 2.4 collective-permute-done.46.three
  265.4 1.7 shard_map.250
  268.2 3.1 %shard_map.251 = (f32[64,2304]{1,0:T(8,128)}, f32[64,2304]{1,0:T(8,128)}, f32[64,2304]{1,0:T(8,128)}) custom-call(s32[3]{0:T(128)} %pad_add_fusion.where_ref.refs_0_, f32[64,1024]{1,0:T(8,128)} %get-tuple-element.190.refs_0_, bf16[192,1024]{1,0:T(8,128)(2,1)} %copy-done.10, bf16[192,1024]{1,0:T(8,128)(2,1)} %copy-done.11, bf16[192,1024]{1,0:T(8,128)(2,1)} %copy-done.12, ...), custom_call_target="tpu_custom_call" | custom-call | flops 1024 | bytes 1024 | tf_op jit(solution)/shard_map/pallas_call | solution.py:114
  (180 shorter events, 30.6 us)
Async XLA Ops:
  7.2 39.7 %copy-start.4 = (bf16[128,1024]{1,0:T(8,128)(2,1)S(1)}, bf16[128,1024]{1,0:T(8,128)(2,1)}, u32[]{:S(2)}) copy-start(bf16[128,1024]{1,0:T(8,128)(2,1)} %param.14) | copy-start | bytes 786436
  7.2 110.5 %all-gather.5.cloned.1.call-start = ((), (), s32[]{:S(2)}) async-start(), calls=%async_computation.3 | async-start | bytes 2621440 | tf_op jit(solution)/shard_map/all_gather | solution.py:892
  9.6 5.6 %collective-permute-start = (bf16[32,1024]{1,0:T(8,128)(2,1)}, bf16[32,1024]{1,0:T(8,128)(2,1)S(1)}, u32[]{:S(2)}, u32[]{:S(2)}) collective-permute-start(bf16[32,1024]{1,0:T(8,128)(2,1)} %get-tuple-element.105), channel_id=1, source_target_pairs={{0,2},{2,0},{4,6},{6,4},{8,10},{10,8},{12,14},{14,12},{16,18},{18,... | collective-permute-start | bytes 196616 | tf_op jit(solution)/shard_map/ppermute | solution.py:99
  12.5 4.5 %collective-permute-start.1 = (bf16[32,1024]{1,0:T(8,128)(2,1)}, bf16[32,1024]{1,0:T(8,128)(2,1)S(1)}, u32[]{:S(2)}, u32[]{:S(2)}) collective-permute-start(bf16[32,1024]{1,0:T(8,128)(2,1)} %get-tuple-element.106), channel_id=1, source_target_pairs={{0,4},{2,6},{4,0},{6,2},{8,12},{10,14},{12,8},{14,10},{16,20},{18,... | collective-permute-start | bytes 196616 | tf_op jit(solution)/shard_map/ppermute | solution.py:99
  14.0 5.4 %collective-permute-start.2 = (bf16[32,1024]{1,0:T(8,128)(2,1)}, bf16[32,1024]{1,0:T(8,128)(2,1)S(1)}, u32[]{:S(2)}, u32[]{:S(2)}) collective-permute-start(bf16[32,1024]{1,0:T(8,128)(2,1)} %get-tuple-element.107), channel_id=1, source_target_pairs={{0,6},{2,4},{4,2},{6,0},{8,14},{10,12},{12,10},{14,8},{16,22},{18,... | collective-permute-start | bytes 196616 | tf_op jit(solution)/shard_map/ppermute | solution.py:99
  21.7 38.9 %copy-start.36 = (f32[64]{0:T(128)S(1)}, f32[64]{0:T(128)}, u32[]{:S(2)}) copy-start(f32[64]{0:T(128)} %param.17) | copy-start | bytes 772
  21.7 38.9 %copy-start.37 = (f32[64]{0:T(128)S(1)}, f32[64]{0:T(128)}, u32[]{:S(2)}) copy-start(f32[64]{0:T(128)} %param.18) | copy-start | bytes 772
  21.7 40.6 %copy-start.15 = (bf16[128,1024]{1,0:T(8,128)(2,1)S(1)}, bf16[128,1024]{1,0:T(8,128)(2,1)}, u32[]{:S(2)}) copy-start(bf16[128,1024]{1,0:T(8,128)(2,1)} %param.27) | copy-start | bytes 786436
  21.7 9.3 %collective-permute-start.9 = (bf16[256,384]{1,0:T(8,128)(2,1)}, bf16[256,384]{1,0:T(8,128)(2,1)S(1)}, u32[]{:S(2)}, u32[]{:S(2)}) collective-permute-start(bf16[256,384]{1,0:T(8,128)(2,1)} %get-tuple-element.124.refs_9_), channel_id=1, source_target_pairs={{0,24},{2,26},{4,28},{6,30},{8,0},{10,2},{12,4},{14,6},{16,8},{18,... | collective-permute-start | bytes 589832 | tf_op jit(solution)/shard_map/ppermute | solution.py:104
  27.5 14.8 %collective-permute-start.10 = (bf16[64,1792]{1,0:T(8,128)(2,1)}, bf16[64,1792]{1,0:T(8,128)(2,1)S(1)}, u32[]{:S(2)}, u32[]{:S(2)}) collective-permute-start(bf16[64,1792]{1,0:T(8,128)(2,1)} %get-tuple-element.115), channel_id=1, source_target_pairs={{0,2},{2,0},{4,6},{6,4},{8,10},{10,8},{12,14},{14,12},{16,18},{18,... | collective-permute-start | bytes 688136 | tf_op jit(solution)/shard_map/ppermute | solution.py:99
  28.1 14.3 %collective-permute-start.11 = (bf16[64,1792]{1,0:T(8,128)(2,1)}, bf16[64,1792]{1,0:T(8,128)(2,1)S(1)}, u32[]{:S(2)}, u32[]{:S(2)}) collective-permute-start(bf16[64,1792]{1,0:T(8,128)(2,1)} %get-tuple-element.116), channel_id=1, source_target_pairs={{0,4},{2,6},{4,0},{6,2},{8,12},{10,14},{12,8},{14,10},{16,20},{18,... | collective-permute-start | bytes 688136 | tf_op jit(solution)/shard_map/ppermute | solution.py:99
  28.6 14.5 %collective-permute-start.12 = (bf16[64,1792]{1,0:T(8,128)(2,1)}, bf16[64,1792]{1,0:T(8,128)(2,1)S(1)}, u32[]{:S(2)}, u32[]{:S(2)}) collective-permute-start(bf16[64,1792]{1,0:T(8,128)(2,1)} %get-tuple-element.117), channel_id=1, source_target_pairs={{0,6},{2,4},{4,2},{6,0},{8,14},{10,12},{12,10},{14,8},{16,22},{18,... | collective-permute-start | bytes 688136 | tf_op jit(solution)/shard_map/ppermute | solution.py:99
  31.0 11.3 %collective-permute-start.8 = (bf16[256,384]{1,0:T(8,128)(2,1)}, bf16[256,384]{1,0:T(8,128)(2,1)S(1)}, u32[]{:S(2)}, u32[]{:S(2)}) collective-permute-start(bf16[256,384]{1,0:T(8,128)(2,1)} %get-tuple-element.124.refs_9_), channel_id=1, source_target_pairs={{0,16},{2,18},{4,20},{6,22},{8,24},{10,26},{12,28},{14,30},{16,0},... | collective-permute-start | bytes 589832 | tf_op jit(solution)/shard_map/ppermute | solution.py:104
  31.0 11.3 %collective-permute-start.7 = (bf16[256,384]{1,0:T(8,128)(2,1)}, bf16[256,384]{1,0:T(8,128)(2,1)S(1)}, u32[]{:S(2)}, u32[]{:S(2)}) collective-permute-start(bf16[256,384]{1,0:T(8,128)(2,1)} %get-tuple-element.124.refs_9_), channel_id=1, source_target_pairs={{0,8},{2,10},{4,12},{6,14},{8,16},{10,18},{12,20},{14,22},{16,24},... | collective-permute-start | bytes 589832 | tf_op jit(solution)/shard_map/ppermute | solution.py:104
  46.9 85.9 %all-gather.3.cloned.1.call-start = ((), (), s32[]{:S(2)}) async-start(), calls=%async_computation.2 | async-start | bytes 1966080 | tf_op jit(solution)/shard_map/all_gather | solution.py:892
  46.9 9.3 %collective-permute-start.3 = (bf16[128,1024]{1,0:T(8,128)(2,1)S(1)}, bf16[128,1024]{1,0:T(8,128)(2,1)S(1)}, u32[]{:S(2)}, u32[]{:S(2)}) collective-permute-start(bf16[128,1024]{1,0:T(8,128)(2,1)S(1)} %copy-done.4), channel_id=1, source_target_pairs={{0,2},{2,0},{4,6},{6,4},{8,10},{10,8},{12,14},{14,12},{16,18},{18,... | collective-permute-start | bytes 786440 | tf_op jit(solution)/shard_map/ppermute | solution.py:99
  47.9 12.5 %collective-permute-start.4 = (bf16[128,1024]{1,0:T(8,128)(2,1)S(1)}, bf16[128,1024]{1,0:T(8,128)(2,1)S(1)}, u32[]{:S(2)}, u32[]{:S(2)}) collective-permute-start(bf16[128,1024]{1,0:T(8,128)(2,1)S(1)} %copy-done.4), channel_id=1, source_target_pairs={{0,4},{2,6},{4,0},{6,2},{8,12},{10,14},{12,8},{14,10},{16,20},{18,... | collective-permute-start | bytes 786440 | tf_op jit(solution)/shard_map/ppermute | solution.py:99
  48.5 11.9 %collective-permute-start.5 = (bf16[128,1024]{1,0:T(8,128)(2,1)S(1)}, bf16[128,1024]{1,0:T(8,128)(2,1)S(1)}, u32[]{:S(2)}, u32[]{:S(2)}) collective-permute-start(bf16[128,1024]{1,0:T(8,128)(2,1)S(1)} %copy-done.4), channel_id=1, source_target_pairs={{0,6},{2,4},{4,2},{6,0},{8,14},{10,12},{12,10},{14,8},{16,22},{18,... | collective-permute-start | bytes 786440 | tf_op jit(solution)/shard_map/ppermute | solution.py:99
  60.5 8.5 %collective-permute-start.6 = (bf16[512,1024]{1,0:T(8,128)(2,1)S(1)}, bf16[512,1024]{1,0:T(8,128)(2,1)S(1)}, u32[]{:S(2)}, u32[]{:S(2)}) collective-permute-start(bf16[512,1024]{1,0:T(8,128)(2,1)S(1)} %constant_dynamic-update-slice_fusion.refs_2_), channel_id=1, source_target_pairs={{0,1},{1,0},{2,3},{3,2},{4,5},{5,4},{6,7},{7,6},{8,9},{9,8},{10,11... | collective-permute-start | bytes 3145736 | tf_op jit(solution)/shard_map/ppermute | solution.py:108
  62.3 17.9 %collective-permute-start.15 = (bf16[128,1024]{1,0:T(8,128)(2,1)S(1)}, bf16[128,1024]{1,0:T(8,128)(2,1)S(1)}, u32[]{:S(2)}, u32[]{:S(2)}) collective-permute-start(bf16[128,1024]{1,0:T(8,128)(2,1)S(1)} %copy-done.15), channel_id=1, source_target_pairs={{0,6},{2,4},{4,2},{6,0},{8,14},{10,12},{12,10},{14,8},{16,22},{18,... | collective-permute-start | bytes 786440 | tf_op jit(solution)/shard_map/ppermute | solution.py:99
  63.5 16.7 %collective-permute-start.14 = (bf16[128,1024]{1,0:T(8,128)(2,1)S(1)}, bf16[128,1024]{1,0:T(8,128)(2,1)S(1)}, u32[]{:S(2)}, u32[]{:S(2)}) collective-permute-start(bf16[128,1024]{1,0:T(8,128)(2,1)S(1)} %copy-done.15), channel_id=1, source_target_pairs={{0,4},{2,6},{4,0},{6,2},{8,12},{10,14},{12,8},{14,10},{16,20},{18,... | collective-permute-start | bytes 786440 | tf_op jit(solution)/shard_map/ppermute | solution.py:99
  65.0 15.2 %collective-permute-start.13 = (bf16[128,1024]{1,0:T(8,128)(2,1)S(1)}, bf16[128,1024]{1,0:T(8,128)(2,1)S(1)}, u32[]{:S(2)}, u32[]{:S(2)}) collective-permute-start(bf16[128,1024]{1,0:T(8,128)(2,1)S(1)} %copy-done.15), channel_id=1, source_target_pairs={{0,2},{2,0},{4,6},{6,4},{8,10},{10,8},{12,14},{14,12},{16,18},{18,... | collective-permute-start | bytes 786440 | tf_op jit(solution)/shard_map/ppermute | solution.py:99
  80.3 2.9 %collective-permute-start.16 = (bf16[512,1024]{1,0:T(8,128)(2,1)}, bf16[512,1024]{1,0:T(8,128)(2,1)S(1)}, u32[]{:S(2)}, u32[]{:S(2)}) collective-permute-start(bf16[512,1024]{1,0:T(8,128)(2,1)} %get-tuple-element.131), channel_id=1, source_target_pairs={{0,1},{1,0},{2,3},{3,2},{4,5},{5,4},{6,7},{7,6},{8,9},{9,8},{10,11... | collective-permute-start | bytes 3145736 | tf_op jit(solution)/shard_map/ppermute | solution.py:108
  87.1 9.4 %collective-permute-start.17 = (bf16[128,1024]{1,0:T(8,128)(2,1)}, bf16[128,1024]{1,0:T(8,128)(2,1)S(1)}, u32[]{:S(2)}, u32[]{:S(2)}) collective-permute-start(bf16[128,1024]{1,0:T(8,128)(2,1)} %get-tuple-element.133), channel_id=1, source_target_pairs={{0,2},{2,0},{4,6},{6,4},{8,10},{10,8},{12,14},{14,12},{16,18},{18,... | collective-permute-start | bytes 786440 | tf_op jit(solution)/shard_map/ppermute | solution.py:99
  88.3 13.9 %collective-permute-start.18 = (bf16[128,1024]{1,0:T(8,128)(2,1)}, bf16[128,1024]{1,0:T(8,128)(2,1)S(1)}, u32[]{:S(2)}, u32[]{:S(2)}) collective-permute-start(bf16[128,1024]{1,0:T(8,128)(2,1)} %get-tuple-element.134), channel_id=1, source_target_pairs={{0,4},{2,6},{4,0},{6,2},{8,12},{10,14},{12,8},{14,10},{16,20},{18,... | collective-permute-start | bytes 786440 | tf_op jit(solution)/shard_map/ppermute | solution.py:99
  88.8 13.4 %collective-permute-start.19 = (bf16[128,1024]{1,0:T(8,128)(2,1)}, bf16[128,1024]{1,0:T(8,128)(2,1)}, u32[]{:S(2)}, u32[]{:S(2)}) collective-permute-start(bf16[128,1024]{1,0:T(8,128)(2,1)} %get-tuple-element.135), channel_id=1, source_target_pairs={{0,6},{2,4},{4,2},{6,0},{8,14},{10,12},{12,10},{14,8},{16,22},{18,... | collective-permute-start | bytes 786440 | tf_op jit(solution)/shard_map/ppermute | solution.py:99
  90.6 85.2 %reduce-scatter.3.cloned.1.call-start = ((), (), s32[]{:S(2)}) async-start(), calls=%async_computation.4 | async-start | bytes 2621440 | tf_op jit(solution)/shard_map/reduce_scatter | solution.py:934
  103.8 10.2 %collective-permute-start.22 = (bf16[128,1024]{1,0:T(8,128)(2,1)S(1)}, bf16[128,1024]{1,0:T(8,128)(2,1)S(1)}, u32[]{:S(2)}, u32[]{:S(2)}) collective-permute-start(bf16[128,1024]{1,0:T(8,128)(2,1)S(1)} %multiply_convert_fusion), channel_id=1, source_target_pairs={{0,6},{2,4},{4,2},{6,0},{8,14},{10,12},{12,10},{14,8},{16,22},{18,... | collective-permute-start | bytes 786440 | tf_op jit(solution)/shard_map/ppermute | solution.py:99
  105.1 12.3 %collective-permute-start.21 = (bf16[128,1024]{1,0:T(8,128)(2,1)S(1)}, bf16[128,1024]{1,0:T(8,128)(2,1)S(1)}, u32[]{:S(2)}, u32[]{:S(2)}) collective-permute-start(bf16[128,1024]{1,0:T(8,128)(2,1)S(1)} %multiply_convert_fusion), channel_id=1, source_target_pairs={{0,4},{2,6},{4,0},{6,2},{8,12},{10,14},{12,8},{14,10},{16,20},{18,... | collective-permute-start | bytes 786440 | tf_op jit(solution)/shard_map/ppermute | solution.py:99
  106.1 11.3 %collective-permute-start.20 = (bf16[128,1024]{1,0:T(8,128)(2,1)S(1)}, bf16[128,1024]{1,0:T(8,128)(2,1)S(1)}, u32[]{:S(2)}, u32[]{:S(2)}) collective-permute-start(bf16[128,1024]{1,0:T(8,128)(2,1)S(1)} %multiply_convert_fusion), channel_id=1, source_target_pairs={{0,2},{2,0},{4,6},{6,4},{8,10},{10,8},{12,14},{14,12},{16,18},{18,... | collective-permute-start | bytes 786440 | tf_op jit(solution)/shard_map/ppermute | solution.py:99
  107.4 10.3 %collective-permute-start.24 = (bf16[512,1024]{1,0:T(8,128)(2,1)S(1)}, bf16[512,1024]{1,0:T(8,128)(2,1)}, u32[]{:S(2)}, u32[]{:S(2)}) collective-permute-start(bf16[512,1024]{1,0:T(8,128)(2,1)S(1)} %constant_dynamic-update-slice_fusion.4.g_m), channel_id=1, source_target_pairs={{0,1},{1,0},{2,3},{3,2},{4,5},{5,4},{6,7},{7,6},{8,9},{9,8},{10,11... | collective-permute-start | bytes 3145736 | tf_op jit(solution)/shard_map/ppermute | solution.py:108
  117.5 2.9 %collective-permute-start.23 = (bf16[512,1024]{1,0:T(8,128)(2,1)S(1)}, bf16[512,1024]{1,0:T(8,128)(2,1)}, u32[]{:S(2)}, u32[]{:S(2)}) collective-permute-start(bf16[512,1024]{1,0:T(8,128)(2,1)S(1)} %pad_maximum_fusion.x_m), channel_id=1, source_target_pairs={{0,1},{1,0},{2,3},{3,2},{4,5},{5,4},{6,7},{7,6},{8,9},{9,8},{10,11... | collective-permute-start | bytes 3145736 | tf_op jit(solution)/shard_map/ppermute | solution.py:108
  132.5 85.3 %reduce-scatter.5.cloned.1.call-start = ((), (), s32[]{:S(2)}) async-start(), calls=%async_computation.5 | async-start | bytes 1966080 | tf_op jit(solution)/shard_map/reduce_scatter | solution.py:940
  148.0 2.9 %collective-permute-start.25 = (bf16[512,1024]{1,0:T(8,128)(2,1)}, bf16[512,1024]{1,0:T(8,128)(2,1)S(1)}, u32[]{:S(2)}, u32[]{:S(2)}) collective-permute-start(bf16[512,1024]{1,0:T(8,128)(2,1)} %get-tuple-element.139), channel_id=1, source_target_pairs={{0,1},{1,0},{2,3},{3,2},{4,5},{5,4},{6,7},{7,6},{8,9},{9,8},{10,11... | collective-permute-start | bytes 3145736 | tf_op jit(solution)/shard_map/ppermute | solution.py:108
  154.9 9.4 %collective-permute-start.27 = (bf16[128,1024]{1,0:T(8,128)(2,1)}, bf16[128,1024]{1,0:T(8,128)(2,1)S(1)}, u32[]{:S(2)}, u32[]{:S(2)}) collective-permute-start(bf16[128,1024]{1,0:T(8,128)(2,1)} %get-tuple-element.141), channel_id=1, source_target_pairs={{0,2},{2,0},{4,6},{6,4},{8,10},{10,8},{12,14},{14,12},{16,18},{18,... | collective-permute-start | bytes 786440 | tf_op jit(solution)/shard_map/ppermute | solution.py:99
  155.8 13.0 %collective-permute-start.28 = (bf16[128,1024]{1,0:T(8,128)(2,1)}, bf16[128,1024]{1,0:T(8,128)(2,1)S(1)}, u32[]{:S(2)}, u32[]{:S(2)}) collective-permute-start(bf16[128,1024]{1,0:T(8,128)(2,1)} %get-tuple-element.142), channel_id=1, source_target_pairs={{0,4},{2,6},{4,0},{6,2},{8,12},{10,14},{12,8},{14,10},{16,20},{18,... | collective-permute-start | bytes 786440 | tf_op jit(solution)/shard_map/ppermute | solution.py:99
  157.2 12.5 %collective-permute-start.29 = (bf16[128,1024]{1,0:T(8,128)(2,1)}, bf16[128,1024]{1,0:T(8,128)(2,1)S(1)}, u32[]{:S(2)}, u32[]{:S(2)}) collective-permute-start(bf16[128,1024]{1,0:T(8,128)(2,1)} %get-tuple-element.143), channel_id=1, source_target_pairs={{0,6},{2,4},{4,2},{6,0},{8,14},{10,12},{12,10},{14,8},{16,22},{18,... | collective-permute-start | bytes 786440 | tf_op jit(solution)/shard_map/ppermute | solution.py:99
  175.9 9.2 %collective-permute-start.30 = (bf16[128,1024]{1,0:T(8,128)(2,1)S(1)}, bf16[128,1024]{1,0:T(8,128)(2,1)S(1)}, u32[]{:S(2)}, u32[]{:S(2)}) collective-permute-start(bf16[128,1024]{1,0:T(8,128)(2,1)S(1)} %get-tuple-element.149), channel_id=1, source_target_pairs={{0,2},{2,0},{4,6},{6,4},{8,10},{10,8},{12,14},{14,12},{16,18},{18,... | collective-permute-start | bytes 786440 | tf_op jit(solution)/shard_map/ppermute | solution.py:99
  177.3 13.2 %collective-permute-start.31 = (bf16[128,1024]{1,0:T(8,128)(2,1)S(1)}, bf16[128,1024]{1,0:T(8,128)(2,1)S(1)}, u32[]{:S(2)}, u32[]{:S(2)}) collective-permute-start(bf16[128,1024]{1,0:T(8,128)(2,1)S(1)} %get-tuple-element.149), channel_id=1, source_target_pairs={{0,4},{2,6},{4,0},{6,2},{8,12},{10,14},{12,8},{14,10},{16,20},{18,... | collective-permute-start | bytes 786440 | tf_op jit(solution)/shard_map/ppermute | solution.py:99
  178.8 11.9 %collective-permute-start.26 = (bf16[512,1024]{1,0:T(8,128)(2,1)}, bf16[512,1024]{1,0:T(8,128)(2,1)}, u32[]{:S(2)}, u32[]{:S(2)}) collective-permute-start(bf16[512,1024]{1,0:T(8,128)(2,1)} %get-tuple-element.146), channel_id=1, source_target_pairs={{0,1},{1,0},{2,3},{3,2},{4,5},{5,4},{6,7},{7,6},{8,9},{9,8},{10,11... | collective-permute-start | bytes 3145736 | tf_op jit(solution)/shard_map/ppermute | solution.py:108
  178.8 11.8 %collective-permute-start.32 = (bf16[128,1024]{1,0:T(8,128)(2,1)S(1)}, bf16[128,1024]{1,0:T(8,128)(2,1)S(1)}, u32[]{:S(2)}, u32[]{:S(2)}) collective-permute-start(bf16[128,1024]{1,0:T(8,128)(2,1)S(1)} %get-tuple-element.149), channel_id=1, source_target_pairs={{0,6},{2,4},{4,2},{6,0},{8,14},{10,12},{12,10},{14,8},{16,22},{18,... | collective-permute-start | bytes 786440 | tf_op jit(solution)/shard_map/ppermute | solution.py:99
  190.7 3.8 %collective-permute-start.33 = (bf16[512,1024]{1,0:T(8,128)(2,1)S(1)}, bf16[512,1024]{1,0:T(8,128)(2,1)}, u32[]{:S(2)}, u32[]{:S(2)}) collective-permute-start(bf16[512,1024]{1,0:T(8,128)(2,1)S(1)} %constant_dynamic-update-slice_fusion.8.refs_9_), channel_id=1, source_target_pairs={{0,1},{1,0},{2,3},{3,2},{4,5},{5,4},{6,7},{7,6},{8,9},{9,8},{10,11... | collective-permute-start | bytes 3145736 | tf_op jit(solution)/shard_map/ppermute | solution.py:108
  194.4 19.6 %collective-permute-start.34 = (bf16[192,1024]{1,0:T(8,128)(2,1)}, bf16[192,1024]{1,0:T(8,128)(2,1)S(1)}, u32[]{:S(2)}, u32[]{:S(2)}) collective-permute-start(bf16[192,1024]{1,0:T(8,128)(2,1)} %get-tuple-element.153), channel_id=1, source_target_pairs={{0,2},{2,0},{4,6},{6,4},{8,10},{10,8},{12,14},{14,12},{16,18},{18,... | collective-permute-start | bytes 1179656 | tf_op jit(solution)/shard_map/ppermute | solution.py:99
  195.6 18.4 %collective-permute-start.35 = (bf16[192,1024]{1,0:T(8,128)(2,1)}, bf16[192,1024]{1,0:T(8,128)(2,1)S(1)}, u32[]{:S(2)}, u32[]{:S(2)}) collective-permute-start(bf16[192,1024]{1,0:T(8,128)(2,1)} %get-tuple-element.154), channel_id=1, source_target_pairs={{0,4},{2,6},{4,0},{6,2},{8,12},{10,14},{12,8},{14,10},{16,20},{18,... | collective-permute-start | bytes 1179656 | tf_op jit(solution)/shard_map/ppermute | solution.py:99
  196.3 18.9 %collective-permute-start.36 = (bf16[192,1024]{1,0:T(8,128)(2,1)}, bf16[192,1024]{1,0:T(8,128)(2,1)S(1)}, u32[]{:S(2)}, u32[]{:S(2)}) collective-permute-start(bf16[192,1024]{1,0:T(8,128)(2,1)} %get-tuple-element.155), channel_id=1, source_target_pairs={{0,6},{2,4},{4,2},{6,0},{8,14},{10,12},{12,10},{14,8},{16,22},{18,... | collective-permute-start | bytes 1179656 | tf_op jit(solution)/shard_map/ppermute | solution.py:99
  214.0 20.7 %copy-start.10 = (bf16[192,1024]{1,0:T(8,128)(2,1)}, bf16[192,1024]{1,0:T(8,128)(2,1)S(1)}, u32[]{:S(2)}) copy-start(bf16[192,1024]{1,0:T(8,128)(2,1)S(1)} %collective-permute-done.34.refs_1_) | copy-start | bytes 1179652
  214.0 20.7 %copy-start.11 = (bf16[192,1024]{1,0:T(8,128)(2,1)}, bf16[192,1024]{1,0:T(8,128)(2,1)S(1)}, u32[]{:S(2)}) copy-start(bf16[192,1024]{1,0:T(8,128)(2,1)S(1)} %collective-permute-done.35.refs_2_) | copy-start | bytes 1179652
  217.8 20.4 %copy-start.38 = (bf16[272,384]{1,0:T(8,128)(2,1)S(1)}, bf16[272,384]{1,0:T(8,128)(2,1)}, u32[]{:S(2)}) copy-start(bf16[272,384]{1,0:T(8,128)(2,1)} %get-tuple-element.180) | copy-start | bytes 626692
  217.8 43.0 %copy-start.27 = (f32[1024]{0:T(1024)S(1)}, f32[1024]{0:T(1024)}, u32[]{:S(2)}) copy-start(f32[1024]{0:T(1024)} %param.16) | copy-start | bytes 12292
  217.8 12.6 %collective-permute-start.39 = (bf16[512,1024]{1,0:T(8,128)(2,1)}, bf16[512,1024]{1,0:T(8,128)(2,1)S(1)}, u32[]{:S(2)}, u32[]{:S(2)}) collective-permute-start(bf16[512,1024]{1,0:T(8,128)(2,1)} %get-tuple-element.172), channel_id=1, source_target_pairs={{0,1},{1,0},{2,3},{3,2},{4,5},{5,4},{6,7},{7,6},{8,9},{9,8},{10,11... | collective-permute-start | bytes 3145736 | tf_op jit(solution)/shard_map/ppermute | solution.py:108
  217.8 9.9 %collective-permute-start.37 = (bf16[272,384]{1,0:T(8,128)(2,1)S(1)}, bf16[272,384]{1,0:T(8,128)(2,1)S(1)}, u32[]{:S(2)}, u32[]{:S(2)}) collective-permute-start(bf16[272,384]{1,0:T(8,128)(2,1)S(1)} %copy-done.40), channel_id=1, source_target_pairs={{0,8},{2,10},{4,12},{6,14},{8,16},{10,18},{12,20},{14,22},{16,24},... | collective-permute-start | bytes 626696 | tf_op jit(solution)/shard_map/ppermute | solution.py:104
  217.9 12.5 %collective-permute-start.38 = (bf16[272,384]{1,0:T(8,128)(2,1)S(1)}, bf16[272,384]{1,0:T(8,128)(2,1)S(1)}, u32[]{:S(2)}, u32[]{:S(2)}) collective-permute-start(bf16[272,384]{1,0:T(8,128)(2,1)S(1)} %copy-done.39), channel_id=1, source_target_pairs={{0,24},{2,26},{4,28},{6,30},{8,0},{10,2},{12,4},{14,6},{16,8},{18,... | collective-permute-start | bytes 626696 | tf_op jit(solution)/shard_map/ppermute | solution.py:104
  227.7 26.8 %copy-start.20 = (bf16[272,384]{1,0:T(8,128)(2,1)}, bf16[272,384]{1,0:T(8,128)(2,1)S(1)}, u32[]{:S(2)}) copy-start(bf16[272,384]{1,0:T(8,128)(2,1)S(1)} %collective-permute-done.37.refs_0_) | copy-start | bytes 626692
  230.4 24.2 %copy-start.21 = (bf16[272,384]{1,0:T(8,128)(2,1)}, bf16[272,384]{1,0:T(8,128)(2,1)S(1)}, u32[]{:S(2)}) copy-start(bf16[272,384]{1,0:T(8,128)(2,1)S(1)} %collective-permute-done.38.refs_2_) | copy-start | bytes 626692
  234.7 32.4 %copy-start.8 = (f32[128,1024]{1,0:T(8,128)S(1)}, f32[128,1024]{1,0:T(8,128)}, u32[]{:S(2)}) copy-start(f32[128,1024]{1,0:T(8,128)} %get-tuple-element.173) | copy-start | bytes 1572868
  234.7 12.3 %collective-permute-start.40 = (bf16[192,1024]{1,0:T(8,128)(2,1)}, bf16[192,1024]{1,0:T(8,128)(2,1)S(1)}, u32[]{:S(2)}, u32[]{:S(2)}) collective-permute-start(bf16[192,1024]{1,0:T(8,128)(2,1)} %get-tuple-element.174), channel_id=1, source_target_pairs={{0,2},{2,0},{4,6},{6,4},{8,10},{10,8},{12,14},{14,12},{16,18},{18,... | collective-permute-start | bytes 1179656 | tf_op jit(solution)/shard_map/ppermute | solution.py:99
  235.6 18.9 %collective-permute-start.41 = (bf16[192,1024]{1,0:T(8,128)(2,1)}, bf16[192,1024]{1,0:T(8,128)(2,1)S(1)}, u32[]{:S(2)}, u32[]{:S(2)}) collective-permute-start(bf16[192,1024]{1,0:T(8,128)(2,1)} %get-tuple-element.175), channel_id=1, source_target_pairs={{0,4},{2,6},{4,0},{6,2},{8,12},{10,14},{12,8},{14,10},{16,20},{18,... | collective-permute-start | bytes 1179656 | tf_op jit(solution)/shard_map/ppermute | solution.py:99
  237.1 23.8 %collective-permute-start.42 = (bf16[192,1024]{1,0:T(8,128)(2,1)}, bf16[192,1024]{1,0:T(8,128)(2,1)S(1)}, u32[]{:S(2)}, u32[]{:S(2)}) collective-permute-start(bf16[192,1024]{1,0:T(8,128)(2,1)} %get-tuple-element.176), channel_id=1, source_target_pairs={{0,6},{2,4},{4,2},{6,0},{8,14},{10,12},{12,10},{14,8},{16,22},{18,... | collective-permute-start | bytes 1179656 | tf_op jit(solution)/shard_map/ppermute | solution.py:99
  238.3 16.3 %collective-permute-start.43 = (bf16[272,384]{1,0:T(8,128)(2,1)S(1)}, bf16[272,384]{1,0:T(8,128)(2,1)S(1)}, u32[]{:S(2)}, u32[]{:S(2)}) collective-permute-start(bf16[272,384]{1,0:T(8,128)(2,1)S(1)} %copy-done.38), channel_id=1, source_target_pairs={{0,16},{2,18},{4,20},{6,22},{8,24},{10,26},{12,28},{14,30},{16,0},... | collective-permute-start | bytes 626696 | tf_op jit(solution)/shard_map/ppermute | solution.py:104
  247.0 21.2 %copy-start.5 = (bf16[192,1024]{1,0:T(8,128)(2,1)}, bf16[192,1024]{1,0:T(8,128)(2,1)S(1)}, u32[]{:S(2)}) copy-start(bf16[192,1024]{1,0:T(8,128)(2,1)S(1)} %collective-permute-done.40.refs_5_) | copy-start | bytes 1179652
  257.4 5.0 %collective-permute-start.44 = (bf16[80,384]{1,0:T(8,128)(2,1)}, bf16[80,384]{1,0:T(8,128)(2,1)S(1)}, u32[]{:S(2)}, u32[]{:S(2)}) collective-permute-start(bf16[80,384]{1,0:T(8,128)(2,1)} %get-tuple-element.182), channel_id=1, source_target_pairs={{0,2},{2,0},{4,6},{6,4},{8,10},{10,8},{12,14},{14,12},{16,18},{18,... | collective-permute-start | bytes 184328 | tf_op jit(solution)/shard_map/ppermute | solution.py:99
  257.4 5.0 %collective-permute-start.45 = (bf16[80,384]{1,0:T(8,128)(2,1)}, bf16[80,384]{1,0:T(8,128)(2,1)S(1)}, u32[]{:S(2)}, u32[]{:S(2)}) collective-permute-start(bf16[80,384]{1,0:T(8,128)(2,1)} %get-tuple-element.183), channel_id=1, source_target_pairs={{0,4},{2,6},{4,0},{6,2},{8,12},{10,14},{12,8},{14,10},{16,20},{18,... | collective-permute-start | bytes 184328 | tf_op jit(solution)/shard_map/ppermute | solution.py:99
  259.4 5.3 %collective-permute-start.46 = (bf16[80,384]{1,0:T(8,128)(2,1)}, bf16[80,384]{1,0:T(8,128)(2,1)S(1)}, u32[]{:S(2)}, u32[]{:S(2)}) collective-permute-start(bf16[80,384]{1,0:T(8,128)(2,1)} %get-tuple-element.184), channel_id=1, source_target_pairs={{0,6},{2,4},{4,2},{6,0},{8,14},{10,12},{12,10},{14,8},{16,22},{18,... | collective-permute-start | bytes 184328 | tf_op jit(solution)/shard_map/ppermute | solution.py:99
  267.1 4.2 %collective-permute-start.47 = (f32[8,384]{1,0:T(8,128)}, f32[8,384]{1,0:T(8,128)S(1)}, u32[]{:S(2)}, u32[]{:S(2)}) collective-permute-start(f32[8,384]{1,0:T(8,128)} %get-tuple-element.185), channel_id=1, source_target_pairs={{0,1},{1,0},{2,3},{3,2},{4,5},{5,4},{6,7},{7,6},{8,9},{9,8},{10,11... | collective-permute-start | bytes 36872 | tf_op jit(solution)/shard_map/ppermute | solution.py:108
  (29 other events, 127.0 us)
Sparse Core Ops, SparseCore 0:
  47.0 44.1 all-gather.4
  92.7 35.8 all-gather.2
  132.6 43.2 reduce-scatter.2
  178.1 34.5 reduce-scatter.4

commit v8 on v6

--- a/solution.py
+++ b/solution.py
@@ -151,17 +151,13 @@
     return (2, rows // 2) if rows % 32 == 0 else (1, max(rows, 16))
 
 
-def pack_kernel(where_ref, lengths_ref, w_q, w_k, w_v, w_o, w_g, w_u, w_d, *outs):
+def pack_attn_kernel(where_ref, lengths_ref, w_q, w_k, w_v, w_o, *outs):
     rows = w_q.shape[0]
     parts, high = attn_rows(rows)
-    tall = max(rows, 16)
-    big = w_g.shape[1] // LANES // PLANE * LANES
-    last = w_g.shape[1] // LANES // PLANE * PLANE
     place = where_ref[0]
     lane = lane_ids((rows, LANES))
-    for mask in range(PLANE):
+    for mask, out in enumerate(outs):
         other = place ^ mask
-        out, second = outs[mask], outs[PLANE + mask]
         at = pl.multiple_of(other * LANES, LANES)
         tile = jnp.where(
             lane < HALF, half_tile(w_k, 0, other, False), half_tile(w_v, 0, other, True)
@@ -181,22 +177,24 @@
             marks = jnp.where(ids == free - LANES + slot, lengths_ref[0, slot].astype(float32), marks)
         out[:, parts * width :] = marks.astype(bfloat16)
 
-        at = pl.multiple_of(other * big, LANES)
-        small = jnp.where(
-            lane < HALF, half_tile(w_g, last, other, False), half_tile(w_u, last, other, True)
+
+def pack_ffn_kernel(where_ref, w_g, w_u, w_d, *outs):
+    rows = w_g.shape[0]
+    big = w_g.shape[1] // LANES // PLANE * LANES
+    last = w_g.shape[1] // LANES // PLANE * PLANE
+    place = where_ref[0]
+    lane = lane_ids((rows, LANES))
+    for mask, out in enumerate(outs):
+        other = place ^ mask
+        at = pl.ds(pl.multiple_of(other * big, LANES), big)
+        parts = [w[:, at].astype(float32) for w in (w_g, w_u, w_d)]
+        parts.append(
+            jnp.where(
+                lane < HALF, half_tile(w_g, last, other, False), half_tile(w_u, last, other, True)
+            )
         )
-        small_down = jnp.where(lane < HALF, half_tile(w_d, last, other, False), 0.0)
-        upper = jnp.concatenate(
-            [w_g[:, pl.ds(at, big)].astype(float32), w_u[:, pl.ds(at, big)].astype(float32)], axis=1
-        )
-        lower = jnp.concatenate(
-            [w_d[:, pl.ds(at, big)].astype(float32), small, small_down], axis=1
-        )
-        second[:tall, :] = padded(upper, tall).astype(bfloat16)
-        second[tall:, : lower.shape[1]] = padded(lower, tall).astype(bfloat16)
-        second[tall:, lower.shape[1] :] = jnp.zeros(
-            (tall, second.shape[1] - lower.shape[1]), bfloat16
-        )
+        parts.append(jnp.where(lane < HALF, half_tile(w_d, last, other, False), 0.0))
+        out[...] = padded(jnp.concatenate(parts, axis=1), out.shape[0]).astype(bfloat16)
 
 
 def unpack_attn_kernel(where_ref, own, one, two, three, attn_out, lens_out, held):
@@ -217,13 +215,10 @@
 
 def unpack_ffn_kernel(where_ref, own, one, two, three, ffn_out, held):
     rows = ffn_out.shape[0] // PLANE
-    tall = max(rows, 16)
     place = where_ref[0]
     for mask, message in enumerate((own, one, two, three)):
         at = pl.ds(pl.multiple_of((place ^ mask) * rows, rows), rows)
-        full = message.shape[1]
-        held[at, :full] = message[:tall, :].astype(float32)[:rows]
-        held[at, full:] = message[tall:, : held.shape[1] - full].astype(float32)[:rows]
+        held[at, :] = message[...].astype(float32)[:rows]
     ffn_out[...] = held[...].astype(bfloat16)
 
 
@@ -276,11 +271,17 @@
     return pl.ds(pl.multiple_of(at, rows), rows)
 
 
-def attn_kernel(where_ref, ends_ref, tok_m, tok_o, a_gain, q_gain, k_gain, cos, sin, weight, *refs):
-    send, keep, pre_out, low_out, mixed_out, held = refs
+def attn_kernel(layers, where_ref, ends_ref, tok_m, tok_o, a_gain, q_gain, k_gain, cos, sin, *refs):
+    pieces, refs = refs[:layers], refs[layers:]
+    send, keep, pre_out, low_out, mixed_out, weight, held = refs
     group = pl.program_id(0)
-    core = where_ref[2]
+    depth, core = where_ref[1], where_ref[2]
     local = tok_m.shape[0]
+
+    @pl.when(group == 0)
+    def _():
+        for step, piece in enumerate(pieces):
+            weight[deep_rows(depth, -step, layers, piece.shape[0]), :] = piece[...]
 
     x = group_rows(core, tok_m[...].astype(float32), tok_o[...].astype(float32))
     normed = (x * inverse_rms(x) * a_gain[...]).astype(bfloat16)
@@ -313,12 +314,14 @@
 
 
 def attn_back_kernel(
-    where_ref, ends_ref, tok_m, tok_o, a_gain, q_gain, k_gain, cos, sin, dh_m, dh_o,
+    layers, where_ref, ends_ref, tok_m, tok_o, a_gain, q_gain, k_gain, cos, sin, dh_m, dh_o,
     pre_ref, low_ref, mixed_ref, weight, gain_ffn, *refs,
 ):
-    send, keep, grad_out, gains_out, held, total, sum_a, sum_qk = refs
+    send, keep, own, gains_out = refs[:4]
+    pieces = refs[4 : 3 + layers]
+    held, total, sum_a, sum_qk = refs[3 + layers :]
     group = pl.program_id(0)
-    core = where_ref[2]
+    depth, core = where_ref[1], where_ref[2]
     local = tok_m.shape[0]
 
     @pl.when(group == 0)
@@ -385,7 +388,15 @@
         qk_sum = jnp.where(lane_ids(q_sum.shape) < HALF, q_sum, k_sum)
         ids = lax.broadcasted_iota(jnp.int32, (GAIN_ROWS, LANES), 0)
         gains_out[:, 2 * LANES :] = jnp.where(ids == 0, qk_sum, 0.0)
-        grad_out[...] = total[...].astype(bfloat16)
+        gains = gains_out[...]
+        top = gains.astype(bfloat16)
+        rest = (gains - top.astype(float32)).astype(bfloat16)
+        tail = jnp.concatenate([top.astype(float32), rest.astype(float32)], axis=0).astype(bfloat16)
+        rows = own.shape[0]
+        own[...] = total[deep_rows(depth, 0, layers, rows), :]
+        for index, piece in enumerate(pieces):
+            piece[:rows, :] = total[deep_rows(depth, index + 1, layers, rows), :].astype(bfloat16)
+            piece[rows:, :] = tail
 
 
 def attn_specs(rows, width, group_height):
@@ -402,46 +413,53 @@
     return pl.BlockSpec(shape, lambda i: (0, 0), pipeline_mode=pl.Buffered(1))
 
 
-def attn(where, ends, tok_mine, tok_other, gains, tables, weight):
+def attn(where, ends, tok_mine, tok_other, gains, tables, pieces):
+    layers = len(pieces)
     rows, width = tok_mine.shape
     local = rows // PLANE
     scalar, block, gain, small, table, wide = attn_specs(local, width, 2 * local)
+    high, columns = pieces[0].shape
+    weight = (layers * high, columns)
     return pl.pallas_call(
-        attn_kernel,
+        lambda *refs: attn_kernel(layers, *refs),
         grid=(PLANE,),
         in_specs=[scalar, scalar, block, block, gain, small, small, table, table]
-        + [whole_spec(weight.shape)],
-        out_specs=[block, block, wide, wide, table],
+        + [whole_spec((high, columns))] * layers,
+        out_specs=[block, block, wide, wide, table, whole_spec(weight)],
         out_shape=[
             jax.ShapeDtypeStruct((rows, width), bfloat16),
             jax.ShapeDtypeStruct((rows, width), float32),
             jax.ShapeDtypeStruct((2 * rows, 2 * LANES), float32),
             jax.ShapeDtypeStruct((2 * rows, 2 * LANES), bfloat16),
             jax.ShapeDtypeStruct((2 * rows, LANES), bfloat16),
+            jax.ShapeDtypeStruct(weight, bfloat16),
         ],
         scratch_shapes=[pltpu.VMEM((2 * local, width), float32)],
         compiler_params=pltpu.CompilerParams(vmem_limit_bytes=VMEM_BYTES),
         cost_estimate=cost(36),
-    )(where, ends, tok_mine, tok_other, *gains, *tables, weight)
-
-
-def attn_back(where, ends, tok_mine, tok_other, gains, tables, dh, saved, weight, gain_ffn):
+    )(where, ends, tok_mine, tok_other, *gains, *tables, *pieces)
+
+
+def attn_back(where, ends, layers, tok_mine, tok_other, gains, tables, dh, saved, weight, gain_ffn):
     rows, width = tok_mine.shape
     local = rows // PLANE
     scalar, block, gain, small, table, wide = attn_specs(local, width, 2 * local)
-    columns = weight.shape[1]
+    high, columns = weight.shape[0] // layers, weight.shape[1]
+    tail = 2 * GAIN_ROWS
     return pl.pallas_call(
-        attn_back_kernel,
+        lambda *refs: attn_back_kernel(layers, *refs),
         grid=(PLANE,),
         in_specs=[scalar, scalar, block, block, gain, small, small, table, table, block, block]
         + [wide, wide, table, whole_spec(weight.shape), gain],
-        out_specs=[block, block, whole_spec(weight.shape), whole_spec((GAIN_ROWS, columns))],
+        out_specs=[block, block, whole_spec((high, columns)), whole_spec((GAIN_ROWS, columns))]
+        + [whole_spec((high + tail, columns))] * (layers - 1),
         out_shape=[
             jax.ShapeDtypeStruct((rows, width), bfloat16),
             jax.ShapeDtypeStruct((rows, width), float32),
-            jax.ShapeDtypeStruct(weight.shape, bfloat16),
+            jax.ShapeDtypeStruct((high, columns), float32),
             jax.ShapeDtypeStruct((GAIN_ROWS, columns), float32),
-        ],
+        ]
+        + [jax.ShapeDtypeStruct((high + tail, columns), bfloat16)] * (layers - 1),
         scratch_shapes=[
             pltpu.VMEM((2 * local, width), float32),
             pltpu.VMEM(weight.shape, float32),
@@ -449,7 +467,7 @@
             pltpu.VMEM((8, LANES), float32),
         ],
         compiler_params=pltpu.CompilerParams(vmem_limit_bytes=VMEM_BYTES),
-        cost_estimate=cost(58),
+        cost_estimate=cost(24),
     )(where, ends, tok_mine, tok_other, *gains, *tables, *dh, *saved, weight, gain_ffn)
 
 
@@ -551,8 +569,12 @@
     return call(chip_sum_kernel, outs, keep, received)
 
 
+def plane_sent(parts):
+    return [parts[0]] + [send_plane(part, mask + 1) for mask, part in enumerate(parts[1:])]
+
+
 def plane_total(parts):
-    return add_up([parts[0]] + [send_plane(part, mask + 1) for mask, part in enumerate(parts[1:])])
+    return add_up(plane_sent(parts))
 
 
 def add_up(parts):
@@ -610,22 +632,29 @@
     return jnp.concatenate([top, rest], axis=0)
 
 
-def split_attn_kernel(where_ref, own, gains, *refs):
+def plane_sum_attn_kernel(where_ref, own, gains, *refs):
     received, outs = refs[: -PLANE - 2], refs[-PLANE - 2 : -2]
     held, held_gains = refs[-2:]
     layers = len(received) + 1
+    value = own[...]
+    high = own.shape[0]
     depth = where_ref[1]
-    for step, part in enumerate((gains,) + received):
-        held_gains[deep_rows(depth, -step, layers, GAIN_ROWS), :] = part[...]
-    held[...] = own[...].astype(float32)
+    held_gains[deep_rows(depth, 0, layers, GAIN_ROWS), :] = joined_gains(split_gains(gains[...]))
+    for step, part in enumerate(received):
+        value = value + part[:high, :].astype(float32)
+        held_gains[deep_rows(depth, -1 - step, layers, GAIN_ROWS), :] = joined_gains(
+            part[high:, :].astype(float32)
+        )
+    held[...] = value
     sums = held_gains[:GAIN_ROWS, :]
     for layer in range(1, layers):
         sums = sums + held_gains[layer * GAIN_ROWS : (layer + 1) * GAIN_ROWS, :]
     tail = split_gains(sums)
     place = where_ref[0]
-    rows = own.shape[0] // PLANE
+    rows = high // PLANE
     for mask, out in enumerate(outs):
-        part = held[pl.ds(pl.multiple_of((place ^ mask) * rows, rows), rows), :]
+        at = pl.multiple_of((place ^ mask) * rows, rows)
+        part = held[pl.ds(at, rows), :]
         if mask:
             tall = out.shape[0] - tail.shape[0]
             out[:tall, :] = padded(part, tall).astype(bfloat16)
@@ -635,7 +664,7 @@
             out[rows:, :] = tail
 
 
-def split_attn(where, own, gains, received):
+def plane_split_attn(where, own, received, gains):
     rows, columns = own.shape[0] // PLANE, own.shape[1]
     tail = 2 * GAIN_ROWS
     shapes = [((rows + tail, columns), float32)]
@@ -644,7 +673,9 @@
         pltpu.VMEM(own.shape, float32),
         pltpu.VMEM(((len(received) + 1) * GAIN_ROWS, columns), float32),
     ]
-    return call(split_attn_kernel, shapes, where, own, gains, *received, scalars=1, scratch=scratch)
+    return call(
+        plane_sum_attn_kernel, shapes, where, own, gains, *received, scalars=1, scratch=scratch
+    )
 
 
 def pick_place(refs, place, target, columns, rows):
@@ -714,6 +745,21 @@
 
 def gather_rows(local):
     return both_cores(plane_parts(local))
+
+
+def row_tables(lens, slots, total_rows):
+    all_lengths = lens.reshape(PLANE, 8, LANES)[:, 0, :slots].astype(jnp.int32)
+    ends = jnp.cumsum(all_lengths, axis=1, dtype=jnp.int32)
+    row_ids = jnp.arange(total_rows, dtype=jnp.int32)
+    begin = jnp.max(
+        jnp.where(row_ids[None, :, None] >= ends[:, None, :], ends[:, None, :], 0), axis=2
+    )
+    position = (row_ids[None, :] - begin).reshape(-1).astype(jnp.float32)
+    spread = jnp.arange(LANES, dtype=jnp.int32) % (HEAD_DIM // 2)
+    freqs = rope_base ** (-spread.astype(jnp.float32) * 2.0 / HEAD_DIM)
+    angles = position[:, None] * freqs[None, :]
+    sign = jnp.where(jnp.arange(LANES) % HEAD_DIM < HEAD_DIM // 2, -1.0, 1.0).astype(jnp.float32)
+    return ends, (jnp.cos(angles), jnp.sin(angles) * sign)
 
 
 def body(
@@ -749,39 +795,40 @@
     parts, high = attn_rows(rows)
     tall = max(rows, 16)
     first = call(
-        pack_kernel,
-        [((high, model), bfloat16)] * PLANE + [((2 * tall, model), bfloat16)] * PLANE,
+        pack_attn_kernel,
+        [((high, model), bfloat16)] * PLANE,
         where,
         lengths,
         w_query,
         w_key,
         w_value,
         w_out,
+        scalars=2,
+    )
+    second = call(
+        pack_ffn_kernel,
+        [((tall, ff_cols), bfloat16)] * PLANE,
+        where,
         w_gate,
         w_up,
         w_down,
-        scalars=2,
-    )
-    first, second = first[:PLANE], first[PLANE:]
+        scalars=1,
+    )
+    first = [first[0]] + [send_plane(first[m], m) for m in range(1, PLANE)]
     attn_piece, lens = call(
         unpack_attn_kernel,
         [((PLANE * rows, attn_cols), bfloat16), ((PLANE * 8, LANES), float32)],
         where,
-        first[0],
-        *[send_plane(first[m], m) for m in range(1, PLANE)],
+        *first,
         scalars=1,
         scratch=[pltpu.VMEM((PLANE * rows, attn_cols), float32)],
     )
-    columns = [list(range(k, layers * PLANE, PLANE)) for k in range(PLANE)]
-    attn_weight = lax.all_gather(
-        attn_piece, "dp", axis=0, tiled=True, axis_index_groups=columns
-    )
+    attn_pieces = [attn_piece] + [send_deep(attn_piece, step) for step in range(1, layers)]
     tok_parts = plane_parts(tokens)
-    tok_parts = after(attn_piece, tok_parts)
-    second = after(tok_parts, second)
-    tok_mine, tok_other = both_cores(tok_parts)
+    second = after((first, tok_parts), second)
     second = [second[0]] + [send_plane(second[m], m) for m in range(1, PLANE)]
-    cotangent_sent = after(second, cotangent)
+    ends, tables = row_tables(lens, lengths.shape[1], total_rows)
+    second = after((attn_pieces, tables), second)
     (ff_piece,) = call(
         unpack_ffn_kernel,
         [((PLANE * rows, ff_cols), bfloat16)],
@@ -790,24 +837,13 @@
         scalars=1,
         scratch=[pltpu.VMEM((PLANE * rows, ff_cols), float32)],
     )
+    columns = [list(range(k, layers * PLANE, PLANE)) for k in range(PLANE)]
     ff_weight = lax.all_gather(ff_piece, "dp", axis=0, tiled=True, axis_index_groups=columns)
-    cot_parts = plane_parts(cotangent_sent)
+    attn_pieces = after(ff_piece, attn_pieces)
+    cot_parts = plane_parts(after(second, cotangent))
+    tok_mine, tok_other = both_cores(tok_parts)
     cot_mine, cot_other = both_cores(cot_parts)
-    attn_weight = after(ff_piece, attn_weight)
-
-    slots = lengths.shape[1]
-    all_lengths = lens.reshape(PLANE, 8, LANES)[:, 0, :slots].astype(jnp.int32)
-    ends = jnp.cumsum(all_lengths, axis=1, dtype=jnp.int32)
-    row_ids = jnp.arange(total_rows, dtype=jnp.int32)
-    begin = jnp.max(
-        jnp.where(row_ids[None, :, None] >= ends[:, None, :], ends[:, None, :], 0), axis=2
-    )
-    position = (row_ids[None, :] - begin).reshape(-1).astype(jnp.float32)
-    spread = jnp.arange(LANES, dtype=jnp.int32) % (HEAD_DIM // 2)
-    freqs = rope_base ** (-spread.astype(jnp.float32) * 2.0 / HEAD_DIM)
-    angles = position[:, None] * freqs[None, :]
-    sign = jnp.where(jnp.arange(LANES) % HEAD_DIM < HEAD_DIM // 2, -1.0, 1.0).astype(jnp.float32)
-    tables = (jnp.cos(angles), jnp.sin(angles) * sign)
+
     gains = (
         attn_gain[None, :],
         jnp.concatenate([query_gain, query_gain])[None, :],
@@ -817,7 +853,9 @@
     inputs = tokens.astype(jnp.float32)
     factor_a = inverse_rms(inputs)
     unit_a = inputs * factor_a
-    send, keep, *saved = attn(where, ends, tok_mine, tok_other, gains, tables, attn_weight)
+    send, keep, *saved, attn_weight = attn(
+        where, ends, tok_mine, tok_other, gains, tables, attn_pieces
+    )
     send = after(cot_parts, send)
     hidden = inputs + plane_total(chip_sum(keep, swap_cores(send)))
     factor_b = inverse_rms(hidden)
@@ -827,41 +865,38 @@
     out_send, out_keep, dn_send, dn_keep, ff_grad = ffn(
         where, ends, x_mine, x_other, cot_mine, cot_other, ff_weight
     )
+    own_ff = lax.psum_scatter(
+        ff_grad, "dp", scatter_dimension=0, tiled=True, axis_index_groups=columns
+    )
     dn_parts = chip_sum(dn_keep, swap_cores(dn_send))
     out_keep = after(dn_parts, out_keep)
     d_normed2 = plane_total(dn_parts)
     grad_out = jnp.where(
-        (jnp.arange(local_rows) + core * local_rows < ends[0, slots - 1])[:, None],
+        (jnp.arange(local_rows) + core * local_rows < ends[0, lengths.shape[1] - 1])[:, None],
         cotangent,
         jnp.zeros_like(cotangent),
     )
     gain_ffn = jnp.sum(d_normed2 * unit_b, axis=0)
     d_hidden = grad_out.astype(jnp.float32) + norm_back(d_normed2 * ffn_gain, unit_b, factor_b)
     h_mine, h_other = gather_rows(d_hidden.astype(jnp.bfloat16))
-    own_ff = lax.psum_scatter(
-        ff_grad, "dp", scatter_dimension=0, tiled=True, axis_index_groups=columns
-    )
     out_parts = chip_sum(out_keep, swap_cores(out_send))
     out_parts = after((h_mine, h_other), out_parts)
-    ffn_branch = plane_total(out_parts)
-    block_out = (hidden + ffn_branch).astype(jnp.bfloat16)
-
-    send, keep, attn_grad, part_gains = attn_back(
-        where, ends, tok_mine, tok_other, gains, tables, (h_mine, h_other), saved, attn_weight,
-        gain_ffn[None, :],
-    )
-    send, keep, attn_grad, part_gains = after(block_out, (send, keep, attn_grad, part_gains))
-    own_attn = lax.psum_scatter(
-        attn_grad, "dp", scatter_dimension=0, tiled=True, axis_index_groups=columns
-    )
-    far_gains = [send_deep(part_gains, step) for step in range(1, layers)]
+    out_parts = plane_sent(out_parts)
+    block_out = (hidden + add_up(out_parts)).astype(jnp.bfloat16)
+
+    send, keep, own_attn, part_gains, *attn_grads = after(
+        out_parts,
+        attn_back(
+            where, ends, layers, tok_mine, tok_other, gains, tables, (h_mine, h_other), saved,
+            attn_weight, gain_ffn[None, :],
+        ),
+    )
+    attn_grads = [send_deep(piece, step + 1) for step, piece in enumerate(attn_grads)]
     own_dn, own_ff, *messages = tail_messages(where, keep, swap_cores(send), own_ff)
+    own_attn = after(messages, own_attn)
     messages = [send_plane(part, mask + 1) for mask, part in enumerate(messages)]
-    own_attn = after(messages, own_attn)
-    attn_parts = split_attn(where, own_attn, part_gains, far_gains)
-    attn_parts = [attn_parts[0]] + [
-        send_plane(part, mask + 1) for mask, part in enumerate(attn_parts[1:])
-    ]
+    attn_parts = plane_split_attn(where, own_attn, attn_grads, part_gains)
+    attn_parts = after(messages[:2], plane_sent(attn_parts))
     d_normed = own_dn + add_up([part[:local_rows] for part in messages])
     grad_tokens = d_hidden + norm_back(d_normed * attn_gain, unit_a, factor_a)
     grad_gate, grad_up, grad_down = call(

time: 285 us -> 264 us (0.926)
  blocking collectives: 29.1 us -> 0 us
  starting transfers between devices: 46.1 us -> 51 us
  Pallas kernels: 72.4 us -> 75.4 us
    all_gather x1 -> x0, blocking collectives: 29.1 us -> none  [body(): lax.all_gather(attn_piece, 'dp', axis=0, tiled=True, axis_index_groups=co...]
    ppermute x3 -> x6, waiting for transfers between devices: 0.01 us -> 14.1 us  [send_deep(): lax.ppermute(values, 'dp', [(i, (i + PLANE * step) % count) for i in rang...]
    ppermute x33, waiting for transfers between devices: 76.3 us -> 62.3 us  [send_plane(): return lax.ppermute(values, 'dp', [(i, i ^ mask) for i in range(count)])]
    all_gather x1, waiting for transfers between devices: 0.01 us -> 13.7 us  [body(): lax.all_gather(ff_piece, 'dp', axis=0, tiled=True, axis_index_groups=colu...]
    reduce_scatter x1 -> x0, waiting for transfers between devices: 6.36 us -> none  [body(): lax.psum_scatter(attn_grad, 'dp', scatter_dimension=0, tiled=True, axis_i...]
    ppermute x3 -> x6, starting transfers between devices: 4.14 us -> 8.73 us  [send_deep(): lax.ppermute(values, 'dp', [(i, (i + PLANE * step) % count) for i in rang...]
    reduce_scatter x1, waiting for transfers between devices: 3.48 us -> 0.21 us  [body(): lax.psum_scatter(ff_grad, 'dp', scatter_dimension=0, tiled=True, axis_ind...]
    pallas_call x10 -> x11, Pallas kernels: 25.8 us -> 28.1 us  [call(): pl.pallas_call(kernel, out_shape=[jax.ShapeDtypeStruct(shape, kind) for s...]
  transfers between devices with their start and end apart: 48 -> 50, of which waited for: 24 -> 21; matrix products, arithmetic and copies ran while one was open for 5% -> 5% of each run, Pallas kernels for 16% -> 20%
where the time goes in v8:
time: 264 us
  waiting for transfers between devices  97.4 us (37%)
  Pallas kernels  75.4 us (29%)
  starting transfers between devices  51 us (19%)
  between operations  14.5 us (5%)
  local copies, waits for them, and re-layouts  12.9 us (5%)
  other arithmetic  12.3 us (5%)
    ppermute x33, waiting for transfers between devices, send_plane(): return lax.ppermute(values, 'dp', [(i, i ^ mask) for i in range(count)])  62.3 us
    ppermute x33, starting transfers between devices, send_plane(): return lax.ppermute(values, 'dp', [(i, i ^ mask) for i in range(count)])  41.7 us
    pallas_call x11, Pallas kernels, call(): pl.pallas_call(kernel, out_shape=[jax.ShapeDtypeStruct(shape, kind) for s...  28.1 us
    pallas_call x1, Pallas kernels, ffn(): pl.pallas_call(ffn_kernel, grid=(2,), in_specs=[scalar, scalar] + [row_sp...  20.5 us
    pallas_call x1, Pallas kernels, attn_back(): pl.pallas_call(lambda *refs: attn_back_kernel(layers, *refs), grid=(PLANE...  16.3 us
    ppermute x6, waiting for transfers between devices, send_deep(): lax.ppermute(values, 'dp', [(i, (i + PLANE * step) % count) for i in rang...  14.1 us
    all_gather x1, waiting for transfers between devices, body(): lax.all_gather(ff_piece, 'dp', axis=0, tiled=True, axis_index_groups=colu...  13.7 us
    pallas_call x1, Pallas kernels, attn(): pl.pallas_call(lambda *refs: attn_kernel(layers, *refs), grid=(PLANE,), i...  10.6 us
  transfers between devices with their start and end apart: 50, of which 21 were waited for; matrix products, arithmetic and copies ran while one was open for 5% of the time, Pallas kernels for 20%

profile of v8, /device:TPU:0, one launch (start us, length us, event | category | flops | bytes accessed | tf_op | source)
XLA Modules:
  0.0 263.6 jit_solution(17475685760124224921)
XLA Ops:
  7.2 4.0 %collective-permute-start.5 = (bf16[128,1024]{1,0:T(8,128)(2,1)}, bf16[128,1024]{1,0:T(8,128)(2,1)S(1)}, u32[]{:S(2)}, u32[]{:S(2)}) collective-permute-start(bf16[128,1024]{1,0:T(8,128)(2,1)} %param.14), channel_id=1, source_target_pairs={{0,6},{2,4},{4,2},{6,0},{8,14},{10,12},{12,10},{14,8},{16,22},{18,... | collective-permute-start | bytes 786440 | tf_op jit(solution)/shard_map/ppermute | solution.py:99
  12.3 1.7 shard_map.237
  14.1 1.9 collective-permute-start.1
  16.1 1.4 collective-permute-start.2
  17.5 2.2 shard_map.239
  20.1 1.5 collective-permute-start.3
  21.6 4.5 %collective-permute-done.1.two = bf16[32,1024]{1,0:T(8,128)(2,1)S(1)} collective-permute-done((bf16[32,1024]{1,0:T(8,128)(2,1)}, bf16[32,1024]{1,0:T(8,128)(2,1)S(1)}, u32[]{:S(2)}, u32[]{:S(2)}) %collective-permute-start.1) | collective-permute-done | bytes 65568 | tf_op jit(solution)/shard_map/ppermute | solution.py:99
  26.8 1.7 shard_map.238
  28.5 3.8 %collective-permute-start.9 = (bf16[256,384]{1,0:T(8,128)(2,1)}, bf16[256,384]{1,0:T(8,128)(2,1)}, u32[]{:S(2)}, u32[]{:S(2)}) collective-permute-start(bf16[256,384]{1,0:T(8,128)(2,1)} %get-tuple-element.119.refs_9_), channel_id=1, source_target_pairs={{0,24},{2,26},{4,28},{6,30},{8,0},{10,2},{12,4},{14,6},{16,8},{18,... | collective-permute-start | bytes 589832 | tf_op jit(solution)/shard_map/ppermute | solution.py:104
  33.3 1.1 collective-permute-start.7
  34.4 1.5 collective-permute-start.10
  36.7 1.3 collective-permute-done.9.refs_12_
  37.9 1.7 collective-permute-start.12
  39.7 3.0 %fusion.6 = (f32[1024,128]{1,0:T(8,128)}, f32[1024,128]{1,0:T(8,128)}) fusion(f32[128]{0:T(128)S(1)} %get-tuple-element.203, f32[128]{0:T(128)S(1)} %get-tuple-element.204, f32[1024]{0:T(1024)S(1)} %bitcast.28), kind=kLoop, calls=%fused_computation.13 | loop fusion | flops 262144 | bytes 1053696 | tf_op jit(solution)/shard_map/mul | solution.py:762
  42.7 6.6 %collective-permute-done.8.refs_11_ = bf16[256,384]{1,0:T(8,128)(2,1)S(1)} collective-permute-done((bf16[256,384]{1,0:T(8,128)(2,1)}, bf16[256,384]{1,0:T(8,128)(2,1)S(1)}, u32[]{:S(2)}, u32[]{:S(2)}) %collective-permute-start.8) | collective-permute-done | bytes 196640 | tf_op jit(solution)/shard_map/ppermute | solution.py:104
  50.3 2.5 shard_map.240
  54.1 2.0 collective-permute-start.14
  58.2 10.6 %shard_map.241 = (bf16[512,1024]{1,0:T(8,128)(2,1)}, f32[512,1024]{1,0:T(8,128)}, f32[1024,256]{1,0:T(8,128)}, bf16[1024,256]{1,0:T(8,128)(2,1)}, bf16[1024,128]{1,0:T(8,128)(2,1)}, /*index=5*/bf16[1024,384]{1,0:T(8,128)(2,1)}) custom-call(s32[3]{0:T(128)} %pad_add_fusion.where_ref.refs_0_, s32[4,4]{1,0:T(4,128)} %copy-done.32, bf16[512,1024]{1,0:T(8,128)(2,1)} %copy-done, ...), custom_call_target="tpu_custom_call" | custom-call | flops 1024 | bytes 36000000 | tf_op jit(solution)/shard_map/pallas_call | solution.py:423
  70.2 2.9 %collective-permute-done.16.received = bf16[512,1024]{1,0:T(8,128)(2,1)S(1)} collective-permute-done((bf16[512,1024]{1,0:T(8,128)(2,1)}, bf16[512,1024]{1,0:T(8,128)(2,1)S(1)}, u32[]{:S(2)}, u32[]{:S(2)}) %collective-permute-start.16) | collective-permute-done | bytes 1048608 | tf_op jit(solution)/shard_map/ppermute | solution.py:108
  74.0 3.0 %shard_map.242 = (f32[128,1024]{1,0:T(8,128)}, bf16[128,1024]{1,0:T(8,128)(2,1)}, bf16[128,1024]{1,0:T(8,128)(2,1)}, bf16[128,1024]{1,0:T(8,128)(2,1)}) custom-call(f32[512,1024]{1,0:T(8,128)} %get-tuple-element.123.keep, bf16[512,1024]{1,0:T(8,128)(2,1)} %copy-done.11), custom_call_target="tpu_custom_call" | custom-call | flops 1024 | bytes 1024 | tf_op jit(solution)/shard_map/pallas_call | solution.py:114
  77.0 1.6 collective-permute-start.17
  78.7 1.9 collective-permute-start.19
  80.6 5.8 %collective-permute-done.17 = bf16[128,1024]{1,0:T(8,128)(2,1)S(1)} collective-permute-done((bf16[128,1024]{1,0:T(8,128)(2,1)}, bf16[128,1024]{1,0:T(8,128)(2,1)S(1)}, u32[]{:S(2)}, u32[]{:S(2)}) %collective-permute-start.17) | collective-permute-done | bytes 262176 | tf_op jit(solution)/shard_map/ppermute | solution.py:99
  86.4 6.0 %collective-permute-done.18 = bf16[128,1024]{1,0:T(8,128)(2,1)S(1)} collective-permute-done((bf16[128,1024]{1,0:T(8,128)(2,1)}, bf16[128,1024]{1,0:T(8,128)(2,1)S(1)}, u32[]{:S(2)}, u32[]{:S(2)}) %collective-permute-start.18) | collective-permute-done | bytes 262176 | tf_op jit(solution)/shard_map/ppermute | solution.py:99
  92.5 1.3 multiply_reduce_fusion.2
  93.9 1.6 collective-permute-start.22
  96.0 1.5 collective-permute-start.20
  97.7 6.5 %collective-permute-done.22 = bf16[128,1024]{1,0:T(8,128)(2,1)S(1)} collective-permute-done((bf16[128,1024]{1,0:T(8,128)(2,1)S(1)}, bf16[128,1024]{1,0:T(8,128)(2,1)S(1)}, u32[]{:S(2)}, u32[]{:S(2)}) %collective-permute-start.22) | collective-permute-done | bytes 262176 | tf_op jit(solution)/shard_map/ppermute | solution.py:99
  104.2 3.8 %collective-permute-done.21 = bf16[128,1024]{1,0:T(8,128)(2,1)S(1)} collective-permute-done((bf16[128,1024]{1,0:T(8,128)(2,1)S(1)}, bf16[128,1024]{1,0:T(8,128)(2,1)S(1)}, u32[]{:S(2)}, u32[]{:S(2)}) %collective-permute-start.21) | collective-permute-done | bytes 262176 | tf_op jit(solution)/shard_map/ppermute | solution.py:99
  108.2 1.1 copy-done.10
  109.3 1.6 collective-permute-done.23.x_o
  110.9 13.7 %all-gather.2.cloned.1.call-done.weight = bf16[1024,1792]{1,0:T(8,128)(2,1)} async-done(((bf16[256,1792]{1,0:T(8,128)(2,1)}), bf16[1024,1792]{1,0:T(8,128)(2,1)}) %all-gather.2.cloned.1.call-update) | async-done | bytes 3670032 | tf_op jit(solution)/shard_map/all_gather | solution.py:841
  124.6 20.5 %shard_map.243 = (bf16[512,1024]{1,0:T(8,128)(2,1)}, f32[512,1024]{1,0:T(8,128)}, bf16[512,1024]{1,0:T(8,128)(2,1)}, f32[512,1024]{1,0:T(8,128)}, bf16[1024,1792]{1,0:T(8,128)(2,1)}) custom-call(s32[3]{0:T(128)} %pad_add_fusion.where_ref.refs_0_, s32[4,4]{1,0:T(4,128)} %copy-done.32, bf16[512,1024]{1,0:T(8,128)(2,1)} %collective-permute-done.23.x_o, ...), custom_call_target="tpu_custom_call" | custom-call | flops 1024 | bytes 74000000 | tf_op jit(solution)/shard_map/pallas_call | solution.py:541
  145.1 1.2 copy-done.38
  146.3 2.7 %collective-permute-done.25.received = bf16[512,1024]{1,0:T(8,128)(2,1)S(1)} collective-permute-done((bf16[512,1024]{1,0:T(8,128)(2,1)S(1)}, bf16[512,1024]{1,0:T(8,128)(2,1)S(1)}, u32[]{:S(2)}, u32[]{:S(2)}) %collective-permute-start.25) | collective-permute-done | bytes 1048608 | tf_op jit(solution)/shard_map/ppermute | solution.py:108
  149.9 3.1 %shard_map.244 = (f32[128,1024]{1,0:T(8,128)}, bf16[128,1024]{1,0:T(8,128)(2,1)}, bf16[128,1024]{1,0:T(8,128)(2,1)}, bf16[128,1024]{1,0:T(8,128)(2,1)}) custom-call(f32[512,1024]{1,0:T(8,128)} %get-tuple-element.131.keep, bf16[512,1024]{1,0:T(8,128)(2,1)} %copy-done.12), custom_call_target="tpu_custom_call" | custom-call | flops 1024 | bytes 1024 | tf_op jit(solution)/shard_map/pallas_call | solution.py:114
  153.0 1.7 collective-permute-start.26
  154.7 1.5 collective-permute-start.27
  156.5 1.3 slice.28
  158.4 3.9 %collective-permute-done.26 = bf16[128,1024]{1,0:T(8,128)(2,1)S(1)} collective-permute-done((bf16[128,1024]{1,0:T(8,128)(2,1)}, bf16[128,1024]{1,0:T(8,128)(2,1)S(1)}, u32[]{:S(2)}, u32[]{:S(2)}) %collective-permute-start.26) | collective-permute-done | bytes 262176 | tf_op jit(solution)/shard_map/ppermute | solution.py:99
  162.4 6.2 %collective-permute-done.27 = bf16[128,1024]{1,0:T(8,128)(2,1)S(1)} collective-permute-done((bf16[128,1024]{1,0:T(8,128)(2,1)}, bf16[128,1024]{1,0:T(8,128)(2,1)S(1)}, u32[]{:S(2)}, u32[]{:S(2)}) %collective-permute-start.27) | collective-permute-done | bytes 262176 | tf_op jit(solution)/shard_map/ppermute | solution.py:99
  168.6 2.0 multiply_reduce_fusion
  170.9 1.6 collective-permute-start.31
  172.4 1.2 collective-permute-start.30
  174.4 6.7 %collective-permute-done.31 = bf16[128,1024]{1,0:T(8,128)(2,1)S(1)} collective-permute-done((bf16[128,1024]{1,0:T(8,128)(2,1)S(1)}, bf16[128,1024]{1,0:T(8,128)(2,1)S(1)}, u32[]{:S(2)}, u32[]{:S(2)}) %collective-permute-start.31) | collective-permute-done | bytes 262176 | tf_op jit(solution)/shard_map/ppermute | solution.py:99
  181.1 3.7 %collective-permute-done.30 = bf16[128,1024]{1,0:T(8,128)(2,1)S(1)} collective-permute-done((bf16[128,1024]{1,0:T(8,128)(2,1)S(1)}, bf16[128,1024]{1,0:T(8,128)(2,1)S(1)}, u32[]{:S(2)}, u32[]{:S(2)}) %collective-permute-start.30) | collective-permute-done | bytes 262176 | tf_op jit(solution)/shard_map/ppermute | solution.py:99
  185.0 3.2 %shard_map.245 = (f32[128,1024]{1,0:T(8,128)}, bf16[128,1024]{1,0:T(8,128)(2,1)}, bf16[128,1024]{1,0:T(8,128)(2,1)}, bf16[128,1024]{1,0:T(8,128)(2,1)}) custom-call(f32[512,1024]{1,0:T(8,128)} %get-tuple-element.138.keep, bf16[512,1024]{1,0:T(8,128)(2,1)} %collective-permute-done.33.received), custom_call_target="tpu_custom_call" | custom-call | flops 1024 | bytes 1024 | tf_op jit(solution)/shard_map/pallas_call | solution.py:114
  188.3 1.4 collective-permute-start.34
  190.3 1.5 collective-permute-start.36
  191.7 16.3 %shard_map.246 = (bf16[512,1024]{1,0:T(8,128)(2,1)}, f32[512,1024]{1,0:T(8,128)}, f32[256,384]{1,0:T(8,128)}, f32[8,384]{1,0:T(8,128)}, bf16[272,384]{1,0:T(8,12...) custom-call(s32[3]{0:T(128)} %pad_add_fusion.where_ref.refs_0_, s32[4,4]{1,0:T(4,128)} %copy-done.32, ...), custom_call_target="tpu_custom_call" | custom-call | flops 1024 | bytes 24000000 | tf_op jit(solution)/shard_map/pallas_call | solution.py:449
  208.2 1.1 collective-permute-start.42
  209.3 2.7 %collective-permute-start.43 = (bf16[272,384]{1,0:T(8,128)(2,1)}, bf16[272,384]{1,0:T(8,128)(2,1)}, u32[]{:S(2)}, u32[]{:S(2)}) collective-permute-start(bf16[272,384]{1,0:T(8,128)(2,1)} %get-tuple-element.171), channel_id=1, source_target_pairs={{0,24},{2,26},{4,28},{6,30},{8,0},{10,2},{12,4},{14,6},{16,8},{18,... | collective-permute-start | bytes 626696 | tf_op jit(solution)/shard_map/ppermute | solution.py:104
  213.0 3.8 %shard_map.247 = (f32[128,1024]{1,0:T(8,128)}, f32[64,1792]{1,0:T(8,128)}, bf16[256,1024]{1,0:T(8,128)(2,1)}, bf16[256,1024]{1,0:T(8,128)(2,1)}, bf16[256,1024]{1,0:T(8,128)(2,1)}) custom-call(s32[3]{0:T(128)} %pad_add_fusion.where_ref.refs_0_, f32[512,1024]{1,0:T(8,128)} %get-tuple-element.159.keep, bf16[512,1024]{1,0:T(8,128)(2,1)} %copy-done.14, ...), custom_call_target="tpu_custom_call" | custom-call | flops 1024 | bytes 1024 | tf_op jit(solution)/shard_map/pallas_call | solution.py:114
  216.8 1.4 collective-permute-start.38
  219.0 1.3 collective-permute-start.40
  220.3 6.2 %collective-permute-done.42.refs_1_ = bf16[272,384]{1,0:T(8,128)(2,1)} collective-permute-done((bf16[272,384]{1,0:T(8,128)(2,1)}, bf16[272,384]{1,0:T(8,128)(2,1)}, u32[]{:S(2)}, u32[]{:S(2)}) %collective-permute-start.42) | collective-permute-done | bytes 208928 | tf_op jit(solution)/shard_map/ppermute | solution.py:104
  226.5 2.1 shard_map.248
  228.6 1.4 collective-permute-start.44
  230.6 12.7 %collective-permute-done.44.one = bf16[80,384]{1,0:T(8,128)(2,1)S(1)} collective-permute-done((bf16[80,384]{1,0:T(8,128)(2,1)}, bf16[80,384]{1,0:T(8,128)(2,1)S(1)}, u32[]{:S(2)}, u32[]{:S(2)}) %collective-permute-start.44) | collective-permute-done | bytes 61472 | tf_op jit(solution)/shard_map/ppermute | solution.py:99
  243.3 1.4 collective-permute-start.46
  244.8 2.0 add_convert_fusion
  246.8 1.9 collective-permute-done.46.three
  249.3 1.9 shard_map.249
  252.6 2.9 %shard_map.250 = (f32[64,2304]{1,0:T(8,128)}, f32[64,2304]{1,0:T(8,128)}, f32[64,2304]{1,0:T(8,128)}) custom-call(s32[3]{0:T(128)} %pad_add_fusion.where_ref.refs_0_, f32[64,1792]{1,0:T(8,128)} %get-tuple-element.185.own, bf16[256,1024]{1,0:T(8,128)(2,1)} %copy-done.5, bf16[256,1024]{1,0:T(8,128)(2,1)} %copy-done.6, bf16[256,1024]{1,0:T(8,128)(2,1)} %copy-done.7), custom_call_target="tpu_custom_call" | custom-call | flops 1024 | bytes 1024 | tf_op jit(solution)/shard_map/pallas_call | solution.py:114
  (166 shorter events, 21.7 us)
Async XLA Ops:
  7.2 117.4 %all-gather.2.cloned.1.call-start = ((), (), s32[]{:S(2)}) async-start(), calls=%async_computation.1 | async-start | bytes 4587520 | tf_op jit(solution)/shard_map/all_gather | solution.py:841
  7.2 26.1 %collective-permute-start.5 = (bf16[128,1024]{1,0:T(8,128)(2,1)}, bf16[128,1024]{1,0:T(8,128)(2,1)S(1)}, u32[]{:S(2)}, u32[]{:S(2)}) collective-permute-start(bf16[128,1024]{1,0:T(8,128)(2,1)} %param.14), channel_id=1, source_target_pairs={{0,6},{2,4},{4,2},{6,0},{8,14},{10,12},{12,10},{14,8},{16,22},{18,... | collective-permute-start | bytes 786440 | tf_op jit(solution)/shard_map/ppermute | solution.py:99
  11.2 23.2 %collective-permute-start.4 = (bf16[128,1024]{1,0:T(8,128)(2,1)}, bf16[128,1024]{1,0:T(8,128)(2,1)S(1)}, u32[]{:S(2)}, u32[]{:S(2)}) collective-permute-start(bf16[128,1024]{1,0:T(8,128)(2,1)} %param.14), channel_id=1, source_target_pairs={{0,4},{2,6},{4,0},{6,2},{8,12},{10,14},{12,8},{14,10},{16,20},{18,... | collective-permute-start | bytes 786440 | tf_op jit(solution)/shard_map/ppermute | solution.py:99
  14.0 6.1 %collective-permute-start = (bf16[32,1024]{1,0:T(8,128)(2,1)}, bf16[32,1024]{1,0:T(8,128)(2,1)S(1)}, u32[]{:S(2)}, u32[]{:S(2)}) collective-permute-start(bf16[32,1024]{1,0:T(8,128)(2,1)} %get-tuple-element.102), channel_id=1, source_target_pairs={{0,2},{2,0},{4,6},{6,4},{8,10},{10,8},{12,14},{14,12},{16,18},{18,... | collective-permute-start | bytes 196616 | tf_op jit(solution)/shard_map/ppermute | solution.py:99
  14.1 12.0 %collective-permute-start.1 = (bf16[32,1024]{1,0:T(8,128)(2,1)}, bf16[32,1024]{1,0:T(8,128)(2,1)S(1)}, u32[]{:S(2)}, u32[]{:S(2)}) collective-permute-start(bf16[32,1024]{1,0:T(8,128)(2,1)} %get-tuple-element.103), channel_id=1, source_target_pairs={{0,4},{2,6},{4,0},{6,2},{8,12},{10,14},{12,8},{14,10},{16,20},{18,... | collective-permute-start | bytes 196616 | tf_op jit(solution)/shard_map/ppermute | solution.py:99
  16.1 10.1 %collective-permute-start.2 = (bf16[32,1024]{1,0:T(8,128)(2,1)}, bf16[32,1024]{1,0:T(8,128)(2,1)S(1)}, u32[]{:S(2)}, u32[]{:S(2)}) collective-permute-start(bf16[32,1024]{1,0:T(8,128)(2,1)} %get-tuple-element.104), channel_id=1, source_target_pairs={{0,6},{2,4},{4,2},{6,0},{8,14},{10,12},{12,10},{14,8},{16,22},{18,... | collective-permute-start | bytes 196616 | tf_op jit(solution)/shard_map/ppermute | solution.py:99
  19.7 33.1 %copy-start.4 = (bf16[128,1024]{1,0:T(8,128)(2,1)S(1)}, bf16[128,1024]{1,0:T(8,128)(2,1)}, u32[]{:S(2)}) copy-start(bf16[128,1024]{1,0:T(8,128)(2,1)} %param.14) | copy-start | bytes 786436
  20.1 6.0 %copy-start.26 = (bf16[32,1024]{1,0:T(8,128)(2,1)}, bf16[32,1024]{1,0:T(8,128)(2,1)S(1)}, u32[]{:S(2)}) copy-start(bf16[32,1024]{1,0:T(8,128)(2,1)S(1)} %collective-permute-done.one) | copy-start | bytes 196612
  20.1 14.3 %collective-permute-start.3 = (bf16[128,1024]{1,0:T(8,128)(2,1)}, bf16[128,1024]{1,0:T(8,128)(2,1)S(1)}, u32[]{:S(2)}, u32[]{:S(2)}) collective-permute-start(bf16[128,1024]{1,0:T(8,128)(2,1)} %param.14), channel_id=1, source_target_pairs={{0,2},{2,0},{4,6},{6,4},{8,10},{10,8},{12,14},{14,12},{16,18},{18,... | collective-permute-start | bytes 786440 | tf_op jit(solution)/shard_map/ppermute | solution.py:99
  28.5 9.5 %collective-permute-start.9 = (bf16[256,384]{1,0:T(8,128)(2,1)}, bf16[256,384]{1,0:T(8,128)(2,1)}, u32[]{:S(2)}, u32[]{:S(2)}) collective-permute-start(bf16[256,384]{1,0:T(8,128)(2,1)} %get-tuple-element.119.refs_9_), channel_id=1, source_target_pairs={{0,24},{2,26},{4,28},{6,30},{8,0},{10,2},{12,4},{14,6},{16,8},{18,... | collective-permute-start | bytes 589832 | tf_op jit(solution)/shard_map/ppermute | solution.py:104
  32.3 17.1 %collective-permute-start.8 = (bf16[256,384]{1,0:T(8,128)(2,1)}, bf16[256,384]{1,0:T(8,128)(2,1)S(1)}, u32[]{:S(2)}, u32[]{:S(2)}) collective-permute-start(bf16[256,384]{1,0:T(8,128)(2,1)} %get-tuple-element.119.refs_9_), channel_id=1, source_target_pairs={{0,16},{2,18},{4,20},{6,22},{8,24},{10,26},{12,28},{14,30},{16,0},... | collective-permute-start | bytes 589832 | tf_op jit(solution)/shard_map/ppermute | solution.py:104
  33.2 19.7 %copy-start.32 = (s32[4,4]{1,0:T(4,128)}, s32[4,4]{1,0:T(4,128)S(1)}, u32[]{:S(2)}) copy-start(s32[4,4]{1,0:T(4,128)S(1)} %reduce_window_sum.11.refs_1_.ends_ref) | copy-start | bytes 196
  33.3 16.1 %collective-permute-start.7 = (bf16[256,384]{1,0:T(8,128)(2,1)}, bf16[256,384]{1,0:T(8,128)(2,1)S(1)}, u32[]{:S(2)}, u32[]{:S(2)}) collective-permute-start(bf16[256,384]{1,0:T(8,128)(2,1)} %get-tuple-element.119.refs_9_), channel_id=1, source_target_pairs={{0,8},{2,10},{4,12},{6,14},{8,16},{10,18},{12,20},{14,22},{16,24},... | collective-permute-start | bytes 589832 | tf_op jit(solution)/shard_map/ppermute | solution.py:104
  34.4 15.0 %collective-permute-start.10 = (bf16[64,1792]{1,0:T(8,128)(2,1)}, bf16[64,1792]{1,0:T(8,128)(2,1)S(1)}, u32[]{:S(2)}, u32[]{:S(2)}) collective-permute-start(bf16[64,1792]{1,0:T(8,128)(2,1)} %get-tuple-element.112), channel_id=1, source_target_pairs={{0,2},{2,0},{4,6},{6,4},{8,10},{10,8},{12,14},{14,12},{16,18},{18,... | collective-permute-start | bytes 688136 | tf_op jit(solution)/shard_map/ppermute | solution.py:99
  35.9 13.5 %collective-permute-start.11 = (bf16[64,1792]{1,0:T(8,128)(2,1)}, bf16[64,1792]{1,0:T(8,128)(2,1)S(1)}, u32[]{:S(2)}, u32[]{:S(2)}) collective-permute-start(bf16[64,1792]{1,0:T(8,128)(2,1)} %get-tuple-element.113), channel_id=1, source_target_pairs={{0,4},{2,6},{4,0},{6,2},{8,12},{10,14},{12,8},{14,10},{16,20},{18,... | collective-permute-start | bytes 688136 | tf_op jit(solution)/shard_map/ppermute | solution.py:99
  37.9 11.5 %collective-permute-start.12 = (bf16[64,1792]{1,0:T(8,128)(2,1)}, bf16[64,1792]{1,0:T(8,128)(2,1)S(1)}, u32[]{:S(2)}, u32[]{:S(2)}) collective-permute-start(bf16[64,1792]{1,0:T(8,128)(2,1)} %get-tuple-element.114), channel_id=1, source_target_pairs={{0,6},{2,4},{4,2},{6,0},{8,14},{10,12},{12,10},{14,8},{16,22},{18,... | collective-permute-start | bytes 688136 | tf_op jit(solution)/shard_map/ppermute | solution.py:99
  50.3 6.4 %copy-start.35 = (f32[64]{0:T(128)S(1)}, f32[64]{0:T(128)}, u32[]{:S(2)}) copy-start(f32[64]{0:T(128)} %param.17) | copy-start | bytes 772
  50.3 6.4 %copy-start.36 = (f32[64]{0:T(128)S(1)}, f32[64]{0:T(128)}, u32[]{:S(2)}) copy-start(f32[64]{0:T(128)} %param.18) | copy-start | bytes 772
  52.8 159.5 %reduce-scatter.2.cloned.1.call-start = ((), (), s32[]{:S(2)}) async-start(), calls=%async_computation.2 | async-start | bytes 4587520 | tf_op jit(solution)/shard_map/reduce_scatter | solution.py:868
  53.0 4.2 %collective-permute-start.6 = (bf16[512,1024]{1,0:T(8,128)(2,1)S(1)}, bf16[512,1024]{1,0:T(8,128)(2,1)S(1)}, u32[]{:S(2)}, u32[]{:S(2)}) collective-permute-start(bf16[512,1024]{1,0:T(8,128)(2,1)S(1)} %constant_dynamic-update-slice_fusion.refs_2_), channel_id=1, source_target_pairs={{0,1},{1,0},{2,3},{3,2},{4,5},{5,4},{6,7},{7,6},{8,9},{9,8},{10,11... | collective-permute-start | bytes 3145736 | tf_op jit(solution)/shard_map/ppermute | solution.py:108
  53.1 15.7 %collective-permute-start.15 = (bf16[128,1024]{1,0:T(8,128)(2,1)S(1)}, bf16[128,1024]{1,0:T(8,128)(2,1)S(1)}, u32[]{:S(2)}, u32[]{:S(2)}) collective-permute-start(bf16[128,1024]{1,0:T(8,128)(2,1)S(1)} %copy-done.13), channel_id=1, source_target_pairs={{0,6},{2,4},{4,2},{6,0},{8,14},{10,12},{12,10},{14,8},{16,22},{18,... | collective-permute-start | bytes 786440 | tf_op jit(solution)/shard_map/ppermute | solution.py:99
  54.1 14.7 %collective-permute-start.14 = (bf16[128,1024]{1,0:T(8,128)(2,1)S(1)}, bf16[128,1024]{1,0:T(8,128)(2,1)S(1)}, u32[]{:S(2)}, u32[]{:S(2)}) collective-permute-start(bf16[128,1024]{1,0:T(8,128)(2,1)S(1)} %copy-done.13), channel_id=1, source_target_pairs={{0,4},{2,6},{4,0},{6,2},{8,12},{10,14},{12,8},{14,10},{16,20},{18,... | collective-permute-start | bytes 786440 | tf_op jit(solution)/shard_map/ppermute | solution.py:99
  56.1 12.7 %collective-permute-start.13 = (bf16[128,1024]{1,0:T(8,128)(2,1)S(1)}, bf16[128,1024]{1,0:T(8,128)(2,1)S(1)}, u32[]{:S(2)}, u32[]{:S(2)}) collective-permute-start(bf16[128,1024]{1,0:T(8,128)(2,1)S(1)} %copy-done.13), channel_id=1, source_target_pairs={{0,2},{2,0},{4,6},{6,4},{8,10},{10,8},{12,14},{14,12},{16,18},{18,... | collective-permute-start | bytes 786440 | tf_op jit(solution)/shard_map/ppermute | solution.py:99
  70.2 2.9 %collective-permute-start.16 = (bf16[512,1024]{1,0:T(8,128)(2,1)}, bf16[512,1024]{1,0:T(8,128)(2,1)S(1)}, u32[]{:S(2)}, u32[]{:S(2)}) collective-permute-start(bf16[512,1024]{1,0:T(8,128)(2,1)} %get-tuple-element.126), channel_id=1, source_target_pairs={{0,1},{1,0},{2,3},{3,2},{4,5},{5,4},{6,7},{7,6},{8,9},{9,8},{10,11... | collective-permute-start | bytes 3145736 | tf_op jit(solution)/shard_map/ppermute | solution.py:108
  77.0 16.8 %copy-start.33 = (f32[1024]{0:T(1024)S(1)}, f32[1024]{0:T(1024)}, u32[]{:S(2)}) copy-start(f32[1024]{0:T(1024)} %param.19) | copy-start | bytes 12292
  77.0 20.5 %copy-start.19 = (bf16[128,1024]{1,0:T(8,128)(2,1)S(1)}, bf16[128,1024]{1,0:T(8,128)(2,1)}, u32[]{:S(2)}) copy-start(bf16[128,1024]{1,0:T(8,128)(2,1)} %copy-done.18) | copy-start | bytes 786436
  77.0 20.5 %copy-start.17 = (bf16[128,1024]{1,0:T(8,128)(2,1)S(1)}, bf16[128,1024]{1,0:T(8,128)(2,1)}, u32[]{:S(2)}) copy-start(bf16[128,1024]{1,0:T(8,128)(2,1)} %copy-done.16) | copy-start | bytes 786436
  77.0 9.4 %collective-permute-start.17 = (bf16[128,1024]{1,0:T(8,128)(2,1)}, bf16[128,1024]{1,0:T(8,128)(2,1)S(1)}, u32[]{:S(2)}, u32[]{:S(2)}) collective-permute-start(bf16[128,1024]{1,0:T(8,128)(2,1)} %get-tuple-element.128), channel_id=1, source_target_pairs={{0,2},{2,0},{4,6},{6,4},{8,10},{10,8},{12,14},{14,12},{16,18},{18,... | collective-permute-start | bytes 786440 | tf_op jit(solution)/shard_map/ppermute | solution.py:99
  78.5 13.9 %collective-permute-start.18 = (bf16[128,1024]{1,0:T(8,128)(2,1)}, bf16[128,1024]{1,0:T(8,128)(2,1)S(1)}, u32[]{:S(2)}, u32[]{:S(2)}) collective-permute-start(bf16[128,1024]{1,0:T(8,128)(2,1)} %get-tuple-element.129), channel_id=1, source_target_pairs={{0,4},{2,6},{4,0},{6,2},{8,12},{10,14},{12,8},{14,10},{16,20},{18,... | collective-permute-start | bytes 786440 | tf_op jit(solution)/shard_map/ppermute | solution.py:99
  78.7 13.8 %collective-permute-start.19 = (bf16[128,1024]{1,0:T(8,128)(2,1)}, bf16[128,1024]{1,0:T(8,128)(2,1)S(1)}, u32[]{:S(2)}, u32[]{:S(2)}) collective-permute-start(bf16[128,1024]{1,0:T(8,128)(2,1)} %get-tuple-element.130), channel_id=1, source_target_pairs={{0,6},{2,4},{4,2},{6,0},{8,14},{10,12},{12,10},{14,8},{16,22},{18,... | collective-permute-start | bytes 786440 | tf_op jit(solution)/shard_map/ppermute | solution.py:99
  93.9 10.2 %collective-permute-start.22 = (bf16[128,1024]{1,0:T(8,128)(2,1)S(1)}, bf16[128,1024]{1,0:T(8,128)(2,1)S(1)}, u32[]{:S(2)}, u32[]{:S(2)}) collective-permute-start(bf16[128,1024]{1,0:T(8,128)(2,1)S(1)} %multiply_convert_fusion), channel_id=1, source_target_pairs={{0,6},{2,4},{4,2},{6,0},{8,14},{10,12},{12,10},{14,8},{16,22},{18,... | collective-permute-start | bytes 786440 | tf_op jit(solution)/shard_map/ppermute | solution.py:99
  95.5 12.4 %collective-permute-start.21 = (bf16[128,1024]{1,0:T(8,128)(2,1)S(1)}, bf16[128,1024]{1,0:T(8,128)(2,1)S(1)}, u32[]{:S(2)}, u32[]{:S(2)}) collective-permute-start(bf16[128,1024]{1,0:T(8,128)(2,1)S(1)} %multiply_convert_fusion), channel_id=1, source_target_pairs={{0,4},{2,6},{4,0},{6,2},{8,12},{10,14},{12,8},{14,10},{16,20},{18,... | collective-permute-start | bytes 786440 | tf_op jit(solution)/shard_map/ppermute | solution.py:99
  96.0 11.9 %collective-permute-start.20 = (bf16[128,1024]{1,0:T(8,128)(2,1)S(1)}, bf16[128,1024]{1,0:T(8,128)(2,1)S(1)}, u32[]{:S(2)}, u32[]{:S(2)}) collective-permute-start(bf16[128,1024]{1,0:T(8,128)(2,1)S(1)} %multiply_convert_fusion), channel_id=1, source_target_pairs={{0,2},{2,0},{4,6},{6,4},{8,10},{10,8},{12,14},{14,12},{16,18},{18,... | collective-permute-start | bytes 786440 | tf_op jit(solution)/shard_map/ppermute | solution.py:99
  97.6 27.0 %copy-start.9 = (bf16[512,1024]{1,0:T(8,128)(2,1)}, bf16[512,1024]{1,0:T(8,128)(2,1)S(1)}, u32[]{:S(2)}) copy-start(bf16[512,1024]{1,0:T(8,128)(2,1)S(1)} %constant_dynamic-update-slice_fusion.4.g_m) | copy-start | bytes 3145732
  97.6 10.6 %collective-permute-start.24 = (bf16[512,1024]{1,0:T(8,128)(2,1)S(1)}, bf16[512,1024]{1,0:T(8,128)(2,1)S(1)}, u32[]{:S(2)}, u32[]{:S(2)}) collective-permute-start(bf16[512,1024]{1,0:T(8,128)(2,1)S(1)} %constant_dynamic-update-slice_fusion.4.g_m), channel_id=1, source_target_pairs={{0,1},{1,0},{2,3},{3,2},{4,5},{5,4},{6,7},{7,6},{8,9},{9,8},{10,11... | collective-permute-start | bytes 3145736 | tf_op jit(solution)/shard_map/ppermute | solution.py:108
  108.0 16.6 %copy-start.3 = (bf16[512,1024]{1,0:T(8,128)(2,1)}, bf16[512,1024]{1,0:T(8,128)(2,1)S(1)}, u32[]{:S(2)}) copy-start(bf16[512,1024]{1,0:T(8,128)(2,1)S(1)} %pad_maximum_fusion.x_m) | copy-start | bytes 3145732
  108.0 2.9 %collective-permute-start.23 = (bf16[512,1024]{1,0:T(8,128)(2,1)S(1)}, bf16[512,1024]{1,0:T(8,128)(2,1)}, u32[]{:S(2)}, u32[]{:S(2)}) collective-permute-start(bf16[512,1024]{1,0:T(8,128)(2,1)S(1)} %pad_maximum_fusion.x_m), channel_id=1, source_target_pairs={{0,1},{1,0},{2,3},{3,2},{4,5},{5,4},{6,7},{7,6},{8,9},{9,8},{10,11... | collective-permute-start | bytes 3145736 | tf_op jit(solution)/shard_map/ppermute | solution.py:108
  146.3 2.7 %collective-permute-start.25 = (bf16[512,1024]{1,0:T(8,128)(2,1)S(1)}, bf16[512,1024]{1,0:T(8,128)(2,1)S(1)}, u32[]{:S(2)}, u32[]{:S(2)}) collective-permute-start(bf16[512,1024]{1,0:T(8,128)(2,1)S(1)} %copy-done.38), channel_id=1, source_target_pairs={{0,1},{1,0},{2,3},{3,2},{4,5},{5,4},{6,7},{7,6},{8,9},{9,8},{10,11... | collective-permute-start | bytes 3145736 | tf_op jit(solution)/shard_map/ppermute | solution.py:108
  153.0 9.4 %collective-permute-start.26 = (bf16[128,1024]{1,0:T(8,128)(2,1)}, bf16[128,1024]{1,0:T(8,128)(2,1)S(1)}, u32[]{:S(2)}, u32[]{:S(2)}) collective-permute-start(bf16[128,1024]{1,0:T(8,128)(2,1)} %get-tuple-element.134), channel_id=1, source_target_pairs={{0,2},{2,0},{4,6},{6,4},{8,10},{10,8},{12,14},{14,12},{16,18},{18,... | collective-permute-start | bytes 786440 | tf_op jit(solution)/shard_map/ppermute | solution.py:99
  154.7 13.9 %collective-permute-start.27 = (bf16[128,1024]{1,0:T(8,128)(2,1)}, bf16[128,1024]{1,0:T(8,128)(2,1)S(1)}, u32[]{:S(2)}, u32[]{:S(2)}) collective-permute-start(bf16[128,1024]{1,0:T(8,128)(2,1)} %get-tuple-element.135), channel_id=1, source_target_pairs={{0,4},{2,6},{4,0},{6,2},{8,12},{10,14},{12,8},{14,10},{16,20},{18,... | collective-permute-start | bytes 786440 | tf_op jit(solution)/shard_map/ppermute | solution.py:99
  156.2 12.5 %collective-permute-start.28 = (bf16[128,1024]{1,0:T(8,128)(2,1)}, bf16[128,1024]{1,0:T(8,128)(2,1)S(1)}, u32[]{:S(2)}, u32[]{:S(2)}) collective-permute-start(bf16[128,1024]{1,0:T(8,128)(2,1)} %get-tuple-element.136), channel_id=1, source_target_pairs={{0,6},{2,4},{4,2},{6,0},{8,14},{10,12},{12,10},{14,8},{16,22},{18,... | collective-permute-start | bytes 786440 | tf_op jit(solution)/shard_map/ppermute | solution.py:99
  170.9 10.2 %collective-permute-start.31 = (bf16[128,1024]{1,0:T(8,128)(2,1)S(1)}, bf16[128,1024]{1,0:T(8,128)(2,1)S(1)}, u32[]{:S(2)}, u32[]{:S(2)}) collective-permute-start(bf16[128,1024]{1,0:T(8,128)(2,1)S(1)} %get-tuple-element.191), channel_id=1, source_target_pairs={{0,6},{2,4},{4,2},{6,0},{8,14},{10,12},{12,10},{14,8},{16,22},{18,... | collective-permute-start | bytes 786440 | tf_op jit(solution)/shard_map/ppermute | solution.py:99
  172.4 12.3 %collective-permute-start.30 = (bf16[128,1024]{1,0:T(8,128)(2,1)S(1)}, bf16[128,1024]{1,0:T(8,128)(2,1)S(1)}, u32[]{:S(2)}, u32[]{:S(2)}) collective-permute-start(bf16[128,1024]{1,0:T(8,128)(2,1)S(1)} %get-tuple-element.191), channel_id=1, source_target_pairs={{0,4},{2,6},{4,0},{6,2},{8,12},{10,14},{12,8},{14,10},{16,20},{18,... | collective-permute-start | bytes 786440 | tf_op jit(solution)/shard_map/ppermute | solution.py:99
  173.6 11.3 %collective-permute-start.29 = (bf16[128,1024]{1,0:T(8,128)(2,1)S(1)}, bf16[128,1024]{1,0:T(8,128)(2,1)S(1)}, u32[]{:S(2)}, u32[]{:S(2)}) collective-permute-start(bf16[128,1024]{1,0:T(8,128)(2,1)S(1)} %get-tuple-element.191), channel_id=1, source_target_pairs={{0,2},{2,0},{4,6},{6,4},{8,10},{10,8},{12,14},{14,12},{16,18},{18,... | collective-permute-start | bytes 786440 | tf_op jit(solution)/shard_map/ppermute | solution.py:99
  174.4 10.6 %collective-permute-start.33 = (bf16[512,1024]{1,0:T(8,128)(2,1)S(1)}, bf16[512,1024]{1,0:T(8,128)(2,1)}, u32[]{:S(2)}, u32[]{:S(2)}) collective-permute-start(bf16[512,1024]{1,0:T(8,128)(2,1)S(1)} %copy-done.37), channel_id=1, source_target_pairs={{0,1},{1,0},{2,3},{3,2},{4,5},{5,4},{6,7},{7,6},{8,9},{9,8},{10,11... | collective-permute-start | bytes 3145736 | tf_op jit(solution)/shard_map/ppermute | solution.py:108
  184.9 6.8 %copy-start.2 = (bf16[512,1024]{1,0:T(8,128)(2,1)}, bf16[512,1024]{1,0:T(8,128)(2,1)S(1)}, u32[]{:S(2)}) copy-start(bf16[512,1024]{1,0:T(8,128)(2,1)S(1)} %pad_maximum_fusion.1.refs_9_) | copy-start | bytes 3145732
  184.9 3.3 %collective-permute-start.32 = (bf16[512,1024]{1,0:T(8,128)(2,1)S(1)}, bf16[512,1024]{1,0:T(8,128)(2,1)}, u32[]{:S(2)}, u32[]{:S(2)}) collective-permute-start(bf16[512,1024]{1,0:T(8,128)(2,1)S(1)} %pad_maximum_fusion.1.refs_9_), channel_id=1, source_target_pairs={{0,1},{1,0},{2,3},{3,2},{4,5},{5,4},{6,7},{7,6},{8,9},{9,8},{10,11... | collective-permute-start | bytes 3145736 | tf_op jit(solution)/shard_map/ppermute | solution.py:108
  188.3 19.8 %collective-permute-start.34 = (bf16[128,1024]{1,0:T(8,128)(2,1)}, bf16[128,1024]{1,0:T(8,128)(2,1)}, u32[]{:S(2)}, u32[]{:S(2)}) collective-permute-start(bf16[128,1024]{1,0:T(8,128)(2,1)} %get-tuple-element.145), channel_id=1, source_target_pairs={{0,2},{2,0},{4,6},{6,4},{8,10},{10,8},{12,14},{14,12},{16,18},{18,... | collective-permute-start | bytes 786440 | tf_op jit(solution)/shard_map/ppermute | solution.py:99
  189.7 18.4 %collective-permute-start.35 = (bf16[128,1024]{1,0:T(8,128)(2,1)}, bf16[128,1024]{1,0:T(8,128)(2,1)}, u32[]{:S(2)}, u32[]{:S(2)}) collective-permute-start(bf16[128,1024]{1,0:T(8,128)(2,1)} %get-tuple-element.146), channel_id=1, source_target_pairs={{0,4},{2,6},{4,0},{6,2},{8,12},{10,14},{12,8},{14,10},{16,20},{18,... | collective-permute-start | bytes 786440 | tf_op jit(solution)/shard_map/ppermute | solution.py:99
  190.3 17.8 %collective-permute-start.36 = (bf16[128,1024]{1,0:T(8,128)(2,1)}, bf16[128,1024]{1,0:T(8,128)(2,1)}, u32[]{:S(2)}, u32[]{:S(2)}) collective-permute-start(bf16[128,1024]{1,0:T(8,128)(2,1)} %get-tuple-element.147), channel_id=1, source_target_pairs={{0,6},{2,4},{4,2},{6,0},{8,14},{10,12},{12,10},{14,8},{16,22},{18,... | collective-permute-start | bytes 786440 | tf_op jit(solution)/shard_map/ppermute | solution.py:99
  208.0 36.7 %copy-start.15 = (f32[128,1024]{1,0:T(8,128)S(1)}, f32[128,1024]{1,0:T(8,128)}, u32[]{:S(2)}) copy-start(f32[128,1024]{1,0:T(8,128)} %get-tuple-element.144) | copy-start | bytes 1572868
  208.1 4.0 %collective-permute-start.37 = (bf16[512,1024]{1,0:T(8,128)(2,1)}, bf16[512,1024]{1,0:T(8,128)(2,1)S(1)}, u32[]{:S(2)}, u32[]{:S(2)}) collective-permute-start(bf16[512,1024]{1,0:T(8,128)(2,1)} %get-tuple-element.160), channel_id=1, source_target_pairs={{0,1},{1,0},{2,3},{3,2},{4,5},{5,4},{6,7},{7,6},{8,9},{9,8},{10,11... | collective-permute-start | bytes 3145736 | tf_op jit(solution)/shard_map/ppermute | solution.py:108
  208.1 10.8 %collective-permute-start.41 = (bf16[272,384]{1,0:T(8,128)(2,1)}, bf16[272,384]{1,0:T(8,128)(2,1)}, u32[]{:S(2)}, u32[]{:S(2)}) collective-permute-start(bf16[272,384]{1,0:T(8,128)(2,1)} %get-tuple-element.169), channel_id=1, source_target_pairs={{0,8},{2,10},{4,12},{6,14},{8,16},{10,18},{12,20},{14,22},{16,24},... | collective-permute-start | bytes 626696 | tf_op jit(solution)/shard_map/ppermute | solution.py:104
  208.2 18.3 %collective-permute-start.42 = (bf16[272,384]{1,0:T(8,128)(2,1)}, bf16[272,384]{1,0:T(8,128)(2,1)}, u32[]{:S(2)}, u32[]{:S(2)}) collective-permute-start(bf16[272,384]{1,0:T(8,128)(2,1)} %get-tuple-element.170), channel_id=1, source_target_pairs={{0,16},{2,18},{4,20},{6,22},{8,24},{10,26},{12,28},{14,30},{16,0},... | collective-permute-start | bytes 626696 | tf_op jit(solution)/shard_map/ppermute | solution.py:104
  209.3 17.2 %collective-permute-start.43 = (bf16[272,384]{1,0:T(8,128)(2,1)}, bf16[272,384]{1,0:T(8,128)(2,1)}, u32[]{:S(2)}, u32[]{:S(2)}) collective-permute-start(bf16[272,384]{1,0:T(8,128)(2,1)} %get-tuple-element.171), channel_id=1, source_target_pairs={{0,24},{2,26},{4,28},{6,30},{8,0},{10,2},{12,4},{14,6},{16,8},{18,... | collective-permute-start | bytes 626696 | tf_op jit(solution)/shard_map/ppermute | solution.py:104
  216.8 34.4 %copy-start.8 = (f32[128,1024]{1,0:T(8,128)S(1)}, f32[128,1024]{1,0:T(8,128)}, u32[]{:S(2)}) copy-start(f32[128,1024]{1,0:T(8,128)} %get-tuple-element.162) | copy-start | bytes 1572868
  216.8 34.4 %copy-start.25 = (f32[1024]{0:T(1024)S(1)}, f32[1024]{0:T(1024)}, u32[]{:S(2)}) copy-start(f32[1024]{0:T(1024)} %param.16) | copy-start | bytes 12292
  216.8 31.9 %collective-permute-start.38 = (bf16[256,1024]{1,0:T(8,128)(2,1)}, bf16[256,1024]{1,0:T(8,128)(2,1)S(1)}, u32[]{:S(2)}, u32[]{:S(2)}) collective-permute-start(bf16[256,1024]{1,0:T(8,128)(2,1)} %get-tuple-element.163), channel_id=1, source_target_pairs={{0,2},{2,0},{4,6},{6,4},{8,10},{10,8},{12,14},{14,12},{16,18},{18,... | collective-permute-start | bytes 1572872 | tf_op jit(solution)/shard_map/ppermute | solution.py:99
  218.2 30.5 %collective-permute-start.39 = (bf16[256,1024]{1,0:T(8,128)(2,1)}, bf16[256,1024]{1,0:T(8,128)(2,1)S(1)}, u32[]{:S(2)}, u32[]{:S(2)}) collective-permute-start(bf16[256,1024]{1,0:T(8,128)(2,1)} %get-tuple-element.164), channel_id=1, source_target_pairs={{0,4},{2,6},{4,0},{6,2},{8,12},{10,14},{12,8},{14,10},{16,20},{18,... | collective-permute-start | bytes 1572872 | tf_op jit(solution)/shard_map/ppermute | solution.py:99
  219.0 32.2 %collective-permute-start.40 = (bf16[256,1024]{1,0:T(8,128)(2,1)}, bf16[256,1024]{1,0:T(8,128)(2,1)S(1)}, u32[]{:S(2)}, u32[]{:S(2)}) collective-permute-start(bf16[256,1024]{1,0:T(8,128)(2,1)} %get-tuple-element.165), channel_id=1, source_target_pairs={{0,6},{2,4},{4,2},{6,0},{8,14},{10,12},{12,10},{14,8},{16,22},{18,... | collective-permute-start | bytes 1572872 | tf_op jit(solution)/shard_map/ppermute | solution.py:99
  228.6 14.8 %collective-permute-start.44 = (bf16[80,384]{1,0:T(8,128)(2,1)}, bf16[80,384]{1,0:T(8,128)(2,1)S(1)}, u32[]{:S(2)}, u32[]{:S(2)}) collective-permute-start(bf16[80,384]{1,0:T(8,128)(2,1)} %get-tuple-element.173), channel_id=1, source_target_pairs={{0,2},{2,0},{4,6},{6,4},{8,10},{10,8},{12,14},{14,12},{16,18},{18,... | collective-permute-start | bytes 184328 | tf_op jit(solution)/shard_map/ppermute | solution.py:99
  230.0 16.8 %collective-permute-start.45 = (bf16[80,384]{1,0:T(8,128)(2,1)}, bf16[80,384]{1,0:T(8,128)(2,1)S(1)}, u32[]{:S(2)}, u32[]{:S(2)}) collective-permute-start(bf16[80,384]{1,0:T(8,128)(2,1)} %get-tuple-element.174), channel_id=1, source_target_pairs={{0,4},{2,6},{4,0},{6,2},{8,12},{10,14},{12,8},{14,10},{16,20},{18,... | collective-permute-start | bytes 184328 | tf_op jit(solution)/shard_map/ppermute | solution.py:99
  243.3 5.3 %collective-permute-start.46 = (bf16[80,384]{1,0:T(8,128)(2,1)}, bf16[80,384]{1,0:T(8,128)(2,1)S(1)}, u32[]{:S(2)}, u32[]{:S(2)}) collective-permute-start(bf16[80,384]{1,0:T(8,128)(2,1)} %get-tuple-element.175), channel_id=1, source_target_pairs={{0,6},{2,4},{4,2},{6,0},{8,14},{10,12},{12,10},{14,8},{16,22},{18,... | collective-permute-start | bytes 184328 | tf_op jit(solution)/shard_map/ppermute | solution.py:99
  251.2 4.3 %collective-permute-start.47 = (f32[8,384]{1,0:T(8,128)}, f32[8,384]{1,0:T(8,128)S(1)}, u32[]{:S(2)}, u32[]{:S(2)}) collective-permute-start(f32[8,384]{1,0:T(8,128)} %get-tuple-element.180), channel_id=1, source_target_pairs={{0,1},{1,0},{2,3},{3,2},{4,5},{5,4},{6,7},{7,6},{8,9},{9,8},{10,11... | collective-permute-start | bytes 36872 | tf_op jit(solution)/shard_map/ppermute | solution.py:108
  (25 other events, 53.1 us)
Sparse Core Ops, SparseCore 0:
  52.9 71.6 all-gather.1
  145.2 66.9 reduce-scatter.1

commit v9 on v8

--- a/solution.py
+++ b/solution.py
@@ -479,10 +479,6 @@
     big = both // 2
     local = x_o.shape[0] // 2
 
-    @pl.when(step == 0)
-    def _():
-        total[...] = jnp.zeros_like(total)
-
     def live_rows(values, group, at_core):
         ids = lax.broadcasted_iota(jnp.int32, values.shape, 0) + at_core * local
         return jnp.where(ids < ends_ref[group, ends_ref.shape[1] - 1], values, jnp.zeros_like(values))
@@ -524,14 +520,22 @@
     partial = matmul_nt(d_both, w_both) + matmul_nt(d_small, w_small)
     dn_send[...] = partial[:half].astype(bfloat16)
     dn_keep[...] = partial[half:]
-    total[:, :both] += matmul_tn(x, d_both)
-    total[:, both : both + big] += matmul_tn(grads, act)
-    total[:, both + big : both + big + LANES] += matmul_tn(x, d_small)
-    total[:, both + big + LANES :] += matmul_tn(grads, act_s)
-
-    @pl.when(step == pl.num_programs(0) - 1)
+    spans = (
+        (slice(0, both), x, d_both),
+        (slice(both, both + big), grads, act),
+        (slice(both + big, both + big + LANES), x, d_small),
+        (slice(both + big + LANES, total.shape[1]), grads, act_s),
+    )
+
+    @pl.when(step == 0)
     def _():
-        grad_out[...] = total[...].astype(bfloat16)
+        for span, left, right in spans:
+            total[:, span] = matmul_tn(left, right)
+
+    @pl.when(step == 1)
+    def _():
+        for span, left, right in spans:
+            grad_out[:, span] = (total[:, span] + matmul_tn(left, right)).astype(bfloat16)
 
 
 def ffn(where, ends, x_mine, x_other, g_mine, g_other, weight):
@@ -824,7 +828,7 @@
         scratch=[pltpu.VMEM((PLANE * rows, attn_cols), float32)],
     )
     attn_pieces = [attn_piece] + [send_deep(attn_piece, step) for step in range(1, layers)]
-    tok_parts = plane_parts(tokens)
+    tok_parts = plane_parts(after(first[1], tokens))
     second = after((first, tok_parts), second)
     second = [second[0]] + [send_plane(second[m], m) for m in range(1, PLANE)]
     ends, tables = row_tables(lens, lengths.shape[1], total_rows)
@@ -893,10 +897,12 @@
     )
     attn_grads = [send_deep(piece, step + 1) for step, piece in enumerate(attn_grads)]
     own_dn, own_ff, *messages = tail_messages(where, keep, swap_cores(send), own_ff)
-    own_attn = after(messages, own_attn)
+    own_attn = after((messages, block_out), own_attn)
+    attn_parts = plane_split_attn(where, own_attn, attn_grads, part_gains)
+    attn_parts = plane_sent(attn_parts)
+    messages = messages[:2] + after(attn_parts[1], messages[2:])
     messages = [send_plane(part, mask + 1) for mask, part in enumerate(messages)]
-    attn_parts = plane_split_attn(where, own_attn, attn_grads, part_gains)
-    attn_parts = after(messages[:2], plane_sent(attn_parts))
+    attn_parts = after(messages[:2], attn_parts)
     d_normed = own_dn + add_up([part[:local_rows] for part in messages])
     grad_tokens = d_hidden + norm_back(d_normed * attn_gain, unit_a, factor_a)
     grad_gate, grad_up, grad_down = call(

time: 264 us -> 277 us (1.049)
  the two profiles are of different devices: /device:TPU:0 before, /device:TPU:27 now
where the time goes in v9:
time: 277 us; the launch traced here: 276 us
  waiting for transfers between devices  99.4 us (36%)
  Pallas kernels  73.8 us (27%)
  starting transfers between devices  61.2 us (22%)
  between operations  14.5 us (5%)
  other arithmetic  14 us (5%)
  local copies, waits for them, and re-layouts  13 us (5%)
    ppermute x33, waiting for transfers between devices, send_plane(): return lax.ppermute(values, 'dp', [(i, i ^ mask) for i in range(count)])  56.1 us
    ppermute x33, starting transfers between devices, send_plane(): return lax.ppermute(values, 'dp', [(i, i ^ mask) for i in range(count)])  29.4 us
    pallas_call x11, Pallas kernels, call(): pl.pallas_call(kernel, out_shape=[jax.ShapeDtypeStruct(shape, kind) for s...  27.4 us
    ppermute x9, starting transfers between devices, swap_cores(): return lax.ppermute(values, 'tensor', [(0, 1), (1, 0)])  25.5 us
    pallas_call x1, Pallas kernels, ffn(): pl.pallas_call(ffn_kernel, grid=(2,), in_specs=[scalar, scalar] + [row_sp...  20 us
    pallas_call x1, Pallas kernels, attn_back(): pl.pallas_call(lambda *refs: attn_back_kernel(layers, *refs), grid=(PLANE...  16.1 us
    ppermute x6, waiting for transfers between devices, send_deep(): lax.ppermute(values, 'dp', [(i, (i + PLANE * step) % count) for i in rang...  15.9 us
    all_gather x1, waiting for transfers between devices, body(): lax.all_gather(ff_piece, 'dp', axis=0, tiled=True, axis_index_groups=colu...  14.8 us
  transfers between devices with their start and end apart: 50, of which 26 were waited for; matrix products, arithmetic and copies ran while one was open for 5% of the time, Pallas kernels for 15%

profile of v9, /device:TPU:27, one launch (start us, length us, event | category | flops | bytes accessed | tf_op | source)
XLA Modules:
  0.0 275.8 jit_solution(946169274619062024)
XLA Ops:
  7.9 1.7 shard_map.237
  9.9 1.2 collective-permute-start.1
  11.1 1.2 collective-permute-start.2
  12.2 2.2 shard_map.239
  14.5 1.2 collective-permute-done.2.three
  16.3 1.7 shard_map.238
  19.1 1.2 collective-permute-start.4
  21.9 2.8 %collective-permute-done.5 = bf16[128,1024]{1,0:T(8,128)(2,1)S(1)} collective-permute-done((bf16[128,1024]{1,0:T(8,128)(2,1)}, bf16[128,1024]{1,0:T(8,128)(2,1)S(1)}, u32[]{:S(2)}, u32[]{:S(2)}) %collective-permute-start.5) | collective-permute-done | bytes 262176 | tf_op jit(solution)/shard_map/ppermute | solution.py:99
  24.7 3.3 %collective-permute-start.7 = (bf16[256,384]{1,0:T(8,128)(2,1)}, bf16[256,384]{1,0:T(8,128)(2,1)S(1)}, u32[]{:S(2)}, u32[]{:S(2)}) collective-permute-start(bf16[256,384]{1,0:T(8,128)(2,1)} %get-tuple-element.122.refs_9_), channel_id=1, source_target_pairs={{0,8},{2,10},{4,12},{6,14},{8,16},{10,18},{12,20},{14,22},{16,24},... | collective-permute-start | bytes 589832 | tf_op jit(solution)/shard_map/ppermute | solution.py:104
  28.0 4.5 %collective-permute-done.4 = bf16[128,1024]{1,0:T(8,128)(2,1)S(1)} collective-permute-done((bf16[128,1024]{1,0:T(8,128)(2,1)}, bf16[128,1024]{1,0:T(8,128)(2,1)S(1)}, u32[]{:S(2)}, u32[]{:S(2)}) %collective-permute-start.4) | collective-permute-done | bytes 262176 | tf_op jit(solution)/shard_map/ppermute | solution.py:99
  33.7 1.6 collective-permute-start.12
  35.2 3.0 %fusion.6 = (f32[1024,128]{1,0:T(8,128)}, f32[1024,128]{1,0:T(8,128)}) fusion(f32[128]{0:T(128)S(1)} %get-tuple-element.207, f32[128]{0:T(128)S(1)} %get-tuple-element.208, f32[1024]{0:T(1024)S(1)} %bitcast.28), kind=kLoop, calls=%fused_computation.13 | loop fusion | flops 262144 | bytes 1053696 | tf_op jit(solution)/shard_map/mul | solution.py:766
  38.3 2.5 collective-permute-done.11.two
  40.8 2.3 collective-permute-done.12.three
  43.8 2.5 shard_map.240
  46.7 3.8 %collective-permute-start.6 = (bf16[512,1024]{1,0:T(8,128)(2,1)S(1)}, bf16[512,1024]{1,0:T(8,128)(2,1)S(1)}, u32[]{:S(2)}, u32[]{:S(2)}) collective-permute-start(bf16[512,1024]{1,0:T(8,128)(2,1)S(1)} %constant_dynamic-update-slice_fusion.refs_2_), channel_id=1, source_target_pairs={{0,1},{1,0},{2,3},{3,2},{4,5},{5,4},{6,7},{7,6},{8,9},{9,8},{10,11... | collective-permute-start | bytes 3145736 | tf_op jit(solution)/shard_map/ppermute | solution.py:108
  54.7 10.2 %shard_map.241 = (bf16[512,1024]{1,0:T(8,128)(2,1)}, f32[512,1024]{1,0:T(8,128)}, f32[1024,256]{1,0:T(8,128)}, bf16[1024,256]{1,0:T(8,128)(2,1)}, bf16[1024,128]{1,0:T(8,128)(2,1)}, /*index=5*/bf16[1024,384]{1,0:T(8,128)(2,1)}) custom-call(s32[3]{0:T(128)} %pad_add_fusion.where_ref.refs_0_, s32[4,4]{1,0:T(4,128)} %copy-done.34, bf16[512,1024]{1,0:T(8,128)(2,1)} %copy-done, ...), custom_call_target="tpu_custom_call" | custom-call | flops 1024 | bytes 36000000 | tf_op jit(solution)/shard_map/pallas_call | solution.py:423
  67.3 2.5 collective-permute-done.16.received
  70.8 3.0 %shard_map.242 = (f32[128,1024]{1,0:T(8,128)}, bf16[128,1024]{1,0:T(8,128)(2,1)}, bf16[128,1024]{1,0:T(8,128)(2,1)}, bf16[128,1024]{1,0:T(8,128)(2,1)}) custom-call(f32[512,1024]{1,0:T(8,128)} %get-tuple-element.126.keep, bf16[512,1024]{1,0:T(8,128)(2,1)} %copy-done.11), custom_call_target="tpu_custom_call" | custom-call | flops 1024 | bytes 1024 | tf_op jit(solution)/shard_map/pallas_call | solution.py:114
  74.9 1.5 collective-permute-start.19
  76.5 5.2 %collective-permute-done.17 = bf16[128,1024]{1,0:T(8,128)(2,1)S(1)} collective-permute-done((bf16[128,1024]{1,0:T(8,128)(2,1)}, bf16[128,1024]{1,0:T(8,128)(2,1)S(1)}, u32[]{:S(2)}, u32[]{:S(2)}) %collective-permute-start.17) | collective-permute-done | bytes 262176 | tf_op jit(solution)/shard_map/ppermute | solution.py:99
  82.0 5.1 %collective-permute-done.19 = bf16[128,1024]{1,0:T(8,128)(2,1)S(1)} collective-permute-done((bf16[128,1024]{1,0:T(8,128)(2,1)}, bf16[128,1024]{1,0:T(8,128)(2,1)S(1)}, u32[]{:S(2)}, u32[]{:S(2)}) %collective-permute-start.19) | collective-permute-done | bytes 262176 | tf_op jit(solution)/shard_map/ppermute | solution.py:99
  87.1 1.3 multiply_reduce_fusion.2
  88.6 1.5 collective-permute-start.22
  91.4 2.5 collective-permute-start.24
  93.9 1.9 collective-permute-done.22
  95.8 7.6 %collective-permute-done.21 = bf16[128,1024]{1,0:T(8,128)(2,1)S(1)} collective-permute-done((bf16[128,1024]{1,0:T(8,128)(2,1)S(1)}, bf16[128,1024]{1,0:T(8,128)(2,1)S(1)}, u32[]{:S(2)}, u32[]{:S(2)}) %collective-permute-start.21) | collective-permute-done | bytes 262176 | tf_op jit(solution)/shard_map/ppermute | solution.py:99
  105.2 1.4 collective-permute-done.23.x_o
  106.6 14.8 %all-gather.2.cloned.1.call-done.weight = bf16[1024,1792]{1,0:T(8,128)(2,1)} async-done(((bf16[256,1792]{1,0:T(8,128)(2,1)}), bf16[1024,1792]{1,0:T(8,128)(2,1)}) %all-gather.2.cloned.1.call-update) | async-done | bytes 3670032 | tf_op jit(solution)/shard_map/all_gather | solution.py:845
  121.5 20.0 %shard_map.243 = (bf16[512,1024]{1,0:T(8,128)(2,1)}, f32[512,1024]{1,0:T(8,128)}, bf16[512,1024]{1,0:T(8,128)(2,1)}, f32[512,1024]{1,0:T(8,128)}, bf16[1024,1792]{1,0:T(8,128)(2,1)}) custom-call(s32[3]{0:T(128)} %pad_add_fusion.where_ref.refs_0_, s32[4,4]{1,0:T(4,128)} %copy-done.34, bf16[512,1024]{1,0:T(8,128)(2,1)} %collective-permute-done.23.x_o, ...), custom_call_target="tpu_custom_call" | custom-call | flops 1024 | bytes 74000000 | tf_op jit(solution)/shard_map/pallas_call | solution.py:545
  141.5 1.2 copy-done.39
  143.2 2.3 collective-permute-done.25.received
  146.5 2.9 %shard_map.244 = (f32[128,1024]{1,0:T(8,128)}, bf16[128,1024]{1,0:T(8,128)(2,1)}, bf16[128,1024]{1,0:T(8,128)(2,1)}, bf16[128,1024]{1,0:T(8,128)(2,1)}) custom-call(f32[512,1024]{1,0:T(8,128)} %get-tuple-element.134.keep, bf16[512,1024]{1,0:T(8,128)(2,1)} %copy-done.12), custom_call_target="tpu_custom_call" | custom-call | flops 1024 | bytes 1024 | tf_op jit(solution)/shard_map/pallas_call | solution.py:114
  149.4 1.4 collective-permute-start.27
  150.9 1.2 collective-permute-start.28
  152.1 1.3 slice.28
  154.0 3.3 %collective-permute-done.26 = bf16[128,1024]{1,0:T(8,128)(2,1)S(1)} collective-permute-done((bf16[128,1024]{1,0:T(8,128)(2,1)}, bf16[128,1024]{1,0:T(8,128)(2,1)S(1)}, u32[]{:S(2)}, u32[]{:S(2)}) %collective-permute-start.26) | collective-permute-done | bytes 262176 | tf_op jit(solution)/shard_map/ppermute | solution.py:99
  157.2 6.5 %collective-permute-done.28 = bf16[128,1024]{1,0:T(8,128)(2,1)S(1)} collective-permute-done((bf16[128,1024]{1,0:T(8,128)(2,1)}, bf16[128,1024]{1,0:T(8,128)(2,1)S(1)}, u32[]{:S(2)}, u32[]{:S(2)}) %collective-permute-start.28) | collective-permute-done | bytes 262176 | tf_op jit(solution)/shard_map/ppermute | solution.py:99
  163.8 2.0 multiply_reduce_fusion
  166.0 1.2 collective-permute-start.31
  168.7 1.9 collective-permute-start.33
  170.7 3.2 %collective-permute-done.31 = bf16[128,1024]{1,0:T(8,128)(2,1)S(1)} collective-permute-done((bf16[128,1024]{1,0:T(8,128)(2,1)S(1)}, bf16[128,1024]{1,0:T(8,128)(2,1)S(1)}, u32[]{:S(2)}, u32[]{:S(2)}) %collective-permute-start.31) | collective-permute-done | bytes 262176 | tf_op jit(solution)/shard_map/ppermute | solution.py:99
  173.8 7.1 %collective-permute-done.30 = bf16[128,1024]{1,0:T(8,128)(2,1)S(1)} collective-permute-done((bf16[128,1024]{1,0:T(8,128)(2,1)S(1)}, bf16[128,1024]{1,0:T(8,128)(2,1)S(1)}, u32[]{:S(2)}, u32[]{:S(2)}) %collective-permute-start.30) | collective-permute-done | bytes 262176 | tf_op jit(solution)/shard_map/ppermute | solution.py:99
  181.5 3.0 %shard_map.245 = (f32[128,1024]{1,0:T(8,128)}, bf16[128,1024]{1,0:T(8,128)(2,1)}, bf16[128,1024]{1,0:T(8,128)(2,1)}, bf16[128,1024]{1,0:T(8,128)(2,1)}) custom-call(f32[512,1024]{1,0:T(8,128)} %get-tuple-element.141.keep, bf16[512,1024]{1,0:T(8,128)(2,1)} %collective-permute-done.33.received), custom_call_target="tpu_custom_call" | custom-call | flops 1024 | bytes 1024 | tf_op jit(solution)/shard_map/pallas_call | solution.py:114
  185.9 1.2 collective-permute-start.36
  187.1 16.1 %shard_map.246 = (bf16[512,1024]{1,0:T(8,128)(2,1)}, f32[512,1024]{1,0:T(8,128)}, f32[256,384]{1,0:T(8,128)}, f32[8,384]{1,0:T(8,128)}, bf16[272,384]{1,0:T(8,12...) custom-call(s32[3]{0:T(128)} %pad_add_fusion.where_ref.refs_0_, s32[4,4]{1,0:T(4,128)} %copy-done.34, ...), custom_call_target="tpu_custom_call" | custom-call | flops 1024 | bytes 24000000 | tf_op jit(solution)/shard_map/pallas_call | solution.py:449
  205.1 2.5 collective-permute-done.37.received
  207.6 2.7 reduce-scatter.2.cloned.1.call-done.own_ff
  210.3 3.8 %shard_map.247 = (f32[128,1024]{1,0:T(8,128)}, f32[64,1792]{1,0:T(8,128)}, bf16[256,1024]{1,0:T(8,128)(2,1)}, bf16[256,1024]{1,0:T(8,128)(2,1)}, bf16[256,1024]{1,0:T(8,128)(2,1)}) custom-call(s32[3]{0:T(128)} %pad_add_fusion.where_ref.refs_0_, f32[512,1024]{1,0:T(8,128)} %get-tuple-element.162.keep, bf16[512,1024]{1,0:T(8,128)(2,1)} %copy-done.14, ...), custom_call_target="tpu_custom_call" | custom-call | flops 1024 | bytes 1024 | tf_op jit(solution)/shard_map/pallas_call | solution.py:114
  214.3 1.3 collective-permute-start.39
  215.5 1.3 collective-permute-start.40
  216.8 1.2 collective-permute-start.41
  218.0 1.8 add_convert_fusion
  219.8 1.5 collective-permute-done.40.refs_0_
  221.3 14.4 %collective-permute-done.41.refs_1_ = bf16[272,384]{1,0:T(8,128)(2,1)} collective-permute-done((bf16[272,384]{1,0:T(8,128)(2,1)}, bf16[272,384]{1,0:T(8,128)(2,1)}, u32[]{:S(2)}, u32[]{:S(2)}) %collective-permute-start.41) | collective-permute-done | bytes 208928 | tf_op jit(solution)/shard_map/ppermute | solution.py:104
  235.8 2.1 shard_map.248
  237.8 1.2 collective-permute-start.43
  239.3 1.2 collective-permute-start.46
  241.1 1.2 collective-permute-start.44
  242.3 1.6 collective-permute-done.46.three
  244.6 1.7 shard_map.249
  246.3 13.8 %collective-permute-start.47 = (f32[8,384]{1,0:T(8,128)}, f32[8,384]{1,0:T(8,128)S(1)}, u32[]{:S(2)}, u32[]{:S(2)}) collective-permute-start(f32[8,384]{1,0:T(8,128)} %get-tuple-element.184), channel_id=1, source_target_pairs={{0,1},{1,0},{2,3},{3,2},{4,5},{5,4},{6,7},{7,6},{8,9},{9,8},{10,11... | collective-permute-start | bytes 36872 | tf_op jit(solution)/shard_map/ppermute | solution.py:108
  263.9 2.9 %shard_map.250 = (f32[64,2304]{1,0:T(8,128)}, f32[64,2304]{1,0:T(8,128)}, f32[64,2304]{1,0:T(8,128)}) custom-call(s32[3]{0:T(128)} %pad_add_fusion.where_ref.refs_0_, f32[64,1792]{1,0:T(8,128)} %get-tuple-element.189.own, bf16[256,1024]{1,0:T(8,128)(2,1)} %copy-done.5, bf16[256,1024]{1,0:T(8,128)(2,1)} %copy-done.6, bf16[256,1024]{1,0:T(8,128)(2,1)} %copy-done.7), custom_call_target="tpu_custom_call" | custom-call | flops 1024 | bytes 1024 | tf_op jit(solution)/shard_map/pallas_call | solution.py:114
  266.8 2.2 fusion.5
  (168 shorter events, 31.7 us)
Async XLA Ops:
  7.2 114.3 %all-gather.2.cloned.1.call-start = ((), (), s32[]{:S(2)}) async-start(), calls=%async_computation.1 | async-start | bytes 4587520 | tf_op jit(solution)/shard_map/all_gather | solution.py:845
  9.6 4.8 %collective-permute-start = (bf16[32,1024]{1,0:T(8,128)(2,1)}, bf16[32,1024]{1,0:T(8,128)(2,1)S(1)}, u32[]{:S(2)}, u32[]{:S(2)}) collective-permute-start(bf16[32,1024]{1,0:T(8,128)(2,1)} %get-tuple-element.104), channel_id=1, source_target_pairs={{0,2},{2,0},{4,6},{6,4},{8,10},{10,8},{12,14},{14,12},{16,18},{18,... | collective-permute-start | bytes 196616 | tf_op jit(solution)/shard_map/ppermute | solution.py:99
  9.9 4.6 %collective-permute-start.1 = (bf16[32,1024]{1,0:T(8,128)(2,1)}, bf16[32,1024]{1,0:T(8,128)(2,1)S(1)}, u32[]{:S(2)}, u32[]{:S(2)}) collective-permute-start(bf16[32,1024]{1,0:T(8,128)(2,1)} %get-tuple-element.105), channel_id=1, source_target_pairs={{0,4},{2,6},{4,0},{6,2},{8,12},{10,14},{12,8},{14,10},{16,20},{18,... | collective-permute-start | bytes 196616 | tf_op jit(solution)/shard_map/ppermute | solution.py:99
  11.1 4.6 %collective-permute-start.2 = (bf16[32,1024]{1,0:T(8,128)(2,1)}, bf16[32,1024]{1,0:T(8,128)(2,1)S(1)}, u32[]{:S(2)}, u32[]{:S(2)}) collective-permute-start(bf16[32,1024]{1,0:T(8,128)(2,1)} %get-tuple-element.106), channel_id=1, source_target_pairs={{0,6},{2,4},{4,2},{6,0},{8,14},{10,12},{12,10},{14,8},{16,22},{18,... | collective-permute-start | bytes 196616 | tf_op jit(solution)/shard_map/ppermute | solution.py:99
  14.4 32.1 %copy-start.4 = (bf16[128,1024]{1,0:T(8,128)(2,1)S(1)}, bf16[128,1024]{1,0:T(8,128)(2,1)}, u32[]{:S(2)}) copy-start(bf16[128,1024]{1,0:T(8,128)(2,1)} %param.14) | copy-start | bytes 786436
  18.0 15.6 %collective-permute-start.9 = (bf16[256,384]{1,0:T(8,128)(2,1)}, bf16[256,384]{1,0:T(8,128)(2,1)S(1)}, u32[]{:S(2)}, u32[]{:S(2)}) collective-permute-start(bf16[256,384]{1,0:T(8,128)(2,1)} %get-tuple-element.122.refs_9_), channel_id=1, source_target_pairs={{0,24},{2,26},{4,28},{6,30},{8,0},{10,2},{12,4},{14,6},{16,8},{18,... | collective-permute-start | bytes 589832 | tf_op jit(solution)/shard_map/ppermute | solution.py:104
  18.2 20.1 %collective-permute-start.8 = (bf16[256,384]{1,0:T(8,128)(2,1)}, bf16[256,384]{1,0:T(8,128)(2,1)S(1)}, u32[]{:S(2)}, u32[]{:S(2)}) collective-permute-start(bf16[256,384]{1,0:T(8,128)(2,1)} %get-tuple-element.122.refs_9_), channel_id=1, source_target_pairs={{0,16},{2,18},{4,20},{6,22},{8,24},{10,26},{12,28},{14,30},{16,0},... | collective-permute-start | bytes 589832 | tf_op jit(solution)/shard_map/ppermute | solution.py:104
  18.3 6.4 %collective-permute-start.5 = (bf16[128,1024]{1,0:T(8,128)(2,1)}, bf16[128,1024]{1,0:T(8,128)(2,1)S(1)}, u32[]{:S(2)}, u32[]{:S(2)}) collective-permute-start(bf16[128,1024]{1,0:T(8,128)(2,1)} %param.14), channel_id=1, source_target_pairs={{0,6},{2,4},{4,2},{6,0},{8,14},{10,12},{12,10},{14,8},{16,22},{18,... | collective-permute-start | bytes 786440 | tf_op jit(solution)/shard_map/ppermute | solution.py:99
  19.1 13.5 %collective-permute-start.4 = (bf16[128,1024]{1,0:T(8,128)(2,1)}, bf16[128,1024]{1,0:T(8,128)(2,1)S(1)}, u32[]{:S(2)}, u32[]{:S(2)}) collective-permute-start(bf16[128,1024]{1,0:T(8,128)(2,1)} %param.14), channel_id=1, source_target_pairs={{0,4},{2,6},{4,0},{6,2},{8,12},{10,14},{12,8},{14,10},{16,20},{18,... | collective-permute-start | bytes 786440 | tf_op jit(solution)/shard_map/ppermute | solution.py:99
  20.3 12.3 %collective-permute-start.3 = (bf16[128,1024]{1,0:T(8,128)(2,1)}, bf16[128,1024]{1,0:T(8,128)(2,1)S(1)}, u32[]{:S(2)}, u32[]{:S(2)}) collective-permute-start(bf16[128,1024]{1,0:T(8,128)(2,1)} %param.14), channel_id=1, source_target_pairs={{0,2},{2,0},{4,6},{6,4},{8,10},{10,8},{12,14},{14,12},{16,18},{18,... | collective-permute-start | bytes 786440 | tf_op jit(solution)/shard_map/ppermute | solution.py:99
  21.8 24.8 %copy-start.34 = (s32[4,4]{1,0:T(4,128)}, s32[4,4]{1,0:T(4,128)S(1)}, u32[]{:S(2)}) copy-start(s32[4,4]{1,0:T(4,128)S(1)} %reduce_window_sum.11.refs_1_.ends_ref) | copy-start | bytes 196
  24.7 13.6 %collective-permute-start.7 = (bf16[256,384]{1,0:T(8,128)(2,1)}, bf16[256,384]{1,0:T(8,128)(2,1)S(1)}, u32[]{:S(2)}, u32[]{:S(2)}) collective-permute-start(bf16[256,384]{1,0:T(8,128)(2,1)} %get-tuple-element.122.refs_9_), channel_id=1, source_target_pairs={{0,8},{2,10},{4,12},{6,14},{8,16},{10,18},{12,20},{14,22},{16,24},... | collective-permute-start | bytes 589832 | tf_op jit(solution)/shard_map/ppermute | solution.py:104
  32.6 5.7 %collective-permute-start.10 = (bf16[64,1792]{1,0:T(8,128)(2,1)}, bf16[64,1792]{1,0:T(8,128)(2,1)S(1)}, u32[]{:S(2)}, u32[]{:S(2)}) collective-permute-start(bf16[64,1792]{1,0:T(8,128)(2,1)} %get-tuple-element.115), channel_id=1, source_target_pairs={{0,2},{2,0},{4,6},{6,4},{8,10},{10,8},{12,14},{14,12},{16,18},{18,... | collective-permute-start | bytes 688136 | tf_op jit(solution)/shard_map/ppermute | solution.py:99
  33.6 7.1 %collective-permute-start.11 = (bf16[64,1792]{1,0:T(8,128)(2,1)}, bf16[64,1792]{1,0:T(8,128)(2,1)S(1)}, u32[]{:S(2)}, u32[]{:S(2)}) collective-permute-start(bf16[64,1792]{1,0:T(8,128)(2,1)} %get-tuple-element.116), channel_id=1, source_target_pairs={{0,4},{2,6},{4,0},{6,2},{8,12},{10,14},{12,8},{14,10},{16,20},{18,... | collective-permute-start | bytes 688136 | tf_op jit(solution)/shard_map/ppermute | solution.py:99
  33.7 9.5 %copy-start.24 = (bf16[256,384]{1,0:T(8,128)(2,1)}, bf16[256,384]{1,0:T(8,128)(2,1)S(1)}, u32[]{:S(2)}) copy-start(bf16[256,384]{1,0:T(8,128)(2,1)S(1)} %collective-permute-done.9.refs_12_) | copy-start | bytes 589828
  33.7 9.5 %collective-permute-start.12 = (bf16[64,1792]{1,0:T(8,128)(2,1)}, bf16[64,1792]{1,0:T(8,128)(2,1)S(1)}, u32[]{:S(2)}, u32[]{:S(2)}) collective-permute-start(bf16[64,1792]{1,0:T(8,128)(2,1)} %get-tuple-element.117), channel_id=1, source_target_pairs={{0,6},{2,4},{4,2},{6,0},{8,14},{10,12},{12,10},{14,8},{16,22},{18,... | collective-permute-start | bytes 688136 | tf_op jit(solution)/shard_map/ppermute | solution.py:99
  43.8 9.4 %copy-start.37 = (f32[64]{0:T(128)S(1)}, f32[64]{0:T(128)}, u32[]{:S(2)}) copy-start(f32[64]{0:T(128)} %param.18) | copy-start | bytes 772
  46.3 164.0 %reduce-scatter.2.cloned.1.call-start = ((), (), s32[]{:S(2)}) async-start(), calls=%async_computation.2 | async-start | bytes 4587520 | tf_op jit(solution)/shard_map/reduce_scatter | solution.py:872
  46.7 7.1 %collective-permute-start.6 = (bf16[512,1024]{1,0:T(8,128)(2,1)S(1)}, bf16[512,1024]{1,0:T(8,128)(2,1)S(1)}, u32[]{:S(2)}, u32[]{:S(2)}) collective-permute-start(bf16[512,1024]{1,0:T(8,128)(2,1)S(1)} %constant_dynamic-update-slice_fusion.refs_2_), channel_id=1, source_target_pairs={{0,1},{1,0},{2,3},{3,2},{4,5},{5,4},{6,7},{7,6},{8,9},{9,8},{10,11... | collective-permute-start | bytes 3145736 | tf_op jit(solution)/shard_map/ppermute | solution.py:108
  50.5 14.5 %collective-permute-start.15 = (bf16[128,1024]{1,0:T(8,128)(2,1)S(1)}, bf16[128,1024]{1,0:T(8,128)(2,1)S(1)}, u32[]{:S(2)}, u32[]{:S(2)}) collective-permute-start(bf16[128,1024]{1,0:T(8,128)(2,1)S(1)} %copy-done.13), channel_id=1, source_target_pairs={{0,6},{2,4},{4,2},{6,0},{8,14},{10,12},{12,10},{14,8},{16,22},{18,... | collective-permute-start | bytes 786440 | tf_op jit(solution)/shard_map/ppermute | solution.py:99
  51.3 13.9 %collective-permute-start.14 = (bf16[128,1024]{1,0:T(8,128)(2,1)S(1)}, bf16[128,1024]{1,0:T(8,128)(2,1)S(1)}, u32[]{:S(2)}, u32[]{:S(2)}) collective-permute-start(bf16[128,1024]{1,0:T(8,128)(2,1)S(1)} %copy-done.13), channel_id=1, source_target_pairs={{0,4},{2,6},{4,0},{6,2},{8,12},{10,14},{12,8},{14,10},{16,20},{18,... | collective-permute-start | bytes 786440 | tf_op jit(solution)/shard_map/ppermute | solution.py:99
  52.1 13.1 %collective-permute-start.13 = (bf16[128,1024]{1,0:T(8,128)(2,1)S(1)}, bf16[128,1024]{1,0:T(8,128)(2,1)S(1)}, u32[]{:S(2)}, u32[]{:S(2)}) collective-permute-start(bf16[128,1024]{1,0:T(8,128)(2,1)S(1)} %copy-done.13), channel_id=1, source_target_pairs={{0,2},{2,0},{4,6},{6,4},{8,10},{10,8},{12,14},{14,12},{16,18},{18,... | collective-permute-start | bytes 786440 | tf_op jit(solution)/shard_map/ppermute | solution.py:99
  66.6 3.2 %collective-permute-start.16 = (bf16[512,1024]{1,0:T(8,128)(2,1)}, bf16[512,1024]{1,0:T(8,128)(2,1)S(1)}, u32[]{:S(2)}, u32[]{:S(2)}) collective-permute-start(bf16[512,1024]{1,0:T(8,128)(2,1)} %get-tuple-element.129), channel_id=1, source_target_pairs={{0,1},{1,0},{2,3},{3,2},{4,5},{5,4},{6,7},{7,6},{8,9},{9,8},{10,11... | collective-permute-start | bytes 3145736 | tf_op jit(solution)/shard_map/ppermute | solution.py:108
  73.7 14.7 %copy-start.35 = (f32[1024]{0:T(1024)S(1)}, f32[1024]{0:T(1024)}, u32[]{:S(2)}) copy-start(f32[1024]{0:T(1024)} %param.19) | copy-start | bytes 12292
  73.7 17.5 %copy-start.19 = (bf16[128,1024]{1,0:T(8,128)(2,1)S(1)}, bf16[128,1024]{1,0:T(8,128)(2,1)}, u32[]{:S(2)}) copy-start(bf16[128,1024]{1,0:T(8,128)(2,1)} %copy-done.18) | copy-start | bytes 786436
  73.7 17.6 %copy-start.17 = (bf16[128,1024]{1,0:T(8,128)(2,1)S(1)}, bf16[128,1024]{1,0:T(8,128)(2,1)}, u32[]{:S(2)}) copy-start(bf16[128,1024]{1,0:T(8,128)(2,1)} %copy-done.16) | copy-start | bytes 786436
  73.7 7.9 %collective-permute-start.17 = (bf16[128,1024]{1,0:T(8,128)(2,1)}, bf16[128,1024]{1,0:T(8,128)(2,1)S(1)}, u32[]{:S(2)}, u32[]{:S(2)}) collective-permute-start(bf16[128,1024]{1,0:T(8,128)(2,1)} %get-tuple-element.131), channel_id=1, source_target_pairs={{0,2},{2,0},{4,6},{6,4},{8,10},{10,8},{12,14},{14,12},{16,18},{18,... | collective-permute-start | bytes 786440 | tf_op jit(solution)/shard_map/ppermute | solution.py:99
  74.2 7.8 %collective-permute-start.18 = (bf16[128,1024]{1,0:T(8,128)(2,1)}, bf16[128,1024]{1,0:T(8,128)(2,1)S(1)}, u32[]{:S(2)}, u32[]{:S(2)}) collective-permute-start(bf16[128,1024]{1,0:T(8,128)(2,1)} %get-tuple-element.132), channel_id=1, source_target_pairs={{0,4},{2,6},{4,0},{6,2},{8,12},{10,14},{12,8},{14,10},{16,20},{18,... | collective-permute-start | bytes 786440 | tf_op jit(solution)/shard_map/ppermute | solution.py:99
  74.9 12.2 %collective-permute-start.19 = (bf16[128,1024]{1,0:T(8,128)(2,1)}, bf16[128,1024]{1,0:T(8,128)(2,1)S(1)}, u32[]{:S(2)}, u32[]{:S(2)}) collective-permute-start(bf16[128,1024]{1,0:T(8,128)(2,1)} %get-tuple-element.133), channel_id=1, source_target_pairs={{0,6},{2,4},{4,2},{6,0},{8,14},{10,12},{12,10},{14,8},{16,22},{18,... | collective-permute-start | bytes 786440 | tf_op jit(solution)/shard_map/ppermute | solution.py:99
  88.6 7.3 %collective-permute-start.22 = (bf16[128,1024]{1,0:T(8,128)(2,1)S(1)}, bf16[128,1024]{1,0:T(8,128)(2,1)S(1)}, u32[]{:S(2)}, u32[]{:S(2)}) collective-permute-start(bf16[128,1024]{1,0:T(8,128)(2,1)S(1)} %multiply_convert_fusion), channel_id=1, source_target_pairs={{0,6},{2,4},{4,2},{6,0},{8,14},{10,12},{12,10},{14,8},{16,22},{18,... | collective-permute-start | bytes 786440 | tf_op jit(solution)/shard_map/ppermute | solution.py:99
  90.1 13.4 %collective-permute-start.21 = (bf16[128,1024]{1,0:T(8,128)(2,1)S(1)}, bf16[128,1024]{1,0:T(8,128)(2,1)S(1)}, u32[]{:S(2)}, u32[]{:S(2)}) collective-permute-start(bf16[128,1024]{1,0:T(8,128)(2,1)S(1)} %multiply_convert_fusion), channel_id=1, source_target_pairs={{0,4},{2,6},{4,0},{6,2},{8,12},{10,14},{12,8},{14,10},{16,20},{18,... | collective-permute-start | bytes 786440 | tf_op jit(solution)/shard_map/ppermute | solution.py:99
  90.8 12.6 %collective-permute-start.20 = (bf16[128,1024]{1,0:T(8,128)(2,1)S(1)}, bf16[128,1024]{1,0:T(8,128)(2,1)S(1)}, u32[]{:S(2)}, u32[]{:S(2)}) collective-permute-start(bf16[128,1024]{1,0:T(8,128)(2,1)S(1)} %multiply_convert_fusion), channel_id=1, source_target_pairs={{0,2},{2,0},{4,6},{6,4},{8,10},{10,8},{12,14},{14,12},{16,18},{18,... | collective-permute-start | bytes 786440 | tf_op jit(solution)/shard_map/ppermute | solution.py:99
  91.4 30.1 %copy-start.9 = (bf16[512,1024]{1,0:T(8,128)(2,1)}, bf16[512,1024]{1,0:T(8,128)(2,1)S(1)}, u32[]{:S(2)}) copy-start(bf16[512,1024]{1,0:T(8,128)(2,1)S(1)} %constant_dynamic-update-slice_fusion.4.g_m) | copy-start | bytes 3145732
  91.4 12.8 %collective-permute-start.24 = (bf16[512,1024]{1,0:T(8,128)(2,1)S(1)}, bf16[512,1024]{1,0:T(8,128)(2,1)S(1)}, u32[]{:S(2)}, u32[]{:S(2)}) collective-permute-start(bf16[512,1024]{1,0:T(8,128)(2,1)S(1)} %constant_dynamic-update-slice_fusion.4.g_m), channel_id=1, source_target_pairs={{0,1},{1,0},{2,3},{3,2},{4,5},{5,4},{6,7},{7,6},{8,9},{9,8},{10,11... | collective-permute-start | bytes 3145736 | tf_op jit(solution)/shard_map/ppermute | solution.py:108
  103.5 17.9 %copy-start.3 = (bf16[512,1024]{1,0:T(8,128)(2,1)}, bf16[512,1024]{1,0:T(8,128)(2,1)S(1)}, u32[]{:S(2)}) copy-start(bf16[512,1024]{1,0:T(8,128)(2,1)S(1)} %pad_maximum_fusion.x_m) | copy-start | bytes 3145732
  103.6 3.1 %collective-permute-start.23 = (bf16[512,1024]{1,0:T(8,128)(2,1)S(1)}, bf16[512,1024]{1,0:T(8,128)(2,1)}, u32[]{:S(2)}, u32[]{:S(2)}) collective-permute-start(bf16[512,1024]{1,0:T(8,128)(2,1)S(1)} %pad_maximum_fusion.x_m), channel_id=1, source_target_pairs={{0,1},{1,0},{2,3},{3,2},{4,5},{5,4},{6,7},{7,6},{8,9},{9,8},{10,11... | collective-permute-start | bytes 3145736 | tf_op jit(solution)/shard_map/ppermute | solution.py:108
  142.7 2.7 collective-permute-start.25
  149.4 7.8 %collective-permute-start.26 = (bf16[128,1024]{1,0:T(8,128)(2,1)}, bf16[128,1024]{1,0:T(8,128)(2,1)S(1)}, u32[]{:S(2)}, u32[]{:S(2)}) collective-permute-start(bf16[128,1024]{1,0:T(8,128)(2,1)} %get-tuple-element.137), channel_id=1, source_target_pairs={{0,2},{2,0},{4,6},{6,4},{8,10},{10,8},{12,14},{14,12},{16,18},{18,... | collective-permute-start | bytes 786440 | tf_op jit(solution)/shard_map/ppermute | solution.py:99
  149.4 7.8 %collective-permute-start.27 = (bf16[128,1024]{1,0:T(8,128)(2,1)}, bf16[128,1024]{1,0:T(8,128)(2,1)S(1)}, u32[]{:S(2)}, u32[]{:S(2)}) collective-permute-start(bf16[128,1024]{1,0:T(8,128)(2,1)} %get-tuple-element.138), channel_id=1, source_target_pairs={{0,4},{2,6},{4,0},{6,2},{8,12},{10,14},{12,8},{14,10},{16,20},{18,... | collective-permute-start | bytes 786440 | tf_op jit(solution)/shard_map/ppermute | solution.py:99
  150.9 12.9 %collective-permute-start.28 = (bf16[128,1024]{1,0:T(8,128)(2,1)}, bf16[128,1024]{1,0:T(8,128)(2,1)S(1)}, u32[]{:S(2)}, u32[]{:S(2)}) collective-permute-start(bf16[128,1024]{1,0:T(8,128)(2,1)} %get-tuple-element.139), channel_id=1, source_target_pairs={{0,6},{2,4},{4,2},{6,0},{8,14},{10,12},{12,10},{14,8},{16,22},{18,... | collective-permute-start | bytes 786440 | tf_op jit(solution)/shard_map/ppermute | solution.py:99
  166.0 7.8 %collective-permute-start.31 = (bf16[128,1024]{1,0:T(8,128)(2,1)S(1)}, bf16[128,1024]{1,0:T(8,128)(2,1)S(1)}, u32[]{:S(2)}, u32[]{:S(2)}) collective-permute-start(bf16[128,1024]{1,0:T(8,128)(2,1)S(1)} %get-tuple-element.195), channel_id=1, source_target_pairs={{0,6},{2,4},{4,2},{6,0},{8,14},{10,12},{12,10},{14,8},{16,22},{18,... | collective-permute-start | bytes 786440 | tf_op jit(solution)/shard_map/ppermute | solution.py:99
  167.2 13.7 %collective-permute-start.30 = (bf16[128,1024]{1,0:T(8,128)(2,1)S(1)}, bf16[128,1024]{1,0:T(8,128)(2,1)S(1)}, u32[]{:S(2)}, u32[]{:S(2)}) collective-permute-start(bf16[128,1024]{1,0:T(8,128)(2,1)S(1)} %get-tuple-element.195), channel_id=1, source_target_pairs={{0,4},{2,6},{4,0},{6,2},{8,12},{10,14},{12,8},{14,10},{16,20},{18,... | collective-permute-start | bytes 786440 | tf_op jit(solution)/shard_map/ppermute | solution.py:99
  167.6 13.3 %collective-permute-start.29 = (bf16[128,1024]{1,0:T(8,128)(2,1)S(1)}, bf16[128,1024]{1,0:T(8,128)(2,1)S(1)}, u32[]{:S(2)}, u32[]{:S(2)}) collective-permute-start(bf16[128,1024]{1,0:T(8,128)(2,1)S(1)} %get-tuple-element.195), channel_id=1, source_target_pairs={{0,2},{2,0},{4,6},{6,4},{8,10},{10,8},{12,14},{14,12},{16,18},{18,... | collective-permute-start | bytes 786440 | tf_op jit(solution)/shard_map/ppermute | solution.py:99
  168.7 12.7 %collective-permute-start.33 = (bf16[512,1024]{1,0:T(8,128)(2,1)S(1)}, bf16[512,1024]{1,0:T(8,128)(2,1)}, u32[]{:S(2)}, u32[]{:S(2)}) collective-permute-start(bf16[512,1024]{1,0:T(8,128)(2,1)S(1)} %copy-done.38), channel_id=1, source_target_pairs={{0,1},{1,0},{2,3},{3,2},{4,5},{5,4},{6,7},{7,6},{8,9},{9,8},{10,11... | collective-permute-start | bytes 3145736 | tf_op jit(solution)/shard_map/ppermute | solution.py:108
  181.0 3.4 %collective-permute-start.32 = (bf16[512,1024]{1,0:T(8,128)(2,1)S(1)}, bf16[512,1024]{1,0:T(8,128)(2,1)}, u32[]{:S(2)}, u32[]{:S(2)}) collective-permute-start(bf16[512,1024]{1,0:T(8,128)(2,1)S(1)} %pad_maximum_fusion.1.refs_9_), channel_id=1, source_target_pairs={{0,1},{1,0},{2,3},{3,2},{4,5},{5,4},{6,7},{7,6},{8,9},{9,8},{10,11... | collective-permute-start | bytes 3145736 | tf_op jit(solution)/shard_map/ppermute | solution.py:108
  184.4 18.8 %collective-permute-start.34 = (bf16[128,1024]{1,0:T(8,128)(2,1)}, bf16[128,1024]{1,0:T(8,128)(2,1)S(1)}, u32[]{:S(2)}, u32[]{:S(2)}) collective-permute-start(bf16[128,1024]{1,0:T(8,128)(2,1)} %get-tuple-element.148), channel_id=1, source_target_pairs={{0,2},{2,0},{4,6},{6,4},{8,10},{10,8},{12,14},{14,12},{16,18},{18,... | collective-permute-start | bytes 786440 | tf_op jit(solution)/shard_map/ppermute | solution.py:99
  184.8 18.4 %collective-permute-start.35 = (bf16[128,1024]{1,0:T(8,128)(2,1)}, bf16[128,1024]{1,0:T(8,128)(2,1)S(1)}, u32[]{:S(2)}, u32[]{:S(2)}) collective-permute-start(bf16[128,1024]{1,0:T(8,128)(2,1)} %get-tuple-element.149), channel_id=1, source_target_pairs={{0,4},{2,6},{4,0},{6,2},{8,12},{10,14},{12,8},{14,10},{16,20},{18,... | collective-permute-start | bytes 786440 | tf_op jit(solution)/shard_map/ppermute | solution.py:99
  185.9 17.3 %collective-permute-start.36 = (bf16[128,1024]{1,0:T(8,128)(2,1)}, bf16[128,1024]{1,0:T(8,128)(2,1)S(1)}, u32[]{:S(2)}, u32[]{:S(2)}) collective-permute-start(bf16[128,1024]{1,0:T(8,128)(2,1)} %get-tuple-element.150), channel_id=1, source_target_pairs={{0,6},{2,4},{4,2},{6,0},{8,14},{10,12},{12,10},{14,8},{16,22},{18,... | collective-permute-start | bytes 786440 | tf_op jit(solution)/shard_map/ppermute | solution.py:99
  203.2 14.8 %copy-start.15 = (f32[128,1024]{1,0:T(8,128)S(1)}, f32[128,1024]{1,0:T(8,128)}, u32[]{:S(2)}) copy-start(f32[128,1024]{1,0:T(8,128)} %get-tuple-element.147) | copy-start | bytes 1572868
  203.9 3.6 %collective-permute-start.37 = (bf16[512,1024]{1,0:T(8,128)(2,1)}, bf16[512,1024]{1,0:T(8,128)(2,1)S(1)}, u32[]{:S(2)}, u32[]{:S(2)}) collective-permute-start(bf16[512,1024]{1,0:T(8,128)(2,1)} %get-tuple-element.163), channel_id=1, source_target_pairs={{0,1},{1,0},{2,3},{3,2},{4,5},{5,4},{6,7},{7,6},{8,9},{9,8},{10,11... | collective-permute-start | bytes 3145736 | tf_op jit(solution)/shard_map/ppermute | solution.py:108
  214.1 49.0 %copy-start.8 = (f32[128,1024]{1,0:T(8,128)S(1)}, f32[128,1024]{1,0:T(8,128)}, u32[]{:S(2)}) copy-start(f32[128,1024]{1,0:T(8,128)} %get-tuple-element.165) | copy-start | bytes 1572868
  214.1 49.0 %copy-start.27 = (f32[1024]{0:T(1024)S(1)}, f32[1024]{0:T(1024)}, u32[]{:S(2)}) copy-start(f32[1024]{0:T(1024)} %param.16) | copy-start | bytes 12292
  214.1 29.9 %collective-permute-start.38 = (bf16[256,1024]{1,0:T(8,128)(2,1)}, bf16[256,1024]{1,0:T(8,128)(2,1)S(1)}, u32[]{:S(2)}, u32[]{:S(2)}) collective-permute-start(bf16[256,1024]{1,0:T(8,128)(2,1)} %get-tuple-element.166), channel_id=1, source_target_pairs={{0,2},{2,0},{4,6},{6,4},{8,10},{10,8},{12,14},{14,12},{16,18},{18,... | collective-permute-start | bytes 1572872 | tf_op jit(solution)/shard_map/ppermute | solution.py:99
  214.3 29.7 %collective-permute-start.39 = (bf16[256,1024]{1,0:T(8,128)(2,1)}, bf16[256,1024]{1,0:T(8,128)(2,1)S(1)}, u32[]{:S(2)}, u32[]{:S(2)}) collective-permute-start(bf16[256,1024]{1,0:T(8,128)(2,1)} %get-tuple-element.167), channel_id=1, source_target_pairs={{0,4},{2,6},{4,0},{6,2},{8,12},{10,14},{12,8},{14,10},{16,20},{18,... | collective-permute-start | bytes 1572872 | tf_op jit(solution)/shard_map/ppermute | solution.py:99
  215.5 5.8 %collective-permute-start.40 = (bf16[272,384]{1,0:T(8,128)(2,1)}, bf16[272,384]{1,0:T(8,128)(2,1)}, u32[]{:S(2)}, u32[]{:S(2)}) collective-permute-start(bf16[272,384]{1,0:T(8,128)(2,1)} %get-tuple-element.172), channel_id=1, source_target_pairs={{0,8},{2,10},{4,12},{6,14},{8,16},{10,18},{12,20},{14,22},{16,24},... | collective-permute-start | bytes 626696 | tf_op jit(solution)/shard_map/ppermute | solution.py:104
  216.8 18.9 %collective-permute-start.41 = (bf16[272,384]{1,0:T(8,128)(2,1)}, bf16[272,384]{1,0:T(8,128)(2,1)}, u32[]{:S(2)}, u32[]{:S(2)}) collective-permute-start(bf16[272,384]{1,0:T(8,128)(2,1)} %get-tuple-element.173), channel_id=1, source_target_pairs={{0,16},{2,18},{4,20},{6,22},{8,24},{10,26},{12,28},{14,30},{16,0},... | collective-permute-start | bytes 626696 | tf_op jit(solution)/shard_map/ppermute | solution.py:104
  218.0 17.8 %collective-permute-start.42 = (bf16[272,384]{1,0:T(8,128)(2,1)}, bf16[272,384]{1,0:T(8,128)(2,1)}, u32[]{:S(2)}, u32[]{:S(2)}) collective-permute-start(bf16[272,384]{1,0:T(8,128)(2,1)} %get-tuple-element.174), channel_id=1, source_target_pairs={{0,24},{2,26},{4,28},{6,30},{8,0},{10,2},{12,4},{14,6},{16,8},{18,... | collective-permute-start | bytes 626696 | tf_op jit(solution)/shard_map/ppermute | solution.py:104
  237.8 3.3 %collective-permute-start.43 = (bf16[80,384]{1,0:T(8,128)(2,1)}, bf16[80,384]{1,0:T(8,128)(2,1)S(1)}, u32[]{:S(2)}, u32[]{:S(2)}) collective-permute-start(bf16[80,384]{1,0:T(8,128)(2,1)} %get-tuple-element.175), channel_id=1, source_target_pairs={{0,2},{2,0},{4,6},{6,4},{8,10},{10,8},{12,14},{14,12},{16,18},{18,... | collective-permute-start | bytes 184328 | tf_op jit(solution)/shard_map/ppermute | solution.py:99
  239.1 3.3 %collective-permute-start.45 = (bf16[80,384]{1,0:T(8,128)(2,1)}, bf16[80,384]{1,0:T(8,128)(2,1)S(1)}, u32[]{:S(2)}, u32[]{:S(2)}) collective-permute-start(bf16[80,384]{1,0:T(8,128)(2,1)} %get-tuple-element.178), channel_id=1, source_target_pairs={{0,4},{2,6},{4,0},{6,2},{8,12},{10,14},{12,8},{14,10},{16,20},{18,... | collective-permute-start | bytes 184328 | tf_op jit(solution)/shard_map/ppermute | solution.py:99
  239.3 4.7 %collective-permute-start.46 = (bf16[80,384]{1,0:T(8,128)(2,1)}, bf16[80,384]{1,0:T(8,128)(2,1)S(1)}, u32[]{:S(2)}, u32[]{:S(2)}) collective-permute-start(bf16[80,384]{1,0:T(8,128)(2,1)} %get-tuple-element.179), channel_id=1, source_target_pairs={{0,6},{2,4},{4,2},{6,0},{8,14},{10,12},{12,10},{14,8},{16,22},{18,... | collective-permute-start | bytes 184328 | tf_op jit(solution)/shard_map/ppermute | solution.py:99
  241.1 22.0 %collective-permute-start.44 = (bf16[256,1024]{1,0:T(8,128)(2,1)}, bf16[256,1024]{1,0:T(8,128)(2,1)S(1)}, u32[]{:S(2)}, u32[]{:S(2)}) collective-permute-start(bf16[256,1024]{1,0:T(8,128)(2,1)} %get-tuple-element.176), channel_id=1, source_target_pairs={{0,6},{2,4},{4,2},{6,0},{8,14},{10,12},{12,10},{14,8},{16,22},{18,... | collective-permute-start | bytes 1572872 | tf_op jit(solution)/shard_map/ppermute | solution.py:99
  244.0 19.4 %copy-start.5 = (bf16[256,1024]{1,0:T(8,128)(2,1)}, bf16[256,1024]{1,0:T(8,128)(2,1)S(1)}, u32[]{:S(2)}) copy-start(bf16[256,1024]{1,0:T(8,128)(2,1)S(1)} %collective-permute-done.38.one) | copy-start | bytes 1572868
  244.0 19.4 %copy-start.6 = (bf16[256,1024]{1,0:T(8,128)(2,1)}, bf16[256,1024]{1,0:T(8,128)(2,1)S(1)}, u32[]{:S(2)}) copy-start(bf16[256,1024]{1,0:T(8,128)(2,1)S(1)} %collective-permute-done.39.two) | copy-start | bytes 1572868
  246.3 14.9 %collective-permute-start.47 = (f32[8,384]{1,0:T(8,128)}, f32[8,384]{1,0:T(8,128)S(1)}, u32[]{:S(2)}, u32[]{:S(2)}) collective-permute-start(f32[8,384]{1,0:T(8,128)} %get-tuple-element.184), channel_id=1, source_target_pairs={{0,1},{1,0},{2,3},{3,2},{4,5},{5,4},{6,7},{7,6},{8,9},{9,8},{10,11... | collective-permute-start | bytes 36872 | tf_op jit(solution)/shard_map/ppermute | solution.py:108
  (26 other events, 74.2 us)
Sparse Core Ops, SparseCore 0:
  46.4 74.9 all-gather.1
  141.6 68.6 reduce-scatter.1

commit v10 on v9

--- a/solution.py
+++ b/solution.py
@@ -90,6 +90,7 @@
 def cost(megabytes):
     return pl.CostEstimate(flops=1024, bytes_accessed=megabytes * 1000000, transcendentals=0)
 GAIN_ROWS = 8
+GROUPS_STEP = 2
 float32 = jnp.float32
 bfloat16 = jnp.bfloat16
 
@@ -274,43 +275,46 @@
 def attn_kernel(layers, where_ref, ends_ref, tok_m, tok_o, a_gain, q_gain, k_gain, cos, sin, *refs):
     pieces, refs = refs[:layers], refs[layers:]
     send, keep, pre_out, low_out, mixed_out, weight, held = refs
-    group = pl.program_id(0)
+    step = pl.program_id(0)
     depth, core = where_ref[1], where_ref[2]
-    local = tok_m.shape[0]
-
-    @pl.when(group == 0)
+    local = tok_m.shape[0] // GROUPS_STEP
+
+    @pl.when(step == 0)
     def _():
-        for step, piece in enumerate(pieces):
-            weight[deep_rows(depth, -step, layers, piece.shape[0]), :] = piece[...]
-
-    x = group_rows(core, tok_m[...].astype(float32), tok_o[...].astype(float32))
-    normed = (x * inverse_rms(x) * a_gain[...]).astype(bfloat16)
-    pre = matmul(normed, weight[:, : 2 * LANES])
-    pre_out[...] = pre
-    cosine, sine = cos[...], sin[...]
-    tiles = []
-    for number, gain in enumerate((q_gain[...], k_gain[...])):
-        tile = pre[:, number * LANES : (number + 1) * LANES]
-        scaled = tile * lax.rsqrt(head_mean(tile * tile) + epsilon) * gain
-        tiles.append(scaled * cosine + turn_halves(scaled) * sine)
-    lane = lane_ids(tiles[0].shape)
-    query = tiles[0].astype(bfloat16)
-    key_value = jnp.where(lane < HALF, tiles[1], pre[:, LANES:])
-    low_out[:, :LANES] = query
-    low_out[:, LANES:] = key_value.astype(bfloat16)
-    begin, row_ids, col_ids = group_mask(ends_ref, group, x.shape[0])
-    turned = pltpu.roll(key_value, HALF, 1)
-    mixed = jnp.zeros(tiles[0].shape, float32)
-    for head in range(2):
-        probs = group_probs(query, at_head(key_value, head), begin, row_ids, col_ids)
-        mixed += matmul(probs.astype(bfloat16), at_head(turned, head))
-    mixed = mixed.astype(bfloat16)
-    mixed_out[...] = mixed
-    held[...] = matmul_nt(mixed, weight[:, 2 * LANES :])
-    mine = pl.multiple_of(core * local, local)
-    other = pl.multiple_of((1 - core) * local, local)
-    send[...] = held[pl.ds(other, local), :].astype(bfloat16)
-    keep[...] = held[pl.ds(mine, local), :]
+        for index, piece in enumerate(pieces):
+            weight[deep_rows(depth, -index, layers, piece.shape[0]), :] = piece[...]
+
+    for k in range(GROUPS_STEP):
+        block = slice(k * local, (k + 1) * local)
+        span = slice(2 * k * local, 2 * (k + 1) * local)
+        x = group_rows(core, tok_m[block, :].astype(float32), tok_o[block, :].astype(float32))
+        normed = (x * inverse_rms(x) * a_gain[...]).astype(bfloat16)
+        pre = matmul(normed, weight[:, : 2 * LANES])
+        pre_out[span, :] = pre
+        cosine, sine = cos[span, :], sin[span, :]
+        tiles = []
+        for number, gain in enumerate((q_gain[...], k_gain[...])):
+            tile = pre[:, number * LANES : (number + 1) * LANES]
+            scaled = tile * lax.rsqrt(head_mean(tile * tile) + epsilon) * gain
+            tiles.append(scaled * cosine + turn_halves(scaled) * sine)
+        lane = lane_ids(tiles[0].shape)
+        query = tiles[0].astype(bfloat16)
+        key_value = jnp.where(lane < HALF, tiles[1], pre[:, LANES:])
+        low_out[span, :LANES] = query
+        low_out[span, LANES:] = key_value.astype(bfloat16)
+        begin, row_ids, col_ids = group_mask(ends_ref, GROUPS_STEP * step + k, x.shape[0])
+        turned = pltpu.roll(key_value, HALF, 1)
+        mixed = jnp.zeros(tiles[0].shape, float32)
+        for head in range(2):
+            probs = group_probs(query, at_head(key_value, head), begin, row_ids, col_ids)
+            mixed += matmul(probs.astype(bfloat16), at_head(turned, head))
+        mixed = mixed.astype(bfloat16)
+        mixed_out[span, :] = mixed
+        held[span, :] = matmul_nt(mixed, weight[:, 2 * LANES :])
+        mine = pl.multiple_of(2 * k * local + core * local, local)
+        other = pl.multiple_of(2 * k * local + (1 - core) * local, local)
+        send[block, :] = held[pl.ds(other, local), :].astype(bfloat16)
+        keep[block, :] = held[pl.ds(mine, local), :]
 
 
 def attn_back_kernel(
@@ -320,65 +324,72 @@
     send, keep, own, gains_out = refs[:4]
     pieces = refs[4 : 3 + layers]
     held, total, sum_a, sum_qk = refs[3 + layers :]
-    group = pl.program_id(0)
+    step = pl.program_id(0)
     depth, core = where_ref[1], where_ref[2]
-    local = tok_m.shape[0]
-
-    @pl.when(group == 0)
+    local = tok_m.shape[0] // GROUPS_STEP
+    scale = HEAD_DIM ** (-0.5)
+
+    @pl.when(step == 0)
     def _():
         total[...] = jnp.zeros_like(total)
         sum_a[...] = jnp.zeros_like(sum_a)
         sum_qk[...] = jnp.zeros_like(sum_qk)
 
-    x = group_rows(core, tok_m[...].astype(float32), tok_o[...].astype(float32))
-    unit_a = x * inverse_rms(x)
-    normed = (unit_a * a_gain[...]).astype(bfloat16)
-    d_hidden = group_rows(core, dh_m[...], dh_o[...])
-    mixed = mixed_ref[...]
-    total[:, 2 * LANES :] += matmul_tn(d_hidden, mixed)
-    d_mixed = matmul(d_hidden, weight[:, 2 * LANES :]).astype(bfloat16)
-    query = low_ref[:, :LANES]
-    key_value = low_ref[:, LANES:].astype(float32)
-    turned = pltpu.roll(key_value, HALF, 1)
-    begin, row_ids, col_ids = group_mask(ends_ref, group, x.shape[0])
-    scale = HEAD_DIM ** (-0.5)
-    shape = mixed.shape
-    d_query = jnp.zeros(shape, float32)
-    d_keys, d_values = [], []
-    for head in range(2):
-        key = at_head(key_value, head)
-        probs = group_probs(query, key, begin, row_ids, col_ids)
-        d_values.append(matmul_tn(probs.astype(bfloat16), d_mixed))
-        d_probs = matmul_nt(d_mixed, at_head(turned, head))
-        centre = jnp.sum(probs * d_probs, axis=1, keepdims=True)
-        d_scores = (probs * (d_probs - centre)).astype(bfloat16)
-        d_query += matmul(d_scores, key)
-        d_keys.append(matmul_tn(d_scores, query))
-    d_key = d_keys[0] + pltpu.roll(d_keys[1], HALF, 1)
-    d_value = pltpu.roll(d_values[0], HALF, 1) + d_values[1]
-    lane = lane_ids(shape)
-    cosine, sine = cos[...], sin[...]
-    tiles = []
-    for number, (grad, gain) in enumerate(((d_query, q_gain[...]), (d_key, k_gain[...]))):
-        grad = grad * scale
-        back = grad * cosine - turn_halves(grad) * sine
-        tile = pre_ref[:, number * LANES : (number + 1) * LANES]
-        factor = lax.rsqrt(head_mean(tile * tile) + epsilon)
-        unit = tile * factor
-        sum_qk[number : number + 1, :] += jnp.sum(back * unit, axis=0, keepdims=True)
-        back = back * gain
-        tiles.append(factor * (back - unit * head_mean(back * unit)))
-    tiles[1] = jnp.where(lane < HALF, tiles[1], d_value)
-    d_qkv = jnp.concatenate(tiles, axis=1).astype(bfloat16)
-    total[:, : 2 * LANES] += matmul_tn(normed, d_qkv)
-    held[...] = matmul_nt(d_qkv, weight[:, : 2 * LANES])
-    sum_a[...] += jnp.sum(held[...] * unit_a, axis=0, keepdims=True)
-    mine = pl.multiple_of(core * local, local)
-    other = pl.multiple_of((1 - core) * local, local)
-    send[...] = held[pl.ds(other, local), :].astype(bfloat16)
-    keep[...] = held[pl.ds(mine, local), :]
-
-    @pl.when(group == pl.num_programs(0) - 1)
+    normed_rows, d_qkv_rows, d_hidden_rows = [], [], []
+    for k in range(GROUPS_STEP):
+        block = slice(k * local, (k + 1) * local)
+        span = slice(2 * k * local, 2 * (k + 1) * local)
+        x = group_rows(core, tok_m[block, :].astype(float32), tok_o[block, :].astype(float32))
+        unit_a = x * inverse_rms(x)
+        normed_rows.append((unit_a * a_gain[...]).astype(bfloat16))
+        d_hidden = group_rows(core, dh_m[block, :], dh_o[block, :])
+        d_hidden_rows.append(d_hidden)
+        d_mixed = matmul(d_hidden, weight[:, 2 * LANES :]).astype(bfloat16)
+        query = low_ref[span, :LANES]
+        key_value = low_ref[span, LANES:].astype(float32)
+        turned = pltpu.roll(key_value, HALF, 1)
+        begin, row_ids, col_ids = group_mask(ends_ref, GROUPS_STEP * step + k, x.shape[0])
+        shape = query.shape
+        d_query = jnp.zeros(shape, float32)
+        d_keys, d_values = [], []
+        for head in range(2):
+            key = at_head(key_value, head)
+            probs = group_probs(query, key, begin, row_ids, col_ids)
+            d_values.append(matmul_tn(probs.astype(bfloat16), d_mixed))
+            d_probs = matmul_nt(d_mixed, at_head(turned, head))
+            centre = jnp.sum(probs * d_probs, axis=1, keepdims=True)
+            d_scores = (probs * (d_probs - centre)).astype(bfloat16)
+            d_query += matmul(d_scores, key)
+            d_keys.append(matmul_tn(d_scores, query))
+        d_key = d_keys[0] + pltpu.roll(d_keys[1], HALF, 1)
+        d_value = pltpu.roll(d_values[0], HALF, 1) + d_values[1]
+        lane = lane_ids(shape)
+        cosine, sine = cos[span, :], sin[span, :]
+        tiles = []
+        for number, (grad, gain) in enumerate(((d_query, q_gain[...]), (d_key, k_gain[...]))):
+            grad = grad * scale
+            back = grad * cosine - turn_halves(grad) * sine
+            tile = pre_ref[span, number * LANES : (number + 1) * LANES]
+            factor = lax.rsqrt(head_mean(tile * tile) + epsilon)
+            unit = tile * factor
+            sum_qk[number : number + 1, :] += jnp.sum(back * unit, axis=0, keepdims=True)
+            back = back * gain
+            tiles.append(factor * (back - unit * head_mean(back * unit)))
+        tiles[1] = jnp.where(lane < HALF, tiles[1], d_value)
+        d_qkv = jnp.concatenate(tiles, axis=1).astype(bfloat16)
+        d_qkv_rows.append(d_qkv)
+        held[span, :] = matmul_nt(d_qkv, weight[:, : 2 * LANES])
+        sum_a[...] += jnp.sum(held[span, :] * unit_a, axis=0, keepdims=True)
+        mine = pl.multiple_of(2 * k * local + core * local, local)
+        other = pl.multiple_of(2 * k * local + (1 - core) * local, local)
+        send[block, :] = held[pl.ds(other, local), :].astype(bfloat16)
+        keep[block, :] = held[pl.ds(mine, local), :]
+    total[:, : 2 * LANES] += matmul_tn(
+        jnp.concatenate(normed_rows, axis=0), jnp.concatenate(d_qkv_rows, axis=0)
+    )
+    total[:, 2 * LANES :] += matmul_tn(jnp.concatenate(d_hidden_rows, axis=0), mixed_ref[...])
+
+    @pl.when(step == pl.num_programs(0) - 1)
     def _():
         for row in range(GAIN_ROWS):
             gains_out[row : row + 1, :LANES] = sum_a[:, row * LANES : (row + 1) * LANES]
@@ -417,12 +428,13 @@
     layers = len(pieces)
     rows, width = tok_mine.shape
     local = rows // PLANE
-    scalar, block, gain, small, table, wide = attn_specs(local, width, 2 * local)
+    step = GROUPS_STEP * local
+    scalar, block, gain, small, table, wide = attn_specs(step, width, 2 * step)
     high, columns = pieces[0].shape
     weight = (layers * high, columns)
     return pl.pallas_call(
         lambda *refs: attn_kernel(layers, *refs),
-        grid=(PLANE,),
+        grid=(PLANE // GROUPS_STEP,),
         in_specs=[scalar, scalar, block, block, gain, small, small, table, table]
         + [whole_spec((high, columns))] * layers,
         out_specs=[block, block, wide, wide, table, whole_spec(weight)],
@@ -434,7 +446,7 @@
             jax.ShapeDtypeStruct((2 * rows, LANES), bfloat16),
             jax.ShapeDtypeStruct(weight, bfloat16),
         ],
-        scratch_shapes=[pltpu.VMEM((2 * local, width), float32)],
+        scratch_shapes=[pltpu.VMEM((2 * step, width), float32)],
         compiler_params=pltpu.CompilerParams(vmem_limit_bytes=VMEM_BYTES),
         cost_estimate=cost(36),
     )(where, ends, tok_mine, tok_other, *gains, *tables, *pieces)
@@ -443,12 +455,13 @@
 def attn_back(where, ends, layers, tok_mine, tok_other, gains, tables, dh, saved, weight, gain_ffn):
     rows, width = tok_mine.shape
     local = rows // PLANE
-    scalar, block, gain, small, table, wide = attn_specs(local, width, 2 * local)
+    step = GROUPS_STEP * local
+    scalar, block, gain, small, table, wide = attn_specs(step, width, 2 * step)
     high, columns = weight.shape[0] // layers, weight.shape[1]
     tail = 2 * GAIN_ROWS
     return pl.pallas_call(
         lambda *refs: attn_back_kernel(layers, *refs),
-        grid=(PLANE,),
+        grid=(PLANE // GROUPS_STEP,),
         in_specs=[scalar, scalar, block, block, gain, small, small, table, table, block, block]
         + [wide, wide, table, whole_spec(weight.shape), gain],
         out_specs=[block, block, whole_spec((high, columns)), whole_spec((GAIN_ROWS, columns))]
@@ -461,7 +474,7 @@
         ]
         + [jax.ShapeDtypeStruct((high + tail, columns), bfloat16)] * (layers - 1),
         scratch_shapes=[
-            pltpu.VMEM((2 * local, width), float32),
+            pltpu.VMEM((2 * step, width), float32),
             pltpu.VMEM(weight.shape, float32),
             pltpu.VMEM((1, width), float32),
             pltpu.VMEM((8, LANES), float32),
@@ -818,7 +831,7 @@
         w_down,
         scalars=1,
     )
-    first = [first[0]] + [send_plane(first[m], m) for m in range(1, PLANE)]
+    first = after(second, [first[0]] + [send_plane(first[m], m) for m in range(1, PLANE)])
     attn_piece, lens = call(
         unpack_attn_kernel,
         [((PLANE * rows, attn_cols), bfloat16), ((PLANE * 8, LANES), float32)],
@@ -828,8 +841,7 @@
         scratch=[pltpu.VMEM((PLANE * rows, attn_cols), float32)],
     )
     attn_pieces = [attn_piece] + [send_deep(attn_piece, step) for step in range(1, layers)]
-    tok_parts = plane_parts(after(first[1], tokens))
-    second = after((first, tok_parts), second)
+    second = after(first, second)
     second = [second[0]] + [send_plane(second[m], m) for m in range(1, PLANE)]
     ends, tables = row_tables(lens, lengths.shape[1], total_rows)
     second = after((attn_pieces, tables), second)
@@ -844,7 +856,8 @@
     columns = [list(range(k, layers * PLANE, PLANE)) for k in range(PLANE)]
     ff_weight = lax.all_gather(ff_piece, "dp", axis=0, tiled=True, axis_index_groups=columns)
     attn_pieces = after(ff_piece, attn_pieces)
-    cot_parts = plane_parts(after(second, cotangent))
+    tok_parts = plane_parts(after(ff_piece, tokens))
+    cot_parts = plane_parts(after(tok_parts, cotangent))
     tok_mine, tok_other = both_cores(tok_parts)
     cot_mine, cot_other = both_cores(cot_parts)
 
@@ -897,12 +910,10 @@
     )
     attn_grads = [send_deep(piece, step + 1) for step, piece in enumerate(attn_grads)]
     own_dn, own_ff, *messages = tail_messages(where, keep, swap_cores(send), own_ff)
-    own_attn = after((messages, block_out), own_attn)
+    own_attn = after(messages, own_attn)
+    messages = [send_plane(part, mask + 1) for mask, part in enumerate(messages)]
     attn_parts = plane_split_attn(where, own_attn, attn_grads, part_gains)
-    attn_parts = plane_sent(attn_parts)
-    messages = messages[:2] + after(attn_parts[1], messages[2:])
-    messages = [send_plane(part, mask + 1) for mask, part in enumerate(messages)]
-    attn_parts = after(messages[:2], attn_parts)
+    attn_parts = after(messages[:2], plane_sent(attn_parts))
     d_normed = own_dn + add_up([part[:local_rows] for part in messages])
     grad_tokens = d_hidden + norm_back(d_normed * attn_gain, unit_a, factor_a)
     grad_gate, grad_up, grad_down = call(

time: 277 us -> 257 us (0.928)
  the two profiles are of different devices: /device:TPU:27 before, /device:TPU:0 now
where the time goes in v10:
time: 257 us; the launch traced here: 256 us
  waiting for transfers between devices  93.4 us (36%)
  Pallas kernels  73.9 us (29%)
  starting transfers between devices  49.2 us (19%)
  between operations  14.6 us (6%)
  other arithmetic  12.4 us (5%)
  local copies, waits for them, and re-layouts  12.1 us (5%)
    ppermute x33, waiting for transfers between devices, send_plane(): return lax.ppermute(values, 'dp', [(i, i ^ mask) for i in range(count)])  67.4 us
    ppermute x33, starting transfers between devices, send_plane(): return lax.ppermute(values, 'dp', [(i, i ^ mask) for i in range(count)])  40.1 us
    pallas_call x11, Pallas kernels, call(): pl.pallas_call(kernel, out_shape=[jax.ShapeDtypeStruct(shape, kind) for s...  28.1 us
    pallas_call x1, Pallas kernels, ffn(): pl.pallas_call(ffn_kernel, grid=(2,), in_specs=[scalar, scalar] + [row_sp...  20 us
    pallas_call x1, Pallas kernels, attn_back(): pl.pallas_call(lambda *refs: attn_back_kernel(layers, *refs), grid=(PLANE...  15.5 us
    ppermute x6, waiting for transfers between devices, send_deep(): lax.ppermute(values, 'dp', [(i, (i + PLANE * step) % count) for i in rang...  14.7 us
    pallas_call x1, Pallas kernels, attn(): pl.pallas_call(lambda *refs: attn_kernel(layers, *refs), grid=(PLANE // G...  10.4 us
    unnamed x87, local copies, waits for them, and re-layouts  8.94 us
  transfers between devices with their start and end apart: 50, of which 23 were waited for; matrix products, arithmetic and copies ran while one was open for 5% of the time, Pallas kernels for 19%

profile of v10, /device:TPU:0, one launch (start us, length us, event | category | flops | bytes accessed | tf_op | source)
XLA Modules:
  0.0 255.6 jit_solution(10216704574669992627)
XLA Ops:
  7.9 1.7 shard_map.238
  9.6 2.9 %collective-permute-start = (bf16[32,1024]{1,0:T(8,128)(2,1)}, bf16[32,1024]{1,0:T(8,128)(2,1)S(1)}, u32[]{:S(2)}, u32[]{:S(2)}) collective-permute-start(bf16[32,1024]{1,0:T(8,128)(2,1)} %get-tuple-element.111), channel_id=1, source_target_pairs={{0,2},{2,0},{4,6},{6,4},{8,10},{10,8},{12,14},{14,12},{16,18},{18,... | collective-permute-start | bytes 196616 | tf_op jit(solution)/shard_map/ppermute | solution.py:100
  12.5 1.5 collective-permute-start.1
  14.1 2.2 shard_map.237
  17.0 2.4 collective-permute-done.2.three
  20.1 1.7 shard_map.239
  21.8 3.6 %collective-permute-start.5 = (bf16[256,384]{1,0:T(8,128)(2,1)}, bf16[256,384]{1,0:T(8,128)(2,1)S(1)}, u32[]{:S(2)}, u32[]{:S(2)}) collective-permute-start(bf16[256,384]{1,0:T(8,128)(2,1)} %get-tuple-element.129.refs_9_), channel_id=1, source_target_pairs={{0,24},{2,26},{4,28},{6,30},{8,0},{10,2},{12,4},{14,6},{16,8},{18,... | collective-permute-start | bytes 589832 | tf_op jit(solution)/shard_map/ppermute | solution.py:105
  28.5 2.6 collective-permute-done.5.refs_12_
  31.6 3.0 %fusion.6 = (f32[1024,128]{1,0:T(8,128)}, f32[1024,128]{1,0:T(8,128)}) fusion(f32[128]{0:T(128)S(1)} %get-tuple-element.213, f32[128]{0:T(128)S(1)} %get-tuple-element.214, f32[1024]{0:T(1024)S(1)} %bitcast.28), kind=kLoop, calls=%fused_computation.13 | loop fusion | flops 262144 | bytes 1053696 | tf_op jit(solution)/shard_map/mul | solution.py:779
  34.6 6.7 %collective-permute-done.4.refs_11_ = bf16[256,384]{1,0:T(8,128)(2,1)S(1)} collective-permute-done((bf16[256,384]{1,0:T(8,128)(2,1)}, bf16[256,384]{1,0:T(8,128)(2,1)S(1)}, u32[]{:S(2)}, u32[]{:S(2)}) %collective-permute-start.4) | collective-permute-done | bytes 196640 | tf_op jit(solution)/shard_map/ppermute | solution.py:105
  42.2 2.5 shard_map.240
  45.9 2.4 collective-permute-start.11
  48.4 5.7 %collective-permute-done.9 = bf16[128,1024]{1,0:T(8,128)(2,1)S(1)} collective-permute-done((bf16[128,1024]{1,0:T(8,128)(2,1)S(1)}, bf16[128,1024]{1,0:T(8,128)(2,1)S(1)}, u32[]{:S(2)}, u32[]{:S(2)}) %collective-permute-start.9) | collective-permute-done | bytes 262176 | tf_op jit(solution)/shard_map/ppermute | solution.py:100
  54.1 3.5 %collective-permute-done.10 = bf16[128,1024]{1,0:T(8,128)(2,1)S(1)} collective-permute-done((bf16[128,1024]{1,0:T(8,128)(2,1)S(1)}, bf16[128,1024]{1,0:T(8,128)(2,1)S(1)}, u32[]{:S(2)}, u32[]{:S(2)}) %collective-permute-start.10) | collective-permute-done | bytes 262176 | tf_op jit(solution)/shard_map/ppermute | solution.py:100
  57.8 1.2 collective-permute-start.15
  59.0 1.4 collective-permute-start.14
  62.9 10.4 %shard_map.241 = (bf16[512,1024]{1,0:T(8,128)(2,1)}, f32[512,1024]{1,0:T(8,128)}, f32[1024,256]{1,0:T(8,128)}, bf16[1024,256]{1,0:T(8,128)(2,1)}, bf16[1024,128]{1,0:T(8,128)(2,1)}, /*index=5*/bf16[1024,384]{1,0:T(8,128)(2,1)}) custom-call(s32[3]{0:T(128)} %pad_add_fusion.where_ref.refs_0_, s32[4,4]{1,0:T(4,128)} %copy-done.33, bf16[512,1024]{1,0:T(8,128)(2,1)} %copy-done, ...), custom_call_target="tpu_custom_call" | custom-call | flops 1024 | bytes 36000000 | tf_op jit(solution)/shard_map/pallas_call | solution.py:435
  74.8 2.9 %collective-permute-done.16.received = bf16[512,1024]{1,0:T(8,128)(2,1)S(1)} collective-permute-done((bf16[512,1024]{1,0:T(8,128)(2,1)}, bf16[512,1024]{1,0:T(8,128)(2,1)S(1)}, u32[]{:S(2)}, u32[]{:S(2)}) %collective-permute-start.16) | collective-permute-done | bytes 1048608 | tf_op jit(solution)/shard_map/ppermute | solution.py:109
  78.6 3.0 %shard_map.242 = (f32[128,1024]{1,0:T(8,128)}, bf16[128,1024]{1,0:T(8,128)(2,1)}, bf16[128,1024]{1,0:T(8,128)(2,1)}, bf16[128,1024]{1,0:T(8,128)(2,1)}) custom-call(f32[512,1024]{1,0:T(8,128)} %get-tuple-element.133.keep, bf16[512,1024]{1,0:T(8,128)(2,1)} %copy-done.11), custom_call_target="tpu_custom_call" | custom-call | flops 1024 | bytes 1024 | tf_op jit(solution)/shard_map/pallas_call | solution.py:115
  81.6 1.1 collective-permute-start.17
  83.3 1.8 collective-permute-start.19
  85.2 5.9 %collective-permute-done.17 = bf16[128,1024]{1,0:T(8,128)(2,1)S(1)} collective-permute-done((bf16[128,1024]{1,0:T(8,128)(2,1)}, bf16[128,1024]{1,0:T(8,128)(2,1)S(1)}, u32[]{:S(2)}, u32[]{:S(2)}) %collective-permute-start.17) | collective-permute-done | bytes 262176 | tf_op jit(solution)/shard_map/ppermute | solution.py:100
  91.0 5.6 %collective-permute-done.18 = bf16[128,1024]{1,0:T(8,128)(2,1)S(1)} collective-permute-done((bf16[128,1024]{1,0:T(8,128)(2,1)}, bf16[128,1024]{1,0:T(8,128)(2,1)S(1)}, u32[]{:S(2)}, u32[]{:S(2)}) %collective-permute-start.18) | collective-permute-done | bytes 262176 | tf_op jit(solution)/shard_map/ppermute | solution.py:100
  96.6 1.3 multiply_reduce_fusion.2
  98.1 1.2 collective-permute-start.22
  99.3 1.2 collective-permute-start.21
  100.6 1.1 collective-permute-start.20
  101.8 6.5 %collective-permute-done.22 = bf16[128,1024]{1,0:T(8,128)(2,1)S(1)} collective-permute-done((bf16[128,1024]{1,0:T(8,128)(2,1)S(1)}, bf16[128,1024]{1,0:T(8,128)(2,1)S(1)}, u32[]{:S(2)}, u32[]{:S(2)}) %collective-permute-start.22) | collective-permute-done | bytes 262176 | tf_op jit(solution)/shard_map/ppermute | solution.py:100
  108.3 3.4 %collective-permute-done.21 = bf16[128,1024]{1,0:T(8,128)(2,1)S(1)} collective-permute-done((bf16[128,1024]{1,0:T(8,128)(2,1)S(1)}, bf16[128,1024]{1,0:T(8,128)(2,1)S(1)}, u32[]{:S(2)}, u32[]{:S(2)}) %collective-permute-start.21) | collective-permute-done | bytes 262176 | tf_op jit(solution)/shard_map/ppermute | solution.py:100
  112.0 1.1 copy-done.10
  113.1 1.5 collective-permute-done.23.x_o
  114.6 3.2 %all-gather.2.cloned.1.call-done.weight = bf16[1024,1792]{1,0:T(8,128)(2,1)} async-done(((bf16[256,1792]{1,0:T(8,128)(2,1)}), bf16[1024,1792]{1,0:T(8,128)(2,1)}) %all-gather.2.cloned.1.call-update) | async-done | bytes 3670032 | tf_op jit(solution)/shard_map/all_gather | solution.py:857
  117.8 20.0 %shard_map.243 = (bf16[512,1024]{1,0:T(8,128)(2,1)}, f32[512,1024]{1,0:T(8,128)}, bf16[512,1024]{1,0:T(8,128)(2,1)}, f32[512,1024]{1,0:T(8,128)}, bf16[1024,1792]{1,0:T(8,128)(2,1)}) custom-call(s32[3]{0:T(128)} %pad_add_fusion.where_ref.refs_0_, s32[4,4]{1,0:T(4,128)} %copy-done.33, bf16[512,1024]{1,0:T(8,128)(2,1)} %collective-permute-done.23.x_o, ...), custom_call_target="tpu_custom_call" | custom-call | flops 1024 | bytes 74000000 | tf_op jit(solution)/shard_map/pallas_call | solution.py:558
  137.9 1.2 copy-done.39
  139.1 2.7 %collective-permute-done.25.received = bf16[512,1024]{1,0:T(8,128)(2,1)S(1)} collective-permute-done((bf16[512,1024]{1,0:T(8,128)(2,1)S(1)}, bf16[512,1024]{1,0:T(8,128)(2,1)S(1)}, u32[]{:S(2)}, u32[]{:S(2)}) %collective-permute-start.25) | collective-permute-done | bytes 1048608 | tf_op jit(solution)/shard_map/ppermute | solution.py:109
  142.8 3.1 %shard_map.244 = (f32[128,1024]{1,0:T(8,128)}, bf16[128,1024]{1,0:T(8,128)(2,1)}, bf16[128,1024]{1,0:T(8,128)(2,1)}, bf16[128,1024]{1,0:T(8,128)(2,1)}) custom-call(f32[512,1024]{1,0:T(8,128)} %get-tuple-element.141.keep, bf16[512,1024]{1,0:T(8,128)(2,1)} %copy-done.12), custom_call_target="tpu_custom_call" | custom-call | flops 1024 | bytes 1024 | tf_op jit(solution)/shard_map/pallas_call | solution.py:115
  145.8 1.7 collective-permute-start.26
  147.5 1.5 collective-permute-start.27
  149.3 1.3 slice.28
  151.3 3.9 %collective-permute-done.26 = bf16[128,1024]{1,0:T(8,128)(2,1)S(1)} collective-permute-done((bf16[128,1024]{1,0:T(8,128)(2,1)}, bf16[128,1024]{1,0:T(8,128)(2,1)S(1)}, u32[]{:S(2)}, u32[]{:S(2)}) %collective-permute-start.26) | collective-permute-done | bytes 262176 | tf_op jit(solution)/shard_map/ppermute | solution.py:100
  155.2 6.2 %collective-permute-done.27 = bf16[128,1024]{1,0:T(8,128)(2,1)S(1)} collective-permute-done((bf16[128,1024]{1,0:T(8,128)(2,1)}, bf16[128,1024]{1,0:T(8,128)(2,1)S(1)}, u32[]{:S(2)}, u32[]{:S(2)}) %collective-permute-start.27) | collective-permute-done | bytes 262176 | tf_op jit(solution)/shard_map/ppermute | solution.py:100
  161.4 2.0 multiply_reduce_fusion
  163.7 1.6 collective-permute-start.31
  165.2 1.2 collective-permute-start.30
  167.2 6.7 %collective-permute-done.31 = bf16[128,1024]{1,0:T(8,128)(2,1)S(1)} collective-permute-done((bf16[128,1024]{1,0:T(8,128)(2,1)S(1)}, bf16[128,1024]{1,0:T(8,128)(2,1)S(1)}, u32[]{:S(2)}, u32[]{:S(2)}) %collective-permute-start.31) | collective-permute-done | bytes 262176 | tf_op jit(solution)/shard_map/ppermute | solution.py:100
  173.9 3.6 %collective-permute-done.30 = bf16[128,1024]{1,0:T(8,128)(2,1)S(1)} collective-permute-done((bf16[128,1024]{1,0:T(8,128)(2,1)S(1)}, bf16[128,1024]{1,0:T(8,128)(2,1)S(1)}, u32[]{:S(2)}, u32[]{:S(2)}) %collective-permute-start.30) | collective-permute-done | bytes 262176 | tf_op jit(solution)/shard_map/ppermute | solution.py:100
  177.8 3.2 %shard_map.245 = (f32[128,1024]{1,0:T(8,128)}, bf16[128,1024]{1,0:T(8,128)(2,1)}, bf16[128,1024]{1,0:T(8,128)(2,1)}, bf16[128,1024]{1,0:T(8,128)(2,1)}) custom-call(f32[512,1024]{1,0:T(8,128)} %get-tuple-element.148.keep, bf16[512,1024]{1,0:T(8,128)(2,1)} %collective-permute-done.33.received), custom_call_target="tpu_custom_call" | custom-call | flops 1024 | bytes 1024 | tf_op jit(solution)/shard_map/pallas_call | solution.py:115
  181.1 1.4 collective-permute-start.34
  183.1 1.5 collective-permute-start.36
  184.6 15.5 %shard_map.246 = (bf16[512,1024]{1,0:T(8,128)(2,1)}, f32[512,1024]{1,0:T(8,128)}, f32[256,384]{1,0:T(8,128)}, f32[8,384]{1,0:T(8,128)}, bf16[272,384]{1,0:T(8,12...) custom-call(s32[3]{0:T(128)} %pad_add_fusion.where_ref.refs_0_, s32[4,4]{1,0:T(4,128)} %copy-done.33, ...), custom_call_target="tpu_custom_call" | custom-call | flops 1024 | bytes 24000000 | tf_op jit(solution)/shard_map/pallas_call | solution.py:462
  200.2 1.1 collective-permute-start.42
  201.3 2.7 %collective-permute-start.43 = (bf16[272,384]{1,0:T(8,128)(2,1)}, bf16[272,384]{1,0:T(8,128)(2,1)}, u32[]{:S(2)}, u32[]{:S(2)}) collective-permute-start(bf16[272,384]{1,0:T(8,128)(2,1)} %get-tuple-element.181), channel_id=1, source_target_pairs={{0,24},{2,26},{4,28},{6,30},{8,0},{10,2},{12,4},{14,6},{16,8},{18,... | collective-permute-start | bytes 626696 | tf_op jit(solution)/shard_map/ppermute | solution.py:105
  205.1 3.8 %shard_map.247 = (f32[128,1024]{1,0:T(8,128)}, f32[64,1792]{1,0:T(8,128)}, bf16[256,1024]{1,0:T(8,128)(2,1)}, bf16[256,1024]{1,0:T(8,128)(2,1)}, bf16[256,1024]{1,0:T(8,128)(2,1)}) custom-call(s32[3]{0:T(128)} %pad_add_fusion.where_ref.refs_0_, f32[512,1024]{1,0:T(8,128)} %get-tuple-element.169.keep, bf16[512,1024]{1,0:T(8,128)(2,1)} %copy-done.14, ...), custom_call_target="tpu_custom_call" | custom-call | flops 1024 | bytes 1024 | tf_op jit(solution)/shard_map/pallas_call | solution.py:115
  208.8 1.5 collective-permute-start.38
  210.3 1.8 collective-permute-start.39
  213.1 5.4 %collective-permute-done.42.refs_1_ = bf16[272,384]{1,0:T(8,128)(2,1)} collective-permute-done((bf16[272,384]{1,0:T(8,128)(2,1)}, bf16[272,384]{1,0:T(8,128)(2,1)}, u32[]{:S(2)}, u32[]{:S(2)}) %collective-permute-start.42) | collective-permute-done | bytes 208928 | tf_op jit(solution)/shard_map/ppermute | solution.py:105
  218.5 2.1 shard_map.248
  220.6 1.4 collective-permute-start.44
  222.0 1.2 collective-permute-start.45
  223.2 12.1 %collective-permute-done.44.one = bf16[80,384]{1,0:T(8,128)(2,1)S(1)} collective-permute-done((bf16[80,384]{1,0:T(8,128)(2,1)}, bf16[80,384]{1,0:T(8,128)(2,1)S(1)}, u32[]{:S(2)}, u32[]{:S(2)}) %collective-permute-start.44) | collective-permute-done | bytes 61472 | tf_op jit(solution)/shard_map/ppermute | solution.py:100
  235.3 2.4 collective-permute-start.46
  237.7 2.0 add_convert_fusion
  241.2 1.9 shard_map.249
  244.6 2.9 %shard_map.250 = (f32[64,2304]{1,0:T(8,128)}, f32[64,2304]{1,0:T(8,128)}, f32[64,2304]{1,0:T(8,128)}) custom-call(s32[3]{0:T(128)} %pad_add_fusion.where_ref.refs_0_, f32[64,1792]{1,0:T(8,128)} %get-tuple-element.195.own, bf16[256,1024]{1,0:T(8,128)(2,1)} %copy-done.5, bf16[256,1024]{1,0:T(8,128)(2,1)} %copy-done.6, bf16[256,1024]{1,0:T(8,128)(2,1)} %copy-done.7), custom_call_target="tpu_custom_call" | custom-call | flops 1024 | bytes 1024 | tf_op jit(solution)/shard_map/pallas_call | solution.py:115
  (168 shorter events, 24.1 us)
Async XLA Ops:
  7.2 110.7 %all-gather.2.cloned.1.call-start = ((), (), s32[]{:S(2)}) async-start(), calls=%async_computation.1 | async-start | bytes 4587520 | tf_op jit(solution)/shard_map/all_gather | solution.py:857
  9.6 6.6 %collective-permute-start = (bf16[32,1024]{1,0:T(8,128)(2,1)}, bf16[32,1024]{1,0:T(8,128)(2,1)S(1)}, u32[]{:S(2)}, u32[]{:S(2)}) collective-permute-start(bf16[32,1024]{1,0:T(8,128)(2,1)} %get-tuple-element.111), channel_id=1, source_target_pairs={{0,2},{2,0},{4,6},{6,4},{8,10},{10,8},{12,14},{14,12},{16,18},{18,... | collective-permute-start | bytes 196616 | tf_op jit(solution)/shard_map/ppermute | solution.py:100
  12.5 4.5 %collective-permute-start.1 = (bf16[32,1024]{1,0:T(8,128)(2,1)}, bf16[32,1024]{1,0:T(8,128)(2,1)S(1)}, u32[]{:S(2)}, u32[]{:S(2)}) collective-permute-start(bf16[32,1024]{1,0:T(8,128)(2,1)} %get-tuple-element.112), channel_id=1, source_target_pairs={{0,4},{2,6},{4,0},{6,2},{8,12},{10,14},{12,8},{14,10},{16,20},{18,... | collective-permute-start | bytes 196616 | tf_op jit(solution)/shard_map/ppermute | solution.py:100
  14.1 5.4 %collective-permute-start.2 = (bf16[32,1024]{1,0:T(8,128)(2,1)}, bf16[32,1024]{1,0:T(8,128)(2,1)S(1)}, u32[]{:S(2)}, u32[]{:S(2)}) collective-permute-start(bf16[32,1024]{1,0:T(8,128)(2,1)} %get-tuple-element.113), channel_id=1, source_target_pairs={{0,6},{2,4},{4,2},{6,0},{8,14},{10,12},{12,10},{14,8},{16,22},{18,... | collective-permute-start | bytes 196616 | tf_op jit(solution)/shard_map/ppermute | solution.py:100
  16.2 28.5 %copy-start.4 = (bf16[128,1024]{1,0:T(8,128)(2,1)S(1)}, bf16[128,1024]{1,0:T(8,128)(2,1)}, u32[]{:S(2)}) copy-start(bf16[128,1024]{1,0:T(8,128)(2,1)} %param.14) | copy-start | bytes 786436
  21.8 9.3 %collective-permute-start.5 = (bf16[256,384]{1,0:T(8,128)(2,1)}, bf16[256,384]{1,0:T(8,128)(2,1)S(1)}, u32[]{:S(2)}, u32[]{:S(2)}) collective-permute-start(bf16[256,384]{1,0:T(8,128)(2,1)} %get-tuple-element.129.refs_9_), channel_id=1, source_target_pairs={{0,24},{2,26},{4,28},{6,30},{8,0},{10,2},{12,4},{14,6},{16,8},{18,... | collective-permute-start | bytes 589832 | tf_op jit(solution)/shard_map/ppermute | solution.py:105
  25.4 15.9 %collective-permute-start.4 = (bf16[256,384]{1,0:T(8,128)(2,1)}, bf16[256,384]{1,0:T(8,128)(2,1)S(1)}, u32[]{:S(2)}, u32[]{:S(2)}) collective-permute-start(bf16[256,384]{1,0:T(8,128)(2,1)} %get-tuple-element.129.refs_9_), channel_id=1, source_target_pairs={{0,16},{2,18},{4,20},{6,22},{8,24},{10,26},{12,28},{14,30},{16,0},... | collective-permute-start | bytes 589832 | tf_op jit(solution)/shard_map/ppermute | solution.py:105
  25.4 15.9 %collective-permute-start.3 = (bf16[256,384]{1,0:T(8,128)(2,1)}, bf16[256,384]{1,0:T(8,128)(2,1)S(1)}, u32[]{:S(2)}, u32[]{:S(2)}) collective-permute-start(bf16[256,384]{1,0:T(8,128)(2,1)} %get-tuple-element.129.refs_9_), channel_id=1, source_target_pairs={{0,8},{2,10},{4,12},{6,14},{8,16},{10,18},{12,20},{14,22},{16,24},... | collective-permute-start | bytes 589832 | tf_op jit(solution)/shard_map/ppermute | solution.py:105
  27.3 21.1 %copy-start.33 = (s32[4,4]{1,0:T(4,128)}, s32[4,4]{1,0:T(4,128)S(1)}, u32[]{:S(2)}) copy-start(s32[4,4]{1,0:T(4,128)S(1)} %reduce_window_sum.11.refs_1_.ends_ref) | copy-start | bytes 196
  27.4 13.9 %collective-permute-start.6 = (bf16[64,1792]{1,0:T(8,128)(2,1)}, bf16[64,1792]{1,0:T(8,128)(2,1)S(1)}, u32[]{:S(2)}, u32[]{:S(2)}) collective-permute-start(bf16[64,1792]{1,0:T(8,128)(2,1)} %get-tuple-element.121), channel_id=1, source_target_pairs={{0,2},{2,0},{4,6},{6,4},{8,10},{10,8},{12,14},{14,12},{16,18},{18,... | collective-permute-start | bytes 688136 | tf_op jit(solution)/shard_map/ppermute | solution.py:100
  28.0 13.3 %collective-permute-start.7 = (bf16[64,1792]{1,0:T(8,128)(2,1)}, bf16[64,1792]{1,0:T(8,128)(2,1)S(1)}, u32[]{:S(2)}, u32[]{:S(2)}) collective-permute-start(bf16[64,1792]{1,0:T(8,128)(2,1)} %get-tuple-element.122), channel_id=1, source_target_pairs={{0,4},{2,6},{4,0},{6,2},{8,12},{10,14},{12,8},{14,10},{16,20},{18,... | collective-permute-start | bytes 688136 | tf_op jit(solution)/shard_map/ppermute | solution.py:100
  31.1 17.3 %copy-start.23 = (bf16[256,384]{1,0:T(8,128)(2,1)}, bf16[256,384]{1,0:T(8,128)(2,1)S(1)}, u32[]{:S(2)}) copy-start(bf16[256,384]{1,0:T(8,128)(2,1)S(1)} %collective-permute-done.5.refs_12_) | copy-start | bytes 589828
  31.1 10.3 %collective-permute-start.8 = (bf16[64,1792]{1,0:T(8,128)(2,1)}, bf16[64,1792]{1,0:T(8,128)(2,1)S(1)}, u32[]{:S(2)}, u32[]{:S(2)}) collective-permute-start(bf16[64,1792]{1,0:T(8,128)(2,1)} %get-tuple-element.123), channel_id=1, source_target_pairs={{0,6},{2,4},{4,2},{6,0},{8,14},{10,12},{12,10},{14,8},{16,22},{18,... | collective-permute-start | bytes 688136 | tf_op jit(solution)/shard_map/ppermute | solution.py:100
  41.3 20.7 %copy-start.24 = (bf16[256,384]{1,0:T(8,128)(2,1)}, bf16[256,384]{1,0:T(8,128)(2,1)S(1)}, u32[]{:S(2)}) copy-start(bf16[256,384]{1,0:T(8,128)(2,1)S(1)} %collective-permute-done.4.refs_11_) | copy-start | bytes 589828
  42.2 15.6 %copy-start.13 = (bf16[128,1024]{1,0:T(8,128)(2,1)S(1)}, bf16[128,1024]{1,0:T(8,128)(2,1)}, u32[]{:S(2)}) copy-start(bf16[128,1024]{1,0:T(8,128)(2,1)} %param.27) | copy-start | bytes 786436
  42.2 19.2 %copy-start.36 = (f32[64]{0:T(128)S(1)}, f32[64]{0:T(128)}, u32[]{:S(2)}) copy-start(f32[64]{0:T(128)} %param.17) | copy-start | bytes 772
  42.2 19.2 %copy-start.37 = (f32[64]{0:T(128)S(1)}, f32[64]{0:T(128)}, u32[]{:S(2)}) copy-start(f32[64]{0:T(128)} %param.18) | copy-start | bytes 772
  44.7 160.3 %reduce-scatter.2.cloned.1.call-start = ((), (), s32[]{:S(2)}) async-start(), calls=%async_computation.2 | async-start | bytes 4587520 | tf_op jit(solution)/shard_map/reduce_scatter | solution.py:885
  44.8 9.3 %collective-permute-start.9 = (bf16[128,1024]{1,0:T(8,128)(2,1)S(1)}, bf16[128,1024]{1,0:T(8,128)(2,1)S(1)}, u32[]{:S(2)}, u32[]{:S(2)}) collective-permute-start(bf16[128,1024]{1,0:T(8,128)(2,1)S(1)} %copy-done.4), channel_id=1, source_target_pairs={{0,2},{2,0},{4,6},{6,4},{8,10},{10,8},{12,14},{14,12},{16,18},{18,... | collective-permute-start | bytes 786440 | tf_op jit(solution)/shard_map/ppermute | solution.py:100
  45.4 12.3 %collective-permute-start.10 = (bf16[128,1024]{1,0:T(8,128)(2,1)S(1)}, bf16[128,1024]{1,0:T(8,128)(2,1)S(1)}, u32[]{:S(2)}, u32[]{:S(2)}) collective-permute-start(bf16[128,1024]{1,0:T(8,128)(2,1)S(1)} %copy-done.4), channel_id=1, source_target_pairs={{0,4},{2,6},{4,0},{6,2},{8,12},{10,14},{12,8},{14,10},{16,20},{18,... | collective-permute-start | bytes 786440 | tf_op jit(solution)/shard_map/ppermute | solution.py:100
  45.9 11.8 %collective-permute-start.11 = (bf16[128,1024]{1,0:T(8,128)(2,1)S(1)}, bf16[128,1024]{1,0:T(8,128)(2,1)S(1)}, u32[]{:S(2)}, u32[]{:S(2)}) collective-permute-start(bf16[128,1024]{1,0:T(8,128)(2,1)S(1)} %copy-done.4), channel_id=1, source_target_pairs={{0,6},{2,4},{4,2},{6,0},{8,14},{10,12},{12,10},{14,8},{16,22},{18,... | collective-permute-start | bytes 786440 | tf_op jit(solution)/shard_map/ppermute | solution.py:100
  57.7 4.2 %collective-permute-start.12 = (bf16[512,1024]{1,0:T(8,128)(2,1)S(1)}, bf16[512,1024]{1,0:T(8,128)(2,1)S(1)}, u32[]{:S(2)}, u32[]{:S(2)}) collective-permute-start(bf16[512,1024]{1,0:T(8,128)(2,1)S(1)} %constant_dynamic-update-slice_fusion.refs_2_), channel_id=1, source_target_pairs={{0,1},{1,0},{2,3},{3,2},{4,5},{5,4},{6,7},{7,6},{8,9},{9,8},{10,11... | collective-permute-start | bytes 3145736 | tf_op jit(solution)/shard_map/ppermute | solution.py:109
  57.8 15.5 %collective-permute-start.15 = (bf16[128,1024]{1,0:T(8,128)(2,1)S(1)}, bf16[128,1024]{1,0:T(8,128)(2,1)S(1)}, u32[]{:S(2)}, u32[]{:S(2)}) collective-permute-start(bf16[128,1024]{1,0:T(8,128)(2,1)S(1)} %copy-done.13), channel_id=1, source_target_pairs={{0,6},{2,4},{4,2},{6,0},{8,14},{10,12},{12,10},{14,8},{16,22},{18,... | collective-permute-start | bytes 786440 | tf_op jit(solution)/shard_map/ppermute | solution.py:100
  59.0 14.3 %collective-permute-start.14 = (bf16[128,1024]{1,0:T(8,128)(2,1)S(1)}, bf16[128,1024]{1,0:T(8,128)(2,1)S(1)}, u32[]{:S(2)}, u32[]{:S(2)}) collective-permute-start(bf16[128,1024]{1,0:T(8,128)(2,1)S(1)} %copy-done.13), channel_id=1, source_target_pairs={{0,4},{2,6},{4,0},{6,2},{8,12},{10,14},{12,8},{14,10},{16,20},{18,... | collective-permute-start | bytes 786440 | tf_op jit(solution)/shard_map/ppermute | solution.py:100
  60.4 12.9 %collective-permute-start.13 = (bf16[128,1024]{1,0:T(8,128)(2,1)S(1)}, bf16[128,1024]{1,0:T(8,128)(2,1)S(1)}, u32[]{:S(2)}, u32[]{:S(2)}) collective-permute-start(bf16[128,1024]{1,0:T(8,128)(2,1)S(1)} %copy-done.13), channel_id=1, source_target_pairs={{0,2},{2,0},{4,6},{6,4},{8,10},{10,8},{12,14},{14,12},{16,18},{18,... | collective-permute-start | bytes 786440 | tf_op jit(solution)/shard_map/ppermute | solution.py:100
  74.8 2.9 %collective-permute-start.16 = (bf16[512,1024]{1,0:T(8,128)(2,1)}, bf16[512,1024]{1,0:T(8,128)(2,1)S(1)}, u32[]{:S(2)}, u32[]{:S(2)}) collective-permute-start(bf16[512,1024]{1,0:T(8,128)(2,1)} %get-tuple-element.136), channel_id=1, source_target_pairs={{0,1},{1,0},{2,3},{3,2},{4,5},{5,4},{6,7},{7,6},{8,9},{9,8},{10,11... | collective-permute-start | bytes 3145736 | tf_op jit(solution)/shard_map/ppermute | solution.py:109
  81.6 16.4 %copy-start.34 = (f32[1024]{0:T(1024)S(1)}, f32[1024]{0:T(1024)}, u32[]{:S(2)}) copy-start(f32[1024]{0:T(1024)} %param.19) | copy-start | bytes 12292
  81.6 20.1 %copy-start.19 = (bf16[128,1024]{1,0:T(8,128)(2,1)S(1)}, bf16[128,1024]{1,0:T(8,128)(2,1)}, u32[]{:S(2)}) copy-start(bf16[128,1024]{1,0:T(8,128)(2,1)} %copy-done.18) | copy-start | bytes 786436
  81.6 20.1 %copy-start.17 = (bf16[128,1024]{1,0:T(8,128)(2,1)S(1)}, bf16[128,1024]{1,0:T(8,128)(2,1)}, u32[]{:S(2)}) copy-start(bf16[128,1024]{1,0:T(8,128)(2,1)} %copy-done.16) | copy-start | bytes 786436
  81.6 9.4 %collective-permute-start.17 = (bf16[128,1024]{1,0:T(8,128)(2,1)}, bf16[128,1024]{1,0:T(8,128)(2,1)S(1)}, u32[]{:S(2)}, u32[]{:S(2)}) collective-permute-start(bf16[128,1024]{1,0:T(8,128)(2,1)} %get-tuple-element.138), channel_id=1, source_target_pairs={{0,2},{2,0},{4,6},{6,4},{8,10},{10,8},{12,14},{14,12},{16,18},{18,... | collective-permute-start | bytes 786440 | tf_op jit(solution)/shard_map/ppermute | solution.py:100
  82.7 13.9 %collective-permute-start.18 = (bf16[128,1024]{1,0:T(8,128)(2,1)}, bf16[128,1024]{1,0:T(8,128)(2,1)S(1)}, u32[]{:S(2)}, u32[]{:S(2)}) collective-permute-start(bf16[128,1024]{1,0:T(8,128)(2,1)} %get-tuple-element.139), channel_id=1, source_target_pairs={{0,4},{2,6},{4,0},{6,2},{8,12},{10,14},{12,8},{14,10},{16,20},{18,... | collective-permute-start | bytes 786440 | tf_op jit(solution)/shard_map/ppermute | solution.py:100
  83.3 13.3 %collective-permute-start.19 = (bf16[128,1024]{1,0:T(8,128)(2,1)}, bf16[128,1024]{1,0:T(8,128)(2,1)S(1)}, u32[]{:S(2)}, u32[]{:S(2)}) collective-permute-start(bf16[128,1024]{1,0:T(8,128)(2,1)} %get-tuple-element.140), channel_id=1, source_target_pairs={{0,6},{2,4},{4,2},{6,0},{8,14},{10,12},{12,10},{14,8},{16,22},{18,... | collective-permute-start | bytes 786440 | tf_op jit(solution)/shard_map/ppermute | solution.py:100
  98.1 10.2 %collective-permute-start.22 = (bf16[128,1024]{1,0:T(8,128)(2,1)S(1)}, bf16[128,1024]{1,0:T(8,128)(2,1)S(1)}, u32[]{:S(2)}, u32[]{:S(2)}) collective-permute-start(bf16[128,1024]{1,0:T(8,128)(2,1)S(1)} %multiply_convert_fusion), channel_id=1, source_target_pairs={{0,6},{2,4},{4,2},{6,0},{8,14},{10,12},{12,10},{14,8},{16,22},{18,... | collective-permute-start | bytes 786440 | tf_op jit(solution)/shard_map/ppermute | solution.py:100
  99.3 12.4 %collective-permute-start.21 = (bf16[128,1024]{1,0:T(8,128)(2,1)S(1)}, bf16[128,1024]{1,0:T(8,128)(2,1)S(1)}, u32[]{:S(2)}, u32[]{:S(2)}) collective-permute-start(bf16[128,1024]{1,0:T(8,128)(2,1)S(1)} %multiply_convert_fusion), channel_id=1, source_target_pairs={{0,4},{2,6},{4,0},{6,2},{8,12},{10,14},{12,8},{14,10},{16,20},{18,... | collective-permute-start | bytes 786440 | tf_op jit(solution)/shard_map/ppermute | solution.py:100
  100.6 11.1 %collective-permute-start.20 = (bf16[128,1024]{1,0:T(8,128)(2,1)S(1)}, bf16[128,1024]{1,0:T(8,128)(2,1)S(1)}, u32[]{:S(2)}, u32[]{:S(2)}) collective-permute-start(bf16[128,1024]{1,0:T(8,128)(2,1)S(1)} %multiply_convert_fusion), channel_id=1, source_target_pairs={{0,2},{2,0},{4,6},{6,4},{8,10},{10,8},{12,14},{14,12},{16,18},{18,... | collective-permute-start | bytes 786440 | tf_op jit(solution)/shard_map/ppermute | solution.py:100
  101.7 16.1 %copy-start.9 = (bf16[512,1024]{1,0:T(8,128)(2,1)}, bf16[512,1024]{1,0:T(8,128)(2,1)S(1)}, u32[]{:S(2)}) copy-start(bf16[512,1024]{1,0:T(8,128)(2,1)S(1)} %constant_dynamic-update-slice_fusion.4.g_m) | copy-start | bytes 3145732
  101.7 10.2 %collective-permute-start.24 = (bf16[512,1024]{1,0:T(8,128)(2,1)S(1)}, bf16[512,1024]{1,0:T(8,128)(2,1)S(1)}, u32[]{:S(2)}, u32[]{:S(2)}) collective-permute-start(bf16[512,1024]{1,0:T(8,128)(2,1)S(1)} %constant_dynamic-update-slice_fusion.4.g_m), channel_id=1, source_target_pairs={{0,1},{1,0},{2,3},{3,2},{4,5},{5,4},{6,7},{7,6},{8,9},{9,8},{10,11... | collective-permute-start | bytes 3145736 | tf_op jit(solution)/shard_map/ppermute | solution.py:109
  111.8 2.9 %collective-permute-start.23 = (bf16[512,1024]{1,0:T(8,128)(2,1)S(1)}, bf16[512,1024]{1,0:T(8,128)(2,1)}, u32[]{:S(2)}, u32[]{:S(2)}) collective-permute-start(bf16[512,1024]{1,0:T(8,128)(2,1)S(1)} %pad_maximum_fusion.x_m), channel_id=1, source_target_pairs={{0,1},{1,0},{2,3},{3,2},{4,5},{5,4},{6,7},{7,6},{8,9},{9,8},{10,11... | collective-permute-start | bytes 3145736 | tf_op jit(solution)/shard_map/ppermute | solution.py:109
  139.1 2.7 %collective-permute-start.25 = (bf16[512,1024]{1,0:T(8,128)(2,1)S(1)}, bf16[512,1024]{1,0:T(8,128)(2,1)S(1)}, u32[]{:S(2)}, u32[]{:S(2)}) collective-permute-start(bf16[512,1024]{1,0:T(8,128)(2,1)S(1)} %copy-done.39), channel_id=1, source_target_pairs={{0,1},{1,0},{2,3},{3,2},{4,5},{5,4},{6,7},{7,6},{8,9},{9,8},{10,11... | collective-permute-start | bytes 3145736 | tf_op jit(solution)/shard_map/ppermute | solution.py:109
  145.8 9.4 %collective-permute-start.26 = (bf16[128,1024]{1,0:T(8,128)(2,1)}, bf16[128,1024]{1,0:T(8,128)(2,1)S(1)}, u32[]{:S(2)}, u32[]{:S(2)}) collective-permute-start(bf16[128,1024]{1,0:T(8,128)(2,1)} %get-tuple-element.144), channel_id=1, source_target_pairs={{0,2},{2,0},{4,6},{6,4},{8,10},{10,8},{12,14},{14,12},{16,18},{18,... | collective-permute-start | bytes 786440 | tf_op jit(solution)/shard_map/ppermute | solution.py:100
  147.5 13.9 %collective-permute-start.27 = (bf16[128,1024]{1,0:T(8,128)(2,1)}, bf16[128,1024]{1,0:T(8,128)(2,1)S(1)}, u32[]{:S(2)}, u32[]{:S(2)}) collective-permute-start(bf16[128,1024]{1,0:T(8,128)(2,1)} %get-tuple-element.145), channel_id=1, source_target_pairs={{0,4},{2,6},{4,0},{6,2},{8,12},{10,14},{12,8},{14,10},{16,20},{18,... | collective-permute-start | bytes 786440 | tf_op jit(solution)/shard_map/ppermute | solution.py:100
  149.0 12.4 %collective-permute-start.28 = (bf16[128,1024]{1,0:T(8,128)(2,1)}, bf16[128,1024]{1,0:T(8,128)(2,1)S(1)}, u32[]{:S(2)}, u32[]{:S(2)}) collective-permute-start(bf16[128,1024]{1,0:T(8,128)(2,1)} %get-tuple-element.146), channel_id=1, source_target_pairs={{0,6},{2,4},{4,2},{6,0},{8,14},{10,12},{12,10},{14,8},{16,22},{18,... | collective-permute-start | bytes 786440 | tf_op jit(solution)/shard_map/ppermute | solution.py:100
  163.7 10.2 %collective-permute-start.31 = (bf16[128,1024]{1,0:T(8,128)(2,1)S(1)}, bf16[128,1024]{1,0:T(8,128)(2,1)S(1)}, u32[]{:S(2)}, u32[]{:S(2)}) collective-permute-start(bf16[128,1024]{1,0:T(8,128)(2,1)S(1)} %get-tuple-element.201), channel_id=1, source_target_pairs={{0,6},{2,4},{4,2},{6,0},{8,14},{10,12},{12,10},{14,8},{16,22},{18,... | collective-permute-start | bytes 786440 | tf_op jit(solution)/shard_map/ppermute | solution.py:100
  165.2 12.3 %collective-permute-start.30 = (bf16[128,1024]{1,0:T(8,128)(2,1)S(1)}, bf16[128,1024]{1,0:T(8,128)(2,1)S(1)}, u32[]{:S(2)}, u32[]{:S(2)}) collective-permute-start(bf16[128,1024]{1,0:T(8,128)(2,1)S(1)} %get-tuple-element.201), channel_id=1, source_target_pairs={{0,4},{2,6},{4,0},{6,2},{8,12},{10,14},{12,8},{14,10},{16,20},{18,... | collective-permute-start | bytes 786440 | tf_op jit(solution)/shard_map/ppermute | solution.py:100
  166.4 11.3 %collective-permute-start.29 = (bf16[128,1024]{1,0:T(8,128)(2,1)S(1)}, bf16[128,1024]{1,0:T(8,128)(2,1)S(1)}, u32[]{:S(2)}, u32[]{:S(2)}) collective-permute-start(bf16[128,1024]{1,0:T(8,128)(2,1)S(1)} %get-tuple-element.201), channel_id=1, source_target_pairs={{0,2},{2,0},{4,6},{6,4},{8,10},{10,8},{12,14},{14,12},{16,18},{18,... | collective-permute-start | bytes 786440 | tf_op jit(solution)/shard_map/ppermute | solution.py:100
  167.2 10.6 %collective-permute-start.33 = (bf16[512,1024]{1,0:T(8,128)(2,1)S(1)}, bf16[512,1024]{1,0:T(8,128)(2,1)}, u32[]{:S(2)}, u32[]{:S(2)}) collective-permute-start(bf16[512,1024]{1,0:T(8,128)(2,1)S(1)} %copy-done.38), channel_id=1, source_target_pairs={{0,1},{1,0},{2,3},{3,2},{4,5},{5,4},{6,7},{7,6},{8,9},{9,8},{10,11... | collective-permute-start | bytes 3145736 | tf_op jit(solution)/shard_map/ppermute | solution.py:109
  177.7 3.3 %collective-permute-start.32 = (bf16[512,1024]{1,0:T(8,128)(2,1)S(1)}, bf16[512,1024]{1,0:T(8,128)(2,1)}, u32[]{:S(2)}, u32[]{:S(2)}) collective-permute-start(bf16[512,1024]{1,0:T(8,128)(2,1)S(1)} %pad_maximum_fusion.1.refs_9_), channel_id=1, source_target_pairs={{0,1},{1,0},{2,3},{3,2},{4,5},{5,4},{6,7},{7,6},{8,9},{9,8},{10,11... | collective-permute-start | bytes 3145736 | tf_op jit(solution)/shard_map/ppermute | solution.py:109
  181.1 19.0 %collective-permute-start.34 = (bf16[128,1024]{1,0:T(8,128)(2,1)}, bf16[128,1024]{1,0:T(8,128)(2,1)}, u32[]{:S(2)}, u32[]{:S(2)}) collective-permute-start(bf16[128,1024]{1,0:T(8,128)(2,1)} %get-tuple-element.155), channel_id=1, source_target_pairs={{0,2},{2,0},{4,6},{6,4},{8,10},{10,8},{12,14},{14,12},{16,18},{18,... | collective-permute-start | bytes 786440 | tf_op jit(solution)/shard_map/ppermute | solution.py:100
  182.5 17.6 %collective-permute-start.35 = (bf16[128,1024]{1,0:T(8,128)(2,1)}, bf16[128,1024]{1,0:T(8,128)(2,1)}, u32[]{:S(2)}, u32[]{:S(2)}) collective-permute-start(bf16[128,1024]{1,0:T(8,128)(2,1)} %get-tuple-element.156), channel_id=1, source_target_pairs={{0,4},{2,6},{4,0},{6,2},{8,12},{10,14},{12,8},{14,10},{16,20},{18,... | collective-permute-start | bytes 786440 | tf_op jit(solution)/shard_map/ppermute | solution.py:100
  183.1 17.0 %collective-permute-start.36 = (bf16[128,1024]{1,0:T(8,128)(2,1)}, bf16[128,1024]{1,0:T(8,128)(2,1)}, u32[]{:S(2)}, u32[]{:S(2)}) collective-permute-start(bf16[128,1024]{1,0:T(8,128)(2,1)} %get-tuple-element.157), channel_id=1, source_target_pairs={{0,6},{2,4},{4,2},{6,0},{8,14},{10,12},{12,10},{14,8},{16,22},{18,... | collective-permute-start | bytes 786440 | tf_op jit(solution)/shard_map/ppermute | solution.py:100
  200.1 37.6 %copy-start.15 = (f32[128,1024]{1,0:T(8,128)S(1)}, f32[128,1024]{1,0:T(8,128)}, u32[]{:S(2)}) copy-start(f32[128,1024]{1,0:T(8,128)} %get-tuple-element.154) | copy-start | bytes 1572868
  200.1 4.0 %collective-permute-start.37 = (bf16[512,1024]{1,0:T(8,128)(2,1)}, bf16[512,1024]{1,0:T(8,128)(2,1)S(1)}, u32[]{:S(2)}, u32[]{:S(2)}) collective-permute-start(bf16[512,1024]{1,0:T(8,128)(2,1)} %get-tuple-element.170), channel_id=1, source_target_pairs={{0,1},{1,0},{2,3},{3,2},{4,5},{5,4},{6,7},{7,6},{8,9},{9,8},{10,11... | collective-permute-start | bytes 3145736 | tf_op jit(solution)/shard_map/ppermute | solution.py:109
  200.1 12.0 %collective-permute-start.41 = (bf16[272,384]{1,0:T(8,128)(2,1)}, bf16[272,384]{1,0:T(8,128)(2,1)}, u32[]{:S(2)}, u32[]{:S(2)}) collective-permute-start(bf16[272,384]{1,0:T(8,128)(2,1)} %get-tuple-element.179), channel_id=1, source_target_pairs={{0,8},{2,10},{4,12},{6,14},{8,16},{10,18},{12,20},{14,22},{16,24},... | collective-permute-start | bytes 626696 | tf_op jit(solution)/shard_map/ppermute | solution.py:105
  200.2 18.3 %collective-permute-start.42 = (bf16[272,384]{1,0:T(8,128)(2,1)}, bf16[272,384]{1,0:T(8,128)(2,1)}, u32[]{:S(2)}, u32[]{:S(2)}) collective-permute-start(bf16[272,384]{1,0:T(8,128)(2,1)} %get-tuple-element.180), channel_id=1, source_target_pairs={{0,16},{2,18},{4,20},{6,22},{8,24},{10,26},{12,28},{14,30},{16,0},... | collective-permute-start | bytes 626696 | tf_op jit(solution)/shard_map/ppermute | solution.py:105
  201.3 17.2 %collective-permute-start.43 = (bf16[272,384]{1,0:T(8,128)(2,1)}, bf16[272,384]{1,0:T(8,128)(2,1)}, u32[]{:S(2)}, u32[]{:S(2)}) collective-permute-start(bf16[272,384]{1,0:T(8,128)(2,1)} %get-tuple-element.181), channel_id=1, source_target_pairs={{0,24},{2,26},{4,28},{6,30},{8,0},{10,2},{12,4},{14,6},{16,8},{18,... | collective-permute-start | bytes 626696 | tf_op jit(solution)/shard_map/ppermute | solution.py:105
  208.8 34.4 %copy-start.8 = (f32[128,1024]{1,0:T(8,128)S(1)}, f32[128,1024]{1,0:T(8,128)}, u32[]{:S(2)}) copy-start(f32[128,1024]{1,0:T(8,128)} %get-tuple-element.172) | copy-start | bytes 1572868
  208.8 34.4 %copy-start.26 = (f32[1024]{0:T(1024)S(1)}, f32[1024]{0:T(1024)}, u32[]{:S(2)}) copy-start(f32[1024]{0:T(1024)} %param.16) | copy-start | bytes 12292
  208.8 31.8 %collective-permute-start.38 = (bf16[256,1024]{1,0:T(8,128)(2,1)}, bf16[256,1024]{1,0:T(8,128)(2,1)S(1)}, u32[]{:S(2)}, u32[]{:S(2)}) collective-permute-start(bf16[256,1024]{1,0:T(8,128)(2,1)} %get-tuple-element.173), channel_id=1, source_target_pairs={{0,2},{2,0},{4,6},{6,4},{8,10},{10,8},{12,14},{14,12},{16,18},{18,... | collective-permute-start | bytes 1572872 | tf_op jit(solution)/shard_map/ppermute | solution.py:100
  210.3 30.3 %collective-permute-start.39 = (bf16[256,1024]{1,0:T(8,128)(2,1)}, bf16[256,1024]{1,0:T(8,128)(2,1)S(1)}, u32[]{:S(2)}, u32[]{:S(2)}) collective-permute-start(bf16[256,1024]{1,0:T(8,128)(2,1)} %get-tuple-element.174), channel_id=1, source_target_pairs={{0,4},{2,6},{4,0},{6,2},{8,12},{10,14},{12,8},{14,10},{16,20},{18,... | collective-permute-start | bytes 1572872 | tf_op jit(solution)/shard_map/ppermute | solution.py:100
  212.1 31.1 %collective-permute-start.40 = (bf16[256,1024]{1,0:T(8,128)(2,1)}, bf16[256,1024]{1,0:T(8,128)(2,1)S(1)}, u32[]{:S(2)}, u32[]{:S(2)}) collective-permute-start(bf16[256,1024]{1,0:T(8,128)(2,1)} %get-tuple-element.175), channel_id=1, source_target_pairs={{0,6},{2,4},{4,2},{6,0},{8,14},{10,12},{12,10},{14,8},{16,22},{18,... | collective-permute-start | bytes 1572872 | tf_op jit(solution)/shard_map/ppermute | solution.py:100
  220.6 14.7 %collective-permute-start.44 = (bf16[80,384]{1,0:T(8,128)(2,1)}, bf16[80,384]{1,0:T(8,128)(2,1)S(1)}, u32[]{:S(2)}, u32[]{:S(2)}) collective-permute-start(bf16[80,384]{1,0:T(8,128)(2,1)} %get-tuple-element.183), channel_id=1, source_target_pairs={{0,2},{2,0},{4,6},{6,4},{8,10},{10,8},{12,14},{14,12},{16,18},{18,... | collective-permute-start | bytes 184328 | tf_op jit(solution)/shard_map/ppermute | solution.py:100
  222.0 17.7 %collective-permute-start.45 = (bf16[80,384]{1,0:T(8,128)(2,1)}, bf16[80,384]{1,0:T(8,128)(2,1)S(1)}, u32[]{:S(2)}, u32[]{:S(2)}) collective-permute-start(bf16[80,384]{1,0:T(8,128)(2,1)} %get-tuple-element.184), channel_id=1, source_target_pairs={{0,4},{2,6},{4,0},{6,2},{8,12},{10,14},{12,8},{14,10},{16,20},{18,... | collective-permute-start | bytes 184328 | tf_op jit(solution)/shard_map/ppermute | solution.py:100
  235.3 5.3 %collective-permute-start.46 = (bf16[80,384]{1,0:T(8,128)(2,1)}, bf16[80,384]{1,0:T(8,128)(2,1)S(1)}, u32[]{:S(2)}, u32[]{:S(2)}) collective-permute-start(bf16[80,384]{1,0:T(8,128)(2,1)} %get-tuple-element.185), channel_id=1, source_target_pairs={{0,6},{2,4},{4,2},{6,0},{8,14},{10,12},{12,10},{14,8},{16,22},{18,... | collective-permute-start | bytes 184328 | tf_op jit(solution)/shard_map/ppermute | solution.py:100
  243.2 4.3 %collective-permute-start.47 = (f32[8,384]{1,0:T(8,128)}, f32[8,384]{1,0:T(8,128)S(1)}, u32[]{:S(2)}, u32[]{:S(2)}) collective-permute-start(f32[8,384]{1,0:T(8,128)} %get-tuple-element.190), channel_id=1, source_target_pairs={{0,1},{1,0},{2,3},{3,2},{4,5},{5,4},{6,7},{7,6},{8,9},{9,8},{10,11... | collective-permute-start | bytes 36872 | tf_op jit(solution)/shard_map/ppermute | solution.py:109
  (26 other events, 64.7 us)
Sparse Core Ops, SparseCore 0:
  44.8 72.9 all-gather.1
  138.0 66.9 reduce-scatter.1

commit v11 on v10

--- a/solution.py
+++ b/solution.py
@@ -485,7 +485,7 @@
 
 
 def ffn_kernel(where_ref, ends_ref, x_o, x_m, g_o, g_m, weight, *refs):
-    out_send, out_keep, dn_send, dn_keep, grad_out, total = refs
+    act_out, d_out, grad_out, total = refs
     step = pl.program_id(0)
     core = where_ref[2]
     both = x_o.shape[1]
@@ -502,7 +502,6 @@
         + [live_rows(g_m[k * local : (k + 1) * local, :], 2 * step + k, core) for k in range(2)],
         axis=0,
     )
-    half = 2 * local
     w_both = weight[:, :both]
     w_down = weight[:, both : both + big]
     w_small = weight[:, both + big : both + big + LANES]
@@ -527,12 +526,10 @@
     act = act.astype(bfloat16)
     d_both = jnp.concatenate([d_gate, d_up], axis=1).astype(bfloat16)
 
-    partial = matmul_nt(act, w_down) + matmul_nt(act_s, w_small_down)
-    out_send[...] = partial[:half].astype(bfloat16)
-    out_keep[...] = partial[half:]
-    partial = matmul_nt(d_both, w_both) + matmul_nt(d_small, w_small)
-    dn_send[...] = partial[:half].astype(bfloat16)
-    dn_keep[...] = partial[half:]
+    act_out[:, :big] = act
+    act_out[:, big:] = act_s
+    d_out[:, :both] = d_both
+    d_out[:, both:] = d_small
     spans = (
         (slice(0, both), x, d_both),
         (slice(both, both + big), grads, act),
@@ -551,39 +548,81 @@
             grad_out[:, span] = (total[:, span] + matmul_tn(left, right)).astype(bfloat16)
 
 
-def ffn(where, ends, x_mine, x_other, g_mine, g_other, weight):
+def ffn_layer(where, ends, x_mine, x_other, g_mine, g_other, weight):
     rows, width = x_mine.shape
     row_spec = pl.BlockSpec((rows // 2, width), lambda i: (i, 0))
     scalar = pl.BlockSpec(memory_space=pltpu.SMEM)
+    widths = (width // 2 + LANES, width + LANES)
     return pl.pallas_call(
         ffn_kernel,
         grid=(2,),
         in_specs=[scalar, scalar] + [row_spec] * 4 + [whole_spec(weight.shape)],
-        out_specs=[row_spec] * 4 + [whole_spec(weight.shape)],
+        out_specs=[pl.BlockSpec((rows, w), lambda i: (i, 0)) for w in widths]
+        + [whole_spec(weight.shape)],
+        out_shape=[jax.ShapeDtypeStruct((2 * rows, w), bfloat16) for w in widths]
+        + [jax.ShapeDtypeStruct(weight.shape, bfloat16)],
+        scratch_shapes=[pltpu.VMEM(weight.shape, float32)],
+        compiler_params=pltpu.CompilerParams(vmem_limit_bytes=VMEM_BYTES),
+        cost_estimate=cost(48),
+    )(where, ends, x_other, x_mine, g_other, g_mine, weight)
+
+
+def ffn_apply_kernel(first, values, weight, send, keep):
+    width = values.shape[1] - LANES
+    big = send.shape[1] // 2
+    small = 3 * big if first == 0 else 3 * big + LANES
+    partial = matmul_nt(values[:, :width], weight[:, first : first + width])
+    partial = partial + matmul_nt(values[:, width:], weight[:, small : small + LANES])
+    half = send.shape[0]
+    send[...] = partial[:half].astype(bfloat16)
+    keep[...] = partial[half:]
+
+
+def ffn_apply(first, values, weight):
+    rows, width = values.shape[0] // 2, weight.shape[0]
+    row_spec = pl.BlockSpec((rows // 2, width), lambda i: (i, 0))
+    return pl.pallas_call(
+        lambda *refs: ffn_apply_kernel(first, *refs),
+        grid=(2,),
+        in_specs=[
+            pl.BlockSpec((rows, values.shape[1]), lambda i: (i, 0)),
+            whole_spec(weight.shape),
+        ],
+        out_specs=[row_spec] * 2,
         out_shape=[
             jax.ShapeDtypeStruct((rows, width), bfloat16),
             jax.ShapeDtypeStruct((rows, width), float32),
-            jax.ShapeDtypeStruct((rows, width), bfloat16),
-            jax.ShapeDtypeStruct((rows, width), float32),
-            jax.ShapeDtypeStruct(weight.shape, bfloat16),
         ],
-        scratch_shapes=[pltpu.VMEM(weight.shape, float32)],
         compiler_params=pltpu.CompilerParams(vmem_limit_bytes=VMEM_BYTES),
-        cost_estimate=cost(74),
-    )(where, ends, x_other, x_mine, g_other, g_mine, weight)
+        cost_estimate=cost(14),
+    )(values, weight)
 
 
 def chip_sum_kernel(keep, received, *outs):
-    rows = outs[0].shape[0]
     for mask, out in enumerate(outs):
-        span = slice(mask * rows, (mask + 1) * rows)
-        out[...] = (keep[span, :] + received[span, :].astype(float32)).astype(out.dtype)
+
+        @pl.when(pl.program_id(0) == mask)
+        def _(out=out):
+            out[...] = (keep[...] + received[...].astype(float32)).astype(out.dtype)
+
+
+def partner_specs(rows, width):
+    return pl.BlockSpec((rows, width), lambda i: (i, 0)), whole_spec((rows, width))
 
 
 def chip_sum(keep, received):
-    shape = (keep.shape[0] // PLANE, keep.shape[1])
-    outs = [(shape, float32)] + [(shape, bfloat16)] * (PLANE - 1)
-    return call(chip_sum_kernel, outs, keep, received)
+    rows, width = keep.shape[0] // PLANE, keep.shape[1]
+    step, whole = partner_specs(rows, width)
+    return pl.pallas_call(
+        chip_sum_kernel,
+        grid=(PLANE,),
+        in_specs=[step, step],
+        out_specs=[whole] * PLANE,
+        out_shape=[jax.ShapeDtypeStruct((rows, width), float32)]
+        + [jax.ShapeDtypeStruct((rows, width), bfloat16)] * (PLANE - 1),
+        compiler_params=pltpu.CompilerParams(vmem_limit_bytes=VMEM_BYTES),
+        cost_estimate=COST,
+    )(keep, received)
 
 
 def plane_sent(parts):
@@ -600,43 +639,53 @@
 
 def tail_kernel(where_ref, keep, received, own_ff, own, ff_out, *refs):
     messages, held = refs[:-1], refs[-1]
-    held[...] = own_ff[...].astype(float32)
     place = where_ref[0]
     local = own.shape[0]
     rows = ff_out.shape[0]
     tall = (messages[0].shape[0] - local) // 2
     width = own.shape[1]
+
+    @pl.when(pl.program_id(0) == 0)
+    def _():
+        held[...] = own_ff[...].astype(float32)
+
+    value = keep[...] + received[...].astype(float32)
     for mask in range(PLANE):
-        span = slice(mask * local, (mask + 1) * local)
-        value = keep[span, :] + received[span, :].astype(float32)
-        grads = held[pl.ds(pl.multiple_of((place ^ mask) * rows, rows), rows), :]
-        if mask == 0:
-            own[...] = value
-            ff_out[...] = grads
-            continue
-        out = messages[mask - 1]
-        out[:local, :] = value.astype(bfloat16)
-        out[local : local + tall, :] = padded(grads[:, :width], tall).astype(bfloat16)
-        rest = grads.shape[1] - width
-        out[local + tall :, :rest] = padded(grads[:, width:], tall).astype(bfloat16)
-        out[local + tall :, rest:] = jnp.zeros((tall, width - rest), bfloat16)
+
+        @pl.when(pl.program_id(0) == mask)
+        def _(mask=mask):
+            grads = held[pl.ds(pl.multiple_of((place ^ mask) * rows, rows), rows), :]
+            if mask == 0:
+                own[...] = value
+                ff_out[...] = grads
+            else:
+                out = messages[mask - 1]
+                out[:local, :] = value.astype(bfloat16)
+                out[local : local + tall, :] = padded(grads[:, :width], tall).astype(bfloat16)
+                rest = grads.shape[1] - width
+                out[local + tall :, :rest] = padded(grads[:, width:], tall).astype(bfloat16)
+                out[local + tall :, rest:] = jnp.zeros((tall, width - rest), bfloat16)
 
 
 def tail_messages(where, keep, received, own_ff):
     local, width = keep.shape[0] // PLANE, keep.shape[1]
     rows, columns = own_ff.shape[0] // PLANE, own_ff.shape[1]
     message = (local + 2 * max(rows, 16), width)
-    return call(
+    step, whole = partner_specs(local, width)
+    return pl.pallas_call(
         tail_kernel,
-        [((local, width), float32), ((rows, columns), float32)]
-        + [(message, bfloat16)] * (PLANE - 1),
-        where,
-        keep,
-        received,
-        own_ff,
-        scalars=1,
-        scratch=[pltpu.VMEM(own_ff.shape, float32)],
-    )
+        grid=(PLANE,),
+        in_specs=[pl.BlockSpec(memory_space=pltpu.SMEM), step, step, whole_spec(own_ff.shape)],
+        out_specs=[whole, whole_spec((rows, columns))] + [whole_spec(message)] * (PLANE - 1),
+        out_shape=[
+            jax.ShapeDtypeStruct((local, width), float32),
+            jax.ShapeDtypeStruct((rows, columns), float32),
+        ]
+        + [jax.ShapeDtypeStruct(message, bfloat16)] * (PLANE - 1),
+        scratch_shapes=[pltpu.VMEM(own_ff.shape, float32)],
+        compiler_params=pltpu.CompilerParams(vmem_limit_bytes=VMEM_BYTES),
+        cost_estimate=COST,
+    )(where, keep, received, own_ff)
 
 
 def joined_gains(tail):
@@ -879,15 +928,16 @@
     unit_b = hidden * factor_b
     x_mine, x_other = gather_rows((unit_b * ffn_gain).astype(jnp.bfloat16))
 
-    out_send, out_keep, dn_send, dn_keep, ff_grad = ffn(
+    act, d_both, ff_grad = ffn_layer(
         where, ends, x_mine, x_other, cot_mine, cot_other, ff_weight
     )
     own_ff = lax.psum_scatter(
         ff_grad, "dp", scatter_dimension=0, tiled=True, axis_index_groups=columns
     )
-    dn_parts = chip_sum(dn_keep, swap_cores(dn_send))
-    out_keep = after(dn_parts, out_keep)
-    d_normed2 = plane_total(dn_parts)
+    dn_send, dn_keep = ffn_apply(0, d_both, ff_weight)
+    dn_parts = plane_sent(chip_sum(dn_keep, swap_cores(dn_send)))
+    out_send, out_keep = ffn_apply(model, after(dn_send, act), ff_weight)
+    d_normed2 = add_up(after(out_send, dn_parts))
     grad_out = jnp.where(
         (jnp.arange(local_rows) + core * local_rows < ends[0, lengths.shape[1] - 1])[:, None],
         cotangent,

time: 257 us -> 258 us (level)
  Pallas kernels: 73.9 us -> 84.3 us
  waiting for transfers between devices: 93.4 us -> 88.4 us
    pallas_call x1 -> x7, Pallas kernels: 20 us -> 43.7 us  [the longest x1 15.5 us: ffn_layer(): pl.pallas_call(ffn_kernel, grid=(2,), in_specs=[scalar, scalar] + [row_sp...]
    pallas_call x11 -> x7, Pallas kernels: 28.1 us -> 14.9 us  [call(): pl.pallas_call(kernel, out_shape=[jax.ShapeDtypeStruct(shape, kind) for s...]
    ppermute x33, waiting for transfers between devices: 67.4 us -> 64.2 us  [send_plane(): return lax.ppermute(values, 'dp', [(i, i ^ mask) for i in range(count)])]
  transfers between devices with their start and end apart: 50 -> 50, of which waited for: 23 -> 21; matrix products, arithmetic and copies ran while one was open for 5% -> 5% of each run, Pallas kernels for 19% -> 24%
where the time goes in v11:
time: 258 us; the launch traced here: 257 us
  waiting for transfers between devices  88.4 us (34%)
  Pallas kernels  84.3 us (33%)
  starting transfers between devices  47 us (18%)
  between operations  14.6 us (6%)
  local copies, waits for them, and re-layouts  12 us (5%)
  other arithmetic  11.1 us (4%)
    ppermute x33, waiting for transfers between devices, send_plane(): return lax.ppermute(values, 'dp', [(i, i ^ mask) for i in range(count)])  64.2 us
    ppermute x33, starting transfers between devices, send_plane(): return lax.ppermute(values, 'dp', [(i, i ^ mask) for i in range(count)])  37.9 us
    pallas_call x1, Pallas kernels, ffn_layer(): pl.pallas_call(ffn_kernel, grid=(2,), in_specs=[scalar, scalar] + [row_sp...  15.5 us
    pallas_call x1, Pallas kernels, attn_back(): pl.pallas_call(lambda *refs: attn_back_kernel(layers, *refs), grid=(PLANE...  15.4 us
    pallas_call x7, Pallas kernels, call(): pl.pallas_call(kernel, out_shape=[jax.ShapeDtypeStruct(shape, kind) for s...  14.9 us
    ppermute x6, waiting for transfers between devices, send_deep(): lax.ppermute(values, 'dp', [(i, (i + PLANE * step) % count) for i in rang...  14.4 us
    pallas_call x2, Pallas kernels, ffn_apply(): pl.pallas_call(lambda *refs: ffn_apply_kernel(first, *refs), grid=(2,), i...  12.2 us
    pallas_call x3, Pallas kernels, chip_sum(): pl.pallas_call(chip_sum_kernel, grid=(PLANE,), in_specs=[step, step], out...  11.3 us
  transfers between devices with their start and end apart: 50, of which 21 were waited for; matrix products, arithmetic and copies ran while one was open for 5% of the time, Pallas kernels for 24%

profile of v11, /device:TPU:0, one launch (start us, length us, event | category | flops | bytes accessed | tf_op | source)
XLA Modules:
  0.0 257.4 jit_solution(12884821055236625930)
XLA Ops:
  7.8 1.7 shard_map.238
  9.5 2.9 %collective-permute-start = (bf16[32,1024]{1,0:T(8,128)(2,1)}, bf16[32,1024]{1,0:T(8,128)(2,1)S(1)}, u32[]{:S(2)}, u32[]{:S(2)}) collective-permute-start(bf16[32,1024]{1,0:T(8,128)(2,1)} %get-tuple-element.117), channel_id=1, source_target_pairs={{0,2},{2,0},{4,6},{6,4},{8,10},{10,8},{12,14},{14,12},{16,18},{18,... | collective-permute-start | bytes 196616 | tf_op jit(solution)/shard_map/ppermute | solution.py:100
  12.5 1.5 collective-permute-start.1
  14.0 2.2 shard_map.237
  16.9 2.4 collective-permute-done.2.three
  20.0 1.7 shard_map.239
  21.6 3.6 %collective-permute-start.5 = (bf16[256,384]{1,0:T(8,128)(2,1)}, bf16[256,384]{1,0:T(8,128)(2,1)S(1)}, u32[]{:S(2)}, u32[]{:S(2)}) collective-permute-start(bf16[256,384]{1,0:T(8,128)(2,1)} %get-tuple-element.135.refs_9_), channel_id=1, source_target_pairs={{0,24},{2,26},{4,28},{6,30},{8,0},{10,2},{12,4},{14,6},{16,8},{18,... | collective-permute-start | bytes 589832 | tf_op jit(solution)/shard_map/ppermute | solution.py:105
  28.4 2.6 collective-permute-done.5.refs_12_
  31.4 3.0 %fusion.6 = (f32[1024,128]{1,0:T(8,128)}, f32[1024,128]{1,0:T(8,128)}) fusion(f32[128]{0:T(128)S(1)} %get-tuple-element.225, f32[128]{0:T(128)S(1)} %get-tuple-element.226, f32[1024]{0:T(1024)S(1)} %bitcast.28), kind=kLoop, calls=%fused_computation.13 | loop fusion | flops 262144 | bytes 1053696 | tf_op jit(solution)/shard_map/mul | solution.py:828
  34.5 6.7 %collective-permute-done.4.refs_11_ = bf16[256,384]{1,0:T(8,128)(2,1)S(1)} collective-permute-done((bf16[256,384]{1,0:T(8,128)(2,1)}, bf16[256,384]{1,0:T(8,128)(2,1)S(1)}, u32[]{:S(2)}, u32[]{:S(2)}) %collective-permute-start.4) | collective-permute-done | bytes 196640 | tf_op jit(solution)/shard_map/ppermute | solution.py:105
  42.1 2.4 shard_map.240
  45.7 2.4 collective-permute-start.11
  48.2 5.7 %collective-permute-done.9 = bf16[128,1024]{1,0:T(8,128)(2,1)S(1)} collective-permute-done((bf16[128,1024]{1,0:T(8,128)(2,1)S(1)}, bf16[128,1024]{1,0:T(8,128)(2,1)S(1)}, u32[]{:S(2)}, u32[]{:S(2)}) %collective-permute-start.9) | collective-permute-done | bytes 262176 | tf_op jit(solution)/shard_map/ppermute | solution.py:100
  54.0 3.5 %collective-permute-done.10 = bf16[128,1024]{1,0:T(8,128)(2,1)S(1)} collective-permute-done((bf16[128,1024]{1,0:T(8,128)(2,1)S(1)}, bf16[128,1024]{1,0:T(8,128)(2,1)S(1)}, u32[]{:S(2)}, u32[]{:S(2)}) %collective-permute-start.10) | collective-permute-done | bytes 262176 | tf_op jit(solution)/shard_map/ppermute | solution.py:100
  57.7 1.2 collective-permute-start.15
  58.9 1.4 collective-permute-start.14
  62.8 10.4 %shard_map.241 = (bf16[512,1024]{1,0:T(8,128)(2,1)}, f32[512,1024]{1,0:T(8,128)}, f32[1024,256]{1,0:T(8,128)}, bf16[1024,256]{1,0:T(8,128)(2,1)}, bf16[1024,128]{1,0:T(8,128)(2,1)}, /*index=5*/bf16[1024,384]{1,0:T(8,128)(2,1)}) custom-call(s32[3]{0:T(128)} %pad_add_fusion.where_ref.refs_0_, s32[4,4]{1,0:T(4,128)} %copy-done.34, bf16[512,1024]{1,0:T(8,128)(2,1)} %copy-done, ...), custom_call_target="tpu_custom_call" | custom-call | flops 1024 | bytes 36000000 | tf_op jit(solution)/shard_map/pallas_call | solution.py:435
  74.6 2.9 %collective-permute-done.16.received = bf16[512,1024]{1,0:T(8,128)(2,1)S(1)} collective-permute-done((bf16[512,1024]{1,0:T(8,128)(2,1)}, bf16[512,1024]{1,0:T(8,128)(2,1)S(1)}, u32[]{:S(2)}, u32[]{:S(2)}) %collective-permute-start.16) | collective-permute-done | bytes 1048608 | tf_op jit(solution)/shard_map/ppermute | solution.py:109
  78.4 3.7 %shard_map.242 = (f32[128,1024]{1,0:T(8,128)}, bf16[128,1024]{1,0:T(8,128)(2,1)}, bf16[128,1024]{1,0:T(8,128)(2,1)}, bf16[128,1024]{1,0:T(8,128)(2,1)}) custom-call(f32[512,1024]{1,0:T(8,128)} %get-tuple-element.139.keep, bf16[512,1024]{1,0:T(8,128)(2,1)} %copy-done.12), custom_call_target="tpu_custom_call" | custom-call | flops 1024 | bytes 1024 | tf_op jit(solution)/shard_map/pallas_call | solution.py:616
  82.2 1.1 collective-permute-start.17
  83.9 1.8 collective-permute-start.19
  85.7 5.9 %collective-permute-done.17 = bf16[128,1024]{1,0:T(8,128)(2,1)S(1)} collective-permute-done((bf16[128,1024]{1,0:T(8,128)(2,1)}, bf16[128,1024]{1,0:T(8,128)(2,1)S(1)}, u32[]{:S(2)}, u32[]{:S(2)}) %collective-permute-start.17) | collective-permute-done | bytes 262176 | tf_op jit(solution)/shard_map/ppermute | solution.py:100
  91.6 5.6 %collective-permute-done.18 = bf16[128,1024]{1,0:T(8,128)(2,1)S(1)} collective-permute-done((bf16[128,1024]{1,0:T(8,128)(2,1)}, bf16[128,1024]{1,0:T(8,128)(2,1)S(1)}, u32[]{:S(2)}, u32[]{:S(2)}) %collective-permute-start.18) | collective-permute-done | bytes 262176 | tf_op jit(solution)/shard_map/ppermute | solution.py:100
  97.2 1.3 multiply_reduce_fusion.2
  98.6 1.2 collective-permute-start.22
  99.9 1.2 collective-permute-start.21
  101.1 1.1 collective-permute-start.20
  102.4 6.5 %collective-permute-done.22 = bf16[128,1024]{1,0:T(8,128)(2,1)S(1)} collective-permute-done((bf16[128,1024]{1,0:T(8,128)(2,1)S(1)}, bf16[128,1024]{1,0:T(8,128)(2,1)S(1)}, u32[]{:S(2)}, u32[]{:S(2)}) %collective-permute-start.22) | collective-permute-done | bytes 262176 | tf_op jit(solution)/shard_map/ppermute | solution.py:100
  108.9 3.3 %collective-permute-done.21 = bf16[128,1024]{1,0:T(8,128)(2,1)S(1)} collective-permute-done((bf16[128,1024]{1,0:T(8,128)(2,1)S(1)}, bf16[128,1024]{1,0:T(8,128)(2,1)S(1)}, u32[]{:S(2)}, u32[]{:S(2)}) %collective-permute-start.21) | collective-permute-done | bytes 262176 | tf_op jit(solution)/shard_map/ppermute | solution.py:100
  112.5 1.2 copy-done.10
  113.7 1.5 collective-permute-done.23.x_o
  115.2 2.5 all-gather.2.cloned.1.call-done.weight.refs_1_
  117.7 15.5 %shard_map.243 = (bf16[1024,640]{1,0:T(8,128)(2,1)}, bf16[1024,1152]{1,0:T(8,128)(2,1)}, bf16[1024,1792]{1,0:T(8,128)(2,1)}) custom-call(s32[3]{0:T(128)} %pad_add_fusion.where_ref.refs_0_, s32[4,4]{1,0:T(4,128)} %copy-done.34, bf16[512,1024]{1,0:T(8,128)(2,1)} %collective-permute-done.23.x_o, bf16[512,1024]{1,0:T(8,128)(2,1)} %copy-done.3, ...), custom_call_target="tpu_custom_call" | custom-call | flops 1024 | bytes 48000000 | tf_op jit(solution)/shard_map/pallas_call | solution.py:556
  133.2 6.6 %shard_map.244 = (bf16[512,1024]{1,0:T(8,128)(2,1)}, f32[512,1024]{1,0:T(8,128)}) custom-call(bf16[1024,1152]{1,0:T(8,128)(2,1)} %get-tuple-element.147.refs_0_, bf16[1024,1792]{1,0:T(8,128)(2,1)} %all-gather.2.cloned.1.call-done.weight.refs_1_), custom_call_target="tpu_custom_call" | custom-call | flops 1024 | bytes 14000000 | tf_op jit(solution)/shard_map/pallas_call | solution.py:584
  139.8 2.9 %collective-permute-done.25.received = bf16[512,1024]{1,0:T(8,128)(2,1)S(1)} collective-permute-done((bf16[512,1024]{1,0:T(8,128)(2,1)}, bf16[512,1024]{1,0:T(8,128)(2,1)S(1)}, u32[]{:S(2)}, u32[]{:S(2)}) %collective-permute-start.25) | collective-permute-done | bytes 1048608 | tf_op jit(solution)/shard_map/ppermute | solution.py:109
  143.7 3.7 %shard_map.246 = (f32[128,1024]{1,0:T(8,128)}, bf16[128,1024]{1,0:T(8,128)(2,1)}, bf16[128,1024]{1,0:T(8,128)(2,1)}, bf16[128,1024]{1,0:T(8,128)(2,1)}) custom-call(f32[512,1024]{1,0:T(8,128)} %get-tuple-element.152.keep, bf16[512,1024]{1,0:T(8,128)(2,1)} %copy-done.11), custom_call_target="tpu_custom_call" | custom-call | flops 1024 | bytes 1024 | tf_op jit(solution)/shard_map/pallas_call | solution.py:616
  147.4 1.5 collective-permute-start.26
  148.9 1.5 collective-permute-start.27
  150.9 1.3 slice.28
  152.8 5.6 %shard_map.245 = (bf16[512,1024]{1,0:T(8,128)(2,1)}, f32[512,1024]{1,0:T(8,128)}) custom-call(bf16[1024,640]{1,0:T(8,128)(2,1)} %get-tuple-element.150.refs_0_, bf16[1024,1792]{1,0:T(8,128)(2,1)} %all-gather.2.cloned.1.call-done.weight.refs_1_), custom_call_target="tpu_custom_call" | custom-call | flops 1024 | bytes 14000000 | tf_op jit(solution)/shard_map/pallas_call | solution.py:584
  158.4 4.4 %collective-permute-done.27 = bf16[128,1024]{1,0:T(8,128)(2,1)S(1)} collective-permute-done((bf16[128,1024]{1,0:T(8,128)(2,1)}, bf16[128,1024]{1,0:T(8,128)(2,1)S(1)}, u32[]{:S(2)}, u32[]{:S(2)}) %collective-permute-start.27) | collective-permute-done | bytes 262176 | tf_op jit(solution)/shard_map/ppermute | solution.py:100
  163.9 1.5 collective-permute-start.31
  165.4 1.2 collective-permute-start.30
  167.4 6.7 %collective-permute-done.31 = bf16[128,1024]{1,0:T(8,128)(2,1)S(1)} collective-permute-done((bf16[128,1024]{1,0:T(8,128)(2,1)S(1)}, bf16[128,1024]{1,0:T(8,128)(2,1)S(1)}, u32[]{:S(2)}, u32[]{:S(2)}) %collective-permute-start.31) | collective-permute-done | bytes 262176 | tf_op jit(solution)/shard_map/ppermute | solution.py:100
  174.1 3.7 %collective-permute-done.30 = bf16[128,1024]{1,0:T(8,128)(2,1)S(1)} collective-permute-done((bf16[128,1024]{1,0:T(8,128)(2,1)S(1)}, bf16[128,1024]{1,0:T(8,128)(2,1)S(1)}, u32[]{:S(2)}, u32[]{:S(2)}) %collective-permute-start.30) | collective-permute-done | bytes 262176 | tf_op jit(solution)/shard_map/ppermute | solution.py:100
  178.0 4.0 %shard_map.247 = (f32[128,1024]{1,0:T(8,128)}, bf16[128,1024]{1,0:T(8,128)(2,1)}, bf16[128,1024]{1,0:T(8,128)(2,1)}, bf16[128,1024]{1,0:T(8,128)(2,1)}) custom-call(f32[512,1024]{1,0:T(8,128)} %get-tuple-element.161.keep, bf16[512,1024]{1,0:T(8,128)(2,1)} %collective-permute-done.33.received), custom_call_target="tpu_custom_call" | custom-call | flops 1024 | bytes 1024 | tf_op jit(solution)/shard_map/pallas_call | solution.py:616
  182.0 1.4 collective-permute-start.34
  183.9 1.5 collective-permute-start.36
  185.5 15.4 %shard_map.248 = (bf16[512,1024]{1,0:T(8,128)(2,1)}, f32[512,1024]{1,0:T(8,128)}, f32[256,384]{1,0:T(8,128)}, f32[8,384]{1,0:T(8,128)}, bf16[272,384]{1,0:T(8,12...) custom-call(s32[3]{0:T(128)} %pad_add_fusion.where_ref.refs_0_, s32[4,4]{1,0:T(4,128)} %copy-done.34, ...), custom_call_target="tpu_custom_call" | custom-call | flops 1024 | bytes 24000000 | tf_op jit(solution)/shard_map/pallas_call | solution.py:462
  201.0 1.4 collective-permute-start.42
  202.5 2.4 collective-permute-start.43
  205.9 4.7 %shard_map.249 = (f32[128,1024]{1,0:T(8,128)}, f32[64,1792]{1,0:T(8,128)}, bf16[256,1024]{1,0:T(8,128)(2,1)}, bf16[256,1024]{1,0:T(8,128)(2,1)}, bf16[256,1024]{1,0:T(8,128)(2,1)}) custom-call(s32[3]{0:T(128)} %pad_add_fusion.where_ref.refs_0_, f32[512,1024]{1,0:T(8,128)} %get-tuple-element.181.keep, bf16[512,1024]{1,0:T(8,128)(2,1)} %copy-done.14, ...), custom_call_target="tpu_custom_call" | custom-call | flops 1024 | bytes 1024 | tf_op jit(solution)/shard_map/pallas_call | solution.py:675
  210.6 1.4 collective-permute-start.38
  212.6 1.5 collective-permute-start.40
  214.1 5.2 %collective-permute-done.42.refs_1_ = bf16[272,384]{1,0:T(8,128)(2,1)} collective-permute-done((bf16[272,384]{1,0:T(8,128)(2,1)}, bf16[272,384]{1,0:T(8,128)(2,1)}, u32[]{:S(2)}, u32[]{:S(2)}) %collective-permute-start.42) | collective-permute-done | bytes 208928 | tf_op jit(solution)/shard_map/ppermute | solution.py:105
  219.3 2.1 shard_map.250
  221.4 1.4 collective-permute-start.44
  223.4 13.7 %collective-permute-done.44.one = bf16[80,384]{1,0:T(8,128)(2,1)S(1)} collective-permute-done((bf16[80,384]{1,0:T(8,128)(2,1)}, bf16[80,384]{1,0:T(8,128)(2,1)S(1)}, u32[]{:S(2)}, u32[]{:S(2)}) %collective-permute-start.44) | collective-permute-done | bytes 61472 | tf_op jit(solution)/shard_map/ppermute | solution.py:100
  237.1 1.5 collective-permute-start.46
  238.6 2.0 add_convert_fusion
  240.6 1.9 collective-permute-done.46.three
  243.1 1.9 shard_map.251
  245.3 1.1 fusion.5
  246.4 2.9 %shard_map.252 = (f32[64,2304]{1,0:T(8,128)}, f32[64,2304]{1,0:T(8,128)}, f32[64,2304]{1,0:T(8,128)}) custom-call(s32[3]{0:T(128)} %pad_add_fusion.where_ref.refs_0_, f32[64,1792]{1,0:T(8,128)} %get-tuple-element.207.own, bf16[256,1024]{1,0:T(8,128)(2,1)} %copy-done.5, bf16[256,1024]{1,0:T(8,128)(2,1)} %copy-done.6, bf16[256,1024]{1,0:T(8,128)(2,1)} %copy-done.7), custom_call_target="tpu_custom_call" | custom-call | flops 1024 | bytes 1024 | tf_op jit(solution)/shard_map/pallas_call | solution.py:115
  (170 shorter events, 23.3 us)
Async XLA Ops:
  7.2 110.5 %all-gather.2.cloned.1.call-start = ((), (), s32[]{:S(2)}) async-start(), calls=%async_computation.1 | async-start | bytes 4587520 | tf_op jit(solution)/shard_map/all_gather | solution.py:906
  9.5 6.6 %collective-permute-start = (bf16[32,1024]{1,0:T(8,128)(2,1)}, bf16[32,1024]{1,0:T(8,128)(2,1)S(1)}, u32[]{:S(2)}, u32[]{:S(2)}) collective-permute-start(bf16[32,1024]{1,0:T(8,128)(2,1)} %get-tuple-element.117), channel_id=1, source_target_pairs={{0,2},{2,0},{4,6},{6,4},{8,10},{10,8},{12,14},{14,12},{16,18},{18,... | collective-permute-start | bytes 196616 | tf_op jit(solution)/shard_map/ppermute | solution.py:100
  12.5 4.5 %collective-permute-start.1 = (bf16[32,1024]{1,0:T(8,128)(2,1)}, bf16[32,1024]{1,0:T(8,128)(2,1)S(1)}, u32[]{:S(2)}, u32[]{:S(2)}) collective-permute-start(bf16[32,1024]{1,0:T(8,128)(2,1)} %get-tuple-element.118), channel_id=1, source_target_pairs={{0,4},{2,6},{4,0},{6,2},{8,12},{10,14},{12,8},{14,10},{16,20},{18,... | collective-permute-start | bytes 196616 | tf_op jit(solution)/shard_map/ppermute | solution.py:100
  14.0 5.4 %collective-permute-start.2 = (bf16[32,1024]{1,0:T(8,128)(2,1)}, bf16[32,1024]{1,0:T(8,128)(2,1)S(1)}, u32[]{:S(2)}, u32[]{:S(2)}) collective-permute-start(bf16[32,1024]{1,0:T(8,128)(2,1)} %get-tuple-element.119), channel_id=1, source_target_pairs={{0,6},{2,4},{4,2},{6,0},{8,14},{10,12},{12,10},{14,8},{16,22},{18,... | collective-permute-start | bytes 196616 | tf_op jit(solution)/shard_map/ppermute | solution.py:100
  16.1 28.5 %copy-start.4 = (bf16[128,1024]{1,0:T(8,128)(2,1)S(1)}, bf16[128,1024]{1,0:T(8,128)(2,1)}, u32[]{:S(2)}) copy-start(bf16[128,1024]{1,0:T(8,128)(2,1)} %param.14) | copy-start | bytes 786436
  21.6 9.3 %collective-permute-start.5 = (bf16[256,384]{1,0:T(8,128)(2,1)}, bf16[256,384]{1,0:T(8,128)(2,1)S(1)}, u32[]{:S(2)}, u32[]{:S(2)}) collective-permute-start(bf16[256,384]{1,0:T(8,128)(2,1)} %get-tuple-element.135.refs_9_), channel_id=1, source_target_pairs={{0,24},{2,26},{4,28},{6,30},{8,0},{10,2},{12,4},{14,6},{16,8},{18,... | collective-permute-start | bytes 589832 | tf_op jit(solution)/shard_map/ppermute | solution.py:105
  25.2 15.9 %collective-permute-start.4 = (bf16[256,384]{1,0:T(8,128)(2,1)}, bf16[256,384]{1,0:T(8,128)(2,1)S(1)}, u32[]{:S(2)}, u32[]{:S(2)}) collective-permute-start(bf16[256,384]{1,0:T(8,128)(2,1)} %get-tuple-element.135.refs_9_), channel_id=1, source_target_pairs={{0,16},{2,18},{4,20},{6,22},{8,24},{10,26},{12,28},{14,30},{16,0},... | collective-permute-start | bytes 589832 | tf_op jit(solution)/shard_map/ppermute | solution.py:105
  25.3 15.9 %collective-permute-start.3 = (bf16[256,384]{1,0:T(8,128)(2,1)}, bf16[256,384]{1,0:T(8,128)(2,1)S(1)}, u32[]{:S(2)}, u32[]{:S(2)}) collective-permute-start(bf16[256,384]{1,0:T(8,128)(2,1)} %get-tuple-element.135.refs_9_), channel_id=1, source_target_pairs={{0,8},{2,10},{4,12},{6,14},{8,16},{10,18},{12,20},{14,22},{16,24},... | collective-permute-start | bytes 589832 | tf_op jit(solution)/shard_map/ppermute | solution.py:105
  27.2 21.0 %copy-start.34 = (s32[4,4]{1,0:T(4,128)}, s32[4,4]{1,0:T(4,128)S(1)}, u32[]{:S(2)}) copy-start(s32[4,4]{1,0:T(4,128)S(1)} %reduce_window_sum.11.refs_1_.ends_ref) | copy-start | bytes 196
  27.3 13.9 %collective-permute-start.6 = (bf16[64,1792]{1,0:T(8,128)(2,1)}, bf16[64,1792]{1,0:T(8,128)(2,1)S(1)}, u32[]{:S(2)}, u32[]{:S(2)}) collective-permute-start(bf16[64,1792]{1,0:T(8,128)(2,1)} %get-tuple-element.127), channel_id=1, source_target_pairs={{0,2},{2,0},{4,6},{6,4},{8,10},{10,8},{12,14},{14,12},{16,18},{18,... | collective-permute-start | bytes 688136 | tf_op jit(solution)/shard_map/ppermute | solution.py:100
  27.9 13.3 %collective-permute-start.7 = (bf16[64,1792]{1,0:T(8,128)(2,1)}, bf16[64,1792]{1,0:T(8,128)(2,1)S(1)}, u32[]{:S(2)}, u32[]{:S(2)}) collective-permute-start(bf16[64,1792]{1,0:T(8,128)(2,1)} %get-tuple-element.128), channel_id=1, source_target_pairs={{0,4},{2,6},{4,0},{6,2},{8,12},{10,14},{12,8},{14,10},{16,20},{18,... | collective-permute-start | bytes 688136 | tf_op jit(solution)/shard_map/ppermute | solution.py:100
  30.9 17.3 %copy-start.24 = (bf16[256,384]{1,0:T(8,128)(2,1)}, bf16[256,384]{1,0:T(8,128)(2,1)S(1)}, u32[]{:S(2)}) copy-start(bf16[256,384]{1,0:T(8,128)(2,1)S(1)} %collective-permute-done.5.refs_12_) | copy-start | bytes 589828
  31.0 10.3 %collective-permute-start.8 = (bf16[64,1792]{1,0:T(8,128)(2,1)}, bf16[64,1792]{1,0:T(8,128)(2,1)S(1)}, u32[]{:S(2)}, u32[]{:S(2)}) collective-permute-start(bf16[64,1792]{1,0:T(8,128)(2,1)} %get-tuple-element.129), channel_id=1, source_target_pairs={{0,6},{2,4},{4,2},{6,0},{8,14},{10,12},{12,10},{14,8},{16,22},{18,... | collective-permute-start | bytes 688136 | tf_op jit(solution)/shard_map/ppermute | solution.py:100
  41.2 20.6 %copy-start.25 = (bf16[256,384]{1,0:T(8,128)(2,1)}, bf16[256,384]{1,0:T(8,128)(2,1)S(1)}, u32[]{:S(2)}) copy-start(bf16[256,384]{1,0:T(8,128)(2,1)S(1)} %collective-permute-done.4.refs_11_) | copy-start | bytes 589828
  42.1 15.6 %copy-start.13 = (bf16[128,1024]{1,0:T(8,128)(2,1)S(1)}, bf16[128,1024]{1,0:T(8,128)(2,1)}, u32[]{:S(2)}) copy-start(bf16[128,1024]{1,0:T(8,128)(2,1)} %param.27) | copy-start | bytes 786436
  42.1 19.1 %copy-start.37 = (f32[64]{0:T(128)S(1)}, f32[64]{0:T(128)}, u32[]{:S(2)}) copy-start(f32[64]{0:T(128)} %param.17) | copy-start | bytes 772
  42.1 19.1 %copy-start.38 = (f32[64]{0:T(128)S(1)}, f32[64]{0:T(128)}, u32[]{:S(2)}) copy-start(f32[64]{0:T(128)} %param.18) | copy-start | bytes 772
  44.6 160.3 %reduce-scatter.2.cloned.1.call-start = ((), (), s32[]{:S(2)}) async-start(), calls=%async_computation.2 | async-start | bytes 4587520 | tf_op jit(solution)/shard_map/reduce_scatter | solution.py:934
  44.6 9.3 %collective-permute-start.9 = (bf16[128,1024]{1,0:T(8,128)(2,1)S(1)}, bf16[128,1024]{1,0:T(8,128)(2,1)S(1)}, u32[]{:S(2)}, u32[]{:S(2)}) collective-permute-start(bf16[128,1024]{1,0:T(8,128)(2,1)S(1)} %copy-done.4), channel_id=1, source_target_pairs={{0,2},{2,0},{4,6},{6,4},{8,10},{10,8},{12,14},{14,12},{16,18},{18,... | collective-permute-start | bytes 786440 | tf_op jit(solution)/shard_map/ppermute | solution.py:100
  45.2 12.3 %collective-permute-start.10 = (bf16[128,1024]{1,0:T(8,128)(2,1)S(1)}, bf16[128,1024]{1,0:T(8,128)(2,1)S(1)}, u32[]{:S(2)}, u32[]{:S(2)}) collective-permute-start(bf16[128,1024]{1,0:T(8,128)(2,1)S(1)} %copy-done.4), channel_id=1, source_target_pairs={{0,4},{2,6},{4,0},{6,2},{8,12},{10,14},{12,8},{14,10},{16,20},{18,... | collective-permute-start | bytes 786440 | tf_op jit(solution)/shard_map/ppermute | solution.py:100
  45.7 11.8 %collective-permute-start.11 = (bf16[128,1024]{1,0:T(8,128)(2,1)S(1)}, bf16[128,1024]{1,0:T(8,128)(2,1)S(1)}, u32[]{:S(2)}, u32[]{:S(2)}) collective-permute-start(bf16[128,1024]{1,0:T(8,128)(2,1)S(1)} %copy-done.4), channel_id=1, source_target_pairs={{0,6},{2,4},{4,2},{6,0},{8,14},{10,12},{12,10},{14,8},{16,22},{18,... | collective-permute-start | bytes 786440 | tf_op jit(solution)/shard_map/ppermute | solution.py:100
  57.6 4.2 %collective-permute-start.12 = (bf16[512,1024]{1,0:T(8,128)(2,1)S(1)}, bf16[512,1024]{1,0:T(8,128)(2,1)S(1)}, u32[]{:S(2)}, u32[]{:S(2)}) collective-permute-start(bf16[512,1024]{1,0:T(8,128)(2,1)S(1)} %constant_dynamic-update-slice_fusion.refs_2_), channel_id=1, source_target_pairs={{0,1},{1,0},{2,3},{3,2},{4,5},{5,4},{6,7},{7,6},{8,9},{9,8},{10,11... | collective-permute-start | bytes 3145736 | tf_op jit(solution)/shard_map/ppermute | solution.py:109
  57.7 15.5 %collective-permute-start.15 = (bf16[128,1024]{1,0:T(8,128)(2,1)S(1)}, bf16[128,1024]{1,0:T(8,128)(2,1)S(1)}, u32[]{:S(2)}, u32[]{:S(2)}) collective-permute-start(bf16[128,1024]{1,0:T(8,128)(2,1)S(1)} %copy-done.13), channel_id=1, source_target_pairs={{0,6},{2,4},{4,2},{6,0},{8,14},{10,12},{12,10},{14,8},{16,22},{18,... | collective-permute-start | bytes 786440 | tf_op jit(solution)/shard_map/ppermute | solution.py:100
  58.9 14.3 %collective-permute-start.14 = (bf16[128,1024]{1,0:T(8,128)(2,1)S(1)}, bf16[128,1024]{1,0:T(8,128)(2,1)S(1)}, u32[]{:S(2)}, u32[]{:S(2)}) collective-permute-start(bf16[128,1024]{1,0:T(8,128)(2,1)S(1)} %copy-done.13), channel_id=1, source_target_pairs={{0,4},{2,6},{4,0},{6,2},{8,12},{10,14},{12,8},{14,10},{16,20},{18,... | collective-permute-start | bytes 786440 | tf_op jit(solution)/shard_map/ppermute | solution.py:100
  60.3 13.0 %collective-permute-start.13 = (bf16[128,1024]{1,0:T(8,128)(2,1)S(1)}, bf16[128,1024]{1,0:T(8,128)(2,1)S(1)}, u32[]{:S(2)}, u32[]{:S(2)}) collective-permute-start(bf16[128,1024]{1,0:T(8,128)(2,1)S(1)} %copy-done.13), channel_id=1, source_target_pairs={{0,2},{2,0},{4,6},{6,4},{8,10},{10,8},{12,14},{14,12},{16,18},{18,... | collective-permute-start | bytes 786440 | tf_op jit(solution)/shard_map/ppermute | solution.py:100
  74.6 2.9 %collective-permute-start.16 = (bf16[512,1024]{1,0:T(8,128)(2,1)}, bf16[512,1024]{1,0:T(8,128)(2,1)S(1)}, u32[]{:S(2)}, u32[]{:S(2)}) collective-permute-start(bf16[512,1024]{1,0:T(8,128)(2,1)} %get-tuple-element.142), channel_id=1, source_target_pairs={{0,1},{1,0},{2,3},{3,2},{4,5},{5,4},{6,7},{7,6},{8,9},{9,8},{10,11... | collective-permute-start | bytes 3145736 | tf_op jit(solution)/shard_map/ppermute | solution.py:109
  82.1 16.4 %copy-start.35 = (f32[1024]{0:T(1024)S(1)}, f32[1024]{0:T(1024)}, u32[]{:S(2)}) copy-start(f32[1024]{0:T(1024)} %param.19) | copy-start | bytes 12292
  82.1 20.1 %copy-start.20 = (bf16[128,1024]{1,0:T(8,128)(2,1)S(1)}, bf16[128,1024]{1,0:T(8,128)(2,1)}, u32[]{:S(2)}) copy-start(bf16[128,1024]{1,0:T(8,128)(2,1)} %copy-done.19) | copy-start | bytes 786436
  82.1 20.1 %copy-start.18 = (bf16[128,1024]{1,0:T(8,128)(2,1)S(1)}, bf16[128,1024]{1,0:T(8,128)(2,1)}, u32[]{:S(2)}) copy-start(bf16[128,1024]{1,0:T(8,128)(2,1)} %copy-done.17) | copy-start | bytes 786436
  82.2 9.4 %collective-permute-start.17 = (bf16[128,1024]{1,0:T(8,128)(2,1)}, bf16[128,1024]{1,0:T(8,128)(2,1)S(1)}, u32[]{:S(2)}, u32[]{:S(2)}) collective-permute-start(bf16[128,1024]{1,0:T(8,128)(2,1)} %get-tuple-element.144), channel_id=1, source_target_pairs={{0,2},{2,0},{4,6},{6,4},{8,10},{10,8},{12,14},{14,12},{16,18},{18,... | collective-permute-start | bytes 786440 | tf_op jit(solution)/shard_map/ppermute | solution.py:100
  83.3 13.9 %collective-permute-start.18 = (bf16[128,1024]{1,0:T(8,128)(2,1)}, bf16[128,1024]{1,0:T(8,128)(2,1)S(1)}, u32[]{:S(2)}, u32[]{:S(2)}) collective-permute-start(bf16[128,1024]{1,0:T(8,128)(2,1)} %get-tuple-element.145), channel_id=1, source_target_pairs={{0,4},{2,6},{4,0},{6,2},{8,12},{10,14},{12,8},{14,10},{16,20},{18,... | collective-permute-start | bytes 786440 | tf_op jit(solution)/shard_map/ppermute | solution.py:100
  83.9 13.3 %collective-permute-start.19 = (bf16[128,1024]{1,0:T(8,128)(2,1)}, bf16[128,1024]{1,0:T(8,128)(2,1)S(1)}, u32[]{:S(2)}, u32[]{:S(2)}) collective-permute-start(bf16[128,1024]{1,0:T(8,128)(2,1)} %get-tuple-element.146), channel_id=1, source_target_pairs={{0,6},{2,4},{4,2},{6,0},{8,14},{10,12},{12,10},{14,8},{16,22},{18,... | collective-permute-start | bytes 786440 | tf_op jit(solution)/shard_map/ppermute | solution.py:100
  98.6 10.2 %collective-permute-start.22 = (bf16[128,1024]{1,0:T(8,128)(2,1)S(1)}, bf16[128,1024]{1,0:T(8,128)(2,1)S(1)}, u32[]{:S(2)}, u32[]{:S(2)}) collective-permute-start(bf16[128,1024]{1,0:T(8,128)(2,1)S(1)} %multiply_convert_fusion), channel_id=1, source_target_pairs={{0,6},{2,4},{4,2},{6,0},{8,14},{10,12},{12,10},{14,8},{16,22},{18,... | collective-permute-start | bytes 786440 | tf_op jit(solution)/shard_map/ppermute | solution.py:100
  99.9 12.3 %collective-permute-start.21 = (bf16[128,1024]{1,0:T(8,128)(2,1)S(1)}, bf16[128,1024]{1,0:T(8,128)(2,1)S(1)}, u32[]{:S(2)}, u32[]{:S(2)}) collective-permute-start(bf16[128,1024]{1,0:T(8,128)(2,1)S(1)} %multiply_convert_fusion), channel_id=1, source_target_pairs={{0,4},{2,6},{4,0},{6,2},{8,12},{10,14},{12,8},{14,10},{16,20},{18,... | collective-permute-start | bytes 786440 | tf_op jit(solution)/shard_map/ppermute | solution.py:100
  101.1 11.1 %collective-permute-start.20 = (bf16[128,1024]{1,0:T(8,128)(2,1)S(1)}, bf16[128,1024]{1,0:T(8,128)(2,1)S(1)}, u32[]{:S(2)}, u32[]{:S(2)}) collective-permute-start(bf16[128,1024]{1,0:T(8,128)(2,1)S(1)} %multiply_convert_fusion), channel_id=1, source_target_pairs={{0,2},{2,0},{4,6},{6,4},{8,10},{10,8},{12,14},{14,12},{16,18},{18,... | collective-permute-start | bytes 786440 | tf_op jit(solution)/shard_map/ppermute | solution.py:100
  102.3 15.4 %copy-start.9 = (bf16[512,1024]{1,0:T(8,128)(2,1)}, bf16[512,1024]{1,0:T(8,128)(2,1)S(1)}, u32[]{:S(2)}) copy-start(bf16[512,1024]{1,0:T(8,128)(2,1)S(1)} %constant_dynamic-update-slice_fusion.4.g_m) | copy-start | bytes 3145732
  102.3 10.2 %collective-permute-start.24 = (bf16[512,1024]{1,0:T(8,128)(2,1)S(1)}, bf16[512,1024]{1,0:T(8,128)(2,1)S(1)}, u32[]{:S(2)}, u32[]{:S(2)}) collective-permute-start(bf16[512,1024]{1,0:T(8,128)(2,1)S(1)} %constant_dynamic-update-slice_fusion.4.g_m), channel_id=1, source_target_pairs={{0,1},{1,0},{2,3},{3,2},{4,5},{5,4},{6,7},{7,6},{8,9},{9,8},{10,11... | collective-permute-start | bytes 3145736 | tf_op jit(solution)/shard_map/ppermute | solution.py:109
  112.3 2.9 %collective-permute-start.23 = (bf16[512,1024]{1,0:T(8,128)(2,1)S(1)}, bf16[512,1024]{1,0:T(8,128)(2,1)}, u32[]{:S(2)}, u32[]{:S(2)}) collective-permute-start(bf16[512,1024]{1,0:T(8,128)(2,1)S(1)} %pad_maximum_fusion.x_m), channel_id=1, source_target_pairs={{0,1},{1,0},{2,3},{3,2},{4,5},{5,4},{6,7},{7,6},{8,9},{9,8},{10,11... | collective-permute-start | bytes 3145736 | tf_op jit(solution)/shard_map/ppermute | solution.py:109
  139.8 2.9 %collective-permute-start.25 = (bf16[512,1024]{1,0:T(8,128)(2,1)}, bf16[512,1024]{1,0:T(8,128)(2,1)S(1)}, u32[]{:S(2)}, u32[]{:S(2)}) collective-permute-start(bf16[512,1024]{1,0:T(8,128)(2,1)} %get-tuple-element.148), channel_id=1, source_target_pairs={{0,1},{1,0},{2,3},{3,2},{4,5},{5,4},{6,7},{7,6},{8,9},{9,8},{10,11... | collective-permute-start | bytes 3145736 | tf_op jit(solution)/shard_map/ppermute | solution.py:109
  147.4 11.0 %collective-permute-start.26 = (bf16[128,1024]{1,0:T(8,128)(2,1)}, bf16[128,1024]{1,0:T(8,128)(2,1)S(1)}, u32[]{:S(2)}, u32[]{:S(2)}) collective-permute-start(bf16[128,1024]{1,0:T(8,128)(2,1)} %get-tuple-element.154), channel_id=1, source_target_pairs={{0,2},{2,0},{4,6},{6,4},{8,10},{10,8},{12,14},{14,12},{16,18},{18,... | collective-permute-start | bytes 786440 | tf_op jit(solution)/shard_map/ppermute | solution.py:100
  148.9 13.9 %collective-permute-start.27 = (bf16[128,1024]{1,0:T(8,128)(2,1)}, bf16[128,1024]{1,0:T(8,128)(2,1)S(1)}, u32[]{:S(2)}, u32[]{:S(2)}) collective-permute-start(bf16[128,1024]{1,0:T(8,128)(2,1)} %get-tuple-element.155), channel_id=1, source_target_pairs={{0,4},{2,6},{4,0},{6,2},{8,12},{10,14},{12,8},{14,10},{16,20},{18,... | collective-permute-start | bytes 786440 | tf_op jit(solution)/shard_map/ppermute | solution.py:100
  150.4 12.4 %collective-permute-start.28 = (bf16[128,1024]{1,0:T(8,128)(2,1)}, bf16[128,1024]{1,0:T(8,128)(2,1)S(1)}, u32[]{:S(2)}, u32[]{:S(2)}) collective-permute-start(bf16[128,1024]{1,0:T(8,128)(2,1)} %get-tuple-element.156), channel_id=1, source_target_pairs={{0,6},{2,4},{4,2},{6,0},{8,14},{10,12},{12,10},{14,8},{16,22},{18,... | collective-permute-start | bytes 786440 | tf_op jit(solution)/shard_map/ppermute | solution.py:100
  163.9 10.2 %collective-permute-start.31 = (bf16[128,1024]{1,0:T(8,128)(2,1)S(1)}, bf16[128,1024]{1,0:T(8,128)(2,1)S(1)}, u32[]{:S(2)}, u32[]{:S(2)}) collective-permute-start(bf16[128,1024]{1,0:T(8,128)(2,1)S(1)} %get-tuple-element.213), channel_id=1, source_target_pairs={{0,6},{2,4},{4,2},{6,0},{8,14},{10,12},{12,10},{14,8},{16,22},{18,... | collective-permute-start | bytes 786440 | tf_op jit(solution)/shard_map/ppermute | solution.py:100
  165.4 12.4 %collective-permute-start.30 = (bf16[128,1024]{1,0:T(8,128)(2,1)S(1)}, bf16[128,1024]{1,0:T(8,128)(2,1)S(1)}, u32[]{:S(2)}, u32[]{:S(2)}) collective-permute-start(bf16[128,1024]{1,0:T(8,128)(2,1)S(1)} %get-tuple-element.213), channel_id=1, source_target_pairs={{0,4},{2,6},{4,0},{6,2},{8,12},{10,14},{12,8},{14,10},{16,20},{18,... | collective-permute-start | bytes 786440 | tf_op jit(solution)/shard_map/ppermute | solution.py:100
  166.6 11.3 %collective-permute-start.29 = (bf16[128,1024]{1,0:T(8,128)(2,1)S(1)}, bf16[128,1024]{1,0:T(8,128)(2,1)S(1)}, u32[]{:S(2)}, u32[]{:S(2)}) collective-permute-start(bf16[128,1024]{1,0:T(8,128)(2,1)S(1)} %get-tuple-element.213), channel_id=1, source_target_pairs={{0,2},{2,0},{4,6},{6,4},{8,10},{10,8},{12,14},{14,12},{16,18},{18,... | collective-permute-start | bytes 786440 | tf_op jit(solution)/shard_map/ppermute | solution.py:100
  167.4 10.6 %collective-permute-start.33 = (bf16[512,1024]{1,0:T(8,128)(2,1)S(1)}, bf16[512,1024]{1,0:T(8,128)(2,1)}, u32[]{:S(2)}, u32[]{:S(2)}) collective-permute-start(bf16[512,1024]{1,0:T(8,128)(2,1)S(1)} %copy-done.39), channel_id=1, source_target_pairs={{0,1},{1,0},{2,3},{3,2},{4,5},{5,4},{6,7},{7,6},{8,9},{9,8},{10,11... | collective-permute-start | bytes 3145736 | tf_op jit(solution)/shard_map/ppermute | solution.py:109
  177.9 4.1 %collective-permute-start.32 = (bf16[512,1024]{1,0:T(8,128)(2,1)S(1)}, bf16[512,1024]{1,0:T(8,128)(2,1)}, u32[]{:S(2)}, u32[]{:S(2)}) collective-permute-start(bf16[512,1024]{1,0:T(8,128)(2,1)S(1)} %pad_maximum_fusion.1.refs_9_), channel_id=1, source_target_pairs={{0,1},{1,0},{2,3},{3,2},{4,5},{5,4},{6,7},{7,6},{8,9},{9,8},{10,11... | collective-permute-start | bytes 3145736 | tf_op jit(solution)/shard_map/ppermute | solution.py:109
  182.0 18.9 %collective-permute-start.34 = (bf16[128,1024]{1,0:T(8,128)(2,1)}, bf16[128,1024]{1,0:T(8,128)(2,1)}, u32[]{:S(2)}, u32[]{:S(2)}) collective-permute-start(bf16[128,1024]{1,0:T(8,128)(2,1)} %get-tuple-element.167), channel_id=1, source_target_pairs={{0,2},{2,0},{4,6},{6,4},{8,10},{10,8},{12,14},{14,12},{16,18},{18,... | collective-permute-start | bytes 786440 | tf_op jit(solution)/shard_map/ppermute | solution.py:100
  183.4 17.5 %collective-permute-start.35 = (bf16[128,1024]{1,0:T(8,128)(2,1)}, bf16[128,1024]{1,0:T(8,128)(2,1)}, u32[]{:S(2)}, u32[]{:S(2)}) collective-permute-start(bf16[128,1024]{1,0:T(8,128)(2,1)} %get-tuple-element.168), channel_id=1, source_target_pairs={{0,4},{2,6},{4,0},{6,2},{8,12},{10,14},{12,8},{14,10},{16,20},{18,... | collective-permute-start | bytes 786440 | tf_op jit(solution)/shard_map/ppermute | solution.py:100
  183.9 16.9 %collective-permute-start.36 = (bf16[128,1024]{1,0:T(8,128)(2,1)}, bf16[128,1024]{1,0:T(8,128)(2,1)}, u32[]{:S(2)}, u32[]{:S(2)}) collective-permute-start(bf16[128,1024]{1,0:T(8,128)(2,1)} %get-tuple-element.169), channel_id=1, source_target_pairs={{0,6},{2,4},{4,2},{6,0},{8,14},{10,12},{12,10},{14,8},{16,22},{18,... | collective-permute-start | bytes 786440 | tf_op jit(solution)/shard_map/ppermute | solution.py:100
  200.9 37.7 %copy-start.15 = (f32[128,1024]{1,0:T(8,128)S(1)}, f32[128,1024]{1,0:T(8,128)}, u32[]{:S(2)}) copy-start(f32[128,1024]{1,0:T(8,128)} %get-tuple-element.166) | copy-start | bytes 1572868
  200.9 4.0 %collective-permute-start.37 = (bf16[512,1024]{1,0:T(8,128)(2,1)}, bf16[512,1024]{1,0:T(8,128)(2,1)S(1)}, u32[]{:S(2)}, u32[]{:S(2)}) collective-permute-start(bf16[512,1024]{1,0:T(8,128)(2,1)} %get-tuple-element.182), channel_id=1, source_target_pairs={{0,1},{1,0},{2,3},{3,2},{4,5},{5,4},{6,7},{7,6},{8,9},{9,8},{10,11... | collective-permute-start | bytes 3145736 | tf_op jit(solution)/shard_map/ppermute | solution.py:109
  201.0 11.7 %collective-permute-start.41 = (bf16[272,384]{1,0:T(8,128)(2,1)}, bf16[272,384]{1,0:T(8,128)(2,1)}, u32[]{:S(2)}, u32[]{:S(2)}) collective-permute-start(bf16[272,384]{1,0:T(8,128)(2,1)} %get-tuple-element.191), channel_id=1, source_target_pairs={{0,8},{2,10},{4,12},{6,14},{8,16},{10,18},{12,20},{14,22},{16,24},... | collective-permute-start | bytes 626696 | tf_op jit(solution)/shard_map/ppermute | solution.py:105
  201.0 18.3 %collective-permute-start.42 = (bf16[272,384]{1,0:T(8,128)(2,1)}, bf16[272,384]{1,0:T(8,128)(2,1)}, u32[]{:S(2)}, u32[]{:S(2)}) collective-permute-start(bf16[272,384]{1,0:T(8,128)(2,1)} %get-tuple-element.192), channel_id=1, source_target_pairs={{0,16},{2,18},{4,20},{6,22},{8,24},{10,26},{12,28},{14,30},{16,0},... | collective-permute-start | bytes 626696 | tf_op jit(solution)/shard_map/ppermute | solution.py:105
  202.5 16.9 %collective-permute-start.43 = (bf16[272,384]{1,0:T(8,128)(2,1)}, bf16[272,384]{1,0:T(8,128)(2,1)}, u32[]{:S(2)}, u32[]{:S(2)}) collective-permute-start(bf16[272,384]{1,0:T(8,128)(2,1)} %get-tuple-element.193), channel_id=1, source_target_pairs={{0,24},{2,26},{4,28},{6,30},{8,0},{10,2},{12,4},{14,6},{16,8},{18,... | collective-permute-start | bytes 626696 | tf_op jit(solution)/shard_map/ppermute | solution.py:105
  210.6 34.5 %copy-start.8 = (f32[128,1024]{1,0:T(8,128)S(1)}, f32[128,1024]{1,0:T(8,128)}, u32[]{:S(2)}) copy-start(f32[128,1024]{1,0:T(8,128)} %get-tuple-element.184) | copy-start | bytes 1572868
  210.6 34.5 %copy-start.27 = (f32[1024]{0:T(1024)S(1)}, f32[1024]{0:T(1024)}, u32[]{:S(2)}) copy-start(f32[1024]{0:T(1024)} %param.16) | copy-start | bytes 12292
  210.6 31.9 %collective-permute-start.38 = (bf16[256,1024]{1,0:T(8,128)(2,1)}, bf16[256,1024]{1,0:T(8,128)(2,1)S(1)}, u32[]{:S(2)}, u32[]{:S(2)}) collective-permute-start(bf16[256,1024]{1,0:T(8,128)(2,1)} %get-tuple-element.185), channel_id=1, source_target_pairs={{0,2},{2,0},{4,6},{6,4},{8,10},{10,8},{12,14},{14,12},{16,18},{18,... | collective-permute-start | bytes 1572872 | tf_op jit(solution)/shard_map/ppermute | solution.py:100
  212.0 30.5 %collective-permute-start.39 = (bf16[256,1024]{1,0:T(8,128)(2,1)}, bf16[256,1024]{1,0:T(8,128)(2,1)S(1)}, u32[]{:S(2)}, u32[]{:S(2)}) collective-permute-start(bf16[256,1024]{1,0:T(8,128)(2,1)} %get-tuple-element.186), channel_id=1, source_target_pairs={{0,4},{2,6},{4,0},{6,2},{8,12},{10,14},{12,8},{14,10},{16,20},{18,... | collective-permute-start | bytes 1572872 | tf_op jit(solution)/shard_map/ppermute | solution.py:100
  212.6 32.4 %collective-permute-start.40 = (bf16[256,1024]{1,0:T(8,128)(2,1)}, bf16[256,1024]{1,0:T(8,128)(2,1)S(1)}, u32[]{:S(2)}, u32[]{:S(2)}) collective-permute-start(bf16[256,1024]{1,0:T(8,128)(2,1)} %get-tuple-element.187), channel_id=1, source_target_pairs={{0,6},{2,4},{4,2},{6,0},{8,14},{10,12},{12,10},{14,8},{16,22},{18,... | collective-permute-start | bytes 1572872 | tf_op jit(solution)/shard_map/ppermute | solution.py:100
  221.4 15.7 %collective-permute-start.44 = (bf16[80,384]{1,0:T(8,128)(2,1)}, bf16[80,384]{1,0:T(8,128)(2,1)S(1)}, u32[]{:S(2)}, u32[]{:S(2)}) collective-permute-start(bf16[80,384]{1,0:T(8,128)(2,1)} %get-tuple-element.195), channel_id=1, source_target_pairs={{0,2},{2,0},{4,6},{6,4},{8,10},{10,8},{12,14},{14,12},{16,18},{18,... | collective-permute-start | bytes 184328 | tf_op jit(solution)/shard_map/ppermute | solution.py:100
  222.8 17.8 %collective-permute-start.45 = (bf16[80,384]{1,0:T(8,128)(2,1)}, bf16[80,384]{1,0:T(8,128)(2,1)S(1)}, u32[]{:S(2)}, u32[]{:S(2)}) collective-permute-start(bf16[80,384]{1,0:T(8,128)(2,1)} %get-tuple-element.196), channel_id=1, source_target_pairs={{0,4},{2,6},{4,0},{6,2},{8,12},{10,14},{12,8},{14,10},{16,20},{18,... | collective-permute-start | bytes 184328 | tf_op jit(solution)/shard_map/ppermute | solution.py:100
  237.1 5.3 %collective-permute-start.46 = (bf16[80,384]{1,0:T(8,128)(2,1)}, bf16[80,384]{1,0:T(8,128)(2,1)S(1)}, u32[]{:S(2)}, u32[]{:S(2)}) collective-permute-start(bf16[80,384]{1,0:T(8,128)(2,1)} %get-tuple-element.197), channel_id=1, source_target_pairs={{0,6},{2,4},{4,2},{6,0},{8,14},{10,12},{12,10},{14,8},{16,22},{18,... | collective-permute-start | bytes 184328 | tf_op jit(solution)/shard_map/ppermute | solution.py:100
  245.0 4.3 %collective-permute-start.47 = (f32[8,384]{1,0:T(8,128)}, f32[8,384]{1,0:T(8,128)S(1)}, u32[]{:S(2)}, u32[]{:S(2)}) collective-permute-start(f32[8,384]{1,0:T(8,128)} %get-tuple-element.202), channel_id=1, source_target_pairs={{0,1},{1,0},{2,3},{3,2},{4,5},{5,4},{6,7},{7,6},{8,9},{9,8},{10,11... | collective-permute-start | bytes 36872 | tf_op jit(solution)/shard_map/ppermute | solution.py:109
  (26 other events, 73.3 us)
Sparse Core Ops, SparseCore 0:
  44.7 72.9 all-gather.1
  133.3 67.0 reduce-scatter.1

commit v12 on v11

--- a/solution.py
+++ b/solution.py
@@ -318,14 +318,12 @@
 
 
 def attn_back_kernel(
-    layers, where_ref, ends_ref, tok_m, tok_o, a_gain, q_gain, k_gain, cos, sin, dh_m, dh_o,
+    where_ref, ends_ref, tok_m, tok_o, a_gain, q_gain, k_gain, cos, sin, dh_m, dh_o,
     pre_ref, low_ref, mixed_ref, weight, gain_ffn, *refs,
 ):
-    send, keep, own, gains_out = refs[:4]
-    pieces = refs[4 : 3 + layers]
-    held, total, sum_a, sum_qk = refs[3 + layers :]
+    send, keep, grad_out, gains_out, held, total, sum_a, sum_qk = refs
     step = pl.program_id(0)
-    depth, core = where_ref[1], where_ref[2]
+    core = where_ref[2]
     local = tok_m.shape[0] // GROUPS_STEP
     scale = HEAD_DIM ** (-0.5)
 
@@ -399,15 +397,7 @@
         qk_sum = jnp.where(lane_ids(q_sum.shape) < HALF, q_sum, k_sum)
         ids = lax.broadcasted_iota(jnp.int32, (GAIN_ROWS, LANES), 0)
         gains_out[:, 2 * LANES :] = jnp.where(ids == 0, qk_sum, 0.0)
-        gains = gains_out[...]
-        top = gains.astype(bfloat16)
-        rest = (gains - top.astype(float32)).astype(bfloat16)
-        tail = jnp.concatenate([top.astype(float32), rest.astype(float32)], axis=0).astype(bfloat16)
-        rows = own.shape[0]
-        own[...] = total[deep_rows(depth, 0, layers, rows), :]
-        for index, piece in enumerate(pieces):
-            piece[:rows, :] = total[deep_rows(depth, index + 1, layers, rows), :].astype(bfloat16)
-            piece[rows:, :] = tail
+        grad_out[...] = total[...].astype(bfloat16)
 
 
 def attn_specs(rows, width, group_height):
@@ -452,27 +442,24 @@
     )(where, ends, tok_mine, tok_other, *gains, *tables, *pieces)
 
 
-def attn_back(where, ends, layers, tok_mine, tok_other, gains, tables, dh, saved, weight, gain_ffn):
+def attn_back(where, ends, tok_mine, tok_other, gains, tables, dh, saved, weight, gain_ffn):
     rows, width = tok_mine.shape
     local = rows // PLANE
     step = GROUPS_STEP * local
     scalar, block, gain, small, table, wide = attn_specs(step, width, 2 * step)
-    high, columns = weight.shape[0] // layers, weight.shape[1]
-    tail = 2 * GAIN_ROWS
+    columns = weight.shape[1]
     return pl.pallas_call(
-        lambda *refs: attn_back_kernel(layers, *refs),
+        attn_back_kernel,
         grid=(PLANE // GROUPS_STEP,),
         in_specs=[scalar, scalar, block, block, gain, small, small, table, table, block, block]
         + [wide, wide, table, whole_spec(weight.shape), gain],
-        out_specs=[block, block, whole_spec((high, columns)), whole_spec((GAIN_ROWS, columns))]
-        + [whole_spec((high + tail, columns))] * (layers - 1),
+        out_specs=[block, block, whole_spec(weight.shape), whole_spec((GAIN_ROWS, columns))],
         out_shape=[
             jax.ShapeDtypeStruct((rows, width), bfloat16),
             jax.ShapeDtypeStruct((rows, width), float32),
-            jax.ShapeDtypeStruct((high, columns), float32),
+            jax.ShapeDtypeStruct(weight.shape, bfloat16),
             jax.ShapeDtypeStruct((GAIN_ROWS, columns), float32),
-        ]
-        + [jax.ShapeDtypeStruct((high + tail, columns), bfloat16)] * (layers - 1),
+        ],
         scratch_shapes=[
             pltpu.VMEM((2 * step, width), float32),
             pltpu.VMEM(weight.shape, float32),
@@ -599,30 +586,16 @@
 
 
 def chip_sum_kernel(keep, received, *outs):
+    rows = outs[0].shape[0]
     for mask, out in enumerate(outs):
-
-        @pl.when(pl.program_id(0) == mask)
-        def _(out=out):
-            out[...] = (keep[...] + received[...].astype(float32)).astype(out.dtype)
-
-
-def partner_specs(rows, width):
-    return pl.BlockSpec((rows, width), lambda i: (i, 0)), whole_spec((rows, width))
+        span = slice(mask * rows, (mask + 1) * rows)
+        out[...] = (keep[span, :] + received[span, :].astype(float32)).astype(out.dtype)
 
 
 def chip_sum(keep, received):
-    rows, width = keep.shape[0] // PLANE, keep.shape[1]
-    step, whole = partner_specs(rows, width)
-    return pl.pallas_call(
-        chip_sum_kernel,
-        grid=(PLANE,),
-        in_specs=[step, step],
-        out_specs=[whole] * PLANE,
-        out_shape=[jax.ShapeDtypeStruct((rows, width), float32)]
-        + [jax.ShapeDtypeStruct((rows, width), bfloat16)] * (PLANE - 1),
-        compiler_params=pltpu.CompilerParams(vmem_limit_bytes=VMEM_BYTES),
-        cost_estimate=COST,
-    )(keep, received)
+    shape = (keep.shape[0] // PLANE, keep.shape[1])
+    outs = [(shape, float32)] + [(shape, bfloat16)] * (PLANE - 1)
+    return call(chip_sum_kernel, outs, keep, received)
 
 
 def plane_sent(parts):
@@ -637,55 +610,26 @@
     return sum(part.astype(float32) for part in parts)
 
 
-def tail_kernel(where_ref, keep, received, own_ff, own, ff_out, *refs):
-    messages, held = refs[:-1], refs[-1]
+def plane_split_kernel(where_ref, own, *refs):
+    outs, held = refs[:-1], refs[-1]
+    held[...] = own[...].astype(float32)
     place = where_ref[0]
-    local = own.shape[0]
-    rows = ff_out.shape[0]
-    tall = (messages[0].shape[0] - local) // 2
-    width = own.shape[1]
-
-    @pl.when(pl.program_id(0) == 0)
-    def _():
-        held[...] = own_ff[...].astype(float32)
-
-    value = keep[...] + received[...].astype(float32)
-    for mask in range(PLANE):
-
-        @pl.when(pl.program_id(0) == mask)
-        def _(mask=mask):
-            grads = held[pl.ds(pl.multiple_of((place ^ mask) * rows, rows), rows), :]
-            if mask == 0:
-                own[...] = value
-                ff_out[...] = grads
-            else:
-                out = messages[mask - 1]
-                out[:local, :] = value.astype(bfloat16)
-                out[local : local + tall, :] = padded(grads[:, :width], tall).astype(bfloat16)
-                rest = grads.shape[1] - width
-                out[local + tall :, :rest] = padded(grads[:, width:], tall).astype(bfloat16)
-                out[local + tall :, rest:] = jnp.zeros((tall, width - rest), bfloat16)
-
-
-def tail_messages(where, keep, received, own_ff):
-    local, width = keep.shape[0] // PLANE, keep.shape[1]
-    rows, columns = own_ff.shape[0] // PLANE, own_ff.shape[1]
-    message = (local + 2 * max(rows, 16), width)
-    step, whole = partner_specs(local, width)
-    return pl.pallas_call(
-        tail_kernel,
-        grid=(PLANE,),
-        in_specs=[pl.BlockSpec(memory_space=pltpu.SMEM), step, step, whole_spec(own_ff.shape)],
-        out_specs=[whole, whole_spec((rows, columns))] + [whole_spec(message)] * (PLANE - 1),
-        out_shape=[
-            jax.ShapeDtypeStruct((local, width), float32),
-            jax.ShapeDtypeStruct((rows, columns), float32),
-        ]
-        + [jax.ShapeDtypeStruct(message, bfloat16)] * (PLANE - 1),
-        scratch_shapes=[pltpu.VMEM(own_ff.shape, float32)],
-        compiler_params=pltpu.CompilerParams(vmem_limit_bytes=VMEM_BYTES),
-        cost_estimate=COST,
-    )(where, keep, received, own_ff)
+    rows = own.shape[0] // PLANE
+    for mask, out in enumerate(outs):
+        at = pl.multiple_of((place ^ mask) * rows, rows)
+        out[...] = held[pl.ds(at, rows), :].astype(out.dtype)
+
+
+def plane_split(where, own):
+    shape = (own.shape[0] // PLANE, own.shape[1])
+    return call(
+        plane_split_kernel,
+        [(shape, bfloat16)] * PLANE,
+        where,
+        own,
+        scalars=1,
+        scratch=[pltpu.VMEM(own.shape, float32)],
+    )
 
 
 def joined_gains(tail):
@@ -698,29 +642,22 @@
     return jnp.concatenate([top, rest], axis=0)
 
 
-def plane_sum_attn_kernel(where_ref, own, gains, *refs):
+def split_attn_kernel(where_ref, own, gains, *refs):
     received, outs = refs[: -PLANE - 2], refs[-PLANE - 2 : -2]
     held, held_gains = refs[-2:]
     layers = len(received) + 1
-    value = own[...]
-    high = own.shape[0]
     depth = where_ref[1]
-    held_gains[deep_rows(depth, 0, layers, GAIN_ROWS), :] = joined_gains(split_gains(gains[...]))
-    for step, part in enumerate(received):
-        value = value + part[:high, :].astype(float32)
-        held_gains[deep_rows(depth, -1 - step, layers, GAIN_ROWS), :] = joined_gains(
-            part[high:, :].astype(float32)
-        )
-    held[...] = value
+    for step, part in enumerate((gains,) + received):
+        held_gains[deep_rows(depth, -step, layers, GAIN_ROWS), :] = part[...]
+    held[...] = own[...].astype(float32)
     sums = held_gains[:GAIN_ROWS, :]
     for layer in range(1, layers):
         sums = sums + held_gains[layer * GAIN_ROWS : (layer + 1) * GAIN_ROWS, :]
     tail = split_gains(sums)
     place = where_ref[0]
-    rows = high // PLANE
+    rows = own.shape[0] // PLANE
     for mask, out in enumerate(outs):
-        at = pl.multiple_of((place ^ mask) * rows, rows)
-        part = held[pl.ds(at, rows), :]
+        part = held[pl.ds(pl.multiple_of((place ^ mask) * rows, rows), rows), :]
         if mask:
             tall = out.shape[0] - tail.shape[0]
             out[:tall, :] = padded(part, tall).astype(bfloat16)
@@ -730,7 +667,7 @@
             out[rows:, :] = tail
 
 
-def plane_split_attn(where, own, received, gains):
+def split_attn(where, own, gains, received):
     rows, columns = own.shape[0] // PLANE, own.shape[1]
     tail = 2 * GAIN_ROWS
     shapes = [((rows + tail, columns), float32)]
@@ -739,9 +676,7 @@
         pltpu.VMEM(own.shape, float32),
         pltpu.VMEM(((len(received) + 1) * GAIN_ROWS, columns), float32),
     ]
-    return call(
-        plane_sum_attn_kernel, shapes, where, own, gains, *received, scalars=1, scratch=scratch
-    )
+    return call(split_attn_kernel, shapes, where, own, gains, *received, scalars=1, scratch=scratch)
 
 
 def pick_place(refs, place, target, columns, rows):
@@ -756,17 +691,8 @@
     rows = out_g.shape[0]
     big = out_g.shape[1] // LANES // PLANE * LANES
     last = PLANE * big
-    width = one.shape[1]
-    tall = max(rows, 16)
-    start = one.shape[0] - 2 * tall
     for mask, ref in enumerate((own, one, two, three)):
-        if mask:
-            top = ref[start : start + tall, :].astype(float32)[:rows]
-            rest = ref[start + tall :, : held.shape[2] - width].astype(float32)[:rows]
-            held[mask, :, :width] = top
-            held[mask, :, width:] = rest
-        else:
-            held[mask] = ref[...]
+        held[mask] = ref[...].astype(float32)
         at = pl.ds(pl.multiple_of((place ^ mask) * big, LANES), big)
         for number, out in enumerate((out_g, out_u, out_d)):
             out[:, at] = held[mask, :, number * big : (number + 1) * big]
@@ -951,27 +877,32 @@
     out_parts = plane_sent(out_parts)
     block_out = (hidden + add_up(out_parts)).astype(jnp.bfloat16)
 
-    send, keep, own_attn, part_gains, *attn_grads = after(
+    send, keep, attn_grad, part_gains = after(
         out_parts,
         attn_back(
-            where, ends, layers, tok_mine, tok_other, gains, tables, (h_mine, h_other), saved,
+            where, ends, tok_mine, tok_other, gains, tables, (h_mine, h_other), saved,
             attn_weight, gain_ffn[None, :],
         ),
     )
-    attn_grads = [send_deep(piece, step + 1) for step, piece in enumerate(attn_grads)]
-    own_dn, own_ff, *messages = tail_messages(where, keep, swap_cores(send), own_ff)
-    own_attn = after(messages, own_attn)
-    messages = [send_plane(part, mask + 1) for mask, part in enumerate(messages)]
-    attn_parts = plane_split_attn(where, own_attn, attn_grads, part_gains)
-    attn_parts = after(messages[:2], plane_sent(attn_parts))
-    d_normed = own_dn + add_up([part[:local_rows] for part in messages])
+    own_attn = lax.psum_scatter(
+        attn_grad, "dp", scatter_dimension=0, tiled=True, axis_index_groups=columns
+    )
+    ff_parts = plane_split(where, own_ff)
+    keep = after(ff_parts, keep)
+    ff_parts = plane_sent(ff_parts)
+    dn_parts = chip_sum(keep, swap_cores(send))
+    part_gains = after(dn_parts, part_gains)
+    dn_parts = plane_sent(after(ff_parts[1], dn_parts))
+    far_gains = [send_deep(part_gains, step) for step in range(1, layers)]
+    own_attn = after((dn_parts[1], block_out, far_gains), own_attn)
+    attn_parts = plane_sent(split_attn(where, own_attn, part_gains, far_gains))
+    d_normed = add_up(dn_parts)
     grad_tokens = d_hidden + norm_back(d_normed * attn_gain, unit_a, factor_a)
     grad_gate, grad_up, grad_down = call(
         place_ffn_kernel,
         [(w_gate.shape, float32)] * 3,
         where,
-        own_ff,
-        *messages,
+        *ff_parts,
         scalars=1,
         scratch=[pltpu.VMEM((PLANE, rows, ff_cols), float32)],
     )

time: 258 us -> 250 us (0.969)
  waiting for transfers between devices: 88.4 us -> 77.6 us
  starting transfers between devices: 47 us -> 51.8 us
  Pallas kernels: 84.3 us -> 81.7 us
    pallas_call x5 -> x1, Pallas kernels: 31.4 us -> 15.4 us  [attn_back(): pl.pallas_call(attn_back_kernel, grid=(PLANE // GROUPS_STEP,), in_specs=[...]
    pallas_call x7 -> x12, Pallas kernels: 14.9 us -> 28.6 us  [call(): pl.pallas_call(kernel, out_shape=[jax.ShapeDtypeStruct(shape, kind) for s...]
    ppermute x33 -> x36, waiting for transfers between devices: 64.2 us -> 53.2 us  [send_plane(): return lax.ppermute(values, 'dp', [(i, i ^ mask) for i in range(count)])]
    ppermute x6, waiting for transfers between devices: 14.4 us -> 9.26 us  [send_deep(): lax.ppermute(values, 'dp', [(i, (i + PLANE * step) % count) for i in rang...]
    reduce_scatter x0 -> x1, waiting for transfers between devices: none -> 3.83 us  [body(): lax.psum_scatter(attn_grad, 'dp', scatter_dimension=0, tiled=True, axis_i...]
    ppermute x33 -> x36, starting transfers between devices: 37.9 us -> 41.3 us  [send_plane(): return lax.ppermute(values, 'dp', [(i, i ^ mask) for i in range(count)])]
    unnamed x87 -> x97, local copies, waits for them, and re-layouts: 8.8 us -> 9.48 us
  transfers between devices with their start and end apart: 50 -> 54, of which waited for: 21 -> 24; matrix products, arithmetic and copies ran while one was open for 5% -> 5% of each run, Pallas kernels for 24% -> 24%
where the time goes in v12:
time: 250 us; the launch traced here: 249 us
  Pallas kernels  81.7 us (33%)
  waiting for transfers between devices  77.6 us (31%)
  starting transfers between devices  51.8 us (21%)
  between operations  14.3 us (6%)
  local copies, waits for them, and re-layouts  12.7 us (5%)
  other arithmetic  11.2 us (4%)
    ppermute x36, waiting for transfers between devices, send_plane(): return lax.ppermute(values, 'dp', [(i, i ^ mask) for i in range(count)])  53.2 us
    ppermute x36, starting transfers between devices, send_plane(): return lax.ppermute(values, 'dp', [(i, i ^ mask) for i in range(count)])  41.3 us
    pallas_call x12, Pallas kernels, call(): pl.pallas_call(kernel, out_shape=[jax.ShapeDtypeStruct(shape, kind) for s...  28.6 us
    pallas_call x1, Pallas kernels, ffn_layer(): pl.pallas_call(ffn_kernel, grid=(2,), in_specs=[scalar, scalar] + [row_sp...  15.5 us
    pallas_call x1, Pallas kernels, attn_back(): pl.pallas_call(attn_back_kernel, grid=(PLANE // GROUPS_STEP,), in_specs=[...  15.4 us
    pallas_call x2, Pallas kernels, ffn_apply(): pl.pallas_call(lambda *refs: ffn_apply_kernel(first, *refs), grid=(2,), i...  12 us
    pallas_call x1, Pallas kernels, attn(): pl.pallas_call(lambda *refs: attn_kernel(layers, *refs), grid=(PLANE // G...  10.2 us
    ppermute x6, starting transfers between devices, send_deep(): lax.ppermute(values, 'dp', [(i, (i + PLANE * step) % count) for i in rang...  9.49 us
  transfers between devices with their start and end apart: 54, of which 24 were waited for; matrix products, arithmetic and copies ran while one was open for 5% of the time, Pallas kernels for 24%

profile of v12, /device:TPU:0, one launch (start us, length us, event | category | flops | bytes accessed | tf_op | source)
XLA Modules:
  0.0 249.3 jit_solution(1766901618129267044)
XLA Ops:
  7.9 1.7 shard_map.238
  9.6 2.9 %collective-permute-start = (bf16[32,1024]{1,0:T(8,128)(2,1)}, bf16[32,1024]{1,0:T(8,128)(2,1)S(1)}, u32[]{:S(2)}, u32[]{:S(2)}) collective-permute-start(bf16[32,1024]{1,0:T(8,128)(2,1)} %get-tuple-element.116), channel_id=1, source_target_pairs={{0,2},{2,0},{4,6},{6,4},{8,10},{10,8},{12,14},{14,12},{16,18},{18,... | collective-permute-start | bytes 196616 | tf_op jit(solution)/shard_map/ppermute | solution.py:100
  12.5 1.5 collective-permute-start.1
  14.1 2.2 shard_map.237
  17.0 2.4 collective-permute-done.2.three
  20.1 1.7 shard_map.239
  21.8 3.6 %collective-permute-start.5 = (bf16[256,384]{1,0:T(8,128)(2,1)}, bf16[256,384]{1,0:T(8,128)(2,1)S(1)}, u32[]{:S(2)}, u32[]{:S(2)}) collective-permute-start(bf16[256,384]{1,0:T(8,128)(2,1)} %get-tuple-element.134.refs_9_), channel_id=1, source_target_pairs={{0,24},{2,26},{4,28},{6,30},{8,0},{10,2},{12,4},{14,6},{16,8},{18,... | collective-permute-start | bytes 589832 | tf_op jit(solution)/shard_map/ppermute | solution.py:105
  28.5 2.6 %collective-permute-done.5.refs_12_ = bf16[256,384]{1,0:T(8,128)(2,1)S(1)} collective-permute-done((bf16[256,384]{1,0:T(8,128)(2,1)}, bf16[256,384]{1,0:T(8,128)(2,1)S(1)}, u32[]{:S(2)}, u32[]{:S(2)}) %collective-permute-start.5) | collective-permute-done | bytes 196640 | tf_op jit(solution)/shard_map/ppermute | solution.py:105
  31.6 3.0 %fusion.6 = (f32[1024,128]{1,0:T(8,128)}, f32[1024,128]{1,0:T(8,128)}) fusion(f32[128]{0:T(128)S(1)} %get-tuple-element.223, f32[128]{0:T(128)S(1)} %get-tuple-element.224, f32[1024]{0:T(1024)S(1)} %bitcast.28), kind=kLoop, calls=%fused_computation.13 | loop fusion | flops 262144 | bytes 1053696 | tf_op jit(solution)/shard_map/mul | solution.py:754
  34.6 6.7 %collective-permute-done.4.refs_11_ = bf16[256,384]{1,0:T(8,128)(2,1)S(1)} collective-permute-done((bf16[256,384]{1,0:T(8,128)(2,1)}, bf16[256,384]{1,0:T(8,128)(2,1)S(1)}, u32[]{:S(2)}, u32[]{:S(2)}) %collective-permute-start.4) | collective-permute-done | bytes 196640 | tf_op jit(solution)/shard_map/ppermute | solution.py:105
  42.2 2.5 shard_map.240
  46.0 2.4 collective-permute-start.11
  48.5 5.7 %collective-permute-done.9 = bf16[128,1024]{1,0:T(8,128)(2,1)S(1)} collective-permute-done((bf16[128,1024]{1,0:T(8,128)(2,1)S(1)}, bf16[128,1024]{1,0:T(8,128)(2,1)S(1)}, u32[]{:S(2)}, u32[]{:S(2)}) %collective-permute-start.9) | collective-permute-done | bytes 262176 | tf_op jit(solution)/shard_map/ppermute | solution.py:100
  54.3 3.5 %collective-permute-done.10 = bf16[128,1024]{1,0:T(8,128)(2,1)S(1)} collective-permute-done((bf16[128,1024]{1,0:T(8,128)(2,1)S(1)}, bf16[128,1024]{1,0:T(8,128)(2,1)S(1)}, u32[]{:S(2)}, u32[]{:S(2)}) %collective-permute-start.10) | collective-permute-done | bytes 262176 | tf_op jit(solution)/shard_map/ppermute | solution.py:100
  58.0 1.2 collective-permute-start.15
  59.2 1.4 collective-permute-start.14
  63.1 10.2 %shard_map.241 = (bf16[512,1024]{1,0:T(8,128)(2,1)}, f32[512,1024]{1,0:T(8,128)}, f32[1024,256]{1,0:T(8,128)}, bf16[1024,256]{1,0:T(8,128)(2,1)}, bf16[1024,128]{1,0:T(8,128)(2,1)}, /*index=5*/bf16[1024,384]{1,0:T(8,128)(2,1)}) custom-call(s32[3]{0:T(128)} %pad_add_fusion.where_ref.refs_0_, s32[4,4]{1,0:T(4,128)} %copy-done.35, bf16[512,1024]{1,0:T(8,128)(2,1)} %copy-done, ...), custom_call_target="tpu_custom_call" | custom-call | flops 1024 | bytes 36000000 | tf_op jit(solution)/shard_map/pallas_call | solution.py:425
  74.8 2.9 %collective-permute-done.16.received = bf16[512,1024]{1,0:T(8,128)(2,1)S(1)} collective-permute-done((bf16[512,1024]{1,0:T(8,128)(2,1)}, bf16[512,1024]{1,0:T(8,128)(2,1)S(1)}, u32[]{:S(2)}, u32[]{:S(2)}) %collective-permute-start.16) | collective-permute-done | bytes 1048608 | tf_op jit(solution)/shard_map/ppermute | solution.py:109
  78.7 3.0 %shard_map.242 = (f32[128,1024]{1,0:T(8,128)}, bf16[128,1024]{1,0:T(8,128)(2,1)}, bf16[128,1024]{1,0:T(8,128)(2,1)}, bf16[128,1024]{1,0:T(8,128)(2,1)}) custom-call(f32[512,1024]{1,0:T(8,128)} %get-tuple-element.138.keep, bf16[512,1024]{1,0:T(8,128)(2,1)} %copy-done.10), custom_call_target="tpu_custom_call" | custom-call | flops 1024 | bytes 1024 | tf_op jit(solution)/shard_map/pallas_call | solution.py:115
  83.4 1.8 collective-permute-start.19
  85.2 5.9 %collective-permute-done.17 = bf16[128,1024]{1,0:T(8,128)(2,1)S(1)} collective-permute-done((bf16[128,1024]{1,0:T(8,128)(2,1)}, bf16[128,1024]{1,0:T(8,128)(2,1)S(1)}, u32[]{:S(2)}, u32[]{:S(2)}) %collective-permute-start.17) | collective-permute-done | bytes 262176 | tf_op jit(solution)/shard_map/ppermute | solution.py:100
  91.1 5.6 %collective-permute-done.18 = bf16[128,1024]{1,0:T(8,128)(2,1)S(1)} collective-permute-done((bf16[128,1024]{1,0:T(8,128)(2,1)}, bf16[128,1024]{1,0:T(8,128)(2,1)S(1)}, u32[]{:S(2)}, u32[]{:S(2)}) %collective-permute-start.18) | collective-permute-done | bytes 262176 | tf_op jit(solution)/shard_map/ppermute | solution.py:100
  96.7 1.3 multiply_reduce_fusion.2
  98.2 1.2 collective-permute-start.22
  99.4 1.2 collective-permute-start.21
  101.9 6.5 %collective-permute-done.22 = bf16[128,1024]{1,0:T(8,128)(2,1)S(1)} collective-permute-done((bf16[128,1024]{1,0:T(8,128)(2,1)S(1)}, bf16[128,1024]{1,0:T(8,128)(2,1)S(1)}, u32[]{:S(2)}, u32[]{:S(2)}) %collective-permute-start.22) | collective-permute-done | bytes 262176 | tf_op jit(solution)/shard_map/ppermute | solution.py:100
  108.4 3.4 %collective-permute-done.21 = bf16[128,1024]{1,0:T(8,128)(2,1)S(1)} collective-permute-done((bf16[128,1024]{1,0:T(8,128)(2,1)S(1)}, bf16[128,1024]{1,0:T(8,128)(2,1)S(1)}, u32[]{:S(2)}, u32[]{:S(2)}) %collective-permute-start.21) | collective-permute-done | bytes 262176 | tf_op jit(solution)/shard_map/ppermute | solution.py:100
  112.0 1.2 copy-done.7
  113.2 1.5 collective-permute-done.23.x_o
  114.7 3.1 %all-gather.2.cloned.1.call-done.weight.refs_1_ = bf16[1024,1792]{1,0:T(8,128)(2,1)} async-done(((bf16[256,1792]{1,0:T(8,128)(2,1)}), bf16[1024,1792]{1,0:T(8,128)(2,1)}) %all-gather.2.cloned.1.call-update) | async-done | bytes 3670032 | tf_op jit(solution)/shard_map/all_gather | solution.py:832
  117.8 15.5 %shard_map.243 = (bf16[1024,640]{1,0:T(8,128)(2,1)}, bf16[1024,1152]{1,0:T(8,128)(2,1)}, bf16[1024,1792]{1,0:T(8,128)(2,1)}) custom-call(s32[3]{0:T(128)} %pad_add_fusion.where_ref.refs_0_, s32[4,4]{1,0:T(4,128)} %copy-done.35, bf16[512,1024]{1,0:T(8,128)(2,1)} %collective-permute-done.23.x_o, bf16[512,1024]{1,0:T(8,128)(2,1)} %copy-done.3, ...), custom_call_target="tpu_custom_call" | custom-call | flops 1024 | bytes 48000000 | tf_op jit(solution)/shard_map/pallas_call | solution.py:543
  133.6 6.6 %shard_map.244 = (bf16[512,1024]{1,0:T(8,128)(2,1)}, f32[512,1024]{1,0:T(8,128)}) custom-call(bf16[1024,1152]{1,0:T(8,128)(2,1)} %get-tuple-element.146.refs_0_, bf16[1024,1792]{1,0:T(8,128)(2,1)} %all-gather.2.cloned.1.call-done.weight.refs_1_), custom_call_target="tpu_custom_call" | custom-call | flops 1024 | bytes 14000000 | tf_op jit(solution)/shard_map/pallas_call | solution.py:571
  140.2 2.9 %collective-permute-done.25.received = bf16[512,1024]{1,0:T(8,128)(2,1)S(1)} collective-permute-done((bf16[512,1024]{1,0:T(8,128)(2,1)}, bf16[512,1024]{1,0:T(8,128)(2,1)S(1)}, u32[]{:S(2)}, u32[]{:S(2)}) %collective-permute-start.25) | collective-permute-done | bytes 1048608 | tf_op jit(solution)/shard_map/ppermute | solution.py:109
  144.1 2.9 %shard_map.246 = (f32[128,1024]{1,0:T(8,128)}, bf16[128,1024]{1,0:T(8,128)(2,1)}, bf16[128,1024]{1,0:T(8,128)(2,1)}, bf16[128,1024]{1,0:T(8,128)(2,1)}) custom-call(f32[512,1024]{1,0:T(8,128)} %get-tuple-element.151.keep, bf16[512,1024]{1,0:T(8,128)(2,1)} %copy-done.9), custom_call_target="tpu_custom_call" | custom-call | flops 1024 | bytes 1024 | tf_op jit(solution)/shard_map/pallas_call | solution.py:115
  147.1 1.5 collective-permute-start.26
  148.6 1.5 collective-permute-start.27
  150.5 1.3 slice.19
  152.5 5.4 %shard_map.245 = (bf16[512,1024]{1,0:T(8,128)(2,1)}, f32[512,1024]{1,0:T(8,128)}) custom-call(bf16[1024,640]{1,0:T(8,128)(2,1)} %get-tuple-element.149.refs_0_, bf16[1024,1792]{1,0:T(8,128)(2,1)} %all-gather.2.cloned.1.call-done.weight.refs_1_), custom_call_target="tpu_custom_call" | custom-call | flops 1024 | bytes 14000000 | tf_op jit(solution)/shard_map/pallas_call | solution.py:571
  157.8 4.6 %collective-permute-done.27 = bf16[128,1024]{1,0:T(8,128)(2,1)S(1)} collective-permute-done((bf16[128,1024]{1,0:T(8,128)(2,1)}, bf16[128,1024]{1,0:T(8,128)(2,1)S(1)}, u32[]{:S(2)}, u32[]{:S(2)}) %collective-permute-start.27) | collective-permute-done | bytes 262176 | tf_op jit(solution)/shard_map/ppermute | solution.py:100
  163.5 1.5 collective-permute-start.31
  165.0 1.2 collective-permute-start.30
  167.1 6.7 %collective-permute-done.31 = bf16[128,1024]{1,0:T(8,128)(2,1)S(1)} collective-permute-done((bf16[128,1024]{1,0:T(8,128)(2,1)S(1)}, bf16[128,1024]{1,0:T(8,128)(2,1)S(1)}, u32[]{:S(2)}, u32[]{:S(2)}) %collective-permute-start.31) | collective-permute-done | bytes 262176 | tf_op jit(solution)/shard_map/ppermute | solution.py:100
  173.7 3.6 %collective-permute-done.30 = bf16[128,1024]{1,0:T(8,128)(2,1)S(1)} collective-permute-done((bf16[128,1024]{1,0:T(8,128)(2,1)S(1)}, bf16[128,1024]{1,0:T(8,128)(2,1)S(1)}, u32[]{:S(2)}, u32[]{:S(2)}) %collective-permute-start.30) | collective-permute-done | bytes 262176 | tf_op jit(solution)/shard_map/ppermute | solution.py:100
  177.6 3.3 %shard_map.247 = (f32[128,1024]{1,0:T(8,128)}, bf16[128,1024]{1,0:T(8,128)(2,1)}, bf16[128,1024]{1,0:T(8,128)(2,1)}, bf16[128,1024]{1,0:T(8,128)(2,1)}) custom-call(f32[512,1024]{1,0:T(8,128)} %get-tuple-element.160.keep, bf16[512,1024]{1,0:T(8,128)(2,1)} %collective-permute-done.33.received), custom_call_target="tpu_custom_call" | custom-call | flops 1024 | bytes 1024 | tf_op jit(solution)/shard_map/pallas_call | solution.py:115
  180.9 1.4 collective-permute-start.34
  182.8 1.6 collective-permute-start.36
  184.4 15.4 %shard_map.249 = (bf16[512,1024]{1,0:T(8,128)(2,1)}, f32[512,1024]{1,0:T(8,128)}, bf16[1024,384]{1,0:T(8,128)(2,1)}, f32[8,384]{1,0:T(8,128)}) custom-call(s32[3]{0:T(128)} %pad_add_fusion.where_ref.refs_0_, s32[4,4]{1,0:T(4,128)} %copy-done.35, bf16[512,1024]{1,0:T(8,128)(2,1)} %copy-done, bf16[512,1024]{1,0:T(8,128)(2,1)} %copy-done.1, ...), custom_call_target="tpu_custom_call" | custom-call | flops 1024 | bytes 24000000 | tf_op jit(solution)/shard_map/pallas_call | solution.py:451
  200.5 2.3 shard_map.248
  202.8 1.5 collective-permute-start.37
  204.2 1.5 collective-permute-start.49
  207.3 3.0 %shard_map.250 = (f32[128,1024]{1,0:T(8,128)}, bf16[128,1024]{1,0:T(8,128)(2,1)}, bf16[128,1024]{1,0:T(8,128)(2,1)}, bf16[128,1024]{1,0:T(8,128)(2,1)}) custom-call(f32[512,1024]{1,0:T(8,128)} %get-tuple-element.183.keep, bf16[512,1024]{1,0:T(8,128)(2,1)} %copy-done.8), custom_call_target="tpu_custom_call" | custom-call | flops 1024 | bytes 1024 | tf_op jit(solution)/shard_map/pallas_call | solution.py:115
  210.2 2.5 collective-permute-start.44
  213.2 1.9 collective-permute-start.42
  215.1 1.5 collective-permute-start.39
  216.6 1.5 collective-permute-start.40
  218.6 2.0 add_convert_fusion
  220.6 2.7 %shard_map.253 = (f32[64,2304]{1,0:T(8,128)}, f32[64,2304]{1,0:T(8,128)}, f32[64,2304]{1,0:T(8,128)}) custom-call(s32[3]{0:T(128)} %pad_add_fusion.where_ref.refs_0_, bf16[64,1792]{1,0:T(8,128)(2,1)} %get-tuple-element.171.own, bf16[64,1792]{1,0:T(8,128)(2,1)} %copy-done.20, bf16[64,1792]{1,0:T(8,128)(2,1)} %copy-done.21, ...), custom_call_target="tpu_custom_call" | custom-call | flops 1024 | bytes 1024 | tf_op jit(solution)/shard_map/pallas_call | solution.py:115
  223.4 3.8 %reduce-scatter.5.cloned.1.call-done.own = bf16[256,384]{1,0:T(8,128)(2,1)} async-done(((bf16[1024,384]{1,0:T(8,128)(2,1)}), bf16[256,384]{1,0:T(8,128)(2,1)}) %reduce-scatter.5.cloned.1.call-update) | async-done | bytes 196624 | tf_op jit(solution)/shard_map/reduce_scatter | solution.py:887
  227.8 1.7 shard_map.251
  229.6 1.4 collective-permute-start.45
  231.0 1.5 collective-permute-start.46
  234.2 1.9 collective-permute-done.46.two
  236.1 1.7 collective-permute-done.47.three
  238.4 1.7 shard_map.252
  (190 shorter events, 30.2 us)
Async XLA Ops:
  7.2 110.7 %all-gather.2.cloned.1.call-start = ((), (), s32[]{:S(2)}) async-start(), calls=%async_computation.2 | async-start | bytes 4587520 | tf_op jit(solution)/shard_map/all_gather | solution.py:832
  9.6 6.7 %collective-permute-start = (bf16[32,1024]{1,0:T(8,128)(2,1)}, bf16[32,1024]{1,0:T(8,128)(2,1)S(1)}, u32[]{:S(2)}, u32[]{:S(2)}) collective-permute-start(bf16[32,1024]{1,0:T(8,128)(2,1)} %get-tuple-element.116), channel_id=1, source_target_pairs={{0,2},{2,0},{4,6},{6,4},{8,10},{10,8},{12,14},{14,12},{16,18},{18,... | collective-permute-start | bytes 196616 | tf_op jit(solution)/shard_map/ppermute | solution.py:100
  12.5 4.5 %collective-permute-start.1 = (bf16[32,1024]{1,0:T(8,128)(2,1)}, bf16[32,1024]{1,0:T(8,128)(2,1)S(1)}, u32[]{:S(2)}, u32[]{:S(2)}) collective-permute-start(bf16[32,1024]{1,0:T(8,128)(2,1)} %get-tuple-element.117), channel_id=1, source_target_pairs={{0,4},{2,6},{4,0},{6,2},{8,12},{10,14},{12,8},{14,10},{16,20},{18,... | collective-permute-start | bytes 196616 | tf_op jit(solution)/shard_map/ppermute | solution.py:100
  14.1 5.4 %collective-permute-start.2 = (bf16[32,1024]{1,0:T(8,128)(2,1)}, bf16[32,1024]{1,0:T(8,128)(2,1)S(1)}, u32[]{:S(2)}, u32[]{:S(2)}) collective-permute-start(bf16[32,1024]{1,0:T(8,128)(2,1)} %get-tuple-element.118), channel_id=1, source_target_pairs={{0,6},{2,4},{4,2},{6,0},{8,14},{10,12},{12,10},{14,8},{16,22},{18,... | collective-permute-start | bytes 196616 | tf_op jit(solution)/shard_map/ppermute | solution.py:100
  16.2 28.7 %copy-start.4 = (bf16[128,1024]{1,0:T(8,128)(2,1)S(1)}, bf16[128,1024]{1,0:T(8,128)(2,1)}, u32[]{:S(2)}) copy-start(bf16[128,1024]{1,0:T(8,128)(2,1)} %param.14) | copy-start | bytes 786436
  21.8 9.3 %collective-permute-start.5 = (bf16[256,384]{1,0:T(8,128)(2,1)}, bf16[256,384]{1,0:T(8,128)(2,1)S(1)}, u32[]{:S(2)}, u32[]{:S(2)}) collective-permute-start(bf16[256,384]{1,0:T(8,128)(2,1)} %get-tuple-element.134.refs_9_), channel_id=1, source_target_pairs={{0,24},{2,26},{4,28},{6,30},{8,0},{10,2},{12,4},{14,6},{16,8},{18,... | collective-permute-start | bytes 589832 | tf_op jit(solution)/shard_map/ppermute | solution.py:105
  25.4 15.9 %collective-permute-start.4 = (bf16[256,384]{1,0:T(8,128)(2,1)}, bf16[256,384]{1,0:T(8,128)(2,1)S(1)}, u32[]{:S(2)}, u32[]{:S(2)}) collective-permute-start(bf16[256,384]{1,0:T(8,128)(2,1)} %get-tuple-element.134.refs_9_), channel_id=1, source_target_pairs={{0,16},{2,18},{4,20},{6,22},{8,24},{10,26},{12,28},{14,30},{16,0},... | collective-permute-start | bytes 589832 | tf_op jit(solution)/shard_map/ppermute | solution.py:105
  25.4 15.9 %collective-permute-start.3 = (bf16[256,384]{1,0:T(8,128)(2,1)}, bf16[256,384]{1,0:T(8,128)(2,1)S(1)}, u32[]{:S(2)}, u32[]{:S(2)}) collective-permute-start(bf16[256,384]{1,0:T(8,128)(2,1)} %get-tuple-element.134.refs_9_), channel_id=1, source_target_pairs={{0,8},{2,10},{4,12},{6,14},{8,16},{10,18},{12,20},{14,22},{16,24},... | collective-permute-start | bytes 589832 | tf_op jit(solution)/shard_map/ppermute | solution.py:105
  27.3 21.2 %copy-start.35 = (s32[4,4]{1,0:T(4,128)}, s32[4,4]{1,0:T(4,128)S(1)}, u32[]{:S(2)}) copy-start(s32[4,4]{1,0:T(4,128)S(1)} %reduce_window_sum.11.refs_1_.ends_ref) | copy-start | bytes 196
  27.4 13.9 %collective-permute-start.6 = (bf16[64,1792]{1,0:T(8,128)(2,1)}, bf16[64,1792]{1,0:T(8,128)(2,1)S(1)}, u32[]{:S(2)}, u32[]{:S(2)}) collective-permute-start(bf16[64,1792]{1,0:T(8,128)(2,1)} %get-tuple-element.126), channel_id=1, source_target_pairs={{0,2},{2,0},{4,6},{6,4},{8,10},{10,8},{12,14},{14,12},{16,18},{18,... | collective-permute-start | bytes 688136 | tf_op jit(solution)/shard_map/ppermute | solution.py:100
  28.0 13.3 %collective-permute-start.7 = (bf16[64,1792]{1,0:T(8,128)(2,1)}, bf16[64,1792]{1,0:T(8,128)(2,1)S(1)}, u32[]{:S(2)}, u32[]{:S(2)}) collective-permute-start(bf16[64,1792]{1,0:T(8,128)(2,1)} %get-tuple-element.127), channel_id=1, source_target_pairs={{0,4},{2,6},{4,0},{6,2},{8,12},{10,14},{12,8},{14,10},{16,20},{18,... | collective-permute-start | bytes 688136 | tf_op jit(solution)/shard_map/ppermute | solution.py:100
  31.1 10.3 %collective-permute-start.8 = (bf16[64,1792]{1,0:T(8,128)(2,1)}, bf16[64,1792]{1,0:T(8,128)(2,1)S(1)}, u32[]{:S(2)}, u32[]{:S(2)}) collective-permute-start(bf16[64,1792]{1,0:T(8,128)(2,1)} %get-tuple-element.128), channel_id=1, source_target_pairs={{0,6},{2,4},{4,2},{6,0},{8,14},{10,12},{12,10},{14,8},{16,22},{18,... | collective-permute-start | bytes 688136 | tf_op jit(solution)/shard_map/ppermute | solution.py:100
  41.3 20.8 %copy-start.26 = (bf16[256,384]{1,0:T(8,128)(2,1)}, bf16[256,384]{1,0:T(8,128)(2,1)S(1)}, u32[]{:S(2)}) copy-start(bf16[256,384]{1,0:T(8,128)(2,1)S(1)} %collective-permute-done.4.refs_11_) | copy-start | bytes 589828
  42.2 19.3 %copy-start.42 = (f32[64]{0:T(128)S(1)}, f32[64]{0:T(128)}, u32[]{:S(2)}) copy-start(f32[64]{0:T(128)} %param.17) | copy-start | bytes 772
  42.2 19.3 %copy-start.43 = (f32[64]{0:T(128)S(1)}, f32[64]{0:T(128)}, u32[]{:S(2)}) copy-start(f32[64]{0:T(128)} %param.18) | copy-start | bytes 772
  44.7 155.8 %reduce-scatter.3.cloned.1.call-start = ((), (), s32[]{:S(2)}) async-start(), calls=%async_computation.3 | async-start | bytes 4587520 | tf_op jit(solution)/shard_map/reduce_scatter | solution.py:860
  44.9 9.3 %collective-permute-start.9 = (bf16[128,1024]{1,0:T(8,128)(2,1)S(1)}, bf16[128,1024]{1,0:T(8,128)(2,1)S(1)}, u32[]{:S(2)}, u32[]{:S(2)}) collective-permute-start(bf16[128,1024]{1,0:T(8,128)(2,1)S(1)} %copy-done.4), channel_id=1, source_target_pairs={{0,2},{2,0},{4,6},{6,4},{8,10},{10,8},{12,14},{14,12},{16,18},{18,... | collective-permute-start | bytes 786440 | tf_op jit(solution)/shard_map/ppermute | solution.py:100
  45.5 12.3 %collective-permute-start.10 = (bf16[128,1024]{1,0:T(8,128)(2,1)S(1)}, bf16[128,1024]{1,0:T(8,128)(2,1)S(1)}, u32[]{:S(2)}, u32[]{:S(2)}) collective-permute-start(bf16[128,1024]{1,0:T(8,128)(2,1)S(1)} %copy-done.4), channel_id=1, source_target_pairs={{0,4},{2,6},{4,0},{6,2},{8,12},{10,14},{12,8},{14,10},{16,20},{18,... | collective-permute-start | bytes 786440 | tf_op jit(solution)/shard_map/ppermute | solution.py:100
  46.0 11.8 %collective-permute-start.11 = (bf16[128,1024]{1,0:T(8,128)(2,1)S(1)}, bf16[128,1024]{1,0:T(8,128)(2,1)S(1)}, u32[]{:S(2)}, u32[]{:S(2)}) collective-permute-start(bf16[128,1024]{1,0:T(8,128)(2,1)S(1)} %copy-done.4), channel_id=1, source_target_pairs={{0,6},{2,4},{4,2},{6,0},{8,14},{10,12},{12,10},{14,8},{16,22},{18,... | collective-permute-start | bytes 786440 | tf_op jit(solution)/shard_map/ppermute | solution.py:100
  57.9 4.2 %collective-permute-start.12 = (bf16[512,1024]{1,0:T(8,128)(2,1)S(1)}, bf16[512,1024]{1,0:T(8,128)(2,1)S(1)}, u32[]{:S(2)}, u32[]{:S(2)}) collective-permute-start(bf16[512,1024]{1,0:T(8,128)(2,1)S(1)} %constant_dynamic-update-slice_fusion.refs_2_.tok_m), channel_id=1, source_target_pairs={{0,1},{1,0},{2,3},{3,2},{4,5},{5,4},{6,7},{7,6},{8,9},{9,8},{10,11... | collective-permute-start | bytes 3145736 | tf_op jit(solution)/shard_map/ppermute | solution.py:109
  58.0 15.4 %collective-permute-start.15 = (bf16[128,1024]{1,0:T(8,128)(2,1)S(1)}, bf16[128,1024]{1,0:T(8,128)(2,1)S(1)}, u32[]{:S(2)}, u32[]{:S(2)}) collective-permute-start(bf16[128,1024]{1,0:T(8,128)(2,1)S(1)} %copy-done.11), channel_id=1, source_target_pairs={{0,6},{2,4},{4,2},{6,0},{8,14},{10,12},{12,10},{14,8},{16,22},{18,... | collective-permute-start | bytes 786440 | tf_op jit(solution)/shard_map/ppermute | solution.py:100
  59.2 14.2 %collective-permute-start.14 = (bf16[128,1024]{1,0:T(8,128)(2,1)S(1)}, bf16[128,1024]{1,0:T(8,128)(2,1)S(1)}, u32[]{:S(2)}, u32[]{:S(2)}) collective-permute-start(bf16[128,1024]{1,0:T(8,128)(2,1)S(1)} %copy-done.11), channel_id=1, source_target_pairs={{0,4},{2,6},{4,0},{6,2},{8,12},{10,14},{12,8},{14,10},{16,20},{18,... | collective-permute-start | bytes 786440 | tf_op jit(solution)/shard_map/ppermute | solution.py:100
  60.6 12.8 %collective-permute-start.13 = (bf16[128,1024]{1,0:T(8,128)(2,1)S(1)}, bf16[128,1024]{1,0:T(8,128)(2,1)S(1)}, u32[]{:S(2)}, u32[]{:S(2)}) collective-permute-start(bf16[128,1024]{1,0:T(8,128)(2,1)S(1)} %copy-done.11), channel_id=1, source_target_pairs={{0,2},{2,0},{4,6},{6,4},{8,10},{10,8},{12,14},{14,12},{16,18},{18,... | collective-permute-start | bytes 786440 | tf_op jit(solution)/shard_map/ppermute | solution.py:100
  74.8 2.9 %collective-permute-start.16 = (bf16[512,1024]{1,0:T(8,128)(2,1)}, bf16[512,1024]{1,0:T(8,128)(2,1)S(1)}, u32[]{:S(2)}, u32[]{:S(2)}) collective-permute-start(bf16[512,1024]{1,0:T(8,128)(2,1)} %get-tuple-element.141), channel_id=1, source_target_pairs={{0,1},{1,0},{2,3},{3,2},{4,5},{5,4},{6,7},{7,6},{8,9},{9,8},{10,11... | collective-permute-start | bytes 3145736 | tf_op jit(solution)/shard_map/ppermute | solution.py:109
  81.6 20.1 %copy-start.17 = (bf16[128,1024]{1,0:T(8,128)(2,1)S(1)}, bf16[128,1024]{1,0:T(8,128)(2,1)}, u32[]{:S(2)}) copy-start(bf16[128,1024]{1,0:T(8,128)(2,1)} %copy-done.16) | copy-start | bytes 786436
  81.7 20.1 %copy-start.15 = (bf16[128,1024]{1,0:T(8,128)(2,1)S(1)}, bf16[128,1024]{1,0:T(8,128)(2,1)}, u32[]{:S(2)}) copy-start(bf16[128,1024]{1,0:T(8,128)(2,1)} %copy-done.14) | copy-start | bytes 786436
  81.7 9.4 %collective-permute-start.17 = (bf16[128,1024]{1,0:T(8,128)(2,1)}, bf16[128,1024]{1,0:T(8,128)(2,1)S(1)}, u32[]{:S(2)}, u32[]{:S(2)}) collective-permute-start(bf16[128,1024]{1,0:T(8,128)(2,1)} %get-tuple-element.143), channel_id=1, source_target_pairs={{0,2},{2,0},{4,6},{6,4},{8,10},{10,8},{12,14},{14,12},{16,18},{18,... | collective-permute-start | bytes 786440 | tf_op jit(solution)/shard_map/ppermute | solution.py:100
  82.8 13.9 %collective-permute-start.18 = (bf16[128,1024]{1,0:T(8,128)(2,1)}, bf16[128,1024]{1,0:T(8,128)(2,1)S(1)}, u32[]{:S(2)}, u32[]{:S(2)}) collective-permute-start(bf16[128,1024]{1,0:T(8,128)(2,1)} %get-tuple-element.144), channel_id=1, source_target_pairs={{0,4},{2,6},{4,0},{6,2},{8,12},{10,14},{12,8},{14,10},{16,20},{18,... | collective-permute-start | bytes 786440 | tf_op jit(solution)/shard_map/ppermute | solution.py:100
  83.4 13.3 %collective-permute-start.19 = (bf16[128,1024]{1,0:T(8,128)(2,1)}, bf16[128,1024]{1,0:T(8,128)(2,1)S(1)}, u32[]{:S(2)}, u32[]{:S(2)}) collective-permute-start(bf16[128,1024]{1,0:T(8,128)(2,1)} %get-tuple-element.145), channel_id=1, source_target_pairs={{0,6},{2,4},{4,2},{6,0},{8,14},{10,12},{12,10},{14,8},{16,22},{18,... | collective-permute-start | bytes 786440 | tf_op jit(solution)/shard_map/ppermute | solution.py:100
  98.2 10.2 %collective-permute-start.22 = (bf16[128,1024]{1,0:T(8,128)(2,1)S(1)}, bf16[128,1024]{1,0:T(8,128)(2,1)S(1)}, u32[]{:S(2)}, u32[]{:S(2)}) collective-permute-start(bf16[128,1024]{1,0:T(8,128)(2,1)S(1)} %multiply_convert_fusion), channel_id=1, source_target_pairs={{0,6},{2,4},{4,2},{6,0},{8,14},{10,12},{12,10},{14,8},{16,22},{18,... | collective-permute-start | bytes 786440 | tf_op jit(solution)/shard_map/ppermute | solution.py:100
  99.4 12.4 %collective-permute-start.21 = (bf16[128,1024]{1,0:T(8,128)(2,1)S(1)}, bf16[128,1024]{1,0:T(8,128)(2,1)S(1)}, u32[]{:S(2)}, u32[]{:S(2)}) collective-permute-start(bf16[128,1024]{1,0:T(8,128)(2,1)S(1)} %multiply_convert_fusion), channel_id=1, source_target_pairs={{0,4},{2,6},{4,0},{6,2},{8,12},{10,14},{12,8},{14,10},{16,20},{18,... | collective-permute-start | bytes 786440 | tf_op jit(solution)/shard_map/ppermute | solution.py:100
  100.6 11.1 %collective-permute-start.20 = (bf16[128,1024]{1,0:T(8,128)(2,1)S(1)}, bf16[128,1024]{1,0:T(8,128)(2,1)S(1)}, u32[]{:S(2)}, u32[]{:S(2)}) collective-permute-start(bf16[128,1024]{1,0:T(8,128)(2,1)S(1)} %multiply_convert_fusion), channel_id=1, source_target_pairs={{0,2},{2,0},{4,6},{6,4},{8,10},{10,8},{12,14},{14,12},{16,18},{18,... | collective-permute-start | bytes 786440 | tf_op jit(solution)/shard_map/ppermute | solution.py:100
  101.8 10.2 %collective-permute-start.24 = (bf16[512,1024]{1,0:T(8,128)(2,1)S(1)}, bf16[512,1024]{1,0:T(8,128)(2,1)S(1)}, u32[]{:S(2)}, u32[]{:S(2)}) collective-permute-start(bf16[512,1024]{1,0:T(8,128)(2,1)S(1)} %constant_dynamic-update-slice_fusion.4.g_m), channel_id=1, source_target_pairs={{0,1},{1,0},{2,3},{3,2},{4,5},{5,4},{6,7},{7,6},{8,9},{9,8},{10,11... | collective-permute-start | bytes 3145736 | tf_op jit(solution)/shard_map/ppermute | solution.py:109
  111.8 2.9 %collective-permute-start.23 = (bf16[512,1024]{1,0:T(8,128)(2,1)S(1)}, bf16[512,1024]{1,0:T(8,128)(2,1)}, u32[]{:S(2)}, u32[]{:S(2)}) collective-permute-start(bf16[512,1024]{1,0:T(8,128)(2,1)S(1)} %pad_maximum_fusion.x_m), channel_id=1, source_target_pairs={{0,1},{1,0},{2,3},{3,2},{4,5},{5,4},{6,7},{7,6},{8,9},{9,8},{10,11... | collective-permute-start | bytes 3145736 | tf_op jit(solution)/shard_map/ppermute | solution.py:109
  133.3 93.9 %reduce-scatter.5.cloned.1.call-start = ((), (), s32[]{:S(2)}) async-start(), calls=%async_computation.4 | async-start | bytes 983040 | tf_op jit(solution)/shard_map/reduce_scatter | solution.py:887
  140.2 2.9 %collective-permute-start.25 = (bf16[512,1024]{1,0:T(8,128)(2,1)}, bf16[512,1024]{1,0:T(8,128)(2,1)S(1)}, u32[]{:S(2)}, u32[]{:S(2)}) collective-permute-start(bf16[512,1024]{1,0:T(8,128)(2,1)} %get-tuple-element.147), channel_id=1, source_target_pairs={{0,1},{1,0},{2,3},{3,2},{4,5},{5,4},{6,7},{7,6},{8,9},{9,8},{10,11... | collective-permute-start | bytes 3145736 | tf_op jit(solution)/shard_map/ppermute | solution.py:109
  147.1 10.8 %collective-permute-start.26 = (bf16[128,1024]{1,0:T(8,128)(2,1)}, bf16[128,1024]{1,0:T(8,128)(2,1)S(1)}, u32[]{:S(2)}, u32[]{:S(2)}) collective-permute-start(bf16[128,1024]{1,0:T(8,128)(2,1)} %get-tuple-element.153), channel_id=1, source_target_pairs={{0,2},{2,0},{4,6},{6,4},{8,10},{10,8},{12,14},{14,12},{16,18},{18,... | collective-permute-start | bytes 786440 | tf_op jit(solution)/shard_map/ppermute | solution.py:100
  148.6 13.9 %collective-permute-start.27 = (bf16[128,1024]{1,0:T(8,128)(2,1)}, bf16[128,1024]{1,0:T(8,128)(2,1)S(1)}, u32[]{:S(2)}, u32[]{:S(2)}) collective-permute-start(bf16[128,1024]{1,0:T(8,128)(2,1)} %get-tuple-element.154), channel_id=1, source_target_pairs={{0,4},{2,6},{4,0},{6,2},{8,12},{10,14},{12,8},{14,10},{16,20},{18,... | collective-permute-start | bytes 786440 | tf_op jit(solution)/shard_map/ppermute | solution.py:100
  150.0 12.4 %collective-permute-start.28 = (bf16[128,1024]{1,0:T(8,128)(2,1)}, bf16[128,1024]{1,0:T(8,128)(2,1)S(1)}, u32[]{:S(2)}, u32[]{:S(2)}) collective-permute-start(bf16[128,1024]{1,0:T(8,128)(2,1)} %get-tuple-element.155), channel_id=1, source_target_pairs={{0,6},{2,4},{4,2},{6,0},{8,14},{10,12},{12,10},{14,8},{16,22},{18,... | collective-permute-start | bytes 786440 | tf_op jit(solution)/shard_map/ppermute | solution.py:100
  163.5 10.2 %collective-permute-start.31 = (bf16[128,1024]{1,0:T(8,128)(2,1)S(1)}, bf16[128,1024]{1,0:T(8,128)(2,1)S(1)}, u32[]{:S(2)}, u32[]{:S(2)}) collective-permute-start(bf16[128,1024]{1,0:T(8,128)(2,1)S(1)} %get-tuple-element.211), channel_id=1, source_target_pairs={{0,6},{2,4},{4,2},{6,0},{8,14},{10,12},{12,10},{14,8},{16,22},{18,... | collective-permute-start | bytes 786440 | tf_op jit(solution)/shard_map/ppermute | solution.py:100
  165.0 12.3 %collective-permute-start.30 = (bf16[128,1024]{1,0:T(8,128)(2,1)S(1)}, bf16[128,1024]{1,0:T(8,128)(2,1)S(1)}, u32[]{:S(2)}, u32[]{:S(2)}) collective-permute-start(bf16[128,1024]{1,0:T(8,128)(2,1)S(1)} %get-tuple-element.211), channel_id=1, source_target_pairs={{0,4},{2,6},{4,0},{6,2},{8,12},{10,14},{12,8},{14,10},{16,20},{18,... | collective-permute-start | bytes 786440 | tf_op jit(solution)/shard_map/ppermute | solution.py:100
  166.2 11.2 %collective-permute-start.29 = (bf16[128,1024]{1,0:T(8,128)(2,1)S(1)}, bf16[128,1024]{1,0:T(8,128)(2,1)S(1)}, u32[]{:S(2)}, u32[]{:S(2)}) collective-permute-start(bf16[128,1024]{1,0:T(8,128)(2,1)S(1)} %get-tuple-element.211), channel_id=1, source_target_pairs={{0,2},{2,0},{4,6},{6,4},{8,10},{10,8},{12,14},{14,12},{16,18},{18,... | collective-permute-start | bytes 786440 | tf_op jit(solution)/shard_map/ppermute | solution.py:100
  167.1 10.6 %collective-permute-start.33 = (bf16[512,1024]{1,0:T(8,128)(2,1)S(1)}, bf16[512,1024]{1,0:T(8,128)(2,1)}, u32[]{:S(2)}, u32[]{:S(2)}) collective-permute-start(bf16[512,1024]{1,0:T(8,128)(2,1)S(1)} %copy-done.44), channel_id=1, source_target_pairs={{0,1},{1,0},{2,3},{3,2},{4,5},{5,4},{6,7},{7,6},{8,9},{9,8},{10,11... | collective-permute-start | bytes 3145736 | tf_op jit(solution)/shard_map/ppermute | solution.py:109
  177.5 3.4 %collective-permute-start.32 = (bf16[512,1024]{1,0:T(8,128)(2,1)S(1)}, bf16[512,1024]{1,0:T(8,128)(2,1)}, u32[]{:S(2)}, u32[]{:S(2)}) collective-permute-start(bf16[512,1024]{1,0:T(8,128)(2,1)S(1)} %pad_maximum_fusion.1.dh_m), channel_id=1, source_target_pairs={{0,1},{1,0},{2,3},{3,2},{4,5},{5,4},{6,7},{7,6},{8,9},{9,8},{10,11... | collective-permute-start | bytes 3145736 | tf_op jit(solution)/shard_map/ppermute | solution.py:109
  180.9 18.9 %collective-permute-start.34 = (bf16[128,1024]{1,0:T(8,128)(2,1)}, bf16[128,1024]{1,0:T(8,128)(2,1)S(1)}, u32[]{:S(2)}, u32[]{:S(2)}) collective-permute-start(bf16[128,1024]{1,0:T(8,128)(2,1)} %get-tuple-element.166), channel_id=1, source_target_pairs={{0,2},{2,0},{4,6},{6,4},{8,10},{10,8},{12,14},{14,12},{16,18},{18,... | collective-permute-start | bytes 786440 | tf_op jit(solution)/shard_map/ppermute | solution.py:100
  182.3 17.5 %collective-permute-start.35 = (bf16[128,1024]{1,0:T(8,128)(2,1)}, bf16[128,1024]{1,0:T(8,128)(2,1)S(1)}, u32[]{:S(2)}, u32[]{:S(2)}) collective-permute-start(bf16[128,1024]{1,0:T(8,128)(2,1)} %get-tuple-element.167), channel_id=1, source_target_pairs={{0,4},{2,6},{4,0},{6,2},{8,12},{10,14},{12,8},{14,10},{16,20},{18,... | collective-permute-start | bytes 786440 | tf_op jit(solution)/shard_map/ppermute | solution.py:100
  182.8 17.0 %collective-permute-start.36 = (bf16[128,1024]{1,0:T(8,128)(2,1)}, bf16[128,1024]{1,0:T(8,128)(2,1)}, u32[]{:S(2)}, u32[]{:S(2)}) collective-permute-start(bf16[128,1024]{1,0:T(8,128)(2,1)} %get-tuple-element.168), channel_id=1, source_target_pairs={{0,6},{2,4},{4,2},{6,0},{8,14},{10,12},{12,10},{14,8},{16,22},{18,... | collective-permute-start | bytes 786440 | tf_op jit(solution)/shard_map/ppermute | solution.py:100
  199.9 18.8 %copy-start.12 = (f32[128,1024]{1,0:T(8,128)S(1)}, f32[128,1024]{1,0:T(8,128)}, u32[]{:S(2)}) copy-start(f32[128,1024]{1,0:T(8,128)} %get-tuple-element.165) | copy-start | bytes 1572868
  199.9 6.4 %collective-permute-start.38 = (bf16[512,1024]{1,0:T(8,128)(2,1)}, bf16[512,1024]{1,0:T(8,128)(2,1)S(1)}, u32[]{:S(2)}, u32[]{:S(2)}) collective-permute-start(bf16[512,1024]{1,0:T(8,128)(2,1)} %get-tuple-element.184), channel_id=1, source_target_pairs={{0,1},{1,0},{2,3},{3,2},{4,5},{5,4},{6,7},{7,6},{8,9},{9,8},{10,11... | collective-permute-start | bytes 3145736 | tf_op jit(solution)/shard_map/ppermute | solution.py:109
  202.8 10.4 %collective-permute-start.37 = (bf16[64,1792]{1,0:T(8,128)(2,1)}, bf16[64,1792]{1,0:T(8,128)(2,1)S(1)}, u32[]{:S(2)}, u32[]{:S(2)}) collective-permute-start(bf16[64,1792]{1,0:T(8,128)(2,1)} %get-tuple-element.170), channel_id=1, source_target_pairs={{0,2},{2,0},{4,6},{6,4},{8,10},{10,8},{12,14},{14,12},{16,18},{18,... | collective-permute-start | bytes 688136 | tf_op jit(solution)/shard_map/ppermute | solution.py:100
  204.2 12.4 %collective-permute-start.49 = (bf16[64,1792]{1,0:T(8,128)(2,1)}, bf16[64,1792]{1,0:T(8,128)(2,1)S(1)}, u32[]{:S(2)}, u32[]{:S(2)}) collective-permute-start(bf16[64,1792]{1,0:T(8,128)(2,1)} %get-tuple-element.172), channel_id=1, source_target_pairs={{0,4},{2,6},{4,0},{6,2},{8,12},{10,14},{12,8},{14,10},{16,20},{18,... | collective-permute-start | bytes 688136 | tf_op jit(solution)/shard_map/ppermute | solution.py:100
  205.7 12.4 %collective-permute-start.50 = (bf16[64,1792]{1,0:T(8,128)(2,1)}, bf16[64,1792]{1,0:T(8,128)(2,1)}, u32[]{:S(2)}, u32[]{:S(2)}) collective-permute-start(bf16[64,1792]{1,0:T(8,128)(2,1)} %get-tuple-element.173), channel_id=1, source_target_pairs={{0,6},{2,4},{4,2},{6,0},{8,14},{10,12},{12,10},{14,8},{16,22},{18,... | collective-permute-start | bytes 688136 | tf_op jit(solution)/shard_map/ppermute | solution.py:100
  210.2 22.8 %copy-start.5 = (f32[128,1024]{1,0:T(8,128)S(1)}, f32[128,1024]{1,0:T(8,128)}, u32[]{:S(2)}) copy-start(f32[128,1024]{1,0:T(8,128)} %get-tuple-element.189) | copy-start | bytes 1572868
  210.2 22.8 %copy-start.28 = (f32[1024]{0:T(1024)S(1)}, f32[1024]{0:T(1024)}, u32[]{:S(2)}) copy-start(f32[1024]{0:T(1024)} %param.16) | copy-start | bytes 12292
  210.2 4.9 %collective-permute-start.44 = (f32[8,384]{1,0:T(8,128)S(1)}, f32[8,384]{1,0:T(8,128)S(1)}, u32[]{:S(2)}, u32[]{:S(2)}) collective-permute-start(f32[8,384]{1,0:T(8,128)S(1)} %copy-done.38), channel_id=1, source_target_pairs={{0,24},{2,26},{4,28},{6,30},{8,0},{10,2},{12,4},{14,6},{16,8},{18,... | collective-permute-start | bytes 36872 | tf_op jit(solution)/shard_map/ppermute | solution.py:105
  212.7 14.5 %collective-permute-start.43 = (f32[8,384]{1,0:T(8,128)S(1)}, f32[8,384]{1,0:T(8,128)S(1)}, u32[]{:S(2)}, u32[]{:S(2)}) collective-permute-start(f32[8,384]{1,0:T(8,128)S(1)} %copy-done.38), channel_id=1, source_target_pairs={{0,16},{2,18},{4,20},{6,22},{8,24},{10,26},{12,28},{14,30},{16,0},... | collective-permute-start | bytes 36872 | tf_op jit(solution)/shard_map/ppermute | solution.py:105
  213.2 14.0 %collective-permute-start.42 = (f32[8,384]{1,0:T(8,128)S(1)}, f32[8,384]{1,0:T(8,128)S(1)}, u32[]{:S(2)}, u32[]{:S(2)}) collective-permute-start(f32[8,384]{1,0:T(8,128)S(1)} %copy-done.38), channel_id=1, source_target_pairs={{0,8},{2,10},{4,12},{6,14},{8,16},{10,18},{12,20},{14,22},{16,24},... | collective-permute-start | bytes 36872 | tf_op jit(solution)/shard_map/ppermute | solution.py:105
  215.1 12.1 %collective-permute-start.39 = (bf16[128,1024]{1,0:T(8,128)(2,1)}, bf16[128,1024]{1,0:T(8,128)(2,1)S(1)}, u32[]{:S(2)}, u32[]{:S(2)}) collective-permute-start(bf16[128,1024]{1,0:T(8,128)(2,1)} %get-tuple-element.190), channel_id=1, source_target_pairs={{0,2},{2,0},{4,6},{6,4},{8,10},{10,8},{12,14},{14,12},{16,18},{18,... | collective-permute-start | bytes 786440 | tf_op jit(solution)/shard_map/ppermute | solution.py:100
  216.6 16.4 %collective-permute-start.40 = (bf16[128,1024]{1,0:T(8,128)(2,1)}, bf16[128,1024]{1,0:T(8,128)(2,1)S(1)}, u32[]{:S(2)}, u32[]{:S(2)}) collective-permute-start(bf16[128,1024]{1,0:T(8,128)(2,1)} %get-tuple-element.191), channel_id=1, source_target_pairs={{0,4},{2,6},{4,0},{6,2},{8,12},{10,14},{12,8},{14,10},{16,20},{18,... | collective-permute-start | bytes 786440 | tf_op jit(solution)/shard_map/ppermute | solution.py:100
  218.1 15.0 %collective-permute-start.41 = (bf16[128,1024]{1,0:T(8,128)(2,1)}, bf16[128,1024]{1,0:T(8,128)(2,1)S(1)}, u32[]{:S(2)}, u32[]{:S(2)}) collective-permute-start(bf16[128,1024]{1,0:T(8,128)(2,1)} %get-tuple-element.192), channel_id=1, source_target_pairs={{0,6},{2,4},{4,2},{6,0},{8,14},{10,12},{12,10},{14,8},{16,22},{18,... | collective-permute-start | bytes 786440 | tf_op jit(solution)/shard_map/ppermute | solution.py:100
  229.6 4.6 %collective-permute-start.45 = (bf16[80,384]{1,0:T(8,128)(2,1)}, bf16[80,384]{1,0:T(8,128)(2,1)S(1)}, u32[]{:S(2)}, u32[]{:S(2)}) collective-permute-start(bf16[80,384]{1,0:T(8,128)(2,1)} %get-tuple-element.198), channel_id=1, source_target_pairs={{0,2},{2,0},{4,6},{6,4},{8,10},{10,8},{12,14},{14,12},{16,18},{18,... | collective-permute-start | bytes 184328 | tf_op jit(solution)/shard_map/ppermute | solution.py:100
  231.0 5.1 %collective-permute-start.46 = (bf16[80,384]{1,0:T(8,128)(2,1)}, bf16[80,384]{1,0:T(8,128)(2,1)S(1)}, u32[]{:S(2)}, u32[]{:S(2)}) collective-permute-start(bf16[80,384]{1,0:T(8,128)(2,1)} %get-tuple-element.199), channel_id=1, source_target_pairs={{0,4},{2,6},{4,0},{6,2},{8,12},{10,14},{12,8},{14,10},{16,20},{18,... | collective-permute-start | bytes 184328 | tf_op jit(solution)/shard_map/ppermute | solution.py:100
  232.5 5.3 %collective-permute-start.47 = (bf16[80,384]{1,0:T(8,128)(2,1)}, bf16[80,384]{1,0:T(8,128)(2,1)S(1)}, u32[]{:S(2)}, u32[]{:S(2)}) collective-permute-start(bf16[80,384]{1,0:T(8,128)(2,1)} %get-tuple-element.200), channel_id=1, source_target_pairs={{0,6},{2,4},{4,2},{6,0},{8,14},{10,12},{12,10},{14,8},{16,22},{18,... | collective-permute-start | bytes 184328 | tf_op jit(solution)/shard_map/ppermute | solution.py:100
  240.2 1.4 collective-permute-start.48
  (35 other events, 172.9 us)
Sparse Core Ops, SparseCore 0:
  44.8 72.9 all-gather.1
  133.5 67.0 reduce-scatter.2
  202.8 24.3 reduce-scatter.4

commit v13 on v12

--- a/solution.py
+++ b/solution.py
@@ -314,7 +314,7 @@
         mine = pl.multiple_of(2 * k * local + core * local, local)
         other = pl.multiple_of(2 * k * local + (1 - core) * local, local)
         send[block, :] = held[pl.ds(other, local), :].astype(bfloat16)
-        keep[block, :] = held[pl.ds(mine, local), :]
+        keep[block, :] = held[pl.ds(mine, local), :].astype(bfloat16)
 
 
 def attn_back_kernel(
@@ -381,7 +381,7 @@
         mine = pl.multiple_of(2 * k * local + core * local, local)
         other = pl.multiple_of(2 * k * local + (1 - core) * local, local)
         send[block, :] = held[pl.ds(other, local), :].astype(bfloat16)
-        keep[block, :] = held[pl.ds(mine, local), :]
+        keep[block, :] = held[pl.ds(mine, local), :].astype(bfloat16)
     total[:, : 2 * LANES] += matmul_tn(
         jnp.concatenate(normed_rows, axis=0), jnp.concatenate(d_qkv_rows, axis=0)
     )
@@ -430,7 +430,7 @@
         out_specs=[block, block, wide, wide, table, whole_spec(weight)],
         out_shape=[
             jax.ShapeDtypeStruct((rows, width), bfloat16),
-            jax.ShapeDtypeStruct((rows, width), float32),
+            jax.ShapeDtypeStruct((rows, width), bfloat16),
             jax.ShapeDtypeStruct((2 * rows, 2 * LANES), float32),
             jax.ShapeDtypeStruct((2 * rows, 2 * LANES), bfloat16),
             jax.ShapeDtypeStruct((2 * rows, LANES), bfloat16),
@@ -456,7 +456,7 @@
         out_specs=[block, block, whole_spec(weight.shape), whole_spec((GAIN_ROWS, columns))],
         out_shape=[
             jax.ShapeDtypeStruct((rows, width), bfloat16),
-            jax.ShapeDtypeStruct((rows, width), float32),
+            jax.ShapeDtypeStruct((rows, width), bfloat16),
             jax.ShapeDtypeStruct(weight.shape, bfloat16),
             jax.ShapeDtypeStruct((GAIN_ROWS, columns), float32),
         ],
@@ -554,42 +554,46 @@
     )(where, ends, x_other, x_mine, g_other, g_mine, weight)
 
 
-def ffn_apply_kernel(first, values, weight, send, keep):
-    width = values.shape[1] - LANES
-    big = send.shape[1] // 2
-    small = 3 * big if first == 0 else 3 * big + LANES
-    partial = matmul_nt(values[:, :width], weight[:, first : first + width])
-    partial = partial + matmul_nt(values[:, width:], weight[:, small : small + LANES])
+def ffn_apply_kernel(values, weight, small, send, keep):
+    width = weight.shape[1]
+    partial = matmul_nt(values[:, :width], weight[...])
+    partial = partial + matmul_nt(values[:, width:], small[...])
     half = send.shape[0]
     send[...] = partial[:half].astype(bfloat16)
-    keep[...] = partial[half:]
-
-
-def ffn_apply(first, values, weight):
+    keep[...] = partial[half:].astype(bfloat16)
+
+
+def ffn_apply(first, last, values, weight):
     rows, width = values.shape[0] // 2, weight.shape[0]
+    columns = values.shape[1] - LANES
     row_spec = pl.BlockSpec((rows // 2, width), lambda i: (i, 0))
+
+    def column_spec(start, size):
+        return pl.BlockSpec(
+            (width, size), lambda i: (0, start // size), pipeline_mode=pl.Buffered(1)
+        )
+
     return pl.pallas_call(
-        lambda *refs: ffn_apply_kernel(first, *refs),
+        ffn_apply_kernel,
         grid=(2,),
         in_specs=[
             pl.BlockSpec((rows, values.shape[1]), lambda i: (i, 0)),
-            whole_spec(weight.shape),
+            column_spec(first, columns),
+            column_spec(last, LANES),
         ],
         out_specs=[row_spec] * 2,
-        out_shape=[
-            jax.ShapeDtypeStruct((rows, width), bfloat16),
-            jax.ShapeDtypeStruct((rows, width), float32),
-        ],
+        out_shape=[jax.ShapeDtypeStruct((rows, width), bfloat16)] * 2,
         compiler_params=pltpu.CompilerParams(vmem_limit_bytes=VMEM_BYTES),
         cost_estimate=cost(14),
-    )(values, weight)
+    )(values, weight, weight)
 
 
 def chip_sum_kernel(keep, received, *outs):
     rows = outs[0].shape[0]
     for mask, out in enumerate(outs):
         span = slice(mask * rows, (mask + 1) * rows)
-        out[...] = (keep[span, :] + received[span, :].astype(float32)).astype(out.dtype)
+        total = keep[span, :].astype(float32) + received[span, :].astype(float32)
+        out[...] = total.astype(out.dtype)
 
 
 def chip_sum(keep, received):
@@ -860,9 +864,9 @@
     own_ff = lax.psum_scatter(
         ff_grad, "dp", scatter_dimension=0, tiled=True, axis_index_groups=columns
     )
-    dn_send, dn_keep = ffn_apply(0, d_both, ff_weight)
+    dn_send, dn_keep = ffn_apply(0, ff_cols - 2 * LANES, d_both, ff_weight)
     dn_parts = plane_sent(chip_sum(dn_keep, swap_cores(dn_send)))
-    out_send, out_keep = ffn_apply(model, after(dn_send, act), ff_weight)
+    out_send, out_keep = ffn_apply(model, ff_cols - LANES, after(dn_send, act), ff_weight)
     d_normed2 = add_up(after(out_send, dn_parts))
     grad_out = jnp.where(
         (jnp.arange(local_rows) + core * local_rows < ends[0, lengths.shape[1] - 1])[:, None],
@@ -891,7 +895,7 @@
     keep = after(ff_parts, keep)
     ff_parts = plane_sent(ff_parts)
     dn_parts = chip_sum(keep, swap_cores(send))
-    part_gains = after(dn_parts, part_gains)
+    part_gains = after(dn_parts, part_gains + swap_cores(part_gains))
     dn_parts = plane_sent(after(ff_parts[1], dn_parts))
     far_gains = [send_deep(part_gains, step) for step in range(1, layers)]
     own_attn = after((dn_parts[1], block_out, far_gains), own_attn)
@@ -914,7 +918,6 @@
         *attn_parts,
         scalars=1,
     )
-    sums = sums + swap_cores(sums)
     return (
         block_out,
         grad_tokens,

time: 250 us -> 250 us (level)
  Pallas kernels: 81.7 us -> 78.5 us
    unnamed x97 -> x91, local copies, waits for them, and re-layouts: 9.48 us -> 9.37 us
  transfers between devices with their start and end apart: 54 -> 54, of which waited for: 24 -> 23; matrix products, arithmetic and copies ran while one was open for 5% -> 5% of each run, Pallas kernels for 24% -> 22%
where the time goes in v13:
time: 250 us; the launch traced here: 249 us
  Pallas kernels  78.5 us (31%)
  waiting for transfers between devices  78.5 us (31%)
  starting transfers between devices  52.3 us (21%)
  between operations  14.2 us (6%)
  local copies, waits for them, and re-layouts  14 us (6%)
  other arithmetic  11.8 us (5%)
    ppermute x36, waiting for transfers between devices, send_plane(): return lax.ppermute(values, 'dp', [(i, i ^ mask) for i in range(count)])  53.3 us
    ppermute x36, starting transfers between devices, send_plane(): return lax.ppermute(values, 'dp', [(i, i ^ mask) for i in range(count)])  41.2 us
    pallas_call x12, Pallas kernels, call(): pl.pallas_call(kernel, out_shape=[jax.ShapeDtypeStruct(shape, kind) for s...  27.5 us
    pallas_call x1, Pallas kernels, ffn_layer(): pl.pallas_call(ffn_kernel, grid=(2,), in_specs=[scalar, scalar] + [row_sp...  15.5 us
    pallas_call x1, Pallas kernels, attn_back(): pl.pallas_call(attn_back_kernel, grid=(PLANE // GROUPS_STEP,), in_specs=[...  15.1 us
    pallas_call x2, Pallas kernels, ffn_apply(): pl.pallas_call(ffn_apply_kernel, grid=(2,), in_specs=[pl.BlockSpec((rows,...  10.4 us
    pallas_call x1, Pallas kernels, attn(): pl.pallas_call(lambda *refs: attn_kernel(layers, *refs), grid=(PLANE // G...  9.95 us
    ppermute x6, starting transfers between devices, send_deep(): lax.ppermute(values, 'dp', [(i, (i + PLANE * step) % count) for i in rang...  9.44 us
  transfers between devices with their start and end apart: 54, of which 23 were waited for; matrix products, arithmetic and copies ran while one was open for 5% of the time, Pallas kernels for 22%

profile of v13, /device:TPU:0, one launch (start us, length us, event | category | flops | bytes accessed | tf_op | source)
XLA Modules:
  0.0 249.2 jit_solution(9853807886586791887)
XLA Ops:
  7.9 1.7 shard_map.238
  9.6 2.9 %collective-permute-start = (bf16[32,1024]{1,0:T(8,128)(2,1)}, bf16[32,1024]{1,0:T(8,128)(2,1)S(1)}, u32[]{:S(2)}, u32[]{:S(2)}) collective-permute-start(bf16[32,1024]{1,0:T(8,128)(2,1)} %get-tuple-element.116), channel_id=1, source_target_pairs={{0,2},{2,0},{4,6},{6,4},{8,10},{10,8},{12,14},{14,12},{16,18},{18,... | collective-permute-start | bytes 196616 | tf_op jit(solution)/shard_map/ppermute | solution.py:100
  12.5 1.5 collective-permute-start.1
  14.0 2.2 shard_map.237
  17.0 2.4 collective-permute-done.2.three
  20.0 1.7 shard_map.239
  21.7 3.6 %collective-permute-start.5 = (bf16[256,384]{1,0:T(8,128)(2,1)}, bf16[256,384]{1,0:T(8,128)(2,1)S(1)}, u32[]{:S(2)}, u32[]{:S(2)}) collective-permute-start(bf16[256,384]{1,0:T(8,128)(2,1)} %get-tuple-element.134.refs_9_), channel_id=1, source_target_pairs={{0,24},{2,26},{4,28},{6,30},{8,0},{10,2},{12,4},{14,6},{16,8},{18,... | collective-permute-start | bytes 589832 | tf_op jit(solution)/shard_map/ppermute | solution.py:105
  28.5 2.6 %collective-permute-done.5.refs_12_ = bf16[256,384]{1,0:T(8,128)(2,1)S(1)} collective-permute-done((bf16[256,384]{1,0:T(8,128)(2,1)}, bf16[256,384]{1,0:T(8,128)(2,1)S(1)}, u32[]{:S(2)}, u32[]{:S(2)}) %collective-permute-start.5) | collective-permute-done | bytes 196640 | tf_op jit(solution)/shard_map/ppermute | solution.py:105
  31.5 3.0 %fusion.6 = (f32[1024,128]{1,0:T(8,128)}, f32[1024,128]{1,0:T(8,128)}) fusion(f32[128]{0:T(128)S(1)} %get-tuple-element.223, f32[128]{0:T(128)S(1)} %get-tuple-element.224, f32[1024]{0:T(1024)S(1)} %bitcast.28), kind=kLoop, calls=%fused_computation.13 | loop fusion | flops 262144 | bytes 1053696 | tf_op jit(solution)/shard_map/mul | solution.py:758
  34.6 6.7 %collective-permute-done.4.refs_11_ = bf16[256,384]{1,0:T(8,128)(2,1)S(1)} collective-permute-done((bf16[256,384]{1,0:T(8,128)(2,1)}, bf16[256,384]{1,0:T(8,128)(2,1)S(1)}, u32[]{:S(2)}, u32[]{:S(2)}) %collective-permute-start.4) | collective-permute-done | bytes 196640 | tf_op jit(solution)/shard_map/ppermute | solution.py:105
  42.2 2.5 shard_map.240
  46.0 2.4 collective-permute-start.11
  48.5 5.7 %collective-permute-done.9 = bf16[128,1024]{1,0:T(8,128)(2,1)S(1)} collective-permute-done((bf16[128,1024]{1,0:T(8,128)(2,1)S(1)}, bf16[128,1024]{1,0:T(8,128)(2,1)S(1)}, u32[]{:S(2)}, u32[]{:S(2)}) %collective-permute-start.9) | collective-permute-done | bytes 262176 | tf_op jit(solution)/shard_map/ppermute | solution.py:100
  54.2 3.5 %collective-permute-done.10 = bf16[128,1024]{1,0:T(8,128)(2,1)S(1)} collective-permute-done((bf16[128,1024]{1,0:T(8,128)(2,1)S(1)}, bf16[128,1024]{1,0:T(8,128)(2,1)S(1)}, u32[]{:S(2)}, u32[]{:S(2)}) %collective-permute-start.10) | collective-permute-done | bytes 262176 | tf_op jit(solution)/shard_map/ppermute | solution.py:100
  59.1 1.4 collective-permute-start.14
  63.1 9.9 %shard_map.241 = (bf16[512,1024]{1,0:T(8,128)(2,1)}, bf16[512,1024]{1,0:T(8,128)(2,1)}, f32[1024,256]{1,0:T(8,128)}, bf16[1024,256]{1,0:T(8,128)(2,1)}, bf16[102...) custom-call(s32[3]{0:T(128)} %pad_add_fusion.where_ref.refs_0_, s32[4,4]{1,0:T(4,128)} %copy-done.33, ...), custom_call_target="tpu_custom_call" | custom-call | flops 1024 | bytes 36000000 | tf_op jit(solution)/shard_map/pallas_call | solution.py:425
  74.6 2.8 %collective-permute-done.16.received = bf16[512,1024]{1,0:T(8,128)(2,1)S(1)} collective-permute-done((bf16[512,1024]{1,0:T(8,128)(2,1)}, bf16[512,1024]{1,0:T(8,128)(2,1)S(1)}, u32[]{:S(2)}, u32[]{:S(2)}) %collective-permute-start.16) | collective-permute-done | bytes 1048608 | tf_op jit(solution)/shard_map/ppermute | solution.py:109
  78.4 2.7 %shard_map.242 = (f32[128,1024]{1,0:T(8,128)}, bf16[128,1024]{1,0:T(8,128)(2,1)}, bf16[128,1024]{1,0:T(8,128)(2,1)}, bf16[128,1024]{1,0:T(8,128)(2,1)}) custom-call(bf16[512,1024]{1,0:T(8,128)(2,1)} %get-tuple-element.138.keep, bf16[512,1024]{1,0:T(8,128)(2,1)} %copy-done.11), custom_call_target="tpu_custom_call" | custom-call | flops 1024 | bytes 1024 | tf_op jit(solution)/shard_map/pallas_call | solution.py:115
  82.8 1.8 collective-permute-start.19
  84.6 5.9 %collective-permute-done.17 = bf16[128,1024]{1,0:T(8,128)(2,1)S(1)} collective-permute-done((bf16[128,1024]{1,0:T(8,128)(2,1)}, bf16[128,1024]{1,0:T(8,128)(2,1)S(1)}, u32[]{:S(2)}, u32[]{:S(2)}) %collective-permute-start.17) | collective-permute-done | bytes 262176 | tf_op jit(solution)/shard_map/ppermute | solution.py:100
  90.4 5.6 %collective-permute-done.18 = bf16[128,1024]{1,0:T(8,128)(2,1)S(1)} collective-permute-done((bf16[128,1024]{1,0:T(8,128)(2,1)}, bf16[128,1024]{1,0:T(8,128)(2,1)S(1)}, u32[]{:S(2)}, u32[]{:S(2)}) %collective-permute-start.18) | collective-permute-done | bytes 262176 | tf_op jit(solution)/shard_map/ppermute | solution.py:100
  96.0 1.3 multiply_reduce_fusion.2
  97.5 1.2 collective-permute-start.22
  98.7 1.3 collective-permute-start.21
  101.2 6.5 %collective-permute-done.22 = bf16[128,1024]{1,0:T(8,128)(2,1)S(1)} collective-permute-done((bf16[128,1024]{1,0:T(8,128)(2,1)S(1)}, bf16[128,1024]{1,0:T(8,128)(2,1)S(1)}, u32[]{:S(2)}, u32[]{:S(2)}) %collective-permute-start.22) | collective-permute-done | bytes 262176 | tf_op jit(solution)/shard_map/ppermute | solution.py:100
  107.7 3.5 %collective-permute-done.21 = bf16[128,1024]{1,0:T(8,128)(2,1)S(1)} collective-permute-done((bf16[128,1024]{1,0:T(8,128)(2,1)S(1)}, bf16[128,1024]{1,0:T(8,128)(2,1)S(1)}, u32[]{:S(2)}, u32[]{:S(2)}) %collective-permute-start.21) | collective-permute-done | bytes 262176 | tf_op jit(solution)/shard_map/ppermute | solution.py:100
  112.6 1.5 collective-permute-done.23.x_o
  114.1 3.7 %all-gather.2.cloned.1.call-done.weight.small = bf16[1024,1792]{1,0:T(8,128)(2,1)} async-done(((bf16[256,1792]{1,0:T(8,128)(2,1)}), bf16[1024,1792]{1,0:T(8,128)(2,1)}) %all-gather.2.cloned.1.call-update) | async-done | bytes 3670032 | tf_op jit(solution)/shard_map/all_gather | solution.py:836
  117.8 15.5 %shard_map.243 = (bf16[1024,640]{1,0:T(8,128)(2,1)}, bf16[1024,1152]{1,0:T(8,128)(2,1)}, bf16[1024,1792]{1,0:T(8,128)(2,1)}) custom-call(s32[3]{0:T(128)} %pad_add_fusion.where_ref.refs_0_, s32[4,4]{1,0:T(4,128)} %copy-done.33, bf16[512,1024]{1,0:T(8,128)(2,1)} %collective-permute-done.23.x_o, bf16[512,1024]{1,0:T(8,128)(2,1)} %copy-done.3, ...), custom_call_target="tpu_custom_call" | custom-call | flops 1024 | bytes 48000000 | tf_op jit(solution)/shard_map/pallas_call | solution.py:543
  133.6 6.0 %shard_map.244 = (bf16[512,1024]{1,0:T(8,128)(2,1)}, bf16[512,1024]{1,0:T(8,128)(2,1)}) custom-call(bf16[1024,1152]{1,0:T(8,128)(2,1)} %get-tuple-element.146.values, bf16[1024,1792]{1,0:T(8,128)(2,1)} %all-gather.2.cloned.1.call-done.weight.small, bf16[1024,1792]{1,0:T(8,128)(2,1)} %all-gather.2.cloned.1.call-done.weight.small), custom_call_target="tpu_custom_call" | custom-call | flops 1024 | bytes 14000000 | tf_op jit(solution)/shard_map/pallas_call | solution.py:576
  139.6 2.9 %collective-permute-done.25.received = bf16[512,1024]{1,0:T(8,128)(2,1)S(1)} collective-permute-done((bf16[512,1024]{1,0:T(8,128)(2,1)}, bf16[512,1024]{1,0:T(8,128)(2,1)S(1)}, u32[]{:S(2)}, u32[]{:S(2)}) %collective-permute-start.25) | collective-permute-done | bytes 1048608 | tf_op jit(solution)/shard_map/ppermute | solution.py:109
  143.5 2.6 %shard_map.246 = (f32[128,1024]{1,0:T(8,128)}, bf16[128,1024]{1,0:T(8,128)(2,1)}, bf16[128,1024]{1,0:T(8,128)(2,1)}, bf16[128,1024]{1,0:T(8,128)(2,1)}) custom-call(bf16[512,1024]{1,0:T(8,128)(2,1)} %get-tuple-element.151.keep, bf16[512,1024]{1,0:T(8,128)(2,1)} %copy-done.10), custom_call_target="tpu_custom_call" | custom-call | flops 1024 | bytes 1024 | tf_op jit(solution)/shard_map/pallas_call | solution.py:115
  146.1 1.5 collective-permute-start.26
  147.6 1.5 collective-permute-start.27
  149.6 1.3 slice.19
  151.5 4.4 %shard_map.245 = (bf16[512,1024]{1,0:T(8,128)(2,1)}, bf16[512,1024]{1,0:T(8,128)(2,1)}) custom-call(bf16[1024,640]{1,0:T(8,128)(2,1)} %get-tuple-element.149.values, bf16[1024,1792]{1,0:T(8,128)(2,1)} %all-gather.2.cloned.1.call-done.weight.small, bf16[1024,1792]{1,0:T(8,128)(2,1)} %all-gather.2.cloned.1.call-done.weight.small), custom_call_target="tpu_custom_call" | custom-call | flops 1024 | bytes 14000000 | tf_op jit(solution)/shard_map/pallas_call | solution.py:576
  156.0 5.5 %collective-permute-done.27 = bf16[128,1024]{1,0:T(8,128)(2,1)S(1)} collective-permute-done((bf16[128,1024]{1,0:T(8,128)(2,1)}, bf16[128,1024]{1,0:T(8,128)(2,1)S(1)}, u32[]{:S(2)}, u32[]{:S(2)}) %collective-permute-start.27) | collective-permute-done | bytes 262176 | tf_op jit(solution)/shard_map/ppermute | solution.py:100
  162.6 1.5 collective-permute-start.31
  166.1 6.7 %collective-permute-done.31 = bf16[128,1024]{1,0:T(8,128)(2,1)S(1)} collective-permute-done((bf16[128,1024]{1,0:T(8,128)(2,1)S(1)}, bf16[128,1024]{1,0:T(8,128)(2,1)S(1)}, u32[]{:S(2)}, u32[]{:S(2)}) %collective-permute-start.31) | collective-permute-done | bytes 262176 | tf_op jit(solution)/shard_map/ppermute | solution.py:100
  172.8 3.6 %collective-permute-done.30 = bf16[128,1024]{1,0:T(8,128)(2,1)S(1)} collective-permute-done((bf16[128,1024]{1,0:T(8,128)(2,1)S(1)}, bf16[128,1024]{1,0:T(8,128)(2,1)S(1)}, u32[]{:S(2)}, u32[]{:S(2)}) %collective-permute-start.30) | collective-permute-done | bytes 262176 | tf_op jit(solution)/shard_map/ppermute | solution.py:100
  176.7 2.9 %shard_map.247 = (f32[128,1024]{1,0:T(8,128)}, bf16[128,1024]{1,0:T(8,128)(2,1)}, bf16[128,1024]{1,0:T(8,128)(2,1)}, bf16[128,1024]{1,0:T(8,128)(2,1)}) custom-call(bf16[512,1024]{1,0:T(8,128)(2,1)} %get-tuple-element.160.keep, bf16[512,1024]{1,0:T(8,128)(2,1)} %collective-permute-done.33.received), custom_call_target="tpu_custom_call" | custom-call | flops 1024 | bytes 1024 | tf_op jit(solution)/shard_map/pallas_call | solution.py:115
  179.6 1.3 collective-permute-start.34
  181.7 1.4 collective-permute-start.36
  183.1 15.1 %shard_map.249 = (bf16[512,1024]{1,0:T(8,128)(2,1)}, bf16[512,1024]{1,0:T(8,128)(2,1)}, bf16[1024,384]{1,0:T(8,128)(2,1)}, f32[8,384]{1,0:T(8,128)}) custom-call(s32[3]{0:T(128)} %pad_add_fusion.where_ref.refs_0_, s32[4,4]{1,0:T(4,128)} %copy-done.33, bf16[512,1024]{1,0:T(8,128)(2,1)} %copy-done, bf16[512,1024]{1,0:T(8,128)(2,1)} %copy-done.1, ...), custom_call_target="tpu_custom_call" | custom-call | flops 1024 | bytes 24000000 | tf_op jit(solution)/shard_map/pallas_call | solution.py:451
  198.9 1.6 reduce-scatter.3.cloned.1.call-done.own
  200.5 2.2 shard_map.248
  202.8 1.5 collective-permute-start.37
  204.2 1.5 collective-permute-start.49
  208.0 2.8 %shard_map.250 = (f32[128,1024]{1,0:T(8,128)}, bf16[128,1024]{1,0:T(8,128)(2,1)}, bf16[128,1024]{1,0:T(8,128)(2,1)}, bf16[128,1024]{1,0:T(8,128)(2,1)}) custom-call(bf16[512,1024]{1,0:T(8,128)(2,1)} %get-tuple-element.183.keep, bf16[512,1024]{1,0:T(8,128)(2,1)} %copy-done.9), custom_call_target="tpu_custom_call" | custom-call | flops 1024 | bytes 1024 | tf_op jit(solution)/shard_map/pallas_call | solution.py:115
  210.7 2.3 collective-permute-start.45
  213.6 1.9 collective-permute-start.43
  215.6 1.4 collective-permute-start.39
  217.0 1.5 collective-permute-start.40
  219.1 1.9 add_convert_fusion
  221.0 2.7 %shard_map.253 = (f32[64,2304]{1,0:T(8,128)}, f32[64,2304]{1,0:T(8,128)}, f32[64,2304]{1,0:T(8,128)}) custom-call(s32[3]{0:T(128)} %pad_add_fusion.where_ref.refs_0_, bf16[64,1792]{1,0:T(8,128)(2,1)} %get-tuple-element.171.own, bf16[64,1792]{1,0:T(8,128)(2,1)} %copy-done.18, bf16[64,1792]{1,0:T(8,128)(2,1)} %copy-done.19, ...), custom_call_target="tpu_custom_call" | custom-call | flops 1024 | bytes 1024 | tf_op jit(solution)/shard_map/pallas_call | solution.py:115
  223.7 3.4 %reduce-scatter.5.cloned.1.call-done.own = bf16[256,384]{1,0:T(8,128)(2,1)} async-done(((bf16[1024,384]{1,0:T(8,128)(2,1)}), bf16[256,384]{1,0:T(8,128)(2,1)}) %reduce-scatter.5.cloned.1.call-update) | async-done | bytes 196624 | tf_op jit(solution)/shard_map/reduce_scatter | solution.py:891
  227.7 1.7 shard_map.251
  229.5 1.5 collective-permute-start.46
  231.0 1.4 collective-permute-start.47
  234.3 1.7 collective-permute-done.47.two
  236.0 1.7 collective-permute-done.48.three
  238.4 1.7 shard_map.252
  240.1 1.3 slice_bitcast_fusion.2
  241.4 1.3 slice_bitcast_fusion
  (184 shorter events, 32.4 us)
Async XLA Ops:
  7.2 110.6 %all-gather.2.cloned.1.call-start = ((), (), s32[]{:S(2)}) async-start(), calls=%async_computation.2 | async-start | bytes 4587520 | tf_op jit(solution)/shard_map/all_gather | solution.py:836
  9.6 6.7 %collective-permute-start = (bf16[32,1024]{1,0:T(8,128)(2,1)}, bf16[32,1024]{1,0:T(8,128)(2,1)S(1)}, u32[]{:S(2)}, u32[]{:S(2)}) collective-permute-start(bf16[32,1024]{1,0:T(8,128)(2,1)} %get-tuple-element.116), channel_id=1, source_target_pairs={{0,2},{2,0},{4,6},{6,4},{8,10},{10,8},{12,14},{14,12},{16,18},{18,... | collective-permute-start | bytes 196616 | tf_op jit(solution)/shard_map/ppermute | solution.py:100
  12.5 4.5 %collective-permute-start.1 = (bf16[32,1024]{1,0:T(8,128)(2,1)}, bf16[32,1024]{1,0:T(8,128)(2,1)S(1)}, u32[]{:S(2)}, u32[]{:S(2)}) collective-permute-start(bf16[32,1024]{1,0:T(8,128)(2,1)} %get-tuple-element.117), channel_id=1, source_target_pairs={{0,4},{2,6},{4,0},{6,2},{8,12},{10,14},{12,8},{14,10},{16,20},{18,... | collective-permute-start | bytes 196616 | tf_op jit(solution)/shard_map/ppermute | solution.py:100
  14.0 5.4 %collective-permute-start.2 = (bf16[32,1024]{1,0:T(8,128)(2,1)}, bf16[32,1024]{1,0:T(8,128)(2,1)S(1)}, u32[]{:S(2)}, u32[]{:S(2)}) collective-permute-start(bf16[32,1024]{1,0:T(8,128)(2,1)} %get-tuple-element.118), channel_id=1, source_target_pairs={{0,6},{2,4},{4,2},{6,0},{8,14},{10,12},{12,10},{14,8},{16,22},{18,... | collective-permute-start | bytes 196616 | tf_op jit(solution)/shard_map/ppermute | solution.py:100
  16.2 28.7 %copy-start.4 = (bf16[128,1024]{1,0:T(8,128)(2,1)S(1)}, bf16[128,1024]{1,0:T(8,128)(2,1)}, u32[]{:S(2)}) copy-start(bf16[128,1024]{1,0:T(8,128)(2,1)} %param.14) | copy-start | bytes 786436
  21.7 9.3 %collective-permute-start.5 = (bf16[256,384]{1,0:T(8,128)(2,1)}, bf16[256,384]{1,0:T(8,128)(2,1)S(1)}, u32[]{:S(2)}, u32[]{:S(2)}) collective-permute-start(bf16[256,384]{1,0:T(8,128)(2,1)} %get-tuple-element.134.refs_9_), channel_id=1, source_target_pairs={{0,24},{2,26},{4,28},{6,30},{8,0},{10,2},{12,4},{14,6},{16,8},{18,... | collective-permute-start | bytes 589832 | tf_op jit(solution)/shard_map/ppermute | solution.py:105
  25.3 15.9 %collective-permute-start.4 = (bf16[256,384]{1,0:T(8,128)(2,1)}, bf16[256,384]{1,0:T(8,128)(2,1)S(1)}, u32[]{:S(2)}, u32[]{:S(2)}) collective-permute-start(bf16[256,384]{1,0:T(8,128)(2,1)} %get-tuple-element.134.refs_9_), channel_id=1, source_target_pairs={{0,16},{2,18},{4,20},{6,22},{8,24},{10,26},{12,28},{14,30},{16,0},... | collective-permute-start | bytes 589832 | tf_op jit(solution)/shard_map/ppermute | solution.py:105
  25.3 15.9 %collective-permute-start.3 = (bf16[256,384]{1,0:T(8,128)(2,1)}, bf16[256,384]{1,0:T(8,128)(2,1)S(1)}, u32[]{:S(2)}, u32[]{:S(2)}) collective-permute-start(bf16[256,384]{1,0:T(8,128)(2,1)} %get-tuple-element.134.refs_9_), channel_id=1, source_target_pairs={{0,8},{2,10},{4,12},{6,14},{8,16},{10,18},{12,20},{14,22},{16,24},... | collective-permute-start | bytes 589832 | tf_op jit(solution)/shard_map/ppermute | solution.py:105
  27.3 21.2 %copy-start.33 = (s32[4,4]{1,0:T(4,128)}, s32[4,4]{1,0:T(4,128)S(1)}, u32[]{:S(2)}) copy-start(s32[4,4]{1,0:T(4,128)S(1)} %reduce_window_sum.11.refs_1_.ends_ref) | copy-start | bytes 196
  27.4 13.9 %collective-permute-start.6 = (bf16[64,1792]{1,0:T(8,128)(2,1)}, bf16[64,1792]{1,0:T(8,128)(2,1)S(1)}, u32[]{:S(2)}, u32[]{:S(2)}) collective-permute-start(bf16[64,1792]{1,0:T(8,128)(2,1)} %get-tuple-element.126), channel_id=1, source_target_pairs={{0,2},{2,0},{4,6},{6,4},{8,10},{10,8},{12,14},{14,12},{16,18},{18,... | collective-permute-start | bytes 688136 | tf_op jit(solution)/shard_map/ppermute | solution.py:100
  28.0 13.3 %collective-permute-start.7 = (bf16[64,1792]{1,0:T(8,128)(2,1)}, bf16[64,1792]{1,0:T(8,128)(2,1)S(1)}, u32[]{:S(2)}, u32[]{:S(2)}) collective-permute-start(bf16[64,1792]{1,0:T(8,128)(2,1)} %get-tuple-element.127), channel_id=1, source_target_pairs={{0,4},{2,6},{4,0},{6,2},{8,12},{10,14},{12,8},{14,10},{16,20},{18,... | collective-permute-start | bytes 688136 | tf_op jit(solution)/shard_map/ppermute | solution.py:100
  31.0 10.3 %collective-permute-start.8 = (bf16[64,1792]{1,0:T(8,128)(2,1)}, bf16[64,1792]{1,0:T(8,128)(2,1)S(1)}, u32[]{:S(2)}, u32[]{:S(2)}) collective-permute-start(bf16[64,1792]{1,0:T(8,128)(2,1)} %get-tuple-element.128), channel_id=1, source_target_pairs={{0,6},{2,4},{4,2},{6,0},{8,14},{10,12},{12,10},{14,8},{16,22},{18,... | collective-permute-start | bytes 688136 | tf_op jit(solution)/shard_map/ppermute | solution.py:100
  41.3 20.8 %copy-start.24 = (bf16[256,384]{1,0:T(8,128)(2,1)}, bf16[256,384]{1,0:T(8,128)(2,1)S(1)}, u32[]{:S(2)}) copy-start(bf16[256,384]{1,0:T(8,128)(2,1)S(1)} %collective-permute-done.4.refs_11_) | copy-start | bytes 589828
  41.3 20.8 %copy-start.25 = (bf16[256,384]{1,0:T(8,128)(2,1)}, bf16[256,384]{1,0:T(8,128)(2,1)S(1)}, u32[]{:S(2)}) copy-start(bf16[256,384]{1,0:T(8,128)(2,1)S(1)} %collective-permute-done.3.refs_10_) | copy-start | bytes 589828
  44.6 155.9 %reduce-scatter.3.cloned.1.call-start = ((), (), s32[]{:S(2)}) async-start(), calls=%async_computation.3 | async-start | bytes 4587520 | tf_op jit(solution)/shard_map/reduce_scatter | solution.py:864
  44.9 9.3 %collective-permute-start.9 = (bf16[128,1024]{1,0:T(8,128)(2,1)S(1)}, bf16[128,1024]{1,0:T(8,128)(2,1)S(1)}, u32[]{:S(2)}, u32[]{:S(2)}) collective-permute-start(bf16[128,1024]{1,0:T(8,128)(2,1)S(1)} %copy-done.4), channel_id=1, source_target_pairs={{0,2},{2,0},{4,6},{6,4},{8,10},{10,8},{12,14},{14,12},{16,18},{18,... | collective-permute-start | bytes 786440 | tf_op jit(solution)/shard_map/ppermute | solution.py:100
  45.5 12.3 %collective-permute-start.10 = (bf16[128,1024]{1,0:T(8,128)(2,1)S(1)}, bf16[128,1024]{1,0:T(8,128)(2,1)S(1)}, u32[]{:S(2)}, u32[]{:S(2)}) collective-permute-start(bf16[128,1024]{1,0:T(8,128)(2,1)S(1)} %copy-done.4), channel_id=1, source_target_pairs={{0,4},{2,6},{4,0},{6,2},{8,12},{10,14},{12,8},{14,10},{16,20},{18,... | collective-permute-start | bytes 786440 | tf_op jit(solution)/shard_map/ppermute | solution.py:100
  46.0 11.8 %collective-permute-start.11 = (bf16[128,1024]{1,0:T(8,128)(2,1)S(1)}, bf16[128,1024]{1,0:T(8,128)(2,1)S(1)}, u32[]{:S(2)}, u32[]{:S(2)}) collective-permute-start(bf16[128,1024]{1,0:T(8,128)(2,1)S(1)} %copy-done.4), channel_id=1, source_target_pairs={{0,6},{2,4},{4,2},{6,0},{8,14},{10,12},{12,10},{14,8},{16,22},{18,... | collective-permute-start | bytes 786440 | tf_op jit(solution)/shard_map/ppermute | solution.py:100
  57.8 4.2 %collective-permute-start.12 = (bf16[512,1024]{1,0:T(8,128)(2,1)S(1)}, bf16[512,1024]{1,0:T(8,128)(2,1)S(1)}, u32[]{:S(2)}, u32[]{:S(2)}) collective-permute-start(bf16[512,1024]{1,0:T(8,128)(2,1)S(1)} %constant_dynamic-update-slice_fusion.refs_2_.tok_m), channel_id=1, source_target_pairs={{0,1},{1,0},{2,3},{3,2},{4,5},{5,4},{6,7},{7,6},{8,9},{9,8},{10,11... | collective-permute-start | bytes 3145736 | tf_op jit(solution)/shard_map/ppermute | solution.py:109
  57.9 15.1 %collective-permute-start.15 = (bf16[128,1024]{1,0:T(8,128)(2,1)S(1)}, bf16[128,1024]{1,0:T(8,128)(2,1)S(1)}, u32[]{:S(2)}, u32[]{:S(2)}) collective-permute-start(bf16[128,1024]{1,0:T(8,128)(2,1)S(1)} %copy-done.8), channel_id=1, source_target_pairs={{0,6},{2,4},{4,2},{6,0},{8,14},{10,12},{12,10},{14,8},{16,22},{18,... | collective-permute-start | bytes 786440 | tf_op jit(solution)/shard_map/ppermute | solution.py:100
  59.1 14.0 %collective-permute-start.14 = (bf16[128,1024]{1,0:T(8,128)(2,1)S(1)}, bf16[128,1024]{1,0:T(8,128)(2,1)S(1)}, u32[]{:S(2)}, u32[]{:S(2)}) collective-permute-start(bf16[128,1024]{1,0:T(8,128)(2,1)S(1)} %copy-done.8), channel_id=1, source_target_pairs={{0,4},{2,6},{4,0},{6,2},{8,12},{10,14},{12,8},{14,10},{16,20},{18,... | collective-permute-start | bytes 786440 | tf_op jit(solution)/shard_map/ppermute | solution.py:100
  60.5 12.6 %collective-permute-start.13 = (bf16[128,1024]{1,0:T(8,128)(2,1)S(1)}, bf16[128,1024]{1,0:T(8,128)(2,1)S(1)}, u32[]{:S(2)}, u32[]{:S(2)}) collective-permute-start(bf16[128,1024]{1,0:T(8,128)(2,1)S(1)} %copy-done.8), channel_id=1, source_target_pairs={{0,2},{2,0},{4,6},{6,4},{8,10},{10,8},{12,14},{14,12},{16,18},{18,... | collective-permute-start | bytes 786440 | tf_op jit(solution)/shard_map/ppermute | solution.py:100
  74.5 2.9 %collective-permute-start.16 = (bf16[512,1024]{1,0:T(8,128)(2,1)}, bf16[512,1024]{1,0:T(8,128)(2,1)S(1)}, u32[]{:S(2)}, u32[]{:S(2)}) collective-permute-start(bf16[512,1024]{1,0:T(8,128)(2,1)} %get-tuple-element.141), channel_id=1, source_target_pairs={{0,1},{1,0},{2,3},{3,2},{4,5},{5,4},{6,7},{7,6},{8,9},{9,8},{10,11... | collective-permute-start | bytes 3145736 | tf_op jit(solution)/shard_map/ppermute | solution.py:109
  81.1 20.0 %copy-start.17 = (bf16[128,1024]{1,0:T(8,128)(2,1)S(1)}, bf16[128,1024]{1,0:T(8,128)(2,1)}, u32[]{:S(2)}) copy-start(bf16[128,1024]{1,0:T(8,128)(2,1)} %copy-done.16) | copy-start | bytes 786436
  81.1 20.0 %copy-start.15 = (bf16[128,1024]{1,0:T(8,128)(2,1)S(1)}, bf16[128,1024]{1,0:T(8,128)(2,1)}, u32[]{:S(2)}) copy-start(bf16[128,1024]{1,0:T(8,128)(2,1)} %copy-done.14) | copy-start | bytes 786436
  81.1 9.4 %collective-permute-start.17 = (bf16[128,1024]{1,0:T(8,128)(2,1)}, bf16[128,1024]{1,0:T(8,128)(2,1)S(1)}, u32[]{:S(2)}, u32[]{:S(2)}) collective-permute-start(bf16[128,1024]{1,0:T(8,128)(2,1)} %get-tuple-element.143), channel_id=1, source_target_pairs={{0,2},{2,0},{4,6},{6,4},{8,10},{10,8},{12,14},{14,12},{16,18},{18,... | collective-permute-start | bytes 786440 | tf_op jit(solution)/shard_map/ppermute | solution.py:100
  82.1 13.9 %collective-permute-start.18 = (bf16[128,1024]{1,0:T(8,128)(2,1)}, bf16[128,1024]{1,0:T(8,128)(2,1)S(1)}, u32[]{:S(2)}, u32[]{:S(2)}) collective-permute-start(bf16[128,1024]{1,0:T(8,128)(2,1)} %get-tuple-element.144), channel_id=1, source_target_pairs={{0,4},{2,6},{4,0},{6,2},{8,12},{10,14},{12,8},{14,10},{16,20},{18,... | collective-permute-start | bytes 786440 | tf_op jit(solution)/shard_map/ppermute | solution.py:100
  82.8 13.2 %collective-permute-start.19 = (bf16[128,1024]{1,0:T(8,128)(2,1)}, bf16[128,1024]{1,0:T(8,128)(2,1)S(1)}, u32[]{:S(2)}, u32[]{:S(2)}) collective-permute-start(bf16[128,1024]{1,0:T(8,128)(2,1)} %get-tuple-element.145), channel_id=1, source_target_pairs={{0,6},{2,4},{4,2},{6,0},{8,14},{10,12},{12,10},{14,8},{16,22},{18,... | collective-permute-start | bytes 786440 | tf_op jit(solution)/shard_map/ppermute | solution.py:100
  97.5 10.2 %collective-permute-start.22 = (bf16[128,1024]{1,0:T(8,128)(2,1)S(1)}, bf16[128,1024]{1,0:T(8,128)(2,1)S(1)}, u32[]{:S(2)}, u32[]{:S(2)}) collective-permute-start(bf16[128,1024]{1,0:T(8,128)(2,1)S(1)} %multiply_convert_fusion), channel_id=1, source_target_pairs={{0,6},{2,4},{4,2},{6,0},{8,14},{10,12},{12,10},{14,8},{16,22},{18,... | collective-permute-start | bytes 786440 | tf_op jit(solution)/shard_map/ppermute | solution.py:100
  98.7 12.5 %collective-permute-start.21 = (bf16[128,1024]{1,0:T(8,128)(2,1)S(1)}, bf16[128,1024]{1,0:T(8,128)(2,1)S(1)}, u32[]{:S(2)}, u32[]{:S(2)}) collective-permute-start(bf16[128,1024]{1,0:T(8,128)(2,1)S(1)} %multiply_convert_fusion), channel_id=1, source_target_pairs={{0,4},{2,6},{4,0},{6,2},{8,12},{10,14},{12,8},{14,10},{16,20},{18,... | collective-permute-start | bytes 786440 | tf_op jit(solution)/shard_map/ppermute | solution.py:100
  100.0 11.2 %collective-permute-start.20 = (bf16[128,1024]{1,0:T(8,128)(2,1)S(1)}, bf16[128,1024]{1,0:T(8,128)(2,1)S(1)}, u32[]{:S(2)}, u32[]{:S(2)}) collective-permute-start(bf16[128,1024]{1,0:T(8,128)(2,1)S(1)} %multiply_convert_fusion), channel_id=1, source_target_pairs={{0,2},{2,0},{4,6},{6,4},{8,10},{10,8},{12,14},{14,12},{16,18},{18,... | collective-permute-start | bytes 786440 | tf_op jit(solution)/shard_map/ppermute | solution.py:100
  101.1 10.3 %collective-permute-start.24 = (bf16[512,1024]{1,0:T(8,128)(2,1)S(1)}, bf16[512,1024]{1,0:T(8,128)(2,1)S(1)}, u32[]{:S(2)}, u32[]{:S(2)}) collective-permute-start(bf16[512,1024]{1,0:T(8,128)(2,1)S(1)} %constant_dynamic-update-slice_fusion.4.g_m), channel_id=1, source_target_pairs={{0,1},{1,0},{2,3},{3,2},{4,5},{5,4},{6,7},{7,6},{8,9},{9,8},{10,11... | collective-permute-start | bytes 3145736 | tf_op jit(solution)/shard_map/ppermute | solution.py:109
  111.3 2.9 %collective-permute-start.23 = (bf16[512,1024]{1,0:T(8,128)(2,1)S(1)}, bf16[512,1024]{1,0:T(8,128)(2,1)}, u32[]{:S(2)}, u32[]{:S(2)}) collective-permute-start(bf16[512,1024]{1,0:T(8,128)(2,1)S(1)} %pad_maximum_fusion.x_m), channel_id=1, source_target_pairs={{0,1},{1,0},{2,3},{3,2},{4,5},{5,4},{6,7},{7,6},{8,9},{9,8},{10,11... | collective-permute-start | bytes 3145736 | tf_op jit(solution)/shard_map/ppermute | solution.py:109
  133.3 93.8 %reduce-scatter.5.cloned.1.call-start = ((), (), s32[]{:S(2)}) async-start(), calls=%async_computation.4 | async-start | bytes 983040 | tf_op jit(solution)/shard_map/reduce_scatter | solution.py:891
  139.6 2.9 %collective-permute-start.25 = (bf16[512,1024]{1,0:T(8,128)(2,1)}, bf16[512,1024]{1,0:T(8,128)(2,1)S(1)}, u32[]{:S(2)}, u32[]{:S(2)}) collective-permute-start(bf16[512,1024]{1,0:T(8,128)(2,1)} %get-tuple-element.147), channel_id=1, source_target_pairs={{0,1},{1,0},{2,3},{3,2},{4,5},{5,4},{6,7},{7,6},{8,9},{9,8},{10,11... | collective-permute-start | bytes 3145736 | tf_op jit(solution)/shard_map/ppermute | solution.py:109
  146.1 9.9 %collective-permute-start.26 = (bf16[128,1024]{1,0:T(8,128)(2,1)}, bf16[128,1024]{1,0:T(8,128)(2,1)S(1)}, u32[]{:S(2)}, u32[]{:S(2)}) collective-permute-start(bf16[128,1024]{1,0:T(8,128)(2,1)} %get-tuple-element.153), channel_id=1, source_target_pairs={{0,2},{2,0},{4,6},{6,4},{8,10},{10,8},{12,14},{14,12},{16,18},{18,... | collective-permute-start | bytes 786440 | tf_op jit(solution)/shard_map/ppermute | solution.py:100
  147.6 13.9 %collective-permute-start.27 = (bf16[128,1024]{1,0:T(8,128)(2,1)}, bf16[128,1024]{1,0:T(8,128)(2,1)S(1)}, u32[]{:S(2)}, u32[]{:S(2)}) collective-permute-start(bf16[128,1024]{1,0:T(8,128)(2,1)} %get-tuple-element.154), channel_id=1, source_target_pairs={{0,4},{2,6},{4,0},{6,2},{8,12},{10,14},{12,8},{14,10},{16,20},{18,... | collective-permute-start | bytes 786440 | tf_op jit(solution)/shard_map/ppermute | solution.py:100
  149.1 12.4 %collective-permute-start.28 = (bf16[128,1024]{1,0:T(8,128)(2,1)}, bf16[128,1024]{1,0:T(8,128)(2,1)S(1)}, u32[]{:S(2)}, u32[]{:S(2)}) collective-permute-start(bf16[128,1024]{1,0:T(8,128)(2,1)} %get-tuple-element.155), channel_id=1, source_target_pairs={{0,6},{2,4},{4,2},{6,0},{8,14},{10,12},{12,10},{14,8},{16,22},{18,... | collective-permute-start | bytes 786440 | tf_op jit(solution)/shard_map/ppermute | solution.py:100
  162.6 10.2 %collective-permute-start.31 = (bf16[128,1024]{1,0:T(8,128)(2,1)S(1)}, bf16[128,1024]{1,0:T(8,128)(2,1)S(1)}, u32[]{:S(2)}, u32[]{:S(2)}) collective-permute-start(bf16[128,1024]{1,0:T(8,128)(2,1)S(1)} %get-tuple-element.211), channel_id=1, source_target_pairs={{0,6},{2,4},{4,2},{6,0},{8,14},{10,12},{12,10},{14,8},{16,22},{18,... | collective-permute-start | bytes 786440 | tf_op jit(solution)/shard_map/ppermute | solution.py:100
  164.1 12.3 %collective-permute-start.30 = (bf16[128,1024]{1,0:T(8,128)(2,1)S(1)}, bf16[128,1024]{1,0:T(8,128)(2,1)S(1)}, u32[]{:S(2)}, u32[]{:S(2)}) collective-permute-start(bf16[128,1024]{1,0:T(8,128)(2,1)S(1)} %get-tuple-element.211), channel_id=1, source_target_pairs={{0,4},{2,6},{4,0},{6,2},{8,12},{10,14},{12,8},{14,10},{16,20},{18,... | collective-permute-start | bytes 786440 | tf_op jit(solution)/shard_map/ppermute | solution.py:100
  165.3 11.2 %collective-permute-start.29 = (bf16[128,1024]{1,0:T(8,128)(2,1)S(1)}, bf16[128,1024]{1,0:T(8,128)(2,1)S(1)}, u32[]{:S(2)}, u32[]{:S(2)}) collective-permute-start(bf16[128,1024]{1,0:T(8,128)(2,1)S(1)} %get-tuple-element.211), channel_id=1, source_target_pairs={{0,2},{2,0},{4,6},{6,4},{8,10},{10,8},{12,14},{14,12},{16,18},{18,... | collective-permute-start | bytes 786440 | tf_op jit(solution)/shard_map/ppermute | solution.py:100
  166.1 10.6 %collective-permute-start.33 = (bf16[512,1024]{1,0:T(8,128)(2,1)S(1)}, bf16[512,1024]{1,0:T(8,128)(2,1)}, u32[]{:S(2)}, u32[]{:S(2)}) collective-permute-start(bf16[512,1024]{1,0:T(8,128)(2,1)S(1)} %copy-done.41), channel_id=1, source_target_pairs={{0,1},{1,0},{2,3},{3,2},{4,5},{5,4},{6,7},{7,6},{8,9},{9,8},{10,11... | collective-permute-start | bytes 3145736 | tf_op jit(solution)/shard_map/ppermute | solution.py:109
  176.6 3.0 %collective-permute-start.32 = (bf16[512,1024]{1,0:T(8,128)(2,1)S(1)}, bf16[512,1024]{1,0:T(8,128)(2,1)}, u32[]{:S(2)}, u32[]{:S(2)}) collective-permute-start(bf16[512,1024]{1,0:T(8,128)(2,1)S(1)} %pad_maximum_fusion.1.dh_m), channel_id=1, source_target_pairs={{0,1},{1,0},{2,3},{3,2},{4,5},{5,4},{6,7},{7,6},{8,9},{9,8},{10,11... | collective-permute-start | bytes 3145736 | tf_op jit(solution)/shard_map/ppermute | solution.py:109
  179.6 18.7 %collective-permute-start.34 = (bf16[128,1024]{1,0:T(8,128)(2,1)}, bf16[128,1024]{1,0:T(8,128)(2,1)S(1)}, u32[]{:S(2)}, u32[]{:S(2)}) collective-permute-start(bf16[128,1024]{1,0:T(8,128)(2,1)} %get-tuple-element.166), channel_id=1, source_target_pairs={{0,2},{2,0},{4,6},{6,4},{8,10},{10,8},{12,14},{14,12},{16,18},{18,... | collective-permute-start | bytes 786440 | tf_op jit(solution)/shard_map/ppermute | solution.py:100
  181.0 17.3 %collective-permute-start.35 = (bf16[128,1024]{1,0:T(8,128)(2,1)}, bf16[128,1024]{1,0:T(8,128)(2,1)}, u32[]{:S(2)}, u32[]{:S(2)}) collective-permute-start(bf16[128,1024]{1,0:T(8,128)(2,1)} %get-tuple-element.167), channel_id=1, source_target_pairs={{0,4},{2,6},{4,0},{6,2},{8,12},{10,14},{12,8},{14,10},{16,20},{18,... | collective-permute-start | bytes 786440 | tf_op jit(solution)/shard_map/ppermute | solution.py:100
  181.7 16.6 %collective-permute-start.36 = (bf16[128,1024]{1,0:T(8,128)(2,1)}, bf16[128,1024]{1,0:T(8,128)(2,1)}, u32[]{:S(2)}, u32[]{:S(2)}) collective-permute-start(bf16[128,1024]{1,0:T(8,128)(2,1)} %get-tuple-element.168), channel_id=1, source_target_pairs={{0,6},{2,4},{4,2},{6,0},{8,14},{10,12},{12,10},{14,8},{16,22},{18,... | collective-permute-start | bytes 786440 | tf_op jit(solution)/shard_map/ppermute | solution.py:100
  198.3 20.8 %copy-start.12 = (f32[128,1024]{1,0:T(8,128)S(1)}, f32[128,1024]{1,0:T(8,128)}, u32[]{:S(2)}) copy-start(f32[128,1024]{1,0:T(8,128)} %get-tuple-element.165) | copy-start | bytes 1572868
  198.3 8.6 %collective-permute-start.38 = (bf16[512,1024]{1,0:T(8,128)(2,1)}, bf16[512,1024]{1,0:T(8,128)(2,1)S(1)}, u32[]{:S(2)}, u32[]{:S(2)}) collective-permute-start(bf16[512,1024]{1,0:T(8,128)(2,1)} %get-tuple-element.184), channel_id=1, source_target_pairs={{0,1},{1,0},{2,3},{3,2},{4,5},{5,4},{6,7},{7,6},{8,9},{9,8},{10,11... | collective-permute-start | bytes 3145736 | tf_op jit(solution)/shard_map/ppermute | solution.py:109
  198.4 7.8 %collective-permute-start.42 = (f32[8,384]{1,0:T(8,128)}, f32[8,384]{1,0:T(8,128)S(1)}, u32[]{:S(2)}, u32[]{:S(2)}) collective-permute-start(f32[8,384]{1,0:T(8,128)} %get-tuple-element.193), channel_id=1, source_target_pairs={{0,1},{1,0},{2,3},{3,2},{4,5},{5,4},{6,7},{7,6},{8,9},{9,8},{10,11... | collective-permute-start | bytes 36872 | tf_op jit(solution)/shard_map/ppermute | solution.py:109
  202.8 10.9 %collective-permute-start.37 = (bf16[64,1792]{1,0:T(8,128)(2,1)}, bf16[64,1792]{1,0:T(8,128)(2,1)S(1)}, u32[]{:S(2)}, u32[]{:S(2)}) collective-permute-start(bf16[64,1792]{1,0:T(8,128)(2,1)} %get-tuple-element.170), channel_id=1, source_target_pairs={{0,2},{2,0},{4,6},{6,4},{8,10},{10,8},{12,14},{14,12},{16,18},{18,... | collective-permute-start | bytes 688136 | tf_op jit(solution)/shard_map/ppermute | solution.py:100
  204.2 12.8 %collective-permute-start.49 = (bf16[64,1792]{1,0:T(8,128)(2,1)}, bf16[64,1792]{1,0:T(8,128)(2,1)S(1)}, u32[]{:S(2)}, u32[]{:S(2)}) collective-permute-start(bf16[64,1792]{1,0:T(8,128)(2,1)} %get-tuple-element.172), channel_id=1, source_target_pairs={{0,4},{2,6},{4,0},{6,2},{8,12},{10,14},{12,8},{14,10},{16,20},{18,... | collective-permute-start | bytes 688136 | tf_op jit(solution)/shard_map/ppermute | solution.py:100
  205.7 12.8 %collective-permute-start.50 = (bf16[64,1792]{1,0:T(8,128)(2,1)}, bf16[64,1792]{1,0:T(8,128)(2,1)}, u32[]{:S(2)}, u32[]{:S(2)}) collective-permute-start(bf16[64,1792]{1,0:T(8,128)(2,1)} %get-tuple-element.173), channel_id=1, source_target_pairs={{0,6},{2,4},{4,2},{6,0},{8,14},{10,12},{12,10},{14,8},{16,22},{18,... | collective-permute-start | bytes 688136 | tf_op jit(solution)/shard_map/ppermute | solution.py:100
  207.0 20.2 %copy-start.34 = (f32[8,384]{1,0:T(8,128)}, f32[8,384]{1,0:T(8,128)S(1)}, u32[]{:S(2)}) copy-start(f32[8,384]{1,0:T(8,128)S(1)} %add.127.gains) | copy-start | bytes 36868
  210.7 22.2 %copy-start.5 = (f32[128,1024]{1,0:T(8,128)S(1)}, f32[128,1024]{1,0:T(8,128)}, u32[]{:S(2)}) copy-start(f32[128,1024]{1,0:T(8,128)} %get-tuple-element.189) | copy-start | bytes 1572868
  210.7 22.2 %copy-start.26 = (f32[1024]{0:T(1024)S(1)}, f32[1024]{0:T(1024)}, u32[]{:S(2)}) copy-start(f32[1024]{0:T(1024)} %param.16) | copy-start | bytes 12292
  210.7 4.8 %collective-permute-start.45 = (f32[8,384]{1,0:T(8,128)S(1)}, f32[8,384]{1,0:T(8,128)S(1)}, u32[]{:S(2)}, u32[]{:S(2)}) collective-permute-start(f32[8,384]{1,0:T(8,128)S(1)} %add.127.gains), channel_id=1, source_target_pairs={{0,24},{2,26},{4,28},{6,30},{8,0},{10,2},{12,4},{14,6},{16,8},{18,... | collective-permute-start | bytes 36872 | tf_op jit(solution)/shard_map/ppermute | solution.py:105
  213.1 14.1 %collective-permute-start.44 = (f32[8,384]{1,0:T(8,128)S(1)}, f32[8,384]{1,0:T(8,128)S(1)}, u32[]{:S(2)}, u32[]{:S(2)}) collective-permute-start(f32[8,384]{1,0:T(8,128)S(1)} %add.127.gains), channel_id=1, source_target_pairs={{0,16},{2,18},{4,20},{6,22},{8,24},{10,26},{12,28},{14,30},{16,0},... | collective-permute-start | bytes 36872 | tf_op jit(solution)/shard_map/ppermute | solution.py:105
  213.6 13.5 %collective-permute-start.43 = (f32[8,384]{1,0:T(8,128)S(1)}, f32[8,384]{1,0:T(8,128)S(1)}, u32[]{:S(2)}, u32[]{:S(2)}) collective-permute-start(f32[8,384]{1,0:T(8,128)S(1)} %add.127.gains), channel_id=1, source_target_pairs={{0,8},{2,10},{4,12},{6,14},{8,16},{10,18},{12,20},{14,22},{16,24},... | collective-permute-start | bytes 36872 | tf_op jit(solution)/shard_map/ppermute | solution.py:105
  215.6 11.6 %collective-permute-start.39 = (bf16[128,1024]{1,0:T(8,128)(2,1)}, bf16[128,1024]{1,0:T(8,128)(2,1)S(1)}, u32[]{:S(2)}, u32[]{:S(2)}) collective-permute-start(bf16[128,1024]{1,0:T(8,128)(2,1)} %get-tuple-element.190), channel_id=1, source_target_pairs={{0,2},{2,0},{4,6},{6,4},{8,10},{10,8},{12,14},{14,12},{16,18},{18,... | collective-permute-start | bytes 786440 | tf_op jit(solution)/shard_map/ppermute | solution.py:100
  217.0 15.9 %collective-permute-start.40 = (bf16[128,1024]{1,0:T(8,128)(2,1)}, bf16[128,1024]{1,0:T(8,128)(2,1)S(1)}, u32[]{:S(2)}, u32[]{:S(2)}) collective-permute-start(bf16[128,1024]{1,0:T(8,128)(2,1)} %get-tuple-element.191), channel_id=1, source_target_pairs={{0,4},{2,6},{4,0},{6,2},{8,12},{10,14},{12,8},{14,10},{16,20},{18,... | collective-permute-start | bytes 786440 | tf_op jit(solution)/shard_map/ppermute | solution.py:100
  218.5 14.4 %collective-permute-start.41 = (bf16[128,1024]{1,0:T(8,128)(2,1)}, bf16[128,1024]{1,0:T(8,128)(2,1)S(1)}, u32[]{:S(2)}, u32[]{:S(2)}) collective-permute-start(bf16[128,1024]{1,0:T(8,128)(2,1)} %get-tuple-element.192), channel_id=1, source_target_pairs={{0,6},{2,4},{4,2},{6,0},{8,14},{10,12},{12,10},{14,8},{16,22},{18,... | collective-permute-start | bytes 786440 | tf_op jit(solution)/shard_map/ppermute | solution.py:100
  229.5 4.9 %collective-permute-start.46 = (bf16[80,384]{1,0:T(8,128)(2,1)}, bf16[80,384]{1,0:T(8,128)(2,1)S(1)}, u32[]{:S(2)}, u32[]{:S(2)}) collective-permute-start(bf16[80,384]{1,0:T(8,128)(2,1)} %get-tuple-element.198), channel_id=1, source_target_pairs={{0,2},{2,0},{4,6},{6,4},{8,10},{10,8},{12,14},{14,12},{16,18},{18,... | collective-permute-start | bytes 184328 | tf_op jit(solution)/shard_map/ppermute | solution.py:100
  231.0 5.1 %collective-permute-start.47 = (bf16[80,384]{1,0:T(8,128)(2,1)}, bf16[80,384]{1,0:T(8,128)(2,1)S(1)}, u32[]{:S(2)}, u32[]{:S(2)}) collective-permute-start(bf16[80,384]{1,0:T(8,128)(2,1)} %get-tuple-element.199), channel_id=1, source_target_pairs={{0,4},{2,6},{4,0},{6,2},{8,12},{10,14},{12,8},{14,10},{16,20},{18,... | collective-permute-start | bytes 184328 | tf_op jit(solution)/shard_map/ppermute | solution.py:100
  232.4 5.3 %collective-permute-start.48 = (bf16[80,384]{1,0:T(8,128)(2,1)}, bf16[80,384]{1,0:T(8,128)(2,1)S(1)}, u32[]{:S(2)}, u32[]{:S(2)}) collective-permute-start(bf16[80,384]{1,0:T(8,128)(2,1)} %get-tuple-element.200), channel_id=1, source_target_pairs={{0,6},{2,4},{4,2},{6,0},{8,14},{10,12},{12,10},{14,8},{16,22},{18,... | collective-permute-start | bytes 184328 | tf_op jit(solution)/shard_map/ppermute | solution.py:100
  (32 other events, 184.4 us)
Sparse Core Ops, SparseCore 0:
  44.8 72.9 all-gather.1
  133.5 67.0 reduce-scatter.2
  202.8 24.2 reduce-scatter.4

commit v14 on v13

--- a/solution.py
+++ b/solution.py
@@ -201,26 +201,35 @@
 def unpack_attn_kernel(where_ref, own, one, two, three, attn_out, lens_out, held):
     rows = attn_out.shape[0] // PLANE
     width = attn_out.shape[1]
-    parts, _ = attn_rows(rows)
+    parts, high = attn_rows(rows)
     place = where_ref[0]
     for mask, message in enumerate((own, one, two, three)):
-        at = pl.ds(pl.multiple_of((place ^ mask) * rows, rows), rows)
-        values = [
-            message[:, part * width : (part + 1) * width].astype(float32) for part in range(parts)
-        ]
-        held[at, :] = jnp.concatenate(values, axis=0) if parts == 2 else values[0][:rows]
+        start = (place ^ mask) * rows
+        if parts == 2:
+            for part in range(parts):
+                at = pl.ds(pl.multiple_of(start + part * high, high), high)
+                attn_out[at, :] = message[:, part * width : (part + 1) * width]
+        else:
+            at = pl.ds(pl.multiple_of(start, rows), rows)
+            held[at, :] = message[:, :width].astype(float32)[:rows]
         lens = message[:16, message.shape[1] - LANES :].astype(float32)
         lens_out[mask * 8 : (mask + 1) * 8, :] = lens[:8]
-    attn_out[...] = held[...].astype(bfloat16)
+    if parts != 2:
+        attn_out[...] = held[...].astype(bfloat16)
 
 
 def unpack_ffn_kernel(where_ref, own, one, two, three, ffn_out, held):
     rows = ffn_out.shape[0] // PLANE
     place = where_ref[0]
+    direct = rows % 16 == 0
     for mask, message in enumerate((own, one, two, three)):
         at = pl.ds(pl.multiple_of((place ^ mask) * rows, rows), rows)
-        held[at, :] = message[...].astype(float32)[:rows]
-    ffn_out[...] = held[...].astype(bfloat16)
+        if direct:
+            ffn_out[at, :] = message[...]
+        else:
+            held[at, :] = message[...].astype(float32)[:rows]
+    if not direct:
+        ffn_out[...] = held[...].astype(bfloat16)
 
 
 def head_mean(values):
@@ -711,7 +720,9 @@
         out_d[:, span] = jnp.where(lane < HALF, low[:, LANES:], pltpu.roll(high[:, LANES:], HALF, 1))
 
 
-def place_attn_kernel(where_ref, own, one, two, three, out_q, out_k, out_v, out_o, out_gains):
+def place_attn_kernel(
+    where_ref, own, one, two, three, out_q, out_k, out_v, out_o, gain_a, gain_f, gain_q, gain_k
+):
     place = where_ref[0]
     refs = (own, one, two, three)
     rows = out_q.shape[0]
@@ -727,7 +738,12 @@
         out_k[:, span] = jnp.where(lane < HALF, low, pltpu.roll(high, HALF, 1))
         out_v[:, span] = jnp.where(lane < HALF, pltpu.roll(low, HALF, 1), high)
     tails = [joined_gains(ref[ref.shape[0] - 2 * GAIN_ROWS :, :].astype(float32)) for ref in refs]
-    out_gains[...] = (tails[0] + tails[1]) + (tails[2] + tails[3])
+    sums = (tails[0] + tails[1]) + (tails[2] + tails[3])
+    gain_a[...] = sums[:, :LANES]
+    gain_f[...] = sums[:, LANES : 2 * LANES]
+    pair = sums[:, 2 * LANES :]
+    gain_q[...] = pair[:1, :HALF]
+    gain_k[...] = pltpu.roll(pair, HALF, 1)[:1, :HALF]
 
 
 def plane_parts(local):
@@ -910,10 +926,11 @@
         scalars=1,
         scratch=[pltpu.VMEM((PLANE, rows, ff_cols), float32)],
     )
-    grad_query, grad_key, grad_value, grad_out_w, sums = call(
+    grad_query, grad_key, grad_value, grad_out_w, *sums = call(
         place_attn_kernel,
         [(w.shape, float32) for w in (w_query, w_key, w_value, w_out)]
-        + [((GAIN_ROWS, attn_cols), float32)],
+        + [((GAIN_ROWS, LANES), float32)] * 2
+        + [((1, HEAD_DIM), float32)] * 2,
         where,
         *attn_parts,
         scalars=1,
@@ -921,10 +938,10 @@
     return (
         block_out,
         grad_tokens,
-        sums[:, :LANES].reshape(-1),
-        sums[0, 2 * LANES : 2 * LANES + HEAD_DIM],
-        sums[0, 2 * LANES + HEAD_DIM :],
-        sums[:, LANES : 2 * LANES].reshape(-1),
+        sums[0].reshape(-1),
+        sums[2].reshape(-1),
+        sums[3].reshape(-1),
+        sums[1].reshape(-1),
         grad_query,
         grad_key,
         grad_value,

time: 250 us -> 247 us (0.988)
  local copies, waits for them, and re-layouts: 14 us -> 11.4 us
where the time goes in v14:
time: 247 us; the launch traced here: 246 us
  waiting for transfers between devices  78.6 us (32%)
  Pallas kernels  78.3 us (32%)
  starting transfers between devices  52.1 us (21%)
  between operations  14.2 us (6%)
  other arithmetic  11.8 us (5%)
  local copies, waits for them, and re-layouts  11.4 us (5%)
    ppermute x36, waiting for transfers between devices, send_plane(): return lax.ppermute(values, 'dp', [(i, i ^ mask) for i in range(count)])  53.3 us
    ppermute x36, starting transfers between devices, send_plane(): return lax.ppermute(values, 'dp', [(i, i ^ mask) for i in range(count)])  41.2 us
    pallas_call x12, Pallas kernels, call(): pl.pallas_call(kernel, out_shape=[jax.ShapeDtypeStruct(shape, kind) for s...  27.3 us
    pallas_call x1, Pallas kernels, ffn_layer(): pl.pallas_call(ffn_kernel, grid=(2,), in_specs=[scalar, scalar] + [row_sp...  15.5 us
    pallas_call x1, Pallas kernels, attn_back(): pl.pallas_call(attn_back_kernel, grid=(PLANE // GROUPS_STEP,), in_specs=[...  15.2 us
    pallas_call x2, Pallas kernels, ffn_apply(): pl.pallas_call(ffn_apply_kernel, grid=(2,), in_specs=[pl.BlockSpec((rows,...  10.4 us
    pallas_call x1, Pallas kernels, attn(): pl.pallas_call(lambda *refs: attn_kernel(layers, *refs), grid=(PLANE // G...  9.94 us
    ppermute x6, starting transfers between devices, send_deep(): lax.ppermute(values, 'dp', [(i, (i + PLANE * step) % count) for i in rang...  9.46 us
  transfers between devices with their start and end apart: 54, of which 23 were waited for; matrix products, arithmetic and copies ran while one was open for 5% of the time, Pallas kernels for 22%

profile of v14, /device:TPU:0, one launch (start us, length us, event | category | flops | bytes accessed | tf_op | source)
XLA Modules:
  0.0 246.4 jit_solution(9539379428473674276)
XLA Ops:
  7.9 1.7 shard_map.238
  9.6 2.9 %collective-permute-start = (bf16[32,1024]{1,0:T(8,128)(2,1)}, bf16[32,1024]{1,0:T(8,128)(2,1)S(1)}, u32[]{:S(2)}, u32[]{:S(2)}) collective-permute-start(bf16[32,1024]{1,0:T(8,128)(2,1)} %get-tuple-element.119), channel_id=1, source_target_pairs={{0,2},{2,0},{4,6},{6,4},{8,10},{10,8},{12,14},{14,12},{16,18},{18,... | collective-permute-start | bytes 196616 | tf_op jit(solution)/shard_map/ppermute | solution.py:100
  12.5 1.5 collective-permute-start.1
  14.0 2.2 shard_map.237
  17.0 2.4 collective-permute-done.2.three
  20.0 1.6 shard_map.239
  21.7 3.6 %collective-permute-start.5 = (bf16[256,384]{1,0:T(8,128)(2,1)}, bf16[256,384]{1,0:T(8,128)(2,1)S(1)}, u32[]{:S(2)}, u32[]{:S(2)}) collective-permute-start(bf16[256,384]{1,0:T(8,128)(2,1)} %get-tuple-element.137.refs_9_), channel_id=1, source_target_pairs={{0,24},{2,26},{4,28},{6,30},{8,0},{10,2},{12,4},{14,6},{16,8},{18,... | collective-permute-start | bytes 589832 | tf_op jit(solution)/shard_map/ppermute | solution.py:105
  28.4 2.6 %collective-permute-done.5.refs_12_ = bf16[256,384]{1,0:T(8,128)(2,1)S(1)} collective-permute-done((bf16[256,384]{1,0:T(8,128)(2,1)}, bf16[256,384]{1,0:T(8,128)(2,1)S(1)}, u32[]{:S(2)}, u32[]{:S(2)}) %collective-permute-start.5) | collective-permute-done | bytes 196640 | tf_op jit(solution)/shard_map/ppermute | solution.py:105
  31.5 3.0 %fusion.6 = (f32[1024,128]{1,0:T(8,128)}, f32[1024,128]{1,0:T(8,128)}) fusion(f32[128]{0:T(128)S(1)} %get-tuple-element.225, f32[128]{0:T(128)S(1)} %get-tuple-element.226, f32[1024]{0:T(1024)S(1)} %bitcast.24), kind=kLoop, calls=%fused_computation.13 | loop fusion | flops 262144 | bytes 1053696 | tf_op jit(solution)/shard_map/mul | solution.py:774
  34.5 6.7 %collective-permute-done.4.refs_11_ = bf16[256,384]{1,0:T(8,128)(2,1)S(1)} collective-permute-done((bf16[256,384]{1,0:T(8,128)(2,1)}, bf16[256,384]{1,0:T(8,128)(2,1)S(1)}, u32[]{:S(2)}, u32[]{:S(2)}) %collective-permute-start.4) | collective-permute-done | bytes 196640 | tf_op jit(solution)/shard_map/ppermute | solution.py:105
  42.1 2.3 shard_map.240
  45.6 2.4 collective-permute-start.11
  48.1 5.7 %collective-permute-done.9 = bf16[128,1024]{1,0:T(8,128)(2,1)S(1)} collective-permute-done((bf16[128,1024]{1,0:T(8,128)(2,1)S(1)}, bf16[128,1024]{1,0:T(8,128)(2,1)S(1)}, u32[]{:S(2)}, u32[]{:S(2)}) %collective-permute-start.9) | collective-permute-done | bytes 262176 | tf_op jit(solution)/shard_map/ppermute | solution.py:100
  53.9 3.5 %collective-permute-done.10 = bf16[128,1024]{1,0:T(8,128)(2,1)S(1)} collective-permute-done((bf16[128,1024]{1,0:T(8,128)(2,1)S(1)}, bf16[128,1024]{1,0:T(8,128)(2,1)S(1)}, u32[]{:S(2)}, u32[]{:S(2)}) %collective-permute-start.10) | collective-permute-done | bytes 262176 | tf_op jit(solution)/shard_map/ppermute | solution.py:100
  57.6 1.2 collective-permute-start.15
  58.8 1.4 collective-permute-start.14
  62.7 9.9 %shard_map.241 = (bf16[512,1024]{1,0:T(8,128)(2,1)}, bf16[512,1024]{1,0:T(8,128)(2,1)}, f32[1024,256]{1,0:T(8,128)}, bf16[1024,256]{1,0:T(8,128)(2,1)}, bf16[102...) custom-call(s32[3]{0:T(128)} %pad_add_fusion.where_ref.refs_0_, s32[4,4]{1,0:T(4,128)} %copy-done.33, ...), custom_call_target="tpu_custom_call" | custom-call | flops 1024 | bytes 36000000 | tf_op jit(solution)/shard_map/pallas_call | solution.py:434
  74.3 2.8 %collective-permute-done.16.received = bf16[512,1024]{1,0:T(8,128)(2,1)S(1)} collective-permute-done((bf16[512,1024]{1,0:T(8,128)(2,1)}, bf16[512,1024]{1,0:T(8,128)(2,1)S(1)}, u32[]{:S(2)}, u32[]{:S(2)}) %collective-permute-start.16) | collective-permute-done | bytes 1048608 | tf_op jit(solution)/shard_map/ppermute | solution.py:109
  78.0 2.7 %shard_map.242 = (f32[128,1024]{1,0:T(8,128)}, bf16[128,1024]{1,0:T(8,128)(2,1)}, bf16[128,1024]{1,0:T(8,128)(2,1)}, bf16[128,1024]{1,0:T(8,128)(2,1)}) custom-call(bf16[512,1024]{1,0:T(8,128)(2,1)} %get-tuple-element.141.keep, bf16[512,1024]{1,0:T(8,128)(2,1)} %copy-done.11), custom_call_target="tpu_custom_call" | custom-call | flops 1024 | bytes 1024 | tf_op jit(solution)/shard_map/pallas_call | solution.py:115
  82.5 1.8 collective-permute-start.19
  84.2 5.9 %collective-permute-done.17 = bf16[128,1024]{1,0:T(8,128)(2,1)S(1)} collective-permute-done((bf16[128,1024]{1,0:T(8,128)(2,1)}, bf16[128,1024]{1,0:T(8,128)(2,1)S(1)}, u32[]{:S(2)}, u32[]{:S(2)}) %collective-permute-start.17) | collective-permute-done | bytes 262176 | tf_op jit(solution)/shard_map/ppermute | solution.py:100
  90.1 5.6 %collective-permute-done.18 = bf16[128,1024]{1,0:T(8,128)(2,1)S(1)} collective-permute-done((bf16[128,1024]{1,0:T(8,128)(2,1)}, bf16[128,1024]{1,0:T(8,128)(2,1)S(1)}, u32[]{:S(2)}, u32[]{:S(2)}) %collective-permute-start.18) | collective-permute-done | bytes 262176 | tf_op jit(solution)/shard_map/ppermute | solution.py:100
  95.7 1.3 multiply_reduce_fusion.2
  97.1 1.2 collective-permute-start.22
  98.4 1.3 collective-permute-start.21
  100.9 6.5 %collective-permute-done.22 = bf16[128,1024]{1,0:T(8,128)(2,1)S(1)} collective-permute-done((bf16[128,1024]{1,0:T(8,128)(2,1)S(1)}, bf16[128,1024]{1,0:T(8,128)(2,1)S(1)}, u32[]{:S(2)}, u32[]{:S(2)}) %collective-permute-start.22) | collective-permute-done | bytes 262176 | tf_op jit(solution)/shard_map/ppermute | solution.py:100
  107.4 3.5 %collective-permute-done.21 = bf16[128,1024]{1,0:T(8,128)(2,1)S(1)} collective-permute-done((bf16[128,1024]{1,0:T(8,128)(2,1)S(1)}, bf16[128,1024]{1,0:T(8,128)(2,1)S(1)}, u32[]{:S(2)}, u32[]{:S(2)}) %collective-permute-start.21) | collective-permute-done | bytes 262176 | tf_op jit(solution)/shard_map/ppermute | solution.py:100
  112.2 1.5 collective-permute-done.23.x_o
  113.8 3.9 %all-gather.2.cloned.1.call-done.weight.small = bf16[1024,1792]{1,0:T(8,128)(2,1)} async-done(((bf16[256,1792]{1,0:T(8,128)(2,1)}), bf16[1024,1792]{1,0:T(8,128)(2,1)}) %all-gather.2.cloned.1.call-update) | async-done | bytes 3670032 | tf_op jit(solution)/shard_map/all_gather | solution.py:852
  117.6 15.5 %shard_map.243 = (bf16[1024,640]{1,0:T(8,128)(2,1)}, bf16[1024,1152]{1,0:T(8,128)(2,1)}, bf16[1024,1792]{1,0:T(8,128)(2,1)}) custom-call(s32[3]{0:T(128)} %pad_add_fusion.where_ref.refs_0_, s32[4,4]{1,0:T(4,128)} %copy-done.33, bf16[512,1024]{1,0:T(8,128)(2,1)} %collective-permute-done.23.x_o, bf16[512,1024]{1,0:T(8,128)(2,1)} %copy-done.3, ...), custom_call_target="tpu_custom_call" | custom-call | flops 1024 | bytes 48000000 | tf_op jit(solution)/shard_map/pallas_call | solution.py:552
  133.4 5.9 %shard_map.244 = (bf16[512,1024]{1,0:T(8,128)(2,1)}, bf16[512,1024]{1,0:T(8,128)(2,1)}) custom-call(bf16[1024,1152]{1,0:T(8,128)(2,1)} %get-tuple-element.149.values, bf16[1024,1792]{1,0:T(8,128)(2,1)} %all-gather.2.cloned.1.call-done.weight.small, bf16[1024,1792]{1,0:T(8,128)(2,1)} %all-gather.2.cloned.1.call-done.weight.small), custom_call_target="tpu_custom_call" | custom-call | flops 1024 | bytes 14000000 | tf_op jit(solution)/shard_map/pallas_call | solution.py:585
  139.3 2.9 %collective-permute-done.25.received = bf16[512,1024]{1,0:T(8,128)(2,1)S(1)} collective-permute-done((bf16[512,1024]{1,0:T(8,128)(2,1)}, bf16[512,1024]{1,0:T(8,128)(2,1)S(1)}, u32[]{:S(2)}, u32[]{:S(2)}) %collective-permute-start.25) | collective-permute-done | bytes 1048608 | tf_op jit(solution)/shard_map/ppermute | solution.py:109
  143.2 2.6 %shard_map.246 = (f32[128,1024]{1,0:T(8,128)}, bf16[128,1024]{1,0:T(8,128)(2,1)}, bf16[128,1024]{1,0:T(8,128)(2,1)}, bf16[128,1024]{1,0:T(8,128)(2,1)}) custom-call(bf16[512,1024]{1,0:T(8,128)(2,1)} %get-tuple-element.154.keep, bf16[512,1024]{1,0:T(8,128)(2,1)} %copy-done.10), custom_call_target="tpu_custom_call" | custom-call | flops 1024 | bytes 1024 | tf_op jit(solution)/shard_map/pallas_call | solution.py:115
  145.9 1.5 collective-permute-start.26
  147.4 1.5 collective-permute-start.27
  149.4 1.3 slice.7
  151.3 4.5 %shard_map.245 = (bf16[512,1024]{1,0:T(8,128)(2,1)}, bf16[512,1024]{1,0:T(8,128)(2,1)}) custom-call(bf16[1024,640]{1,0:T(8,128)(2,1)} %get-tuple-element.152.values, bf16[1024,1792]{1,0:T(8,128)(2,1)} %all-gather.2.cloned.1.call-done.weight.small, bf16[1024,1792]{1,0:T(8,128)(2,1)} %all-gather.2.cloned.1.call-done.weight.small), custom_call_target="tpu_custom_call" | custom-call | flops 1024 | bytes 14000000 | tf_op jit(solution)/shard_map/pallas_call | solution.py:585
  155.8 5.5 %collective-permute-done.27 = bf16[128,1024]{1,0:T(8,128)(2,1)S(1)} collective-permute-done((bf16[128,1024]{1,0:T(8,128)(2,1)}, bf16[128,1024]{1,0:T(8,128)(2,1)S(1)}, u32[]{:S(2)}, u32[]{:S(2)}) %collective-permute-start.27) | collective-permute-done | bytes 262176 | tf_op jit(solution)/shard_map/ppermute | solution.py:100
  162.3 1.5 collective-permute-start.31
  163.9 1.2 collective-permute-start.30
  165.9 6.7 %collective-permute-done.31 = bf16[128,1024]{1,0:T(8,128)(2,1)S(1)} collective-permute-done((bf16[128,1024]{1,0:T(8,128)(2,1)S(1)}, bf16[128,1024]{1,0:T(8,128)(2,1)S(1)}, u32[]{:S(2)}, u32[]{:S(2)}) %collective-permute-start.31) | collective-permute-done | bytes 262176 | tf_op jit(solution)/shard_map/ppermute | solution.py:100
  172.6 3.6 %collective-permute-done.30 = bf16[128,1024]{1,0:T(8,128)(2,1)S(1)} collective-permute-done((bf16[128,1024]{1,0:T(8,128)(2,1)S(1)}, bf16[128,1024]{1,0:T(8,128)(2,1)S(1)}, u32[]{:S(2)}, u32[]{:S(2)}) %collective-permute-start.30) | collective-permute-done | bytes 262176 | tf_op jit(solution)/shard_map/ppermute | solution.py:100
  176.5 2.9 %shard_map.247 = (f32[128,1024]{1,0:T(8,128)}, bf16[128,1024]{1,0:T(8,128)(2,1)}, bf16[128,1024]{1,0:T(8,128)(2,1)}, bf16[128,1024]{1,0:T(8,128)(2,1)}) custom-call(bf16[512,1024]{1,0:T(8,128)(2,1)} %get-tuple-element.163.keep, bf16[512,1024]{1,0:T(8,128)(2,1)} %collective-permute-done.33.received), custom_call_target="tpu_custom_call" | custom-call | flops 1024 | bytes 1024 | tf_op jit(solution)/shard_map/pallas_call | solution.py:115
  179.4 1.3 collective-permute-start.34
  181.4 1.5 collective-permute-start.36
  182.9 15.2 %shard_map.249 = (bf16[512,1024]{1,0:T(8,128)(2,1)}, bf16[512,1024]{1,0:T(8,128)(2,1)}, bf16[1024,384]{1,0:T(8,128)(2,1)}, f32[8,384]{1,0:T(8,128)}) custom-call(s32[3]{0:T(128)} %pad_add_fusion.where_ref.refs_0_, s32[4,4]{1,0:T(4,128)} %copy-done.33, bf16[512,1024]{1,0:T(8,128)(2,1)} %copy-done, bf16[512,1024]{1,0:T(8,128)(2,1)} %copy-done.1, ...), custom_call_target="tpu_custom_call" | custom-call | flops 1024 | bytes 24000000 | tf_op jit(solution)/shard_map/pallas_call | solution.py:460
  198.7 1.6 reduce-scatter.3.cloned.1.call-done.own
  200.3 2.2 shard_map.248
  202.6 1.5 collective-permute-start.37
  204.0 1.5 collective-permute-start.49
  207.8 2.8 %shard_map.250 = (f32[128,1024]{1,0:T(8,128)}, bf16[128,1024]{1,0:T(8,128)(2,1)}, bf16[128,1024]{1,0:T(8,128)(2,1)}, bf16[128,1024]{1,0:T(8,128)(2,1)}) custom-call(bf16[512,1024]{1,0:T(8,128)(2,1)} %get-tuple-element.186.keep, bf16[512,1024]{1,0:T(8,128)(2,1)} %copy-done.9), custom_call_target="tpu_custom_call" | custom-call | flops 1024 | bytes 1024 | tf_op jit(solution)/shard_map/pallas_call | solution.py:115
  210.5 2.3 collective-permute-start.45
  213.4 1.9 collective-permute-start.43
  215.4 1.5 collective-permute-start.39
  216.9 1.5 collective-permute-start.40
  218.9 1.9 add_convert_fusion
  220.8 2.7 %shard_map.253 = (f32[64,2304]{1,0:T(8,128)}, f32[64,2304]{1,0:T(8,128)}, f32[64,2304]{1,0:T(8,128)}) custom-call(s32[3]{0:T(128)} %pad_add_fusion.where_ref.refs_0_, bf16[64,1792]{1,0:T(8,128)(2,1)} %get-tuple-element.174.own, bf16[64,1792]{1,0:T(8,128)(2,1)} %copy-done.18, bf16[64,1792]{1,0:T(8,128)(2,1)} %copy-done.19, ...), custom_call_target="tpu_custom_call" | custom-call | flops 1024 | bytes 1024 | tf_op jit(solution)/shard_map/pallas_call | solution.py:115
  223.5 3.4 %reduce-scatter.5.cloned.1.call-done.own = bf16[256,384]{1,0:T(8,128)(2,1)} async-done(((bf16[1024,384]{1,0:T(8,128)(2,1)}), bf16[256,384]{1,0:T(8,128)(2,1)}) %reduce-scatter.5.cloned.1.call-update) | async-done | bytes 196624 | tf_op jit(solution)/shard_map/reduce_scatter | solution.py:907
  227.6 1.7 shard_map.251
  229.3 1.5 collective-permute-start.46
  230.8 1.5 collective-permute-start.47
  234.1 1.7 collective-permute-done.47.two
  235.8 1.7 collective-permute-done.48.three
  238.2 1.7 shard_map.252
  (182 shorter events, 29.8 us)
Async XLA Ops:
  7.2 110.4 %all-gather.2.cloned.1.call-start = ((), (), s32[]{:S(2)}) async-start(), calls=%async_computation.2 | async-start | bytes 4587520 | tf_op jit(solution)/shard_map/all_gather | solution.py:852
  9.6 6.7 %collective-permute-start = (bf16[32,1024]{1,0:T(8,128)(2,1)}, bf16[32,1024]{1,0:T(8,128)(2,1)S(1)}, u32[]{:S(2)}, u32[]{:S(2)}) collective-permute-start(bf16[32,1024]{1,0:T(8,128)(2,1)} %get-tuple-element.119), channel_id=1, source_target_pairs={{0,2},{2,0},{4,6},{6,4},{8,10},{10,8},{12,14},{14,12},{16,18},{18,... | collective-permute-start | bytes 196616 | tf_op jit(solution)/shard_map/ppermute | solution.py:100
  12.5 4.5 %collective-permute-start.1 = (bf16[32,1024]{1,0:T(8,128)(2,1)}, bf16[32,1024]{1,0:T(8,128)(2,1)S(1)}, u32[]{:S(2)}, u32[]{:S(2)}) collective-permute-start(bf16[32,1024]{1,0:T(8,128)(2,1)} %get-tuple-element.120), channel_id=1, source_target_pairs={{0,4},{2,6},{4,0},{6,2},{8,12},{10,14},{12,8},{14,10},{16,20},{18,... | collective-permute-start | bytes 196616 | tf_op jit(solution)/shard_map/ppermute | solution.py:100
  14.0 5.4 %collective-permute-start.2 = (bf16[32,1024]{1,0:T(8,128)(2,1)}, bf16[32,1024]{1,0:T(8,128)(2,1)S(1)}, u32[]{:S(2)}, u32[]{:S(2)}) collective-permute-start(bf16[32,1024]{1,0:T(8,128)(2,1)} %get-tuple-element.121), channel_id=1, source_target_pairs={{0,6},{2,4},{4,2},{6,0},{8,14},{10,12},{12,10},{14,8},{16,22},{18,... | collective-permute-start | bytes 196616 | tf_op jit(solution)/shard_map/ppermute | solution.py:100
  16.2 28.3 %copy-start.4 = (bf16[128,1024]{1,0:T(8,128)(2,1)S(1)}, bf16[128,1024]{1,0:T(8,128)(2,1)}, u32[]{:S(2)}) copy-start(bf16[128,1024]{1,0:T(8,128)(2,1)} %param.14) | copy-start | bytes 786436
  21.7 9.3 %collective-permute-start.5 = (bf16[256,384]{1,0:T(8,128)(2,1)}, bf16[256,384]{1,0:T(8,128)(2,1)S(1)}, u32[]{:S(2)}, u32[]{:S(2)}) collective-permute-start(bf16[256,384]{1,0:T(8,128)(2,1)} %get-tuple-element.137.refs_9_), channel_id=1, source_target_pairs={{0,24},{2,26},{4,28},{6,30},{8,0},{10,2},{12,4},{14,6},{16,8},{18,... | collective-permute-start | bytes 589832 | tf_op jit(solution)/shard_map/ppermute | solution.py:105
  25.3 15.9 %collective-permute-start.4 = (bf16[256,384]{1,0:T(8,128)(2,1)}, bf16[256,384]{1,0:T(8,128)(2,1)S(1)}, u32[]{:S(2)}, u32[]{:S(2)}) collective-permute-start(bf16[256,384]{1,0:T(8,128)(2,1)} %get-tuple-element.137.refs_9_), channel_id=1, source_target_pairs={{0,16},{2,18},{4,20},{6,22},{8,24},{10,26},{12,28},{14,30},{16,0},... | collective-permute-start | bytes 589832 | tf_op jit(solution)/shard_map/ppermute | solution.py:105
  25.3 15.9 %collective-permute-start.3 = (bf16[256,384]{1,0:T(8,128)(2,1)}, bf16[256,384]{1,0:T(8,128)(2,1)S(1)}, u32[]{:S(2)}, u32[]{:S(2)}) collective-permute-start(bf16[256,384]{1,0:T(8,128)(2,1)} %get-tuple-element.137.refs_9_), channel_id=1, source_target_pairs={{0,8},{2,10},{4,12},{6,14},{8,16},{10,18},{12,20},{14,22},{16,24},... | collective-permute-start | bytes 589832 | tf_op jit(solution)/shard_map/ppermute | solution.py:105
  27.2 20.9 %copy-start.33 = (s32[4,4]{1,0:T(4,128)}, s32[4,4]{1,0:T(4,128)S(1)}, u32[]{:S(2)}) copy-start(s32[4,4]{1,0:T(4,128)S(1)} %reduce_window_sum.11.refs_1_.ends_ref) | copy-start | bytes 196
  27.3 13.9 %collective-permute-start.6 = (bf16[64,1792]{1,0:T(8,128)(2,1)}, bf16[64,1792]{1,0:T(8,128)(2,1)S(1)}, u32[]{:S(2)}, u32[]{:S(2)}) collective-permute-start(bf16[64,1792]{1,0:T(8,128)(2,1)} %get-tuple-element.129), channel_id=1, source_target_pairs={{0,2},{2,0},{4,6},{6,4},{8,10},{10,8},{12,14},{14,12},{16,18},{18,... | collective-permute-start | bytes 688136 | tf_op jit(solution)/shard_map/ppermute | solution.py:100
  27.9 13.3 %collective-permute-start.7 = (bf16[64,1792]{1,0:T(8,128)(2,1)}, bf16[64,1792]{1,0:T(8,128)(2,1)S(1)}, u32[]{:S(2)}, u32[]{:S(2)}) collective-permute-start(bf16[64,1792]{1,0:T(8,128)(2,1)} %get-tuple-element.130), channel_id=1, source_target_pairs={{0,4},{2,6},{4,0},{6,2},{8,12},{10,14},{12,8},{14,10},{16,20},{18,... | collective-permute-start | bytes 688136 | tf_op jit(solution)/shard_map/ppermute | solution.py:100
  31.0 10.3 %collective-permute-start.8 = (bf16[64,1792]{1,0:T(8,128)(2,1)}, bf16[64,1792]{1,0:T(8,128)(2,1)S(1)}, u32[]{:S(2)}, u32[]{:S(2)}) collective-permute-start(bf16[64,1792]{1,0:T(8,128)(2,1)} %get-tuple-element.131), channel_id=1, source_target_pairs={{0,6},{2,4},{4,2},{6,0},{8,14},{10,12},{12,10},{14,8},{16,22},{18,... | collective-permute-start | bytes 688136 | tf_op jit(solution)/shard_map/ppermute | solution.py:100
  41.2 20.5 %copy-start.24 = (bf16[256,384]{1,0:T(8,128)(2,1)}, bf16[256,384]{1,0:T(8,128)(2,1)S(1)}, u32[]{:S(2)}) copy-start(bf16[256,384]{1,0:T(8,128)(2,1)S(1)} %collective-permute-done.4.refs_11_) | copy-start | bytes 589828
  41.2 20.5 %copy-start.25 = (bf16[256,384]{1,0:T(8,128)(2,1)}, bf16[256,384]{1,0:T(8,128)(2,1)S(1)}, u32[]{:S(2)}) copy-start(bf16[256,384]{1,0:T(8,128)(2,1)S(1)} %collective-permute-done.3.refs_10_) | copy-start | bytes 589828
  44.5 155.8 %reduce-scatter.3.cloned.1.call-start = ((), (), s32[]{:S(2)}) async-start(), calls=%async_computation.3 | async-start | bytes 4587520 | tf_op jit(solution)/shard_map/reduce_scatter | solution.py:880
  44.5 9.3 %collective-permute-start.9 = (bf16[128,1024]{1,0:T(8,128)(2,1)S(1)}, bf16[128,1024]{1,0:T(8,128)(2,1)S(1)}, u32[]{:S(2)}, u32[]{:S(2)}) collective-permute-start(bf16[128,1024]{1,0:T(8,128)(2,1)S(1)} %copy-done.4), channel_id=1, source_target_pairs={{0,2},{2,0},{4,6},{6,4},{8,10},{10,8},{12,14},{14,12},{16,18},{18,... | collective-permute-start | bytes 786440 | tf_op jit(solution)/shard_map/ppermute | solution.py:100
  45.1 12.3 %collective-permute-start.10 = (bf16[128,1024]{1,0:T(8,128)(2,1)S(1)}, bf16[128,1024]{1,0:T(8,128)(2,1)S(1)}, u32[]{:S(2)}, u32[]{:S(2)}) collective-permute-start(bf16[128,1024]{1,0:T(8,128)(2,1)S(1)} %copy-done.4), channel_id=1, source_target_pairs={{0,4},{2,6},{4,0},{6,2},{8,12},{10,14},{12,8},{14,10},{16,20},{18,... | collective-permute-start | bytes 786440 | tf_op jit(solution)/shard_map/ppermute | solution.py:100
  45.6 11.8 %collective-permute-start.11 = (bf16[128,1024]{1,0:T(8,128)(2,1)S(1)}, bf16[128,1024]{1,0:T(8,128)(2,1)S(1)}, u32[]{:S(2)}, u32[]{:S(2)}) collective-permute-start(bf16[128,1024]{1,0:T(8,128)(2,1)S(1)} %copy-done.4), channel_id=1, source_target_pairs={{0,6},{2,4},{4,2},{6,0},{8,14},{10,12},{12,10},{14,8},{16,22},{18,... | collective-permute-start | bytes 786440 | tf_op jit(solution)/shard_map/ppermute | solution.py:100
  57.5 4.2 %collective-permute-start.12 = (bf16[512,1024]{1,0:T(8,128)(2,1)S(1)}, bf16[512,1024]{1,0:T(8,128)(2,1)S(1)}, u32[]{:S(2)}, u32[]{:S(2)}) collective-permute-start(bf16[512,1024]{1,0:T(8,128)(2,1)S(1)} %constant_dynamic-update-slice_fusion.refs_2_.tok_m), channel_id=1, source_target_pairs={{0,1},{1,0},{2,3},{3,2},{4,5},{5,4},{6,7},{7,6},{8,9},{9,8},{10,11... | collective-permute-start | bytes 3145736 | tf_op jit(solution)/shard_map/ppermute | solution.py:109
  57.6 15.1 %collective-permute-start.15 = (bf16[128,1024]{1,0:T(8,128)(2,1)S(1)}, bf16[128,1024]{1,0:T(8,128)(2,1)S(1)}, u32[]{:S(2)}, u32[]{:S(2)}) collective-permute-start(bf16[128,1024]{1,0:T(8,128)(2,1)S(1)} %copy-done.8), channel_id=1, source_target_pairs={{0,6},{2,4},{4,2},{6,0},{8,14},{10,12},{12,10},{14,8},{16,22},{18,... | collective-permute-start | bytes 786440 | tf_op jit(solution)/shard_map/ppermute | solution.py:100
  58.8 14.0 %collective-permute-start.14 = (bf16[128,1024]{1,0:T(8,128)(2,1)S(1)}, bf16[128,1024]{1,0:T(8,128)(2,1)S(1)}, u32[]{:S(2)}, u32[]{:S(2)}) collective-permute-start(bf16[128,1024]{1,0:T(8,128)(2,1)S(1)} %copy-done.8), channel_id=1, source_target_pairs={{0,4},{2,6},{4,0},{6,2},{8,12},{10,14},{12,8},{14,10},{16,20},{18,... | collective-permute-start | bytes 786440 | tf_op jit(solution)/shard_map/ppermute | solution.py:100
  60.2 12.6 %collective-permute-start.13 = (bf16[128,1024]{1,0:T(8,128)(2,1)S(1)}, bf16[128,1024]{1,0:T(8,128)(2,1)S(1)}, u32[]{:S(2)}, u32[]{:S(2)}) collective-permute-start(bf16[128,1024]{1,0:T(8,128)(2,1)S(1)} %copy-done.8), channel_id=1, source_target_pairs={{0,2},{2,0},{4,6},{6,4},{8,10},{10,8},{12,14},{14,12},{16,18},{18,... | collective-permute-start | bytes 786440 | tf_op jit(solution)/shard_map/ppermute | solution.py:100
  74.2 2.9 %collective-permute-start.16 = (bf16[512,1024]{1,0:T(8,128)(2,1)}, bf16[512,1024]{1,0:T(8,128)(2,1)S(1)}, u32[]{:S(2)}, u32[]{:S(2)}) collective-permute-start(bf16[512,1024]{1,0:T(8,128)(2,1)} %get-tuple-element.144), channel_id=1, source_target_pairs={{0,1},{1,0},{2,3},{3,2},{4,5},{5,4},{6,7},{7,6},{8,9},{9,8},{10,11... | collective-permute-start | bytes 3145736 | tf_op jit(solution)/shard_map/ppermute | solution.py:109
  80.7 20.0 %copy-start.17 = (bf16[128,1024]{1,0:T(8,128)(2,1)S(1)}, bf16[128,1024]{1,0:T(8,128)(2,1)}, u32[]{:S(2)}) copy-start(bf16[128,1024]{1,0:T(8,128)(2,1)} %copy-done.16) | copy-start | bytes 786436
  80.7 20.0 %copy-start.15 = (bf16[128,1024]{1,0:T(8,128)(2,1)S(1)}, bf16[128,1024]{1,0:T(8,128)(2,1)}, u32[]{:S(2)}) copy-start(bf16[128,1024]{1,0:T(8,128)(2,1)} %copy-done.14) | copy-start | bytes 786436
  80.7 9.4 %collective-permute-start.17 = (bf16[128,1024]{1,0:T(8,128)(2,1)}, bf16[128,1024]{1,0:T(8,128)(2,1)S(1)}, u32[]{:S(2)}, u32[]{:S(2)}) collective-permute-start(bf16[128,1024]{1,0:T(8,128)(2,1)} %get-tuple-element.146), channel_id=1, source_target_pairs={{0,2},{2,0},{4,6},{6,4},{8,10},{10,8},{12,14},{14,12},{16,18},{18,... | collective-permute-start | bytes 786440 | tf_op jit(solution)/shard_map/ppermute | solution.py:100
  81.7 13.9 %collective-permute-start.18 = (bf16[128,1024]{1,0:T(8,128)(2,1)}, bf16[128,1024]{1,0:T(8,128)(2,1)S(1)}, u32[]{:S(2)}, u32[]{:S(2)}) collective-permute-start(bf16[128,1024]{1,0:T(8,128)(2,1)} %get-tuple-element.147), channel_id=1, source_target_pairs={{0,4},{2,6},{4,0},{6,2},{8,12},{10,14},{12,8},{14,10},{16,20},{18,... | collective-permute-start | bytes 786440 | tf_op jit(solution)/shard_map/ppermute | solution.py:100
  82.5 13.2 %collective-permute-start.19 = (bf16[128,1024]{1,0:T(8,128)(2,1)}, bf16[128,1024]{1,0:T(8,128)(2,1)S(1)}, u32[]{:S(2)}, u32[]{:S(2)}) collective-permute-start(bf16[128,1024]{1,0:T(8,128)(2,1)} %get-tuple-element.148), channel_id=1, source_target_pairs={{0,6},{2,4},{4,2},{6,0},{8,14},{10,12},{12,10},{14,8},{16,22},{18,... | collective-permute-start | bytes 786440 | tf_op jit(solution)/shard_map/ppermute | solution.py:100
  97.1 10.2 %collective-permute-start.22 = (bf16[128,1024]{1,0:T(8,128)(2,1)S(1)}, bf16[128,1024]{1,0:T(8,128)(2,1)S(1)}, u32[]{:S(2)}, u32[]{:S(2)}) collective-permute-start(bf16[128,1024]{1,0:T(8,128)(2,1)S(1)} %multiply_convert_fusion), channel_id=1, source_target_pairs={{0,6},{2,4},{4,2},{6,0},{8,14},{10,12},{12,10},{14,8},{16,22},{18,... | collective-permute-start | bytes 786440 | tf_op jit(solution)/shard_map/ppermute | solution.py:100
  98.4 12.5 %collective-permute-start.21 = (bf16[128,1024]{1,0:T(8,128)(2,1)S(1)}, bf16[128,1024]{1,0:T(8,128)(2,1)S(1)}, u32[]{:S(2)}, u32[]{:S(2)}) collective-permute-start(bf16[128,1024]{1,0:T(8,128)(2,1)S(1)} %multiply_convert_fusion), channel_id=1, source_target_pairs={{0,4},{2,6},{4,0},{6,2},{8,12},{10,14},{12,8},{14,10},{16,20},{18,... | collective-permute-start | bytes 786440 | tf_op jit(solution)/shard_map/ppermute | solution.py:100
  99.7 11.2 %collective-permute-start.20 = (bf16[128,1024]{1,0:T(8,128)(2,1)S(1)}, bf16[128,1024]{1,0:T(8,128)(2,1)S(1)}, u32[]{:S(2)}, u32[]{:S(2)}) collective-permute-start(bf16[128,1024]{1,0:T(8,128)(2,1)S(1)} %multiply_convert_fusion), channel_id=1, source_target_pairs={{0,2},{2,0},{4,6},{6,4},{8,10},{10,8},{12,14},{14,12},{16,18},{18,... | collective-permute-start | bytes 786440 | tf_op jit(solution)/shard_map/ppermute | solution.py:100
  100.8 10.3 %collective-permute-start.24 = (bf16[512,1024]{1,0:T(8,128)(2,1)S(1)}, bf16[512,1024]{1,0:T(8,128)(2,1)S(1)}, u32[]{:S(2)}, u32[]{:S(2)}) collective-permute-start(bf16[512,1024]{1,0:T(8,128)(2,1)S(1)} %constant_dynamic-update-slice_fusion.4.g_m), channel_id=1, source_target_pairs={{0,1},{1,0},{2,3},{3,2},{4,5},{5,4},{6,7},{7,6},{8,9},{9,8},{10,11... | collective-permute-start | bytes 3145736 | tf_op jit(solution)/shard_map/ppermute | solution.py:109
  110.9 2.9 %collective-permute-start.23 = (bf16[512,1024]{1,0:T(8,128)(2,1)S(1)}, bf16[512,1024]{1,0:T(8,128)(2,1)}, u32[]{:S(2)}, u32[]{:S(2)}) collective-permute-start(bf16[512,1024]{1,0:T(8,128)(2,1)S(1)} %pad_maximum_fusion.x_m), channel_id=1, source_target_pairs={{0,1},{1,0},{2,3},{3,2},{4,5},{5,4},{6,7},{7,6},{8,9},{9,8},{10,11... | collective-permute-start | bytes 3145736 | tf_op jit(solution)/shard_map/ppermute | solution.py:109
  133.2 93.8 %reduce-scatter.5.cloned.1.call-start = ((), (), s32[]{:S(2)}) async-start(), calls=%async_computation.4 | async-start | bytes 983040 | tf_op jit(solution)/shard_map/reduce_scatter | solution.py:907
  139.3 2.9 %collective-permute-start.25 = (bf16[512,1024]{1,0:T(8,128)(2,1)}, bf16[512,1024]{1,0:T(8,128)(2,1)S(1)}, u32[]{:S(2)}, u32[]{:S(2)}) collective-permute-start(bf16[512,1024]{1,0:T(8,128)(2,1)} %get-tuple-element.150), channel_id=1, source_target_pairs={{0,1},{1,0},{2,3},{3,2},{4,5},{5,4},{6,7},{7,6},{8,9},{9,8},{10,11... | collective-permute-start | bytes 3145736 | tf_op jit(solution)/shard_map/ppermute | solution.py:109
  145.9 9.9 %collective-permute-start.26 = (bf16[128,1024]{1,0:T(8,128)(2,1)}, bf16[128,1024]{1,0:T(8,128)(2,1)S(1)}, u32[]{:S(2)}, u32[]{:S(2)}) collective-permute-start(bf16[128,1024]{1,0:T(8,128)(2,1)} %get-tuple-element.156), channel_id=1, source_target_pairs={{0,2},{2,0},{4,6},{6,4},{8,10},{10,8},{12,14},{14,12},{16,18},{18,... | collective-permute-start | bytes 786440 | tf_op jit(solution)/shard_map/ppermute | solution.py:100
  147.4 13.9 %collective-permute-start.27 = (bf16[128,1024]{1,0:T(8,128)(2,1)}, bf16[128,1024]{1,0:T(8,128)(2,1)S(1)}, u32[]{:S(2)}, u32[]{:S(2)}) collective-permute-start(bf16[128,1024]{1,0:T(8,128)(2,1)} %get-tuple-element.157), channel_id=1, source_target_pairs={{0,4},{2,6},{4,0},{6,2},{8,12},{10,14},{12,8},{14,10},{16,20},{18,... | collective-permute-start | bytes 786440 | tf_op jit(solution)/shard_map/ppermute | solution.py:100
  148.8 12.4 %collective-permute-start.28 = (bf16[128,1024]{1,0:T(8,128)(2,1)}, bf16[128,1024]{1,0:T(8,128)(2,1)S(1)}, u32[]{:S(2)}, u32[]{:S(2)}) collective-permute-start(bf16[128,1024]{1,0:T(8,128)(2,1)} %get-tuple-element.158), channel_id=1, source_target_pairs={{0,6},{2,4},{4,2},{6,0},{8,14},{10,12},{12,10},{14,8},{16,22},{18,... | collective-permute-start | bytes 786440 | tf_op jit(solution)/shard_map/ppermute | solution.py:100
  162.3 10.2 %collective-permute-start.31 = (bf16[128,1024]{1,0:T(8,128)(2,1)S(1)}, bf16[128,1024]{1,0:T(8,128)(2,1)S(1)}, u32[]{:S(2)}, u32[]{:S(2)}) collective-permute-start(bf16[128,1024]{1,0:T(8,128)(2,1)S(1)} %get-tuple-element.217), channel_id=1, source_target_pairs={{0,6},{2,4},{4,2},{6,0},{8,14},{10,12},{12,10},{14,8},{16,22},{18,... | collective-permute-start | bytes 786440 | tf_op jit(solution)/shard_map/ppermute | solution.py:100
  163.9 12.3 %collective-permute-start.30 = (bf16[128,1024]{1,0:T(8,128)(2,1)S(1)}, bf16[128,1024]{1,0:T(8,128)(2,1)S(1)}, u32[]{:S(2)}, u32[]{:S(2)}) collective-permute-start(bf16[128,1024]{1,0:T(8,128)(2,1)S(1)} %get-tuple-element.217), channel_id=1, source_target_pairs={{0,4},{2,6},{4,0},{6,2},{8,12},{10,14},{12,8},{14,10},{16,20},{18,... | collective-permute-start | bytes 786440 | tf_op jit(solution)/shard_map/ppermute | solution.py:100
  165.0 11.2 %collective-permute-start.29 = (bf16[128,1024]{1,0:T(8,128)(2,1)S(1)}, bf16[128,1024]{1,0:T(8,128)(2,1)S(1)}, u32[]{:S(2)}, u32[]{:S(2)}) collective-permute-start(bf16[128,1024]{1,0:T(8,128)(2,1)S(1)} %get-tuple-element.217), channel_id=1, source_target_pairs={{0,2},{2,0},{4,6},{6,4},{8,10},{10,8},{12,14},{14,12},{16,18},{18,... | collective-permute-start | bytes 786440 | tf_op jit(solution)/shard_map/ppermute | solution.py:100
  165.9 10.6 %collective-permute-start.33 = (bf16[512,1024]{1,0:T(8,128)(2,1)S(1)}, bf16[512,1024]{1,0:T(8,128)(2,1)}, u32[]{:S(2)}, u32[]{:S(2)}) collective-permute-start(bf16[512,1024]{1,0:T(8,128)(2,1)S(1)} %copy-done.41), channel_id=1, source_target_pairs={{0,1},{1,0},{2,3},{3,2},{4,5},{5,4},{6,7},{7,6},{8,9},{9,8},{10,11... | collective-permute-start | bytes 3145736 | tf_op jit(solution)/shard_map/ppermute | solution.py:109
  176.3 3.0 %collective-permute-start.32 = (bf16[512,1024]{1,0:T(8,128)(2,1)S(1)}, bf16[512,1024]{1,0:T(8,128)(2,1)}, u32[]{:S(2)}, u32[]{:S(2)}) collective-permute-start(bf16[512,1024]{1,0:T(8,128)(2,1)S(1)} %pad_maximum_fusion.1.dh_m), channel_id=1, source_target_pairs={{0,1},{1,0},{2,3},{3,2},{4,5},{5,4},{6,7},{7,6},{8,9},{9,8},{10,11... | collective-permute-start | bytes 3145736 | tf_op jit(solution)/shard_map/ppermute | solution.py:109
  179.4 18.7 %collective-permute-start.34 = (bf16[128,1024]{1,0:T(8,128)(2,1)}, bf16[128,1024]{1,0:T(8,128)(2,1)S(1)}, u32[]{:S(2)}, u32[]{:S(2)}) collective-permute-start(bf16[128,1024]{1,0:T(8,128)(2,1)} %get-tuple-element.169), channel_id=1, source_target_pairs={{0,2},{2,0},{4,6},{6,4},{8,10},{10,8},{12,14},{14,12},{16,18},{18,... | collective-permute-start | bytes 786440 | tf_op jit(solution)/shard_map/ppermute | solution.py:100
  180.7 17.4 %collective-permute-start.35 = (bf16[128,1024]{1,0:T(8,128)(2,1)}, bf16[128,1024]{1,0:T(8,128)(2,1)}, u32[]{:S(2)}, u32[]{:S(2)}) collective-permute-start(bf16[128,1024]{1,0:T(8,128)(2,1)} %get-tuple-element.170), channel_id=1, source_target_pairs={{0,4},{2,6},{4,0},{6,2},{8,12},{10,14},{12,8},{14,10},{16,20},{18,... | collective-permute-start | bytes 786440 | tf_op jit(solution)/shard_map/ppermute | solution.py:100
  181.4 16.7 %collective-permute-start.36 = (bf16[128,1024]{1,0:T(8,128)(2,1)}, bf16[128,1024]{1,0:T(8,128)(2,1)}, u32[]{:S(2)}, u32[]{:S(2)}) collective-permute-start(bf16[128,1024]{1,0:T(8,128)(2,1)} %get-tuple-element.171), channel_id=1, source_target_pairs={{0,6},{2,4},{4,2},{6,0},{8,14},{10,12},{12,10},{14,8},{16,22},{18,... | collective-permute-start | bytes 786440 | tf_op jit(solution)/shard_map/ppermute | solution.py:100
  198.1 20.8 %copy-start.12 = (f32[128,1024]{1,0:T(8,128)S(1)}, f32[128,1024]{1,0:T(8,128)}, u32[]{:S(2)}) copy-start(f32[128,1024]{1,0:T(8,128)} %get-tuple-element.168) | copy-start | bytes 1572868
  198.1 8.6 %collective-permute-start.38 = (bf16[512,1024]{1,0:T(8,128)(2,1)}, bf16[512,1024]{1,0:T(8,128)(2,1)S(1)}, u32[]{:S(2)}, u32[]{:S(2)}) collective-permute-start(bf16[512,1024]{1,0:T(8,128)(2,1)} %get-tuple-element.187), channel_id=1, source_target_pairs={{0,1},{1,0},{2,3},{3,2},{4,5},{5,4},{6,7},{7,6},{8,9},{9,8},{10,11... | collective-permute-start | bytes 3145736 | tf_op jit(solution)/shard_map/ppermute | solution.py:109
  198.2 7.8 %collective-permute-start.42 = (f32[8,384]{1,0:T(8,128)}, f32[8,384]{1,0:T(8,128)S(1)}, u32[]{:S(2)}, u32[]{:S(2)}) collective-permute-start(f32[8,384]{1,0:T(8,128)} %get-tuple-element.196), channel_id=1, source_target_pairs={{0,1},{1,0},{2,3},{3,2},{4,5},{5,4},{6,7},{7,6},{8,9},{9,8},{10,11... | collective-permute-start | bytes 36872 | tf_op jit(solution)/shard_map/ppermute | solution.py:109
  202.6 10.9 %collective-permute-start.37 = (bf16[64,1792]{1,0:T(8,128)(2,1)}, bf16[64,1792]{1,0:T(8,128)(2,1)S(1)}, u32[]{:S(2)}, u32[]{:S(2)}) collective-permute-start(bf16[64,1792]{1,0:T(8,128)(2,1)} %get-tuple-element.173), channel_id=1, source_target_pairs={{0,2},{2,0},{4,6},{6,4},{8,10},{10,8},{12,14},{14,12},{16,18},{18,... | collective-permute-start | bytes 688136 | tf_op jit(solution)/shard_map/ppermute | solution.py:100
  204.0 12.8 %collective-permute-start.49 = (bf16[64,1792]{1,0:T(8,128)(2,1)}, bf16[64,1792]{1,0:T(8,128)(2,1)S(1)}, u32[]{:S(2)}, u32[]{:S(2)}) collective-permute-start(bf16[64,1792]{1,0:T(8,128)(2,1)} %get-tuple-element.175), channel_id=1, source_target_pairs={{0,4},{2,6},{4,0},{6,2},{8,12},{10,14},{12,8},{14,10},{16,20},{18,... | collective-permute-start | bytes 688136 | tf_op jit(solution)/shard_map/ppermute | solution.py:100
  205.5 12.8 %collective-permute-start.50 = (bf16[64,1792]{1,0:T(8,128)(2,1)}, bf16[64,1792]{1,0:T(8,128)(2,1)}, u32[]{:S(2)}, u32[]{:S(2)}) collective-permute-start(bf16[64,1792]{1,0:T(8,128)(2,1)} %get-tuple-element.176), channel_id=1, source_target_pairs={{0,6},{2,4},{4,2},{6,0},{8,14},{10,12},{12,10},{14,8},{16,22},{18,... | collective-permute-start | bytes 688136 | tf_op jit(solution)/shard_map/ppermute | solution.py:100
  206.8 20.2 %copy-start.34 = (f32[8,384]{1,0:T(8,128)}, f32[8,384]{1,0:T(8,128)S(1)}, u32[]{:S(2)}) copy-start(f32[8,384]{1,0:T(8,128)S(1)} %add.127.gains) | copy-start | bytes 36868
  210.5 22.3 %copy-start.5 = (f32[128,1024]{1,0:T(8,128)S(1)}, f32[128,1024]{1,0:T(8,128)}, u32[]{:S(2)}) copy-start(f32[128,1024]{1,0:T(8,128)} %get-tuple-element.192) | copy-start | bytes 1572868
  210.5 22.3 %copy-start.26 = (f32[1024]{0:T(1024)S(1)}, f32[1024]{0:T(1024)}, u32[]{:S(2)}) copy-start(f32[1024]{0:T(1024)} %param.16) | copy-start | bytes 12292
  210.5 4.9 %collective-permute-start.45 = (f32[8,384]{1,0:T(8,128)S(1)}, f32[8,384]{1,0:T(8,128)S(1)}, u32[]{:S(2)}, u32[]{:S(2)}) collective-permute-start(f32[8,384]{1,0:T(8,128)S(1)} %add.127.gains), channel_id=1, source_target_pairs={{0,24},{2,26},{4,28},{6,30},{8,0},{10,2},{12,4},{14,6},{16,8},{18,... | collective-permute-start | bytes 36872 | tf_op jit(solution)/shard_map/ppermute | solution.py:105
  212.9 14.1 %collective-permute-start.44 = (f32[8,384]{1,0:T(8,128)S(1)}, f32[8,384]{1,0:T(8,128)S(1)}, u32[]{:S(2)}, u32[]{:S(2)}) collective-permute-start(f32[8,384]{1,0:T(8,128)S(1)} %add.127.gains), channel_id=1, source_target_pairs={{0,16},{2,18},{4,20},{6,22},{8,24},{10,26},{12,28},{14,30},{16,0},... | collective-permute-start | bytes 36872 | tf_op jit(solution)/shard_map/ppermute | solution.py:105
  213.4 13.5 %collective-permute-start.43 = (f32[8,384]{1,0:T(8,128)S(1)}, f32[8,384]{1,0:T(8,128)S(1)}, u32[]{:S(2)}, u32[]{:S(2)}) collective-permute-start(f32[8,384]{1,0:T(8,128)S(1)} %add.127.gains), channel_id=1, source_target_pairs={{0,8},{2,10},{4,12},{6,14},{8,16},{10,18},{12,20},{14,22},{16,24},... | collective-permute-start | bytes 36872 | tf_op jit(solution)/shard_map/ppermute | solution.py:105
  215.4 11.6 %collective-permute-start.39 = (bf16[128,1024]{1,0:T(8,128)(2,1)}, bf16[128,1024]{1,0:T(8,128)(2,1)S(1)}, u32[]{:S(2)}, u32[]{:S(2)}) collective-permute-start(bf16[128,1024]{1,0:T(8,128)(2,1)} %get-tuple-element.193), channel_id=1, source_target_pairs={{0,2},{2,0},{4,6},{6,4},{8,10},{10,8},{12,14},{14,12},{16,18},{18,... | collective-permute-start | bytes 786440 | tf_op jit(solution)/shard_map/ppermute | solution.py:100
  216.9 15.9 %collective-permute-start.40 = (bf16[128,1024]{1,0:T(8,128)(2,1)}, bf16[128,1024]{1,0:T(8,128)(2,1)S(1)}, u32[]{:S(2)}, u32[]{:S(2)}) collective-permute-start(bf16[128,1024]{1,0:T(8,128)(2,1)} %get-tuple-element.194), channel_id=1, source_target_pairs={{0,4},{2,6},{4,0},{6,2},{8,12},{10,14},{12,8},{14,10},{16,20},{18,... | collective-permute-start | bytes 786440 | tf_op jit(solution)/shard_map/ppermute | solution.py:100
  218.3 14.4 %collective-permute-start.41 = (bf16[128,1024]{1,0:T(8,128)(2,1)}, bf16[128,1024]{1,0:T(8,128)(2,1)S(1)}, u32[]{:S(2)}, u32[]{:S(2)}) collective-permute-start(bf16[128,1024]{1,0:T(8,128)(2,1)} %get-tuple-element.195), channel_id=1, source_target_pairs={{0,6},{2,4},{4,2},{6,0},{8,14},{10,12},{12,10},{14,8},{16,22},{18,... | collective-permute-start | bytes 786440 | tf_op jit(solution)/shard_map/ppermute | solution.py:100
  229.3 4.9 %collective-permute-start.46 = (bf16[80,384]{1,0:T(8,128)(2,1)}, bf16[80,384]{1,0:T(8,128)(2,1)S(1)}, u32[]{:S(2)}, u32[]{:S(2)}) collective-permute-start(bf16[80,384]{1,0:T(8,128)(2,1)} %get-tuple-element.201), channel_id=1, source_target_pairs={{0,2},{2,0},{4,6},{6,4},{8,10},{10,8},{12,14},{14,12},{16,18},{18,... | collective-permute-start | bytes 184328 | tf_op jit(solution)/shard_map/ppermute | solution.py:100
  230.8 5.1 %collective-permute-start.47 = (bf16[80,384]{1,0:T(8,128)(2,1)}, bf16[80,384]{1,0:T(8,128)(2,1)S(1)}, u32[]{:S(2)}, u32[]{:S(2)}) collective-permute-start(bf16[80,384]{1,0:T(8,128)(2,1)} %get-tuple-element.202), channel_id=1, source_target_pairs={{0,4},{2,6},{4,0},{6,2},{8,12},{10,14},{12,8},{14,10},{16,20},{18,... | collective-permute-start | bytes 184328 | tf_op jit(solution)/shard_map/ppermute | solution.py:100
  232.2 5.3 %collective-permute-start.48 = (bf16[80,384]{1,0:T(8,128)(2,1)}, bf16[80,384]{1,0:T(8,128)(2,1)S(1)}, u32[]{:S(2)}, u32[]{:S(2)}) collective-permute-start(bf16[80,384]{1,0:T(8,128)(2,1)} %get-tuple-element.203), channel_id=1, source_target_pairs={{0,6},{2,4},{4,2},{6,0},{8,14},{10,12},{12,10},{14,8},{16,22},{18,... | collective-permute-start | bytes 184328 | tf_op jit(solution)/shard_map/ppermute | solution.py:100
  (32 other events, 183.5 us)
Sparse Core Ops, SparseCore 0:
  44.6 72.9 all-gather.1
  133.3 66.9 reduce-scatter.2
  202.6 24.2 reduce-scatter.4

commit v15 on v14

--- a/solution.py
+++ b/solution.py
@@ -505,7 +505,7 @@
     lane = lane_ids((x.shape[0], LANES))
 
     def parts_of(gate, up, d_act):
-        sigma = 1.0 / (1.0 + jnp.exp(-gate))
+        sigma = 0.5 * jnp.tanh(0.5 * gate) + 0.5
         silu = gate * sigma
         act = silu * up
         d_gate = d_act * up * sigma * (1.0 + gate * (1.0 - sigma))

time: 247 us -> 247 us (level)
  transfers between devices with their start and end apart: 54 -> 54, of which waited for: 23 -> 23; matrix products, arithmetic and copies ran while one was open for 5% -> 5% of each run, Pallas kernels for 22% -> 23%
where the time goes in v15:
time: 247 us; the launch traced here: 246 us
  waiting for transfers between devices  78.6 us (32%)
  Pallas kernels  78.2 us (32%)
  starting transfers between devices  52 us (21%)
  between operations  14.2 us (6%)
  other arithmetic  11.8 us (5%)
  local copies, waits for them, and re-layouts  11.4 us (5%)
    ppermute x36, waiting for transfers between devices, send_plane(): return lax.ppermute(values, 'dp', [(i, i ^ mask) for i in range(count)])  53.3 us
    ppermute x36, starting transfers between devices, send_plane(): return lax.ppermute(values, 'dp', [(i, i ^ mask) for i in range(count)])  41.2 us
    pallas_call x12, Pallas kernels, call(): pl.pallas_call(kernel, out_shape=[jax.ShapeDtypeStruct(shape, kind) for s...  27.3 us
    pallas_call x1, Pallas kernels, ffn_layer(): pl.pallas_call(ffn_kernel, grid=(2,), in_specs=[scalar, scalar] + [row_sp...  15.4 us
    pallas_call x1, Pallas kernels, attn_back(): pl.pallas_call(attn_back_kernel, grid=(PLANE // GROUPS_STEP,), in_specs=[...  15.2 us
    pallas_call x2, Pallas kernels, ffn_apply(): pl.pallas_call(ffn_apply_kernel, grid=(2,), in_specs=[pl.BlockSpec((rows,...  10.4 us
    pallas_call x1, Pallas kernels, attn(): pl.pallas_call(lambda *refs: attn_kernel(layers, *refs), grid=(PLANE // G...  9.94 us
    ppermute x6, starting transfers between devices, send_deep(): lax.ppermute(values, 'dp', [(i, (i + PLANE * step) % count) for i in rang...  9.43 us
  transfers between devices with their start and end apart: 54, of which 23 were waited for; matrix products, arithmetic and copies ran while one was open for 5% of the time, Pallas kernels for 23%

profile of v15, /device:TPU:0, one launch (start us, length us, event | category | flops | bytes accessed | tf_op | source)
XLA Modules:
  0.0 246.3 jit_solution(3492211454146512306)
XLA Ops:
  7.9 1.7 shard_map.238
  9.6 2.9 %collective-permute-start = (bf16[32,1024]{1,0:T(8,128)(2,1)}, bf16[32,1024]{1,0:T(8,128)(2,1)S(1)}, u32[]{:S(2)}, u32[]{:S(2)}) collective-permute-start(bf16[32,1024]{1,0:T(8,128)(2,1)} %get-tuple-element.119), channel_id=1, source_target_pairs={{0,2},{2,0},{4,6},{6,4},{8,10},{10,8},{12,14},{14,12},{16,18},{18,... | collective-permute-start | bytes 196616 | tf_op jit(solution)/shard_map/ppermute | solution.py:100
  12.5 1.5 collective-permute-start.1
  14.0 2.2 shard_map.237
  17.0 2.4 collective-permute-done.2.three
  20.0 1.6 shard_map.239
  21.7 3.6 %collective-permute-start.5 = (bf16[256,384]{1,0:T(8,128)(2,1)}, bf16[256,384]{1,0:T(8,128)(2,1)S(1)}, u32[]{:S(2)}, u32[]{:S(2)}) collective-permute-start(bf16[256,384]{1,0:T(8,128)(2,1)} %get-tuple-element.137.refs_9_), channel_id=1, source_target_pairs={{0,24},{2,26},{4,28},{6,30},{8,0},{10,2},{12,4},{14,6},{16,8},{18,... | collective-permute-start | bytes 589832 | tf_op jit(solution)/shard_map/ppermute | solution.py:105
  28.4 2.6 %collective-permute-done.5.refs_12_ = bf16[256,384]{1,0:T(8,128)(2,1)S(1)} collective-permute-done((bf16[256,384]{1,0:T(8,128)(2,1)}, bf16[256,384]{1,0:T(8,128)(2,1)S(1)}, u32[]{:S(2)}, u32[]{:S(2)}) %collective-permute-start.5) | collective-permute-done | bytes 196640 | tf_op jit(solution)/shard_map/ppermute | solution.py:105
  31.5 3.0 %fusion.6 = (f32[1024,128]{1,0:T(8,128)}, f32[1024,128]{1,0:T(8,128)}) fusion(f32[128]{0:T(128)S(1)} %get-tuple-element.225, f32[128]{0:T(128)S(1)} %get-tuple-element.226, f32[1024]{0:T(1024)S(1)} %bitcast.24), kind=kLoop, calls=%fused_computation.13 | loop fusion | flops 262144 | bytes 1053696 | tf_op jit(solution)/shard_map/mul | solution.py:774
  34.5 6.7 %collective-permute-done.4.refs_11_ = bf16[256,384]{1,0:T(8,128)(2,1)S(1)} collective-permute-done((bf16[256,384]{1,0:T(8,128)(2,1)}, bf16[256,384]{1,0:T(8,128)(2,1)S(1)}, u32[]{:S(2)}, u32[]{:S(2)}) %collective-permute-start.4) | collective-permute-done | bytes 196640 | tf_op jit(solution)/shard_map/ppermute | solution.py:105
  42.1 2.3 shard_map.240
  45.6 2.4 collective-permute-start.11
  48.1 5.7 %collective-permute-done.9 = bf16[128,1024]{1,0:T(8,128)(2,1)S(1)} collective-permute-done((bf16[128,1024]{1,0:T(8,128)(2,1)S(1)}, bf16[128,1024]{1,0:T(8,128)(2,1)S(1)}, u32[]{:S(2)}, u32[]{:S(2)}) %collective-permute-start.9) | collective-permute-done | bytes 262176 | tf_op jit(solution)/shard_map/ppermute | solution.py:100
  53.9 3.5 %collective-permute-done.10 = bf16[128,1024]{1,0:T(8,128)(2,1)S(1)} collective-permute-done((bf16[128,1024]{1,0:T(8,128)(2,1)S(1)}, bf16[128,1024]{1,0:T(8,128)(2,1)S(1)}, u32[]{:S(2)}, u32[]{:S(2)}) %collective-permute-start.10) | collective-permute-done | bytes 262176 | tf_op jit(solution)/shard_map/ppermute | solution.py:100
  57.6 1.2 collective-permute-start.15
  58.8 1.4 collective-permute-start.14
  62.7 9.9 %shard_map.241 = (bf16[512,1024]{1,0:T(8,128)(2,1)}, bf16[512,1024]{1,0:T(8,128)(2,1)}, f32[1024,256]{1,0:T(8,128)}, bf16[1024,256]{1,0:T(8,128)(2,1)}, bf16[102...) custom-call(s32[3]{0:T(128)} %pad_add_fusion.where_ref.refs_0_, s32[4,4]{1,0:T(4,128)} %copy-done.33, ...), custom_call_target="tpu_custom_call" | custom-call | flops 1024 | bytes 36000000 | tf_op jit(solution)/shard_map/pallas_call | solution.py:434
  74.3 2.8 %collective-permute-done.16.received = bf16[512,1024]{1,0:T(8,128)(2,1)S(1)} collective-permute-done((bf16[512,1024]{1,0:T(8,128)(2,1)}, bf16[512,1024]{1,0:T(8,128)(2,1)S(1)}, u32[]{:S(2)}, u32[]{:S(2)}) %collective-permute-start.16) | collective-permute-done | bytes 1048608 | tf_op jit(solution)/shard_map/ppermute | solution.py:109
  78.0 2.7 %shard_map.242 = (f32[128,1024]{1,0:T(8,128)}, bf16[128,1024]{1,0:T(8,128)(2,1)}, bf16[128,1024]{1,0:T(8,128)(2,1)}, bf16[128,1024]{1,0:T(8,128)(2,1)}) custom-call(bf16[512,1024]{1,0:T(8,128)(2,1)} %get-tuple-element.141.keep, bf16[512,1024]{1,0:T(8,128)(2,1)} %copy-done.11), custom_call_target="tpu_custom_call" | custom-call | flops 1024 | bytes 1024 | tf_op jit(solution)/shard_map/pallas_call | solution.py:115
  82.5 1.8 collective-permute-start.19
  84.2 5.9 %collective-permute-done.17 = bf16[128,1024]{1,0:T(8,128)(2,1)S(1)} collective-permute-done((bf16[128,1024]{1,0:T(8,128)(2,1)}, bf16[128,1024]{1,0:T(8,128)(2,1)S(1)}, u32[]{:S(2)}, u32[]{:S(2)}) %collective-permute-start.17) | collective-permute-done | bytes 262176 | tf_op jit(solution)/shard_map/ppermute | solution.py:100
  90.1 5.6 %collective-permute-done.18 = bf16[128,1024]{1,0:T(8,128)(2,1)S(1)} collective-permute-done((bf16[128,1024]{1,0:T(8,128)(2,1)}, bf16[128,1024]{1,0:T(8,128)(2,1)S(1)}, u32[]{:S(2)}, u32[]{:S(2)}) %collective-permute-start.18) | collective-permute-done | bytes 262176 | tf_op jit(solution)/shard_map/ppermute | solution.py:100
  95.7 1.3 multiply_reduce_fusion.2
  97.1 1.2 collective-permute-start.22
  98.4 1.3 collective-permute-start.21
  100.9 6.5 %collective-permute-done.22 = bf16[128,1024]{1,0:T(8,128)(2,1)S(1)} collective-permute-done((bf16[128,1024]{1,0:T(8,128)(2,1)S(1)}, bf16[128,1024]{1,0:T(8,128)(2,1)S(1)}, u32[]{:S(2)}, u32[]{:S(2)}) %collective-permute-start.22) | collective-permute-done | bytes 262176 | tf_op jit(solution)/shard_map/ppermute | solution.py:100
  107.4 3.5 %collective-permute-done.21 = bf16[128,1024]{1,0:T(8,128)(2,1)S(1)} collective-permute-done((bf16[128,1024]{1,0:T(8,128)(2,1)S(1)}, bf16[128,1024]{1,0:T(8,128)(2,1)S(1)}, u32[]{:S(2)}, u32[]{:S(2)}) %collective-permute-start.21) | collective-permute-done | bytes 262176 | tf_op jit(solution)/shard_map/ppermute | solution.py:100
  112.2 1.5 collective-permute-done.23.x_o
  113.8 3.9 %all-gather.2.cloned.1.call-done.weight.small = bf16[1024,1792]{1,0:T(8,128)(2,1)} async-done(((bf16[256,1792]{1,0:T(8,128)(2,1)}), bf16[1024,1792]{1,0:T(8,128)(2,1)}) %all-gather.2.cloned.1.call-update) | async-done | bytes 3670032 | tf_op jit(solution)/shard_map/all_gather | solution.py:852
  117.6 15.4 %shard_map.243 = (bf16[1024,640]{1,0:T(8,128)(2,1)}, bf16[1024,1152]{1,0:T(8,128)(2,1)}, bf16[1024,1792]{1,0:T(8,128)(2,1)}) custom-call(s32[3]{0:T(128)} %pad_add_fusion.where_ref.refs_0_, s32[4,4]{1,0:T(4,128)} %copy-done.33, bf16[512,1024]{1,0:T(8,128)(2,1)} %collective-permute-done.23.x_o, bf16[512,1024]{1,0:T(8,128)(2,1)} %copy-done.3, ...), custom_call_target="tpu_custom_call" | custom-call | flops 1024 | bytes 48000000 | tf_op jit(solution)/shard_map/pallas_call | solution.py:552
  133.2 5.9 %shard_map.244 = (bf16[512,1024]{1,0:T(8,128)(2,1)}, bf16[512,1024]{1,0:T(8,128)(2,1)}) custom-call(bf16[1024,1152]{1,0:T(8,128)(2,1)} %get-tuple-element.149.values, bf16[1024,1792]{1,0:T(8,128)(2,1)} %all-gather.2.cloned.1.call-done.weight.small, bf16[1024,1792]{1,0:T(8,128)(2,1)} %all-gather.2.cloned.1.call-done.weight.small), custom_call_target="tpu_custom_call" | custom-call | flops 1024 | bytes 14000000 | tf_op jit(solution)/shard_map/pallas_call | solution.py:585
  139.2 2.9 %collective-permute-done.25.received = bf16[512,1024]{1,0:T(8,128)(2,1)S(1)} collective-permute-done((bf16[512,1024]{1,0:T(8,128)(2,1)}, bf16[512,1024]{1,0:T(8,128)(2,1)S(1)}, u32[]{:S(2)}, u32[]{:S(2)}) %collective-permute-start.25) | collective-permute-done | bytes 1048608 | tf_op jit(solution)/shard_map/ppermute | solution.py:109
  143.1 2.6 %shard_map.246 = (f32[128,1024]{1,0:T(8,128)}, bf16[128,1024]{1,0:T(8,128)(2,1)}, bf16[128,1024]{1,0:T(8,128)(2,1)}, bf16[128,1024]{1,0:T(8,128)(2,1)}) custom-call(bf16[512,1024]{1,0:T(8,128)(2,1)} %get-tuple-element.154.keep, bf16[512,1024]{1,0:T(8,128)(2,1)} %copy-done.10), custom_call_target="tpu_custom_call" | custom-call | flops 1024 | bytes 1024 | tf_op jit(solution)/shard_map/pallas_call | solution.py:115
  145.7 1.5 collective-permute-start.26
  147.2 1.5 collective-permute-start.27
  149.2 1.3 slice.7
  151.2 4.5 %shard_map.245 = (bf16[512,1024]{1,0:T(8,128)(2,1)}, bf16[512,1024]{1,0:T(8,128)(2,1)}) custom-call(bf16[1024,640]{1,0:T(8,128)(2,1)} %get-tuple-element.152.values, bf16[1024,1792]{1,0:T(8,128)(2,1)} %all-gather.2.cloned.1.call-done.weight.small, bf16[1024,1792]{1,0:T(8,128)(2,1)} %all-gather.2.cloned.1.call-done.weight.small), custom_call_target="tpu_custom_call" | custom-call | flops 1024 | bytes 14000000 | tf_op jit(solution)/shard_map/pallas_call | solution.py:585
  155.6 5.5 %collective-permute-done.27 = bf16[128,1024]{1,0:T(8,128)(2,1)S(1)} collective-permute-done((bf16[128,1024]{1,0:T(8,128)(2,1)}, bf16[128,1024]{1,0:T(8,128)(2,1)S(1)}, u32[]{:S(2)}, u32[]{:S(2)}) %collective-permute-start.27) | collective-permute-done | bytes 262176 | tf_op jit(solution)/shard_map/ppermute | solution.py:100
  162.2 1.5 collective-permute-start.31
  163.7 1.2 collective-permute-start.30
  165.7 6.7 %collective-permute-done.31 = bf16[128,1024]{1,0:T(8,128)(2,1)S(1)} collective-permute-done((bf16[128,1024]{1,0:T(8,128)(2,1)S(1)}, bf16[128,1024]{1,0:T(8,128)(2,1)S(1)}, u32[]{:S(2)}, u32[]{:S(2)}) %collective-permute-start.31) | collective-permute-done | bytes 262176 | tf_op jit(solution)/shard_map/ppermute | solution.py:100
  172.4 3.6 %collective-permute-done.30 = bf16[128,1024]{1,0:T(8,128)(2,1)S(1)} collective-permute-done((bf16[128,1024]{1,0:T(8,128)(2,1)S(1)}, bf16[128,1024]{1,0:T(8,128)(2,1)S(1)}, u32[]{:S(2)}, u32[]{:S(2)}) %collective-permute-start.30) | collective-permute-done | bytes 262176 | tf_op jit(solution)/shard_map/ppermute | solution.py:100
  176.3 2.9 %shard_map.247 = (f32[128,1024]{1,0:T(8,128)}, bf16[128,1024]{1,0:T(8,128)(2,1)}, bf16[128,1024]{1,0:T(8,128)(2,1)}, bf16[128,1024]{1,0:T(8,128)(2,1)}) custom-call(bf16[512,1024]{1,0:T(8,128)(2,1)} %get-tuple-element.163.keep, bf16[512,1024]{1,0:T(8,128)(2,1)} %collective-permute-done.33.received), custom_call_target="tpu_custom_call" | custom-call | flops 1024 | bytes 1024 | tf_op jit(solution)/shard_map/pallas_call | solution.py:115
  179.2 1.3 collective-permute-start.34
  181.3 1.5 collective-permute-start.36
  182.7 15.2 %shard_map.249 = (bf16[512,1024]{1,0:T(8,128)(2,1)}, bf16[512,1024]{1,0:T(8,128)(2,1)}, bf16[1024,384]{1,0:T(8,128)(2,1)}, f32[8,384]{1,0:T(8,128)}) custom-call(s32[3]{0:T(128)} %pad_add_fusion.where_ref.refs_0_, s32[4,4]{1,0:T(4,128)} %copy-done.33, bf16[512,1024]{1,0:T(8,128)(2,1)} %copy-done, bf16[512,1024]{1,0:T(8,128)(2,1)} %copy-done.1, ...), custom_call_target="tpu_custom_call" | custom-call | flops 1024 | bytes 24000000 | tf_op jit(solution)/shard_map/pallas_call | solution.py:460
  198.6 1.6 reduce-scatter.3.cloned.1.call-done.own
  200.2 2.2 shard_map.248
  202.4 1.5 collective-permute-start.37
  203.9 1.5 collective-permute-start.49
  207.6 2.8 %shard_map.250 = (f32[128,1024]{1,0:T(8,128)}, bf16[128,1024]{1,0:T(8,128)(2,1)}, bf16[128,1024]{1,0:T(8,128)(2,1)}, bf16[128,1024]{1,0:T(8,128)(2,1)}) custom-call(bf16[512,1024]{1,0:T(8,128)(2,1)} %get-tuple-element.186.keep, bf16[512,1024]{1,0:T(8,128)(2,1)} %copy-done.9), custom_call_target="tpu_custom_call" | custom-call | flops 1024 | bytes 1024 | tf_op jit(solution)/shard_map/pallas_call | solution.py:115
  210.4 2.3 collective-permute-start.45
  213.3 1.9 collective-permute-start.43
  215.2 1.5 collective-permute-start.39
  216.7 1.5 collective-permute-start.40
  218.7 1.9 add_convert_fusion
  220.6 2.7 %shard_map.253 = (f32[64,2304]{1,0:T(8,128)}, f32[64,2304]{1,0:T(8,128)}, f32[64,2304]{1,0:T(8,128)}) custom-call(s32[3]{0:T(128)} %pad_add_fusion.where_ref.refs_0_, bf16[64,1792]{1,0:T(8,128)(2,1)} %get-tuple-element.174.own, bf16[64,1792]{1,0:T(8,128)(2,1)} %copy-done.18, bf16[64,1792]{1,0:T(8,128)(2,1)} %copy-done.19, ...), custom_call_target="tpu_custom_call" | custom-call | flops 1024 | bytes 1024 | tf_op jit(solution)/shard_map/pallas_call | solution.py:115
  223.4 3.4 %reduce-scatter.5.cloned.1.call-done.own = bf16[256,384]{1,0:T(8,128)(2,1)} async-done(((bf16[1024,384]{1,0:T(8,128)(2,1)}), bf16[256,384]{1,0:T(8,128)(2,1)}) %reduce-scatter.5.cloned.1.call-update) | async-done | bytes 196624 | tf_op jit(solution)/shard_map/reduce_scatter | solution.py:907
  227.4 1.7 shard_map.251
  229.1 1.5 collective-permute-start.46
  230.6 1.5 collective-permute-start.47
  234.0 1.7 collective-permute-done.47.two
  235.7 1.7 collective-permute-done.48.three
  238.0 1.7 shard_map.252
  (182 shorter events, 29.7 us)
Async XLA Ops:
  7.2 110.4 %all-gather.2.cloned.1.call-start = ((), (), s32[]{:S(2)}) async-start(), calls=%async_computation.2 | async-start | bytes 4587520 | tf_op jit(solution)/shard_map/all_gather | solution.py:852
  9.6 6.7 %collective-permute-start = (bf16[32,1024]{1,0:T(8,128)(2,1)}, bf16[32,1024]{1,0:T(8,128)(2,1)S(1)}, u32[]{:S(2)}, u32[]{:S(2)}) collective-permute-start(bf16[32,1024]{1,0:T(8,128)(2,1)} %get-tuple-element.119), channel_id=1, source_target_pairs={{0,2},{2,0},{4,6},{6,4},{8,10},{10,8},{12,14},{14,12},{16,18},{18,... | collective-permute-start | bytes 196616 | tf_op jit(solution)/shard_map/ppermute | solution.py:100
  12.5 4.5 %collective-permute-start.1 = (bf16[32,1024]{1,0:T(8,128)(2,1)}, bf16[32,1024]{1,0:T(8,128)(2,1)S(1)}, u32[]{:S(2)}, u32[]{:S(2)}) collective-permute-start(bf16[32,1024]{1,0:T(8,128)(2,1)} %get-tuple-element.120), channel_id=1, source_target_pairs={{0,4},{2,6},{4,0},{6,2},{8,12},{10,14},{12,8},{14,10},{16,20},{18,... | collective-permute-start | bytes 196616 | tf_op jit(solution)/shard_map/ppermute | solution.py:100
  14.0 5.4 %collective-permute-start.2 = (bf16[32,1024]{1,0:T(8,128)(2,1)}, bf16[32,1024]{1,0:T(8,128)(2,1)S(1)}, u32[]{:S(2)}, u32[]{:S(2)}) collective-permute-start(bf16[32,1024]{1,0:T(8,128)(2,1)} %get-tuple-element.121), channel_id=1, source_target_pairs={{0,6},{2,4},{4,2},{6,0},{8,14},{10,12},{12,10},{14,8},{16,22},{18,... | collective-permute-start | bytes 196616 | tf_op jit(solution)/shard_map/ppermute | solution.py:100
  16.2 28.3 %copy-start.4 = (bf16[128,1024]{1,0:T(8,128)(2,1)S(1)}, bf16[128,1024]{1,0:T(8,128)(2,1)}, u32[]{:S(2)}) copy-start(bf16[128,1024]{1,0:T(8,128)(2,1)} %param.14) | copy-start | bytes 786436
  21.7 9.3 %collective-permute-start.5 = (bf16[256,384]{1,0:T(8,128)(2,1)}, bf16[256,384]{1,0:T(8,128)(2,1)S(1)}, u32[]{:S(2)}, u32[]{:S(2)}) collective-permute-start(bf16[256,384]{1,0:T(8,128)(2,1)} %get-tuple-element.137.refs_9_), channel_id=1, source_target_pairs={{0,24},{2,26},{4,28},{6,30},{8,0},{10,2},{12,4},{14,6},{16,8},{18,... | collective-permute-start | bytes 589832 | tf_op jit(solution)/shard_map/ppermute | solution.py:105
  25.3 15.9 %collective-permute-start.4 = (bf16[256,384]{1,0:T(8,128)(2,1)}, bf16[256,384]{1,0:T(8,128)(2,1)S(1)}, u32[]{:S(2)}, u32[]{:S(2)}) collective-permute-start(bf16[256,384]{1,0:T(8,128)(2,1)} %get-tuple-element.137.refs_9_), channel_id=1, source_target_pairs={{0,16},{2,18},{4,20},{6,22},{8,24},{10,26},{12,28},{14,30},{16,0},... | collective-permute-start | bytes 589832 | tf_op jit(solution)/shard_map/ppermute | solution.py:105
  25.3 15.9 %collective-permute-start.3 = (bf16[256,384]{1,0:T(8,128)(2,1)}, bf16[256,384]{1,0:T(8,128)(2,1)S(1)}, u32[]{:S(2)}, u32[]{:S(2)}) collective-permute-start(bf16[256,384]{1,0:T(8,128)(2,1)} %get-tuple-element.137.refs_9_), channel_id=1, source_target_pairs={{0,8},{2,10},{4,12},{6,14},{8,16},{10,18},{12,20},{14,22},{16,24},... | collective-permute-start | bytes 589832 | tf_op jit(solution)/shard_map/ppermute | solution.py:105
  27.2 20.9 %copy-start.33 = (s32[4,4]{1,0:T(4,128)}, s32[4,4]{1,0:T(4,128)S(1)}, u32[]{:S(2)}) copy-start(s32[4,4]{1,0:T(4,128)S(1)} %reduce_window_sum.11.refs_1_.ends_ref) | copy-start | bytes 196
  27.3 13.9 %collective-permute-start.6 = (bf16[64,1792]{1,0:T(8,128)(2,1)}, bf16[64,1792]{1,0:T(8,128)(2,1)S(1)}, u32[]{:S(2)}, u32[]{:S(2)}) collective-permute-start(bf16[64,1792]{1,0:T(8,128)(2,1)} %get-tuple-element.129), channel_id=1, source_target_pairs={{0,2},{2,0},{4,6},{6,4},{8,10},{10,8},{12,14},{14,12},{16,18},{18,... | collective-permute-start | bytes 688136 | tf_op jit(solution)/shard_map/ppermute | solution.py:100
  27.9 13.3 %collective-permute-start.7 = (bf16[64,1792]{1,0:T(8,128)(2,1)}, bf16[64,1792]{1,0:T(8,128)(2,1)S(1)}, u32[]{:S(2)}, u32[]{:S(2)}) collective-permute-start(bf16[64,1792]{1,0:T(8,128)(2,1)} %get-tuple-element.130), channel_id=1, source_target_pairs={{0,4},{2,6},{4,0},{6,2},{8,12},{10,14},{12,8},{14,10},{16,20},{18,... | collective-permute-start | bytes 688136 | tf_op jit(solution)/shard_map/ppermute | solution.py:100
  31.0 10.3 %collective-permute-start.8 = (bf16[64,1792]{1,0:T(8,128)(2,1)}, bf16[64,1792]{1,0:T(8,128)(2,1)S(1)}, u32[]{:S(2)}, u32[]{:S(2)}) collective-permute-start(bf16[64,1792]{1,0:T(8,128)(2,1)} %get-tuple-element.131), channel_id=1, source_target_pairs={{0,6},{2,4},{4,2},{6,0},{8,14},{10,12},{12,10},{14,8},{16,22},{18,... | collective-permute-start | bytes 688136 | tf_op jit(solution)/shard_map/ppermute | solution.py:100
  41.2 20.5 %copy-start.24 = (bf16[256,384]{1,0:T(8,128)(2,1)}, bf16[256,384]{1,0:T(8,128)(2,1)S(1)}, u32[]{:S(2)}) copy-start(bf16[256,384]{1,0:T(8,128)(2,1)S(1)} %collective-permute-done.4.refs_11_) | copy-start | bytes 589828
  41.2 20.5 %copy-start.25 = (bf16[256,384]{1,0:T(8,128)(2,1)}, bf16[256,384]{1,0:T(8,128)(2,1)S(1)}, u32[]{:S(2)}) copy-start(bf16[256,384]{1,0:T(8,128)(2,1)S(1)} %collective-permute-done.3.refs_10_) | copy-start | bytes 589828
  44.5 155.7 %reduce-scatter.3.cloned.1.call-start = ((), (), s32[]{:S(2)}) async-start(), calls=%async_computation.3 | async-start | bytes 4587520 | tf_op jit(solution)/shard_map/reduce_scatter | solution.py:880
  44.5 9.3 %collective-permute-start.9 = (bf16[128,1024]{1,0:T(8,128)(2,1)S(1)}, bf16[128,1024]{1,0:T(8,128)(2,1)S(1)}, u32[]{:S(2)}, u32[]{:S(2)}) collective-permute-start(bf16[128,1024]{1,0:T(8,128)(2,1)S(1)} %copy-done.4), channel_id=1, source_target_pairs={{0,2},{2,0},{4,6},{6,4},{8,10},{10,8},{12,14},{14,12},{16,18},{18,... | collective-permute-start | bytes 786440 | tf_op jit(solution)/shard_map/ppermute | solution.py:100
  45.1 12.3 %collective-permute-start.10 = (bf16[128,1024]{1,0:T(8,128)(2,1)S(1)}, bf16[128,1024]{1,0:T(8,128)(2,1)S(1)}, u32[]{:S(2)}, u32[]{:S(2)}) collective-permute-start(bf16[128,1024]{1,0:T(8,128)(2,1)S(1)} %copy-done.4), channel_id=1, source_target_pairs={{0,4},{2,6},{4,0},{6,2},{8,12},{10,14},{12,8},{14,10},{16,20},{18,... | collective-permute-start | bytes 786440 | tf_op jit(solution)/shard_map/ppermute | solution.py:100
  45.6 11.8 %collective-permute-start.11 = (bf16[128,1024]{1,0:T(8,128)(2,1)S(1)}, bf16[128,1024]{1,0:T(8,128)(2,1)S(1)}, u32[]{:S(2)}, u32[]{:S(2)}) collective-permute-start(bf16[128,1024]{1,0:T(8,128)(2,1)S(1)} %copy-done.4), channel_id=1, source_target_pairs={{0,6},{2,4},{4,2},{6,0},{8,14},{10,12},{12,10},{14,8},{16,22},{18,... | collective-permute-start | bytes 786440 | tf_op jit(solution)/shard_map/ppermute | solution.py:100
  57.5 4.2 %collective-permute-start.12 = (bf16[512,1024]{1,0:T(8,128)(2,1)S(1)}, bf16[512,1024]{1,0:T(8,128)(2,1)S(1)}, u32[]{:S(2)}, u32[]{:S(2)}) collective-permute-start(bf16[512,1024]{1,0:T(8,128)(2,1)S(1)} %constant_dynamic-update-slice_fusion.refs_2_.tok_m), channel_id=1, source_target_pairs={{0,1},{1,0},{2,3},{3,2},{4,5},{5,4},{6,7},{7,6},{8,9},{9,8},{10,11... | collective-permute-start | bytes 3145736 | tf_op jit(solution)/shard_map/ppermute | solution.py:109
  57.6 15.1 %collective-permute-start.15 = (bf16[128,1024]{1,0:T(8,128)(2,1)S(1)}, bf16[128,1024]{1,0:T(8,128)(2,1)S(1)}, u32[]{:S(2)}, u32[]{:S(2)}) collective-permute-start(bf16[128,1024]{1,0:T(8,128)(2,1)S(1)} %copy-done.8), channel_id=1, source_target_pairs={{0,6},{2,4},{4,2},{6,0},{8,14},{10,12},{12,10},{14,8},{16,22},{18,... | collective-permute-start | bytes 786440 | tf_op jit(solution)/shard_map/ppermute | solution.py:100
  58.8 14.0 %collective-permute-start.14 = (bf16[128,1024]{1,0:T(8,128)(2,1)S(1)}, bf16[128,1024]{1,0:T(8,128)(2,1)S(1)}, u32[]{:S(2)}, u32[]{:S(2)}) collective-permute-start(bf16[128,1024]{1,0:T(8,128)(2,1)S(1)} %copy-done.8), channel_id=1, source_target_pairs={{0,4},{2,6},{4,0},{6,2},{8,12},{10,14},{12,8},{14,10},{16,20},{18,... | collective-permute-start | bytes 786440 | tf_op jit(solution)/shard_map/ppermute | solution.py:100
  60.2 12.6 %collective-permute-start.13 = (bf16[128,1024]{1,0:T(8,128)(2,1)S(1)}, bf16[128,1024]{1,0:T(8,128)(2,1)S(1)}, u32[]{:S(2)}, u32[]{:S(2)}) collective-permute-start(bf16[128,1024]{1,0:T(8,128)(2,1)S(1)} %copy-done.8), channel_id=1, source_target_pairs={{0,2},{2,0},{4,6},{6,4},{8,10},{10,8},{12,14},{14,12},{16,18},{18,... | collective-permute-start | bytes 786440 | tf_op jit(solution)/shard_map/ppermute | solution.py:100
  74.2 2.9 %collective-permute-start.16 = (bf16[512,1024]{1,0:T(8,128)(2,1)}, bf16[512,1024]{1,0:T(8,128)(2,1)S(1)}, u32[]{:S(2)}, u32[]{:S(2)}) collective-permute-start(bf16[512,1024]{1,0:T(8,128)(2,1)} %get-tuple-element.144), channel_id=1, source_target_pairs={{0,1},{1,0},{2,3},{3,2},{4,5},{5,4},{6,7},{7,6},{8,9},{9,8},{10,11... | collective-permute-start | bytes 3145736 | tf_op jit(solution)/shard_map/ppermute | solution.py:109
  80.7 20.0 %copy-start.17 = (bf16[128,1024]{1,0:T(8,128)(2,1)S(1)}, bf16[128,1024]{1,0:T(8,128)(2,1)}, u32[]{:S(2)}) copy-start(bf16[128,1024]{1,0:T(8,128)(2,1)} %copy-done.16) | copy-start | bytes 786436
  80.7 20.0 %copy-start.15 = (bf16[128,1024]{1,0:T(8,128)(2,1)S(1)}, bf16[128,1024]{1,0:T(8,128)(2,1)}, u32[]{:S(2)}) copy-start(bf16[128,1024]{1,0:T(8,128)(2,1)} %copy-done.14) | copy-start | bytes 786436
  80.7 9.4 %collective-permute-start.17 = (bf16[128,1024]{1,0:T(8,128)(2,1)}, bf16[128,1024]{1,0:T(8,128)(2,1)S(1)}, u32[]{:S(2)}, u32[]{:S(2)}) collective-permute-start(bf16[128,1024]{1,0:T(8,128)(2,1)} %get-tuple-element.146), channel_id=1, source_target_pairs={{0,2},{2,0},{4,6},{6,4},{8,10},{10,8},{12,14},{14,12},{16,18},{18,... | collective-permute-start | bytes 786440 | tf_op jit(solution)/shard_map/ppermute | solution.py:100
  81.7 13.9 %collective-permute-start.18 = (bf16[128,1024]{1,0:T(8,128)(2,1)}, bf16[128,1024]{1,0:T(8,128)(2,1)S(1)}, u32[]{:S(2)}, u32[]{:S(2)}) collective-permute-start(bf16[128,1024]{1,0:T(8,128)(2,1)} %get-tuple-element.147), channel_id=1, source_target_pairs={{0,4},{2,6},{4,0},{6,2},{8,12},{10,14},{12,8},{14,10},{16,20},{18,... | collective-permute-start | bytes 786440 | tf_op jit(solution)/shard_map/ppermute | solution.py:100
  82.5 13.2 %collective-permute-start.19 = (bf16[128,1024]{1,0:T(8,128)(2,1)}, bf16[128,1024]{1,0:T(8,128)(2,1)S(1)}, u32[]{:S(2)}, u32[]{:S(2)}) collective-permute-start(bf16[128,1024]{1,0:T(8,128)(2,1)} %get-tuple-element.148), channel_id=1, source_target_pairs={{0,6},{2,4},{4,2},{6,0},{8,14},{10,12},{12,10},{14,8},{16,22},{18,... | collective-permute-start | bytes 786440 | tf_op jit(solution)/shard_map/ppermute | solution.py:100
  97.1 10.2 %collective-permute-start.22 = (bf16[128,1024]{1,0:T(8,128)(2,1)S(1)}, bf16[128,1024]{1,0:T(8,128)(2,1)S(1)}, u32[]{:S(2)}, u32[]{:S(2)}) collective-permute-start(bf16[128,1024]{1,0:T(8,128)(2,1)S(1)} %multiply_convert_fusion), channel_id=1, source_target_pairs={{0,6},{2,4},{4,2},{6,0},{8,14},{10,12},{12,10},{14,8},{16,22},{18,... | collective-permute-start | bytes 786440 | tf_op jit(solution)/shard_map/ppermute | solution.py:100
  98.4 12.5 %collective-permute-start.21 = (bf16[128,1024]{1,0:T(8,128)(2,1)S(1)}, bf16[128,1024]{1,0:T(8,128)(2,1)S(1)}, u32[]{:S(2)}, u32[]{:S(2)}) collective-permute-start(bf16[128,1024]{1,0:T(8,128)(2,1)S(1)} %multiply_convert_fusion), channel_id=1, source_target_pairs={{0,4},{2,6},{4,0},{6,2},{8,12},{10,14},{12,8},{14,10},{16,20},{18,... | collective-permute-start | bytes 786440 | tf_op jit(solution)/shard_map/ppermute | solution.py:100
  99.7 11.2 %collective-permute-start.20 = (bf16[128,1024]{1,0:T(8,128)(2,1)S(1)}, bf16[128,1024]{1,0:T(8,128)(2,1)S(1)}, u32[]{:S(2)}, u32[]{:S(2)}) collective-permute-start(bf16[128,1024]{1,0:T(8,128)(2,1)S(1)} %multiply_convert_fusion), channel_id=1, source_target_pairs={{0,2},{2,0},{4,6},{6,4},{8,10},{10,8},{12,14},{14,12},{16,18},{18,... | collective-permute-start | bytes 786440 | tf_op jit(solution)/shard_map/ppermute | solution.py:100
  100.8 10.3 %collective-permute-start.24 = (bf16[512,1024]{1,0:T(8,128)(2,1)S(1)}, bf16[512,1024]{1,0:T(8,128)(2,1)S(1)}, u32[]{:S(2)}, u32[]{:S(2)}) collective-permute-start(bf16[512,1024]{1,0:T(8,128)(2,1)S(1)} %constant_dynamic-update-slice_fusion.4.g_m), channel_id=1, source_target_pairs={{0,1},{1,0},{2,3},{3,2},{4,5},{5,4},{6,7},{7,6},{8,9},{9,8},{10,11... | collective-permute-start | bytes 3145736 | tf_op jit(solution)/shard_map/ppermute | solution.py:109
  110.9 2.9 %collective-permute-start.23 = (bf16[512,1024]{1,0:T(8,128)(2,1)S(1)}, bf16[512,1024]{1,0:T(8,128)(2,1)}, u32[]{:S(2)}, u32[]{:S(2)}) collective-permute-start(bf16[512,1024]{1,0:T(8,128)(2,1)S(1)} %pad_maximum_fusion.x_m), channel_id=1, source_target_pairs={{0,1},{1,0},{2,3},{3,2},{4,5},{5,4},{6,7},{7,6},{8,9},{9,8},{10,11... | collective-permute-start | bytes 3145736 | tf_op jit(solution)/shard_map/ppermute | solution.py:109
  133.0 93.8 %reduce-scatter.5.cloned.1.call-start = ((), (), s32[]{:S(2)}) async-start(), calls=%async_computation.4 | async-start | bytes 983040 | tf_op jit(solution)/shard_map/reduce_scatter | solution.py:907
  139.2 2.9 %collective-permute-start.25 = (bf16[512,1024]{1,0:T(8,128)(2,1)}, bf16[512,1024]{1,0:T(8,128)(2,1)S(1)}, u32[]{:S(2)}, u32[]{:S(2)}) collective-permute-start(bf16[512,1024]{1,0:T(8,128)(2,1)} %get-tuple-element.150), channel_id=1, source_target_pairs={{0,1},{1,0},{2,3},{3,2},{4,5},{5,4},{6,7},{7,6},{8,9},{9,8},{10,11... | collective-permute-start | bytes 3145736 | tf_op jit(solution)/shard_map/ppermute | solution.py:109
  145.7 9.9 %collective-permute-start.26 = (bf16[128,1024]{1,0:T(8,128)(2,1)}, bf16[128,1024]{1,0:T(8,128)(2,1)S(1)}, u32[]{:S(2)}, u32[]{:S(2)}) collective-permute-start(bf16[128,1024]{1,0:T(8,128)(2,1)} %get-tuple-element.156), channel_id=1, source_target_pairs={{0,2},{2,0},{4,6},{6,4},{8,10},{10,8},{12,14},{14,12},{16,18},{18,... | collective-permute-start | bytes 786440 | tf_op jit(solution)/shard_map/ppermute | solution.py:100
  147.2 13.9 %collective-permute-start.27 = (bf16[128,1024]{1,0:T(8,128)(2,1)}, bf16[128,1024]{1,0:T(8,128)(2,1)S(1)}, u32[]{:S(2)}, u32[]{:S(2)}) collective-permute-start(bf16[128,1024]{1,0:T(8,128)(2,1)} %get-tuple-element.157), channel_id=1, source_target_pairs={{0,4},{2,6},{4,0},{6,2},{8,12},{10,14},{12,8},{14,10},{16,20},{18,... | collective-permute-start | bytes 786440 | tf_op jit(solution)/shard_map/ppermute | solution.py:100
  148.7 12.4 %collective-permute-start.28 = (bf16[128,1024]{1,0:T(8,128)(2,1)}, bf16[128,1024]{1,0:T(8,128)(2,1)S(1)}, u32[]{:S(2)}, u32[]{:S(2)}) collective-permute-start(bf16[128,1024]{1,0:T(8,128)(2,1)} %get-tuple-element.158), channel_id=1, source_target_pairs={{0,6},{2,4},{4,2},{6,0},{8,14},{10,12},{12,10},{14,8},{16,22},{18,... | collective-permute-start | bytes 786440 | tf_op jit(solution)/shard_map/ppermute | solution.py:100
  162.2 10.2 %collective-permute-start.31 = (bf16[128,1024]{1,0:T(8,128)(2,1)S(1)}, bf16[128,1024]{1,0:T(8,128)(2,1)S(1)}, u32[]{:S(2)}, u32[]{:S(2)}) collective-permute-start(bf16[128,1024]{1,0:T(8,128)(2,1)S(1)} %get-tuple-element.217), channel_id=1, source_target_pairs={{0,6},{2,4},{4,2},{6,0},{8,14},{10,12},{12,10},{14,8},{16,22},{18,... | collective-permute-start | bytes 786440 | tf_op jit(solution)/shard_map/ppermute | solution.py:100
  163.7 12.3 %collective-permute-start.30 = (bf16[128,1024]{1,0:T(8,128)(2,1)S(1)}, bf16[128,1024]{1,0:T(8,128)(2,1)S(1)}, u32[]{:S(2)}, u32[]{:S(2)}) collective-permute-start(bf16[128,1024]{1,0:T(8,128)(2,1)S(1)} %get-tuple-element.217), channel_id=1, source_target_pairs={{0,4},{2,6},{4,0},{6,2},{8,12},{10,14},{12,8},{14,10},{16,20},{18,... | collective-permute-start | bytes 786440 | tf_op jit(solution)/shard_map/ppermute | solution.py:100
  164.9 11.2 %collective-permute-start.29 = (bf16[128,1024]{1,0:T(8,128)(2,1)S(1)}, bf16[128,1024]{1,0:T(8,128)(2,1)S(1)}, u32[]{:S(2)}, u32[]{:S(2)}) collective-permute-start(bf16[128,1024]{1,0:T(8,128)(2,1)S(1)} %get-tuple-element.217), channel_id=1, source_target_pairs={{0,2},{2,0},{4,6},{6,4},{8,10},{10,8},{12,14},{14,12},{16,18},{18,... | collective-permute-start | bytes 786440 | tf_op jit(solution)/shard_map/ppermute | solution.py:100
  165.7 10.6 %collective-permute-start.33 = (bf16[512,1024]{1,0:T(8,128)(2,1)S(1)}, bf16[512,1024]{1,0:T(8,128)(2,1)}, u32[]{:S(2)}, u32[]{:S(2)}) collective-permute-start(bf16[512,1024]{1,0:T(8,128)(2,1)S(1)} %copy-done.41), channel_id=1, source_target_pairs={{0,1},{1,0},{2,3},{3,2},{4,5},{5,4},{6,7},{7,6},{8,9},{9,8},{10,11... | collective-permute-start | bytes 3145736 | tf_op jit(solution)/shard_map/ppermute | solution.py:109
  176.2 3.0 %collective-permute-start.32 = (bf16[512,1024]{1,0:T(8,128)(2,1)S(1)}, bf16[512,1024]{1,0:T(8,128)(2,1)}, u32[]{:S(2)}, u32[]{:S(2)}) collective-permute-start(bf16[512,1024]{1,0:T(8,128)(2,1)S(1)} %pad_maximum_fusion.1.dh_m), channel_id=1, source_target_pairs={{0,1},{1,0},{2,3},{3,2},{4,5},{5,4},{6,7},{7,6},{8,9},{9,8},{10,11... | collective-permute-start | bytes 3145736 | tf_op jit(solution)/shard_map/ppermute | solution.py:109
  179.2 18.7 %collective-permute-start.34 = (bf16[128,1024]{1,0:T(8,128)(2,1)}, bf16[128,1024]{1,0:T(8,128)(2,1)S(1)}, u32[]{:S(2)}, u32[]{:S(2)}) collective-permute-start(bf16[128,1024]{1,0:T(8,128)(2,1)} %get-tuple-element.169), channel_id=1, source_target_pairs={{0,2},{2,0},{4,6},{6,4},{8,10},{10,8},{12,14},{14,12},{16,18},{18,... | collective-permute-start | bytes 786440 | tf_op jit(solution)/shard_map/ppermute | solution.py:100
  180.6 17.4 %collective-permute-start.35 = (bf16[128,1024]{1,0:T(8,128)(2,1)}, bf16[128,1024]{1,0:T(8,128)(2,1)}, u32[]{:S(2)}, u32[]{:S(2)}) collective-permute-start(bf16[128,1024]{1,0:T(8,128)(2,1)} %get-tuple-element.170), channel_id=1, source_target_pairs={{0,4},{2,6},{4,0},{6,2},{8,12},{10,14},{12,8},{14,10},{16,20},{18,... | collective-permute-start | bytes 786440 | tf_op jit(solution)/shard_map/ppermute | solution.py:100
  181.3 16.7 %collective-permute-start.36 = (bf16[128,1024]{1,0:T(8,128)(2,1)}, bf16[128,1024]{1,0:T(8,128)(2,1)}, u32[]{:S(2)}, u32[]{:S(2)}) collective-permute-start(bf16[128,1024]{1,0:T(8,128)(2,1)} %get-tuple-element.171), channel_id=1, source_target_pairs={{0,6},{2,4},{4,2},{6,0},{8,14},{10,12},{12,10},{14,8},{16,22},{18,... | collective-permute-start | bytes 786440 | tf_op jit(solution)/shard_map/ppermute | solution.py:100
  197.9 20.8 %copy-start.12 = (f32[128,1024]{1,0:T(8,128)S(1)}, f32[128,1024]{1,0:T(8,128)}, u32[]{:S(2)}) copy-start(f32[128,1024]{1,0:T(8,128)} %get-tuple-element.168) | copy-start | bytes 1572868
  198.0 8.6 %collective-permute-start.38 = (bf16[512,1024]{1,0:T(8,128)(2,1)}, bf16[512,1024]{1,0:T(8,128)(2,1)S(1)}, u32[]{:S(2)}, u32[]{:S(2)}) collective-permute-start(bf16[512,1024]{1,0:T(8,128)(2,1)} %get-tuple-element.187), channel_id=1, source_target_pairs={{0,1},{1,0},{2,3},{3,2},{4,5},{5,4},{6,7},{7,6},{8,9},{9,8},{10,11... | collective-permute-start | bytes 3145736 | tf_op jit(solution)/shard_map/ppermute | solution.py:109
  198.1 7.8 %collective-permute-start.42 = (f32[8,384]{1,0:T(8,128)}, f32[8,384]{1,0:T(8,128)S(1)}, u32[]{:S(2)}, u32[]{:S(2)}) collective-permute-start(f32[8,384]{1,0:T(8,128)} %get-tuple-element.196), channel_id=1, source_target_pairs={{0,1},{1,0},{2,3},{3,2},{4,5},{5,4},{6,7},{7,6},{8,9},{9,8},{10,11... | collective-permute-start | bytes 36872 | tf_op jit(solution)/shard_map/ppermute | solution.py:109
  202.4 10.8 %collective-permute-start.37 = (bf16[64,1792]{1,0:T(8,128)(2,1)}, bf16[64,1792]{1,0:T(8,128)(2,1)S(1)}, u32[]{:S(2)}, u32[]{:S(2)}) collective-permute-start(bf16[64,1792]{1,0:T(8,128)(2,1)} %get-tuple-element.173), channel_id=1, source_target_pairs={{0,2},{2,0},{4,6},{6,4},{8,10},{10,8},{12,14},{14,12},{16,18},{18,... | collective-permute-start | bytes 688136 | tf_op jit(solution)/shard_map/ppermute | solution.py:100
  203.9 12.8 %collective-permute-start.49 = (bf16[64,1792]{1,0:T(8,128)(2,1)}, bf16[64,1792]{1,0:T(8,128)(2,1)S(1)}, u32[]{:S(2)}, u32[]{:S(2)}) collective-permute-start(bf16[64,1792]{1,0:T(8,128)(2,1)} %get-tuple-element.175), channel_id=1, source_target_pairs={{0,4},{2,6},{4,0},{6,2},{8,12},{10,14},{12,8},{14,10},{16,20},{18,... | collective-permute-start | bytes 688136 | tf_op jit(solution)/shard_map/ppermute | solution.py:100
  205.4 12.8 %collective-permute-start.50 = (bf16[64,1792]{1,0:T(8,128)(2,1)}, bf16[64,1792]{1,0:T(8,128)(2,1)}, u32[]{:S(2)}, u32[]{:S(2)}) collective-permute-start(bf16[64,1792]{1,0:T(8,128)(2,1)} %get-tuple-element.176), channel_id=1, source_target_pairs={{0,6},{2,4},{4,2},{6,0},{8,14},{10,12},{12,10},{14,8},{16,22},{18,... | collective-permute-start | bytes 688136 | tf_op jit(solution)/shard_map/ppermute | solution.py:100
  206.6 20.2 %copy-start.34 = (f32[8,384]{1,0:T(8,128)}, f32[8,384]{1,0:T(8,128)S(1)}, u32[]{:S(2)}) copy-start(f32[8,384]{1,0:T(8,128)S(1)} %add.127.gains) | copy-start | bytes 36868
  210.4 22.3 %copy-start.5 = (f32[128,1024]{1,0:T(8,128)S(1)}, f32[128,1024]{1,0:T(8,128)}, u32[]{:S(2)}) copy-start(f32[128,1024]{1,0:T(8,128)} %get-tuple-element.192) | copy-start | bytes 1572868
  210.4 22.3 %copy-start.26 = (f32[1024]{0:T(1024)S(1)}, f32[1024]{0:T(1024)}, u32[]{:S(2)}) copy-start(f32[1024]{0:T(1024)} %param.16) | copy-start | bytes 12292
  210.4 4.8 %collective-permute-start.45 = (f32[8,384]{1,0:T(8,128)S(1)}, f32[8,384]{1,0:T(8,128)S(1)}, u32[]{:S(2)}, u32[]{:S(2)}) collective-permute-start(f32[8,384]{1,0:T(8,128)S(1)} %add.127.gains), channel_id=1, source_target_pairs={{0,24},{2,26},{4,28},{6,30},{8,0},{10,2},{12,4},{14,6},{16,8},{18,... | collective-permute-start | bytes 36872 | tf_op jit(solution)/shard_map/ppermute | solution.py:105
  212.7 14.1 %collective-permute-start.44 = (f32[8,384]{1,0:T(8,128)S(1)}, f32[8,384]{1,0:T(8,128)S(1)}, u32[]{:S(2)}, u32[]{:S(2)}) collective-permute-start(f32[8,384]{1,0:T(8,128)S(1)} %add.127.gains), channel_id=1, source_target_pairs={{0,16},{2,18},{4,20},{6,22},{8,24},{10,26},{12,28},{14,30},{16,0},... | collective-permute-start | bytes 36872 | tf_op jit(solution)/shard_map/ppermute | solution.py:105
  213.3 13.6 %collective-permute-start.43 = (f32[8,384]{1,0:T(8,128)S(1)}, f32[8,384]{1,0:T(8,128)S(1)}, u32[]{:S(2)}, u32[]{:S(2)}) collective-permute-start(f32[8,384]{1,0:T(8,128)S(1)} %add.127.gains), channel_id=1, source_target_pairs={{0,8},{2,10},{4,12},{6,14},{8,16},{10,18},{12,20},{14,22},{16,24},... | collective-permute-start | bytes 36872 | tf_op jit(solution)/shard_map/ppermute | solution.py:105
  215.2 11.6 %collective-permute-start.39 = (bf16[128,1024]{1,0:T(8,128)(2,1)}, bf16[128,1024]{1,0:T(8,128)(2,1)S(1)}, u32[]{:S(2)}, u32[]{:S(2)}) collective-permute-start(bf16[128,1024]{1,0:T(8,128)(2,1)} %get-tuple-element.193), channel_id=1, source_target_pairs={{0,2},{2,0},{4,6},{6,4},{8,10},{10,8},{12,14},{14,12},{16,18},{18,... | collective-permute-start | bytes 786440 | tf_op jit(solution)/shard_map/ppermute | solution.py:100
  216.7 15.9 %collective-permute-start.40 = (bf16[128,1024]{1,0:T(8,128)(2,1)}, bf16[128,1024]{1,0:T(8,128)(2,1)S(1)}, u32[]{:S(2)}, u32[]{:S(2)}) collective-permute-start(bf16[128,1024]{1,0:T(8,128)(2,1)} %get-tuple-element.194), channel_id=1, source_target_pairs={{0,4},{2,6},{4,0},{6,2},{8,12},{10,14},{12,8},{14,10},{16,20},{18,... | collective-permute-start | bytes 786440 | tf_op jit(solution)/shard_map/ppermute | solution.py:100
  218.2 14.4 %collective-permute-start.41 = (bf16[128,1024]{1,0:T(8,128)(2,1)}, bf16[128,1024]{1,0:T(8,128)(2,1)S(1)}, u32[]{:S(2)}, u32[]{:S(2)}) collective-permute-start(bf16[128,1024]{1,0:T(8,128)(2,1)} %get-tuple-element.195), channel_id=1, source_target_pairs={{0,6},{2,4},{4,2},{6,0},{8,14},{10,12},{12,10},{14,8},{16,22},{18,... | collective-permute-start | bytes 786440 | tf_op jit(solution)/shard_map/ppermute | solution.py:100
  229.1 4.9 %collective-permute-start.46 = (bf16[80,384]{1,0:T(8,128)(2,1)}, bf16[80,384]{1,0:T(8,128)(2,1)S(1)}, u32[]{:S(2)}, u32[]{:S(2)}) collective-permute-start(bf16[80,384]{1,0:T(8,128)(2,1)} %get-tuple-element.201), channel_id=1, source_target_pairs={{0,2},{2,0},{4,6},{6,4},{8,10},{10,8},{12,14},{14,12},{16,18},{18,... | collective-permute-start | bytes 184328 | tf_op jit(solution)/shard_map/ppermute | solution.py:100
  230.6 5.1 %collective-permute-start.47 = (bf16[80,384]{1,0:T(8,128)(2,1)}, bf16[80,384]{1,0:T(8,128)(2,1)S(1)}, u32[]{:S(2)}, u32[]{:S(2)}) collective-permute-start(bf16[80,384]{1,0:T(8,128)(2,1)} %get-tuple-element.202), channel_id=1, source_target_pairs={{0,4},{2,6},{4,0},{6,2},{8,12},{10,14},{12,8},{14,10},{16,20},{18,... | collective-permute-start | bytes 184328 | tf_op jit(solution)/shard_map/ppermute | solution.py:100
  232.1 5.3 %collective-permute-start.48 = (bf16[80,384]{1,0:T(8,128)(2,1)}, bf16[80,384]{1,0:T(8,128)(2,1)S(1)}, u32[]{:S(2)}, u32[]{:S(2)}) collective-permute-start(bf16[80,384]{1,0:T(8,128)(2,1)} %get-tuple-element.203), channel_id=1, source_target_pairs={{0,6},{2,4},{4,2},{6,0},{8,14},{10,12},{12,10},{14,8},{16,22},{18,... | collective-permute-start | bytes 184328 | tf_op jit(solution)/shard_map/ppermute | solution.py:100
  (32 other events, 183.5 us)
Sparse Core Ops, SparseCore 0:
  44.6 72.9 all-gather.1
  133.1 66.9 reduce-scatter.2
  202.5 24.2 reduce-scatter.4
